TPU v7x, 32 devices: a whole 2x2x4 slice. The times are simulated.
32 devices in a mesh: shard: 32 (over z, y, x, core).
Axes of the slice: x: 2, y: 2, z: 4, core: 2. Of those that a mesh axis runs over, the one named last changes fastest.
Arguments:
- queries: bfloat16 [512, 8, 9600], P('shard'), may hold values from -6 to 6
- index_videos: bfloat16 [4096, 8, 9600], P('shard'), may hold values from -6 to 6
- candidates: int32 [512, 8], P('shard'), may hold values from 0 to 4095, as said below
- conv_one: bfloat16 [32, 1, 3, 3], replicated, may hold values from -2 to 2
- conv_two: bfloat16 [64, 32, 3, 3], replicated, may hold values from -0.375 to 0.375
- conv_three: bfloat16 [1, 64, 3, 3], replicated, may hold values from -0.25 to 0.25
Outputs:
- scores: float32 [512, 8], P('shard')
Inputs may be any that keep to these rules, and one draw needn't show every extreme that they name: `candidates`: each new video's 8 ids are distinct. The videos of id v are held by device v // 128. Of one device's pairs at most 8 name videos of one holder; in every draw some holders receive exactly 8 from every device.
All inputs are finite; a program needn't handle non-finite values.
Results may differ from a plain program's by a relative error of at most 0.0041.
Values may be sent and summed in bfloat16 or wider, within the bound.
No kernel may reach another device: no remote copies, remote signals or barrier semaphores. Data moves between devices by JAX's collectives and lax.ppermute only.
A program may use at most 256 MiB of HBM per device.

v0:
```python
import math

import jax
import jax.numpy as jnp
from jax import lax
from jax.sharding import PartitionSpec as P

F = 8
R = 5
REGION_FEATURES = 1920


def conv_same(x, w):
    return lax.conv_general_dilated(
        x,
        w,
        (1, 1),
        "SAME",
        dimension_numbers=("NCHW", "OIHW", "NCHW"),
        preferred_element_type=jnp.float32,
    )


def pool_two(x):
    b, c, h, w = x.shape
    return jnp.max(x.reshape(b, c, h // 2, 2, w // 2, 2), axis=(3, 5))


def pair_scores(left, right, conv_one, conv_two, conv_three):
    count = left.shape[0]
    left_region_features = left.reshape(count, F * R, REGION_FEATURES)
    right_region_features = right.reshape(count, F * R, REGION_FEATURES)
    region_similarities = jnp.einsum(
        "avs,afs->avf",
        left_region_features,
        right_region_features,
        preferred_element_type=jnp.float32,
    ) * (1.0 / math.sqrt(REGION_FEATURES))
    region_similarities = region_similarities.reshape(count, F, R, F, R)
    frame_map = jnp.mean(jnp.max(region_similarities, axis=4), axis=2).astype(jnp.bfloat16)
    first = pool_two(jax.nn.relu(conv_same(frame_map[:, None], conv_one))).astype(jnp.bfloat16)
    second = pool_two(jax.nn.relu(conv_same(first, conv_two))).astype(jnp.bfloat16)
    final = conv_same(second, conv_three)[:, 0]
    return jnp.mean(jnp.max(jnp.clip(final, -1.0, 1.0), axis=2), axis=1)


def score_blocks(left_table, left_ids, right_table, right_ids, weights):
    count = left_ids.shape[0]
    block = math.gcd(count, 32)
    left_blocks = left_ids.reshape(count // block, block)
    right_blocks = right_ids.reshape(count // block, block)

    def one_block(pair_ids):
        return pair_scores(
            left_table[pair_ids[0]], right_table[pair_ids[1]], weights[0], weights[1], weights[2]
        )

    return lax.map(one_block, (left_blocks, right_blocks)).reshape(count)


def body(queries, index_videos, candidates, conv_one, conv_two, conv_three):
    devices = lax.axis_size("shard")
    q_dev = queries.shape[0]
    k_count = candidates.shape[1]
    idx_dev = index_videos.shape[0]
    frames = queries.shape[1]
    width = queries.shape[2]
    pairs = q_dev * k_count
    cap = max(2, (2 * pairs + devices - 1) // devices)
    weights = (conv_one, conv_two, conv_three)
    flat = candidates.reshape(pairs)
    holder = flat // idx_dev
    local = flat % idx_dev
    onehot = (holder[:, None] == jnp.arange(devices, dtype=jnp.int32)[None, :]).astype(jnp.int32)
    before = jnp.cumsum(onehot, axis=0) - onehot
    rank = jnp.sum(before * onehot, axis=1)
    slot = holder * cap + rank
    pair_query = jnp.arange(pairs) // k_count
    wanted = jnp.zeros((devices * cap,), jnp.int32).at[slot].set(local).reshape(devices, cap)
    rows = jnp.zeros((devices * cap, frames, width), jnp.bfloat16).at[slot].set(queries[pair_query])
    rows = rows.reshape(devices, cap, frames, width)
    got_rows = lax.all_to_all(rows, "shard", split_axis=0, concat_axis=0, tiled=True)
    received_ids = lax.all_to_all(wanted, "shard", split_axis=0, concat_axis=0, tiled=True)
    senders = got_rows.shape[0]
    items = got_rows.shape[1]
    table = got_rows.reshape(senders * items, frames, width)
    order = jnp.arange(senders * items, dtype=jnp.int32)
    result = score_blocks(
        table, order, index_videos, received_ids.reshape(senders * items), weights
    )
    scores_per_slot = result.reshape(senders, items)
    back = lax.all_to_all(scores_per_slot, "shard", split_axis=0, concat_axis=0, tiled=True)
    result = back.reshape(devices * cap)[slot]
    return result.reshape(q_dev, k_count)


def solution(mesh):
    placed = (P("shard", None, None), P("shard", None, None), P("shard", None), P(), P(), P())
    return jax.shard_map(
        body, mesh=mesh, in_specs=placed, out_specs=P("shard", None), check_vma=False
    )
```

profile of v0, /device:TPU:0, one launch (start us, length us, event | category | flops | bytes accessed | tf_op | source)
XLA Modules:
  0.0 1311.3 jit_solution(8537286979410029790)
XLA Ops:
  0.0 0.9 copy.21
  1.6 1.0 scatter_custom_fusion.1
  2.6 0.7 all_to_all.16
  3.2 7.3 all-to-all-start.1
  10.6 9.5 gather_fusion.2
  20.0 13.0 broadcast_in_dim.8
  33.1 47.2 %scatter_fusion = bf16[256,8,9600]{2,1,0:T(8,128)(2,1)} fusion(bf16[256,8,9600]{2,1,0:T(8,128)(2,1)} %broadcast_in_dim.8, s32[128]{0:T(128)S(1)} %fusion.9, bf16[128,8,9600]{2,1,0:T(8,128)(2,1)} %gather_fusion.2), kind=kCustom, calls=%fused_computation.4 | custom fusion | bytes 58982912 | tf_op jit(solution)/shard_map/scatter | solution.py:80
  80.3 6.2 all-to-all-start
  87.2 0.7 reduce.7
  88.0 877.8 %all-to-all-done = bf16[32,8,8,9600]{3,2,1,0:T(8,128)(2,1)} async-done(((bf16[32,8,8,9600]{3,2,1,0:T(8,128)(2,1)}), bf16[32,8,8,9600]{3,2,1,0:T(8,128)(2,1)}, u32[]{:S(2)}, u32[]{:S(2)}) %all-to-all-start) | async-done | bytes 39321632 | tf_op jit(solution)/shard_map/all_to_all | solution.py:82
  965.8 331.7 %while.10 = (s32[]{:T(128)}, f32[8,32]{1,0:T(8,128)S(1)}, bf16[1,64,3,3]{1,0,3,2:T(2,128)(2,1)S(1)}, s32[8,32]{1,0:T(8,128)S(1)}, bf16[256,8,9600]{2,1,0:T(8,128...) while((s32[]{:T(128)}, f32[8,32]{1,0:T(8,128)S(1)}, ...), condition=%wide.region_11.12_spmd, body=%wide.region_4.11_spmd.sunk | while | flops 211149248 | bytes 51030232 | solution.py:58
  965.8 5.6 gather_fusion
  971.4 9.0 reshape.361
  980.5 9.8 gather_fusion.1
  990.3 9.0 reshape.362
  999.3 5.4 convolution_multiply_fusion.2
  1006.1 0.8 convolution_maximum_fusion.5
  1007.3 5.6 gather_fusion
  1012.9 9.0 reshape.361
  1021.9 9.8 gather_fusion.1
  1031.7 9.0 reshape.362
  1040.8 5.4 convolution_multiply_fusion.2
  1047.6 0.8 convolution_maximum_fusion.5
  1048.7 5.6 gather_fusion
  1054.4 9.0 reshape.361
  1063.4 9.8 gather_fusion.1
  1073.2 9.0 reshape.362
  1082.2 5.4 convolution_multiply_fusion.2
  1089.1 0.8 convolution_maximum_fusion.5
  1090.2 5.6 gather_fusion
  1095.8 9.0 reshape.361
  1104.9 9.8 gather_fusion.1
  1114.7 9.0 reshape.362
  1123.7 5.4 convolution_multiply_fusion.2
  1130.5 0.8 convolution_maximum_fusion.5
  1131.6 5.6 gather_fusion
  1137.3 9.0 reshape.361
  1146.3 9.8 gather_fusion.1
  1156.1 9.0 reshape.362
  1165.1 5.4 convolution_multiply_fusion.2
  1172.0 0.8 convolution_maximum_fusion.5
  1173.1 5.6 gather_fusion
  1178.7 9.0 reshape.361
  1187.8 9.8 gather_fusion.1
  1197.6 9.0 reshape.362
  1206.6 5.4 convolution_multiply_fusion.2
  1213.4 0.8 convolution_maximum_fusion.5
  1214.6 5.6 gather_fusion
  1220.2 9.0 reshape.361
  1229.2 9.8 gather_fusion.1
  1239.0 9.0 reshape.362
  1248.1 5.4 convolution_multiply_fusion.2
  1254.9 0.8 convolution_maximum_fusion.5
  1256.0 5.6 gather_fusion
  1261.7 9.0 reshape.361
  1270.7 9.8 gather_fusion.1
  1280.5 9.0 reshape.362
  1289.5 5.4 convolution_multiply_fusion.2
  1296.4 0.8 convolution_maximum_fusion.5
  1298.1 2.7 all-to-all-start.2
  1300.8 7.1 all-to-all-done.2
  1308.5 0.7 reduce.8
  1309.3 1.3 gather_fusion.3
  1310.6 0.7 copy.27
  (159 shorter events, 16.1 us)
Async XLA Ops:
  0.0 10.6 copy-start
  3.2 77.1 %all-to-all-start.1 = ((s32[32,1,8]{2,1,0:T(1,128)}), s32[32,1,8]{2,1,0:T(1,128)S(1)}, u32[]{:S(2)}, u32[]{:S(2)}) async-start(s32[32,1,8]{2,1,0:T(1,128)} %bitcast.13), calls=%async_computation.1 | async-start | bytes 32768 | tf_op jit(solution)/shard_map/all_to_all | solution.py:83
  80.3 6.2 copy-start.3
  80.3 6.3 copy-start.4
  80.3 885.5 %copy-start.2 = (bf16[64,32,3,3]{0,1,3,2:T(8,128)(2,1)S(1)}, bf16[64,32,3,3]{0,1,3,2:T(8,128)(2,1)}, u32[]{:S(2)}) copy-start(bf16[64,32,3,3]{0,1,3,2:T(8,128)(2,1)} %param.12) | copy-start | bytes 110596
  80.3 885.5 %all-to-all-start = ((bf16[32,8,8,9600]{3,2,1,0:T(8,128)(2,1)}), bf16[32,8,8,9600]{3,2,1,0:T(8,128)(2,1)}, u32[]{:S(2)}, u32[]{:S(2)}) async-start(bf16[32,8,8,9600]{3,2,1,0:T(8,128)(2,1)} %bitcast.61), calls=%async_computation | async-start | bytes 78643200 | tf_op jit(solution)/shard_map/all_to_all | solution.py:82
  1297.4 13.9 %copy-start.1 = (bf16[16,8,9600]{2,1,0:T(8,128)(2,1)S(1)}, bf16[16,8,9600]{2,1,0:T(8,128)(2,1)}, u32[]{:S(2)}) copy-start(bf16[16,8,9600]{2,1,0:T(8,128)(2,1)} %param.8) | copy-start | bytes 7372804
  1298.1 9.9 all-to-all-start.2
where the time goes:
time: 1320 us; the launch traced here: 1310 us
  waiting for transfers between devices  885 us (67%)
  local copies, waits for them, and re-layouts  348 us (26%)
  matrix products  53.9 us (4%)
  starting transfers between devices  16.2 us (1%)
    all_to_all x1, waiting for transfers between devices, body(): lax.all_to_all(rows, 'shard', split_axis=0, concat_axis=0, tiled=True)  878 us
    gather x8, local copies, waits for them, and re-layouts, one_block(): right_table[pair_ids[1]]  78.4 us
    reshape x8, local copies, waits for them, and re-layouts, pair_scores(): left_region_features = left.reshape(count, F * R, REGION_FEATURES)  72.3 us
    reshape x8, local copies, waits for them, and re-layouts, pair_scores(): right_region_features = right.reshape(count, F * R, REGION_FEATURES)  72.1 us
    scatter x1, local copies, waits for them, and re-layouts, body(): jnp.zeros((devices * cap, frames, width), jnp.bfloat16).at[slot]  47.2 us
    gather x8, local copies, waits for them, and re-layouts, one_block(): left_table[pair_ids[0]]  45.1 us
    dot_general x8, matrix products, pair_scores(): jnp.einsum('avs,afs->avf', left_region_features, right_region_features, p...  43.2 us
  transfers between devices with their start and end apart: 3, of which 2 were waited for; matrix products, arithmetic and copies ran while one was open for 5% of the time, Pallas kernels for 0%

commit v1 on v0

v1 whole, which is shorter than its diff:
```python
import functools
import math

import jax
import jax.numpy as jnp
import numpy as np
from jax import lax
from jax.experimental import pallas as pl
from jax.experimental.pallas import tpu as pltpu
from jax.sharding import PartitionSpec as P

R = 5
GROUP = 16
NONE = 1 << 30


def shifts(size):
    k, i, y = np.meshgrid(np.arange(3), np.arange(size), np.arange(size), indexing="ij")
    return (i == y + k - 1).astype(np.float32)


def conv_matrix(w, size):
    s = jnp.asarray(shifts(size), jnp.bfloat16)
    half = jnp.einsum("ockl,kiy->oclyi", w, s, preferred_element_type=jnp.float32).astype(jnp.bfloat16)
    full = jnp.einsum("oclyi,ljx->cijoyx", half, s, preferred_element_type=jnp.float32)
    return full.astype(jnp.bfloat16)


def pooled_matrix(w, size):
    m = conv_matrix(w, size)
    c, _, _, o, _, _ = m.shape
    m = m.reshape(c, size, size, o, size // 2, 2, size // 2, 2)
    m = m.transpose(0, 1, 2, 5, 7, 3, 4, 6)
    return m.reshape(c * size * size, o * size * size)


def head_matrices(conv_one, conv_two, conv_three):
    one = pooled_matrix(conv_one, 8)
    two = pooled_matrix(conv_two, 4)
    three = conv_matrix(conv_three, 2)[:, :, :, 0]
    c = three.shape[0]
    three = jnp.swapaxes(three.reshape(c * 4, 2, 2), 1, 2)
    three = jnp.pad(three, ((0, 0), (0, 0), (0, 126))).reshape(c * 4, 256)
    return one, two, three


def dot(a, b):
    return jnp.dot(a, b, preferred_element_type=jnp.float32)


def pair_kernel(frames, senders, group, scale, rows_ref, vids_ref, count_ref, entry_ref,
                one_ref, two_ref, three_ref, q_hbm, own_hbm, other_hbm, out_ref,
                q_in, v_in, q_rows, v_rows, maps, q_sem, v_sem):
    idx_dev = own_hbm.shape[0]
    width = q_hbm.shape[2] // R
    side = group * frames
    count = count_ref[0]
    groups = (count + group - 1) // group

    def fetch(step, slot):
        def one_pair(p, _):
            row = rows_ref[step * group + p]
            vid = vids_ref[step * group + p]
            pltpu.make_async_copy(q_hbm.at[row], q_in.at[slot, p], q_sem.at[slot]).start()

            @pl.when(vid < idx_dev)
            def _():
                pltpu.make_async_copy(own_hbm.at[vid], v_in.at[slot, p], v_sem.at[slot]).start()

            @pl.when(vid >= idx_dev)
            def _():
                pltpu.make_async_copy(
                    other_hbm.at[vid - idx_dev], v_in.at[slot, p], v_sem.at[slot]
                ).start()
            return 0
        lax.fori_loop(0, group, one_pair, 0)

    row_id = lax.broadcasted_iota(jnp.int32, (side, side), 0)
    col_id = lax.broadcasted_iota(jnp.int32, (side, side), 1)
    same_pair = row_id // frames == col_id // frames
    cells = frames * frames
    lane = lax.broadcasted_iota(jnp.int32, (side, cells), 1)
    sub = lax.broadcasted_iota(jnp.int32, (side, cells), 0)
    spread = (lane % frames == sub % frames).astype(jnp.bfloat16)
    own_frame = lane // frames == sub % frames
    fold = (
        lax.broadcasted_iota(jnp.int32, (group, side), 1) // frames
        == lax.broadcasted_iota(jnp.int32, (group, side), 0)
    ).astype(jnp.bfloat16)

    maps[...] = jnp.zeros_like(maps)

    @pl.when(groups > 0)
    def _():
        fetch(0, 0)

    def step(g, _):
        slot = lax.rem(g, 2)

        @pl.when(g + 1 < groups)
        def _():
            fetch(g + 1, 1 - slot)

        pltpu.make_async_copy(q_in.at[slot], q_in.at[slot], q_sem.at[slot]).wait()
        pltpu.make_async_copy(v_in.at[slot], v_in.at[slot], v_sem.at[slot]).wait()
        for r in range(R):
            cols = pl.ds(r * width, width)
            q_rows[pl.ds(r * side, side), :] = q_in[slot, :, :, cols].reshape(side, width)
            v_rows[pl.ds(r * side, side), :] = v_in[slot, :, :, cols].reshape(side, width)
        total = jnp.zeros((side, side), jnp.float32)
        for r in range(R):
            sim = lax.dot_general(
                q_rows[pl.ds(r * side, side), :], v_rows[...], (((1,), (1,)), ((), ())),
                preferred_element_type=jnp.float32,
            )
            best = sim[:, :side]
            for s in range(1, R):
                best = jnp.maximum(best, sim[:, s * side:(s + 1) * side])
            total = total + best
        mean = jnp.where(same_pair, total * scale, 0.0).astype(jnp.bfloat16)
        wide = jnp.where(own_frame, dot(mean, spread), 0.0).astype(jnp.bfloat16)
        maps[pl.ds(pl.multiple_of(g * group, group), group), :] = dot(fold, wide)
        return 0

    lax.fori_loop(0, groups, step, 0)

    def pooled(x, parts):
        n = x.shape[1] // parts
        best = x[:, :n]
        for i in range(1, parts):
            best = jnp.maximum(best, x[:, i * n:(i + 1) * n])
        return jnp.maximum(best, 0.0).astype(jnp.bfloat16)

    first = pooled(dot(maps[...].astype(jnp.bfloat16), one_ref[...]), 4)
    second = pooled(dot(first, two_ref[...]), 4)
    final = jnp.clip(dot(second, three_ref[...]), -1.0, 1.0)
    best = jnp.maximum(final[:, :128], final[:, 128:])
    score = (best[:, 0:1] + best[:, 1:2]) * 0.5
    pairs = out_ref.shape[1]
    place = lax.broadcasted_iota(jnp.int32, (score.shape[0], pairs), 1)
    for s in range(senders):
        hit = entry_ref[...] == place + s * pairs
        out_ref[pl.ds(s, 1), :] = jnp.sum(jnp.where(hit, score, 0.0), axis=0, keepdims=True)


def pair_scores(gathered, own, other, rows, vids, count, entry, heads, senders, pairs):
    frames, width = gathered.shape[1], gathered.shape[2]
    cap = rows.shape[0]
    side = GROUP * frames
    scale = 1.0 / (math.sqrt(width // R) * R)
    smem = pl.BlockSpec(memory_space=pltpu.SMEM)
    vmem = pl.BlockSpec(memory_space=pltpu.VMEM)
    hbm = pl.BlockSpec(memory_space=pl.ANY)
    return pl.pallas_call(
        functools.partial(pair_kernel, frames, senders, GROUP, scale),
        out_shape=jax.ShapeDtypeStruct((senders, pairs), jnp.float32),
        in_specs=[smem, smem, smem, vmem, vmem, vmem, vmem, hbm, hbm, hbm],
        out_specs=vmem,
        scratch_shapes=[
            pltpu.VMEM((2, GROUP, frames, width), jnp.bfloat16),
            pltpu.VMEM((2, GROUP, frames, width), jnp.bfloat16),
            pltpu.VMEM((R * side, width // R), jnp.bfloat16),
            pltpu.VMEM((R * side, width // R), jnp.bfloat16),
            pltpu.VMEM((cap, frames * frames), jnp.float32),
            pltpu.SemaphoreType.DMA((2,)),
            pltpu.SemaphoreType.DMA((2,)),
        ],
        compiler_params=pltpu.CompilerParams(vmem_limit_bytes=48 * 1024 * 1024),
        cost_estimate=pl.CostEstimate(
            flops=2 * cap * side * R * R * frames * (width // R),
            bytes_accessed=cap * frames * width * 4, transcendentals=0,
        ),
        name="pair_scores",
    )(rows, vids, count, entry, *heads, gathered, own, other)


def body(queries, index_videos, candidates, conv_one, conv_two, conv_three):
    devices = lax.axis_size("shard")
    q_dev, frames, width = queries.shape
    k_count = candidates.shape[1]
    idx_dev = index_videos.shape[0]
    pairs = q_dev * k_count
    chips = devices // 2
    per_holder = max(2, (2 * pairs + devices - 1) // devices)
    cap = chips * 2 * per_holder
    me = lax.axis_index("shard")
    chip, core = me // 2, me % 2
    same_core = [[2 * i + c for i in range(chips)] for c in range(2)]

    ids = lax.all_gather(
        candidates.reshape(1, pairs), "shard", axis=0, tiled=True, axis_index_groups=same_core
    )
    gathered = lax.all_gather(
        queries, "shard", axis=0, tiled=True, axis_index_groups=same_core
    )
    other = lax.ppermute(index_videos, "shard", [(d, d ^ 1) for d in range(devices)])

    flat = ids.reshape(chips * pairs)
    mine = flat // (2 * idx_dev) == chip
    local = flat % (2 * idx_dev)
    local = jnp.where(local // idx_dev == core, local % idx_dev, local % idx_dev + idx_dev)
    entry = jnp.arange(chips * pairs, dtype=jnp.int32)
    code = jnp.where(mine, entry * (2 * idx_dev) + local, NONE)
    code = jnp.sort(code)[:cap]
    count = jnp.sum(mine.astype(jnp.int32)).reshape(1)
    valid = code < NONE
    entry = jnp.where(valid, code // (2 * idx_dev), NONE)
    rows = jnp.where(valid, entry // k_count, 0)
    vids = jnp.where(valid, code % (2 * idx_dev), 0)

    heads = head_matrices(conv_one, conv_two, conv_three)
    table = pair_scores(
        gathered, index_videos, other, rows, vids, count, entry.reshape(cap, 1), heads, chips, pairs
    )
    back = lax.all_to_all(
        table, "shard", split_axis=0, concat_axis=0, tiled=True, axis_index_groups=same_core
    )
    return jnp.sum(back, axis=0).reshape(q_dev, k_count)


def solution(mesh):
    placed = (P("shard", None, None), P("shard", None, None), P("shard", None), P(), P(), P())
    return jax.shard_map(
        body, mesh=mesh, in_specs=placed, out_specs=P("shard", None), check_vma=False
    )
```

time: 1320 us -> 492 us (0.37)
  waiting for transfers between devices: 885 us -> 244 us
  local copies, waits for them, and re-layouts: 348 us -> 116 us
  blocking collectives: 0 us -> 69.5 us
  matrix products: 53.9 us -> 3.97 us
  Pallas kernels: 0 us -> 39.1 us
  starting transfers between devices: 16.2 us -> 0.52 us
  between operations: 0.2 us -> 13.6 us
    all_to_all x3 -> x0, waiting for transfers between devices: 885 us -> none  [the longest x1 878 us: body(): lax.all_to_all(rows, 'shard', split_axis=0, concat_axis=0, tiled=True)]
    all_gather x0 -> x1, waiting for transfers between devices: none -> 243 us  [body(): lax.all_gather(queries, 'shard', axis=0, tiled=True, axis_index_groups=sa...]
    gather x18 -> x0, local copies, waits for them, and re-layouts: 134 us -> none  [the longest x8 78.4 us: one_block(): right_table[pair_ids[1]]]
    scatter x2 -> x0, local copies, waits for them, and re-layouts: 48.2 us -> none  [the longest x1 47.2 us: body(): jnp.zeros((devices * cap, frames, width), jnp.bfloat16).at[slot]]
    all_gather x0 -> x1, blocking collectives: none -> 42.3 us  [body(): lax.all_gather(candidates.reshape(1, pairs), 'shard', axis=0, tiled=True,...]
    dot_general x8 -> x6, matrix products: 43.2 us -> 3.97 us  [the longest x3 2.49 us: conv_matrix(): jnp.einsum('oclyi,ljx->cijoyx', half, s, preferred_element_type=jnp.float32)]
    pallas_call x0 -> x1, Pallas kernels: none -> 39.1 us  [pair_scores(): pl.pallas_call(functools.partial(pair_kernel, frames, senders, GROUP, sca...]
    reshape x29 -> x9, local copies, waits for them, and re-layouts: 146 us -> 114 us  [the longest x4 69.8 us: pooled_matrix(): return m.reshape(c * size * size, o * size * size)]
  transfers between devices with their start and end apart: 3 -> 2, of which waited for: 2 -> 1; matrix products, arithmetic and copies ran while one was open for 5% -> 25% of each run, Pallas kernels for 0% -> 0%
where the time goes in v1:
time: 492 us
  waiting for transfers between devices  244 us (50%)
  local copies, waits for them, and re-layouts  116 us (24%)
  blocking collectives  69.5 us (14%)
  Pallas kernels  39.1 us (8%)
  between operations  13.6 us (3%)
  other arithmetic  5.75 us (1%)
    all_gather x1, waiting for transfers between devices, body(): lax.all_gather(queries, 'shard', axis=0, tiled=True, axis_index_groups=sa...  243 us
    reshape x4, local copies, waits for them, and re-layouts, pooled_matrix(): return m.reshape(c * size * size, o * size * size)  69.8 us
    reshape x2, local copies, waits for them, and re-layouts, pooled_matrix(): m = m.reshape(c, size, size, o, size // 2, 2, size // 2, 2)  43.7 us
    all_gather x1, blocking collectives, body(): lax.all_gather(candidates.reshape(1, pairs), 'shard', axis=0, tiled=True,...  42.3 us
    pallas_call x1, Pallas kernels, pair_scores(): pl.pallas_call(functools.partial(pair_kernel, frames, senders, GROUP, sca...  39.1 us
    all_to_all x1, blocking collectives, body(): lax.all_to_all(table, 'shard', split_axis=0, concat_axis=0, tiled=True, a...  27.2 us
  transfers between devices with their start and end apart: 2, of which 1 were waited for; matrix products, arithmetic and copies ran while one was open for 25% of the time, Pallas kernels for 0%

profile of v1, /device:TPU:0, one launch (start us, length us, event | category | flops | bytes accessed | tf_op | source)
XLA Modules:
  0.0 492.1 jit_solution(1170175115822084605)
XLA Ops:
  6.5 0.0 all-gather.3.cloned.1.call-start
  6.5 0.7 all-gather.3.cloned.1.call-update
  7.3 0.5 collective-permute-start
  7.8 0.8 copy.31
  8.5 0.1 reshape.66
  8.6 42.3 %all-gather = s32[16,1,128]{2,1,0:T(1,128)S(1)} all-gather(s32[1,1,128]{2,1,0:T(1,128)S(1)} %reshape.66), channel_id=1, replica_groups={{0,2,4,6,8,10,12,14,16,18,20,22,24,26,28,30},{1,3,5,7,9,11,13,15,17,19,..., dimensions={0}, use_global_device_ids=true | all-gather | bytes 8704 | tf_op jit(solution)/shard_map/all_gather | solution.py:190
  51.0 5.0 %sort.15 = (s32[2048]{0:T(1024)S(1)}, s32[2048]{0:T(1024)}) sort(s32[2048]{0:T(1024)S(1)} %fusion.11, s32[2048]{0:T(1024)S(1)} %iota.7), dimensions={0}, to_apply=%region_0.1 | sort | flops 22528 | bytes 32768 | tf_op jit(solution)/shard_map/jit(sort)/sort | solution.py:204
  56.1 0.1 copy.42.entry_ref
  56.2 1.2 fusion
  57.4 1.9 convolution_convert_fusion
  59.3 36.0 %copy.37 = bf16[32,4,4,64,2,2,2,2]{2,1,0,6,4,3,7,5:T(4,128)(2,1)} copy(bf16[32,4,4,64,2,2,2,2]{3,7,6,2,1,5,4,0:T(2,128)(2,1)S(1)} %bitcast.97) | data formatting | bytes 2097152 | tf_op jit(solution)/shard_map/reshape | solution.py:32
  95.3 0.0 copy-start.1
  95.3 0.0 copy-start.2
  95.3 0.0 copy-start
  95.3 64.0 %reshape.61 = bf16[512,1024]{0,1:T(8,128)(2,1)S(1)} reshape(bf16[32,4,4,2,2,64,2,2]{2,1,0,7,6,5,4,3:T(4,128)(2,1)} %bitcast.95) | data formatting | bytes 2097152 | tf_op jit(solution)/shard_map/reshape | solution.py:34
  159.2 0.5 copy.44.two_ref
  159.8 0.0 copy-done.1
  159.8 0.0 copy-done.2
  159.8 0.2 fusion.1
  160.0 0.0 copy-done
  160.0 0.5 convolution_convert_fusion.1
  160.5 0.0 copy-start.3
  160.5 0.0 copy-start.5
  160.5 0.0 copy-start.4
  160.5 7.7 %copy.34 = bf16[1,8,8,32,4,2,4,2]{2,1,6,4,3,7,5,0:T(8,128)(2,1)} copy(bf16[1,8,8,32,4,2,4,2]{3,7,6,2,1,5,4,0:T(2,128)(2,1)S(1)} %bitcast.98) | data formatting | bytes 524288 | tf_op jit(solution)/shard_map/reshape | solution.py:32
  168.2 5.1 %reshape.59 = bf16[64,2048]{0,1:T(8,128)(2,1)S(1)} reshape(bf16[1,8,8,2,2,32,4,4]{2,1,7,6,5,4,3,0:T(8,128)(2,1)} %bitcast.96) | data formatting | bytes 524288 | tf_op jit(solution)/shard_map/reshape | solution.py:34
  173.3 0.2 copy.43.one_ref
  173.5 0.0 copy-done.3
  173.5 0.0 copy-done.5
  173.5 0.1 fusion.3
  173.7 0.0 copy-done.4
  173.7 0.1 fusion.2
  173.8 0.2 copy.40
  173.9 0.2 reshape_squeeze.3
  174.1 0.2 copy.62
  174.3 0.1 pad.4.clone
  174.5 0.6 convert_reduce_fusion
  175.1 0.0 collective-permute-done.other_hbm
  175.1 243.1 %all-gather.3.cloned.1.call-done.q_hbm = bf16[256,8,9600]{2,1,0:T(8,128)(2,1)} async-done(((bf16[16,8,9600]{2,1,0:T(8,128)(2,1)}), bf16[256,8,9600]{2,1,0:T(8,128)(2,1)}) %all-gather.3.cloned.1.call-update) | async-done | bytes 39321616 | tf_op jit(solution)/shard_map/all_gather | solution.py:193
  418.3 39.1 %pair_scores.1 = f32[16,128]{1,0:T(8,128)S(1)} custom-call(s32[256]{0:T(256)S(1)} %get-tuple-element.8.rows_ref, s32[256]{0:T(256)S(1)} %get-tuple-element.10.vids_ref, s32[1]{0:T(128)} %bitcast.2.count_ref, s32[256,1]{1,0:T(8,128)S(1)} %copy.42.entry_ref, bf16[64,2048]{1,0:T(8,128)(2,1)S(1)} %copy.43.one_ref, bf16[512,1024]{1,0:T(8,128)(2,1)S(1)} %copy.44.two_ref, ...), custom_call_target="tpu_custom_call" | custom-call | flops 25165824000 | bytes 78643200 | tf_op jit(solution)/shard_map/pair_scores/pallas_call | solution.py:154
  457.3 27.2 %all_to_all.9 = f32[16,1,128]{2,1,0:T(1,128)S(1)} all-to-all(f32[16,1,128]{2,1,0:T(1,128)S(1)} %bitcast.94), channel_id=1, replica_groups={{0,2,4,6,8,10,12,14,16,18,20,22,24,26,28,30},{1,3,5,7,9,11,13,15,17,19,..., dimensions={0} | all-to-all | bytes 16384 | tf_op jit(solution)/shard_map/all_to_all | solution.py:215
  484.5 0.1 reshape.65
  484.6 0.7 copy.46
  (5 shorter events, 0.1 us)
Async XLA Ops:
  6.5 411.7 %all-gather.3.cloned.1.call-start = ((), (), s32[]{:S(2)}) async-start(), calls=%async_computation.1 | async-start | bytes 41779200 | tf_op jit(solution)/shard_map/all_gather | solution.py:193
  7.3 167.9 %collective-permute-start = (bf16[128,8,9600]{2,1,0:T(8,128)(2,1)}, bf16[128,8,9600]{2,1,0:T(8,128)(2,1)}, u32[]{:S(2)}, u32[]{:S(2)}) collective-permute-start(bf16[128,8,9600]{2,1,0:T(8,128)(2,1)} %own_hbm.1), channel_id=1, source_target_pairs={{0,1},{1,0},{2,3},{3,2},{4,5},{5,4},{6,7},{7,6},{8,9},{9,8},{10,11... | collective-permute-start | bytes 58982408 | tf_op jit(solution)/shard_map/ppermute | solution.py:196
  95.3 64.5 %copy-start.1 = (bf16[3,8,8,1]{2,0,3,1:T(4,128)(2,1)S(1)}, bf16[3,8,8,1]{2,0,3,1:T(4,128)(2,1)}, u32[]{:S(2)}) copy-start(bf16[3,8,8,1]{2,0,3,1:T(4,128)(2,1)} %constant.126) | copy-start | bytes 1156
  95.3 64.5 %copy-start.2 = (bf16[32,1,3,3]{0,3,2,1:T(4,128)(2,1)S(1)}, bf16[32,1,3,3]{0,3,2,1:T(4,128)(2,1)}, u32[]{:S(2)}) copy-start(bf16[32,1,3,3]{0,3,2,1:T(4,128)(2,1)} %param.12) | copy-start | bytes 1732
  95.3 64.7 %copy-start = (bf16[3,8,8,1,1]{2,0,1,4,3:T(4,128)(2,1)S(1)}, bf16[3,8,8,1,1]{2,0,1,4,3:T(4,128)(2,1)}, u32[]{:S(2)}) copy-start(bf16[3,8,8,1,1]{2,0,1,4,3:T(4,128)(2,1)} %constant.127) | copy-start | bytes 1156
  160.5 13.0 %copy-start.3 = (bf16[1,64,3,3]{1,3,2,0:T(4,128)(2,1)S(1)}, bf16[1,64,3,3]{1,3,2,0:T(4,128)(2,1)}, u32[]{:S(2)}) copy-start(bf16[1,64,3,3]{1,3,2,0:T(4,128)(2,1)} %param.14) | copy-start | bytes 3460
  160.5 13.0 %copy-start.5 = (bf16[3,2,2,1]{0,2,3,1:T(2,128)(2,1)S(1)}, bf16[3,2,2,1]{0,2,3,1:T(2,128)(2,1)}, u32[]{:S(2)}) copy-start(bf16[3,2,2,1]{0,2,3,1:T(2,128)(2,1)} %constant.130) | copy-start | bytes 76
  160.5 13.2 %copy-start.4 = (bf16[3,2,2,1,1]{0,2,1,4,3:T(2,128)(2,1)S(1)}, bf16[3,2,2,1,1]{0,2,1,4,3:T(2,128)(2,1)}, u32[]{:S(2)}) copy-start(bf16[3,2,2,1,1]{0,2,1,4,3:T(2,128)(2,1)} %constant.131) | copy-start | bytes 76
Sparse Core Ops, SparseCore 0:
  10.2 408.0 all-gather.2

commit v2 on v1

v2 whole, which is shorter than its diff:
```python
import functools
import math

import jax
import jax.numpy as jnp
import numpy as np
from jax import lax
from jax.experimental import pallas as pl
from jax.experimental.pallas import tpu as pltpu
from jax.sharding import PartitionSpec as P

R = 5
GROUP = 16
NONE = 1 << 30
ROUTES = (("zxy", 8), ("zyx", 8))


def dot(a, b):
    return jnp.dot(a, b, preferred_element_type=jnp.float32)


def iota(shape, dim):
    return lax.broadcasted_iota(jnp.int32, shape, dim)


def head_kernel(one_w, two_w, three_w, one_ref, two_ref, three_ref, one_acc, two_acc, three_acc):
    one_acc[...] = jnp.zeros_like(one_acc)
    two_acc[...] = jnp.zeros_like(two_acc)
    three_acc[...] = jnp.zeros_like(three_acc)
    c1, c2 = two_w.shape[1], two_w.shape[2]
    b1, b2 = c1.bit_length() - 1, c2.bit_length() - 1

    def tap(t, _):
        k = lax.div(t, 3) - 1
        l = lax.rem(t, 3) - 1

        n = one_acc.shape[1]
        row, col = iota((64, n), 0), iota((64, n), 1) >> b1
        y = ((col >> 2) & 3) * 2 + ((col >> 5) & 1)
        x = (col & 3) * 2 + ((col >> 4) & 1)
        hit = ((row >> 3) == y + k) & ((row & 7) == x + l)
        spread = ((iota((c1, n), 1) & (c1 - 1)) == iota((c1, n), 0)).astype(jnp.bfloat16)
        val = dot(jnp.broadcast_to(one_w[t], (16, c1)), spread)[:1]
        one_acc[...] = jnp.where(hit, val, one_acc[...])

        n = two_acc.shape[1]
        spread = ((iota((c2, n), 1) & (c2 - 1)) == iota((c2, n), 0)).astype(jnp.bfloat16)
        val = dot(two_w[t], spread)

        def cell(ij, _):
            col = iota((c1, n), 1) >> b2
            y = ((col >> 1) & 1) * 2 + ((col >> 3) & 1)
            x = (col & 1) * 2 + ((col >> 2) & 1)
            hit = (lax.div(ij, 4) == y + k) & (lax.rem(ij, 4) == x + l)
            rows = pl.ds(pl.multiple_of(ij * c1, c1), c1)
            two_acc[rows, :] = jnp.where(hit, val, two_acc[rows, :])
            return 0
        lax.fori_loop(0, 16, cell, 0)

        m, n = three_acc.shape
        pick = ((iota((m, c2), 0) & (c2 - 1)) == iota((m, c2), 1)).astype(jnp.bfloat16)
        val = lax.dot_general(
            pick, jnp.broadcast_to(three_w[t], (128, c2)), (((1,), (1,)), ((), ())),
            preferred_element_type=jnp.float32,
        )[:, :1]
        row, col = iota((m, n), 0) >> b2, iota((m, n), 1)
        y, x = col & 127, col >> 7
        hit = ((row >> 1) == y + k) & ((row & 1) == x + l) & (y < 2)
        three_acc[...] = jnp.where(hit, val, three_acc[...])
        return 0

    lax.fori_loop(0, 9, tap, 0)
    one_ref[...] = one_acc[...].astype(jnp.bfloat16)
    two_ref[...] = two_acc[...].astype(jnp.bfloat16)
    three_ref[...] = three_acc[...].astype(jnp.bfloat16)


def head_matrices(conv_one, conv_two, conv_three):
    c1, c2 = conv_two.shape[1], conv_two.shape[0]
    one_w = conv_one.transpose(2, 3, 1, 0).reshape(9, 1, c1)
    two_w = conv_two.transpose(2, 3, 1, 0).reshape(9, c1, c2)
    three_w = conv_three.transpose(2, 3, 0, 1).reshape(9, 1, c2)
    shapes = [(64, 64 * c1), (16 * c1, 16 * c2), (4 * c2, 256)]
    vmem = pl.BlockSpec(memory_space=pltpu.VMEM)
    return pl.pallas_call(
        head_kernel,
        out_shape=[jax.ShapeDtypeStruct(s, jnp.bfloat16) for s in shapes],
        in_specs=[vmem] * 3,
        out_specs=[vmem] * 3,
        scratch_shapes=[pltpu.VMEM(s, jnp.float32) for s in shapes],
        compiler_params=pltpu.CompilerParams(vmem_limit_bytes=24 * 1024 * 1024),
        cost_estimate=pl.CostEstimate(flops=10**9, bytes_accessed=3 * 10**6, transcendentals=0),
        name="head_matrices",
    )(one_w, two_w, three_w)


def pair_kernel(frames, buffers, q_dev, scale, rows_ref, vids_ref, count_ref, entry_ref, one_ref,
                two_ref, three_ref, before_ref, own_hbm, other_hbm, *rest):
    q_hbm, rest = rest[:buffers], rest[buffers:]
    out_ref, q_in, v_in, q_rows, v_rows, maps, q_sem, v_sem = rest
    idx_dev = own_hbm.shape[0]
    width = own_hbm.shape[2] // R
    side = GROUP * frames
    count = count_ref[0]
    groups = (count + GROUP - 1) // GROUP

    def fetch(step, slot):
        def one_pair(p, _):
            row = rows_ref[step * GROUP + p]
            vid = vids_ref[step * GROUP + p]
            buf, row = lax.div(row, q_dev), lax.rem(row, q_dev)
            for b in range(buffers):
                @pl.when(buf == b)
                def _():
                    pltpu.make_async_copy(
                        q_hbm[b].at[row], q_in.at[slot, p], q_sem.at[slot]
                    ).start()

            @pl.when(vid < idx_dev)
            def _():
                pltpu.make_async_copy(own_hbm.at[vid], v_in.at[slot, p], v_sem.at[slot]).start()

            @pl.when(vid >= idx_dev)
            def _():
                pltpu.make_async_copy(
                    other_hbm.at[vid - idx_dev], v_in.at[slot, p], v_sem.at[slot]
                ).start()
            return 0
        lax.fori_loop(0, GROUP, one_pair, 0)

    maps[...] = jnp.zeros_like(maps)

    @pl.when(groups > 0)
    def _():
        fetch(0, 0)

    def step(g, _):
        slot = lax.rem(g, 2)

        @pl.when(g + 1 < groups)
        def _():
            fetch(g + 1, 1 - slot)

        pltpu.make_async_copy(q_in.at[slot], q_in.at[slot], q_sem.at[slot]).wait()
        pltpu.make_async_copy(v_in.at[slot], v_in.at[slot], v_sem.at[slot]).wait()
        for r in range(R):
            cols = pl.ds(r * width, width)
            q_rows[pl.ds(r * side, side), :] = q_in[slot, :, :, cols].reshape(side, width)
            v_rows[pl.ds(r * side, side), :] = v_in[slot, :, :, cols].reshape(side, width)

        def region(r, total):
            sim = lax.dot_general(
                q_rows[pl.ds(pl.multiple_of(r * side, side), side), :], v_rows[...],
                (((1,), (1,)), ((), ())), preferred_element_type=jnp.float32,
            )
            best = sim[:, :side]
            for s in range(1, R):
                best = jnp.maximum(best, sim[:, s * side:(s + 1) * side])
            return total + best

        total = lax.fori_loop(0, R, region, jnp.zeros((side, side), jnp.float32))
        cells = frames * frames
        same_pair = iota((side, side), 0) // frames == iota((side, side), 1) // frames
        lane, sub = iota((side, cells), 1), iota((side, cells), 0)
        spread = (lane % frames == sub % frames).astype(jnp.bfloat16)
        own_frame = lane // frames == sub % frames
        fold = (iota((GROUP, side), 1) // frames == iota((GROUP, side), 0)).astype(jnp.bfloat16)
        mean = jnp.where(same_pair, total * scale, 0.0).astype(jnp.bfloat16)
        wide = jnp.where(own_frame, dot(mean, spread), 0.0).astype(jnp.bfloat16)
        maps[pl.ds(pl.multiple_of(g * GROUP, GROUP), GROUP), :] = dot(fold, wide)
        return 0

    lax.fori_loop(0, groups, step, 0)

    def pooled(x):
        n = x.shape[1] // 4
        best = x[:, :n]
        for i in range(1, 4):
            best = jnp.maximum(best, x[:, i * n:(i + 1) * n])
        return jnp.maximum(best, 0.0).astype(jnp.bfloat16)

    first = pooled(dot(maps[...].astype(jnp.bfloat16), one_ref[...]))
    second = pooled(dot(first, two_ref[...]))
    final = jnp.clip(dot(second, three_ref[...]), -1.0, 1.0)
    best = jnp.maximum(final[:, :128], final[:, 128:])
    score = (best[:, 0:1] + best[:, 1:2]) * 0.5
    senders, pairs = out_ref.shape
    shape = (score.shape[0], pairs)
    score = jnp.broadcast_to(score, shape)
    place = jnp.broadcast_to(entry_ref[...], shape) - iota(shape, 1)
    for s in range(senders):
        out_ref[pl.ds(s, 1), :] = before_ref[pl.ds(s, 1), :] + jnp.sum(
            jnp.where(place == s * pairs, score, 0.0), axis=0, keepdims=True
        )


def pair_scores(blocks, own, other, rows, vids, count, entry, heads, before, q_dev, name):
    frames, width = own.shape[1], own.shape[2]
    cap = rows.shape[0]
    side = GROUP * frames
    scale = 1.0 / (math.sqrt(width // R) * R)
    smem = pl.BlockSpec(memory_space=pltpu.SMEM)
    vmem = pl.BlockSpec(memory_space=pltpu.VMEM)
    hbm = pl.BlockSpec(memory_space=pl.ANY)
    return pl.pallas_call(
        functools.partial(pair_kernel, frames, len(blocks), q_dev, scale),
        out_shape=jax.ShapeDtypeStruct(before.shape, jnp.float32),
        in_specs=[smem] * 3 + [vmem] * 5 + [hbm] * (2 + len(blocks)),
        out_specs=vmem,
        scratch_shapes=[
            pltpu.VMEM((2, GROUP, frames, width), jnp.bfloat16),
            pltpu.VMEM((2, GROUP, frames, width), jnp.bfloat16),
            pltpu.VMEM((R * side, width // R), jnp.bfloat16),
            pltpu.VMEM((R * side, width // R), jnp.bfloat16),
            pltpu.VMEM((cap, frames * frames), jnp.float32),
            pltpu.SemaphoreType.DMA((2,)),
            pltpu.SemaphoreType.DMA((2,)),
        ],
        compiler_params=pltpu.CompilerParams(vmem_limit_bytes=40 * 1024 * 1024),
        cost_estimate=pl.CostEstimate(
            flops=2 * cap * side * R * R * frames * (width // R),
            bytes_accessed=cap * frames * width * 4, transcendentals=0,
        ),
        name=name,
    )(rows, vids, count, entry, *heads, before, own, other, *blocks)


def chip_places(mesh):
    devices = list(mesh.devices.flat)[::2]
    places = [tuple(getattr(d, "coords", ()) or ()) for d in devices]
    if any(len(p) != 3 for p in places):
        return [(i, 0, 0) for i in range(len(devices))]
    return [tuple(reversed(p)) for p in places]


def ring_position(coordinate, size):
    if size <= 2:
        return coordinate
    order = list(range(1, size, 2)) + list(reversed(range(0, size, 2)))
    order = [0] + [c for c in order if c != 0]
    return order.index(coordinate)


def body(places, sizes, queries, index_videos, candidates, conv_one, conv_two, conv_three):
    devices = lax.axis_size("shard")
    q_dev, frames, width = queries.shape
    k_count = candidates.shape[1]
    idx_dev = index_videos.shape[0]
    pairs = q_dev * k_count
    chips = devices // 2
    per_holder = max(2, (2 * pairs + devices - 1) // devices)
    me = lax.axis_index("shard")
    chip, core = me // 2, me % 2
    same_core = [[2 * i + c for i in range(chips)] for c in range(2)]

    rings = [tuple(ring_position(c, n) for c, n in zip(p, sizes)) for p in places]
    where = {r: i for i, r in enumerate(rings)}
    offsets = [(z, y, x) for z in range(sizes[0]) for y in range(sizes[1]) for x in range(sizes[2])]
    back = np.array(
        [[where[tuple((r - o) % n for r, o, n in zip(ring, off, sizes))] for off in offsets]
         for ring in rings], np.int32,
    )

    def step_along(axis):
        out = []
        for i, ring in enumerate(rings):
            to = list(ring)
            to[axis] = (to[axis] + 1) % sizes[axis]
            out += [(2 * i + c, 2 * where[tuple(to)] + c) for c in range(2)]
        return out

    steps = [step_along(a) for a in range(3)]

    ids = lax.all_gather(
        candidates.reshape(1, pairs), "shard", axis=0, tiled=True, axis_index_groups=same_core
    )
    other = lax.ppermute(index_videos, "shard", [(d, d ^ 1) for d in range(devices)])

    parts = sum(n for _, n in ROUTES)
    starts, blocks = [], []
    start = 0
    for order, share in ROUTES:
        n = q_dev * share // parts
        have = {(0, 0, 0): queries[start:start + n]}
        for letter in order:
            axis = "zyx".index(letter)
            for off, block in list(have.items()):
                for k in range(1, sizes[axis]):
                    block = lax.ppermute(block, "shard", steps[axis])
                    off = off[:axis] + (k,) + off[axis + 1:]
                    have[off] = block
        starts.append(start)
        blocks.append(have)
        start += n
    routes = len(ROUTES)

    plane = sizes[1] * sizes[2]
    offsets_of = [offsets[z * plane:(z + 1) * plane] for z in range(sizes[0])]
    phases = []
    for z in range(sizes[0]):
        every = [(i, r) for i in range(plane) for r in range(routes)]
        late = []
        if z == sizes[0] - 1 and sizes[0] > 1:
            late = [
                (i, r) for i, r in every
                if offsets_of[z][i]["zyx".index(ROUTES[r][0][-1])] == sizes["zyx".index(ROUTES[r][0][-1])] - 1
            ]
        phases.append((z, [e for e in every if e not in late]))
        if late:
            phases.append((z, late))

    senders = lax.dynamic_index_in_dim(jnp.asarray(back), chip, 0, keepdims=False)
    flat = jnp.take(ids, senders, axis=0).reshape(sizes[0], plane * pairs)
    flat = jnp.take(flat, np.array([z for z, _ in phases]), axis=0)
    pos = np.arange(plane * pairs, dtype=np.int32)
    pair = pos % pairs
    route = np.sum(np.array(starts)[None, :] <= (pair // k_count)[:, None], axis=1) - 1
    inside = np.array(
        [[(int(p) // pairs, int(r)) in set(chosen) for p, r in zip(pos, route)]
         for _, chosen in phases], bool,
    )
    mine = (flat // (2 * idx_dev) == chip) & inside
    local = flat % (2 * idx_dev)
    local = jnp.where(local // idx_dev == core, local % idx_dev, local % idx_dev + idx_dev)
    code = jnp.where(mine, pos[None, :] * (2 * idx_dev) + local, NONE)
    cap = min(plane * 2 * per_holder, plane * pairs)
    cap = -(-cap // GROUP) * GROUP
    code = jnp.sort(code, axis=1)[:, :cap]
    count = jnp.sum(mine.astype(jnp.int32), axis=1)
    valid = code < NONE
    place = jnp.where(valid, code // (2 * idx_dev), 0)
    vids = jnp.where(valid, code % (2 * idx_dev), 0)
    number, pair = place // pairs, place % pairs
    query = pair // k_count
    sender = jnp.zeros_like(place)
    by_phase = senders.reshape(sizes[0], plane)[np.array([z for z, _ in phases])]
    for i in range(plane):
        sender = jnp.where(number == i, by_phase[:, i:i + 1], sender)
    entry = jnp.where(valid, sender * pairs + pair, NONE)
    rows = jnp.zeros_like(place)
    for p, (_, chosen) in enumerate(phases):
        for b, (i, r) in enumerate(chosen):
            end = starts[r + 1] if r + 1 < routes else q_dev
            hit = (number[p] == i) & (query[p] >= starts[r]) & (query[p] < end)
            rows = rows.at[p].set(
                jnp.where(hit & valid[p], b * q_dev + query[p] - starts[r], rows[p])
            )

    heads = head_matrices(conv_one, conv_two, conv_three)
    table = jnp.zeros((chips, pairs), jnp.float32)
    for p, (z, chosen) in enumerate(phases):
        table = pair_scores(
            [blocks[r][offsets_of[z][i]] for i, r in chosen], index_videos, other, rows[p], vids[p],
            count[p:p + 1], entry[p].reshape(cap, 1), heads, table, q_dev, "phase_" + str(p),
        )
    scores = lax.all_to_all(
        table, "shard", split_axis=0, concat_axis=0, tiled=True, axis_index_groups=same_core
    )
    return jnp.sum(scores, axis=0).reshape(q_dev, k_count)


def solution(mesh):
    places = chip_places(mesh)
    low = [min(p[a] for p in places) for a in range(3)]
    places = [tuple(c - m for c, m in zip(p, low)) for p in places]
    sizes = [max(p[a] for p in places) + 1 for a in range(3)]
    placed = (P("shard", None, None), P("shard", None, None), P("shard", None), P(), P(), P())
    return jax.shard_map(
        functools.partial(body, places, sizes), mesh=mesh, in_specs=placed,
        out_specs=P("shard", None), check_vma=False,
    )
```

time: 492 us -> 432 us (0.88)
  local copies, waits for them, and re-layouts: 116 us -> 24.7 us
  waiting for transfers between devices: 244 us -> 191 us
  Pallas kernels: 39.1 us -> 83 us
  starting transfers between devices: 0.52 us -> 30.8 us
  blocking collectives: 69.5 us -> 86.1 us
    all_gather x1 -> x0, waiting for transfers between devices: 243 us -> none  [body(): lax.all_gather(queries, 'shard', axis=0, tiled=True, axis_index_groups=sa...]
    ppermute x0 -> x30, waiting for transfers between devices: none -> 191 us  [body(): block = lax.ppermute(block, 'shard', steps[axis])]
    reshape x9 -> x4, local copies, waits for them, and re-layouts: 114 us -> 0.79 us  [the longest x2 0.76 us: body(): return jnp.sum(scores, axis=0).reshape(q_dev, k_count)]
    pallas_call x1 -> x6, Pallas kernels: 39.1 us -> 83 us  [the longest x5 74.4 us: pair_scores(): pl.pallas_call(functools.partial(pair_kernel, frames, len(blocks), q_dev,...]
    ppermute x0 -> x30, starting transfers between devices: none -> 30.3 us  [body(): block = lax.ppermute(block, 'shard', steps[axis])]
    unnamed x16 -> x56, local copies, waits for them, and re-layouts: 1.08 us -> 17.7 us
    all_gather x1, blocking collectives: 42.3 us -> 55.2 us  [body(): lax.all_gather(candidates.reshape(1, pairs), 'shard', axis=0, tiled=True,...]
    sort x1 -> x0, other arithmetic: 5.03 us -> none  [body(): code = jnp.sort(code)[:cap]]
  transfers between devices with their start and end apart: 2 -> 31, of which waited for: 1 -> 11; matrix products, arithmetic and copies ran while one was open for 25% -> 2% of each run, Pallas kernels for 0% -> 17%
where the time goes in v2:
time: 432 us
  waiting for transfers between devices  191 us (44%)
  blocking collectives  86.1 us (20%)
  Pallas kernels  83 us (19%)
  starting transfers between devices  30.8 us (7%)
  local copies, waits for them, and re-layouts  24.7 us (6%)
  between operations  13.8 us (3%)
    ppermute x30, waiting for transfers between devices, body(): block = lax.ppermute(block, 'shard', steps[axis])  191 us
    pallas_call x5, Pallas kernels, pair_scores(): pl.pallas_call(functools.partial(pair_kernel, frames, len(blocks), q_dev,...  74.4 us
    all_gather x1, blocking collectives, body(): lax.all_gather(candidates.reshape(1, pairs), 'shard', axis=0, tiled=True,...  55.2 us
    all_to_all x1, blocking collectives, body(): lax.all_to_all(table, 'shard', split_axis=0, concat_axis=0, tiled=True, a...  30.9 us
    ppermute x30, starting transfers between devices, body(): block = lax.ppermute(block, 'shard', steps[axis])  30.3 us
    unnamed x56, local copies, waits for them, and re-layouts  17.7 us
  transfers between devices with their start and end apart: 31, of which 11 were waited for; matrix products, arithmetic and copies ran while one was open for 2% of the time, Pallas kernels for 17%

profile of v2, /device:TPU:0, one launch (start us, length us, event | category | flops | bytes accessed | tf_op | source)
XLA Modules:
  0.0 432.4 jit_solution(3947059023544269951)
XLA Ops:
  6.6 0.5 collective-permute-start
  7.1 1.8 fusion.23
  8.9 2.6 collective-permute-start.1
  11.5 1.5 collective-permute-start.4
  13.0 0.5 collective-permute-start.2
  13.6 25.8 %collective-permute-done.1.rest_2_ = bf16[8,8,9600]{2,1,0:T(8,128)(2,1)S(1)} collective-permute-done((bf16[8,8,9600]{2,1,0:T(8,128)(2,1)S(1)}, bf16[8,8,9600]{2,1,0:T(8,128)(2,1)S(1)}, u32[]{:S(2)}, u32[]{:S(2)}) %collective-permute-start.1) | collective-permute-done | bytes 1228832 | tf_op jit(solution)/shard_map/ppermute | solution.py:289
  39.4 2.0 collective-permute-start.7
  41.4 1.0 copy-done
  42.5 2.6 collective-permute-start.8
  45.1 20.5 %collective-permute-done.2.rest_3_ = bf16[8,8,9600]{2,1,0:T(8,128)(2,1)S(1)} collective-permute-done((bf16[8,8,9600]{2,1,0:T(8,128)(2,1)S(1)}, bf16[8,8,9600]{2,1,0:T(8,128)(2,1)S(1)}, u32[]{:S(2)}, u32[]{:S(2)}) %collective-permute-start.2) | collective-permute-done | bytes 1228832 | tf_op jit(solution)/shard_map/ppermute | solution.py:289
  65.5 1.0 copy-done.10
  66.6 1.8 collective-permute-start.5
  68.3 1.1 copy-done.4
  69.4 1.0 copy-done.12
  70.4 1.5 collective-permute-start.6
  71.9 1.1 copy-done.6
  73.0 0.5 collective-permute-start.9
  73.6 21.8 %collective-permute-done.8.rest_1_ = bf16[8,8,9600]{2,1,0:T(8,128)(2,1)} collective-permute-done((bf16[8,8,9600]{2,1,0:T(8,128)(2,1)S(1)}, bf16[8,8,9600]{2,1,0:T(8,128)(2,1)}, u32[]{:S(2)}, u32[]{:S(2)}) %collective-permute-start.8) | collective-permute-done | bytes 1228832 | tf_op jit(solution)/shard_map/ppermute | solution.py:289
  95.4 1.6 collective-permute-start.12
  96.9 1.0 copy-done.14
  98.0 1.5 collective-permute-start.10
  99.5 0.9 collective-permute-done.6.rest_7_
  100.4 1.1 copy-done.16
  101.5 0.2 collective-permute-start.11
  101.7 25.0 %collective-permute-done.9.rest_2_ = bf16[8,8,9600]{2,1,0:T(8,128)(2,1)S(1)} collective-permute-done((bf16[8,8,9600]{2,1,0:T(8,128)(2,1)S(1)}, bf16[8,8,9600]{2,1,0:T(8,128)(2,1)S(1)}, u32[]{:S(2)}, u32[]{:S(2)}) %collective-permute-start.9) | collective-permute-done | bytes 1228832 | tf_op jit(solution)/shard_map/ppermute | solution.py:289
  126.7 1.6 collective-permute-start.15
  128.3 1.0 copy-done.2
  129.5 0.7 dynamic-slice_reduce_fusion
  130.2 55.2 %all-gather = s32[16,1,128]{2,1,0:T(1,128)S(1)} all-gather(s32[1,1,128]{2,1,0:T(1,128)S(1)} %reshape.1187), channel_id=1, replica_groups={{0,2,4,6,8,10,12,14,16,18,20,22,24,26,28,30},{1,3,5,7,9,11,13,15,17,19,..., dimensions={0}, use_global_device_ids=true | all-gather | bytes 8704 | tf_op jit(solution)/shard_map/all_gather | solution.py:274
  185.6 2.0 collective-permute-start.17
  187.6 0.7 fusion.17
  188.3 0.6 gather_fusion
  189.1 0.6 gather_fusion.1
  189.8 22.7 %collective-permute-done.16.rest_1_ = bf16[8,8,9600]{2,1,0:T(8,128)(2,1)} collective-permute-done((bf16[8,8,9600]{2,1,0:T(8,128)(2,1)}, bf16[8,8,9600]{2,1,0:T(8,128)(2,1)}, u32[]{:S(2)}, u32[]{:S(2)}) %collective-permute-start.16) | collective-permute-done | bytes 1228832 | tf_op jit(solution)/shard_map/ppermute | solution.py:289
  212.5 3.3 collective-permute-done.14.rest_7_
  215.9 26.2 %collective-permute-done.17.rest_2_ = bf16[8,8,9600]{2,1,0:T(8,128)(2,1)S(1)} collective-permute-done((bf16[8,8,9600]{2,1,0:T(8,128)(2,1)}, bf16[8,8,9600]{2,1,0:T(8,128)(2,1)S(1)}, u32[]{:S(2)}, u32[]{:S(2)}) %collective-permute-start.17) | collective-permute-done | bytes 1228832 | tf_op jit(solution)/shard_map/ppermute | solution.py:289
  242.1 0.7 fusion.3
  242.8 0.6 gather_fusion.2
  243.4 0.7 fusion.24
  244.3 8.5 %head_matrices.1 = (bf16[64,2048]{1,0:T(8,128)(2,1)S(1)}, bf16[512,1024]{1,0:T(8,128)(2,1)S(1)}, bf16[256,256]{1,0:T(8,128)(2,1)S(1)}) custom-call(bf16[9,1,32]{2,1,0:T(2,128)(2,1)S(1)} %reshape.1190.one_w, bf16[9,32,64]{2,1,0:T(8,128)(2,1)S(1)} %bitcast.52, bf16[9,1,64]{2,1,0:T(2,128)(2,1)S(1)} %reshape.1191.three_w), custom_call_target="tpu_custom_call" | custom-call | flops 1000000000 | bytes 3000000 | tf_op jit(solution)/shard_map/head_matrices/pallas_call | solution.py:85
  252.9 0.8 add_select_fusion.10
  253.7 0.7 fusion.11
  254.7 2.0 collective-permute-start.19
  256.7 7.6 %collective-permute-done.18.rest_3_ = bf16[8,8,9600]{2,1,0:T(8,128)(2,1)} collective-permute-done((bf16[8,8,9600]{2,1,0:T(8,128)(2,1)}, bf16[8,8,9600]{2,1,0:T(8,128)(2,1)}, u32[]{:S(2)}, u32[]{:S(2)}) %collective-permute-start.18) | collective-permute-done | bytes 1228832 | tf_op jit(solution)/shard_map/ppermute | solution.py:289
  264.3 2.7 collective-permute-start.21
  267.5 2.0 collective-permute-start.22
  269.9 1.3 copy-done.1
  271.2 1.3 copy-done.5
  272.5 1.3 copy-done.7
  273.8 1.3 copy-done.11
  275.1 1.3 copy-done.13
  276.4 1.3 copy-done.15
  277.7 1.3 copy-done.17
  279.0 19.6 %phase_0.1.before_ref = f32[16,128]{1,0:T(8,128)S(1)} custom-call(s32[64]{0:T(128)S(1)} %get-tuple-element.439.rows_ref, s32[64]{0:T(128)S(1)} %get-tuple-element.434.vids_ref, s32[1]{0:T(128)} %get-tuple-element.440.count_ref, s32[64,1]{1,0:T(8,128)S(1)} %copy.34.entry_ref, bf16[64,2048]{1,0:T(8,128)(2,1)S(1)} %get-tuple-element.392.one_ref, ...), custom_call_target="tpu_custom_call" | custom-call | flops 6291456000 | bytes 19660800 | tf_op jit(solution)/shard_map/phase_0/pallas_call | solution.py:205
  298.7 12.6 %collective-permute-done.21.rest_6_ = bf16[8,8,9600]{2,1,0:T(8,128)(2,1)} collective-permute-done((bf16[8,8,9600]{2,1,0:T(8,128)(2,1)}, bf16[8,8,9600]{2,1,0:T(8,128)(2,1)}, u32[]{:S(2)}, u32[]{:S(2)}) %collective-permute-start.21) | collective-permute-done | bytes 1228832 | tf_op jit(solution)/shard_map/ppermute | solution.py:289
  311.3 1.9 collective-permute-start.28
  313.4 24.3 %collective-permute-done.26.rest_3_ = bf16[8,8,9600]{2,1,0:T(8,128)(2,1)} collective-permute-done((bf16[8,8,9600]{2,1,0:T(8,128)(2,1)}, bf16[8,8,9600]{2,1,0:T(8,128)(2,1)}, u32[]{:S(2)}, u32[]{:S(2)}) %collective-permute-start.26) | collective-permute-done | bytes 1228832 | tf_op jit(solution)/shard_map/ppermute | solution.py:289
  337.7 1.2 collective-permute-start.30
  338.9 15.0 %phase_1.1.before_ref = f32[16,128]{1,0:T(8,128)S(1)} custom-call(s32[64]{0:T(128)S(1)} %bitcast.51, s32[64]{0:T(128)S(1)} %get-tuple-element.435.vids_ref, s32[1]{0:T(128)} %get-tuple-element.441.count_ref, s32[64,1]{1,0:T(8,128)S(1)} %copy.35.entry_ref, bf16[64,2048]{1,0:T(8,128)(2,1)S(1)} %get-tuple-element.392.one_ref, ...), custom_call_target="tpu_custom_call" | custom-call | flops 6291456000 | bytes 19660800 | tf_op jit(solution)/shard_map/phase_1/pallas_call | solution.py:205
  353.9 13.9 %phase_2.1.before_ref = f32[16,128]{1,0:T(8,128)S(1)} custom-call(s32[64]{0:T(128)S(1)} %get-tuple-element.426.rows_ref, s32[64]{0:T(128)S(1)} %get-tuple-element.436.vids_ref, s32[1]{0:T(128)} %get-tuple-element.442.count_ref, s32[64,1]{1,0:T(8,128)S(1)} %copy.36.entry_ref, bf16[64,2048]{1,0:T(8,128)(2,1)S(1)} %get-tuple-element.392.one_ref, ...), custom_call_target="tpu_custom_call" | custom-call | flops 6291456000 | bytes 19660800 | tf_op jit(solution)/shard_map/phase_2/pallas_call | solution.py:205
  367.8 14.8 %phase_3.1.before_ref = f32[16,128]{1,0:T(8,128)S(1)} custom-call(s32[64]{0:T(128)S(1)} %get-tuple-element.427.rows_ref, s32[64]{0:T(128)S(1)} %get-tuple-element.437.vids_ref, s32[1]{0:T(128)} %get-tuple-element.443.count_ref, s32[64,1]{1,0:T(8,128)S(1)} %copy.37.entry_ref, bf16[64,2048]{1,0:T(8,128)(2,1)S(1)} %get-tuple-element.392.one_ref, ...), custom_call_target="tpu_custom_call" | custom-call | flops 6291456000 | bytes 19660800 | tf_op jit(solution)/shard_map/phase_3/pallas_call | solution.py:205
  382.7 11.2 %phase_4.1 = f32[16,128]{1,0:T(8,128)S(1)} custom-call(s32[64]{0:T(128)S(1)} %get-tuple-element.428.rows_ref, s32[64]{0:T(128)S(1)} %get-tuple-element.438.vids_ref, s32[1]{0:T(128)} %get-tuple-element.444.count_ref, s32[64,1]{1,0:T(8,128)S(1)} %copy.38.entry_ref, bf16[64,2048]{1,0:T(8,128)(2,1)S(1)} %get-tuple-element.392.one_ref, ...), custom_call_target="tpu_custom_call" | custom-call | flops 6291456000 | bytes 19660800 | tf_op jit(solution)/shard_map/phase_4/pallas_call | solution.py:205
  393.9 30.9 %all_to_all.9 = f32[16,1,128]{2,1,0:T(1,128)S(1)} all-to-all(f32[16,1,128]{2,1,0:T(1,128)S(1)} %bitcast.50), channel_id=1, replica_groups={{0,2,4,6,8,10,12,14,16,18,20,22,24,26,28,30},{1,3,5,7,9,11,13,15,17,19,..., dimensions={0} | all-to-all | bytes 16384 | tf_op jit(solution)/shard_map/all_to_all | solution.py:356
  424.9 0.7 copy.40
  (114 shorter events, 2.6 us)
Async XLA Ops:
  6.5 182.4 %copy-start.25 = (s32[5]{0:T(128)S(1)}, s32[5]{0:T(128)}, u32[]{:S(2)}) copy-start(s32[5]{0:T(128)} %constant.915) | copy-start | bytes 64
  6.5 183.1 %copy-start.22 = (pred[5,512]{1,0:T(8,128)(4,1)S(1)}, pred[5,512]{1,0:T(8,128)(4,1)}, u32[]{:S(2)}) copy-start(pred[5,512]{1,0:T(8,128)(4,1)} %constant.897.clone) | copy-start | bytes 7684
  6.5 122.8 %copy-start.21 = (s32[16,8]{0,1:T(8,128)S(1)}, s32[16,8]{0,1:T(8,128)}, u32[]{:S(2)}) copy-start(s32[16,8]{0,1:T(8,128)} %param.78) | copy-start | bytes 1540
  6.5 236.8 %copy-start.23 = (bf16[32,1,3,3]{0,3,2,1:T(4,128)(2,1)S(1)}, bf16[32,1,3,3]{0,3,2,1:T(4,128)(2,1)}, u32[]{:S(2)}) copy-start(bf16[32,1,3,3]{0,3,2,1:T(4,128)(2,1)} %param.79) | copy-start | bytes 1732
  6.5 236.9 %copy-start.24 = (bf16[1,64,3,3]{1,3,2,0:T(4,128)(2,1)S(1)}, bf16[1,64,3,3]{1,3,2,0:T(4,128)(2,1)}, u32[]{:S(2)}) copy-start(bf16[1,64,3,3]{1,3,2,0:T(4,128)(2,1)} %param.81) | copy-start | bytes 3460
  6.5 237.8 %copy-start.20 = (bf16[64,32,3,3]{0,1,3,2:T(8,128)(2,1)S(1)}, bf16[64,32,3,3]{0,1,3,2:T(8,128)(2,1)}, u32[]{:S(2)}) copy-start(bf16[64,32,3,3]{0,1,3,2:T(8,128)(2,1)} %param.80) | copy-start | bytes 110596
  6.6 246.3 %sort.10.cloned.1.call-start = ((), (), s32[]{:S(2)}) async-start(), calls=%async_computation.1 | async-start | bytes 49184 | tf_op jit(solution)/shard_map/jit(sort)/sort | solution.py:328
  6.6 260.8 %collective-permute-start = (bf16[128,8,9600]{2,1,0:T(8,128)(2,1)}, bf16[128,8,9600]{2,1,0:T(8,128)(2,1)}, u32[]{:S(2)}, u32[]{:S(2)}) collective-permute-start(bf16[128,8,9600]{2,1,0:T(8,128)(2,1)} %own_hbm.9), channel_id=1, source_target_pairs={{0,1},{1,0},{2,3},{3,2},{4,5},{5,4},{6,7},{7,6},{8,9},{9,8},{10,11... | collective-permute-start | bytes 58982408 | tf_op jit(solution)/shard_map/ppermute | solution.py:277
  8.9 30.4 %collective-permute-start.1 = (bf16[8,8,9600]{2,1,0:T(8,128)(2,1)S(1)}, bf16[8,8,9600]{2,1,0:T(8,128)(2,1)S(1)}, u32[]{:S(2)}, u32[]{:S(2)}) collective-permute-start(bf16[8,8,9600]{2,1,0:T(8,128)(2,1)S(1)} %get-tuple-element.422.rest_0_), channel_id=1, source_target_pairs={{0,2},{1,3},{2,0},{3,1},{4,6},{5,7},{6,4},{7,5},{8,10},{9,11},{10,... | collective-permute-start | bytes 3686408 | tf_op jit(solution)/shard_map/ppermute | solution.py:289
  11.5 30.9 %collective-permute-start.4 = (bf16[8,8,9600]{2,1,0:T(8,128)(2,1)S(1)}, bf16[8,8,9600]{2,1,0:T(8,128)(2,1)S(1)}, u32[]{:S(2)}, u32[]{:S(2)}) collective-permute-start(bf16[8,8,9600]{2,1,0:T(8,128)(2,1)S(1)} %get-tuple-element.421.rest_1_), channel_id=1, source_target_pairs={{0,4},{1,5},{2,6},{3,7},{4,0},{5,1},{6,2},{7,3},{8,12},{9,13},{10,... | collective-permute-start | bytes 3686408 | tf_op jit(solution)/shard_map/ppermute | solution.py:289
  13.0 52.5 %collective-permute-start.2 = (bf16[8,8,9600]{2,1,0:T(8,128)(2,1)S(1)}, bf16[8,8,9600]{2,1,0:T(8,128)(2,1)S(1)}, u32[]{:S(2)}, u32[]{:S(2)}) collective-permute-start(bf16[8,8,9600]{2,1,0:T(8,128)(2,1)S(1)} %get-tuple-element.421.rest_1_), channel_id=1, source_target_pairs={{0,2},{1,3},{2,0},{3,1},{4,6},{5,7},{6,4},{7,5},{8,10},{9,11},{10,... | collective-permute-start | bytes 3686408 | tf_op jit(solution)/shard_map/ppermute | solution.py:289
  13.6 55.8 %collective-permute-start.3 = (bf16[8,8,9600]{2,1,0:T(8,128)(2,1)S(1)}, bf16[8,8,9600]{2,1,0:T(8,128)(2,1)S(1)}, u32[]{:S(2)}, u32[]{:S(2)}) collective-permute-start(bf16[8,8,9600]{2,1,0:T(8,128)(2,1)S(1)} %get-tuple-element.422.rest_0_), channel_id=1, source_target_pairs={{0,4},{1,5},{2,6},{3,7},{4,0},{5,1},{6,2},{7,3},{8,12},{9,13},{10,... | collective-permute-start | bytes 3686408 | tf_op jit(solution)/shard_map/ppermute | solution.py:289
  39.4 33.6 %collective-permute-start.7 = (bf16[8,8,9600]{2,1,0:T(8,128)(2,1)S(1)}, bf16[8,8,9600]{2,1,0:T(8,128)(2,1)S(1)}, u32[]{:S(2)}, u32[]{:S(2)}) collective-permute-start(bf16[8,8,9600]{2,1,0:T(8,128)(2,1)S(1)} %get-tuple-element.422.rest_0_), channel_id=1, source_target_pairs={{0,8},{1,9},{2,10},{3,11},{4,12},{5,13},{6,14},{7,15},{8,24},{9,25... | collective-permute-start | bytes 3686408 | tf_op jit(solution)/shard_map/ppermute | solution.py:289
  41.4 1.0 copy-start
  42.5 52.9 %collective-permute-start.8 = (bf16[8,8,9600]{2,1,0:T(8,128)(2,1)S(1)}, bf16[8,8,9600]{2,1,0:T(8,128)(2,1)}, u32[]{:S(2)}, u32[]{:S(2)}) collective-permute-start(bf16[8,8,9600]{2,1,0:T(8,128)(2,1)S(1)} %get-tuple-element.421.rest_1_), channel_id=1, source_target_pairs={{0,8},{1,9},{2,10},{3,11},{4,12},{5,13},{6,14},{7,15},{8,24},{9,25... | collective-permute-start | bytes 3686408 | tf_op jit(solution)/shard_map/ppermute | solution.py:289
  65.5 1.0 copy-start.10
  66.6 30.4 %collective-permute-start.5 = (bf16[8,8,9600]{2,1,0:T(8,128)(2,1)S(1)}, bf16[8,8,9600]{2,1,0:T(8,128)(2,1)S(1)}, u32[]{:S(2)}, u32[]{:S(2)}) collective-permute-start(bf16[8,8,9600]{2,1,0:T(8,128)(2,1)S(1)} %collective-permute-done.1.rest_2_), channel_id=1, source_target_pairs={{0,4},{1,5},{2,6},{3,7},{4,0},{5,1},{6,2},{7,3},{8,12},{9,13},{10,... | collective-permute-start | bytes 3686408 | tf_op jit(solution)/shard_map/ppermute | solution.py:289
  68.3 1.1 copy-start.4
  69.4 1.0 copy-start.12
  70.4 30.0 %collective-permute-start.6 = (bf16[8,8,9600]{2,1,0:T(8,128)(2,1)S(1)}, bf16[8,8,9600]{2,1,0:T(8,128)(2,1)S(1)}, u32[]{:S(2)}, u32[]{:S(2)}) collective-permute-start(bf16[8,8,9600]{2,1,0:T(8,128)(2,1)S(1)} %collective-permute-done.4.rest_5_), channel_id=1, source_target_pairs={{0,2},{1,3},{2,0},{3,1},{4,6},{5,7},{6,4},{7,5},{8,10},{9,11},{10,... | collective-permute-start | bytes 3686408 | tf_op jit(solution)/shard_map/ppermute | solution.py:289
  71.9 1.1 copy-start.6
  73.0 53.7 %collective-permute-start.9 = (bf16[8,8,9600]{2,1,0:T(8,128)(2,1)S(1)}, bf16[8,8,9600]{2,1,0:T(8,128)(2,1)S(1)}, u32[]{:S(2)}, u32[]{:S(2)}) collective-permute-start(bf16[8,8,9600]{2,1,0:T(8,128)(2,1)S(1)} %collective-permute-done.7.rest_0_), channel_id=1, source_target_pairs={{0,2},{1,3},{2,0},{3,1},{4,6},{5,7},{6,4},{7,5},{8,10},{9,11},{10,... | collective-permute-start | bytes 3686408 | tf_op jit(solution)/shard_map/ppermute | solution.py:289
  95.4 90.0 %collective-permute-start.12 = (bf16[8,8,9600]{2,1,0:T(8,128)(2,1)}, bf16[8,8,9600]{2,1,0:T(8,128)(2,1)}, u32[]{:S(2)}, u32[]{:S(2)}) collective-permute-start(bf16[8,8,9600]{2,1,0:T(8,128)(2,1)} %collective-permute-done.8.rest_1_), channel_id=1, source_target_pairs={{0,4},{1,5},{2,6},{3,7},{4,0},{5,1},{6,2},{7,3},{8,12},{9,13},{10,... | collective-permute-start | bytes 3686408 | tf_op jit(solution)/shard_map/ppermute | solution.py:289
  96.9 1.0 copy-start.14
  98.0 87.5 %collective-permute-start.10 = (bf16[8,8,9600]{2,1,0:T(8,128)(2,1)}, bf16[8,8,9600]{2,1,0:T(8,128)(2,1)}, u32[]{:S(2)}, u32[]{:S(2)}) collective-permute-start(bf16[8,8,9600]{2,1,0:T(8,128)(2,1)} %collective-permute-done.8.rest_1_), channel_id=1, source_target_pairs={{0,2},{1,3},{2,0},{3,1},{4,6},{5,7},{6,4},{7,5},{8,10},{9,11},{10,... | collective-permute-start | bytes 3686408 | tf_op jit(solution)/shard_map/ppermute | solution.py:289
  100.4 1.1 copy-start.16
  101.5 84.0 %collective-permute-start.11 = (bf16[8,8,9600]{2,1,0:T(8,128)(2,1)S(1)}, bf16[8,8,9600]{2,1,0:T(8,128)(2,1)}, u32[]{:S(2)}, u32[]{:S(2)}) collective-permute-start(bf16[8,8,9600]{2,1,0:T(8,128)(2,1)S(1)} %collective-permute-done.7.rest_0_), channel_id=1, source_target_pairs={{0,4},{1,5},{2,6},{3,7},{4,0},{5,1},{6,2},{7,3},{8,12},{9,13},{10,... | collective-permute-start | bytes 3686408 | tf_op jit(solution)/shard_map/ppermute | solution.py:289
  126.7 1.6 copy-start.8
  126.7 58.9 %collective-permute-start.15 = (bf16[8,8,9600]{2,1,0:T(8,128)(2,1)S(1)}, bf16[8,8,9600]{2,1,0:T(8,128)(2,1)}, u32[]{:S(2)}, u32[]{:S(2)}) collective-permute-start(bf16[8,8,9600]{2,1,0:T(8,128)(2,1)S(1)} %collective-permute-done.7.rest_0_), channel_id=1, source_target_pairs={{0,8},{1,9},{2,10},{3,11},{4,12},{5,13},{6,14},{7,15},{8,24},{9,25... | collective-permute-start | bytes 3686408 | tf_op jit(solution)/shard_map/ppermute | solution.py:289
  128.3 1.0 copy-start.2
  185.4 27.1 %collective-permute-start.16 = (bf16[8,8,9600]{2,1,0:T(8,128)(2,1)}, bf16[8,8,9600]{2,1,0:T(8,128)(2,1)}, u32[]{:S(2)}, u32[]{:S(2)}) collective-permute-start(bf16[8,8,9600]{2,1,0:T(8,128)(2,1)} %collective-permute-done.8.rest_1_), channel_id=1, source_target_pairs={{0,8},{1,9},{2,10},{3,11},{4,12},{5,13},{6,14},{7,15},{8,24},{9,25... | collective-permute-start | bytes 3686408 | tf_op jit(solution)/shard_map/ppermute | solution.py:289
  185.4 27.1 %collective-permute-start.13 = (bf16[8,8,9600]{2,1,0:T(8,128)(2,1)}, bf16[8,8,9600]{2,1,0:T(8,128)(2,1)}, u32[]{:S(2)}, u32[]{:S(2)}) collective-permute-start(bf16[8,8,9600]{2,1,0:T(8,128)(2,1)} %copy-done.8), channel_id=1, source_target_pairs={{0,4},{1,5},{2,6},{3,7},{4,0},{5,1},{6,2},{7,3},{8,12},{9,13},{10,... | collective-permute-start | bytes 3686408 | tf_op jit(solution)/shard_map/ppermute | solution.py:289
  185.5 30.3 %collective-permute-start.14 = (bf16[8,8,9600]{2,1,0:T(8,128)(2,1)}, bf16[8,8,9600]{2,1,0:T(8,128)(2,1)}, u32[]{:S(2)}, u32[]{:S(2)}) collective-permute-start(bf16[8,8,9600]{2,1,0:T(8,128)(2,1)} %collective-permute-done.12.rest_5_), channel_id=1, source_target_pairs={{0,2},{1,3},{2,0},{3,1},{4,6},{5,7},{6,4},{7,5},{8,10},{9,11},{10,... | collective-permute-start | bytes 3686408 | tf_op jit(solution)/shard_map/ppermute | solution.py:289
  185.6 56.5 %collective-permute-start.17 = (bf16[8,8,9600]{2,1,0:T(8,128)(2,1)}, bf16[8,8,9600]{2,1,0:T(8,128)(2,1)S(1)}, u32[]{:S(2)}, u32[]{:S(2)}) collective-permute-start(bf16[8,8,9600]{2,1,0:T(8,128)(2,1)} %collective-permute-done.15.rest_0_), channel_id=1, source_target_pairs={{0,2},{1,3},{2,0},{3,1},{4,6},{5,7},{6,4},{7,5},{8,10},{9,11},{10,... | collective-permute-start | bytes 3686408 | tf_op jit(solution)/shard_map/ppermute | solution.py:289
  212.5 42.1 %collective-permute-start.20 = (bf16[8,8,9600]{2,1,0:T(8,128)(2,1)}, bf16[8,8,9600]{2,1,0:T(8,128)(2,1)}, u32[]{:S(2)}, u32[]{:S(2)}) collective-permute-start(bf16[8,8,9600]{2,1,0:T(8,128)(2,1)} %collective-permute-done.16.rest_1_), channel_id=1, source_target_pairs={{0,4},{1,5},{2,6},{3,7},{4,0},{5,1},{6,2},{7,3},{8,12},{9,13},{10,... | collective-permute-start | bytes 3686408 | tf_op jit(solution)/shard_map/ppermute | solution.py:289
  212.5 51.8 %collective-permute-start.18 = (bf16[8,8,9600]{2,1,0:T(8,128)(2,1)}, bf16[8,8,9600]{2,1,0:T(8,128)(2,1)}, u32[]{:S(2)}, u32[]{:S(2)}) collective-permute-start(bf16[8,8,9600]{2,1,0:T(8,128)(2,1)} %collective-permute-done.16.rest_1_), channel_id=1, source_target_pairs={{0,2},{1,3},{2,0},{3,1},{4,6},{5,7},{6,4},{7,5},{8,10},{9,11},{10,... | collective-permute-start | bytes 3686408 | tf_op jit(solution)/shard_map/ppermute | solution.py:289
  215.9 51.2 %collective-permute-start.23 = (bf16[8,8,9600]{2,1,0:T(8,128)(2,1)}, bf16[8,8,9600]{2,1,0:T(8,128)(2,1)}, u32[]{:S(2)}, u32[]{:S(2)}) collective-permute-start(bf16[8,8,9600]{2,1,0:T(8,128)(2,1)} %collective-permute-done.15.rest_0_), channel_id=1, source_target_pairs={{0,8},{1,9},{2,10},{3,11},{4,12},{5,13},{6,14},{7,15},{8,24},{9,25... | collective-permute-start | bytes 3686408 | tf_op jit(solution)/shard_map/ppermute | solution.py:289
  242.1 2.2 copy-start.18
  242.1 24.9 %collective-permute-start.24 = (bf16[8,8,9600]{2,1,0:T(8,128)(2,1)}, bf16[8,8,9600]{2,1,0:T(8,128)(2,1)}, u32[]{:S(2)}, u32[]{:S(2)}) collective-permute-start(bf16[8,8,9600]{2,1,0:T(8,128)(2,1)} %collective-permute-done.16.rest_1_), channel_id=1, source_target_pairs={{0,8},{1,9},{2,10},{3,11},{4,12},{5,13},{6,14},{7,15},{8,24},{9,25... | collective-permute-start | bytes 3686408 | tf_op jit(solution)/shard_map/ppermute | solution.py:289
  254.7 43.9 %collective-permute-start.19 = (bf16[8,8,9600]{2,1,0:T(8,128)(2,1)}, bf16[8,8,9600]{2,1,0:T(8,128)(2,1)}, u32[]{:S(2)}, u32[]{:S(2)}) collective-permute-start(bf16[8,8,9600]{2,1,0:T(8,128)(2,1)} %collective-permute-done.15.rest_0_), channel_id=1, source_target_pairs={{0,4},{1,5},{2,6},{3,7},{4,0},{5,1},{6,2},{7,3},{8,12},{9,13},{10,... | collective-permute-start | bytes 3686408 | tf_op jit(solution)/shard_map/ppermute | solution.py:289
  264.3 47.0 %collective-permute-start.21 = (bf16[8,8,9600]{2,1,0:T(8,128)(2,1)}, bf16[8,8,9600]{2,1,0:T(8,128)(2,1)}, u32[]{:S(2)}, u32[]{:S(2)}) collective-permute-start(bf16[8,8,9600]{2,1,0:T(8,128)(2,1)} %copy-done.18), channel_id=1, source_target_pairs={{0,4},{1,5},{2,6},{3,7},{4,0},{5,1},{6,2},{7,3},{8,12},{9,13},{10,... | collective-permute-start | bytes 3686408 | tf_op jit(solution)/shard_map/ppermute | solution.py:289
  267.0 46.3 %collective-permute-start.25 = (bf16[8,8,9600]{2,1,0:T(8,128)(2,1)}, bf16[8,8,9600]{2,1,0:T(8,128)(2,1)}, u32[]{:S(2)}, u32[]{:S(2)}) collective-permute-start(bf16[8,8,9600]{2,1,0:T(8,128)(2,1)} %collective-permute-done.23.rest_0_), channel_id=1, source_target_pairs={{0,2},{1,3},{2,0},{3,1},{4,6},{5,7},{6,4},{7,5},{8,10},{9,11},{10,... | collective-permute-start | bytes 3686408 | tf_op jit(solution)/shard_map/ppermute | solution.py:289
  267.0 70.7 %collective-permute-start.26 = (bf16[8,8,9600]{2,1,0:T(8,128)(2,1)}, bf16[8,8,9600]{2,1,0:T(8,128)(2,1)}, u32[]{:S(2)}, u32[]{:S(2)}) collective-permute-start(bf16[8,8,9600]{2,1,0:T(8,128)(2,1)} %collective-permute-done.24.rest_1_), channel_id=1, source_target_pairs={{0,4},{1,5},{2,6},{3,7},{4,0},{5,1},{6,2},{7,3},{8,12},{9,13},{10,... | collective-permute-start | bytes 3686408 | tf_op jit(solution)/shard_map/ppermute | solution.py:289
  267.5 86.5 %collective-permute-start.22 = (bf16[8,8,9600]{2,1,0:T(8,128)(2,1)}, bf16[8,8,9600]{2,1,0:T(8,128)(2,1)}, u32[]{:S(2)}, u32[]{:S(2)}) collective-permute-start(bf16[8,8,9600]{2,1,0:T(8,128)(2,1)} %collective-permute-done.20.rest_5_), channel_id=1, source_target_pairs={{0,2},{1,3},{2,0},{3,1},{4,6},{5,7},{6,4},{7,5},{8,10},{9,11},{10,... | collective-permute-start | bytes 3686408 | tf_op jit(solution)/shard_map/ppermute | solution.py:289
  269.9 1.3 copy-start.1
  271.2 1.3 copy-start.5
  272.5 1.3 copy-start.7
  273.8 1.3 copy-start.11
  275.1 1.3 copy-start.13
  276.4 1.3 copy-start.15
  277.7 1.3 copy-start.17
  279.0 60.0 %copy-start.3 = (bf16[8,8,9600]{2,1,0:T(8,128)(2,1)S(1)}, bf16[8,8,9600]{2,1,0:T(8,128)(2,1)}, u32[]{:S(2)}) copy-start(bf16[8,8,9600]{2,1,0:T(8,128)(2,1)} %copy-done.2) | copy-start | bytes 3686404
  279.0 60.0 %copy-start.9 = (bf16[8,8,9600]{2,1,0:T(8,128)(2,1)S(1)}, bf16[8,8,9600]{2,1,0:T(8,128)(2,1)}, u32[]{:S(2)}) copy-start(bf16[8,8,9600]{2,1,0:T(8,128)(2,1)} %copy-done.8) | copy-start | bytes 3686404
  298.6 84.1 %collective-permute-start.27 = (bf16[8,8,9600]{2,1,0:T(8,128)(2,1)}, bf16[8,8,9600]{2,1,0:T(8,128)(2,1)S(1)}, u32[]{:S(2)}, u32[]{:S(2)}) collective-permute-start(bf16[8,8,9600]{2,1,0:T(8,128)(2,1)} %collective-permute-done.24.rest_1_), channel_id=1, source_target_pairs={{0,2},{1,3},{2,0},{3,1},{4,6},{5,7},{6,4},{7,5},{8,10},{9,11},{10,... | collective-permute-start | bytes 3686408 | tf_op jit(solution)/shard_map/ppermute | solution.py:289
  311.3 71.3 %collective-permute-start.28 = (bf16[8,8,9600]{2,1,0:T(8,128)(2,1)}, bf16[8,8,9600]{2,1,0:T(8,128)(2,1)S(1)}, u32[]{:S(2)}, u32[]{:S(2)}) collective-permute-start(bf16[8,8,9600]{2,1,0:T(8,128)(2,1)} %collective-permute-done.23.rest_0_), channel_id=1, source_target_pairs={{0,4},{1,5},{2,6},{3,7},{4,0},{5,1},{6,2},{7,3},{8,12},{9,13},{10,... | collective-permute-start | bytes 3686408 | tf_op jit(solution)/shard_map/ppermute | solution.py:289
  313.3 69.4 %collective-permute-start.29 = (bf16[8,8,9600]{2,1,0:T(8,128)(2,1)}, bf16[8,8,9600]{2,1,0:T(8,128)(2,1)S(1)}, u32[]{:S(2)}, u32[]{:S(2)}) collective-permute-start(bf16[8,8,9600]{2,1,0:T(8,128)(2,1)} %collective-permute-done.25.rest_2_), channel_id=1, source_target_pairs={{0,4},{1,5},{2,6},{3,7},{4,0},{5,1},{6,2},{7,3},{8,12},{9,13},{10,... | collective-permute-start | bytes 3686408 | tf_op jit(solution)/shard_map/ppermute | solution.py:289
  337.7 45.0 %collective-permute-start.30 = (bf16[8,8,9600]{2,1,0:T(8,128)(2,1)}, bf16[8,8,9600]{2,1,0:T(8,128)(2,1)S(1)}, u32[]{:S(2)}, u32[]{:S(2)}) collective-permute-start(bf16[8,8,9600]{2,1,0:T(8,128)(2,1)} %collective-permute-done.26.rest_3_), channel_id=1, source_target_pairs={{0,2},{1,3},{2,0},{3,1},{4,6},{5,7},{6,4},{7,5},{8,10},{9,11},{10,... | collective-permute-start | bytes 3686408 | tf_op jit(solution)/shard_map/ppermute | solution.py:289
  338.9 15.0 %copy-start.19 = (bf16[8,8,9600]{2,1,0:T(8,128)(2,1)S(1)}, bf16[8,8,9600]{2,1,0:T(8,128)(2,1)}, u32[]{:S(2)}) copy-start(bf16[8,8,9600]{2,1,0:T(8,128)(2,1)} %copy-done.18) | copy-start | bytes 3686404
Sparse Core Ops, SparseCore 0:
  243.0 3.8 sort.12.cloned.1.call-done
  (1 shorter events, 0.0 us)

commit v3 on v2

--- a/solution.py
+++ b/solution.py
@@ -12,7 +12,10 @@
 R = 5
 GROUP = 16
 NONE = 1 << 30
-ROUTES = (("zxy", 8), ("zyx", 8))
+ROUTES = (("zxy", 6), ("zyx", 6), ("xyz", 2), ("yxz", 2))
+PHASE_ENDS = (0.45, 0.7, 0.88, 1.0)
+IN_FLIGHT = 2
+SLACK = 2.0
 
 
 def dot(a, b):
@@ -94,7 +97,7 @@
     )(one_w, two_w, three_w)
 
 
-def pair_kernel(frames, buffers, q_dev, scale, rows_ref, vids_ref, count_ref, entry_ref, one_ref,
+def pair_kernel(frames, buffers, stride, scale, rows_ref, vids_ref, count_ref, entry_ref, one_ref,
                 two_ref, three_ref, before_ref, own_hbm, other_hbm, *rest):
     q_hbm, rest = rest[:buffers], rest[buffers:]
     out_ref, q_in, v_in, q_rows, v_rows, maps, q_sem, v_sem = rest
@@ -108,7 +111,7 @@
         def one_pair(p, _):
             row = rows_ref[step * GROUP + p]
             vid = vids_ref[step * GROUP + p]
-            buf, row = lax.div(row, q_dev), lax.rem(row, q_dev)
+            buf, row = lax.div(row, stride), lax.rem(row, stride)
             for b in range(buffers):
                 @pl.when(buf == b)
                 def _():
@@ -148,17 +151,16 @@
             q_rows[pl.ds(r * side, side), :] = q_in[slot, :, :, cols].reshape(side, width)
             v_rows[pl.ds(r * side, side), :] = v_in[slot, :, :, cols].reshape(side, width)
 
-        def region(r, total):
+        total = jnp.zeros((side, side), jnp.float32)
+        for r in range(R):
             sim = lax.dot_general(
-                q_rows[pl.ds(pl.multiple_of(r * side, side), side), :], v_rows[...],
-                (((1,), (1,)), ((), ())), preferred_element_type=jnp.float32,
+                q_rows[pl.ds(r * side, side), :], v_rows[...], (((1,), (1,)), ((), ())),
+                preferred_element_type=jnp.float32,
             )
             best = sim[:, :side]
             for s in range(1, R):
                 best = jnp.maximum(best, sim[:, s * side:(s + 1) * side])
-            return total + best
-
-        total = lax.fori_loop(0, R, region, jnp.zeros((side, side), jnp.float32))
+            total = total + best
         cells = frames * frames
         same_pair = iota((side, side), 0) // frames == iota((side, side), 1) // frames
         lane, sub = iota((side, cells), 1), iota((side, cells), 0)
@@ -194,16 +196,16 @@
         )
 
 
-def pair_scores(blocks, own, other, rows, vids, count, entry, heads, before, q_dev, name):
+def pair_scores(blocks, own, other, rows, vids, count, entry, heads, before, stride, name):
     frames, width = own.shape[1], own.shape[2]
     cap = rows.shape[0]
     side = GROUP * frames
     scale = 1.0 / (math.sqrt(width // R) * R)
     smem = pl.BlockSpec(memory_space=pltpu.SMEM)
     vmem = pl.BlockSpec(memory_space=pltpu.VMEM)
-    hbm = pl.BlockSpec(memory_space=pl.ANY)
+    hbm = pl.BlockSpec(memory_space=pltpu.HBM)
     return pl.pallas_call(
-        functools.partial(pair_kernel, frames, len(blocks), q_dev, scale),
+        functools.partial(pair_kernel, frames, len(blocks), stride, scale),
         out_shape=jax.ShapeDtypeStruct(before.shape, jnp.float32),
         in_specs=[smem] * 3 + [vmem] * 5 + [hbm] * (2 + len(blocks)),
         out_specs=vmem,
@@ -216,7 +218,7 @@
             pltpu.SemaphoreType.DMA((2,)),
             pltpu.SemaphoreType.DMA((2,)),
         ],
-        compiler_params=pltpu.CompilerParams(vmem_limit_bytes=40 * 1024 * 1024),
+        compiler_params=pltpu.CompilerParams(vmem_limit_bytes=58 * 1024 * 1024),
         cost_estimate=pl.CostEstimate(
             flops=2 * cap * side * R * R * frames * (width // R),
             bytes_accessed=cap * frames * width * 4, transcendentals=0,
@@ -239,6 +241,64 @@
     order = list(range(1, size, 2)) + list(reversed(range(0, size, 2)))
     order = [0] + [c for c in order if c != 0]
     return order.index(coordinate)
+
+
+def plan(sizes, q_dev):
+    parts = sum(n for _, n in ROUTES)
+    messages = []
+    starts, start = [], 0
+    for r, (order, share) in enumerate(ROUTES):
+        n = q_dev * share // parts
+        starts.append((start, n))
+        start += n
+        have = [(r, 0, 0, 0)]
+        for at, letter in enumerate(order):
+            axis = "zyx".index(letter)
+            if letter == "z" and at == 2:
+                for k in range(1, sizes[0]):
+                    messages.append((0, (r, k - 1), (r, k), n * sizes[1] * sizes[2]))
+                break
+            for block in list(have):
+                for k in range(1, sizes[axis]):
+                    to = list(block)
+                    to[1 + axis] = k
+                    messages.append((axis, block, tuple(to), n))
+                    block = tuple(to)
+                    have.append(block)
+    users = {}
+    for m in messages:
+        users.setdefault(m[1], []).append(m)
+
+    def planes(block):
+        r, z = block[:2]
+        if len(block) == 4 and ROUTES[r][0][2] == "z":
+            return users.get((r, 0), [])
+        return []
+
+    @functools.cache
+    def tail(m):
+        after = users.get(m[2], []) + planes(m[2])
+        return m[3] + max([tail(a) for a in after], default=0)
+
+    ready = {(r, 0, 0, 0): 0.0 for r in range(len(ROUTES))}
+    free = [0.0, 0.0, 0.0]
+    waiting, order = list(messages), []
+
+    def when(block):
+        if len(block) == 2 and block[1] == 0:
+            cells = [(block[0], 0, y, x) for y in range(sizes[1]) for x in range(sizes[2])]
+            return max(ready.get(c, math.inf) for c in cells)
+        return ready.get(block, math.inf)
+
+    begins = {}
+    while waiting:
+        best = min(waiting, key=lambda m: (max(free[m[0]], when(m[1])), -tail(m), m))
+        begin = max(free[best[0]], when(best[1]))
+        free[best[0]] = ready[best[2]] = begin + best[3] + 0.5
+        begins[best] = begin
+        order.append(best)
+        waiting.remove(best)
+    return starts, order, begins, ready
 
 
 def body(places, sizes, queries, index_videos, candidates, conv_one, conv_two, conv_three):
@@ -251,15 +311,9 @@
     per_holder = max(2, (2 * pairs + devices - 1) // devices)
     me = lax.axis_index("shard")
     chip, core = me // 2, me % 2
-    same_core = [[2 * i + c for i in range(chips)] for c in range(2)]
 
     rings = [tuple(ring_position(c, n) for c, n in zip(p, sizes)) for p in places]
     where = {r: i for i, r in enumerate(rings)}
-    offsets = [(z, y, x) for z in range(sizes[0]) for y in range(sizes[1]) for x in range(sizes[2])]
-    back = np.array(
-        [[where[tuple((r - o) % n for r, o, n in zip(ring, off, sizes))] for off in offsets]
-         for ring in rings], np.int32,
-    )
 
     def step_along(axis):
         out = []
@@ -271,90 +325,113 @@
 
     steps = [step_along(a) for a in range(3)]
 
-    ids = lax.all_gather(
-        candidates.reshape(1, pairs), "shard", axis=0, tiled=True, axis_index_groups=same_core
+    all_ids = lax.all_to_all(
+        jnp.broadcast_to(candidates.reshape(1, pairs), (devices, pairs)), "shard", split_axis=0,
+        concat_axis=0, tiled=True,
     )
     other = lax.ppermute(index_videos, "shard", [(d, d ^ 1) for d in range(devices)])
 
-    parts = sum(n for _, n in ROUTES)
-    starts, blocks = [], []
-    start = 0
-    for order, share in ROUTES:
-        n = q_dev * share // parts
-        have = {(0, 0, 0): queries[start:start + n]}
-        for letter in order:
-            axis = "zyx".index(letter)
-            for off, block in list(have.items()):
-                for k in range(1, sizes[axis]):
-                    block = lax.ppermute(block, "shard", steps[axis])
-                    off = off[:axis] + (k,) + off[axis + 1:]
-                    have[off] = block
-        starts.append(start)
-        blocks.append(have)
-        start += n
-    routes = len(ROUTES)
-
-    plane = sizes[1] * sizes[2]
-    offsets_of = [offsets[z * plane:(z + 1) * plane] for z in range(sizes[0])]
-    phases = []
-    for z in range(sizes[0]):
-        every = [(i, r) for i in range(plane) for r in range(routes)]
-        late = []
-        if z == sizes[0] - 1 and sizes[0] > 1:
-            late = [
-                (i, r) for i, r in every
-                if offsets_of[z][i]["zyx".index(ROUTES[r][0][-1])] == sizes["zyx".index(ROUTES[r][0][-1])] - 1
-            ]
-        phases.append((z, [e for e in every if e not in late]))
-        if late:
-            phases.append((z, late))
-
-    senders = lax.dynamic_index_in_dim(jnp.asarray(back), chip, 0, keepdims=False)
-    flat = jnp.take(ids, senders, axis=0).reshape(sizes[0], plane * pairs)
-    flat = jnp.take(flat, np.array([z for z, _ in phases]), axis=0)
-    pos = np.arange(plane * pairs, dtype=np.int32)
-    pair = pos % pairs
-    route = np.sum(np.array(starts)[None, :] <= (pair // k_count)[:, None], axis=1) - 1
-    inside = np.array(
-        [[(int(p) // pairs, int(r)) in set(chosen) for p, r in zip(pos, route)]
-         for _, chosen in phases], bool,
+    starts, order, begins, arrival = plan(sizes, q_dev)
+    plane = [(y, x) for y in range(sizes[1]) for x in range(sizes[2])]
+
+    last = max(arrival.values())
+    phase_of = lambda key: next(
+        p for p, end in enumerate(PHASE_ENDS) if arrival[key] <= end * last + 1e-6
     )
-    mine = (flat // (2 * idx_dev) == chip) & inside
-    local = flat % (2 * idx_dev)
+    phases = [[] for _ in PHASE_ENDS]
+    place = {}
+    for r, (start, n) in enumerate(starts):
+        for z in range(sizes[0]):
+            whole = ROUTES[r][0][2] == "z" and z > 0
+            for i, (y, x) in enumerate(plane):
+                key = (r, z) if whole else (r, z, y, x)
+                p = phase_of(key)
+                if key not in phases[p]:
+                    phases[p].append(key)
+                for q in range(n):
+                    place[(z, y, x), start + q] = (p, phases[p].index(key), q + (i * n if whole else 0))
+    stride = 1 << max(4, (len(plane) * max(n for _, n in starts) - 1).bit_length())
+    most = max(len(p) for p in phases)
+    spot = np.zeros((chips, chips, q_dev), np.int32)
+    caps = [0] * len(phases)
+    offsets = sorted({off for off, _ in place})
+    for off in offsets:
+        for p in range(len(phases)):
+            here = sum(place[off, q][0] == p for q in range(q_dev))
+            caps[p] += min(here * k_count, 2 * per_holder)
+    for c in range(chips):
+        for s in range(chips):
+            off = tuple((a - b) % n for a, b, n in zip(rings[c], rings[s], sizes))
+            for q in range(q_dev):
+                p, b, row = place[off, q]
+                spot[c, s, q] = (p * most + b) * stride + row
+    caps = [-(-c // GROUP) * GROUP for c in caps]
+
+    spot = lax.dynamic_index_in_dim(jnp.asarray(spot), chip, 0, keepdims=False)
+    spot = jnp.broadcast_to(spot[:, :, None], (chips, q_dev, k_count)).reshape(chips * pairs)
+    ids = all_ids.reshape(chips, 2, pairs)
+    ids = jnp.where(core == 0, ids[:, 0], ids[:, 1]).reshape(chips * pairs)
+    mine = ids // (2 * idx_dev) == chip
+    local = ids % (2 * idx_dev)
     local = jnp.where(local // idx_dev == core, local % idx_dev, local % idx_dev + idx_dev)
-    code = jnp.where(mine, pos[None, :] * (2 * idx_dev) + local, NONE)
-    cap = min(plane * 2 * per_holder, plane * pairs)
-    cap = -(-cap // GROUP) * GROUP
-    code = jnp.sort(code, axis=1)[:, :cap]
-    count = jnp.sum(mine.astype(jnp.int32), axis=1)
-    valid = code < NONE
-    place = jnp.where(valid, code // (2 * idx_dev), 0)
-    vids = jnp.where(valid, code % (2 * idx_dev), 0)
-    number, pair = place // pairs, place % pairs
-    query = pair // k_count
-    sender = jnp.zeros_like(place)
-    by_phase = senders.reshape(sizes[0], plane)[np.array([z for z, _ in phases])]
-    for i in range(plane):
-        sender = jnp.where(number == i, by_phase[:, i:i + 1], sender)
-    entry = jnp.where(valid, sender * pairs + pair, NONE)
-    rows = jnp.zeros_like(place)
-    for p, (_, chosen) in enumerate(phases):
-        for b, (i, r) in enumerate(chosen):
-            end = starts[r + 1] if r + 1 < routes else q_dev
-            hit = (number[p] == i) & (query[p] >= starts[r]) & (query[p] < end)
-            rows = rows.at[p].set(
-                jnp.where(hit & valid[p], b * q_dev + query[p] - starts[r], rows[p])
-            )
+    code = jnp.where(mine, spot * (2 * idx_dev) + local, NONE)
+    code, entry = lax.sort((code, jnp.arange(chips * pairs, dtype=jnp.int32)), num_keys=1)
+    total = chips * 2 * per_holder
+    code = jnp.concatenate([code[:total], jnp.full((max(caps),), NONE, jnp.int32)])
+    entry = jnp.concatenate([entry[:total], jnp.zeros((max(caps),), jnp.int32)])
+    spots = code // (2 * idx_dev)
+    phase = jnp.where(code < NONE, spots // (most * stride), len(phases))
+    counts = jnp.sum(
+        (phase[:, None] == jnp.arange(len(phases))[None, :]).astype(jnp.int32), axis=0
+    )
+    firsts = jnp.cumsum(counts) - counts
+    spots = spots % (most * stride)
+    vids = code % (2 * idx_dev)
 
     heads = head_matrices(conv_one, conv_two, conv_three)
-    table = jnp.zeros((chips, pairs), jnp.float32)
-    for p, (z, chosen) in enumerate(phases):
-        table = pair_scores(
-            [blocks[r][offsets_of[z][i]] for i, r in chosen], index_videos, other, rows[p], vids[p],
-            count[p:p + 1], entry[p].reshape(cap, 1), heads, table, q_dev, "phase_" + str(p),
-        )
+    tables = [jnp.zeros((chips, pairs), jnp.float32)]
+
+    def score(p):
+        cut = lambda a: lax.dynamic_slice(a, (firsts[p],), (caps[p],))
+        valid = jnp.arange(caps[p]) < counts[p]
+        rows, vid = jnp.where(valid, cut(spots), 0), jnp.where(valid, cut(vids), 0)
+        entries = jnp.where(valid, cut(entry), NONE)
+        tables.append(pair_scores(
+            [blocks[k] for k in phases[p]], index_videos, other, rows, vid, counts[p:p + 1],
+            entries.reshape(caps[p], 1), heads, tables[-1], stride, "phase_" + str(p),
+        ))
+
+    blocks = {}
+    for r, (start, n) in enumerate(starts):
+        blocks[(r, 0, 0, 0)] = queries[start:start + n]
+
+    def block_of(key):
+        if key not in blocks:
+            blocks[key] = jnp.concatenate([blocks[(key[0], 0, y, x)] for y, x in plane], axis=0)
+        return blocks[key]
+
+    done = [[], [], []]
+    for m in order:
+        axis, source, target, _ = m
+        behind = done[axis][-IN_FLIGHT:][:1] if len(done[axis]) >= IN_FLIGHT else []
+        if len(done[axis]) == 1:
+            behind.append(all_ids)
+        if len(done[axis]) == 3 and axis == 0:
+            behind.append(other)
+        while len(tables) < len(phases) and begins[m] > PHASE_ENDS[len(tables) - 1] * last + SLACK:
+            score(len(tables) - 1)
+            behind.append(tables[-1])
+        sent = block_of(source)
+        if behind:
+            sent = lax.optimization_barrier((sent, *behind))[0]
+        blocks[target] = lax.ppermute(sent, "shard", steps[axis])
+        done[axis].append(blocks[target])
+    while len(tables) <= len(phases):
+        score(len(tables) - 1)
+    table = tables[-1]
+    table = jnp.where(jnp.arange(2)[None, :, None] == core, table[:, None], 0.0)
     scores = lax.all_to_all(
-        table, "shard", split_axis=0, concat_axis=0, tiled=True, axis_index_groups=same_core
+        table.reshape(devices, pairs), "shard", split_axis=0, concat_axis=0, tiled=True
     )
     return jnp.sum(scores, axis=0).reshape(q_dev, k_count)
 

time: 432 us -> 374 us (0.87)
  starting transfers between devices: 30.8 us -> 105 us
  blocking collectives: 86.1 us -> 15 us
  waiting for transfers between devices: 191 us -> 142 us
  other arithmetic: 3.13 us -> 15.6 us
  Pallas kernels: 83 us -> 71.7 us
  local copies, waits for them, and re-layouts: 24.7 us -> 15.1 us
  between operations: 13.8 us -> 8.15 us
    ppermute x30 -> x42, starting transfers between devices: 30.3 us -> 97.9 us  [body(): blocks[target] = lax.ppermute(sent, 'shard', steps[axis])]
    ppermute x30 -> x42, waiting for transfers between devices: 191 us -> 129 us  [body(): blocks[target] = lax.ppermute(sent, 'shard', steps[axis])]
    all_gather x1 -> x0, blocking collectives: 55.2 us -> none  [body(): lax.all_gather(candidates.reshape(1, pairs), 'shard', axis=0, tiled=True,...]
    all_to_all x1, blocking collectives: 30.9 us -> 15 us  [body(): lax.all_to_all(table.reshape(devices, pairs), 'shard', split_axis=0, conc...]
    all_to_all x0 -> x1, waiting for transfers between devices: none -> 13 us  [body(): lax.all_to_all(jnp.broadcast_to(candidates.reshape(1, pairs), (devices, p...]
    unnamed x56 -> x61, local copies, waits for them, and re-layouts: 17.7 us -> 5.13 us
    pallas_call x5 -> x4, Pallas kernels: 74.4 us -> 63.2 us  [pair_scores(): pl.pallas_call(functools.partial(pair_kernel, frames, len(blocks), stride...]
    all_to_all x0 -> x1, starting transfers between devices: none -> 6.96 us  [body(): lax.all_to_all(jnp.broadcast_to(candidates.reshape(1, pairs), (devices, p...]
  transfers between devices with their start and end apart: 31 -> 44, of which waited for: 11 -> 16; matrix products, arithmetic and copies ran while one was open for 2% -> 7% of each run, Pallas kernels for 17% -> 16%
where the time goes in v3:
time: 374 us; the launch traced here: 373 us
  waiting for transfers between devices  142 us (38%)
  starting transfers between devices  105 us (28%)
  Pallas kernels  71.7 us (19%)
  other arithmetic  15.6 us (4%)
  local copies, waits for them, and re-layouts  15.1 us (4%)
  blocking collectives  15 us (4%)
  between operations  8.15 us (2%)
    ppermute x42, waiting for transfers between devices, body(): blocks[target] = lax.ppermute(sent, 'shard', steps[axis])  129 us
    ppermute x42, starting transfers between devices, body(): blocks[target] = lax.ppermute(sent, 'shard', steps[axis])  97.9 us
    pallas_call x4, Pallas kernels, pair_scores(): pl.pallas_call(functools.partial(pair_kernel, frames, len(blocks), stride...  63.2 us
    all_to_all x1, blocking collectives, body(): lax.all_to_all(table.reshape(devices, pairs), 'shard', split_axis=0, conc...  15 us
    all_to_all x1, waiting for transfers between devices, body(): lax.all_to_all(jnp.broadcast_to(candidates.reshape(1, pairs), (devices, p...  13 us
    pallas_call x1, Pallas kernels, head_matrices(): pl.pallas_call(head_kernel, out_shape=[jax.ShapeDtypeStruct(s, jnp.bfloat...  8.54 us
  transfers between devices with their start and end apart: 44, of which 16 were waited for; matrix products, arithmetic and copies ran while one was open for 7% of the time, Pallas kernels for 16%

profile of v3, /device:TPU:0, one launch (start us, length us, event | category | flops | bytes accessed | tf_op | source)
XLA Modules:
  0.0 373.3 jit_solution(14389473496536753124)
XLA Ops:
  1.9 7.0 %all-to-all-start = ((s32[32,1,128]{2,1,0:T(1,128)}), s32[32,1,128]{2,1,0:T(1,128)S(1)}, u32[]{:S(2)}, u32[]{:S(2)}) async-start(s32[32,1,128]{2,1,0:T(1,128)} %broadcast_in_dim.92), calls=%async_computation | async-start | bytes 32768 | tf_op jit(solution)/shard_map/all_to_all | solution.py:328
  8.9 1.6 fusion.12
  10.5 1.8 collective-permute-start.7
  12.3 1.1 fusion.11
  13.5 1.5 collective-permute-start.8
  15.0 1.5 collective-permute-start.9
  16.5 13.0 %all-to-all-done = s32[32,1,128]{2,1,0:T(1,128)S(1)} async-done(((s32[32,1,128]{2,1,0:T(1,128)}), s32[32,1,128]{2,1,0:T(1,128)S(1)}, u32[]{:S(2)}, u32[]{:S(2)}) %all-to-all-start) | async-done | bytes 16416 | tf_op jit(solution)/shard_map/all_to_all | solution.py:328
  29.5 2.8 collective-permute-start.1
  33.2 1.7 collective-permute-start.3
  35.3 4.6 %collective-permute-done.1.rest_22_ = bf16[2,8,9600]{2,1,0:T(8,128)(2,1)} collective-permute-done((bf16[2,8,9600]{2,1,0:T(8,128)(2,1)S(1)}, bf16[2,8,9600]{2,1,0:T(8,128)(2,1)}, u32[]{:S(2)}, u32[]{:S(2)}) %collective-permute-start.1) | collective-permute-done | bytes 307232 | tf_op jit(solution)/shard_map/ppermute | solution.py:427
  40.0 1.7 collective-permute-start.10
  41.7 8.5 %head_matrices.1 = (bf16[64,2048]{1,0:T(8,128)(2,1)S(1)}, bf16[512,1024]{1,0:T(8,128)(2,1)S(1)}, bf16[256,256]{1,0:T(8,128)(2,1)S(1)}) custom-call(bf16[9,1,32]{2,1,0:T(2,128)(2,1)S(1)} %reshape.136.one_w, bf16[9,32,64]{2,1,0:T(8,128)(2,1)S(1)} %bitcast.34, bf16[9,1,64]{2,1,0:T(2,128)(2,1)S(1)} %reshape.137.three_w), custom_call_target="tpu_custom_call" | custom-call | flops 1000000000 | bytes 3000000 | tf_op jit(solution)/shard_map/head_matrices/pallas_call | solution.py:88
  50.3 1.0 copy-done
  52.6 1.6 collective-permute-start.16
  54.8 1.7 collective-permute-start.4
  56.5 2.5 collective-permute-start.12
  59.0 4.4 %sort.15 = (s32[2048]{0:T(1024)S(1)}, s32[2048]{0:T(1024)S(1)}) sort(s32[2048]{0:T(1024)S(1)} %fusion.3, s32[2048]{0:T(1024)S(1)} %iota.26), dimensions={0}, to_apply=%region_0.1 | sort | flops 22528 | bytes 32768 | tf_op jit(solution)/shard_map/sort | solution.py:378
  68.5 8.5 %collective-permute-done.16.rest_12_ = bf16[6,8,9600]{2,1,0:T(8,128)(2,1)} collective-permute-done((bf16[6,8,9600]{2,1,0:T(8,128)(2,1)S(1)}, bf16[6,8,9600]{2,1,0:T(8,128)(2,1)}, u32[]{:S(2)}, u32[]{:S(2)}) %collective-permute-start.16) | collective-permute-done | bytes 921632 | tf_op jit(solution)/shard_map/ppermute | solution.py:427
  77.3 1.8 collective-permute-start.18
  79.4 15.6 %collective-permute-done.12.rest_6_ = bf16[6,8,9600]{2,1,0:T(8,128)(2,1)} collective-permute-done((bf16[6,8,9600]{2,1,0:T(8,128)(2,1)}, bf16[6,8,9600]{2,1,0:T(8,128)(2,1)}, u32[]{:S(2)}, u32[]{:S(2)}) %collective-permute-start.12) | collective-permute-done | bytes 921632 | tf_op jit(solution)/shard_map/ppermute | solution.py:427
  95.4 0.9 collective-permute-start.19
  96.3 1.1 pad_maximum_fusion
  97.5 3.4 collective-permute-start.21
  100.9 1.3 dynamic-slice_select_fusion.1
  102.2 14.1 %collective-permute-done.5.rest_2_ = bf16[6,8,9600]{2,1,0:T(8,128)(2,1)S(1)} collective-permute-done((bf16[6,8,9600]{2,1,0:T(8,128)(2,1)S(1)}, bf16[6,8,9600]{2,1,0:T(8,128)(2,1)S(1)}, u32[]{:S(2)}, u32[]{:S(2)}) %collective-permute-start.5) | collective-permute-done | bytes 921632 | tf_op jit(solution)/shard_map/ppermute | solution.py:427
  116.3 1.7 collective-permute-start.14
  118.0 2.1 collective-permute-start.6
  120.2 1.3 collective-permute-start.20
  121.5 1.2 pad_maximum_fusion.1
  122.7 17.0 %collective-permute-done.14.rest_9_ = bf16[6,8,9600]{2,1,0:T(8,128)(2,1)S(1)} collective-permute-done((bf16[6,8,9600]{2,1,0:T(8,128)(2,1)S(1)}, bf16[6,8,9600]{2,1,0:T(8,128)(2,1)S(1)}, u32[]{:S(2)}, u32[]{:S(2)}) %collective-permute-start.14) | collective-permute-done | bytes 921632 | tf_op jit(solution)/shard_map/ppermute | solution.py:427
  139.7 1.7 collective-permute-start.26
  141.4 18.0 %collective-permute-done.15.rest_11_ = bf16[6,8,9600]{2,1,0:T(8,128)(2,1)S(1)} collective-permute-done((bf16[6,8,9600]{2,1,0:T(8,128)(2,1)}, bf16[6,8,9600]{2,1,0:T(8,128)(2,1)S(1)}, u32[]{:S(2)}, u32[]{:S(2)}) %collective-permute-start.15) | collective-permute-done | bytes 921632 | tf_op jit(solution)/shard_map/ppermute | solution.py:427
  159.4 1.7 collective-permute-start.28
  161.2 1.7 collective-permute-start.29
  162.9 0.9 copy-done.28
  164.4 19.3 %phase_0.1.before_ref = f32[16,128]{1,0:T(8,128)} custom-call(s32[176]{0:T(256)} %get-tuple-element.110.rows_ref, s32[176]{0:T(256)} %get-tuple-element.109.vids_ref, s32[1]{0:T(128)} %get-tuple-element.100.count_ref, s32[176,1]{1,0:T(8,128)} %copy.40.entry_ref, bf16[64,2048]{1,0:T(8,128)(2,1)} %copy-done.1, bf16[512,1024]{1,0:T(8,128)(2,1)} %copy-done, ...), custom_call_target="tpu_custom_call" | custom-call | flops 17301504000 | bytes 54067200 | tf_op jit(solution)/shard_map/phase_0/pallas_call | solution.py:207
  183.7 7.1 %collective-permute-start.25 = (bf16[6,8,9600]{2,1,0:T(8,128)(2,1)}, bf16[6,8,9600]{2,1,0:T(8,128)(2,1)}, u32[]{:S(2)}, u32[]{:S(2)}) collective-permute-start(bf16[6,8,9600]{2,1,0:T(8,128)(2,1)} %collective-permute-done.12.rest_6_), channel_id=1, source_target_pairs={{0,8},{1,9},{2,10},{3,11},{4,12},{5,13},{6,14},{7,15},{8,24},{9,25... | collective-permute-start | bytes 2764808 | tf_op jit(solution)/shard_map/ppermute | solution.py:427
  190.7 1.7 collective-permute-start.22
  192.8 2.0 collective-permute-done.28.rest_6_
  194.8 2.0 collective-permute-start.30
  196.8 5.8 %collective-permute-start.34 = (bf16[6,8,9600]{2,1,0:T(8,128)(2,1)}, bf16[6,8,9600]{2,1,0:T(8,128)(2,1)}, u32[]{:S(2)}, u32[]{:S(2)}) collective-permute-start(bf16[6,8,9600]{2,1,0:T(8,128)(2,1)} %collective-permute-done.19.rest_14_), channel_id=1, source_target_pairs={{0,2},{1,3},{2,0},{3,1},{4,6},{5,7},{6,4},{7,5},{8,10},{9,11},{10,... | collective-permute-start | bytes 2764808 | tf_op jit(solution)/shard_map/ppermute | solution.py:427
  202.5 11.7 %collective-permute-done.25.rest_3_ = bf16[6,8,9600]{2,1,0:T(8,128)(2,1)} collective-permute-done((bf16[6,8,9600]{2,1,0:T(8,128)(2,1)}, bf16[6,8,9600]{2,1,0:T(8,128)(2,1)}, u32[]{:S(2)}, u32[]{:S(2)}) %collective-permute-start.25) | collective-permute-done | bytes 921632 | tf_op jit(solution)/shard_map/ppermute | solution.py:427
  214.4 8.6 %collective-permute-start.24 = (bf16[6,8,9600]{2,1,0:T(8,128)(2,1)}, bf16[6,8,9600]{2,1,0:T(8,128)(2,1)}, u32[]{:S(2)}, u32[]{:S(2)}) collective-permute-start(bf16[6,8,9600]{2,1,0:T(8,128)(2,1)} %collective-permute-done.12.rest_6_), channel_id=1, source_target_pairs={{0,4},{1,5},{2,6},{3,7},{4,0},{5,1},{6,2},{7,3},{8,12},{9,13},{10,... | collective-permute-start | bytes 2764808 | tf_op jit(solution)/shard_map/ppermute | solution.py:427
  224.9 9.3 %collective-permute-done.23.rest_1_ = bf16[6,8,9600]{2,1,0:T(8,128)(2,1)} collective-permute-done((bf16[6,8,9600]{2,1,0:T(8,128)(2,1)}, bf16[6,8,9600]{2,1,0:T(8,128)(2,1)}, u32[]{:S(2)}, u32[]{:S(2)}) %collective-permute-start.23) | collective-permute-done | bytes 921632 | tf_op jit(solution)/shard_map/ppermute | solution.py:427
  234.2 1.0 collective-permute-start.37
  236.6 1.2 dynamic-slice_select_fusion.3
  237.7 1.7 collective-permute-start.32
  239.4 9.0 %collective-permute-start.36 = (bf16[6,8,9600]{2,1,0:T(8,128)(2,1)}, bf16[6,8,9600]{2,1,0:T(8,128)(2,1)}, u32[]{:S(2)}, u32[]{:S(2)}) collective-permute-start(bf16[6,8,9600]{2,1,0:T(8,128)(2,1)} %collective-permute-done.30.rest_7_), channel_id=1, source_target_pairs={{0,2},{1,3},{2,0},{3,1},{4,6},{5,7},{6,4},{7,5},{8,10},{9,11},{10,... | collective-permute-start | bytes 2764808 | tf_op jit(solution)/shard_map/ppermute | solution.py:427
  248.4 4.5 %collective-permute-done.24.rest_2_ = bf16[6,8,9600]{2,1,0:T(8,128)(2,1)} collective-permute-done((bf16[6,8,9600]{2,1,0:T(8,128)(2,1)}, bf16[6,8,9600]{2,1,0:T(8,128)(2,1)}, u32[]{:S(2)}, u32[]{:S(2)}) %collective-permute-start.24) | collective-permute-done | bytes 921632 | tf_op jit(solution)/shard_map/ppermute | solution.py:427
  252.9 10.1 %collective-permute-start.35 = (bf16[6,8,9600]{2,1,0:T(8,128)(2,1)}, bf16[6,8,9600]{2,1,0:T(8,128)(2,1)}, u32[]{:S(2)}, u32[]{:S(2)}) collective-permute-start(bf16[6,8,9600]{2,1,0:T(8,128)(2,1)} %collective-permute-done.20.rest_15_), channel_id=1, source_target_pairs={{0,2},{1,3},{2,0},{3,1},{4,6},{5,7},{6,4},{7,5},{8,10},{9,11},{10,... | collective-permute-start | bytes 2764808 | tf_op jit(solution)/shard_map/ppermute | solution.py:427
  263.0 18.4 %phase_1.1.before_ref = f32[16,128]{1,0:T(8,128)} custom-call(s32[112]{0:T(128)} %get-tuple-element.112.rows_ref, s32[112]{0:T(128)} %get-tuple-element.111.vids_ref, s32[1]{0:T(128)} %get-tuple-element.101.count_ref, s32[112,1]{1,0:T(8,128)} %copy.41.entry_ref, bf16[64,2048]{1,0:T(8,128)(2,1)} %copy-done.1, bf16[512,1024]{1,0:T(8,128)(2,1)} %copy-done, ...), custom_call_target="tpu_custom_call" | custom-call | flops 11010048000 | bytes 34406400 | tf_op jit(solution)/shard_map/phase_1/pallas_call | solution.py:207
  281.5 2.0 collective-permute-start.33
  286.9 1.3 dynamic-slice_select_fusion.5
  288.2 6.9 %collective-permute-done.31.rest_0_ = bf16[6,8,9600]{2,1,0:T(8,128)(2,1)S(1)} collective-permute-done((bf16[6,8,9600]{2,1,0:T(8,128)(2,1)}, bf16[6,8,9600]{2,1,0:T(8,128)(2,1)S(1)}, u32[]{:S(2)}, u32[]{:S(2)}) %collective-permute-start.31) | collective-permute-done | bytes 921632 | tf_op jit(solution)/shard_map/ppermute | solution.py:427
  295.1 10.0 %collective-permute-done.33.rest_1_ = bf16[6,8,9600]{2,1,0:T(8,128)(2,1)} collective-permute-done((bf16[6,8,9600]{2,1,0:T(8,128)(2,1)}, bf16[6,8,9600]{2,1,0:T(8,128)(2,1)}, u32[]{:S(2)}, u32[]{:S(2)}) %collective-permute-start.33) | collective-permute-done | bytes 921632 | tf_op jit(solution)/shard_map/ppermute | solution.py:427
  305.1 14.9 %phase_2.1.before_ref = f32[16,128]{1,0:T(8,128)} custom-call(s32[96]{0:T(128)} %get-tuple-element.114.rows_ref, s32[96]{0:T(128)} %get-tuple-element.113.vids_ref, s32[1]{0:T(128)} %get-tuple-element.102.count_ref, s32[96,1]{1,0:T(8,128)} %copy.42.entry_ref, bf16[64,2048]{1,0:T(8,128)(2,1)} %copy-done.1, bf16[512,1024]{1,0:T(8,128)(2,1)} %copy-done, ...), custom_call_target="tpu_custom_call" | custom-call | flops 9437184000 | bytes 29491200 | tf_op jit(solution)/shard_map/phase_2/pallas_call | solution.py:207
  320.1 7.7 %collective-permute-start.40 = (bf16[6,8,9600]{2,1,0:T(8,128)(2,1)}, bf16[6,8,9600]{2,1,0:T(8,128)(2,1)}, u32[]{:S(2)}, u32[]{:S(2)}) collective-permute-start(bf16[6,8,9600]{2,1,0:T(8,128)(2,1)} %collective-permute-done.32.rest_5_), channel_id=1, source_target_pairs={{0,2},{1,3},{2,0},{3,1},{4,6},{5,7},{6,4},{7,5},{8,10},{9,11},{10,... | collective-permute-start | bytes 2764808 | tf_op jit(solution)/shard_map/ppermute | solution.py:427
  327.8 5.7 %collective-permute-start.39 = (bf16[6,8,9600]{2,1,0:T(8,128)(2,1)S(1)}, bf16[6,8,9600]{2,1,0:T(8,128)(2,1)}, u32[]{:S(2)}, u32[]{:S(2)}) collective-permute-start(bf16[6,8,9600]{2,1,0:T(8,128)(2,1)S(1)} %copy-done.12), channel_id=1, source_target_pairs={{0,4},{1,5},{2,6},{3,7},{4,0},{5,1},{6,2},{7,3},{8,12},{9,13},{10,... | collective-permute-start | bytes 2764808 | tf_op jit(solution)/shard_map/ppermute | solution.py:427
  337.0 1.2 dynamic-slice_select_fusion.7
  338.2 1.3 collective-permute-done.40.rest_1_
  339.5 5.5 %collective-permute-done.39.rest_0_ = bf16[6,8,9600]{2,1,0:T(8,128)(2,1)} collective-permute-done((bf16[6,8,9600]{2,1,0:T(8,128)(2,1)S(1)}, bf16[6,8,9600]{2,1,0:T(8,128)(2,1)}, u32[]{:S(2)}, u32[]{:S(2)}) %collective-permute-start.39) | collective-permute-done | bytes 921632 | tf_op jit(solution)/shard_map/ppermute | solution.py:427
  345.1 1.0 copy-done.8
  346.1 10.6 %phase_3.1 = f32[16,128]{1,0:T(8,128)} custom-call(s32[64]{0:T(128)} %get-tuple-element.116.rows_ref, s32[64]{0:T(128)} %get-tuple-element.115.vids_ref, s32[1]{0:T(128)} %get-tuple-element.103.count_ref, s32[64,1]{1,0:T(8,128)} %copy.43.entry_ref, bf16[64,2048]{1,0:T(8,128)(2,1)} %copy-done.1, bf16[512,1024]{1,0:T(8,128)(2,1)} %copy-done, ...), custom_call_target="tpu_custom_call" | custom-call | flops 6291456000 | bytes 19660800 | tf_op jit(solution)/shard_map/phase_3/pallas_call | solution.py:207
  357.5 15.0 %all_to_all.15 = f32[32,1,128]{2,1,0:T(1,128)S(1)} all-to-all(f32[32,1,128]{2,1,0:T(1,128)S(1)} %broadcast_select_fusion), channel_id=1, replica_groups=mesh['shard'=32] {'shard'}, dimensions={0} | all-to-all | bytes 32768 | tf_op jit(solution)/shard_map/all_to_all | solution.py:433
  (133 shorter events, 16.7 us)
Async XLA Ops:
  0.0 95.4 %collective-permute-start = (bf16[128,8,9600]{2,1,0:T(8,128)(2,1)}, bf16[128,8,9600]{2,1,0:T(8,128)(2,1)}, u32[]{:S(2)}, u32[]{:S(2)}) collective-permute-start(bf16[128,8,9600]{2,1,0:T(8,128)(2,1)} %own_hbm.7), channel_id=1, source_target_pairs={{0,1},{1,0},{2,3},{3,2},{4,5},{5,4},{6,7},{7,6},{8,9},{9,8},{10,11... | collective-permute-start | bytes 58982408 | tf_op jit(solution)/shard_map/ppermute | solution.py:332
  1.9 27.5 %all-to-all-start = ((s32[32,1,128]{2,1,0:T(1,128)}), s32[32,1,128]{2,1,0:T(1,128)S(1)}, u32[]{:S(2)}, u32[]{:S(2)}) async-start(s32[32,1,128]{2,1,0:T(1,128)} %broadcast_in_dim.92), calls=%async_computation | async-start | bytes 32768 | tf_op jit(solution)/shard_map/all_to_all | solution.py:328
  10.5 68.6 %copy-start.10 = (bf16[6,8,9600]{2,1,0:T(8,128)(2,1)}, bf16[6,8,9600]{2,1,0:T(8,128)(2,1)S(1)}, u32[]{:S(2)}) copy-start(bf16[6,8,9600]{2,1,0:T(8,128)(2,1)S(1)} %get-tuple-element.58.rest_0_) | copy-start | bytes 2764804
  10.5 105.8 %copy-start.9 = (bf16[6,8,9600]{2,1,0:T(8,128)(2,1)}, bf16[6,8,9600]{2,1,0:T(8,128)(2,1)S(1)}, u32[]{:S(2)}) copy-start(bf16[6,8,9600]{2,1,0:T(8,128)(2,1)S(1)} %get-tuple-element.66.rest_8_) | copy-start | bytes 2764804
  10.5 22.7 %copy-start.22 = (bf16[32,1,3,3]{0,3,2,1:T(4,128)(2,1)S(1)}, bf16[32,1,3,3]{0,3,2,1:T(4,128)(2,1)}, u32[]{:S(2)}) copy-start(bf16[32,1,3,3]{0,3,2,1:T(4,128)(2,1)} %param.10) | copy-start | bytes 1732
  10.5 22.7 %copy-start.23 = (bf16[1,64,3,3]{1,3,2,0:T(4,128)(2,1)S(1)}, bf16[1,64,3,3]{1,3,2,0:T(4,128)(2,1)}, u32[]{:S(2)}) copy-start(bf16[1,64,3,3]{1,3,2,0:T(4,128)(2,1)} %param.12) | copy-start | bytes 3460
  10.5 31.2 %copy-start.3 = (bf16[64,32,3,3]{0,1,3,2:T(8,128)(2,1)S(1)}, bf16[64,32,3,3]{0,1,3,2:T(8,128)(2,1)}, u32[]{:S(2)}) copy-start(bf16[64,32,3,3]{0,1,3,2:T(8,128)(2,1)} %param.11) | copy-start | bytes 110596
  10.5 43.7 %collective-permute-start.7 = (bf16[6,8,9600]{2,1,0:T(8,128)(2,1)S(1)}, bf16[6,8,9600]{2,1,0:T(8,128)(2,1)}, u32[]{:S(2)}, u32[]{:S(2)}) collective-permute-start(bf16[6,8,9600]{2,1,0:T(8,128)(2,1)S(1)} %get-tuple-element.58.rest_0_), channel_id=1, source_target_pairs={{0,8},{1,9},{2,10},{3,11},{4,12},{5,13},{6,14},{7,15},{8,24},{9,25... | collective-permute-start | bytes 2764808 | tf_op jit(solution)/shard_map/ppermute | solution.py:427
  13.5 82.9 %copy-start.6 = (bf16[2,8,9600]{2,1,0:T(8,128)(2,1)}, bf16[2,8,9600]{2,1,0:T(8,128)(2,1)S(1)}, u32[]{:S(2)}) copy-start(bf16[2,8,9600]{2,1,0:T(8,128)(2,1)S(1)} %get-tuple-element.56.rest_16_) | copy-start | bytes 921604
  13.5 108.0 %copy-start.7 = (bf16[2,8,9600]{2,1,0:T(8,128)(2,1)}, bf16[2,8,9600]{2,1,0:T(8,128)(2,1)S(1)}, u32[]{:S(2)}) copy-start(bf16[2,8,9600]{2,1,0:T(8,128)(2,1)S(1)} %get-tuple-element.54.rest_21_) | copy-start | bytes 921604
  13.5 19.7 %collective-permute-start.8 = (bf16[2,8,9600]{2,1,0:T(8,128)(2,1)S(1)}, bf16[2,8,9600]{2,1,0:T(8,128)(2,1)S(1)}, u32[]{:S(2)}, u32[]{:S(2)}) collective-permute-start(bf16[2,8,9600]{2,1,0:T(8,128)(2,1)S(1)} %get-tuple-element.54.rest_21_), channel_id=1, source_target_pairs={{0,4},{1,5},{2,6},{3,7},{4,0},{5,1},{6,2},{7,3},{8,12},{9,13},{10,... | collective-permute-start | bytes 921608 | tf_op jit(solution)/shard_map/ppermute | solution.py:427
  15.0 20.0 %collective-permute-start.9 = (bf16[2,8,9600]{2,1,0:T(8,128)(2,1)S(1)}, bf16[2,8,9600]{2,1,0:T(8,128)(2,1)S(1)}, u32[]{:S(2)}, u32[]{:S(2)}) collective-permute-start(bf16[2,8,9600]{2,1,0:T(8,128)(2,1)S(1)} %get-tuple-element.56.rest_16_), channel_id=1, source_target_pairs={{0,2},{1,3},{2,0},{3,1},{4,6},{5,7},{6,4},{7,5},{8,10},{9,11},{10,... | collective-permute-start | bytes 921608 | tf_op jit(solution)/shard_map/ppermute | solution.py:427
  29.5 10.5 %collective-permute-start.1 = (bf16[2,8,9600]{2,1,0:T(8,128)(2,1)S(1)}, bf16[2,8,9600]{2,1,0:T(8,128)(2,1)}, u32[]{:S(2)}, u32[]{:S(2)}) collective-permute-start(bf16[2,8,9600]{2,1,0:T(8,128)(2,1)S(1)} %get-tuple-element.54.rest_21_), channel_id=1, source_target_pairs={{0,2},{1,3},{2,0},{3,1},{4,6},{5,7},{6,4},{7,5},{8,10},{9,11},{10,... | collective-permute-start | bytes 921608 | tf_op jit(solution)/shard_map/ppermute | solution.py:427
  33.2 88.3 %copy-start.16 = (bf16[2,8,9600]{2,1,0:T(8,128)(2,1)}, bf16[2,8,9600]{2,1,0:T(8,128)(2,1)S(1)}, u32[]{:S(2)}) copy-start(bf16[2,8,9600]{2,1,0:T(8,128)(2,1)S(1)} %collective-permute-done.8.rest_23_) | copy-start | bytes 921604
  33.2 19.4 %collective-permute-start.3 = (bf16[2,8,9600]{2,1,0:T(8,128)(2,1)S(1)}, bf16[2,8,9600]{2,1,0:T(8,128)(2,1)S(1)}, u32[]{:S(2)}, u32[]{:S(2)}) collective-permute-start(bf16[2,8,9600]{2,1,0:T(8,128)(2,1)S(1)} %get-tuple-element.56.rest_16_), channel_id=1, source_target_pairs={{0,4},{1,5},{2,6},{3,7},{4,0},{5,1},{6,2},{7,3},{8,12},{9,13},{10,... | collective-permute-start | bytes 921608 | tf_op jit(solution)/shard_map/ppermute | solution.py:427
  35.0 61.4 %copy-start.17 = (bf16[2,8,9600]{2,1,0:T(8,128)(2,1)}, bf16[2,8,9600]{2,1,0:T(8,128)(2,1)S(1)}, u32[]{:S(2)}) copy-start(bf16[2,8,9600]{2,1,0:T(8,128)(2,1)S(1)} %collective-permute-done.9.rest_17_) | copy-start | bytes 921604
  35.0 19.8 %collective-permute-start.17 = (bf16[2,8,9600]{2,1,0:T(8,128)(2,1)S(1)}, bf16[2,8,9600]{2,1,0:T(8,128)(2,1)S(1)}, u32[]{:S(2)}, u32[]{:S(2)}) collective-permute-start(bf16[2,8,9600]{2,1,0:T(8,128)(2,1)S(1)} %collective-permute-done.9.rest_17_), channel_id=1, source_target_pairs={{0,4},{1,5},{2,6},{3,7},{4,0},{5,1},{6,2},{7,3},{8,12},{9,13},{10,... | collective-permute-start | bytes 921608 | tf_op jit(solution)/shard_map/ppermute | solution.py:427
  40.0 16.5 %collective-permute-start.10 = (bf16[2,8,9600]{2,1,0:T(8,128)(2,1)S(1)}, bf16[2,8,9600]{2,1,0:T(8,128)(2,1)S(1)}, u32[]{:S(2)}, u32[]{:S(2)}) collective-permute-start(bf16[2,8,9600]{2,1,0:T(8,128)(2,1)S(1)} %collective-permute-done.8.rest_23_), channel_id=1, source_target_pairs={{0,2},{1,3},{2,0},{3,1},{4,6},{5,7},{6,4},{7,5},{8,10},{9,11},{10,... | collective-permute-start | bytes 921608 | tf_op jit(solution)/shard_map/ppermute | solution.py:427
  41.7 21.7 %copy-start.24 = (pred[432]{0:T(512)(128)(4,1)S(1)}, pred[432]{0:T(512)(128)(4,1)}, u32[]{:S(2)}) copy-start(pred[432]{0:T(512)(128)(4,1)} %constant.119.clone.1) | copy-start | bytes 1300
  52.6 67.6 %copy-start.18 = (bf16[2,8,9600]{2,1,0:T(8,128)(2,1)}, bf16[2,8,9600]{2,1,0:T(8,128)(2,1)S(1)}, u32[]{:S(2)}) copy-start(bf16[2,8,9600]{2,1,0:T(8,128)(2,1)S(1)} %collective-permute-done.3.rest_18_) | copy-start | bytes 921604
  52.6 24.4 %collective-permute-start.16 = (bf16[6,8,9600]{2,1,0:T(8,128)(2,1)S(1)}, bf16[6,8,9600]{2,1,0:T(8,128)(2,1)}, u32[]{:S(2)}, u32[]{:S(2)}) collective-permute-start(bf16[6,8,9600]{2,1,0:T(8,128)(2,1)S(1)} %get-tuple-element.66.rest_8_), channel_id=1, source_target_pairs={{0,8},{1,9},{2,10},{3,11},{4,12},{5,13},{6,14},{7,15},{8,24},{9,25... | collective-permute-start | bytes 2764808 | tf_op jit(solution)/shard_map/ppermute | solution.py:427
  54.3 24.9 %collective-permute-start.2 = (bf16[6,8,9600]{2,1,0:T(8,128)(2,1)S(1)}, bf16[6,8,9600]{2,1,0:T(8,128)(2,1)}, u32[]{:S(2)}, u32[]{:S(2)}) collective-permute-start(bf16[6,8,9600]{2,1,0:T(8,128)(2,1)S(1)} %get-tuple-element.58.rest_0_), channel_id=1, source_target_pairs={{0,2},{1,3},{2,0},{3,1},{4,6},{5,7},{6,4},{7,5},{8,10},{9,11},{10,... | collective-permute-start | bytes 2764808 | tf_op jit(solution)/shard_map/ppermute | solution.py:427
  54.8 22.5 %collective-permute-start.4 = (bf16[6,8,9600]{2,1,0:T(8,128)(2,1)S(1)}, bf16[6,8,9600]{2,1,0:T(8,128)(2,1)}, u32[]{:S(2)}, u32[]{:S(2)}) collective-permute-start(bf16[6,8,9600]{2,1,0:T(8,128)(2,1)S(1)} %get-tuple-element.66.rest_8_), channel_id=1, source_target_pairs={{0,4},{1,5},{2,6},{3,7},{4,0},{5,1},{6,2},{7,3},{8,12},{9,13},{10,... | collective-permute-start | bytes 2764808 | tf_op jit(solution)/shard_map/ppermute | solution.py:427
  56.5 38.5 %collective-permute-start.12 = (bf16[6,8,9600]{2,1,0:T(8,128)(2,1)}, bf16[6,8,9600]{2,1,0:T(8,128)(2,1)}, u32[]{:S(2)}, u32[]{:S(2)}) collective-permute-start(bf16[6,8,9600]{2,1,0:T(8,128)(2,1)} %collective-permute-done.7.rest_4_), channel_id=1, source_target_pairs={{0,8},{1,9},{2,10},{3,11},{4,12},{5,13},{6,14},{7,15},{8,24},{9,25... | collective-permute-start | bytes 2764808 | tf_op jit(solution)/shard_map/ppermute | solution.py:427
  68.5 53.0 %copy-start.21 = (bf16[2,8,9600]{2,1,0:T(8,128)(2,1)S(1)}, bf16[2,8,9600]{2,1,0:T(8,128)(2,1)}, u32[]{:S(2)}) copy-start(bf16[2,8,9600]{2,1,0:T(8,128)(2,1)} %copy-done.20) | copy-start | bytes 921604
  77.1 20.4 %collective-permute-start.11 = (bf16[6,8,9600]{2,1,0:T(8,128)(2,1)}, bf16[6,8,9600]{2,1,0:T(8,128)(2,1)}, u32[]{:S(2)}, u32[]{:S(2)}) collective-permute-start(bf16[6,8,9600]{2,1,0:T(8,128)(2,1)} %collective-permute-done.7.rest_4_), channel_id=1, source_target_pairs={{0,2},{1,3},{2,0},{3,1},{4,6},{5,7},{6,4},{7,5},{8,10},{9,11},{10,... | collective-permute-start | bytes 2764808 | tf_op jit(solution)/shard_map/ppermute | solution.py:427
  77.3 42.8 %collective-permute-start.18 = (bf16[6,8,9600]{2,1,0:T(8,128)(2,1)}, bf16[6,8,9600]{2,1,0:T(8,128)(2,1)}, u32[]{:S(2)}, u32[]{:S(2)}) collective-permute-start(bf16[6,8,9600]{2,1,0:T(8,128)(2,1)} %collective-permute-done.16.rest_12_), channel_id=1, source_target_pairs={{0,4},{1,5},{2,6},{3,7},{4,0},{5,1},{6,2},{7,3},{8,12},{9,13},{10,... | collective-permute-start | bytes 2764808 | tf_op jit(solution)/shard_map/ppermute | solution.py:427
  79.1 37.2 %collective-permute-start.5 = (bf16[6,8,9600]{2,1,0:T(8,128)(2,1)S(1)}, bf16[6,8,9600]{2,1,0:T(8,128)(2,1)S(1)}, u32[]{:S(2)}, u32[]{:S(2)}) collective-permute-start(bf16[6,8,9600]{2,1,0:T(8,128)(2,1)S(1)} %get-tuple-element.58.rest_0_), channel_id=1, source_target_pairs={{0,4},{1,5},{2,6},{3,7},{4,0},{5,1},{6,2},{7,3},{8,12},{9,13},{10,... | collective-permute-start | bytes 2764808 | tf_op jit(solution)/shard_map/ppermute | solution.py:427
  94.9 23.1 %collective-permute-start.13 = (bf16[6,8,9600]{2,1,0:T(8,128)(2,1)}, bf16[6,8,9600]{2,1,0:T(8,128)(2,1)}, u32[]{:S(2)}, u32[]{:S(2)}) collective-permute-start(bf16[6,8,9600]{2,1,0:T(8,128)(2,1)} %collective-permute-done.12.rest_6_), channel_id=1, source_target_pairs={{0,2},{1,3},{2,0},{3,1},{4,6},{5,7},{6,4},{7,5},{8,10},{9,11},{10,... | collective-permute-start | bytes 2764808 | tf_op jit(solution)/shard_map/ppermute | solution.py:427
  95.4 24.8 %collective-permute-start.19 = (bf16[6,8,9600]{2,1,0:T(8,128)(2,1)}, bf16[6,8,9600]{2,1,0:T(8,128)(2,1)}, u32[]{:S(2)}, u32[]{:S(2)}) collective-permute-start(bf16[6,8,9600]{2,1,0:T(8,128)(2,1)} %collective-permute-done.16.rest_12_), channel_id=1, source_target_pairs={{0,8},{1,9},{2,10},{3,11},{4,12},{5,13},{6,14},{7,15},{8,24},{9,25... | collective-permute-start | bytes 2764808 | tf_op jit(solution)/shard_map/ppermute | solution.py:427
  97.5 63.7 %collective-permute-start.21 = (bf16[8,8,9600]{2,1,0:T(8,128)(2,1)S(1)}, bf16[8,8,9600]{2,1,0:T(8,128)(2,1)S(1)}, u32[]{:S(2)}, u32[]{:S(2)}) collective-permute-start(bf16[8,8,9600]{2,1,0:T(8,128)(2,1)S(1)} %pad_maximum_fusion), channel_id=1, source_target_pairs={{0,8},{1,9},{2,10},{3,11},{4,12},{5,13},{6,14},{7,15},{8,24},{9,25... | collective-permute-start | bytes 3686408 | tf_op jit(solution)/shard_map/ppermute | solution.py:427
  116.3 6.3 %copy-start.26 = (bf16[6,8,9600]{2,1,0:T(8,128)(2,1)}, bf16[6,8,9600]{2,1,0:T(8,128)(2,1)S(1)}, u32[]{:S(2)}) copy-start(bf16[6,8,9600]{2,1,0:T(8,128)(2,1)S(1)} %collective-permute-done.5.rest_2_) | copy-start | bytes 2764804
  116.3 23.4 %collective-permute-start.14 = (bf16[6,8,9600]{2,1,0:T(8,128)(2,1)S(1)}, bf16[6,8,9600]{2,1,0:T(8,128)(2,1)S(1)}, u32[]{:S(2)}, u32[]{:S(2)}) collective-permute-start(bf16[6,8,9600]{2,1,0:T(8,128)(2,1)S(1)} %get-tuple-element.66.rest_8_), channel_id=1, source_target_pairs={{0,2},{1,3},{2,0},{3,1},{4,6},{5,7},{6,4},{7,5},{8,10},{9,11},{10,... | collective-permute-start | bytes 2764808 | tf_op jit(solution)/shard_map/ppermute | solution.py:427
  118.0 44.9 %collective-permute-start.6 = (bf16[6,8,9600]{2,1,0:T(8,128)(2,1)}, bf16[6,8,9600]{2,1,0:T(8,128)(2,1)S(1)}, u32[]{:S(2)}, u32[]{:S(2)}) collective-permute-start(bf16[6,8,9600]{2,1,0:T(8,128)(2,1)} %collective-permute-done.2.rest_1_), channel_id=1, source_target_pairs={{0,4},{1,5},{2,6},{3,7},{4,0},{5,1},{6,2},{7,3},{8,12},{9,13},{10,... | collective-permute-start | bytes 2764808 | tf_op jit(solution)/shard_map/ppermute | solution.py:427
  120.1 39.3 %collective-permute-start.15 = (bf16[6,8,9600]{2,1,0:T(8,128)(2,1)}, bf16[6,8,9600]{2,1,0:T(8,128)(2,1)S(1)}, u32[]{:S(2)}, u32[]{:S(2)}) collective-permute-start(bf16[6,8,9600]{2,1,0:T(8,128)(2,1)} %collective-permute-done.4.rest_10_), channel_id=1, source_target_pairs={{0,2},{1,3},{2,0},{3,1},{4,6},{5,7},{6,4},{7,5},{8,10},{9,11},{10,... | collective-permute-start | bytes 2764808 | tf_op jit(solution)/shard_map/ppermute | solution.py:427
  120.2 42.7 %collective-permute-start.20 = (bf16[6,8,9600]{2,1,0:T(8,128)(2,1)}, bf16[6,8,9600]{2,1,0:T(8,128)(2,1)}, u32[]{:S(2)}, u32[]{:S(2)}) collective-permute-start(bf16[6,8,9600]{2,1,0:T(8,128)(2,1)} %collective-permute-done.19.rest_14_), channel_id=1, source_target_pairs={{0,4},{1,5},{2,6},{3,7},{4,0},{5,1},{6,2},{7,3},{8,12},{9,13},{10,... | collective-permute-start | bytes 2764808 | tf_op jit(solution)/shard_map/ppermute | solution.py:427
  139.7 23.2 %copy-start.27 = (bf16[6,8,9600]{2,1,0:T(8,128)(2,1)}, bf16[6,8,9600]{2,1,0:T(8,128)(2,1)S(1)}, u32[]{:S(2)}) copy-start(bf16[6,8,9600]{2,1,0:T(8,128)(2,1)S(1)} %collective-permute-done.14.rest_9_) | copy-start | bytes 2764804
  139.7 57.1 %collective-permute-start.26 = (bf16[6,8,9600]{2,1,0:T(8,128)(2,1)}, bf16[6,8,9600]{2,1,0:T(8,128)(2,1)S(1)}, u32[]{:S(2)}, u32[]{:S(2)}) collective-permute-start(bf16[6,8,9600]{2,1,0:T(8,128)(2,1)} %collective-permute-done.16.rest_12_), channel_id=1, source_target_pairs={{0,2},{1,3},{2,0},{3,1},{4,6},{5,7},{6,4},{7,5},{8,10},{9,11},{10,... | collective-permute-start | bytes 2764808 | tf_op jit(solution)/shard_map/ppermute | solution.py:427
  159.4 35.3 %collective-permute-start.28 = (bf16[6,8,9600]{2,1,0:T(8,128)(2,1)}, bf16[6,8,9600]{2,1,0:T(8,128)(2,1)S(1)}, u32[]{:S(2)}, u32[]{:S(2)}) collective-permute-start(bf16[6,8,9600]{2,1,0:T(8,128)(2,1)} %collective-permute-done.18.rest_13_), channel_id=1, source_target_pairs={{0,2},{1,3},{2,0},{3,1},{4,6},{5,7},{6,4},{7,5},{8,10},{9,11},{10,... | collective-permute-start | bytes 2764808 | tf_op jit(solution)/shard_map/ppermute | solution.py:427
  161.2 31.3 %collective-permute-start.29 = (bf16[8,8,9600]{2,1,0:T(8,128)(2,1)S(1)}, bf16[8,8,9600]{2,1,0:T(8,128)(2,1)S(1)}, u32[]{:S(2)}, u32[]{:S(2)}) collective-permute-start(bf16[8,8,9600]{2,1,0:T(8,128)(2,1)S(1)} %pad_maximum_fusion.1), channel_id=1, source_target_pairs={{0,8},{1,9},{2,10},{3,11},{4,12},{5,13},{6,14},{7,15},{8,24},{9,25... | collective-permute-start | bytes 3686408 | tf_op jit(solution)/shard_map/ppermute | solution.py:427
  183.7 30.6 %collective-permute-start.25 = (bf16[6,8,9600]{2,1,0:T(8,128)(2,1)}, bf16[6,8,9600]{2,1,0:T(8,128)(2,1)}, u32[]{:S(2)}, u32[]{:S(2)}) collective-permute-start(bf16[6,8,9600]{2,1,0:T(8,128)(2,1)} %collective-permute-done.12.rest_6_), channel_id=1, source_target_pairs={{0,8},{1,9},{2,10},{3,11},{4,12},{5,13},{6,14},{7,15},{8,24},{9,25... | collective-permute-start | bytes 2764808 | tf_op jit(solution)/shard_map/ppermute | solution.py:427
  190.7 23.7 %collective-permute-start.22 = (bf16[6,8,9600]{2,1,0:T(8,128)(2,1)}, bf16[6,8,9600]{2,1,0:T(8,128)(2,1)}, u32[]{:S(2)}, u32[]{:S(2)}) collective-permute-start(bf16[6,8,9600]{2,1,0:T(8,128)(2,1)} %collective-permute-done.7.rest_4_), channel_id=1, source_target_pairs={{0,4},{1,5},{2,6},{3,7},{4,0},{5,1},{6,2},{7,3},{8,12},{9,13},{10,... | collective-permute-start | bytes 2764808 | tf_op jit(solution)/shard_map/ppermute | solution.py:427
  192.4 70.6 %copy-start.4 = (bf16[8,8,9600]{2,1,0:T(8,128)(2,1)}, bf16[8,8,9600]{2,1,0:T(8,128)(2,1)S(1)}, u32[]{:S(2)}) copy-start(bf16[8,8,9600]{2,1,0:T(8,128)(2,1)S(1)} %collective-permute-done.29.rest_8_) | copy-start | bytes 3686404
  192.4 41.8 %collective-permute-start.23 = (bf16[6,8,9600]{2,1,0:T(8,128)(2,1)}, bf16[6,8,9600]{2,1,0:T(8,128)(2,1)}, u32[]{:S(2)}, u32[]{:S(2)}) collective-permute-start(bf16[6,8,9600]{2,1,0:T(8,128)(2,1)} %collective-permute-done.11.rest_5_), channel_id=1, source_target_pairs={{0,4},{1,5},{2,6},{3,7},{4,0},{5,1},{6,2},{7,3},{8,12},{9,13},{10,... | collective-permute-start | bytes 2764808 | tf_op jit(solution)/shard_map/ppermute | solution.py:427
  194.8 30.1 %copy-start.14 = (bf16[6,8,9600]{2,1,0:T(8,128)(2,1)}, bf16[6,8,9600]{2,1,0:T(8,128)(2,1)S(1)}, u32[]{:S(2)}) copy-start(bf16[6,8,9600]{2,1,0:T(8,128)(2,1)S(1)} %collective-permute-done.28.rest_6_) | copy-start | bytes 2764804
  194.8 43.0 %collective-permute-start.30 = (bf16[6,8,9600]{2,1,0:T(8,128)(2,1)}, bf16[6,8,9600]{2,1,0:T(8,128)(2,1)}, u32[]{:S(2)}, u32[]{:S(2)}) collective-permute-start(bf16[6,8,9600]{2,1,0:T(8,128)(2,1)} %collective-permute-done.19.rest_14_), channel_id=1, source_target_pairs={{0,8},{1,9},{2,10},{3,11},{4,12},{5,13},{6,14},{7,15},{8,24},{9,25... | collective-permute-start | bytes 2764808 | tf_op jit(solution)/shard_map/ppermute | solution.py:427
  196.8 42.6 %collective-permute-start.34 = (bf16[6,8,9600]{2,1,0:T(8,128)(2,1)}, bf16[6,8,9600]{2,1,0:T(8,128)(2,1)}, u32[]{:S(2)}, u32[]{:S(2)}) collective-permute-start(bf16[6,8,9600]{2,1,0:T(8,128)(2,1)} %collective-permute-done.19.rest_14_), channel_id=1, source_target_pairs={{0,2},{1,3},{2,0},{3,1},{4,6},{5,7},{6,4},{7,5},{8,10},{9,11},{10,... | collective-permute-start | bytes 2764808 | tf_op jit(solution)/shard_map/ppermute | solution.py:427
  214.2 34.1 %collective-permute-start.27 = (bf16[6,8,9600]{2,1,0:T(8,128)(2,1)}, bf16[6,8,9600]{2,1,0:T(8,128)(2,1)S(1)}, u32[]{:S(2)}, u32[]{:S(2)}) collective-permute-start(bf16[6,8,9600]{2,1,0:T(8,128)(2,1)} %collective-permute-done.25.rest_3_), channel_id=1, source_target_pairs={{0,2},{1,3},{2,0},{3,1},{4,6},{5,7},{6,4},{7,5},{8,10},{9,11},{10,... | collective-permute-start | bytes 2764808 | tf_op jit(solution)/shard_map/ppermute | solution.py:427
  214.4 38.5 %collective-permute-start.24 = (bf16[6,8,9600]{2,1,0:T(8,128)(2,1)}, bf16[6,8,9600]{2,1,0:T(8,128)(2,1)}, u32[]{:S(2)}, u32[]{:S(2)}) collective-permute-start(bf16[6,8,9600]{2,1,0:T(8,128)(2,1)} %collective-permute-done.12.rest_6_), channel_id=1, source_target_pairs={{0,4},{1,5},{2,6},{3,7},{4,0},{5,1},{6,2},{7,3},{8,12},{9,13},{10,... | collective-permute-start | bytes 2764808 | tf_op jit(solution)/shard_map/ppermute | solution.py:427
  234.2 47.3 %collective-permute-start.37 = (bf16[8,8,9600]{2,1,0:T(8,128)(2,1)}, bf16[8,8,9600]{2,1,0:T(8,128)(2,1)S(1)}, u32[]{:S(2)}, u32[]{:S(2)}) collective-permute-start(bf16[8,8,9600]{2,1,0:T(8,128)(2,1)} %copy-done.25), channel_id=1, source_target_pairs={{0,8},{1,9},{2,10},{3,11},{4,12},{5,13},{6,14},{7,15},{8,24},{9,25... | collective-permute-start | bytes 3686408 | tf_op jit(solution)/shard_map/ppermute | solution.py:427
  237.7 43.7 %collective-permute-start.32 = (bf16[6,8,9600]{2,1,0:T(8,128)(2,1)}, bf16[6,8,9600]{2,1,0:T(8,128)(2,1)}, u32[]{:S(2)}, u32[]{:S(2)}) collective-permute-start(bf16[6,8,9600]{2,1,0:T(8,128)(2,1)} %collective-permute-done.30.rest_7_), channel_id=1, source_target_pairs={{0,4},{1,5},{2,6},{3,7},{4,0},{5,1},{6,2},{7,3},{8,12},{9,13},{10,... | collective-permute-start | bytes 2764808 | tf_op jit(solution)/shard_map/ppermute | solution.py:427
  239.4 48.8 %collective-permute-start.36 = (bf16[6,8,9600]{2,1,0:T(8,128)(2,1)}, bf16[6,8,9600]{2,1,0:T(8,128)(2,1)}, u32[]{:S(2)}, u32[]{:S(2)}) collective-permute-start(bf16[6,8,9600]{2,1,0:T(8,128)(2,1)} %collective-permute-done.30.rest_7_), channel_id=1, source_target_pairs={{0,2},{1,3},{2,0},{3,1},{4,6},{5,7},{6,4},{7,5},{8,10},{9,11},{10,... | collective-permute-start | bytes 2764808 | tf_op jit(solution)/shard_map/ppermute | solution.py:427
  248.4 14.6 %copy-start.11 = (bf16[6,8,9600]{2,1,0:T(8,128)(2,1)}, bf16[6,8,9600]{2,1,0:T(8,128)(2,1)S(1)}, u32[]{:S(2)}) copy-start(bf16[6,8,9600]{2,1,0:T(8,128)(2,1)S(1)} %collective-permute-done.27.rest_4_) | copy-start | bytes 2764804
  248.4 39.8 %collective-permute-start.38 = (bf16[8,8,9600]{2,1,0:T(8,128)(2,1)S(1)}, bf16[8,8,9600]{2,1,0:T(8,128)(2,1)}, u32[]{:S(2)}, u32[]{:S(2)}) collective-permute-start(bf16[8,8,9600]{2,1,0:T(8,128)(2,1)S(1)} %collective-permute-done.29.rest_8_), channel_id=1, source_target_pairs={{0,8},{1,9},{2,10},{3,11},{4,12},{5,13},{6,14},{7,15},{8,24},{9,25... | collective-permute-start | bytes 3686408 | tf_op jit(solution)/shard_map/ppermute | solution.py:427
  252.9 35.3 %collective-permute-start.35 = (bf16[6,8,9600]{2,1,0:T(8,128)(2,1)}, bf16[6,8,9600]{2,1,0:T(8,128)(2,1)}, u32[]{:S(2)}, u32[]{:S(2)}) collective-permute-start(bf16[6,8,9600]{2,1,0:T(8,128)(2,1)} %collective-permute-done.20.rest_15_), channel_id=1, source_target_pairs={{0,2},{1,3},{2,0},{3,1},{4,6},{5,7},{6,4},{7,5},{8,10},{9,11},{10,... | collective-permute-start | bytes 2764808 | tf_op jit(solution)/shard_map/ppermute | solution.py:427
  281.4 13.7 %collective-permute-start.31 = (bf16[6,8,9600]{2,1,0:T(8,128)(2,1)}, bf16[6,8,9600]{2,1,0:T(8,128)(2,1)S(1)}, u32[]{:S(2)}, u32[]{:S(2)}) collective-permute-start(bf16[6,8,9600]{2,1,0:T(8,128)(2,1)} %collective-permute-done.13.rest_7_), channel_id=1, source_target_pairs={{0,4},{1,5},{2,6},{3,7},{4,0},{5,1},{6,2},{7,3},{8,12},{9,13},{10,... | collective-permute-start | bytes 2764808 | tf_op jit(solution)/shard_map/ppermute | solution.py:427
  281.5 23.6 %copy-start.5 = (bf16[8,8,9600]{2,1,0:T(8,128)(2,1)}, bf16[8,8,9600]{2,1,0:T(8,128)(2,1)S(1)}, u32[]{:S(2)}) copy-start(bf16[8,8,9600]{2,1,0:T(8,128)(2,1)S(1)} %collective-permute-done.37.rest_6_) | copy-start | bytes 3686404
  281.5 23.6 %collective-permute-start.33 = (bf16[6,8,9600]{2,1,0:T(8,128)(2,1)}, bf16[6,8,9600]{2,1,0:T(8,128)(2,1)}, u32[]{:S(2)}, u32[]{:S(2)}) collective-permute-start(bf16[6,8,9600]{2,1,0:T(8,128)(2,1)} %collective-permute-done.25.rest_3_), channel_id=1, source_target_pairs={{0,4},{1,5},{2,6},{3,7},{4,0},{5,1},{6,2},{7,3},{8,12},{9,13},{10,... | collective-permute-start | bytes 2764808 | tf_op jit(solution)/shard_map/ppermute | solution.py:427
  288.2 50.0 %collective-permute-start.41 = (bf16[8,8,9600]{2,1,0:T(8,128)(2,1)S(1)}, bf16[8,8,9600]{2,1,0:T(8,128)(2,1)}, u32[]{:S(2)}, u32[]{:S(2)}) collective-permute-start(bf16[8,8,9600]{2,1,0:T(8,128)(2,1)S(1)} %collective-permute-done.37.rest_6_), channel_id=1, source_target_pairs={{0,8},{1,9},{2,10},{3,11},{4,12},{5,13},{6,14},{7,15},{8,24},{9,25... | collective-permute-start | bytes 3686408 | tf_op jit(solution)/shard_map/ppermute | solution.py:427
  295.1 10.0 %copy-start.15 = (bf16[6,8,9600]{2,1,0:T(8,128)(2,1)}, bf16[6,8,9600]{2,1,0:T(8,128)(2,1)S(1)}, u32[]{:S(2)}) copy-start(bf16[6,8,9600]{2,1,0:T(8,128)(2,1)S(1)} %collective-permute-done.31.rest_0_) | copy-start | bytes 2764804
  305.1 22.7 %copy-start.12 = (bf16[6,8,9600]{2,1,0:T(8,128)(2,1)S(1)}, bf16[6,8,9600]{2,1,0:T(8,128)(2,1)}, u32[]{:S(2)}) copy-start(bf16[6,8,9600]{2,1,0:T(8,128)(2,1)} %copy-done.11) | copy-start | bytes 2764804
  320.0 25.1 %collective-permute-start.42 = (bf16[8,8,9600]{2,1,0:T(8,128)(2,1)}, bf16[8,8,9600]{2,1,0:T(8,128)(2,1)S(1)}, u32[]{:S(2)}, u32[]{:S(2)}) collective-permute-start(bf16[8,8,9600]{2,1,0:T(8,128)(2,1)} %collective-permute-done.38.rest_7_), channel_id=1, source_target_pairs={{0,8},{1,9},{2,10},{3,11},{4,12},{5,13},{6,14},{7,15},{8,24},{9,25... | collective-permute-start | bytes 3686408 | tf_op jit(solution)/shard_map/ppermute | solution.py:427
  320.1 19.4 %collective-permute-start.40 = (bf16[6,8,9600]{2,1,0:T(8,128)(2,1)}, bf16[6,8,9600]{2,1,0:T(8,128)(2,1)}, u32[]{:S(2)}, u32[]{:S(2)}) collective-permute-start(bf16[6,8,9600]{2,1,0:T(8,128)(2,1)} %collective-permute-done.32.rest_5_), channel_id=1, source_target_pairs={{0,2},{1,3},{2,0},{3,1},{4,6},{5,7},{6,4},{7,5},{8,10},{9,11},{10,... | collective-permute-start | bytes 2764808 | tf_op jit(solution)/shard_map/ppermute | solution.py:427
  327.8 17.3 %collective-permute-start.39 = (bf16[6,8,9600]{2,1,0:T(8,128)(2,1)S(1)}, bf16[6,8,9600]{2,1,0:T(8,128)(2,1)}, u32[]{:S(2)}, u32[]{:S(2)}) collective-permute-start(bf16[6,8,9600]{2,1,0:T(8,128)(2,1)S(1)} %copy-done.12), channel_id=1, source_target_pairs={{0,4},{1,5},{2,6},{3,7},{4,0},{5,1},{6,2},{7,3},{8,12},{9,13},{10,... | collective-permute-start | bytes 2764808 | tf_op jit(solution)/shard_map/ppermute | solution.py:427
  (10 other events, 20.3 us)

commit v4 on v3

--- a/solution.py
+++ b/solution.py
@@ -13,9 +13,11 @@
 GROUP = 16
 NONE = 1 << 30
 ROUTES = (("zxy", 6), ("zyx", 6), ("xyz", 2), ("yxz", 2))
-PHASE_ENDS = (0.45, 0.7, 0.88, 1.0)
+PHASE_ENDS = (0.3, 0.5, 0.67, 0.82, 1.0)
 IN_FLIGHT = 2
-SLACK = 2.0
+SLACK = 15.0
+HEAD = 64
+WEIGHT = 8
 
 
 def dot(a, b):
@@ -97,27 +99,31 @@
     )(one_w, two_w, three_w)
 
 
-def pair_kernel(frames, buffers, stride, scale, rows_ref, vids_ref, count_ref, entry_ref, one_ref,
+def pair_kernel(frames, buffers, scale, rows_ref, vids_ref, ends_ref, entry_ref, one_ref,
                 two_ref, three_ref, before_ref, own_hbm, other_hbm, *rest):
     q_hbm, rest = rest[:buffers], rest[buffers:]
     out_ref, q_in, v_in, q_rows, v_rows, maps, q_sem, v_sem = rest
     idx_dev = own_hbm.shape[0]
     width = own_hbm.shape[2] // R
     side = GROUP * frames
-    count = count_ref[0]
+    count = ends_ref[buffers - 1]
     groups = (count + GROUP - 1) // GROUP
 
     def fetch(step, slot):
-        def one_pair(p, _):
-            row = rows_ref[step * GROUP + p]
-            vid = vids_ref[step * GROUP + p]
-            buf, row = lax.div(row, stride), lax.rem(row, stride)
-            for b in range(buffers):
-                @pl.when(buf == b)
-                def _():
-                    pltpu.make_async_copy(
-                        q_hbm[b].at[row], q_in.at[slot, p], q_sem.at[slot]
-                    ).start()
+        first = step * GROUP
+        for b in range(buffers):
+            low = 0 if b == 0 else jnp.clip(ends_ref[b - 1] - first, 0, GROUP)
+            high = GROUP if b == buffers - 1 else jnp.clip(ends_ref[b] - first, 0, GROUP)
+
+            def one_query(p, _):
+                pltpu.make_async_copy(
+                    q_hbm[b].at[rows_ref[first + p]], q_in.at[slot, p], q_sem.at[slot]
+                ).start()
+                return 0
+            lax.fori_loop(low, high, one_query, 0)
+
+        def one_video(p, _):
+            vid = vids_ref[first + p]
 
             @pl.when(vid < idx_dev)
             def _():
@@ -129,7 +135,7 @@
                     other_hbm.at[vid - idx_dev], v_in.at[slot, p], v_sem.at[slot]
                 ).start()
             return 0
-        lax.fori_loop(0, GROUP, one_pair, 0)
+        lax.fori_loop(0, GROUP, one_video, 0)
 
     maps[...] = jnp.zeros_like(maps)
 
@@ -151,16 +157,15 @@
             q_rows[pl.ds(r * side, side), :] = q_in[slot, :, :, cols].reshape(side, width)
             v_rows[pl.ds(r * side, side), :] = v_in[slot, :, :, cols].reshape(side, width)
 
-        total = jnp.zeros((side, side), jnp.float32)
-        for r in range(R):
-            sim = lax.dot_general(
-                q_rows[pl.ds(r * side, side), :], v_rows[...], (((1,), (1,)), ((), ())),
-                preferred_element_type=jnp.float32,
-            )
-            best = sim[:, :side]
-            for s in range(1, R):
-                best = jnp.maximum(best, sim[:, s * side:(s + 1) * side])
-            total = total + best
+        sim = lax.dot_general(
+            q_rows[...], v_rows[...], (((1,), (1,)), ((), ())), preferred_element_type=jnp.float32
+        )
+        best = sim[:, :side]
+        for s in range(1, R):
+            best = jnp.maximum(best, sim[:, s * side:(s + 1) * side])
+        total = best[:side]
+        for r in range(1, R):
+            total = total + best[r * side:(r + 1) * side]
         cells = frames * frames
         same_pair = iota((side, side), 0) // frames == iota((side, side), 1) // frames
         lane, sub = iota((side, cells), 1), iota((side, cells), 0)
@@ -181,22 +186,28 @@
             best = jnp.maximum(best, x[:, i * n:(i + 1) * n])
         return jnp.maximum(best, 0.0).astype(jnp.bfloat16)
 
-    first = pooled(dot(maps[...].astype(jnp.bfloat16), one_ref[...]))
-    second = pooled(dot(first, two_ref[...]))
-    final = jnp.clip(dot(second, three_ref[...]), -1.0, 1.0)
-    best = jnp.maximum(final[:, :128], final[:, 128:])
-    score = (best[:, 0:1] + best[:, 1:2]) * 0.5
+    out_ref[...] = before_ref[...]
     senders, pairs = out_ref.shape
-    shape = (score.shape[0], pairs)
-    score = jnp.broadcast_to(score, shape)
-    place = jnp.broadcast_to(entry_ref[...], shape) - iota(shape, 1)
-    for s in range(senders):
-        out_ref[pl.ds(s, 1), :] = before_ref[pl.ds(s, 1), :] + jnp.sum(
-            jnp.where(place == s * pairs, score, 0.0), axis=0, keepdims=True
-        )
-
-
-def pair_scores(blocks, own, other, rows, vids, count, entry, heads, before, stride, name):
+
+    def head(g, _):
+        here = pl.ds(pl.multiple_of(g * HEAD, HEAD), HEAD)
+        first = pooled(dot(maps[here, :].astype(jnp.bfloat16), one_ref[...]))
+        second = pooled(dot(first, two_ref[...]))
+        final = jnp.clip(dot(second, three_ref[...]), -1.0, 1.0)
+        best = jnp.maximum(final[:, :128], final[:, 128:])
+        shape = (HEAD, pairs)
+        score = jnp.broadcast_to((best[:, 0:1] + best[:, 1:2]) * 0.5, shape)
+        place = jnp.broadcast_to(entry_ref[here, :], shape) - iota(shape, 1)
+        for s in range(senders):
+            out_ref[pl.ds(s, 1), :] = out_ref[pl.ds(s, 1), :] + jnp.sum(
+                jnp.where(place == s * pairs, score, 0.0), axis=0, keepdims=True
+            )
+        return 0
+
+    lax.fori_loop(0, (count + HEAD - 1) // HEAD, head, 0)
+
+
+def pair_scores(blocks, own, other, rows, vids, ends, entry, heads, before, name):
     frames, width = own.shape[1], own.shape[2]
     cap = rows.shape[0]
     side = GROUP * frames
@@ -205,7 +216,7 @@
     vmem = pl.BlockSpec(memory_space=pltpu.VMEM)
     hbm = pl.BlockSpec(memory_space=pltpu.HBM)
     return pl.pallas_call(
-        functools.partial(pair_kernel, frames, len(blocks), stride, scale),
+        functools.partial(pair_kernel, frames, len(blocks), scale),
         out_shape=jax.ShapeDtypeStruct(before.shape, jnp.float32),
         in_specs=[smem] * 3 + [vmem] * 5 + [hbm] * (2 + len(blocks)),
         out_specs=vmem,
@@ -220,11 +231,11 @@
         ],
         compiler_params=pltpu.CompilerParams(vmem_limit_bytes=58 * 1024 * 1024),
         cost_estimate=pl.CostEstimate(
-            flops=2 * cap * side * R * R * frames * (width // R),
+            flops=WEIGHT * 2 * cap * side * R * R * frames * (width // R),
             bytes_accessed=cap * frames * width * 4, transcendentals=0,
         ),
         name=name,
-    )(rows, vids, count, entry, *heads, before, own, other, *blocks)
+    )(rows, vids, ends, entry, *heads, before, own, other, *blocks)
 
 
 def chip_places(mesh):
@@ -365,7 +376,7 @@
             for q in range(q_dev):
                 p, b, row = place[off, q]
                 spot[c, s, q] = (p * most + b) * stride + row
-    caps = [-(-c // GROUP) * GROUP for c in caps]
+    caps = [-(-c // HEAD) * HEAD for c in caps]
 
     spot = lax.dynamic_index_in_dim(jnp.asarray(spot), chip, 0, keepdims=False)
     spot = jnp.broadcast_to(spot[:, :, None], (chips, q_dev, k_count)).reshape(chips * pairs)
@@ -394,11 +405,16 @@
     def score(p):
         cut = lambda a: lax.dynamic_slice(a, (firsts[p],), (caps[p],))
         valid = jnp.arange(caps[p]) < counts[p]
-        rows, vid = jnp.where(valid, cut(spots), 0), jnp.where(valid, cut(vids), 0)
+        spot, vid = cut(spots), jnp.where(valid, cut(vids), 0)
+        rows = jnp.where(valid, spot % stride, 0)
         entries = jnp.where(valid, cut(entry), NONE)
+        ends = jnp.sum(
+            (valid[None, :] & (spot[None, :] // stride <= jnp.arange(len(phases[p]))[:, None]))
+            .astype(jnp.int32), axis=1,
+        )
         tables.append(pair_scores(
-            [blocks[k] for k in phases[p]], index_videos, other, rows, vid, counts[p:p + 1],
-            entries.reshape(caps[p], 1), heads, tables[-1], stride, "phase_" + str(p),
+            [blocks[k] for k in phases[p]], index_videos, other, rows, vid, ends,
+            entries.reshape(caps[p], 1), heads, tables[-1], "phase_" + str(p),
         ))
 
     blocks = {}
@@ -414,7 +430,7 @@
     for m in order:
         axis, source, target, _ = m
         behind = done[axis][-IN_FLIGHT:][:1] if len(done[axis]) >= IN_FLIGHT else []
-        if len(done[axis]) == 1:
+        if len(done[axis]) == 4:
             behind.append(all_ids)
         if len(done[axis]) == 3 and axis == 0:
             behind.append(other)

time: 374 us -> 363 us (0.971)
  starting transfers between devices: 105 us -> 65.5 us
  other arithmetic: 15.6 us -> 31.2 us
  waiting for transfers between devices: 142 us -> 152 us
    ppermute x42, starting transfers between devices: 97.9 us -> 58.1 us  [body(): blocks[target] = lax.ppermute(sent, 'shard', steps[axis])]
    ppermute x42, waiting for transfers between devices: 129 us -> 152 us  [body(): blocks[target] = lax.ppermute(sent, 'shard', steps[axis])]
    all_to_all x1, waiting for transfers between devices: 13 us -> 0.01 us  [body(): lax.all_to_all(jnp.broadcast_to(candidates.reshape(1, pairs), (devices, p...]
    select_n x4 -> x9, other arithmetic: 4.92 us -> 11.9 us  [the longest x4 5.56 us: score(): rows = jnp.where(valid, spot % stride, 0)]
    pallas_call x4 -> x5, Pallas kernels: 63.2 us -> 61.6 us  [pair_scores(): pl.pallas_call(functools.partial(pair_kernel, frames, len(blocks), scale)...]
  transfers between devices with their start and end apart: 44 -> 44, of which waited for: 16 -> 20; matrix products, arithmetic and copies ran while one was open for 7% -> 12% of each run, Pallas kernels for 16% -> 17%
where the time goes in v4:
time: 363 us; the launch traced here: 359 us
  waiting for transfers between devices  152 us (42%)
  Pallas kernels  70.2 us (19%)
  starting transfers between devices  65.5 us (18%)
  other arithmetic  31.2 us (9%)
  local copies, waits for them, and re-layouts  17.5 us (5%)
  blocking collectives  12.9 us (4%)
  between operations  10.2 us (3%)
    ppermute x42, waiting for transfers between devices, body(): blocks[target] = lax.ppermute(sent, 'shard', steps[axis])  152 us
    pallas_call x5, Pallas kernels, pair_scores(): pl.pallas_call(functools.partial(pair_kernel, frames, len(blocks), scale)...  61.6 us
    ppermute x42, starting transfers between devices, body(): blocks[target] = lax.ppermute(sent, 'shard', steps[axis])  58.1 us
    all_to_all x1, blocking collectives, body(): lax.all_to_all(table.reshape(devices, pairs), 'shard', split_axis=0, conc...  12.9 us
    pallas_call x1, Pallas kernels, head_matrices(): pl.pallas_call(head_kernel, out_shape=[jax.ShapeDtypeStruct(s, jnp.bfloat...  8.54 us
  transfers between devices with their start and end apart: 44, of which 20 were waited for; matrix products, arithmetic and copies ran while one was open for 12% of the time, Pallas kernels for 17%

profile of v4, /device:TPU:0, one launch (start us, length us, event | category | flops | bytes accessed | tf_op | source)
XLA Modules:
  0.0 359.1 jit_solution(9776630226256290059)
XLA Ops:
  1.9 7.0 %all-to-all-start = ((s32[32,1,128]{2,1,0:T(1,128)}), s32[32,1,128]{2,1,0:T(1,128)S(1)}, u32[]{:S(2)}, u32[]{:S(2)}) async-start(s32[32,1,128]{2,1,0:T(1,128)} %broadcast_in_dim.99), calls=%async_computation | async-start | bytes 32768 | tf_op jit(solution)/shard_map/all_to_all | solution.py:339
  8.9 1.6 fusion.22
  10.5 1.8 collective-permute-start.6
  13.5 1.5 collective-permute-start.7
  15.0 1.5 collective-permute-start.8
  16.5 2.5 collective-permute-start.13
  19.7 8.5 %head_matrices.1 = (bf16[64,2048]{1,0:T(8,128)(2,1)S(1)}, bf16[512,1024]{1,0:T(8,128)(2,1)S(1)}, bf16[256,256]{1,0:T(8,128)(2,1)S(1)}) custom-call(bf16[9,1,32]{2,1,0:T(2,128)(2,1)S(1)} %reshape.255.one_w, bf16[9,32,64]{2,1,0:T(8,128)(2,1)S(1)} %bitcast.38, bf16[9,1,64]{2,1,0:T(2,128)(2,1)S(1)} %reshape.256.three_w), custom_call_target="tpu_custom_call" | custom-call | flops 1000000000 | bytes 3000000 | tf_op jit(solution)/shard_map/head_matrices/pallas_call | solution.py:90
  31.5 4.4 %sort.15 = (s32[2048]{0:T(1024)S(1)}, s32[2048]{0:T(1024)S(1)}) sort(s32[2048]{0:T(1024)S(1)} %fusion.4, s32[2048]{0:T(1024)S(1)} %iota.54), dimensions={0}, to_apply=%region_0.1 | sort | flops 22528 | bytes 32768 | tf_op jit(solution)/shard_map/sort | solution.py:389
  42.6 1.7 collective-permute-start.3
  45.5 1.3 dynamic-slice_select_fusion.1.vids_ref
  46.8 3.4 collective-permute-done.1.rest_17_
  50.2 1.7 collective-permute-start.9
  52.0 1.7 collective-permute-start.14
  55.6 3.2 collective-permute-done.9.rest_19_
  58.9 1.7 collective-permute-start.2
  60.6 1.7 collective-permute-start.4
  62.8 1.6 collective-permute-start.11
  71.4 2.5 dynamic-slice_select_fusion.2
  73.9 2.6 select_bitcast_fusion
  76.5 1.3 and_select_fusion
  81.3 1.7 collective-permute-start.15
  83.0 1.3 collective-permute-start.5
  84.3 1.5 collective-permute-start.12
  85.8 16.3 %collective-permute-done.10.rest_4_ = bf16[6,8,9600]{2,1,0:T(8,128)(2,1)} collective-permute-done((bf16[6,8,9600]{2,1,0:T(8,128)(2,1)}, bf16[6,8,9600]{2,1,0:T(8,128)(2,1)}, u32[]{:S(2)}, u32[]{:S(2)}) %collective-permute-start.10) | collective-permute-done | bytes 921632 | tf_op jit(solution)/shard_map/ppermute | solution.py:443
  102.1 1.7 collective-permute-start.18
  103.8 1.7 collective-permute-start.16
  105.6 2.2 pad_maximum_fusion
  107.8 13.9 %collective-permute-done.12.rest_6_ = bf16[6,8,9600]{2,1,0:T(8,128)(2,1)S(1)} collective-permute-done((bf16[6,8,9600]{2,1,0:T(8,128)(2,1)}, bf16[6,8,9600]{2,1,0:T(8,128)(2,1)S(1)}, u32[]{:S(2)}, u32[]{:S(2)}) %collective-permute-start.12) | collective-permute-done | bytes 921632 | tf_op jit(solution)/shard_map/ppermute | solution.py:443
  121.7 1.8 collective-permute-start.21
  123.6 15.4 %collective-permute-done.18.rest_1_ = bf16[6,8,9600]{2,1,0:T(8,128)(2,1)S(1)} collective-permute-done((bf16[6,8,9600]{2,1,0:T(8,128)(2,1)S(1)}, bf16[6,8,9600]{2,1,0:T(8,128)(2,1)S(1)}, u32[]{:S(2)}, u32[]{:S(2)}) %collective-permute-start.18) | collective-permute-done | bytes 921632 | tf_op jit(solution)/shard_map/ppermute | solution.py:443
  139.0 1.7 collective-permute-start.19
  141.0 1.9 collective-permute-start.20
  144.5 16.1 %phase_0.1.before_ref = f32[16,128]{1,0:T(8,128)} custom-call(s32[192]{0:T(256)} %get-tuple-element.103.rows_ref, s32[192]{0:T(256)} %dynamic-slice_select_fusion.1.vids_ref, s32[20]{0:T(128)} %convert_reduce_fusion.ends_ref, s32[192,1]{1,0:T(8,128)} %copy.44.entry_ref, bf16[64,2048]{1,0:T(8,128)(2,1)} %copy-done.2, bf16[512,1024]{1,0:T(8,128)(2,1)} %copy-done.1, ...), custom_call_target="tpu_custom_call" | custom-call | flops 150994944000 | bytes 58982400 | tf_op jit(solution)/shard_map/phase_0/pallas_call | solution.py:218
  161.1 2.1 collective-permute-start.22
  164.6 3.0 collective-permute-start.29
  167.7 14.8 %collective-permute-done.27.rest_5_ = bf16[6,8,9600]{2,1,0:T(8,128)(2,1)} collective-permute-done((bf16[6,8,9600]{2,1,0:T(8,128)(2,1)}, bf16[6,8,9600]{2,1,0:T(8,128)(2,1)}, u32[]{:S(2)}, u32[]{:S(2)}) %collective-permute-start.27) | collective-permute-done | bytes 921632 | tf_op jit(solution)/shard_map/ppermute | solution.py:443
  182.4 1.9 collective-permute-start.23
  185.8 1.4 select_bitcast_fusion.3
  190.2 1.2 fusion.18.rows_ref
  193.8 2.0 fusion.17
  196.1 6.0 %collective-permute-done.29.rest_6_ = bf16[6,8,9600]{2,1,0:T(8,128)(2,1)S(1)} collective-permute-done((bf16[6,8,9600]{2,1,0:T(8,128)(2,1)}, bf16[6,8,9600]{2,1,0:T(8,128)(2,1)S(1)}, u32[]{:S(2)}, u32[]{:S(2)}) %collective-permute-start.29) | collective-permute-done | bytes 921632 | tf_op jit(solution)/shard_map/ppermute | solution.py:443
  202.1 1.7 collective-permute-start.32
  203.8 3.8 %collective-permute-done.22.rest_5_ = bf16[8,8,9600]{2,1,0:T(8,128)(2,1)} collective-permute-done((bf16[8,8,9600]{2,1,0:T(8,128)(2,1)S(1)}, bf16[8,8,9600]{2,1,0:T(8,128)(2,1)}, u32[]{:S(2)}, u32[]{:S(2)}) %collective-permute-start.22) | collective-permute-done | bytes 1228832 | tf_op jit(solution)/shard_map/ppermute | solution.py:443
  208.0 3.4 collective-permute-start.30
  211.3 10.6 %collective-permute-done.28.rest_4_ = bf16[6,8,9600]{2,1,0:T(8,128)(2,1)} collective-permute-done((bf16[6,8,9600]{2,1,0:T(8,128)(2,1)S(1)}, bf16[6,8,9600]{2,1,0:T(8,128)(2,1)}, u32[]{:S(2)}, u32[]{:S(2)}) %collective-permute-start.28) | collective-permute-done | bytes 921632 | tf_op jit(solution)/shard_map/ppermute | solution.py:443
  221.9 1.9 collective-permute-start.25
  223.9 11.4 %phase_1.1.before_ref = f32[16,128]{1,0:T(8,128)} custom-call(s32[128]{0:T(128)} %fusion.20.rows_ref, s32[128]{0:T(128)} %get-tuple-element.107.vids_ref, s32[6]{0:T(128)} %convert_reduce_fusion.2.ends_ref, s32[128,1]{1,0:T(8,128)} %copy.45.entry_ref, bf16[64,2048]{1,0:T(8,128)(2,1)} %copy-done.2, bf16[512,1024]{1,0:T(8,128)(2,1)} %copy-done.1, ...), custom_call_target="tpu_custom_call" | custom-call | flops 100663296000 | bytes 39321600 | tf_op jit(solution)/shard_map/phase_1/pallas_call | solution.py:218
  236.0 17.8 %collective-permute-done.30.rest_7_ = bf16[6,8,9600]{2,1,0:T(8,128)(2,1)} collective-permute-done((bf16[6,8,9600]{2,1,0:T(8,128)(2,1)}, bf16[6,8,9600]{2,1,0:T(8,128)(2,1)}, u32[]{:S(2)}, u32[]{:S(2)}) %collective-permute-start.30) | collective-permute-done | bytes 921632 | tf_op jit(solution)/shard_map/ppermute | solution.py:443
  253.8 1.7 collective-permute-start.36
  255.5 2.7 collective-permute-start.39
  259.2 13.5 %phase_2.1.before_ref = f32[16,128]{1,0:T(8,128)} custom-call(s32[128]{0:T(128)} %fusion.19.rows_ref, s32[128]{0:T(128)} %get-tuple-element.108.vids_ref, s32[8]{0:T(128)} %convert_reduce_fusion.3.ends_ref, s32[128,1]{1,0:T(8,128)} %copy.46.entry_ref, bf16[64,2048]{1,0:T(8,128)(2,1)} %copy-done.2, bf16[512,1024]{1,0:T(8,128)(2,1)} %copy-done.1, ...), custom_call_target="tpu_custom_call" | custom-call | flops 100663296000 | bytes 39321600 | tf_op jit(solution)/shard_map/phase_2/pallas_call | solution.py:218
  272.7 4.8 %collective-permute-done.34.rest_3_ = bf16[6,8,9600]{2,1,0:T(8,128)(2,1)} collective-permute-done((bf16[6,8,9600]{2,1,0:T(8,128)(2,1)}, bf16[6,8,9600]{2,1,0:T(8,128)(2,1)}, u32[]{:S(2)}, u32[]{:S(2)}) %collective-permute-start.34) | collective-permute-done | bytes 921632 | tf_op jit(solution)/shard_map/ppermute | solution.py:443
  277.5 1.6 collective-permute-start.41
  279.2 5.8 %collective-permute-done.36.rest_5_ = bf16[8,8,9600]{2,1,0:T(8,128)(2,1)S(1)} collective-permute-done((bf16[8,8,9600]{2,1,0:T(8,128)(2,1)}, bf16[8,8,9600]{2,1,0:T(8,128)(2,1)S(1)}, u32[]{:S(2)}, u32[]{:S(2)}) %collective-permute-start.36) | collective-permute-done | bytes 1228832 | tf_op jit(solution)/shard_map/ppermute | solution.py:443
  285.0 1.8 collective-permute-start.40
  286.8 10.5 %collective-permute-done.31.rest_0_ = bf16[6,8,9600]{2,1,0:T(8,128)(2,1)} collective-permute-done((bf16[6,8,9600]{2,1,0:T(8,128)(2,1)S(1)}, bf16[6,8,9600]{2,1,0:T(8,128)(2,1)}, u32[]{:S(2)}, u32[]{:S(2)}) %collective-permute-start.31) | collective-permute-done | bytes 921632 | tf_op jit(solution)/shard_map/ppermute | solution.py:443
  297.3 1.6 collective-permute-start.42
  298.9 10.3 %phase_3.1.before_ref = f32[16,128]{1,0:T(8,128)} custom-call(s32[128]{0:T(128)} %fusion.18.rows_ref, s32[128]{0:T(128)} %get-tuple-element.109.vids_ref, s32[6]{0:T(128)} %convert_reduce_fusion.4.ends_ref, s32[128,1]{1,0:T(8,128)} %copy.47.entry_ref, bf16[64,2048]{1,0:T(8,128)(2,1)} %copy-done.2, bf16[512,1024]{1,0:T(8,128)(2,1)} %copy-done.1, ...), custom_call_target="tpu_custom_call" | custom-call | flops 100663296000 | bytes 39321600 | tf_op jit(solution)/shard_map/phase_3/pallas_call | solution.py:218
  309.2 2.1 collective-permute-done.41.rest_4_
  311.3 5.7 %collective-permute-done.37.rest_0_ = bf16[6,8,9600]{2,1,0:T(8,128)(2,1)} collective-permute-done((bf16[6,8,9600]{2,1,0:T(8,128)(2,1)S(1)}, bf16[6,8,9600]{2,1,0:T(8,128)(2,1)}, u32[]{:S(2)}, u32[]{:S(2)}) %collective-permute-start.37) | collective-permute-done | bytes 921632 | tf_op jit(solution)/shard_map/ppermute | solution.py:443
  317.0 14.1 %collective-permute-done.38.rest_1_ = bf16[6,8,9600]{2,1,0:T(8,128)(2,1)} collective-permute-done((bf16[6,8,9600]{2,1,0:T(8,128)(2,1)}, bf16[6,8,9600]{2,1,0:T(8,128)(2,1)}, u32[]{:S(2)}, u32[]{:S(2)}) %collective-permute-start.38) | collective-permute-done | bytes 921632 | tf_op jit(solution)/shard_map/ppermute | solution.py:443
  331.1 2.2 collective-permute-done.42.rest_5_
  334.3 10.3 %phase_4.1 = f32[16,128]{1,0:T(8,128)} custom-call(s32[64]{0:T(128)} %get-tuple-element.125.rows_ref, s32[64]{0:T(128)} %get-tuple-element.126.vids_ref, s32[6]{0:T(128)} %convert_reduce_fusion.5.ends_ref, s32[64,1]{1,0:T(8,128)} %copy.48.entry_ref, bf16[64,2048]{1,0:T(8,128)(2,1)} %copy-done.2, bf16[512,1024]{1,0:T(8,128)(2,1)} %copy-done.1, ...), custom_call_target="tpu_custom_call" | custom-call | flops 50331648000 | bytes 19660800 | tf_op jit(solution)/shard_map/phase_4/pallas_call | solution.py:218
  345.4 12.9 %all_to_all.15 = f32[32,1,128]{2,1,0:T(1,128)S(1)} all-to-all(f32[32,1,128]{2,1,0:T(1,128)S(1)} %broadcast_select_fusion), channel_id=1, replica_groups=mesh['shard'=32] {'shard'}, dimensions={0} | all-to-all | bytes 32768 | tf_op jit(solution)/shard_map/all_to_all | solution.py:449
  (179 shorter events, 33.6 us)
Async XLA Ops:
  0.0 103.8 %collective-permute-start = (bf16[128,8,9600]{2,1,0:T(8,128)(2,1)}, bf16[128,8,9600]{2,1,0:T(8,128)(2,1)}, u32[]{:S(2)}, u32[]{:S(2)}) collective-permute-start(bf16[128,8,9600]{2,1,0:T(8,128)(2,1)} %own_hbm.9), channel_id=1, source_target_pairs={{0,1},{1,0},{2,3},{3,2},{4,5},{5,4},{6,7},{7,6},{8,9},{9,8},{10,11... | collective-permute-start | bytes 58982408 | tf_op jit(solution)/shard_map/ppermute | solution.py:343
  1.9 29.5 %all-to-all-start = ((s32[32,1,128]{2,1,0:T(1,128)}), s32[32,1,128]{2,1,0:T(1,128)S(1)}, u32[]{:S(2)}, u32[]{:S(2)}) async-start(s32[32,1,128]{2,1,0:T(1,128)} %broadcast_in_dim.99), calls=%async_computation | async-start | bytes 32768 | tf_op jit(solution)/shard_map/all_to_all | solution.py:339
  10.5 72.5 %copy-start.8 = (bf16[6,8,9600]{2,1,0:T(8,128)(2,1)}, bf16[6,8,9600]{2,1,0:T(8,128)(2,1)S(1)}, u32[]{:S(2)}) copy-start(bf16[6,8,9600]{2,1,0:T(8,128)(2,1)S(1)} %get-tuple-element.53.rest_0_) | copy-start | bytes 2764804
  10.5 91.6 %copy-start.7 = (bf16[6,8,9600]{2,1,0:T(8,128)(2,1)}, bf16[6,8,9600]{2,1,0:T(8,128)(2,1)S(1)}, u32[]{:S(2)}) copy-start(bf16[6,8,9600]{2,1,0:T(8,128)(2,1)S(1)} %get-tuple-element.62.rest_7_) | copy-start | bytes 2764804
  10.5 50.1 %collective-permute-start.6 = (bf16[6,8,9600]{2,1,0:T(8,128)(2,1)S(1)}, bf16[6,8,9600]{2,1,0:T(8,128)(2,1)}, u32[]{:S(2)}, u32[]{:S(2)}) collective-permute-start(bf16[6,8,9600]{2,1,0:T(8,128)(2,1)S(1)} %get-tuple-element.53.rest_0_), channel_id=1, source_target_pairs={{0,8},{1,9},{2,10},{3,11},{4,12},{5,13},{6,14},{7,15},{8,24},{9,25... | collective-permute-start | bytes 2764808 | tf_op jit(solution)/shard_map/ppermute | solution.py:443
  13.5 28.3 %copy-start.4 = (bf16[2,8,9600]{2,1,0:T(8,128)(2,1)}, bf16[2,8,9600]{2,1,0:T(8,128)(2,1)S(1)}, u32[]{:S(2)}) copy-start(bf16[2,8,9600]{2,1,0:T(8,128)(2,1)S(1)} %get-tuple-element.96.rest_16_) | copy-start | bytes 921604
  13.5 92.1 %copy-start.6 = (bf16[2,8,9600]{2,1,0:T(8,128)(2,1)}, bf16[2,8,9600]{2,1,0:T(8,128)(2,1)S(1)}, u32[]{:S(2)}) copy-start(bf16[2,8,9600]{2,1,0:T(8,128)(2,1)S(1)} %get-tuple-element.95.rest_12_) | copy-start | bytes 921604
  13.5 28.3 %collective-permute-start.7 = (bf16[2,8,9600]{2,1,0:T(8,128)(2,1)S(1)}, bf16[2,8,9600]{2,1,0:T(8,128)(2,1)S(1)}, u32[]{:S(2)}, u32[]{:S(2)}) collective-permute-start(bf16[2,8,9600]{2,1,0:T(8,128)(2,1)S(1)} %get-tuple-element.96.rest_16_), channel_id=1, source_target_pairs={{0,4},{1,5},{2,6},{3,7},{4,0},{5,1},{6,2},{7,3},{8,12},{9,13},{10,... | collective-permute-start | bytes 921608 | tf_op jit(solution)/shard_map/ppermute | solution.py:443
  15.0 27.6 %collective-permute-start.8 = (bf16[2,8,9600]{2,1,0:T(8,128)(2,1)S(1)}, bf16[2,8,9600]{2,1,0:T(8,128)(2,1)S(1)}, u32[]{:S(2)}, u32[]{:S(2)}) collective-permute-start(bf16[2,8,9600]{2,1,0:T(8,128)(2,1)S(1)} %get-tuple-element.95.rest_12_), channel_id=1, source_target_pairs={{0,2},{1,3},{2,0},{3,1},{4,6},{5,7},{6,4},{7,5},{8,10},{9,11},{10,... | collective-permute-start | bytes 921608 | tf_op jit(solution)/shard_map/ppermute | solution.py:443
  16.5 46.4 %collective-permute-start.13 = (bf16[6,8,9600]{2,1,0:T(8,128)(2,1)S(1)}, bf16[6,8,9600]{2,1,0:T(8,128)(2,1)}, u32[]{:S(2)}, u32[]{:S(2)}) collective-permute-start(bf16[6,8,9600]{2,1,0:T(8,128)(2,1)S(1)} %get-tuple-element.62.rest_7_), channel_id=1, source_target_pairs={{0,8},{1,9},{2,10},{3,11},{4,12},{5,13},{6,14},{7,15},{8,24},{9,25... | collective-permute-start | bytes 2764808 | tf_op jit(solution)/shard_map/ppermute | solution.py:443
  36.0 71.8 %copy-start.18 = (s32[448]{0:T(512)}, s32[448]{0:T(512)S(1)}, u32[]{:S(2)}) copy-start(s32[448]{0:T(512)S(1)} %get-tuple-element.99) | copy-start | bytes 5380
  36.0 71.8 %copy-start.19 = (s32[448]{0:T(512)}, s32[448]{0:T(512)S(1)}, u32[]{:S(2)}) copy-start(s32[448]{0:T(512)S(1)} %get-tuple-element.124) | copy-start | bytes 5380
  41.7 66.0 %copy-start.9 = (bf16[2,8,9600]{2,1,0:T(8,128)(2,1)}, bf16[2,8,9600]{2,1,0:T(8,128)(2,1)S(1)}, u32[]{:S(2)}) copy-start(bf16[2,8,9600]{2,1,0:T(8,128)(2,1)S(1)} %collective-permute-done.7.rest_18_) | copy-start | bytes 921604
  41.7 8.5 %collective-permute-start.1 = (bf16[2,8,9600]{2,1,0:T(8,128)(2,1)S(1)}, bf16[2,8,9600]{2,1,0:T(8,128)(2,1)S(1)}, u32[]{:S(2)}, u32[]{:S(2)}) collective-permute-start(bf16[2,8,9600]{2,1,0:T(8,128)(2,1)S(1)} %get-tuple-element.96.rest_16_), channel_id=1, source_target_pairs={{0,2},{1,3},{2,0},{3,1},{4,6},{5,7},{6,4},{7,5},{8,10},{9,11},{10,... | collective-permute-start | bytes 921608 | tf_op jit(solution)/shard_map/ppermute | solution.py:443
  42.6 65.2 %copy-start.11 = (bf16[2,8,9600]{2,1,0:T(8,128)(2,1)}, bf16[2,8,9600]{2,1,0:T(8,128)(2,1)S(1)}, u32[]{:S(2)}) copy-start(bf16[2,8,9600]{2,1,0:T(8,128)(2,1)S(1)} %collective-permute-done.8.rest_13_) | copy-start | bytes 921604
  42.6 9.4 %collective-permute-start.3 = (bf16[2,8,9600]{2,1,0:T(8,128)(2,1)S(1)}, bf16[2,8,9600]{2,1,0:T(8,128)(2,1)S(1)}, u32[]{:S(2)}, u32[]{:S(2)}) collective-permute-start(bf16[2,8,9600]{2,1,0:T(8,128)(2,1)S(1)} %get-tuple-element.95.rest_12_), channel_id=1, source_target_pairs={{0,4},{1,5},{2,6},{3,7},{4,0},{5,1},{6,2},{7,3},{8,12},{9,13},{10,... | collective-permute-start | bytes 921608 | tf_op jit(solution)/shard_map/ppermute | solution.py:443
  50.2 8.6 %collective-permute-start.9 = (bf16[2,8,9600]{2,1,0:T(8,128)(2,1)S(1)}, bf16[2,8,9600]{2,1,0:T(8,128)(2,1)S(1)}, u32[]{:S(2)}, u32[]{:S(2)}) collective-permute-start(bf16[2,8,9600]{2,1,0:T(8,128)(2,1)S(1)} %collective-permute-done.7.rest_18_), channel_id=1, source_target_pairs={{0,2},{1,3},{2,0},{3,1},{4,6},{5,7},{6,4},{7,5},{8,10},{9,11},{10,... | collective-permute-start | bytes 921608 | tf_op jit(solution)/shard_map/ppermute | solution.py:443
  52.0 92.5 %copy-start.16 = (bf16[2,8,9600]{2,1,0:T(8,128)(2,1)}, bf16[2,8,9600]{2,1,0:T(8,128)(2,1)S(1)}, u32[]{:S(2)}) copy-start(bf16[2,8,9600]{2,1,0:T(8,128)(2,1)S(1)} %collective-permute-done.3.rest_14_) | copy-start | bytes 921604
  52.0 10.3 %collective-permute-start.14 = (bf16[2,8,9600]{2,1,0:T(8,128)(2,1)S(1)}, bf16[2,8,9600]{2,1,0:T(8,128)(2,1)S(1)}, u32[]{:S(2)}, u32[]{:S(2)}) collective-permute-start(bf16[2,8,9600]{2,1,0:T(8,128)(2,1)S(1)} %collective-permute-done.8.rest_13_), channel_id=1, source_target_pairs={{0,4},{1,5},{2,6},{3,7},{4,0},{5,1},{6,2},{7,3},{8,12},{9,13},{10,... | collective-permute-start | bytes 921608 | tf_op jit(solution)/shard_map/ppermute | solution.py:443
  58.9 48.9 %copy-start.14 = (bf16[2,8,9600]{2,1,0:T(8,128)(2,1)}, bf16[2,8,9600]{2,1,0:T(8,128)(2,1)S(1)}, u32[]{:S(2)}) copy-start(bf16[2,8,9600]{2,1,0:T(8,128)(2,1)S(1)} %collective-permute-done.9.rest_19_) | copy-start | bytes 921604
  58.9 24.1 %collective-permute-start.2 = (bf16[6,8,9600]{2,1,0:T(8,128)(2,1)S(1)}, bf16[6,8,9600]{2,1,0:T(8,128)(2,1)}, u32[]{:S(2)}, u32[]{:S(2)}) collective-permute-start(bf16[6,8,9600]{2,1,0:T(8,128)(2,1)S(1)} %get-tuple-element.53.rest_0_), channel_id=1, source_target_pairs={{0,2},{1,3},{2,0},{3,1},{4,6},{5,7},{6,4},{7,5},{8,10},{9,11},{10,... | collective-permute-start | bytes 2764808 | tf_op jit(solution)/shard_map/ppermute | solution.py:443
  60.6 20.7 %collective-permute-start.4 = (bf16[6,8,9600]{2,1,0:T(8,128)(2,1)S(1)}, bf16[6,8,9600]{2,1,0:T(8,128)(2,1)}, u32[]{:S(2)}, u32[]{:S(2)}) collective-permute-start(bf16[6,8,9600]{2,1,0:T(8,128)(2,1)S(1)} %get-tuple-element.62.rest_7_), channel_id=1, source_target_pairs={{0,4},{1,5},{2,6},{3,7},{4,0},{5,1},{6,2},{7,3},{8,12},{9,13},{10,... | collective-permute-start | bytes 2764808 | tf_op jit(solution)/shard_map/ppermute | solution.py:443
  62.3 39.8 %collective-permute-start.10 = (bf16[6,8,9600]{2,1,0:T(8,128)(2,1)}, bf16[6,8,9600]{2,1,0:T(8,128)(2,1)}, u32[]{:S(2)}, u32[]{:S(2)}) collective-permute-start(bf16[6,8,9600]{2,1,0:T(8,128)(2,1)} %collective-permute-done.6.rest_3_), channel_id=1, source_target_pairs={{0,2},{1,3},{2,0},{3,1},{4,6},{5,7},{6,4},{7,5},{8,10},{9,11},{10,... | collective-permute-start | bytes 2764808 | tf_op jit(solution)/shard_map/ppermute | solution.py:443
  62.8 21.4 %collective-permute-start.11 = (bf16[6,8,9600]{2,1,0:T(8,128)(2,1)}, bf16[6,8,9600]{2,1,0:T(8,128)(2,1)}, u32[]{:S(2)}, u32[]{:S(2)}) collective-permute-start(bf16[6,8,9600]{2,1,0:T(8,128)(2,1)} %collective-permute-done.6.rest_3_), channel_id=1, source_target_pairs={{0,8},{1,9},{2,10},{3,11},{4,12},{5,13},{6,14},{7,15},{8,24},{9,25... | collective-permute-start | bytes 2764808 | tf_op jit(solution)/shard_map/ppermute | solution.py:443
  81.3 59.4 %collective-permute-start.15 = (bf16[6,8,9600]{2,1,0:T(8,128)(2,1)}, bf16[6,8,9600]{2,1,0:T(8,128)(2,1)}, u32[]{:S(2)}, u32[]{:S(2)}) collective-permute-start(bf16[6,8,9600]{2,1,0:T(8,128)(2,1)} %collective-permute-done.13.rest_9_), channel_id=1, source_target_pairs={{0,4},{1,5},{2,6},{3,7},{4,0},{5,1},{6,2},{7,3},{8,12},{9,13},{10,... | collective-permute-start | bytes 2764808 | tf_op jit(solution)/shard_map/ppermute | solution.py:443
  83.0 60.0 %collective-permute-start.5 = (bf16[6,8,9600]{2,1,0:T(8,128)(2,1)S(1)}, bf16[6,8,9600]{2,1,0:T(8,128)(2,1)S(1)}, u32[]{:S(2)}, u32[]{:S(2)}) collective-permute-start(bf16[6,8,9600]{2,1,0:T(8,128)(2,1)S(1)} %get-tuple-element.53.rest_0_), channel_id=1, source_target_pairs={{0,4},{1,5},{2,6},{3,7},{4,0},{5,1},{6,2},{7,3},{8,12},{9,13},{10,... | collective-permute-start | bytes 2764808 | tf_op jit(solution)/shard_map/ppermute | solution.py:443
  84.3 37.5 %collective-permute-start.12 = (bf16[6,8,9600]{2,1,0:T(8,128)(2,1)}, bf16[6,8,9600]{2,1,0:T(8,128)(2,1)S(1)}, u32[]{:S(2)}, u32[]{:S(2)}) collective-permute-start(bf16[6,8,9600]{2,1,0:T(8,128)(2,1)} %collective-permute-done.11.rest_5_), channel_id=1, source_target_pairs={{0,2},{1,3},{2,0},{3,1},{4,6},{5,7},{6,4},{7,5},{8,10},{9,11},{10,... | collective-permute-start | bytes 2764808 | tf_op jit(solution)/shard_map/ppermute | solution.py:443
  102.1 36.9 %collective-permute-start.18 = (bf16[6,8,9600]{2,1,0:T(8,128)(2,1)S(1)}, bf16[6,8,9600]{2,1,0:T(8,128)(2,1)S(1)}, u32[]{:S(2)}, u32[]{:S(2)}) collective-permute-start(bf16[6,8,9600]{2,1,0:T(8,128)(2,1)S(1)} %get-tuple-element.62.rest_7_), channel_id=1, source_target_pairs={{0,2},{1,3},{2,0},{3,1},{4,6},{5,7},{6,4},{7,5},{8,10},{9,11},{10,... | collective-permute-start | bytes 2764808 | tf_op jit(solution)/shard_map/ppermute | solution.py:443
  103.8 37.2 %collective-permute-start.16 = (bf16[6,8,9600]{2,1,0:T(8,128)(2,1)}, bf16[6,8,9600]{2,1,0:T(8,128)(2,1)}, u32[]{:S(2)}, u32[]{:S(2)}) collective-permute-start(bf16[6,8,9600]{2,1,0:T(8,128)(2,1)} %collective-permute-done.13.rest_9_), channel_id=1, source_target_pairs={{0,8},{1,9},{2,10},{3,11},{4,12},{5,13},{6,14},{7,15},{8,24},{9,25... | collective-permute-start | bytes 2764808 | tf_op jit(solution)/shard_map/ppermute | solution.py:443
  121.7 22.8 %copy-start.36 = (bf16[6,8,9600]{2,1,0:T(8,128)(2,1)}, bf16[6,8,9600]{2,1,0:T(8,128)(2,1)S(1)}, u32[]{:S(2)}) copy-start(bf16[6,8,9600]{2,1,0:T(8,128)(2,1)S(1)} %collective-permute-done.12.rest_6_) | copy-start | bytes 2764804
  121.7 39.0 %collective-permute-start.21 = (bf16[8,8,9600]{2,1,0:T(8,128)(2,1)}, bf16[8,8,9600]{2,1,0:T(8,128)(2,1)}, u32[]{:S(2)}, u32[]{:S(2)}) collective-permute-start(bf16[8,8,9600]{2,1,0:T(8,128)(2,1)} %pad_maximum_fusion), channel_id=1, source_target_pairs={{0,8},{1,9},{2,10},{3,11},{4,12},{5,13},{6,14},{7,15},{8,24},{9,25... | collective-permute-start | bytes 3686408 | tf_op jit(solution)/shard_map/ppermute | solution.py:443
  139.0 25.6 %collective-permute-start.19 = (bf16[6,8,9600]{2,1,0:T(8,128)(2,1)}, bf16[6,8,9600]{2,1,0:T(8,128)(2,1)}, u32[]{:S(2)}, u32[]{:S(2)}) collective-permute-start(bf16[6,8,9600]{2,1,0:T(8,128)(2,1)} %collective-permute-done.4.rest_8_), channel_id=1, source_target_pairs={{0,2},{1,3},{2,0},{3,1},{4,6},{5,7},{6,4},{7,5},{8,10},{9,11},{10,... | collective-permute-start | bytes 2764808 | tf_op jit(solution)/shard_map/ppermute | solution.py:443
  140.7 41.7 %collective-permute-start.27 = (bf16[6,8,9600]{2,1,0:T(8,128)(2,1)}, bf16[6,8,9600]{2,1,0:T(8,128)(2,1)}, u32[]{:S(2)}, u32[]{:S(2)}) collective-permute-start(bf16[6,8,9600]{2,1,0:T(8,128)(2,1)} %collective-permute-done.13.rest_9_), channel_id=1, source_target_pairs={{0,2},{1,3},{2,0},{3,1},{4,6},{5,7},{6,4},{7,5},{8,10},{9,11},{10,... | collective-permute-start | bytes 2764808 | tf_op jit(solution)/shard_map/ppermute | solution.py:443
  141.0 23.6 %collective-permute-start.20 = (bf16[6,8,9600]{2,1,0:T(8,128)(2,1)}, bf16[6,8,9600]{2,1,0:T(8,128)(2,1)}, u32[]{:S(2)}, u32[]{:S(2)}) collective-permute-start(bf16[6,8,9600]{2,1,0:T(8,128)(2,1)} %collective-permute-done.16.rest_11_), channel_id=1, source_target_pairs={{0,4},{1,5},{2,6},{3,7},{4,0},{5,1},{6,2},{7,3},{8,12},{9,13},{10,... | collective-permute-start | bytes 2764808 | tf_op jit(solution)/shard_map/ppermute | solution.py:443
  160.7 27.3 %copy-start.25 = (s32[128,1]{0,1:T(1,128)S(1)}, s32[128,1]{0,1:T(1,128)}, u32[]{:S(2)}) copy-start(s32[128,1]{0,1:T(1,128)} %get-tuple-element.106) | copy-start | bytes 1540
  160.7 28.0 %copy-start.24 = (s32[128,1]{0,1:T(1,128)S(1)}, s32[128,1]{0,1:T(1,128)}, u32[]{:S(2)}) copy-start(s32[128,1]{0,1:T(1,128)} %get-tuple-element.105) | copy-start | bytes 1540
  160.7 28.7 %copy-start.23 = (s32[128,1]{0,1:T(1,128)S(1)}, s32[128,1]{0,1:T(1,128)}, u32[]{:S(2)}) copy-start(s32[128,1]{0,1:T(1,128)} %get-tuple-element.104) | copy-start | bytes 1540
  160.7 29.4 %copy-start.29 = (s32[128]{0:T(128)S(1)}, s32[128]{0:T(128)}, u32[]{:S(2)}) copy-start(s32[128]{0:T(128)} %get-tuple-element.111) | copy-start | bytes 1540
  160.7 30.7 %copy-start.28 = (s32[128]{0:T(128)S(1)}, s32[128]{0:T(128)}, u32[]{:S(2)}) copy-start(s32[128]{0:T(128)} %get-tuple-element.113) | copy-start | bytes 1540
  160.7 31.9 %copy-start.27 = (s32[128]{0:T(128)S(1)}, s32[128]{0:T(128)}, u32[]{:S(2)}) copy-start(s32[128]{0:T(128)} %get-tuple-element.88) | copy-start | bytes 1540
  160.7 33.0 %copy-start.26 = (s32[64]{0:T(128)S(1)}, s32[64]{0:T(128)}, u32[]{:S(2)}) copy-start(s32[64]{0:T(128)} %get-tuple-element.94) | copy-start | bytes 772
  160.8 24.5 %collective-permute-start.26 = (bf16[6,8,9600]{2,1,0:T(8,128)(2,1)}, bf16[6,8,9600]{2,1,0:T(8,128)(2,1)S(1)}, u32[]{:S(2)}, u32[]{:S(2)}) collective-permute-start(bf16[6,8,9600]{2,1,0:T(8,128)(2,1)} %collective-permute-done.11.rest_5_), channel_id=1, source_target_pairs={{0,8},{1,9},{2,10},{3,11},{4,12},{5,13},{6,14},{7,15},{8,24},{9,25... | collective-permute-start | bytes 2764808 | tf_op jit(solution)/shard_map/ppermute | solution.py:443
  161.1 46.6 %collective-permute-start.22 = (bf16[8,8,9600]{2,1,0:T(8,128)(2,1)S(1)}, bf16[8,8,9600]{2,1,0:T(8,128)(2,1)}, u32[]{:S(2)}, u32[]{:S(2)}) collective-permute-start(bf16[8,8,9600]{2,1,0:T(8,128)(2,1)S(1)} %pad_maximum_fusion.1), channel_id=1, source_target_pairs={{0,8},{1,9},{2,10},{3,11},{4,12},{5,13},{6,14},{7,15},{8,24},{9,25... | collective-permute-start | bytes 3686408 | tf_op jit(solution)/shard_map/ppermute | solution.py:443
  164.5 31.2 %collective-permute-start.17 = (bf16[6,8,9600]{2,1,0:T(8,128)(2,1)}, bf16[6,8,9600]{2,1,0:T(8,128)(2,1)}, u32[]{:S(2)}, u32[]{:S(2)}) collective-permute-start(bf16[6,8,9600]{2,1,0:T(8,128)(2,1)} %collective-permute-done.2.rest_1_), channel_id=1, source_target_pairs={{0,4},{1,5},{2,6},{3,7},{4,0},{5,1},{6,2},{7,3},{8,12},{9,13},{10,... | collective-permute-start | bytes 2764808 | tf_op jit(solution)/shard_map/ppermute | solution.py:443
  164.6 37.4 %collective-permute-start.29 = (bf16[6,8,9600]{2,1,0:T(8,128)(2,1)}, bf16[6,8,9600]{2,1,0:T(8,128)(2,1)S(1)}, u32[]{:S(2)}, u32[]{:S(2)}) collective-permute-start(bf16[6,8,9600]{2,1,0:T(8,128)(2,1)} %collective-permute-done.15.rest_10_), channel_id=1, source_target_pairs={{0,2},{1,3},{2,0},{3,1},{4,6},{5,7},{6,4},{7,5},{8,10},{9,11},{10,... | collective-permute-start | bytes 2764808 | tf_op jit(solution)/shard_map/ppermute | solution.py:443
  182.4 25.6 %collective-permute-start.23 = (bf16[6,8,9600]{2,1,0:T(8,128)(2,1)}, bf16[6,8,9600]{2,1,0:T(8,128)(2,1)}, u32[]{:S(2)}, u32[]{:S(2)}) collective-permute-start(bf16[6,8,9600]{2,1,0:T(8,128)(2,1)} %collective-permute-done.6.rest_3_), channel_id=1, source_target_pairs={{0,4},{1,5},{2,6},{3,7},{4,0},{5,1},{6,2},{7,3},{8,12},{9,13},{10,... | collective-permute-start | bytes 2764808 | tf_op jit(solution)/shard_map/ppermute | solution.py:443
  185.3 50.0 %copy-start.38 = (bf16[6,8,9600]{2,1,0:T(8,128)(2,1)}, bf16[6,8,9600]{2,1,0:T(8,128)(2,1)S(1)}, u32[]{:S(2)}) copy-start(bf16[6,8,9600]{2,1,0:T(8,128)(2,1)S(1)} %collective-permute-done.26.rest_3_) | copy-start | bytes 2764804
  185.3 36.6 %collective-permute-start.28 = (bf16[6,8,9600]{2,1,0:T(8,128)(2,1)S(1)}, bf16[6,8,9600]{2,1,0:T(8,128)(2,1)}, u32[]{:S(2)}, u32[]{:S(2)}) collective-permute-start(bf16[6,8,9600]{2,1,0:T(8,128)(2,1)S(1)} %collective-permute-done.26.rest_3_), channel_id=1, source_target_pairs={{0,2},{1,3},{2,0},{3,1},{4,6},{5,7},{6,4},{7,5},{8,10},{9,11},{10,... | collective-permute-start | bytes 2764808 | tf_op jit(solution)/shard_map/ppermute | solution.py:443
  195.7 39.6 %collective-permute-start.24 = (bf16[6,8,9600]{2,1,0:T(8,128)(2,1)}, bf16[6,8,9600]{2,1,0:T(8,128)(2,1)S(1)}, u32[]{:S(2)}, u32[]{:S(2)}) collective-permute-start(bf16[6,8,9600]{2,1,0:T(8,128)(2,1)} %collective-permute-done.10.rest_4_), channel_id=1, source_target_pairs={{0,4},{1,5},{2,6},{3,7},{4,0},{5,1},{6,2},{7,3},{8,12},{9,13},{10,... | collective-permute-start | bytes 2764808 | tf_op jit(solution)/shard_map/ppermute | solution.py:443
  202.1 51.8 %collective-permute-start.32 = (bf16[6,8,9600]{2,1,0:T(8,128)(2,1)}, bf16[6,8,9600]{2,1,0:T(8,128)(2,1)}, u32[]{:S(2)}, u32[]{:S(2)}) collective-permute-start(bf16[6,8,9600]{2,1,0:T(8,128)(2,1)} %collective-permute-done.16.rest_11_), channel_id=1, source_target_pairs={{0,2},{1,3},{2,0},{3,1},{4,6},{5,7},{6,4},{7,5},{8,10},{9,11},{10,... | collective-permute-start | bytes 2764808 | tf_op jit(solution)/shard_map/ppermute | solution.py:443
  207.6 47.9 %collective-permute-start.35 = (bf16[8,8,9600]{2,1,0:T(8,128)(2,1)}, bf16[8,8,9600]{2,1,0:T(8,128)(2,1)S(1)}, u32[]{:S(2)}, u32[]{:S(2)}) collective-permute-start(bf16[8,8,9600]{2,1,0:T(8,128)(2,1)} %collective-permute-done.21.rest_4_), channel_id=1, source_target_pairs={{0,8},{1,9},{2,10},{3,11},{4,12},{5,13},{6,14},{7,15},{8,24},{9,25... | collective-permute-start | bytes 3686408 | tf_op jit(solution)/shard_map/ppermute | solution.py:443
  208.0 45.8 %collective-permute-start.30 = (bf16[6,8,9600]{2,1,0:T(8,128)(2,1)}, bf16[6,8,9600]{2,1,0:T(8,128)(2,1)}, u32[]{:S(2)}, u32[]{:S(2)}) collective-permute-start(bf16[6,8,9600]{2,1,0:T(8,128)(2,1)} %collective-permute-done.16.rest_11_), channel_id=1, source_target_pairs={{0,8},{1,9},{2,10},{3,11},{4,12},{5,13},{6,14},{7,15},{8,24},{9,25... | collective-permute-start | bytes 2764808 | tf_op jit(solution)/shard_map/ppermute | solution.py:443
  221.9 36.3 %collective-permute-start.25 = (bf16[6,8,9600]{2,1,0:T(8,128)(2,1)}, bf16[6,8,9600]{2,1,0:T(8,128)(2,1)S(1)}, u32[]{:S(2)}, u32[]{:S(2)}) collective-permute-start(bf16[6,8,9600]{2,1,0:T(8,128)(2,1)} %collective-permute-done.11.rest_5_), channel_id=1, source_target_pairs={{0,4},{1,5},{2,6},{3,7},{4,0},{5,1},{6,2},{7,3},{8,12},{9,13},{10,... | collective-permute-start | bytes 2764808 | tf_op jit(solution)/shard_map/ppermute | solution.py:443
  223.9 34.4 %copy-start.37 = (bf16[6,8,9600]{2,1,0:T(8,128)(2,1)S(1)}, bf16[6,8,9600]{2,1,0:T(8,128)(2,1)}, u32[]{:S(2)}) copy-start(bf16[6,8,9600]{2,1,0:T(8,128)(2,1)} %copy-done.36) | copy-start | bytes 2764804
  235.3 43.8 %collective-permute-start.33 = (bf16[6,8,9600]{2,1,0:T(8,128)(2,1)}, bf16[6,8,9600]{2,1,0:T(8,128)(2,1)}, u32[]{:S(2)}, u32[]{:S(2)}) collective-permute-start(bf16[6,8,9600]{2,1,0:T(8,128)(2,1)} %collective-permute-done.20.rest_3_), channel_id=1, source_target_pairs={{0,2},{1,3},{2,0},{3,1},{4,6},{5,7},{6,4},{7,5},{8,10},{9,11},{10,... | collective-permute-start | bytes 2764808 | tf_op jit(solution)/shard_map/ppermute | solution.py:443
  253.8 23.7 %collective-permute-start.34 = (bf16[6,8,9600]{2,1,0:T(8,128)(2,1)}, bf16[6,8,9600]{2,1,0:T(8,128)(2,1)}, u32[]{:S(2)}, u32[]{:S(2)}) collective-permute-start(bf16[6,8,9600]{2,1,0:T(8,128)(2,1)} %collective-permute-done.30.rest_7_), channel_id=1, source_target_pairs={{0,4},{1,5},{2,6},{3,7},{4,0},{5,1},{6,2},{7,3},{8,12},{9,13},{10,... | collective-permute-start | bytes 2764808 | tf_op jit(solution)/shard_map/ppermute | solution.py:443
  253.8 31.1 %collective-permute-start.36 = (bf16[8,8,9600]{2,1,0:T(8,128)(2,1)}, bf16[8,8,9600]{2,1,0:T(8,128)(2,1)S(1)}, u32[]{:S(2)}, u32[]{:S(2)}) collective-permute-start(bf16[8,8,9600]{2,1,0:T(8,128)(2,1)} %collective-permute-done.22.rest_5_), channel_id=1, source_target_pairs={{0,8},{1,9},{2,10},{3,11},{4,12},{5,13},{6,14},{7,15},{8,24},{9,25... | collective-permute-start | bytes 3686408 | tf_op jit(solution)/shard_map/ppermute | solution.py:443
  255.5 43.4 %collective-permute-start.39 = (bf16[6,8,9600]{2,1,0:T(8,128)(2,1)}, bf16[6,8,9600]{2,1,0:T(8,128)(2,1)}, u32[]{:S(2)}, u32[]{:S(2)}) collective-permute-start(bf16[6,8,9600]{2,1,0:T(8,128)(2,1)} %collective-permute-done.30.rest_7_), channel_id=1, source_target_pairs={{0,2},{1,3},{2,0},{3,1},{4,6},{5,7},{6,4},{7,5},{8,10},{9,11},{10,... | collective-permute-start | bytes 2764808 | tf_op jit(solution)/shard_map/ppermute | solution.py:443
  258.2 39.0 %collective-permute-start.31 = (bf16[6,8,9600]{2,1,0:T(8,128)(2,1)S(1)}, bf16[6,8,9600]{2,1,0:T(8,128)(2,1)}, u32[]{:S(2)}, u32[]{:S(2)}) collective-permute-start(bf16[6,8,9600]{2,1,0:T(8,128)(2,1)S(1)} %copy-done.37), channel_id=1, source_target_pairs={{0,4},{1,5},{2,6},{3,7},{4,0},{5,1},{6,2},{7,3},{8,12},{9,13},{10,... | collective-permute-start | bytes 2764808 | tf_op jit(solution)/shard_map/ppermute | solution.py:443
  277.5 33.8 %collective-permute-start.41 = (bf16[8,8,9600]{2,1,0:T(8,128)(2,1)S(1)}, bf16[8,8,9600]{2,1,0:T(8,128)(2,1)S(1)}, u32[]{:S(2)}, u32[]{:S(2)}) collective-permute-start(bf16[8,8,9600]{2,1,0:T(8,128)(2,1)S(1)} %collective-permute-done.35.rest_4_), channel_id=1, source_target_pairs={{0,8},{1,9},{2,10},{3,11},{4,12},{5,13},{6,14},{7,15},{8,24},{9,25... | collective-permute-start | bytes 3686408 | tf_op jit(solution)/shard_map/ppermute | solution.py:443
  279.1 37.9 %collective-permute-start.37 = (bf16[6,8,9600]{2,1,0:T(8,128)(2,1)S(1)}, bf16[6,8,9600]{2,1,0:T(8,128)(2,1)}, u32[]{:S(2)}, u32[]{:S(2)}) collective-permute-start(bf16[6,8,9600]{2,1,0:T(8,128)(2,1)S(1)} %copy-done.39), channel_id=1, source_target_pairs={{0,4},{1,5},{2,6},{3,7},{4,0},{5,1},{6,2},{7,3},{8,12},{9,13},{10,... | collective-permute-start | bytes 2764808 | tf_op jit(solution)/shard_map/ppermute | solution.py:443
  285.0 32.1 %collective-permute-start.40 = (bf16[6,8,9600]{2,1,0:T(8,128)(2,1)}, bf16[6,8,9600]{2,1,0:T(8,128)(2,1)}, u32[]{:S(2)}, u32[]{:S(2)}) collective-permute-start(bf16[6,8,9600]{2,1,0:T(8,128)(2,1)} %collective-permute-done.34.rest_3_), channel_id=1, source_target_pairs={{0,2},{1,3},{2,0},{3,1},{4,6},{5,7},{6,4},{7,5},{8,10},{9,11},{10,... | collective-permute-start | bytes 2764808 | tf_op jit(solution)/shard_map/ppermute | solution.py:443
  297.3 36.0 %collective-permute-start.42 = (bf16[8,8,9600]{2,1,0:T(8,128)(2,1)S(1)}, bf16[8,8,9600]{2,1,0:T(8,128)(2,1)S(1)}, u32[]{:S(2)}, u32[]{:S(2)}) collective-permute-start(bf16[8,8,9600]{2,1,0:T(8,128)(2,1)S(1)} %collective-permute-done.36.rest_5_), channel_id=1, source_target_pairs={{0,8},{1,9},{2,10},{3,11},{4,12},{5,13},{6,14},{7,15},{8,24},{9,25... | collective-permute-start | bytes 3686408 | tf_op jit(solution)/shard_map/ppermute | solution.py:443
  298.9 32.2 %collective-permute-start.38 = (bf16[6,8,9600]{2,1,0:T(8,128)(2,1)}, bf16[6,8,9600]{2,1,0:T(8,128)(2,1)}, u32[]{:S(2)}, u32[]{:S(2)}) collective-permute-start(bf16[6,8,9600]{2,1,0:T(8,128)(2,1)} %collective-permute-done.28.rest_4_), channel_id=1, source_target_pairs={{0,4},{1,5},{2,6},{3,7},{4,0},{5,1},{6,2},{7,3},{8,12},{9,13},{10,... | collective-permute-start | bytes 2764808 | tf_op jit(solution)/shard_map/ppermute | solution.py:443
  (25 other events, 281.7 us)

commit v5 on v4

--- a/solution.py
+++ b/solution.py
@@ -12,10 +12,7 @@
 R = 5
 GROUP = 16
 NONE = 1 << 30
-ROUTES = (("zxy", 6), ("zyx", 6), ("xyz", 2), ("yxz", 2))
-PHASE_ENDS = (0.3, 0.5, 0.67, 0.82, 1.0)
-IN_FLIGHT = 2
-SLACK = 15.0
+SHARES = (7, 7, 1, 1)
 HEAD = 64
 WEIGHT = 8
 
@@ -100,11 +97,10 @@
 
 
 def pair_kernel(frames, buffers, scale, rows_ref, vids_ref, ends_ref, entry_ref, one_ref,
-                two_ref, three_ref, before_ref, own_hbm, other_hbm, *rest):
+                two_ref, three_ref, before_ref, v_hbm, *rest):
     q_hbm, rest = rest[:buffers], rest[buffers:]
     out_ref, q_in, v_in, q_rows, v_rows, maps, q_sem, v_sem = rest
-    idx_dev = own_hbm.shape[0]
-    width = own_hbm.shape[2] // R
+    width = v_hbm.shape[2] // R
     side = GROUP * frames
     count = ends_ref[buffers - 1]
     groups = (count + GROUP - 1) // GROUP
@@ -123,17 +119,9 @@
             lax.fori_loop(low, high, one_query, 0)
 
         def one_video(p, _):
-            vid = vids_ref[first + p]
-
-            @pl.when(vid < idx_dev)
-            def _():
-                pltpu.make_async_copy(own_hbm.at[vid], v_in.at[slot, p], v_sem.at[slot]).start()
-
-            @pl.when(vid >= idx_dev)
-            def _():
-                pltpu.make_async_copy(
-                    other_hbm.at[vid - idx_dev], v_in.at[slot, p], v_sem.at[slot]
-                ).start()
+            pltpu.make_async_copy(
+                v_hbm.at[vids_ref[first + p]], v_in.at[slot, p], v_sem.at[slot]
+            ).start()
             return 0
         lax.fori_loop(0, GROUP, one_video, 0)
 
@@ -207,8 +195,8 @@
     lax.fori_loop(0, (count + HEAD - 1) // HEAD, head, 0)
 
 
-def pair_scores(blocks, own, other, rows, vids, ends, entry, heads, before, name):
-    frames, width = own.shape[1], own.shape[2]
+def pair_scores(blocks, videos, rows, vids, ends, entry, heads, before, name):
+    frames, width = videos.shape[1], videos.shape[2]
     cap = rows.shape[0]
     side = GROUP * frames
     scale = 1.0 / (math.sqrt(width // R) * R)
@@ -218,7 +206,7 @@
     return pl.pallas_call(
         functools.partial(pair_kernel, frames, len(blocks), scale),
         out_shape=jax.ShapeDtypeStruct(before.shape, jnp.float32),
-        in_specs=[smem] * 3 + [vmem] * 5 + [hbm] * (2 + len(blocks)),
+        in_specs=[smem] * 3 + [vmem] * 5 + [hbm] * (1 + len(blocks)),
         out_specs=vmem,
         scratch_shapes=[
             pltpu.VMEM((2, GROUP, frames, width), jnp.bfloat16),
@@ -235,7 +223,7 @@
             bytes_accessed=cap * frames * width * 4, transcendentals=0,
         ),
         name=name,
-    )(rows, vids, ends, entry, *heads, before, own, other, *blocks)
+    )(rows, vids, ends, entry, *heads, before, videos, *blocks)
 
 
 def chip_places(mesh):
@@ -254,62 +242,112 @@
     return order.index(coordinate)
 
 
-def plan(sizes, q_dev):
-    parts = sum(n for _, n in ROUTES)
-    messages = []
-    starts, start = [], 0
-    for r, (order, share) in enumerate(ROUTES):
-        n = q_dev * share // parts
-        starts.append((start, n))
-        start += n
-        have = [(r, 0, 0, 0)]
-        for at, letter in enumerate(order):
-            axis = "zyx".index(letter)
-            if letter == "z" and at == 2:
-                for k in range(1, sizes[0]):
-                    messages.append((0, (r, k - 1), (r, k), n * sizes[1] * sizes[2]))
-                break
-            for block in list(have):
-                for k in range(1, sizes[axis]):
-                    to = list(block)
-                    to[1 + axis] = k
-                    messages.append((axis, block, tuple(to), n))
-                    block = tuple(to)
-                    have.append(block)
-    users = {}
-    for m in messages:
-        users.setdefault(m[1], []).append(m)
-
-    def planes(block):
-        r, z = block[:2]
-        if len(block) == 4 and ROUTES[r][0][2] == "z":
-            return users.get((r, 0), [])
-        return []
-
-    @functools.cache
-    def tail(m):
-        after = users.get(m[2], []) + planes(m[2])
-        return m[3] + max([tail(a) for a in after], default=0)
-
-    ready = {(r, 0, 0, 0): 0.0 for r in range(len(ROUTES))}
-    free = [0.0, 0.0, 0.0]
-    waiting, order = list(messages), []
-
-    def when(block):
-        if len(block) == 2 and block[1] == 0:
-            cells = [(block[0], 0, y, x) for y in range(sizes[1]) for x in range(sizes[2])]
-            return max(ready.get(c, math.inf) for c in cells)
-        return ready.get(block, math.inf)
-
-    begins = {}
-    while waiting:
-        best = min(waiting, key=lambda m: (max(free[m[0]], when(m[1])), -tail(m), m))
-        begin = max(free[best[0]], when(best[1]))
-        free[best[0]] = ready[best[2]] = begin + best[3] + 0.5
-        begins[best] = begin
-        order.append(best)
-        waiting.remove(best)
-    return starts, order, begins, ready
+class Gather:
+    def __init__(self, sizes, steps, queries):
+        self.steps = steps
+        q_dev = queries.shape[0]
+        depth, height, width = sizes
+        counts = [q_dev * s // sum(SHARES) for s in SHARES]
+        starts = [sum(counts[:r]) for r in range(4)]
+        a = counts[0] + counts[1]
+        self.blocks, self.cells, self.arrival = {}, {}, {}
+
+        def put(key, array, cells, at):
+            self.blocks[key], self.cells[key], self.arrival[key] = array, cells, at
+
+        def moved(cells, axis, k):
+            out = []
+            for off, q, n in cells:
+                off = list(off)
+                off[axis] = k
+                out.append((tuple(off), q, n))
+            return out
+
+        here = (0, 0, 0)
+        put(("a", 0), queries[:a], [(here, 0, a)], -1)
+        for r in (2, 3):
+            put(("b", r), queries[starts[r]:starts[r] + counts[r]], [(here, starts[r], counts[r])], -1)
+
+        self.describe = {}
+
+        def ring(axis, source, name, cells):
+            out = []
+            for k in range(1, sizes[axis]):
+                target = name + (k,)
+                self.describe[target] = moved(cells, axis, k)
+                out.append((axis, source, target))
+                source = target
+            return out
+
+        first, second = [], []
+        joins = {}
+        for r, (p, q) in ((2, (2, 1)), (3, (1, 2))):
+            cells = self.cells[("b", r)]
+            line = ring(p, ("b", r), ("b", r, "line"), cells)
+            first.append(line)
+            joins[("b", r, "row")] = [("b", r)] + [m[2] for m in line]
+            row = [c for k in range(sizes[p]) for c in moved(cells, p, k)]
+            self.describe[("b", r, "row")] = row
+            turn = ring(q, ("b", r, "row"), ("b", r, "turn"), row)
+            second.append(turn)
+            joins[("b", r, "plane")] = [("b", r, "row")] + [m[2] for m in turn]
+            self.describe[("b", r, "plane")] = [c for k in range(sizes[q]) for c in moved(row, q, k)]
+        joins[("b", 0)] = [("b", 2, "plane"), ("b", 3, "plane")]
+        self.describe[("b", 0)] = [c for r in (2, 3) for c in self.describe[("b", r, "plane")]]
+        self.joins = joins
+        self.halves = {}
+
+        rounds = []
+        for k in range(depth):
+            for r, (p, q) in ((0, (2, 1)), (1, (1, 2))):
+                own = ("a", k, r)
+                self.halves[own] = (("a", k), starts[r], counts[r])
+                self.describe[own] = [((k, 0, 0), starts[r], counts[r])]
+            lists = {1: [], 2: []}
+            later = {1: [], 2: []}
+            for r, (p, q) in ((0, (2, 1)), (1, (1, 2))):
+                own = ("a", k, r)
+                line = ring(p, own, ("a", k, r, "line"), self.describe[own])
+                lists[p] += line
+                for i, source in enumerate([own] + [m[2] for m in line]):
+                    later[q] += ring(q, source, ("a", k, r, "turn", i), self.describe[source])
+            both = [lists[axis] + later[axis] for axis in (2, 1)]
+            for i in range(max(map(len, both))):
+                rounds.append([l[i] for l in both if i < len(l)])
+        pairs_of = lambda ls: [[l[i] for l in ls if i < len(l)] for i in range(max(map(len, ls)))]
+        lead, middle = pairs_of(first), pairs_of(second)
+
+        deep = ring(0, ("a", 0), ("a",), self.cells[("a", 0)]) + ring(
+            0, ("b", 0), ("b",), self.describe[("b", 0)]
+        )
+        gap = max(1, len(rounds) // max(1, len(deep)))
+        while len(rounds) < gap * len(deep):
+            rounds.append([])
+        for i, m in enumerate(deep):
+            rounds[i * gap].append(m)
+        self.per_plane = len(rounds) // depth
+        at = min(2, len(rounds))
+        self.rounds = lead + rounds[:at] + middle + rounds[at:]
+        self.offset = len(lead) + len(middle)
+        for i, messages in enumerate(self.rounds):
+            for axis, _, target in messages:
+                self.arrival[target] = i if axis else i + gap - 1
+                self.cells[target] = self.describe[target]
+        self.arrival[("b", 0)] = len(lead) + at + len(middle) - 1
+        self.cells[("b", 0)] = self.describe[("b", 0)]
+
+    def block(self, key):
+        if key not in self.blocks:
+            if key in self.joins:
+                self.blocks[key] = jnp.concatenate([self.block(k) for k in self.joins[key]], axis=0)
+            else:
+                whole, start, n = self.halves[key]
+                self.blocks[key] = self.block(whole)[start:start + n]
+        return self.blocks[key]
+
+    def buffers(self):
+        keys = [k for k in self.arrival if k[0] == "a" and (len(k) == 2 or len(k) > 3)]
+        return keys + [k for k in self.arrival if k[0] == "b" and len(k) == 2 and isinstance(k[1], int)]
 
 
 def body(places, sizes, queries, index_videos, candidates, conv_one, conv_two, conv_three):
@@ -334,118 +372,106 @@
             out += [(2 * i + c, 2 * where[tuple(to)] + c) for c in range(2)]
         return out
 
-    steps = [step_along(a) for a in range(3)]
-
-    all_ids = lax.all_to_all(
-        jnp.broadcast_to(candidates.reshape(1, pairs), (devices, pairs)), "shard", split_axis=0,
-        concat_axis=0, tiled=True,
+    videos = lax.all_gather(
+        index_videos, "shard", axis=0, tiled=True,
+        axis_index_groups=[[2 * c, 2 * c + 1] for c in range(chips)],
     )
-    other = lax.ppermute(index_videos, "shard", [(d, d ^ 1) for d in range(devices)])
-
-    starts, order, begins, arrival = plan(sizes, q_dev)
-    plane = [(y, x) for y in range(sizes[1]) for x in range(sizes[2])]
-
-    last = max(arrival.values())
-    phase_of = lambda key: next(
-        p for p, end in enumerate(PHASE_ENDS) if arrival[key] <= end * last + 1e-6
-    )
-    phases = [[] for _ in PHASE_ENDS]
+    gather = Gather(sizes, [step_along(a) for a in range(3)], queries)
+    rounds = gather.rounds
+
+    total = len(rounds)
+    ends = [gather.offset + gather.per_plane * (z + 1) - 1 for z in range(sizes[0] - 1)]
+    ends = sorted({e for e in ends if 0 <= e < total - 2} | {total - 2, total - 1})
+    phases = [[] for _ in ends]
     place = {}
-    for r, (start, n) in enumerate(starts):
-        for z in range(sizes[0]):
-            whole = ROUTES[r][0][2] == "z" and z > 0
-            for i, (y, x) in enumerate(plane):
-                key = (r, z) if whole else (r, z, y, x)
-                p = phase_of(key)
-                if key not in phases[p]:
-                    phases[p].append(key)
-                for q in range(n):
-                    place[(z, y, x), start + q] = (p, phases[p].index(key), q + (i * n if whole else 0))
-    stride = 1 << max(4, (len(plane) * max(n for _, n in starts) - 1).bit_length())
+    for key in gather.buffers():
+        p = next(i for i, e in enumerate(ends) if gather.arrival[key] <= e)
+        row = 0
+        for off, first, n in gather.cells[key]:
+            for q in range(first, first + n):
+                place[off, q] = (p, len(phases[p]), row)
+                row += 1
+        phases[p].append(key)
+    stride = 1 << max(row for _, _, row in place.values()).bit_length()
     most = max(len(p) for p in phases)
-    spot = np.zeros((chips, chips, q_dev), np.int32)
     caps = [0] * len(phases)
-    offsets = sorted({off for off, _ in place})
-    for off in offsets:
+    for off in sorted({off for off, _ in place}):
         for p in range(len(phases)):
             here = sum(place[off, q][0] == p for q in range(q_dev))
             caps[p] += min(here * k_count, 2 * per_holder)
+    caps = [-(-c // HEAD) * HEAD for c in caps]
+    spot = np.zeros((chips, chips, q_dev), np.int32)
     for c in range(chips):
         for s in range(chips):
             off = tuple((a - b) % n for a, b, n in zip(rings[c], rings[s], sizes))
             for q in range(q_dev):
                 p, b, row = place[off, q]
                 spot[c, s, q] = (p * most + b) * stride + row
-    caps = [-(-c // HEAD) * HEAD for c in caps]
-
-    spot = lax.dynamic_index_in_dim(jnp.asarray(spot), chip, 0, keepdims=False)
-    spot = jnp.broadcast_to(spot[:, :, None], (chips, q_dev, k_count)).reshape(chips * pairs)
-    ids = all_ids.reshape(chips, 2, pairs)
-    ids = jnp.where(core == 0, ids[:, 0], ids[:, 1]).reshape(chips * pairs)
-    mine = ids // (2 * idx_dev) == chip
-    local = ids % (2 * idx_dev)
-    local = jnp.where(local // idx_dev == core, local % idx_dev, local % idx_dev + idx_dev)
-    code = jnp.where(mine, spot * (2 * idx_dev) + local, NONE)
-    code, entry = lax.sort((code, jnp.arange(chips * pairs, dtype=jnp.int32)), num_keys=1)
-    total = chips * 2 * per_holder
-    code = jnp.concatenate([code[:total], jnp.full((max(caps),), NONE, jnp.int32)])
-    entry = jnp.concatenate([entry[:total], jnp.zeros((max(caps),), jnp.int32)])
-    spots = code // (2 * idx_dev)
-    phase = jnp.where(code < NONE, spots // (most * stride), len(phases))
-    counts = jnp.sum(
-        (phase[:, None] == jnp.arange(len(phases))[None, :]).astype(jnp.int32), axis=0
-    )
-    firsts = jnp.cumsum(counts) - counts
-    spots = spots % (most * stride)
-    vids = code % (2 * idx_dev)
+
+    state = {}
+
+    def lists(all_ids):
+        spots = lax.dynamic_index_in_dim(jnp.asarray(spot), chip, 0, keepdims=False)
+        spots = jnp.broadcast_to(spots[:, :, None], (chips, q_dev, k_count)).reshape(chips * pairs)
+        ids = all_ids.reshape(chips, 2, pairs)
+        ids = jnp.where(core == 0, ids[:, 0], ids[:, 1]).reshape(chips * pairs)
+        mine = ids // (2 * idx_dev) == chip
+        code = jnp.where(mine, spots * (2 * idx_dev) + ids % (2 * idx_dev), NONE)
+        code, entry = lax.sort((code, jnp.arange(chips * pairs, dtype=jnp.int32)), num_keys=1)
+        keep = chips * 2 * per_holder
+        code = jnp.concatenate([code[:keep], jnp.full((max(caps),), NONE, jnp.int32)])
+        entry = jnp.concatenate([entry[:keep], jnp.zeros((max(caps),), jnp.int32)])
+        spots = code // (2 * idx_dev)
+        phase = jnp.where(code < NONE, spots // (most * stride), len(phases))
+        counts = jnp.sum(
+            (phase[:, None] == jnp.arange(len(phases))[None, :]).astype(jnp.int32), axis=0
+        )
+        return spots % (most * stride), code % (2 * idx_dev), entry, counts, jnp.cumsum(counts) - counts
 
     heads = head_matrices(conv_one, conv_two, conv_three)
     tables = [jnp.zeros((chips, pairs), jnp.float32)]
 
-    def score(p):
+    def score():
+        p = len(tables) - 1
+        spots, vids, entry, counts, firsts = state["lists"]
         cut = lambda a: lax.dynamic_slice(a, (firsts[p],), (caps[p],))
         valid = jnp.arange(caps[p]) < counts[p]
-        spot, vid = cut(spots), jnp.where(valid, cut(vids), 0)
-        rows = jnp.where(valid, spot % stride, 0)
+        at, vid = cut(spots), jnp.where(valid, cut(vids), 0)
+        rows = jnp.where(valid, at % stride, 0)
         entries = jnp.where(valid, cut(entry), NONE)
-        ends = jnp.sum(
-            (valid[None, :] & (spot[None, :] // stride <= jnp.arange(len(phases[p]))[:, None]))
+        upto = jnp.sum(
+            (valid[None, :] & (at[None, :] // stride <= jnp.arange(len(phases[p]))[:, None]))
             .astype(jnp.int32), axis=1,
         )
         tables.append(pair_scores(
-            [blocks[k] for k in phases[p]], index_videos, other, rows, vid, ends,
+            [gather.block(k) for k in phases[p]], videos, rows, vid, upto,
             entries.reshape(caps[p], 1), heads, tables[-1], "phase_" + str(p),
         ))
 
-    blocks = {}
-    for r, (start, n) in enumerate(starts):
-        blocks[(r, 0, 0, 0)] = queries[start:start + n]
-
-    def block_of(key):
-        if key not in blocks:
-            blocks[key] = jnp.concatenate([blocks[(key[0], 0, y, x)] for y, x in plane], axis=0)
-        return blocks[key]
-
-    done = [[], [], []]
-    for m in order:
-        axis, source, target, _ = m
-        behind = done[axis][-IN_FLIGHT:][:1] if len(done[axis]) >= IN_FLIGHT else []
-        if len(done[axis]) == 4:
-            behind.append(all_ids)
-        if len(done[axis]) == 3 and axis == 0:
-            behind.append(other)
-        while len(tables) < len(phases) and begins[m] > PHASE_ENDS[len(tables) - 1] * last + SLACK:
-            score(len(tables) - 1)
-            behind.append(tables[-1])
-        sent = block_of(source)
-        if behind:
-            sent = lax.optimization_barrier((sent, *behind))[0]
-        blocks[target] = lax.ppermute(sent, "shard", steps[axis])
-        done[axis].append(blocks[target])
-    while len(tables) <= len(phases):
-        score(len(tables) - 1)
-    table = tables[-1]
-    table = jnp.where(jnp.arange(2)[None, :, None] == core, table[:, None], 0.0)
+    done, deep = [], []
+    for i, messages in enumerate(rounds):
+        behind = list(done[i - 2]) if i >= 2 else []
+        if any(axis == 0 for axis, _, _ in messages):
+            behind += deep[-1:]
+        if len(tables) <= len(ends) and i >= 2:
+            if i == min(ends[len(tables) - 1] + 4, total - 1) and ends[len(tables) - 1] <= i - 2:
+                score()
+                behind.append(tables[-1])
+        sent = [gather.block(source) for _, source, _ in messages]
+        sent = lax.optimization_barrier((*sent, *behind))[:len(sent)]
+        done.append([])
+        for (axis, _, target), block in zip(messages, sent):
+            gather.blocks[target] = lax.ppermute(block, "shard", gather.steps[axis])
+            (done[i] if axis else deep).append(gather.blocks[target])
+        if i == 0:
+            ids = lax.optimization_barrier((candidates, *done[0]))[0].reshape(1, pairs)
+            state["lists"] = lists(lax.all_to_all(
+                jnp.broadcast_to(ids, (devices, pairs)), "shard", split_axis=0, concat_axis=0,
+                tiled=True,
+            ))
+    while len(tables) <= len(ends):
+        score()
+    table = jnp.where(jnp.arange(2)[None, :, None] == core, tables[-1][:, None], 0.0)
     scores = lax.all_to_all(
         table.reshape(devices, pairs), "shard", split_axis=0, concat_axis=0, tiled=True
     )

time: 363 us -> 382 us (1.052)
  waiting for transfers between devices: 152 us -> 189 us
  starting transfers between devices: 65.5 us -> 39.1 us
  between operations: 10.2 us -> 23.2 us
  local copies, waits for them, and re-layouts: 17.5 us -> 27.2 us
  Pallas kernels: 70.2 us -> 63.4 us
  other arithmetic: 31.2 us -> 26 us
    all_to_all x1, waiting for transfers between devices: 0.01 us -> 27.1 us  [body(): lax.all_to_all(jnp.broadcast_to(ids, (devices, pairs)), 'shard', split_ax...]
    ppermute x43 -> x34, starting transfers between devices: 58.6 us -> 34.2 us  [body(): gather.blocks[target] = lax.ppermute(block, 'shard', gather.steps[axis])]
    ppermute x43 -> x34, waiting for transfers between devices: 152 us -> 161 us  [body(): gather.blocks[target] = lax.ppermute(block, 'shard', gather.steps[axis])]
    pallas_call x5, Pallas kernels: 61.6 us -> 54.8 us  [pair_scores(): pl.pallas_call(functools.partial(pair_kernel, frames, len(blocks), scale)...]
    slice x2 -> x5, local copies, waits for them, and re-layouts: 2.68 us -> 8.83 us  [the longest x4 7.35 us: block(): self.blocks[key] = self.block(whole)[start:start + n]]
    select_n x14 -> x12, other arithmetic: 12.7 us -> 9.72 us  [the longest x5 6.15 us: score(): rows = jnp.where(valid, at % stride, 0)]
    unnamed x91 -> x49, local copies, waits for them, and re-layouts: 6.16 us -> 8.91 us
  transfers between devices with their start and end apart: 44 -> 36, of which waited for: 20 -> 19; matrix products, arithmetic and copies ran while one was open for 12% -> 12% of each run, Pallas kernels for 17% -> 15%
where the time goes in v5:
time: 382 us; the launch traced here: 381 us
  waiting for transfers between devices  189 us (49%)
  Pallas kernels  63.4 us (17%)
  starting transfers between devices  39.1 us (10%)
  local copies, waits for them, and re-layouts  27.2 us (7%)
  other arithmetic  26 us (7%)
  between operations  23.2 us (6%)
  blocking collectives  12.6 us (3%)
    ppermute x34, waiting for transfers between devices, body(): gather.blocks[target] = lax.ppermute(block, 'shard', gather.steps[axis])  161 us
    pallas_call x5, Pallas kernels, pair_scores(): pl.pallas_call(functools.partial(pair_kernel, frames, len(blocks), scale)...  54.8 us
    ppermute x34, starting transfers between devices, body(): gather.blocks[target] = lax.ppermute(block, 'shard', gather.steps[axis])  34.2 us
    all_to_all x1, waiting for transfers between devices, body(): lax.all_to_all(jnp.broadcast_to(ids, (devices, pairs)), 'shard', split_ax...  27.1 us
    all_to_all x1, blocking collectives, body(): lax.all_to_all(table.reshape(devices, pairs), 'shard', split_axis=0, conc...  12.6 us
    unnamed x49, local copies, waits for them, and re-layouts  8.91 us
    pallas_call x1, Pallas kernels, head_matrices(): pl.pallas_call(head_kernel, out_shape=[jax.ShapeDtypeStruct(s, jnp.bfloat...  8.54 us
  transfers between devices with their start and end apart: 36, of which 19 were waited for; matrix products, arithmetic and copies ran while one was open for 12% of the time, Pallas kernels for 15%

profile of v5, /device:TPU:0, one launch (start us, length us, event | category | flops | bytes accessed | tf_op | source)
XLA Modules:
  0.0 380.7 jit_solution(11722246570579679865)
XLA Ops:
  7.3 1.0 copy-done.4
  8.9 2.9 collective-permute-start
  11.8 1.5 collective-permute-start.1
  13.4 1.5 slice.105.rest_0_
  14.9 1.5 fusion.18
  16.9 2.1 collective-permute-start.4
  20.6 8.5 %head_matrices.1 = (bf16[64,2048]{1,0:T(8,128)(2,1)S(1)}, bf16[512,1024]{1,0:T(8,128)(2,1)S(1)}, bf16[256,256]{1,0:T(8,128)(2,1)S(1)}) custom-call(bf16[9,1,32]{2,1,0:T(2,128)(2,1)S(1)} %reshape.255.one_w, bf16[9,32,64]{2,1,0:T(8,128)(2,1)S(1)} %bitcast.38, bf16[9,1,64]{2,1,0:T(2,128)(2,1)S(1)} %reshape.256.three_w), custom_call_target="tpu_custom_call" | custom-call | flops 1000000000 | bytes 3000000 | tf_op jit(solution)/shard_map/head_matrices/pallas_call | solution.py:87
  29.1 1.0 copy-done.1
  32.3 4.8 %all-to-all-start = ((s32[32,1,128]{2,1,0:T(1,128)}), s32[32,1,128]{2,1,0:T(1,128)S(1)}, u32[]{:S(2)}, u32[]{:S(2)}) async-start(s32[32,1,128]{2,1,0:T(1,128)} %broadcast_in_dim.96), calls=%async_computation | async-start | bytes 32768 | tf_op jit(solution)/shard_map/all_to_all | solution.py:468
  37.2 1.8 collective-permute-start.5
  39.0 1.5 collective-permute-start.6
  40.5 0.8 pad_maximum_fusion
  41.9 27.1 %all-to-all-done = s32[32,1,128]{2,1,0:T(1,128)S(1)} async-done(((s32[32,1,128]{2,1,0:T(1,128)}), s32[32,1,128]{2,1,0:T(1,128)S(1)}, u32[]{:S(2)}, u32[]{:S(2)}) %all-to-all-start) | async-done | bytes 16416 | tf_op jit(solution)/shard_map/all_to_all | solution.py:468
  69.1 4.4 %sort.15 = (s32[2048]{0:T(1024)S(1)}, s32[2048]{0:T(1024)S(1)}) sort(s32[2048]{0:T(1024)S(1)} %fusion.2, s32[2048]{0:T(1024)S(1)} %iota.59), dimensions={0}, to_apply=%region_0.1 | sort | flops 22528 | bytes 32768 | tf_op jit(solution)/shard_map/sort | solution.py:420
  82.1 0.8 select_bitcast_fusion.4
  86.1 2.7 select_bitcast_fusion
  90.3 0.7 copy.46.entry_ref
  98.6 1.2 fusion.14.rows_ref
  99.8 1.2 fusion.15.rows_ref
  100.9 1.2 fusion.16.rows_ref
  102.1 1.2 fusion.17.rows_ref
  103.9 3.2 dynamic-slice_select_fusion
  107.1 1.4 fusion.13
  109.1 3.5 collective-permute-done.9
  112.6 0.7 constant_dynamic-update-slice_fusion.3
  116.4 2.7 fusion.21
  119.2 1.5 collective-permute-start.12
  120.6 1.4 collective-permute-start.13
  122.0 0.7 constant_dynamic-update-slice_fusion.rest_8_
  122.8 40.5 %collective-permute-done.12.rest_1_ = bf16[7,8,9600]{2,1,0:T(8,128)(2,1)S(1)} collective-permute-done((bf16[7,8,9600]{2,1,0:T(8,128)(2,1)S(1)}, bf16[7,8,9600]{2,1,0:T(8,128)(2,1)S(1)}, u32[]{:S(2)}, u32[]{:S(2)}) %collective-permute-start.12) | collective-permute-done | bytes 1075232 | tf_op jit(solution)/shard_map/ppermute | solution.py:464
  163.3 1.1 collective-permute-start.17
  164.4 1.0 collective-permute-start.18
  165.5 1.6 collective-permute-start.14
  168.1 1.5 fusion.20
  169.6 20.5 %collective-permute-done.17.rest_6_ = bf16[7,8,9600]{2,1,0:T(8,128)(2,1)S(1)} collective-permute-done((bf16[7,8,9600]{2,1,0:T(8,128)(2,1)S(1)}, bf16[7,8,9600]{2,1,0:T(8,128)(2,1)S(1)}, u32[]{:S(2)}, u32[]{:S(2)}) %collective-permute-start.17) | collective-permute-done | bytes 1075232 | tf_op jit(solution)/shard_map/ppermute | solution.py:464
  190.1 1.1 collective-permute-done.18.rest_7_
  191.1 1.0 copy-done.17
  192.1 1.0 collective-permute-start.21
  193.1 1.5 collective-permute-start.22
  195.2 13.9 %phase_0.1.before_ref = f32[16,128]{1,0:T(8,128)} custom-call(s32[128]{0:T(128)} %fusion.17.rows_ref, s32[128]{0:T(128)} %get-tuple-element.113.vids_ref, s32[9]{0:T(128)} %convert_reduce_fusion.1.ends_ref, s32[128,1]{1,0:T(8,128)} %copy.45.entry_ref, bf16[64,2048]{1,0:T(8,128)(2,1)} %copy-done.2, bf16[512,1024]{1,0:T(8,128)(2,1)} %copy-done.1, ...), custom_call_target="tpu_custom_call" | custom-call | flops 100663296000 | bytes 39321600 | tf_op jit(solution)/shard_map/phase_0/pallas_call | solution.py:206
  209.2 4.0 %collective-permute-done.14.rest_3_ = bf16[7,8,9600]{2,1,0:T(8,128)(2,1)} collective-permute-done((bf16[7,8,9600]{2,1,0:T(8,128)(2,1)}, bf16[7,8,9600]{2,1,0:T(8,128)(2,1)}, u32[]{:S(2)}, u32[]{:S(2)}) %collective-permute-start.14) | collective-permute-done | bytes 1075232 | tf_op jit(solution)/shard_map/ppermute | solution.py:464
  213.2 1.1 collective-permute-done.15.rest_4_
  215.4 1.5 collective-permute-start.20
  217.2 1.7 fusion.19
  218.9 37.9 %collective-permute-done.19.rest_0_ = bf16[7,8,9600]{2,1,0:T(8,128)(2,1)S(1)} collective-permute-done((bf16[7,8,9600]{2,1,0:T(8,128)(2,1)}, bf16[7,8,9600]{2,1,0:T(8,128)(2,1)S(1)}, u32[]{:S(2)}, u32[]{:S(2)}) %collective-permute-start.19) | collective-permute-done | bytes 1075232 | tf_op jit(solution)/shard_map/ppermute | solution.py:464
  257.2 1.5 collective-permute-start.24
  258.7 1.5 collective-permute-start.25
  260.6 14.1 %phase_1.1.before_ref = f32[16,128]{1,0:T(8,128)} custom-call(s32[128]{0:T(128)} %fusion.16.rows_ref, s32[128]{0:T(128)} %get-tuple-element.114.vids_ref, s32[8]{0:T(128)} %convert_reduce_fusion.2.ends_ref, s32[128,1]{1,0:T(8,128)} %copy.46.entry_ref, bf16[64,2048]{1,0:T(8,128)(2,1)} %copy-done.2, bf16[512,1024]{1,0:T(8,128)(2,1)} %copy-done.1, ...), custom_call_target="tpu_custom_call" | custom-call | flops 100663296000 | bytes 39321600 | tf_op jit(solution)/shard_map/phase_1/pallas_call | solution.py:206
  275.4 1.2 collective-permute-start.27
  276.6 7.6 %collective-permute-done.24.rest_4_ = bf16[7,8,9600]{2,1,0:T(8,128)(2,1)} collective-permute-done((bf16[7,8,9600]{2,1,0:T(8,128)(2,1)}, bf16[7,8,9600]{2,1,0:T(8,128)(2,1)}, u32[]{:S(2)}, u32[]{:S(2)}) %collective-permute-start.24) | collective-permute-done | bytes 1075232 | tf_op jit(solution)/shard_map/ppermute | solution.py:464
  284.2 1.3 collective-permute-done.25.rest_5_
  285.5 1.5 collective-permute-done.28.rest_4_
  288.1 11.2 %phase_2.1.before_ref = f32[16,128]{1,0:T(8,128)} custom-call(s32[128]{0:T(128)} %fusion.15.rows_ref, s32[128]{0:T(128)} %get-tuple-element.115.vids_ref, s32[7]{0:T(128)} %convert_reduce_fusion.3.ends_ref, s32[128,1]{1,0:T(8,128)} %copy.47.entry_ref, bf16[64,2048]{1,0:T(8,128)(2,1)} %copy-done.2, bf16[512,1024]{1,0:T(8,128)(2,1)} %copy-done.1, ...), custom_call_target="tpu_custom_call" | custom-call | flops 100663296000 | bytes 39321600 | tf_op jit(solution)/shard_map/phase_2/pallas_call | solution.py:206
  299.4 7.9 %collective-permute-done.26.rest_0_ = bf16[7,8,9600]{2,1,0:T(8,128)(2,1)} collective-permute-done((bf16[7,8,9600]{2,1,0:T(8,128)(2,1)S(1)}, bf16[7,8,9600]{2,1,0:T(8,128)(2,1)}, u32[]{:S(2)}, u32[]{:S(2)}) %collective-permute-start.26) | collective-permute-done | bytes 1075232 | tf_op jit(solution)/shard_map/ppermute | solution.py:464
  307.3 1.3 collective-permute-done.27.rest_1_
  309.1 1.5 collective-permute-start.32
  310.6 19.6 %collective-permute-done.29.rest_2_ = bf16[7,8,9600]{2,1,0:T(8,128)(2,1)S(1)} collective-permute-done((bf16[7,8,9600]{2,1,0:T(8,128)(2,1)S(1)}, bf16[7,8,9600]{2,1,0:T(8,128)(2,1)S(1)}, u32[]{:S(2)}, u32[]{:S(2)}) %collective-permute-start.29) | collective-permute-done | bytes 1075232 | tf_op jit(solution)/shard_map/ppermute | solution.py:464
  330.2 1.4 collective-permute-done.30.rest_3_
  331.6 7.8 %phase_3.1.before_ref = f32[16,128]{1,0:T(8,128)} custom-call(s32[128]{0:T(128)} %fusion.14.rows_ref, s32[128]{0:T(128)} %get-tuple-element.116.vids_ref, s32[5]{0:T(128)} %convert_reduce_fusion.4.ends_ref, s32[128,1]{1,0:T(8,128)} %copy.48.entry_ref, bf16[64,2048]{1,0:T(8,128)(2,1)} %copy-done.2, bf16[512,1024]{1,0:T(8,128)(2,1)} %copy-done.1, ...), custom_call_target="tpu_custom_call" | custom-call | flops 100663296000 | bytes 39321600 | tf_op jit(solution)/shard_map/phase_3/pallas_call | solution.py:206
  339.4 10.5 %collective-permute-done.31.rest_0_ = bf16[7,8,9600]{2,1,0:T(8,128)(2,1)} collective-permute-done((bf16[7,8,9600]{2,1,0:T(8,128)(2,1)}, bf16[7,8,9600]{2,1,0:T(8,128)(2,1)}, u32[]{:S(2)}, u32[]{:S(2)}) %collective-permute-start.31) | collective-permute-done | bytes 1075232 | tf_op jit(solution)/shard_map/ppermute | solution.py:464
  349.9 0.9 collective-permute-done.32.rest_1_
  350.8 1.0 copy-done.13
  351.8 7.8 %phase_4.1 = f32[16,128]{1,0:T(8,128)} custom-call(s32[64]{0:T(128)} %get-tuple-element.134.rows_ref, s32[64]{0:T(128)} %get-tuple-element.135.vids_ref, s32[3]{0:T(128)} %convert_reduce_fusion.5.ends_ref, s32[64,1]{1,0:T(8,128)} %copy.49.entry_ref, bf16[64,2048]{1,0:T(8,128)(2,1)} %copy-done.2, bf16[512,1024]{1,0:T(8,128)(2,1)} %copy-done.1, ...), custom_call_target="tpu_custom_call" | custom-call | flops 50331648000 | bytes 19660800 | tf_op jit(solution)/shard_map/phase_4/pallas_call | solution.py:206
  360.5 12.6 %all_to_all.12 = f32[32,1,128]{2,1,0:T(1,128)S(1)} all-to-all(f32[32,1,128]{2,1,0:T(1,128)S(1)} %broadcast_select_fusion), channel_id=1, replica_groups=mesh['shard'=32] {'shard'}, dimensions={0} | all-to-all | bytes 32768 | tf_op jit(solution)/shard_map/all_to_all | solution.py:475
  (125 shorter events, 30.0 us)
Async XLA Ops:
  6.5 1.7 copy-start.4
  6.5 188.1 %all-gather.2.cloned.1.call-start = ((), (), s32[]{:S(2)}) async-start(), calls=%async_computation.2 | async-start | bytes 58982400 | tf_op jit(solution)/shard_map/all_gather | solution.py:375
  8.9 22.6 %collective-permute-start = (bf16[1,8,9600]{2,1,0:T(8,128)(2,1)S(1)}, bf16[1,8,9600]{2,1,0:T(8,128)(2,1)S(1)}, u32[]{:S(2)}, u32[]{:S(2)}) collective-permute-start(bf16[1,8,9600]{2,1,0:T(8,128)(2,1)S(1)} %get-tuple-element.45), channel_id=1, source_target_pairs={{0,2},{1,3},{2,0},{3,1},{4,6},{5,7},{6,4},{7,5},{8,10},{9,11},{10,... | collective-permute-start | bytes 460808 | tf_op jit(solution)/shard_map/ppermute | solution.py:464
  11.8 19.7 %collective-permute-start.1 = (bf16[1,8,9600]{2,1,0:T(8,128)(2,1)S(1)}, bf16[1,8,9600]{2,1,0:T(8,128)(2,1)S(1)}, u32[]{:S(2)}, u32[]{:S(2)}) collective-permute-start(bf16[1,8,9600]{2,1,0:T(8,128)(2,1)S(1)} %get-tuple-element.46), channel_id=1, source_target_pairs={{0,4},{1,5},{2,6},{3,7},{4,0},{5,1},{6,2},{7,3},{8,12},{9,13},{10,... | collective-permute-start | bytes 460808 | tf_op jit(solution)/shard_map/ppermute | solution.py:464
  14.9 5.0 %copy-start.7 = (bf16[32,1,3,3]{0,3,2,1:T(4,128)(2,1)S(1)}, bf16[32,1,3,3]{0,3,2,1:T(4,128)(2,1)}, u32[]{:S(2)}) copy-start(bf16[32,1,3,3]{0,3,2,1:T(4,128)(2,1)} %param.10) | copy-start | bytes 1732
  14.9 5.1 %copy-start.8 = (bf16[1,64,3,3]{1,3,2,0:T(4,128)(2,1)S(1)}, bf16[1,64,3,3]{1,3,2,0:T(4,128)(2,1)}, u32[]{:S(2)}) copy-start(bf16[1,64,3,3]{1,3,2,0:T(4,128)(2,1)} %param.12) | copy-start | bytes 3460
  14.9 5.7 %copy-start = (bf16[64,32,3,3]{0,1,3,2:T(8,128)(2,1)S(1)}, bf16[64,32,3,3]{0,1,3,2:T(8,128)(2,1)}, u32[]{:S(2)}) copy-start(bf16[64,32,3,3]{0,1,3,2:T(8,128)(2,1)} %param.11) | copy-start | bytes 110596
  16.3 87.0 %collective-permute-start.2 = (bf16[7,8,9600]{2,1,0:T(8,128)(2,1)}, bf16[7,8,9600]{2,1,0:T(8,128)(2,1)}, u32[]{:S(2)}, u32[]{:S(2)}) collective-permute-start(bf16[7,8,9600]{2,1,0:T(8,128)(2,1)} %get-tuple-element.57), channel_id=1, source_target_pairs={{0,2},{1,3},{2,0},{3,1},{4,6},{5,7},{6,4},{7,5},{8,10},{9,11},{10,... | collective-permute-start | bytes 3225608 | tf_op jit(solution)/shard_map/ppermute | solution.py:464
  16.9 86.5 %collective-permute-start.3 = (bf16[7,8,9600]{2,1,0:T(8,128)(2,1)}, bf16[7,8,9600]{2,1,0:T(8,128)(2,1)}, u32[]{:S(2)}, u32[]{:S(2)}) collective-permute-start(bf16[7,8,9600]{2,1,0:T(8,128)(2,1)} %get-tuple-element.56), channel_id=1, source_target_pairs={{0,4},{1,5},{2,6},{3,7},{4,0},{5,1},{6,2},{7,3},{8,12},{9,13},{10,... | collective-permute-start | bytes 3225608 | tf_op jit(solution)/shard_map/ppermute | solution.py:464
  16.9 97.9 %collective-permute-start.4 = (bf16[14,8,9600]{2,1,0:T(8,128)(2,1)}, bf16[14,8,9600]{2,1,0:T(8,128)(2,1)}, u32[]{:S(2)}, u32[]{:S(2)}) collective-permute-start(bf16[14,8,9600]{2,1,0:T(8,128)(2,1)} %slice.105.rest_0_), channel_id=1, source_target_pairs={{0,8},{1,9},{2,10},{3,11},{4,12},{5,13},{6,14},{7,15},{8,24},{9,25... | collective-permute-start | bytes 6451208 | tf_op jit(solution)/shard_map/ppermute | solution.py:464
  20.6 10.9 %copy-start.6 = (s32[16,8]{0,1:T(8,128)S(1)}, s32[16,8]{0,1:T(8,128)}, u32[]{:S(2)}) copy-start(s32[16,8]{0,1:T(8,128)} %param.9) | copy-start | bytes 1540
  29.1 1.0 copy-start.1
  30.1 0.7 copy-start.2
  30.8 0.7 copy-start.3
  31.5 42.1 %copy-start.10 = (pred[384]{0:T(512)(128)(4,1)S(1)}, pred[384]{0:T(512)(128)(4,1)}, u32[]{:S(2)}) copy-start(pred[384]{0:T(512)(128)(4,1)} %constant.173.clone.1) | copy-start | bytes 1156
  32.3 36.8 %all-to-all-start = ((s32[32,1,128]{2,1,0:T(1,128)}), s32[32,1,128]{2,1,0:T(1,128)S(1)}, u32[]{:S(2)}, u32[]{:S(2)}) async-start(s32[32,1,128]{2,1,0:T(1,128)} %broadcast_in_dim.96), calls=%async_computation | async-start | bytes 32768 | tf_op jit(solution)/shard_map/all_to_all | solution.py:468
  37.2 77.6 %collective-permute-start.5 = (bf16[7,8,9600]{2,1,0:T(8,128)(2,1)}, bf16[7,8,9600]{2,1,0:T(8,128)(2,1)}, u32[]{:S(2)}, u32[]{:S(2)}) collective-permute-start(bf16[7,8,9600]{2,1,0:T(8,128)(2,1)} %get-tuple-element.56), channel_id=1, source_target_pairs={{0,2},{1,3},{2,0},{3,1},{4,6},{5,7},{6,4},{7,5},{8,10},{9,11},{10,... | collective-permute-start | bytes 3225608 | tf_op jit(solution)/shard_map/ppermute | solution.py:464
  39.0 75.7 %collective-permute-start.6 = (bf16[7,8,9600]{2,1,0:T(8,128)(2,1)}, bf16[7,8,9600]{2,1,0:T(8,128)(2,1)}, u32[]{:S(2)}, u32[]{:S(2)}) collective-permute-start(bf16[7,8,9600]{2,1,0:T(8,128)(2,1)} %get-tuple-element.57), channel_id=1, source_target_pairs={{0,4},{1,5},{2,6},{3,7},{4,0},{5,1},{6,2},{7,3},{8,12},{9,13},{10,... | collective-permute-start | bytes 3225608 | tf_op jit(solution)/shard_map/ppermute | solution.py:464
  103.4 9.3 %collective-permute-start.9 = (bf16[2,8,9600]{2,1,0:T(8,128)(2,1)}, bf16[2,8,9600]{2,1,0:T(8,128)(2,1)S(1)}, u32[]{:S(2)}, u32[]{:S(2)}) collective-permute-start(bf16[2,8,9600]{2,1,0:T(8,128)(2,1)} %pad_maximum_fusion), channel_id=1, source_target_pairs={{0,4},{1,5},{2,6},{3,7},{4,0},{5,1},{6,2},{7,3},{8,12},{9,13},{10,... | collective-permute-start | bytes 921608 | tf_op jit(solution)/shard_map/ppermute | solution.py:464
  108.5 10.7 %collective-permute-start.10 = (bf16[2,8,9600]{2,1,0:T(8,128)(2,1)S(1)}, bf16[2,8,9600]{2,1,0:T(8,128)(2,1)S(1)}, u32[]{:S(2)}, u32[]{:S(2)}) collective-permute-start(bf16[2,8,9600]{2,1,0:T(8,128)(2,1)S(1)} %pad_maximum_fusion.1), channel_id=1, source_target_pairs={{0,2},{1,3},{2,0},{3,1},{4,6},{5,7},{6,4},{7,5},{8,10},{9,11},{10,... | collective-permute-start | bytes 921608 | tf_op jit(solution)/shard_map/ppermute | solution.py:464
  114.7 50.7 %collective-permute-start.7 = (bf16[7,8,9600]{2,1,0:T(8,128)(2,1)}, bf16[7,8,9600]{2,1,0:T(8,128)(2,1)S(1)}, u32[]{:S(2)}, u32[]{:S(2)}) collective-permute-start(bf16[7,8,9600]{2,1,0:T(8,128)(2,1)} %collective-permute-done.3.rest_2_), channel_id=1, source_target_pairs={{0,2},{1,3},{2,0},{3,1},{4,6},{5,7},{6,4},{7,5},{8,10},{9,11},{10,... | collective-permute-start | bytes 3225608 | tf_op jit(solution)/shard_map/ppermute | solution.py:464
  115.3 50.1 %collective-permute-start.8 = (bf16[7,8,9600]{2,1,0:T(8,128)(2,1)}, bf16[7,8,9600]{2,1,0:T(8,128)(2,1)S(1)}, u32[]{:S(2)}, u32[]{:S(2)}) collective-permute-start(bf16[7,8,9600]{2,1,0:T(8,128)(2,1)} %collective-permute-done.2.rest_1_), channel_id=1, source_target_pairs={{0,4},{1,5},{2,6},{3,7},{4,0},{5,1},{6,2},{7,3},{8,12},{9,13},{10,... | collective-permute-start | bytes 3225608 | tf_op jit(solution)/shard_map/ppermute | solution.py:464
  115.9 49.6 %collective-permute-start.11 = (bf16[14,8,9600]{2,1,0:T(8,128)(2,1)}, bf16[14,8,9600]{2,1,0:T(8,128)(2,1)S(1)}, u32[]{:S(2)}, u32[]{:S(2)}) collective-permute-start(bf16[14,8,9600]{2,1,0:T(8,128)(2,1)} %collective-permute-done.4.rest_3_), channel_id=1, source_target_pairs={{0,8},{1,9},{2,10},{3,11},{4,12},{5,13},{6,14},{7,15},{8,24},{9,25... | collective-permute-start | bytes 6451208 | tf_op jit(solution)/shard_map/ppermute | solution.py:464
  119.2 44.1 %collective-permute-start.12 = (bf16[7,8,9600]{2,1,0:T(8,128)(2,1)S(1)}, bf16[7,8,9600]{2,1,0:T(8,128)(2,1)S(1)}, u32[]{:S(2)}, u32[]{:S(2)}) collective-permute-start(bf16[7,8,9600]{2,1,0:T(8,128)(2,1)S(1)} %get-tuple-element.66), channel_id=1, source_target_pairs={{0,2},{1,3},{2,0},{3,1},{4,6},{5,7},{6,4},{7,5},{8,10},{9,11},{10,... | collective-permute-start | bytes 3225608 | tf_op jit(solution)/shard_map/ppermute | solution.py:464
  120.6 42.7 %collective-permute-start.13 = (bf16[7,8,9600]{2,1,0:T(8,128)(2,1)}, bf16[7,8,9600]{2,1,0:T(8,128)(2,1)S(1)}, u32[]{:S(2)}, u32[]{:S(2)}) collective-permute-start(bf16[7,8,9600]{2,1,0:T(8,128)(2,1)} %get-tuple-element.65), channel_id=1, source_target_pairs={{0,4},{1,5},{2,6},{3,7},{4,0},{5,1},{6,2},{7,3},{8,12},{9,13},{10,... | collective-permute-start | bytes 3225608 | tf_op jit(solution)/shard_map/ppermute | solution.py:464
  163.3 6.3 %copy-start.14 = (bf16[7,8,9600]{2,1,0:T(8,128)(2,1)}, bf16[7,8,9600]{2,1,0:T(8,128)(2,1)S(1)}, u32[]{:S(2)}) copy-start(bf16[7,8,9600]{2,1,0:T(8,128)(2,1)S(1)} %collective-permute-done.12.rest_1_) | copy-start | bytes 3225604
  163.3 6.3 %copy-start.15 = (bf16[7,8,9600]{2,1,0:T(8,128)(2,1)}, bf16[7,8,9600]{2,1,0:T(8,128)(2,1)S(1)}, u32[]{:S(2)}) copy-start(bf16[7,8,9600]{2,1,0:T(8,128)(2,1)S(1)} %collective-permute-done.13.rest_2_) | copy-start | bytes 3225604
  163.3 26.7 %collective-permute-start.17 = (bf16[7,8,9600]{2,1,0:T(8,128)(2,1)S(1)}, bf16[7,8,9600]{2,1,0:T(8,128)(2,1)S(1)}, u32[]{:S(2)}, u32[]{:S(2)}) collective-permute-start(bf16[7,8,9600]{2,1,0:T(8,128)(2,1)S(1)} %collective-permute-done.13.rest_2_), channel_id=1, source_target_pairs={{0,2},{1,3},{2,0},{3,1},{4,6},{5,7},{6,4},{7,5},{8,10},{9,11},{10,... | collective-permute-start | bytes 3225608 | tf_op jit(solution)/shard_map/ppermute | solution.py:464
  164.4 26.7 %collective-permute-start.18 = (bf16[7,8,9600]{2,1,0:T(8,128)(2,1)S(1)}, bf16[7,8,9600]{2,1,0:T(8,128)(2,1)S(1)}, u32[]{:S(2)}, u32[]{:S(2)}) collective-permute-start(bf16[7,8,9600]{2,1,0:T(8,128)(2,1)S(1)} %collective-permute-done.12.rest_1_), channel_id=1, source_target_pairs={{0,4},{1,5},{2,6},{3,7},{4,0},{5,1},{6,2},{7,3},{8,12},{9,13},{10,... | collective-permute-start | bytes 3225608 | tf_op jit(solution)/shard_map/ppermute | solution.py:464
  165.4 26.7 %copy-start.18 = (bf16[7,8,9600]{2,1,0:T(8,128)(2,1)}, bf16[7,8,9600]{2,1,0:T(8,128)(2,1)S(1)}, u32[]{:S(2)}) copy-start(bf16[7,8,9600]{2,1,0:T(8,128)(2,1)S(1)} %collective-permute-done.7.rest_6_) | copy-start | bytes 3225604
  165.5 27.7 %copy-start.19 = (bf16[7,8,9600]{2,1,0:T(8,128)(2,1)}, bf16[7,8,9600]{2,1,0:T(8,128)(2,1)S(1)}, u32[]{:S(2)}) copy-start(bf16[7,8,9600]{2,1,0:T(8,128)(2,1)S(1)} %collective-permute-done.8.rest_7_) | copy-start | bytes 3225604
  165.5 4.1 %copy-start.5 = (bf16[14,8,9600]{2,1,0:T(8,128)(2,1)}, bf16[14,8,9600]{2,1,0:T(8,128)(2,1)S(1)}, u32[]{:S(2)}) copy-start(bf16[14,8,9600]{2,1,0:T(8,128)(2,1)S(1)} %collective-permute-done.11.rest_0_) | copy-start | bytes 6451204
  165.5 47.7 %collective-permute-start.14 = (bf16[7,8,9600]{2,1,0:T(8,128)(2,1)}, bf16[7,8,9600]{2,1,0:T(8,128)(2,1)}, u32[]{:S(2)}, u32[]{:S(2)}) collective-permute-start(bf16[7,8,9600]{2,1,0:T(8,128)(2,1)} %get-tuple-element.65), channel_id=1, source_target_pairs={{0,2},{1,3},{2,0},{3,1},{4,6},{5,7},{6,4},{7,5},{8,10},{9,11},{10,... | collective-permute-start | bytes 3225608 | tf_op jit(solution)/shard_map/ppermute | solution.py:464
  167.0 47.2 %collective-permute-start.15 = (bf16[7,8,9600]{2,1,0:T(8,128)(2,1)S(1)}, bf16[7,8,9600]{2,1,0:T(8,128)(2,1)}, u32[]{:S(2)}, u32[]{:S(2)}) collective-permute-start(bf16[7,8,9600]{2,1,0:T(8,128)(2,1)S(1)} %get-tuple-element.66), channel_id=1, source_target_pairs={{0,4},{1,5},{2,6},{3,7},{4,0},{5,1},{6,2},{7,3},{8,12},{9,13},{10,... | collective-permute-start | bytes 3225608 | tf_op jit(solution)/shard_map/ppermute | solution.py:464
  167.5 47.3 %collective-permute-start.16 = (bf16[14,8,9600]{2,1,0:T(8,128)(2,1)S(1)}, bf16[14,8,9600]{2,1,0:T(8,128)(2,1)}, u32[]{:S(2)}, u32[]{:S(2)}) collective-permute-start(bf16[14,8,9600]{2,1,0:T(8,128)(2,1)S(1)} %collective-permute-done.11.rest_0_), channel_id=1, source_target_pairs={{0,8},{1,9},{2,10},{3,11},{4,12},{5,13},{6,14},{7,15},{8,24},{9,25... | collective-permute-start | bytes 6451208 | tf_op jit(solution)/shard_map/ppermute | solution.py:464
  190.1 1.1 copy-start.16
  191.1 1.0 copy-start.17
  192.1 82.6 %collective-permute-start.21 = (bf16[7,8,9600]{2,1,0:T(8,128)(2,1)}, bf16[7,8,9600]{2,1,0:T(8,128)(2,1)}, u32[]{:S(2)}, u32[]{:S(2)}) collective-permute-start(bf16[7,8,9600]{2,1,0:T(8,128)(2,1)} %get-tuple-element.72), channel_id=1, source_target_pairs={{0,2},{1,3},{2,0},{3,1},{4,6},{5,7},{6,4},{7,5},{8,10},{9,11},{10,... | collective-permute-start | bytes 3225608 | tf_op jit(solution)/shard_map/ppermute | solution.py:464
  193.1 81.6 %collective-permute-start.22 = (bf16[7,8,9600]{2,1,0:T(8,128)(2,1)}, bf16[7,8,9600]{2,1,0:T(8,128)(2,1)}, u32[]{:S(2)}, u32[]{:S(2)}) collective-permute-start(bf16[7,8,9600]{2,1,0:T(8,128)(2,1)} %get-tuple-element.73), channel_id=1, source_target_pairs={{0,4},{1,5},{2,6},{3,7},{4,0},{5,1},{6,2},{7,3},{8,12},{9,13},{10,... | collective-permute-start | bytes 3225608 | tf_op jit(solution)/shard_map/ppermute | solution.py:464
  214.8 42.0 %collective-permute-start.19 = (bf16[7,8,9600]{2,1,0:T(8,128)(2,1)}, bf16[7,8,9600]{2,1,0:T(8,128)(2,1)S(1)}, u32[]{:S(2)}, u32[]{:S(2)}) collective-permute-start(bf16[7,8,9600]{2,1,0:T(8,128)(2,1)} %get-tuple-element.73), channel_id=1, source_target_pairs={{0,2},{1,3},{2,0},{3,1},{4,6},{5,7},{6,4},{7,5},{8,10},{9,11},{10,... | collective-permute-start | bytes 3225608 | tf_op jit(solution)/shard_map/ppermute | solution.py:464
  215.4 41.9 %collective-permute-start.20 = (bf16[7,8,9600]{2,1,0:T(8,128)(2,1)}, bf16[7,8,9600]{2,1,0:T(8,128)(2,1)}, u32[]{:S(2)}, u32[]{:S(2)}) collective-permute-start(bf16[7,8,9600]{2,1,0:T(8,128)(2,1)} %get-tuple-element.72), channel_id=1, source_target_pairs={{0,4},{1,5},{2,6},{3,7},{4,0},{5,1},{6,2},{7,3},{8,12},{9,13},{10,... | collective-permute-start | bytes 3225608 | tf_op jit(solution)/shard_map/ppermute | solution.py:464
  216.8 40.4 %collective-permute-start.23 = (bf16[8,8,9600]{2,1,0:T(8,128)(2,1)}, bf16[8,8,9600]{2,1,0:T(8,128)(2,1)S(1)}, u32[]{:S(2)}, u32[]{:S(2)}) collective-permute-start(bf16[8,8,9600]{2,1,0:T(8,128)(2,1)} %constant_dynamic-update-slice_fusion.rest_8_), channel_id=1, source_target_pairs={{0,8},{1,9},{2,10},{3,11},{4,12},{5,13},{6,14},{7,15},{8,24},{9,25... | collective-permute-start | bytes 3686408 | tf_op jit(solution)/shard_map/ppermute | solution.py:464
  256.8 17.9 %copy-start.20 = (bf16[7,8,9600]{2,1,0:T(8,128)(2,1)}, bf16[7,8,9600]{2,1,0:T(8,128)(2,1)S(1)}, u32[]{:S(2)}) copy-start(bf16[7,8,9600]{2,1,0:T(8,128)(2,1)S(1)} %collective-permute-done.19.rest_0_) | copy-start | bytes 3225604
  257.2 17.5 %copy-start.12 = (bf16[8,8,9600]{2,1,0:T(8,128)(2,1)}, bf16[8,8,9600]{2,1,0:T(8,128)(2,1)S(1)}, u32[]{:S(2)}) copy-start(bf16[8,8,9600]{2,1,0:T(8,128)(2,1)S(1)} %collective-permute-done.23.rest_6_) | copy-start | bytes 3686404
  257.2 27.0 %collective-permute-start.24 = (bf16[7,8,9600]{2,1,0:T(8,128)(2,1)}, bf16[7,8,9600]{2,1,0:T(8,128)(2,1)}, u32[]{:S(2)}, u32[]{:S(2)}) collective-permute-start(bf16[7,8,9600]{2,1,0:T(8,128)(2,1)} %collective-permute-done.20.rest_1_), channel_id=1, source_target_pairs={{0,2},{1,3},{2,0},{3,1},{4,6},{5,7},{6,4},{7,5},{8,10},{9,11},{10,... | collective-permute-start | bytes 3225608 | tf_op jit(solution)/shard_map/ppermute | solution.py:464
  258.7 26.8 %collective-permute-start.25 = (bf16[7,8,9600]{2,1,0:T(8,128)(2,1)S(1)}, bf16[7,8,9600]{2,1,0:T(8,128)(2,1)}, u32[]{:S(2)}, u32[]{:S(2)}) collective-permute-start(bf16[7,8,9600]{2,1,0:T(8,128)(2,1)S(1)} %collective-permute-done.19.rest_0_), channel_id=1, source_target_pairs={{0,4},{1,5},{2,6},{3,7},{4,0},{5,1},{6,2},{7,3},{8,12},{9,13},{10,... | collective-permute-start | bytes 3225608 | tf_op jit(solution)/shard_map/ppermute | solution.py:464
  260.2 26.7 %collective-permute-start.28 = (bf16[8,8,9600]{2,1,0:T(8,128)(2,1)S(1)}, bf16[8,8,9600]{2,1,0:T(8,128)(2,1)S(1)}, u32[]{:S(2)}, u32[]{:S(2)}) collective-permute-start(bf16[8,8,9600]{2,1,0:T(8,128)(2,1)S(1)} %collective-permute-done.23.rest_6_), channel_id=1, source_target_pairs={{0,8},{1,9},{2,10},{3,11},{4,12},{5,13},{6,14},{7,15},{8,24},{9,25... | collective-permute-start | bytes 3686408 | tf_op jit(solution)/shard_map/ppermute | solution.py:464
  274.7 32.5 %collective-permute-start.26 = (bf16[7,8,9600]{2,1,0:T(8,128)(2,1)S(1)}, bf16[7,8,9600]{2,1,0:T(8,128)(2,1)}, u32[]{:S(2)}, u32[]{:S(2)}) collective-permute-start(bf16[7,8,9600]{2,1,0:T(8,128)(2,1)S(1)} %get-tuple-element.81), channel_id=1, source_target_pairs={{0,2},{1,3},{2,0},{3,1},{4,6},{5,7},{6,4},{7,5},{8,10},{9,11},{10,... | collective-permute-start | bytes 3225608 | tf_op jit(solution)/shard_map/ppermute | solution.py:464
  275.4 33.1 %collective-permute-start.27 = (bf16[7,8,9600]{2,1,0:T(8,128)(2,1)S(1)}, bf16[7,8,9600]{2,1,0:T(8,128)(2,1)}, u32[]{:S(2)}, u32[]{:S(2)}) collective-permute-start(bf16[7,8,9600]{2,1,0:T(8,128)(2,1)S(1)} %get-tuple-element.80), channel_id=1, source_target_pairs={{0,4},{1,5},{2,6},{3,7},{4,0},{5,1},{6,2},{7,3},{8,12},{9,13},{10,... | collective-permute-start | bytes 3225608 | tf_op jit(solution)/shard_map/ppermute | solution.py:464
  287.0 23.6 %copy-start.11 = (bf16[8,8,9600]{2,1,0:T(8,128)(2,1)}, bf16[8,8,9600]{2,1,0:T(8,128)(2,1)S(1)}, u32[]{:S(2)}) copy-start(bf16[8,8,9600]{2,1,0:T(8,128)(2,1)S(1)} %collective-permute-done.28.rest_4_) | copy-start | bytes 3686404
  287.0 43.2 %collective-permute-start.29 = (bf16[7,8,9600]{2,1,0:T(8,128)(2,1)S(1)}, bf16[7,8,9600]{2,1,0:T(8,128)(2,1)S(1)}, u32[]{:S(2)}, u32[]{:S(2)}) collective-permute-start(bf16[7,8,9600]{2,1,0:T(8,128)(2,1)S(1)} %get-tuple-element.80), channel_id=1, source_target_pairs={{0,2},{1,3},{2,0},{3,1},{4,6},{5,7},{6,4},{7,5},{8,10},{9,11},{10,... | collective-permute-start | bytes 3225608 | tf_op jit(solution)/shard_map/ppermute | solution.py:464
  287.6 44.0 %collective-permute-start.30 = (bf16[7,8,9600]{2,1,0:T(8,128)(2,1)S(1)}, bf16[7,8,9600]{2,1,0:T(8,128)(2,1)}, u32[]{:S(2)}, u32[]{:S(2)}) collective-permute-start(bf16[7,8,9600]{2,1,0:T(8,128)(2,1)S(1)} %get-tuple-element.81), channel_id=1, source_target_pairs={{0,4},{1,5},{2,6},{3,7},{4,0},{5,1},{6,2},{7,3},{8,12},{9,13},{10,... | collective-permute-start | bytes 3225608 | tf_op jit(solution)/shard_map/ppermute | solution.py:464
  308.5 41.4 %collective-permute-start.31 = (bf16[7,8,9600]{2,1,0:T(8,128)(2,1)}, bf16[7,8,9600]{2,1,0:T(8,128)(2,1)}, u32[]{:S(2)}, u32[]{:S(2)}) collective-permute-start(bf16[7,8,9600]{2,1,0:T(8,128)(2,1)} %collective-permute-done.27.rest_1_), channel_id=1, source_target_pairs={{0,2},{1,3},{2,0},{3,1},{4,6},{5,7},{6,4},{7,5},{8,10},{9,11},{10,... | collective-permute-start | bytes 3225608 | tf_op jit(solution)/shard_map/ppermute | solution.py:464
  309.1 41.7 %collective-permute-start.32 = (bf16[7,8,9600]{2,1,0:T(8,128)(2,1)}, bf16[7,8,9600]{2,1,0:T(8,128)(2,1)}, u32[]{:S(2)}, u32[]{:S(2)}) collective-permute-start(bf16[7,8,9600]{2,1,0:T(8,128)(2,1)} %collective-permute-done.26.rest_0_), channel_id=1, source_target_pairs={{0,4},{1,5},{2,6},{3,7},{4,0},{5,1},{6,2},{7,3},{8,12},{9,13},{10,... | collective-permute-start | bytes 3225608 | tf_op jit(solution)/shard_map/ppermute | solution.py:464
  310.6 40.2 %collective-permute-start.33 = (bf16[8,8,9600]{2,1,0:T(8,128)(2,1)S(1)}, bf16[8,8,9600]{2,1,0:T(8,128)(2,1)S(1)}, u32[]{:S(2)}, u32[]{:S(2)}) collective-permute-start(bf16[8,8,9600]{2,1,0:T(8,128)(2,1)S(1)} %collective-permute-done.28.rest_4_), channel_id=1, source_target_pairs={{0,8},{1,9},{2,10},{3,11},{4,12},{5,13},{6,14},{7,15},{8,24},{9,25... | collective-permute-start | bytes 3686408 | tf_op jit(solution)/shard_map/ppermute | solution.py:464
  330.2 1.4 copy-start.21
  350.8 1.0 copy-start.13
  351.8 8.5 %copy-start.9 = (pred[32]{0:T(512)(128)(4,1)S(1)}, pred[32]{0:T(512)(128)(4,1)}, u32[]{:S(2)}) copy-start(pred[32]{0:T(512)(128)(4,1)} %broadcast_in_dim.93) | copy-start | bytes 100
Sparse Core Ops, SparseCore 0:
  8.9 62.2 all-gather.1

commit v6 on v5

--- a/solution.py
+++ b/solution.py
@@ -11,7 +11,6 @@
 
 R = 5
 GROUP = 16
-NONE = 1 << 30
 SHARES = (7, 7, 1, 1)
 HEAD = 64
 WEIGHT = 8
@@ -96,13 +95,36 @@
     )(one_w, two_w, three_w)
 
 
-def pair_kernel(frames, buffers, scale, rows_ref, vids_ref, ends_ref, entry_ref, one_ref,
+def pair_kernel(frames, idx_dev, k_count, bounds, scale, who_ref, ids_ref, queries_ref, one_ref,
                 two_ref, three_ref, before_ref, v_hbm, *rest):
+    buffers = len(bounds) - 1
     q_hbm, rest = rest[:buffers], rest[buffers:]
-    out_ref, q_in, v_in, q_rows, v_rows, maps, q_sem, v_sem = rest
+    (out_ref, q_in, v_in, q_rows, v_rows, maps, scores, rows_ref, vids_ref, entry_ref, ends_ref,
+     q_sem, v_sem) = rest
     width = v_hbm.shape[2] // R
     side = GROUP * frames
-    count = ends_ref[buffers - 1]
+    senders, pairs = out_ref.shape
+    chip, core = who_ref[0], who_ref[1]
+
+    count = jnp.int32(0)
+    for b in range(buffers):
+        def one_of(t, n):
+            packed = queries_ref[t]
+            row, query = packed & 255, (packed >> 8) & 255
+            sender = who_ref[2 + (packed >> 16)]
+            for k in range(k_count):
+                pair = query * k_count + k
+                vid = ids_ref[2 * sender + core, pair]
+                rows_ref[n] = row
+                vids_ref[n] = lax.rem(vid, 2 * idx_dev)
+                entry_ref[n] = sender * pairs + pair
+                n = n + (lax.div(vid, 2 * idx_dev) == chip).astype(jnp.int32)
+            return n
+        count = lax.fori_loop(bounds[b], bounds[b + 1], one_of, count)
+        ends_ref[b] = count
+    for p in range(GROUP):
+        rows_ref[count + p] = 0
+        vids_ref[count + p] = 0
     groups = (count + GROUP - 1) // GROUP
 
     def fetch(step, slot):
@@ -174,39 +196,41 @@
             best = jnp.maximum(best, x[:, i * n:(i + 1) * n])
         return jnp.maximum(best, 0.0).astype(jnp.bfloat16)
 
-    out_ref[...] = before_ref[...]
-    senders, pairs = out_ref.shape
-
     def head(g, _):
         here = pl.ds(pl.multiple_of(g * HEAD, HEAD), HEAD)
         first = pooled(dot(maps[here, :].astype(jnp.bfloat16), one_ref[...]))
         second = pooled(dot(first, two_ref[...]))
         final = jnp.clip(dot(second, three_ref[...]), -1.0, 1.0)
         best = jnp.maximum(final[:, :128], final[:, 128:])
-        shape = (HEAD, pairs)
-        score = jnp.broadcast_to((best[:, 0:1] + best[:, 1:2]) * 0.5, shape)
-        place = jnp.broadcast_to(entry_ref[here, :], shape) - iota(shape, 1)
-        for s in range(senders):
-            out_ref[pl.ds(s, 1), :] = out_ref[pl.ds(s, 1), :] + jnp.sum(
-                jnp.where(place == s * pairs, score, 0.0), axis=0, keepdims=True
-            )
+        scores[here, :] = jnp.broadcast_to((best[:, 0:1] + best[:, 1:2]) * 0.5, (HEAD, pairs))
         return 0
 
     lax.fori_loop(0, (count + HEAD - 1) // HEAD, head, 0)
 
-
-def pair_scores(blocks, videos, rows, vids, ends, entry, heads, before, name):
+    out_ref[...] = before_ref[...]
+
+    def write(i, _):
+        entry = entry_ref[i]
+        at = pl.ds(lax.div(entry, pairs), 1)
+        hit = iota((1, pairs), 1) == lax.rem(entry, pairs)
+        out_ref[at, :] = jnp.where(hit, scores[pl.ds(i, 1), :], out_ref[at, :])
+        return 0
+
+    lax.fori_loop(0, count, write, 0)
+
+
+def pair_scores(blocks, videos, who, ids, queries, bounds, cap, heads, before, k_count, idx_dev, name):
     frames, width = videos.shape[1], videos.shape[2]
-    cap = rows.shape[0]
+    pairs = before.shape[1]
     side = GROUP * frames
     scale = 1.0 / (math.sqrt(width // R) * R)
     smem = pl.BlockSpec(memory_space=pltpu.SMEM)
     vmem = pl.BlockSpec(memory_space=pltpu.VMEM)
     hbm = pl.BlockSpec(memory_space=pltpu.HBM)
     return pl.pallas_call(
-        functools.partial(pair_kernel, frames, len(blocks), scale),
+        functools.partial(pair_kernel, frames, idx_dev, k_count, bounds, scale),
         out_shape=jax.ShapeDtypeStruct(before.shape, jnp.float32),
-        in_specs=[smem] * 3 + [vmem] * 5 + [hbm] * (1 + len(blocks)),
+        in_specs=[smem] * 3 + [vmem] * 4 + [hbm] * (1 + len(blocks)),
         out_specs=vmem,
         scratch_shapes=[
             pltpu.VMEM((2, GROUP, frames, width), jnp.bfloat16),
@@ -214,6 +238,11 @@
             pltpu.VMEM((R * side, width // R), jnp.bfloat16),
             pltpu.VMEM((R * side, width // R), jnp.bfloat16),
             pltpu.VMEM((cap, frames * frames), jnp.float32),
+            pltpu.VMEM((cap, pairs), jnp.float32),
+            pltpu.SMEM((cap + GROUP,), jnp.int32),
+            pltpu.SMEM((cap + GROUP,), jnp.int32),
+            pltpu.SMEM((cap + GROUP,), jnp.int32),
+            pltpu.SMEM((len(blocks),), jnp.int32),
             pltpu.SemaphoreType.DMA((2,)),
             pltpu.SemaphoreType.DMA((2,)),
         ],
@@ -223,7 +252,7 @@
             bytes_accessed=cap * frames * width * 4, transcendentals=0,
         ),
         name=name,
-    )(rows, vids, ends, entry, *heads, before, videos, *blocks)
+    )(who, ids, queries, *heads, before, videos, *blocks)
 
 
 def chip_places(mesh):
@@ -383,69 +412,39 @@
     ends = [gather.offset + gather.per_plane * (z + 1) - 1 for z in range(sizes[0] - 1)]
     ends = sorted({e for e in ends if 0 <= e < total - 2} | {total - 2, total - 1})
     phases = [[] for _ in ends]
-    place = {}
     for key in gather.buffers():
-        p = next(i for i, e in enumerate(ends) if gather.arrival[key] <= e)
-        row = 0
-        for off, first, n in gather.cells[key]:
-            for q in range(first, first + n):
-                place[off, q] = (p, len(phases[p]), row)
-                row += 1
-        phases[p].append(key)
-    stride = 1 << max(row for _, _, row in place.values()).bit_length()
-    most = max(len(p) for p in phases)
-    caps = [0] * len(phases)
-    for off in sorted({off for off, _ in place}):
-        for p in range(len(phases)):
-            here = sum(place[off, q][0] == p for q in range(q_dev))
-            caps[p] += min(here * k_count, 2 * per_holder)
-    caps = [-(-c // HEAD) * HEAD for c in caps]
-    spot = np.zeros((chips, chips, q_dev), np.int32)
-    for c in range(chips):
-        for s in range(chips):
-            off = tuple((a - b) % n for a, b, n in zip(rings[c], rings[s], sizes))
-            for q in range(q_dev):
-                p, b, row = place[off, q]
-                spot[c, s, q] = (p * most + b) * stride + row
+        phases[next(i for i, e in enumerate(ends) if gather.arrival[key] <= e)].append(key)
+    offsets = [(z, y, x) for z in range(sizes[0]) for y in range(sizes[1]) for x in range(sizes[2])]
+    back = np.array(
+        [[where[tuple((r - o) % n for r, o, n in zip(ring, off, sizes))] for off in offsets]
+         for ring in rings], np.int32,
+    )
+    who = jnp.concatenate(
+        [jnp.stack([chip, core]), lax.dynamic_index_in_dim(jnp.asarray(back), chip, 0, keepdims=False)]
+    )
+
+    def contents(p):
+        packed, bounds, found = [], [0], {}
+        for key in phases[p]:
+            row = 0
+            for off, first, n in gather.cells[key]:
+                found[off] = found.get(off, 0) + n
+                for q in range(first, first + n):
+                    packed.append((offsets.index(off) << 16) + (q << 8) + row)
+                    row += 1
+            bounds.append(len(packed))
+        cap = sum(min(n * k_count, 2 * per_holder) for n in found.values())
+        return jnp.asarray(np.array(packed, np.int32)), bounds, -(-cap // HEAD) * HEAD
 
     state = {}
-
-    def lists(all_ids):
-        spots = lax.dynamic_index_in_dim(jnp.asarray(spot), chip, 0, keepdims=False)
-        spots = jnp.broadcast_to(spots[:, :, None], (chips, q_dev, k_count)).reshape(chips * pairs)
-        ids = all_ids.reshape(chips, 2, pairs)
-        ids = jnp.where(core == 0, ids[:, 0], ids[:, 1]).reshape(chips * pairs)
-        mine = ids // (2 * idx_dev) == chip
-        code = jnp.where(mine, spots * (2 * idx_dev) + ids % (2 * idx_dev), NONE)
-        code, entry = lax.sort((code, jnp.arange(chips * pairs, dtype=jnp.int32)), num_keys=1)
-        keep = chips * 2 * per_holder
-        code = jnp.concatenate([code[:keep], jnp.full((max(caps),), NONE, jnp.int32)])
-        entry = jnp.concatenate([entry[:keep], jnp.zeros((max(caps),), jnp.int32)])
-        spots = code // (2 * idx_dev)
-        phase = jnp.where(code < NONE, spots // (most * stride), len(phases))
-        counts = jnp.sum(
-            (phase[:, None] == jnp.arange(len(phases))[None, :]).astype(jnp.int32), axis=0
-        )
-        return spots % (most * stride), code % (2 * idx_dev), entry, counts, jnp.cumsum(counts) - counts
-
     heads = head_matrices(conv_one, conv_two, conv_three)
     tables = [jnp.zeros((chips, pairs), jnp.float32)]
 
     def score():
         p = len(tables) - 1
-        spots, vids, entry, counts, firsts = state["lists"]
-        cut = lambda a: lax.dynamic_slice(a, (firsts[p],), (caps[p],))
-        valid = jnp.arange(caps[p]) < counts[p]
-        at, vid = cut(spots), jnp.where(valid, cut(vids), 0)
-        rows = jnp.where(valid, at % stride, 0)
-        entries = jnp.where(valid, cut(entry), NONE)
-        upto = jnp.sum(
-            (valid[None, :] & (at[None, :] // stride <= jnp.arange(len(phases[p]))[:, None]))
-            .astype(jnp.int32), axis=1,
-        )
         tables.append(pair_scores(
-            [gather.block(k) for k in phases[p]], videos, rows, vid, upto,
-            entries.reshape(caps[p], 1), heads, tables[-1], "phase_" + str(p),
+            [gather.block(k) for k in phases[p]], videos, who, state["ids"], *contents(p), heads,
+            tables[-1], k_count, idx_dev, "phase_" + str(p),
         ))
 
     done, deep = [], []
@@ -465,10 +464,10 @@
             (done[i] if axis else deep).append(gather.blocks[target])
         if i == 0:
             ids = lax.optimization_barrier((candidates, *done[0]))[0].reshape(1, pairs)
-            state["lists"] = lists(lax.all_to_all(
+            state["ids"] = lax.all_to_all(
                 jnp.broadcast_to(ids, (devices, pairs)), "shard", split_axis=0, concat_axis=0,
                 tiled=True,
-            ))
+            )
     while len(tables) <= len(ends):
         score()
     table = jnp.where(jnp.arange(2)[None, :, None] == core, tables[-1][:, None], 0.0)

time: 382 us -> 342 us (0.90)
  waiting for transfers between devices: 189 us -> 162 us
  other arithmetic: 26 us -> 0.82 us
  Pallas kernels: 63.4 us -> 79.8 us
  starting transfers between devices: 39.1 us -> 51.9 us
  between operations: 23.2 us -> 13.7 us
  local copies, waits for them, and re-layouts: 27.2 us -> 21.7 us
    all_to_all x1, waiting for transfers between devices: 27.1 us -> 0.01 us  [body(): lax.all_to_all(jnp.broadcast_to(ids, (devices, pairs)), 'shard', split_ax...]
    pallas_call x5, Pallas kernels: 54.8 us -> 71.3 us  [pair_scores(): pl.pallas_call(functools.partial(pair_kernel, frames, idx_dev, k_count, b...]
    ppermute x34, starting transfers between devices: 34.2 us -> 47.1 us  [body(): gather.blocks[target] = lax.ppermute(block, 'shard', gather.steps[axis])]
    select_n x11 -> x0, other arithmetic: 9.62 us -> none  [the longest x5 6.15 us: score(): rows = jnp.where(valid, at % stride, 0)]
    sort x1 -> x0, other arithmetic: 4.44 us -> none  [lists(): lax.sort((code, jnp.arange(chips * pairs, dtype=jnp.int32)), num_keys=1)]
    unnamed x49 -> x53, local copies, waits for them, and re-layouts: 8.91 us -> 7.9 us
  transfers between devices with their start and end apart: 36 -> 36, of which waited for: 19 -> 17; matrix products, arithmetic and copies ran while one was open for 12% -> 5% of each run, Pallas kernels for 15% -> 21%
where the time goes in v6:
time: 342 us; the launch traced here: 341 us
  waiting for transfers between devices  162 us (47%)
  Pallas kernels  79.8 us (23%)
  starting transfers between devices  51.9 us (15%)
  local copies, waits for them, and re-layouts  21.7 us (6%)
  between operations  13.7 us (4%)
  blocking collectives  11.7 us (3%)
    ppermute x34, waiting for transfers between devices, body(): gather.blocks[target] = lax.ppermute(block, 'shard', gather.steps[axis])  161 us
    pallas_call x5, Pallas kernels, pair_scores(): pl.pallas_call(functools.partial(pair_kernel, frames, idx_dev, k_count, b...  71.3 us
    ppermute x34, starting transfers between devices, body(): gather.blocks[target] = lax.ppermute(block, 'shard', gather.steps[axis])  47.1 us
    all_to_all x1, blocking collectives, body(): lax.all_to_all(table.reshape(devices, pairs), 'shard', split_axis=0, conc...  11.7 us
    pallas_call x1, Pallas kernels, head_matrices(): pl.pallas_call(head_kernel, out_shape=[jax.ShapeDtypeStruct(s, jnp.bfloat...  8.54 us
    unnamed x53, local copies, waits for them, and re-layouts  7.9 us
    slice x4, local copies, waits for them, and re-layouts, block(): self.blocks[key] = self.block(whole)[start:start + n]  7.35 us
  transfers between devices with their start and end apart: 36, of which 17 were waited for; matrix products, arithmetic and copies ran while one was open for 5% of the time, Pallas kernels for 21%

profile of v6, /device:TPU:0, one launch (start us, length us, event | category | flops | bytes accessed | tf_op | source)
XLA Modules:
  0.0 341.4 jit_solution(12316005393740908889)
XLA Ops:
  6.5 0.7 all-gather.2.cloned.1.call-update
  7.3 1.0 copy-done.4
  8.2 0.7 constant_dynamic-update-slice_fusion.5
  8.9 2.9 collective-permute-start
  11.9 1.5 collective-permute-start.1
  13.4 1.5 slice.37.rest_0_
  14.9 1.5 fusion
  17.0 2.1 collective-permute-start.4
  19.1 0.7 dynamic-slice_bitcast_fusion
  19.8 8.5 %head_matrices.1 = (bf16[64,2048]{1,0:T(8,128)(2,1)S(1)}, bf16[512,1024]{1,0:T(8,128)(2,1)S(1)}, bf16[256,256]{1,0:T(8,128)(2,1)S(1)}) custom-call(bf16[9,1,32]{2,1,0:T(2,128)(2,1)S(1)} %reshape.74.one_w, bf16[9,32,64]{2,1,0:T(8,128)(2,1)S(1)} %bitcast.16, bf16[9,1,64]{2,1,0:T(2,128)(2,1)S(1)} %reshape.75.three_w), custom_call_target="tpu_custom_call" | custom-call | flops 1000000000 | bytes 3000000 | tf_op jit(solution)/shard_map/head_matrices/pallas_call | solution.py:86
  28.4 1.0 copy-done.1
  29.4 0.7 copy-done.2
  32.8 4.8 %all-to-all-start = ((s32[32,1,128]{2,1,0:T(1,128)}), s32[32,1,128]{2,1,0:T(1,128)S(1)}, u32[]{:S(2)}, u32[]{:S(2)}) async-start(s32[32,1,128]{2,1,0:T(1,128)} %broadcast_in_dim.42), calls=%async_computation | async-start | bytes 32768 | tf_op jit(solution)/shard_map/all_to_all | solution.py:467
  37.6 1.8 collective-permute-start.5
  39.5 1.5 collective-permute-start.6
  41.0 1.5 collective-permute-done.2.rest_1_
  42.5 0.7 constant_dynamic-update-slice_fusion.4
  43.2 1.8 collective-permute-start.10
  44.9 27.0 %collective-permute-done.9 = bf16[2,8,9600]{2,1,0:T(8,128)(2,1)S(1)} collective-permute-done((bf16[2,8,9600]{2,1,0:T(8,128)(2,1)S(1)}, bf16[2,8,9600]{2,1,0:T(8,128)(2,1)S(1)}, u32[]{:S(2)}, u32[]{:S(2)}) %collective-permute-start.9) | collective-permute-done | bytes 307232 | tf_op jit(solution)/shard_map/ppermute | solution.py:463
  71.9 0.8 constant_dynamic-update-slice_fusion.3
  72.6 0.7 constant_dynamic-update-slice_fusion.2
  73.3 0.7 constant_dynamic-update-slice_fusion.1
  74.0 1.3 collective-permute-start.7
  75.3 0.8 collective-permute-start.8
  76.1 1.5 collective-permute-start.11
  77.6 2.7 fusion.3
  80.3 1.5 collective-permute-start.12
  82.3 0.7 constant_dynamic-update-slice_fusion.rest_8_
  83.1 38.9 %collective-permute-done.12.rest_1_ = bf16[7,8,9600]{2,1,0:T(8,128)(2,1)S(1)} collective-permute-done((bf16[7,8,9600]{2,1,0:T(8,128)(2,1)S(1)}, bf16[7,8,9600]{2,1,0:T(8,128)(2,1)S(1)}, u32[]{:S(2)}, u32[]{:S(2)}) %collective-permute-start.12) | collective-permute-done | bytes 1075232 | tf_op jit(solution)/shard_map/ppermute | solution.py:463
  122.0 1.3 collective-permute-done.13.rest_2_
  123.8 1.4 collective-permute-start.18
  125.8 1.6 collective-permute-start.15
  127.4 1.7 collective-permute-start.16
  129.1 1.4 fusion.2
  130.5 19.4 %collective-permute-done.17.rest_6_ = bf16[7,8,9600]{2,1,0:T(8,128)(2,1)S(1)} collective-permute-done((bf16[7,8,9600]{2,1,0:T(8,128)(2,1)S(1)}, bf16[7,8,9600]{2,1,0:T(8,128)(2,1)S(1)}, u32[]{:S(2)}, u32[]{:S(2)}) %collective-permute-start.17) | collective-permute-done | bytes 1075232 | tf_op jit(solution)/shard_map/ppermute | solution.py:463
  150.4 1.5 collective-permute-start.21
  152.0 0.9 collective-permute-start.22
  153.5 19.7 %phase_0.1.before_ref = f32[16,128]{1,0:T(8,128)} custom-call(s32[18]{0:T(128)} %pad_add_fusion.who_ref, s32[32,128]{1,0:T(8,128)} %bitcast.19, s32[78]{0:T(128)} %constant.49.clone.queries_ref, bf16[64,2048]{1,0:T(8,128)(2,1)} %copy-done.2, bf16[512,1024]{1,0:T(8,128)(2,1)} %copy-done.1, bf16[256,256]{1,0:T(8,128)(2,1)} %copy-done.3, ...), custom_call_target="tpu_custom_call" | custom-call | flops 100663296000 | bytes 39321600 | tf_op jit(solution)/shard_map/phase_0/pallas_call | solution.py:230
  174.1 1.0 collective-permute-start.19
  175.1 2.0 collective-permute-start.20
  177.5 1.7 fusion.1
  179.2 36.9 %collective-permute-done.19.rest_0_ = bf16[7,8,9600]{2,1,0:T(8,128)(2,1)S(1)} collective-permute-done((bf16[7,8,9600]{2,1,0:T(8,128)(2,1)}, bf16[7,8,9600]{2,1,0:T(8,128)(2,1)S(1)}, u32[]{:S(2)}, u32[]{:S(2)}) %collective-permute-start.19) | collective-permute-done | bytes 1075232 | tf_op jit(solution)/shard_map/ppermute | solution.py:463
  216.6 1.4 collective-permute-start.24
  218.3 1.7 collective-permute-start.28
  220.0 15.3 %phase_1.1.before_ref = f32[16,128]{1,0:T(8,128)} custom-call(s32[18]{0:T(128)} %pad_add_fusion.who_ref, s32[32,128]{1,0:T(8,128)} %bitcast.20, s32[70]{0:T(128)} %constant.50.clone.queries_ref, bf16[64,2048]{1,0:T(8,128)(2,1)} %copy-done.2, bf16[512,1024]{1,0:T(8,128)(2,1)} %copy-done.1, bf16[256,256]{1,0:T(8,128)(2,1)} %copy-done.3, ...), custom_call_target="tpu_custom_call" | custom-call | flops 100663296000 | bytes 39321600 | tf_op jit(solution)/shard_map/phase_1/pallas_call | solution.py:230
  235.4 4.9 %collective-permute-start.26 = (bf16[7,8,9600]{2,1,0:T(8,128)(2,1)S(1)}, bf16[7,8,9600]{2,1,0:T(8,128)(2,1)}, u32[]{:S(2)}, u32[]{:S(2)}) collective-permute-start(bf16[7,8,9600]{2,1,0:T(8,128)(2,1)S(1)} %get-tuple-element.77), channel_id=1, source_target_pairs={{0,2},{1,3},{2,0},{3,1},{4,6},{5,7},{6,4},{7,5},{8,10},{9,11},{10,... | collective-permute-start | bytes 3225608 | tf_op jit(solution)/shard_map/ppermute | solution.py:463
  240.3 4.0 %collective-permute-start.27 = (bf16[7,8,9600]{2,1,0:T(8,128)(2,1)S(1)}, bf16[7,8,9600]{2,1,0:T(8,128)(2,1)}, u32[]{:S(2)}, u32[]{:S(2)}) collective-permute-start(bf16[7,8,9600]{2,1,0:T(8,128)(2,1)S(1)} %get-tuple-element.76), channel_id=1, source_target_pairs={{0,4},{1,5},{2,6},{3,7},{4,0},{5,1},{6,2},{7,3},{8,12},{9,13},{10,... | collective-permute-start | bytes 3225608 | tf_op jit(solution)/shard_map/ppermute | solution.py:463
  244.5 1.0 collective-permute-start.29
  245.5 1.5 collective-permute-start.30
  247.0 13.8 %phase_2.1.before_ref = f32[16,128]{1,0:T(8,128)} custom-call(s32[18]{0:T(128)} %pad_add_fusion.who_ref, s32[32,128]{1,0:T(8,128)} %bitcast.21, s32[50]{0:T(128)} %constant.51.clone.queries_ref, bf16[64,2048]{1,0:T(8,128)(2,1)} %copy-done.2, bf16[512,1024]{1,0:T(8,128)(2,1)} %copy-done.1, bf16[256,256]{1,0:T(8,128)(2,1)} %copy-done.3, ...), custom_call_target="tpu_custom_call" | custom-call | flops 100663296000 | bytes 39321600 | tf_op jit(solution)/shard_map/phase_2/pallas_call | solution.py:230
  260.9 4.2 %collective-permute-done.26.rest_0_ = bf16[7,8,9600]{2,1,0:T(8,128)(2,1)} collective-permute-done((bf16[7,8,9600]{2,1,0:T(8,128)(2,1)S(1)}, bf16[7,8,9600]{2,1,0:T(8,128)(2,1)}, u32[]{:S(2)}, u32[]{:S(2)}) %collective-permute-start.26) | collective-permute-done | bytes 1075232 | tf_op jit(solution)/shard_map/ppermute | solution.py:463
  265.1 4.0 %collective-permute-done.27.rest_1_ = bf16[7,8,9600]{2,1,0:T(8,128)(2,1)} collective-permute-done((bf16[7,8,9600]{2,1,0:T(8,128)(2,1)S(1)}, bf16[7,8,9600]{2,1,0:T(8,128)(2,1)}, u32[]{:S(2)}, u32[]{:S(2)}) %collective-permute-start.27) | collective-permute-done | bytes 1075232 | tf_op jit(solution)/shard_map/ppermute | solution.py:463
  269.1 2.0 collective-permute-start.32
  271.2 0.8 collective-permute-start.33
  272.0 16.0 %collective-permute-done.29.rest_2_ = bf16[7,8,9600]{2,1,0:T(8,128)(2,1)S(1)} collective-permute-done((bf16[7,8,9600]{2,1,0:T(8,128)(2,1)S(1)}, bf16[7,8,9600]{2,1,0:T(8,128)(2,1)S(1)}, u32[]{:S(2)}, u32[]{:S(2)}) %collective-permute-start.29) | collective-permute-done | bytes 1075232 | tf_op jit(solution)/shard_map/ppermute | solution.py:463
  288.0 4.1 %collective-permute-done.30.rest_3_ = bf16[7,8,9600]{2,1,0:T(8,128)(2,1)} collective-permute-done((bf16[7,8,9600]{2,1,0:T(8,128)(2,1)S(1)}, bf16[7,8,9600]{2,1,0:T(8,128)(2,1)}, u32[]{:S(2)}, u32[]{:S(2)}) %collective-permute-start.30) | collective-permute-done | bytes 1075232 | tf_op jit(solution)/shard_map/ppermute | solution.py:463
  292.1 12.8 %phase_3.1.before_ref = f32[16,128]{1,0:T(8,128)} custom-call(s32[18]{0:T(128)} %pad_add_fusion.who_ref, s32[32,128]{1,0:T(8,128)} %bitcast.22, s32[36]{0:T(128)} %constant.52.clone.queries_ref, bf16[64,2048]{1,0:T(8,128)(2,1)} %copy-done.2, bf16[512,1024]{1,0:T(8,128)(2,1)} %copy-done.1, bf16[256,256]{1,0:T(8,128)(2,1)} %copy-done.3, ...), custom_call_target="tpu_custom_call" | custom-call | flops 100663296000 | bytes 39321600 | tf_op jit(solution)/shard_map/phase_3/pallas_call | solution.py:230
  304.9 3.8 %collective-permute-done.31.rest_0_ = bf16[7,8,9600]{2,1,0:T(8,128)(2,1)} collective-permute-done((bf16[7,8,9600]{2,1,0:T(8,128)(2,1)}, bf16[7,8,9600]{2,1,0:T(8,128)(2,1)}, u32[]{:S(2)}, u32[]{:S(2)}) %collective-permute-start.31) | collective-permute-done | bytes 1075232 | tf_op jit(solution)/shard_map/ppermute | solution.py:463
  308.8 1.8 collective-permute-done.32.rest_1_
  310.6 1.0 copy-done.13
  311.6 9.6 %phase_4.1 = f32[16,128]{1,0:T(8,128)} custom-call(s32[18]{0:T(128)} %pad_add_fusion.who_ref, s32[32,128]{1,0:T(8,128)} %bitcast.23, s32[22]{0:T(128)} %constant.53.clone.queries_ref, bf16[64,2048]{1,0:T(8,128)(2,1)} %copy-done.2, bf16[512,1024]{1,0:T(8,128)(2,1)} %copy-done.1, bf16[256,256]{1,0:T(8,128)(2,1)} %copy-done.3, f32[16,128]{1,0:T(8,128)} %phase_3.1.before_ref, ...), custom_call_target="tpu_custom_call" | custom-call | flops 50331648000 | bytes 19660800 | tf_op jit(solution)/shard_map/phase_4/pallas_call | solution.py:230
  321.3 0.7 broadcast_in_dim.44
  322.1 11.7 %all_to_all.14 = f32[32,1,128]{2,1,0:T(1,128)S(1)} all-to-all(f32[32,1,128]{2,1,0:T(1,128)S(1)} %broadcast_select_fusion), channel_id=1, replica_groups=mesh['shard'=32] {'shard'}, dimensions={0} | all-to-all | bytes 32768 | tf_op jit(solution)/shard_map/all_to_all | solution.py:474
  333.9 0.7 copy.31
  (93 shorter events, 8.8 us)
Async XLA Ops:
  6.5 1.7 copy-start.4
  6.5 146.3 %all-gather.2.cloned.1.call-start = ((), (), s32[]{:S(2)}) async-start(), calls=%async_computation.2 | async-start | bytes 58982400 | tf_op jit(solution)/shard_map/all_gather | solution.py:404
  8.9 23.1 %collective-permute-start = (bf16[1,8,9600]{2,1,0:T(8,128)(2,1)S(1)}, bf16[1,8,9600]{2,1,0:T(8,128)(2,1)S(1)}, u32[]{:S(2)}, u32[]{:S(2)}) collective-permute-start(bf16[1,8,9600]{2,1,0:T(8,128)(2,1)S(1)} %get-tuple-element.43), channel_id=1, source_target_pairs={{0,2},{1,3},{2,0},{3,1},{4,6},{5,7},{6,4},{7,5},{8,10},{9,11},{10,... | collective-permute-start | bytes 460808 | tf_op jit(solution)/shard_map/ppermute | solution.py:463
  11.9 20.1 %collective-permute-start.1 = (bf16[1,8,9600]{2,1,0:T(8,128)(2,1)S(1)}, bf16[1,8,9600]{2,1,0:T(8,128)(2,1)S(1)}, u32[]{:S(2)}, u32[]{:S(2)}) collective-permute-start(bf16[1,8,9600]{2,1,0:T(8,128)(2,1)S(1)} %get-tuple-element.44), channel_id=1, source_target_pairs={{0,4},{1,5},{2,6},{3,7},{4,0},{5,1},{6,2},{7,3},{8,12},{9,13},{10,... | collective-permute-start | bytes 460808 | tf_op jit(solution)/shard_map/ppermute | solution.py:463
  14.9 4.1 %copy-start.8 = (bf16[32,1,3,3]{0,3,2,1:T(4,128)(2,1)S(1)}, bf16[32,1,3,3]{0,3,2,1:T(4,128)(2,1)}, u32[]{:S(2)}) copy-start(bf16[32,1,3,3]{0,3,2,1:T(4,128)(2,1)} %param.15) | copy-start | bytes 1732
  14.9 4.1 %copy-start.9 = (bf16[1,64,3,3]{1,3,2,0:T(4,128)(2,1)S(1)}, bf16[1,64,3,3]{1,3,2,0:T(4,128)(2,1)}, u32[]{:S(2)}) copy-start(bf16[1,64,3,3]{1,3,2,0:T(4,128)(2,1)} %param.17) | copy-start | bytes 3460
  14.9 4.9 %copy-start = (bf16[64,32,3,3]{0,1,3,2:T(8,128)(2,1)S(1)}, bf16[64,32,3,3]{0,1,3,2:T(8,128)(2,1)}, u32[]{:S(2)}) copy-start(bf16[64,32,3,3]{0,1,3,2:T(8,128)(2,1)} %param.16) | copy-start | bytes 110596
  16.4 26.0 %collective-permute-start.2 = (bf16[7,8,9600]{2,1,0:T(8,128)(2,1)}, bf16[7,8,9600]{2,1,0:T(8,128)(2,1)}, u32[]{:S(2)}, u32[]{:S(2)}) collective-permute-start(bf16[7,8,9600]{2,1,0:T(8,128)(2,1)} %get-tuple-element.53), channel_id=1, source_target_pairs={{0,2},{1,3},{2,0},{3,1},{4,6},{5,7},{6,4},{7,5},{8,10},{9,11},{10,... | collective-permute-start | bytes 3225608 | tf_op jit(solution)/shard_map/ppermute | solution.py:463
  17.0 25.5 %collective-permute-start.3 = (bf16[7,8,9600]{2,1,0:T(8,128)(2,1)}, bf16[7,8,9600]{2,1,0:T(8,128)(2,1)}, u32[]{:S(2)}, u32[]{:S(2)}) collective-permute-start(bf16[7,8,9600]{2,1,0:T(8,128)(2,1)} %get-tuple-element.52), channel_id=1, source_target_pairs={{0,4},{1,5},{2,6},{3,7},{4,0},{5,1},{6,2},{7,3},{8,12},{9,13},{10,... | collective-permute-start | bytes 3225608 | tf_op jit(solution)/shard_map/ppermute | solution.py:463
  17.0 57.0 %collective-permute-start.4 = (bf16[14,8,9600]{2,1,0:T(8,128)(2,1)}, bf16[14,8,9600]{2,1,0:T(8,128)(2,1)}, u32[]{:S(2)}, u32[]{:S(2)}) collective-permute-start(bf16[14,8,9600]{2,1,0:T(8,128)(2,1)} %slice.37.rest_0_), channel_id=1, source_target_pairs={{0,8},{1,9},{2,10},{3,11},{4,12},{5,13},{6,14},{7,15},{8,24},{9,25... | collective-permute-start | bytes 6451208 | tf_op jit(solution)/shard_map/ppermute | solution.py:463
  19.8 12.2 %copy-start.7 = (s32[16,8]{0,1:T(8,128)S(1)}, s32[16,8]{0,1:T(8,128)}, u32[]{:S(2)}) copy-start(s32[16,8]{0,1:T(8,128)} %param.14) | copy-start | bytes 1540
  28.4 1.0 copy-start.1
  29.4 0.7 copy-start.2
  30.1 0.6 copy-start.3
  32.8 120.1 %all-to-all-start = ((s32[32,1,128]{2,1,0:T(1,128)}), s32[32,1,128]{2,1,0:T(1,128)S(1)}, u32[]{:S(2)}, u32[]{:S(2)}) async-start(s32[32,1,128]{2,1,0:T(1,128)} %broadcast_in_dim.42), calls=%async_computation | async-start | bytes 32768 | tf_op jit(solution)/shard_map/all_to_all | solution.py:467
  37.6 36.4 %collective-permute-start.5 = (bf16[7,8,9600]{2,1,0:T(8,128)(2,1)}, bf16[7,8,9600]{2,1,0:T(8,128)(2,1)S(1)}, u32[]{:S(2)}, u32[]{:S(2)}) collective-permute-start(bf16[7,8,9600]{2,1,0:T(8,128)(2,1)} %get-tuple-element.52), channel_id=1, source_target_pairs={{0,2},{1,3},{2,0},{3,1},{4,6},{5,7},{6,4},{7,5},{8,10},{9,11},{10,... | collective-permute-start | bytes 3225608 | tf_op jit(solution)/shard_map/ppermute | solution.py:463
  39.5 34.5 %collective-permute-start.6 = (bf16[7,8,9600]{2,1,0:T(8,128)(2,1)}, bf16[7,8,9600]{2,1,0:T(8,128)(2,1)S(1)}, u32[]{:S(2)}, u32[]{:S(2)}) collective-permute-start(bf16[7,8,9600]{2,1,0:T(8,128)(2,1)} %get-tuple-element.53), channel_id=1, source_target_pairs={{0,4},{1,5},{2,6},{3,7},{4,0},{5,1},{6,2},{7,3},{8,12},{9,13},{10,... | collective-permute-start | bytes 3225608 | tf_op jit(solution)/shard_map/ppermute | solution.py:463
  42.5 29.4 %collective-permute-start.9 = (bf16[2,8,9600]{2,1,0:T(8,128)(2,1)S(1)}, bf16[2,8,9600]{2,1,0:T(8,128)(2,1)S(1)}, u32[]{:S(2)}, u32[]{:S(2)}) collective-permute-start(bf16[2,8,9600]{2,1,0:T(8,128)(2,1)S(1)} %pad_maximum_fusion), channel_id=1, source_target_pairs={{0,4},{1,5},{2,6},{3,7},{4,0},{5,1},{6,2},{7,3},{8,12},{9,13},{10,... | collective-permute-start | bytes 921608 | tf_op jit(solution)/shard_map/ppermute | solution.py:463
  43.2 37.2 %collective-permute-start.10 = (bf16[2,8,9600]{2,1,0:T(8,128)(2,1)S(1)}, bf16[2,8,9600]{2,1,0:T(8,128)(2,1)S(1)}, u32[]{:S(2)}, u32[]{:S(2)}) collective-permute-start(bf16[2,8,9600]{2,1,0:T(8,128)(2,1)S(1)} %pad_maximum_fusion.1), channel_id=1, source_target_pairs={{0,2},{1,3},{2,0},{3,1},{4,6},{5,7},{6,4},{7,5},{8,10},{9,11},{10,... | collective-permute-start | bytes 921608 | tf_op jit(solution)/shard_map/ppermute | solution.py:463
  74.0 2.1 copy-start.14
  74.0 2.1 copy-start.15
  74.0 51.2 %collective-permute-start.7 = (bf16[7,8,9600]{2,1,0:T(8,128)(2,1)}, bf16[7,8,9600]{2,1,0:T(8,128)(2,1)S(1)}, u32[]{:S(2)}, u32[]{:S(2)}) collective-permute-start(bf16[7,8,9600]{2,1,0:T(8,128)(2,1)} %collective-permute-done.3.rest_2_), channel_id=1, source_target_pairs={{0,2},{1,3},{2,0},{3,1},{4,6},{5,7},{6,4},{7,5},{8,10},{9,11},{10,... | collective-permute-start | bytes 3225608 | tf_op jit(solution)/shard_map/ppermute | solution.py:463
  75.3 49.9 %collective-permute-start.8 = (bf16[7,8,9600]{2,1,0:T(8,128)(2,1)}, bf16[7,8,9600]{2,1,0:T(8,128)(2,1)S(1)}, u32[]{:S(2)}, u32[]{:S(2)}) collective-permute-start(bf16[7,8,9600]{2,1,0:T(8,128)(2,1)} %collective-permute-done.2.rest_1_), channel_id=1, source_target_pairs={{0,4},{1,5},{2,6},{3,7},{4,0},{5,1},{6,2},{7,3},{8,12},{9,13},{10,... | collective-permute-start | bytes 3225608 | tf_op jit(solution)/shard_map/ppermute | solution.py:463
  76.1 49.1 %collective-permute-start.11 = (bf16[14,8,9600]{2,1,0:T(8,128)(2,1)}, bf16[14,8,9600]{2,1,0:T(8,128)(2,1)S(1)}, u32[]{:S(2)}, u32[]{:S(2)}) collective-permute-start(bf16[14,8,9600]{2,1,0:T(8,128)(2,1)} %collective-permute-done.4.rest_3_), channel_id=1, source_target_pairs={{0,8},{1,9},{2,10},{3,11},{4,12},{5,13},{6,14},{7,15},{8,24},{9,25... | collective-permute-start | bytes 6451208 | tf_op jit(solution)/shard_map/ppermute | solution.py:463
  80.3 41.7 %collective-permute-start.12 = (bf16[7,8,9600]{2,1,0:T(8,128)(2,1)S(1)}, bf16[7,8,9600]{2,1,0:T(8,128)(2,1)S(1)}, u32[]{:S(2)}, u32[]{:S(2)}) collective-permute-start(bf16[7,8,9600]{2,1,0:T(8,128)(2,1)S(1)} %get-tuple-element.62), channel_id=1, source_target_pairs={{0,2},{1,3},{2,0},{3,1},{4,6},{5,7},{6,4},{7,5},{8,10},{9,11},{10,... | collective-permute-start | bytes 3225608 | tf_op jit(solution)/shard_map/ppermute | solution.py:463
  81.8 41.5 %collective-permute-start.13 = (bf16[7,8,9600]{2,1,0:T(8,128)(2,1)}, bf16[7,8,9600]{2,1,0:T(8,128)(2,1)S(1)}, u32[]{:S(2)}, u32[]{:S(2)}) collective-permute-start(bf16[7,8,9600]{2,1,0:T(8,128)(2,1)} %get-tuple-element.61), channel_id=1, source_target_pairs={{0,4},{1,5},{2,6},{3,7},{4,0},{5,1},{6,2},{7,3},{8,12},{9,13},{10,... | collective-permute-start | bytes 3225608 | tf_op jit(solution)/shard_map/ppermute | solution.py:463
  122.0 8.5 %copy-start.16 = (bf16[7,8,9600]{2,1,0:T(8,128)(2,1)}, bf16[7,8,9600]{2,1,0:T(8,128)(2,1)S(1)}, u32[]{:S(2)}) copy-start(bf16[7,8,9600]{2,1,0:T(8,128)(2,1)S(1)} %collective-permute-done.12.rest_1_) | copy-start | bytes 3225604
  123.3 7.3 %copy-start.17 = (bf16[7,8,9600]{2,1,0:T(8,128)(2,1)}, bf16[7,8,9600]{2,1,0:T(8,128)(2,1)S(1)}, u32[]{:S(2)}) copy-start(bf16[7,8,9600]{2,1,0:T(8,128)(2,1)S(1)} %collective-permute-done.13.rest_2_) | copy-start | bytes 3225604
  123.3 26.7 %collective-permute-start.17 = (bf16[7,8,9600]{2,1,0:T(8,128)(2,1)S(1)}, bf16[7,8,9600]{2,1,0:T(8,128)(2,1)S(1)}, u32[]{:S(2)}, u32[]{:S(2)}) collective-permute-start(bf16[7,8,9600]{2,1,0:T(8,128)(2,1)S(1)} %collective-permute-done.13.rest_2_), channel_id=1, source_target_pairs={{0,2},{1,3},{2,0},{3,1},{4,6},{5,7},{6,4},{7,5},{8,10},{9,11},{10,... | collective-permute-start | bytes 3225608 | tf_op jit(solution)/shard_map/ppermute | solution.py:463
  123.8 26.7 %collective-permute-start.18 = (bf16[7,8,9600]{2,1,0:T(8,128)(2,1)S(1)}, bf16[7,8,9600]{2,1,0:T(8,128)(2,1)S(1)}, u32[]{:S(2)}, u32[]{:S(2)}) collective-permute-start(bf16[7,8,9600]{2,1,0:T(8,128)(2,1)S(1)} %collective-permute-done.12.rest_1_), channel_id=1, source_target_pairs={{0,4},{1,5},{2,6},{3,7},{4,0},{5,1},{6,2},{7,3},{8,12},{9,13},{10,... | collective-permute-start | bytes 3225608 | tf_op jit(solution)/shard_map/ppermute | solution.py:463
  125.2 26.8 %copy-start.20 = (bf16[7,8,9600]{2,1,0:T(8,128)(2,1)}, bf16[7,8,9600]{2,1,0:T(8,128)(2,1)S(1)}, u32[]{:S(2)}) copy-start(bf16[7,8,9600]{2,1,0:T(8,128)(2,1)S(1)} %collective-permute-done.7.rest_6_) | copy-start | bytes 3225604
  125.2 26.8 %copy-start.21 = (bf16[7,8,9600]{2,1,0:T(8,128)(2,1)}, bf16[7,8,9600]{2,1,0:T(8,128)(2,1)S(1)}, u32[]{:S(2)}) copy-start(bf16[7,8,9600]{2,1,0:T(8,128)(2,1)S(1)} %collective-permute-done.8.rest_7_) | copy-start | bytes 3225604
  125.2 5.3 %copy-start.5 = (bf16[14,8,9600]{2,1,0:T(8,128)(2,1)}, bf16[14,8,9600]{2,1,0:T(8,128)(2,1)S(1)}, u32[]{:S(2)}) copy-start(bf16[14,8,9600]{2,1,0:T(8,128)(2,1)S(1)} %collective-permute-done.11.rest_0_) | copy-start | bytes 6451204
  125.2 47.9 %collective-permute-start.14 = (bf16[7,8,9600]{2,1,0:T(8,128)(2,1)}, bf16[7,8,9600]{2,1,0:T(8,128)(2,1)}, u32[]{:S(2)}, u32[]{:S(2)}) collective-permute-start(bf16[7,8,9600]{2,1,0:T(8,128)(2,1)} %get-tuple-element.61), channel_id=1, source_target_pairs={{0,2},{1,3},{2,0},{3,1},{4,6},{5,7},{6,4},{7,5},{8,10},{9,11},{10,... | collective-permute-start | bytes 3225608 | tf_op jit(solution)/shard_map/ppermute | solution.py:463
  125.8 47.7 %collective-permute-start.15 = (bf16[7,8,9600]{2,1,0:T(8,128)(2,1)S(1)}, bf16[7,8,9600]{2,1,0:T(8,128)(2,1)}, u32[]{:S(2)}, u32[]{:S(2)}) collective-permute-start(bf16[7,8,9600]{2,1,0:T(8,128)(2,1)S(1)} %get-tuple-element.62), channel_id=1, source_target_pairs={{0,4},{1,5},{2,6},{3,7},{4,0},{5,1},{6,2},{7,3},{8,12},{9,13},{10,... | collective-permute-start | bytes 3225608 | tf_op jit(solution)/shard_map/ppermute | solution.py:463
  127.4 46.7 %collective-permute-start.16 = (bf16[14,8,9600]{2,1,0:T(8,128)(2,1)S(1)}, bf16[14,8,9600]{2,1,0:T(8,128)(2,1)}, u32[]{:S(2)}, u32[]{:S(2)}) collective-permute-start(bf16[14,8,9600]{2,1,0:T(8,128)(2,1)S(1)} %collective-permute-done.11.rest_0_), channel_id=1, source_target_pairs={{0,8},{1,9},{2,10},{3,11},{4,12},{5,13},{6,14},{7,15},{8,24},{9,25... | collective-permute-start | bytes 6451208 | tf_op jit(solution)/shard_map/ppermute | solution.py:463
  149.9 2.0 copy-start.18
  150.4 1.5 copy-start.19
  150.4 85.0 %collective-permute-start.21 = (bf16[7,8,9600]{2,1,0:T(8,128)(2,1)}, bf16[7,8,9600]{2,1,0:T(8,128)(2,1)}, u32[]{:S(2)}, u32[]{:S(2)}) collective-permute-start(bf16[7,8,9600]{2,1,0:T(8,128)(2,1)} %get-tuple-element.68), channel_id=1, source_target_pairs={{0,2},{1,3},{2,0},{3,1},{4,6},{5,7},{6,4},{7,5},{8,10},{9,11},{10,... | collective-permute-start | bytes 3225608 | tf_op jit(solution)/shard_map/ppermute | solution.py:463
  152.0 83.4 %collective-permute-start.22 = (bf16[7,8,9600]{2,1,0:T(8,128)(2,1)}, bf16[7,8,9600]{2,1,0:T(8,128)(2,1)}, u32[]{:S(2)}, u32[]{:S(2)}) collective-permute-start(bf16[7,8,9600]{2,1,0:T(8,128)(2,1)} %get-tuple-element.69), channel_id=1, source_target_pairs={{0,4},{1,5},{2,6},{3,7},{4,0},{5,1},{6,2},{7,3},{8,12},{9,13},{10,... | collective-permute-start | bytes 3225608 | tf_op jit(solution)/shard_map/ppermute | solution.py:463
  152.8 0.6 copy-start.6
  174.1 42.0 %collective-permute-start.19 = (bf16[7,8,9600]{2,1,0:T(8,128)(2,1)}, bf16[7,8,9600]{2,1,0:T(8,128)(2,1)S(1)}, u32[]{:S(2)}, u32[]{:S(2)}) collective-permute-start(bf16[7,8,9600]{2,1,0:T(8,128)(2,1)} %get-tuple-element.69), channel_id=1, source_target_pairs={{0,2},{1,3},{2,0},{3,1},{4,6},{5,7},{6,4},{7,5},{8,10},{9,11},{10,... | collective-permute-start | bytes 3225608 | tf_op jit(solution)/shard_map/ppermute | solution.py:463
  175.1 41.5 %collective-permute-start.20 = (bf16[7,8,9600]{2,1,0:T(8,128)(2,1)}, bf16[7,8,9600]{2,1,0:T(8,128)(2,1)}, u32[]{:S(2)}, u32[]{:S(2)}) collective-permute-start(bf16[7,8,9600]{2,1,0:T(8,128)(2,1)} %get-tuple-element.68), channel_id=1, source_target_pairs={{0,4},{1,5},{2,6},{3,7},{4,0},{5,1},{6,2},{7,3},{8,12},{9,13},{10,... | collective-permute-start | bytes 3225608 | tf_op jit(solution)/shard_map/ppermute | solution.py:463
  177.1 39.5 %collective-permute-start.23 = (bf16[8,8,9600]{2,1,0:T(8,128)(2,1)}, bf16[8,8,9600]{2,1,0:T(8,128)(2,1)S(1)}, u32[]{:S(2)}, u32[]{:S(2)}) collective-permute-start(bf16[8,8,9600]{2,1,0:T(8,128)(2,1)} %constant_dynamic-update-slice_fusion.rest_8_), channel_id=1, source_target_pairs={{0,8},{1,9},{2,10},{3,11},{4,12},{5,13},{6,14},{7,15},{8,24},{9,25... | collective-permute-start | bytes 3686408 | tf_op jit(solution)/shard_map/ppermute | solution.py:463
  216.2 19.2 %copy-start.22 = (bf16[7,8,9600]{2,1,0:T(8,128)(2,1)}, bf16[7,8,9600]{2,1,0:T(8,128)(2,1)S(1)}, u32[]{:S(2)}) copy-start(bf16[7,8,9600]{2,1,0:T(8,128)(2,1)S(1)} %collective-permute-done.19.rest_0_) | copy-start | bytes 3225604
  216.6 18.7 %copy-start.12 = (bf16[8,8,9600]{2,1,0:T(8,128)(2,1)}, bf16[8,8,9600]{2,1,0:T(8,128)(2,1)S(1)}, u32[]{:S(2)}) copy-start(bf16[8,8,9600]{2,1,0:T(8,128)(2,1)S(1)} %collective-permute-done.23.rest_6_) | copy-start | bytes 3686404
  216.6 27.7 %collective-permute-start.24 = (bf16[7,8,9600]{2,1,0:T(8,128)(2,1)}, bf16[7,8,9600]{2,1,0:T(8,128)(2,1)}, u32[]{:S(2)}, u32[]{:S(2)}) collective-permute-start(bf16[7,8,9600]{2,1,0:T(8,128)(2,1)} %collective-permute-done.20.rest_1_), channel_id=1, source_target_pairs={{0,2},{1,3},{2,0},{3,1},{4,6},{5,7},{6,4},{7,5},{8,10},{9,11},{10,... | collective-permute-start | bytes 3225608 | tf_op jit(solution)/shard_map/ppermute | solution.py:463
  218.0 26.3 %collective-permute-start.25 = (bf16[7,8,9600]{2,1,0:T(8,128)(2,1)S(1)}, bf16[7,8,9600]{2,1,0:T(8,128)(2,1)}, u32[]{:S(2)}, u32[]{:S(2)}) collective-permute-start(bf16[7,8,9600]{2,1,0:T(8,128)(2,1)S(1)} %collective-permute-done.19.rest_0_), channel_id=1, source_target_pairs={{0,4},{1,5},{2,6},{3,7},{4,0},{5,1},{6,2},{7,3},{8,12},{9,13},{10,... | collective-permute-start | bytes 3225608 | tf_op jit(solution)/shard_map/ppermute | solution.py:463
  218.3 26.2 %collective-permute-start.28 = (bf16[8,8,9600]{2,1,0:T(8,128)(2,1)S(1)}, bf16[8,8,9600]{2,1,0:T(8,128)(2,1)S(1)}, u32[]{:S(2)}, u32[]{:S(2)}) collective-permute-start(bf16[8,8,9600]{2,1,0:T(8,128)(2,1)S(1)} %collective-permute-done.23.rest_6_), channel_id=1, source_target_pairs={{0,8},{1,9},{2,10},{3,11},{4,12},{5,13},{6,14},{7,15},{8,24},{9,25... | collective-permute-start | bytes 3686408 | tf_op jit(solution)/shard_map/ppermute | solution.py:463
  235.4 29.7 %collective-permute-start.26 = (bf16[7,8,9600]{2,1,0:T(8,128)(2,1)S(1)}, bf16[7,8,9600]{2,1,0:T(8,128)(2,1)}, u32[]{:S(2)}, u32[]{:S(2)}) collective-permute-start(bf16[7,8,9600]{2,1,0:T(8,128)(2,1)S(1)} %get-tuple-element.77), channel_id=1, source_target_pairs={{0,2},{1,3},{2,0},{3,1},{4,6},{5,7},{6,4},{7,5},{8,10},{9,11},{10,... | collective-permute-start | bytes 3225608 | tf_op jit(solution)/shard_map/ppermute | solution.py:463
  240.3 28.7 %collective-permute-start.27 = (bf16[7,8,9600]{2,1,0:T(8,128)(2,1)S(1)}, bf16[7,8,9600]{2,1,0:T(8,128)(2,1)}, u32[]{:S(2)}, u32[]{:S(2)}) collective-permute-start(bf16[7,8,9600]{2,1,0:T(8,128)(2,1)S(1)} %get-tuple-element.76), channel_id=1, source_target_pairs={{0,4},{1,5},{2,6},{3,7},{4,0},{5,1},{6,2},{7,3},{8,12},{9,13},{10,... | collective-permute-start | bytes 3225608 | tf_op jit(solution)/shard_map/ppermute | solution.py:463
  244.5 26.7 %copy-start.11 = (bf16[8,8,9600]{2,1,0:T(8,128)(2,1)}, bf16[8,8,9600]{2,1,0:T(8,128)(2,1)S(1)}, u32[]{:S(2)}) copy-start(bf16[8,8,9600]{2,1,0:T(8,128)(2,1)S(1)} %collective-permute-done.28.rest_4_) | copy-start | bytes 3686404
  244.5 43.5 %collective-permute-start.29 = (bf16[7,8,9600]{2,1,0:T(8,128)(2,1)S(1)}, bf16[7,8,9600]{2,1,0:T(8,128)(2,1)S(1)}, u32[]{:S(2)}, u32[]{:S(2)}) collective-permute-start(bf16[7,8,9600]{2,1,0:T(8,128)(2,1)S(1)} %get-tuple-element.76), channel_id=1, source_target_pairs={{0,2},{1,3},{2,0},{3,1},{4,6},{5,7},{6,4},{7,5},{8,10},{9,11},{10,... | collective-permute-start | bytes 3225608 | tf_op jit(solution)/shard_map/ppermute | solution.py:463
  245.5 46.6 %collective-permute-start.30 = (bf16[7,8,9600]{2,1,0:T(8,128)(2,1)S(1)}, bf16[7,8,9600]{2,1,0:T(8,128)(2,1)}, u32[]{:S(2)}, u32[]{:S(2)}) collective-permute-start(bf16[7,8,9600]{2,1,0:T(8,128)(2,1)S(1)} %get-tuple-element.77), channel_id=1, source_target_pairs={{0,4},{1,5},{2,6},{3,7},{4,0},{5,1},{6,2},{7,3},{8,12},{9,13},{10,... | collective-permute-start | bytes 3225608 | tf_op jit(solution)/shard_map/ppermute | solution.py:463
  269.1 39.7 %collective-permute-start.31 = (bf16[7,8,9600]{2,1,0:T(8,128)(2,1)}, bf16[7,8,9600]{2,1,0:T(8,128)(2,1)}, u32[]{:S(2)}, u32[]{:S(2)}) collective-permute-start(bf16[7,8,9600]{2,1,0:T(8,128)(2,1)} %collective-permute-done.27.rest_1_), channel_id=1, source_target_pairs={{0,2},{1,3},{2,0},{3,1},{4,6},{5,7},{6,4},{7,5},{8,10},{9,11},{10,... | collective-permute-start | bytes 3225608 | tf_op jit(solution)/shard_map/ppermute | solution.py:463
  269.1 41.5 %collective-permute-start.32 = (bf16[7,8,9600]{2,1,0:T(8,128)(2,1)}, bf16[7,8,9600]{2,1,0:T(8,128)(2,1)}, u32[]{:S(2)}, u32[]{:S(2)}) collective-permute-start(bf16[7,8,9600]{2,1,0:T(8,128)(2,1)} %collective-permute-done.26.rest_0_), channel_id=1, source_target_pairs={{0,4},{1,5},{2,6},{3,7},{4,0},{5,1},{6,2},{7,3},{8,12},{9,13},{10,... | collective-permute-start | bytes 3225608 | tf_op jit(solution)/shard_map/ppermute | solution.py:463
  271.2 39.4 %collective-permute-start.33 = (bf16[8,8,9600]{2,1,0:T(8,128)(2,1)S(1)}, bf16[8,8,9600]{2,1,0:T(8,128)(2,1)S(1)}, u32[]{:S(2)}, u32[]{:S(2)}) collective-permute-start(bf16[8,8,9600]{2,1,0:T(8,128)(2,1)S(1)} %collective-permute-done.28.rest_4_), channel_id=1, source_target_pairs={{0,8},{1,9},{2,10},{3,11},{4,12},{5,13},{6,14},{7,15},{8,24},{9,25... | collective-permute-start | bytes 3686408 | tf_op jit(solution)/shard_map/ppermute | solution.py:463
  288.0 4.1 %copy-start.23 = (bf16[7,8,9600]{2,1,0:T(8,128)(2,1)}, bf16[7,8,9600]{2,1,0:T(8,128)(2,1)S(1)}, u32[]{:S(2)}) copy-start(bf16[7,8,9600]{2,1,0:T(8,128)(2,1)S(1)} %collective-permute-done.29.rest_2_) | copy-start | bytes 3225604
  304.9 17.0 %copy-start.10 = (pred[32]{0:T(512)(128)(4,1)S(1)}, pred[32]{0:T(512)(128)(4,1)}, u32[]{:S(2)}) copy-start(pred[32]{0:T(512)(128)(4,1)} %broadcast_in_dim.39) | copy-start | bytes 100
  310.6 1.0 copy-start.13
Sparse Core Ops, SparseCore 0:
  8.9 62.0 all-gather.1

commit v7 on v6

--- a/solution.py
+++ b/solution.py
@@ -11,7 +11,7 @@
 
 R = 5
 GROUP = 16
-SHARES = (7, 7, 1, 1)
+SHARES = (1, 7, 7, 1)
 HEAD = 64
 WEIGHT = 8
 
@@ -99,32 +99,33 @@
                 two_ref, three_ref, before_ref, v_hbm, *rest):
     buffers = len(bounds) - 1
     q_hbm, rest = rest[:buffers], rest[buffers:]
-    (out_ref, q_in, v_in, q_rows, v_rows, maps, scores, rows_ref, vids_ref, entry_ref, ends_ref,
-     q_sem, v_sem) = rest
+    out_ref, q_in, v_in, q_rows, v_rows, maps, scores, list_ref, ends_ref, q_sem, v_sem = rest
     width = v_hbm.shape[2] // R
     side = GROUP * frames
     senders, pairs = out_ref.shape
     chip, core = who_ref[0], who_ref[1]
 
+    chip_videos = 2 * idx_dev
+    bits = (chip_videos - 1).bit_length()
+    assert chip_videos == 1 << bits and senders * pairs <= 1 << (23 - bits)
+    begin = chip * chip_videos
     count = jnp.int32(0)
     for b in range(buffers):
         def one_of(t, n):
             packed = queries_ref[t]
-            row, query = packed & 255, (packed >> 8) & 255
+            row, first = packed & 255, ((packed >> 8) & 255) * k_count
             sender = who_ref[2 + (packed >> 16)]
+            base = ((sender * pairs + first) << (8 + bits)) + (row << bits)
+            line = 2 * sender + core
             for k in range(k_count):
-                pair = query * k_count + k
-                vid = ids_ref[2 * sender + core, pair]
-                rows_ref[n] = row
-                vids_ref[n] = lax.rem(vid, 2 * idx_dev)
-                entry_ref[n] = sender * pairs + pair
-                n = n + (lax.div(vid, 2 * idx_dev) == chip).astype(jnp.int32)
+                vid = ids_ref[line, first + k] - begin
+                list_ref[n] = base + (k << (8 + bits)) + (vid & (chip_videos - 1))
+                n = n + ((vid >> bits) == 0).astype(jnp.int32)
             return n
         count = lax.fori_loop(bounds[b], bounds[b + 1], one_of, count)
         ends_ref[b] = count
     for p in range(GROUP):
-        rows_ref[count + p] = 0
-        vids_ref[count + p] = 0
+        list_ref[count + p] = 0
     groups = (count + GROUP - 1) // GROUP
 
     def fetch(step, slot):
@@ -135,15 +136,15 @@
 
             def one_query(p, _):
                 pltpu.make_async_copy(
-                    q_hbm[b].at[rows_ref[first + p]], q_in.at[slot, p], q_sem.at[slot]
+                    q_hbm[b].at[(list_ref[first + p] >> bits) & 255], q_in.at[slot, p],
+                    q_sem.at[slot],
                 ).start()
                 return 0
             lax.fori_loop(low, high, one_query, 0)
 
         def one_video(p, _):
-            pltpu.make_async_copy(
-                v_hbm.at[vids_ref[first + p]], v_in.at[slot, p], v_sem.at[slot]
-            ).start()
+            vid = list_ref[first + p] & (chip_videos - 1)
+            pltpu.make_async_copy(v_hbm.at[vid], v_in.at[slot, p], v_sem.at[slot]).start()
             return 0
         lax.fori_loop(0, GROUP, one_video, 0)
 
@@ -210,7 +211,7 @@
     out_ref[...] = before_ref[...]
 
     def write(i, _):
-        entry = entry_ref[i]
+        entry = list_ref[i] >> (8 + bits)
         at = pl.ds(lax.div(entry, pairs), 1)
         hit = iota((1, pairs), 1) == lax.rem(entry, pairs)
         out_ref[at, :] = jnp.where(hit, scores[pl.ds(i, 1), :], out_ref[at, :])
@@ -240,8 +241,6 @@
             pltpu.VMEM((cap, frames * frames), jnp.float32),
             pltpu.VMEM((cap, pairs), jnp.float32),
             pltpu.SMEM((cap + GROUP,), jnp.int32),
-            pltpu.SMEM((cap + GROUP,), jnp.int32),
-            pltpu.SMEM((cap + GROUP,), jnp.int32),
             pltpu.SMEM((len(blocks),), jnp.int32),
             pltpu.SemaphoreType.DMA((2,)),
             pltpu.SemaphoreType.DMA((2,)),
@@ -276,13 +275,12 @@
         self.steps = steps
         q_dev = queries.shape[0]
         depth, height, width = sizes
-        counts = [q_dev * s // sum(SHARES) for s in SHARES]
-        starts = [sum(counts[:r]) for r in range(4)]
-        a = counts[0] + counts[1]
-        self.blocks, self.cells, self.arrival = {}, {}, {}
-
-        def put(key, array, cells, at):
-            self.blocks[key], self.cells[key], self.arrival[key] = array, cells, at
+        b1, a1, a2, b2 = [q_dev * s // sum(SHARES) for s in SHARES]
+        here = (0, 0, 0)
+        self.blocks = {("a", 0): queries}
+        self.cells = {("a", 0): [(here, 0, q_dev)]}
+        self.arrival = {("a", 0): -1}
+        self.pieces = {("deep",): [(("a", 0), b1, a1 + a2)]}
 
         def moved(cells, axis, k):
             out = []
@@ -292,91 +290,61 @@
                 out.append((tuple(off), q, n))
             return out
 
-        here = (0, 0, 0)
-        put(("a", 0), queries[:a], [(here, 0, a)], -1)
-        for r in (2, 3):
-            put(("b", r), queries[starts[r]:starts[r] + counts[r]], [(here, starts[r], counts[r])], -1)
-
-        self.describe = {}
-
         def ring(axis, source, name, cells):
             out = []
             for k in range(1, sizes[axis]):
                 target = name + (k,)
-                self.describe[target] = moved(cells, axis, k)
+                self.cells[target] = moved(cells, axis, k)
                 out.append((axis, source, target))
                 source = target
             return out
 
-        first, second = [], []
-        joins = {}
-        for r, (p, q) in ((2, (2, 1)), (3, (1, 2))):
-            cells = self.cells[("b", r)]
-            line = ring(p, ("b", r), ("b", r, "line"), cells)
-            first.append(line)
-            joins[("b", r, "row")] = [("b", r)] + [m[2] for m in line]
-            row = [c for k in range(sizes[p]) for c in moved(cells, p, k)]
-            self.describe[("b", r, "row")] = row
-            turn = ring(q, ("b", r, "row"), ("b", r, "turn"), row)
-            second.append(turn)
-            joins[("b", r, "plane")] = [("b", r, "row")] + [m[2] for m in turn]
-            self.describe[("b", r, "plane")] = [c for k in range(sizes[q]) for c in moved(row, q, k)]
-        joins[("b", 0)] = [("b", 2, "plane"), ("b", 3, "plane")]
-        self.describe[("b", 0)] = [c for r in (2, 3) for c in self.describe[("b", r, "plane")]]
-        self.joins = joins
-        self.halves = {}
-
+        deep = ring(0, ("deep",), ("a",), [(here, b1, a1 + a2)])
         rounds = []
+        planes = []
         for k in range(depth):
+            lists, later = {1: [], 2: []}, {1: [], 2: []}
             for r, (p, q) in ((0, (2, 1)), (1, (1, 2))):
-                own = ("a", k, r)
-                self.halves[own] = (("a", k), starts[r], counts[r])
-                self.describe[own] = [((k, 0, 0), starts[r], counts[r])]
-            lists = {1: [], 2: []}
-            later = {1: [], 2: []}
-            for r, (p, q) in ((0, (2, 1)), (1, (1, 2))):
-                own = ("a", k, r)
-                line = ring(p, own, ("a", k, r, "line"), self.describe[own])
+                own = ("half", k, r)
+                if k == 0:
+                    start, n = (0, b1 + a1) if r == 0 else (b1 + a1, a2 + b2)
+                    first = start
+                else:
+                    start, n = (0, a1) if r == 0 else (a1, a2)
+                    first = start + b1
+                self.pieces[own] = [(("a", k), start, n)]
+                self.cells[own] = [((k, 0, 0), first, n)]
+                line = ring(p, own, ("a", k, r, "line"), self.cells[own])
                 lists[p] += line
-                for i, source in enumerate([own] + [m[2] for m in line]):
-                    later[q] += ring(q, source, ("a", k, r, "turn", i), self.describe[source])
+                found = [own] + [m[2] for m in line]
+                for i, source in enumerate(list(found)):
+                    turn = ring(q, source, ("a", k, r, "turn", i), self.cells[source])
+                    later[q] += turn
+                    found += [m[2] for m in turn]
+                if k == 0:
+                    planes += [(key, 0, b1) if r == 0 else (key, a2, b2) for key in found]
             both = [lists[axis] + later[axis] for axis in (2, 1)]
             for i in range(max(map(len, both))):
                 rounds.append([l[i] for l in both if i < len(l)])
-        pairs_of = lambda ls: [[l[i] for l in ls if i < len(l)] for i in range(max(map(len, ls)))]
-        lead, middle = pairs_of(first), pairs_of(second)
-
-        deep = ring(0, ("a", 0), ("a",), self.cells[("a", 0)]) + ring(
-            0, ("b", 0), ("b",), self.describe[("b", 0)]
-        )
+        self.pieces[("b", 0)] = planes
+        cells = [(self.cells[key][0][0], self.cells[key][0][1] + at, n) for key, at, n in planes]
+        deep += ring(0, ("b", 0), ("b",), cells)
         gap = max(1, len(rounds) // max(1, len(deep)))
         while len(rounds) < gap * len(deep):
             rounds.append([])
         for i, m in enumerate(deep):
             rounds[i * gap].append(m)
         self.per_plane = len(rounds) // depth
-        at = min(2, len(rounds))
-        self.rounds = lead + rounds[:at] + middle + rounds[at:]
-        self.offset = len(lead) + len(middle)
-        for i, messages in enumerate(self.rounds):
+        self.rounds = rounds
+        for i, messages in enumerate(rounds):
             for axis, _, target in messages:
                 self.arrival[target] = i if axis else i + gap - 1
-                self.cells[target] = self.describe[target]
-        self.arrival[("b", 0)] = len(lead) + at + len(middle) - 1
-        self.cells[("b", 0)] = self.describe[("b", 0)]
 
     def block(self, key):
         if key not in self.blocks:
-            if key in self.joins:
-                self.blocks[key] = jnp.concatenate([self.block(k) for k in self.joins[key]], axis=0)
-            else:
-                whole, start, n = self.halves[key]
-                self.blocks[key] = self.block(whole)[start:start + n]
+            parts = [self.block(k)[at:at + n] for k, at, n in self.pieces[key]]
+            self.blocks[key] = parts[0] if len(parts) == 1 else jnp.concatenate(parts, axis=0)
         return self.blocks[key]
-
-    def buffers(self):
-        keys = [k for k in self.arrival if k[0] == "a" and (len(k) == 2 or len(k) > 3)]
-        return keys + [k for k in self.arrival if k[0] == "b" and len(k) == 2 and isinstance(k[1], int)]
 
 
 def body(places, sizes, queries, index_videos, candidates, conv_one, conv_two, conv_three):
@@ -409,10 +377,10 @@
     rounds = gather.rounds
 
     total = len(rounds)
-    ends = [gather.offset + gather.per_plane * (z + 1) - 1 for z in range(sizes[0] - 1)]
+    ends = [gather.per_plane * (z + 1) - 1 for z in range(sizes[0] - 1)]
     ends = sorted({e for e in ends if 0 <= e < total - 2} | {total - 2, total - 1})
     phases = [[] for _ in ends]
-    for key in gather.buffers():
+    for key in gather.arrival:
         phases[next(i for i, e in enumerate(ends) if gather.arrival[key] <= e)].append(key)
     offsets = [(z, y, x) for z in range(sizes[0]) for y in range(sizes[1]) for x in range(sizes[2])]
     back = np.array(
@@ -447,21 +415,21 @@
             tables[-1], k_count, idx_dev, "phase_" + str(p),
         ))
 
-    done, deep = [], []
+    done = []
     for i, messages in enumerate(rounds):
         behind = list(done[i - 2]) if i >= 2 else []
-        if any(axis == 0 for axis, _, _ in messages):
-            behind += deep[-1:]
         if len(tables) <= len(ends) and i >= 2:
             if i == min(ends[len(tables) - 1] + 4, total - 1) and ends[len(tables) - 1] <= i - 2:
                 score()
                 behind.append(tables[-1])
-        sent = [gather.block(source) for _, source, _ in messages]
-        sent = lax.optimization_barrier((*sent, *behind))[:len(sent)]
         done.append([])
-        for (axis, _, target), block in zip(messages, sent):
-            gather.blocks[target] = lax.ppermute(block, "shard", gather.steps[axis])
-            (done[i] if axis else deep).append(gather.blocks[target])
+        for together in ([m for m in messages if m[0]], [m for m in messages if not m[0]]):
+            sent = [gather.block(source) for _, source, _ in together]
+            sent = lax.optimization_barrier((*sent, *behind))[:len(sent)] if sent else []
+            for (axis, _, target), block in zip(together, sent):
+                gather.blocks[target] = lax.ppermute(block, "shard", gather.steps[axis])
+                if axis:
+                    done[i].append(gather.blocks[target])
         if i == 0:
             ids = lax.optimization_barrier((candidates, *done[0]))[0].reshape(1, pairs)
             state["ids"] = lax.all_to_all(

time: 342 us -> 339 us (level)
  Pallas kernels: 79.8 us -> 72.1 us
  local copies, waits for them, and re-layouts: 21.7 us -> 29.3 us
  starting transfers between devices: 51.9 us -> 45 us
    pallas_call x5, Pallas kernels: 71.3 us -> 63.6 us  [pair_scores(): pl.pallas_call(functools.partial(pair_kernel, frames, idx_dev, k_count, b...]
    unnamed x53 -> x51, local copies, waits for them, and re-layouts: 7.9 us -> 15.1 us
    ppermute x34 -> x30, starting transfers between devices: 47.1 us -> 40.1 us  [body(): gather.blocks[target] = lax.ppermute(block, 'shard', gather.steps[axis])]
    ppermute x34 -> x30, waiting for transfers between devices: 161 us -> 162 us  [body(): gather.blocks[target] = lax.ppermute(block, 'shard', gather.steps[axis])]
  transfers between devices with their start and end apart: 36 -> 32, of which waited for: 17 -> 19; matrix products, arithmetic and copies ran while one was open for 5% -> 6% of each run, Pallas kernels for 21% -> 19%
where the time goes in v7:
time: 339 us; the launch traced here: 338 us
  waiting for transfers between devices  163 us (48%)
  Pallas kernels  72.1 us (21%)
  starting transfers between devices  45 us (13%)
  local copies, waits for them, and re-layouts  29.3 us (9%)
  blocking collectives  14.2 us (4%)
  between operations  13.6 us (4%)
    ppermute x30, waiting for transfers between devices, body(): gather.blocks[target] = lax.ppermute(block, 'shard', gather.steps[axis])  162 us
    pallas_call x5, Pallas kernels, pair_scores(): pl.pallas_call(functools.partial(pair_kernel, frames, idx_dev, k_count, b...  63.6 us
    ppermute x30, starting transfers between devices, body(): gather.blocks[target] = lax.ppermute(block, 'shard', gather.steps[axis])  40.1 us
    unnamed x51, local copies, waits for them, and re-layouts  15.1 us
    all_to_all x1, blocking collectives, body(): lax.all_to_all(table.reshape(devices, pairs), 'shard', split_axis=0, conc...  14.2 us
    slice x5, local copies, waits for them, and re-layouts, block(): parts = [self.block(k)[at:at + n] for k, at, n in self.pieces[key]]  9.34 us
    pallas_call x1, Pallas kernels, head_matrices(): pl.pallas_call(head_kernel, out_shape=[jax.ShapeDtypeStruct(s, jnp.bfloat...  8.54 us
  transfers between devices with their start and end apart: 32, of which 19 were waited for; matrix products, arithmetic and copies ran while one was open for 6% of the time, Pallas kernels for 19%

profile of v7, /device:TPU:0, one launch (start us, length us, event | category | flops | bytes accessed | tf_op | source)
XLA Modules:
  0.0 338.1 jit_solution(15882062696249232814)
XLA Ops:
  6.5 0.7 all-gather.2.cloned.1.call-update
  7.3 1.0 copy-done.4
  8.2 1.6 fusion
  9.8 2.9 collective-permute-start
  12.7 1.5 collective-permute-start.1
  14.3 1.5 slice.55
  15.8 1.6 collective-permute-start.2
  19.1 8.5 %head_matrices.1 = (bf16[64,2048]{1,0:T(8,128)(2,1)S(1)}, bf16[512,1024]{1,0:T(8,128)(2,1)S(1)}, bf16[256,256]{1,0:T(8,128)(2,1)S(1)}) custom-call(bf16[9,1,32]{2,1,0:T(2,128)(2,1)S(1)} %reshape.74.one_w, bf16[9,32,64]{2,1,0:T(8,128)(2,1)S(1)} %bitcast.16, bf16[9,1,64]{2,1,0:T(2,128)(2,1)S(1)} %reshape.75.three_w), custom_call_target="tpu_custom_call" | custom-call | flops 1000000000 | bytes 3000000 | tf_op jit(solution)/shard_map/head_matrices/pallas_call | solution.py:86
  27.7 1.0 copy-done.1
  28.6 0.7 copy-done.2
  30.0 0.7 dynamic-slice_bitcast_fusion
  31.3 0.7 slice_dynamic-update-slice_fusion.7
  32.0 8.9 %collective-permute-done.rest_1_ = bf16[8,8,9600]{2,1,0:T(8,128)(2,1)} collective-permute-done((bf16[8,8,9600]{2,1,0:T(8,128)(2,1)}, bf16[8,8,9600]{2,1,0:T(8,128)(2,1)}, u32[]{:S(2)}, u32[]{:S(2)}) %collective-permute-start) | collective-permute-done | bytes 1228832 | tf_op jit(solution)/shard_map/ppermute | solution.py:430
  40.9 2.1 collective-permute-done.1.rest_2_
  43.8 4.9 %all-to-all-start = ((s32[32,1,128]{2,1,0:T(1,128)}), s32[32,1,128]{2,1,0:T(1,128)S(1)}, u32[]{:S(2)}, u32[]{:S(2)}) async-start(s32[32,1,128]{2,1,0:T(1,128)} %broadcast_in_dim.42), calls=%async_computation | async-start | bytes 32768 | tf_op jit(solution)/shard_map/all_to_all | solution.py:435
  48.7 1.8 collective-permute-start.5
  50.5 1.5 collective-permute-start.6
  52.0 1.6 slice_dynamic-update-slice_fusion.5
  53.6 15.9 %collective-permute-done.4.rest_5_ = bf16[8,8,9600]{2,1,0:T(8,128)(2,1)} collective-permute-done((bf16[8,8,9600]{2,1,0:T(8,128)(2,1)}, bf16[8,8,9600]{2,1,0:T(8,128)(2,1)}, u32[]{:S(2)}, u32[]{:S(2)}) %collective-permute-start.4) | collective-permute-done | bytes 1228832 | tf_op jit(solution)/shard_map/ppermute | solution.py:430
  69.5 1.6 slice_dynamic-update-slice_fusion.4
  71.1 1.6 collective-permute-start.7
  72.6 3.1 fusion.3
  76.2 1.5 collective-permute-start.9
  77.8 15.9 %collective-permute-done.5.rest_6_ = bf16[8,8,9600]{2,1,0:T(8,128)(2,1)S(1)} collective-permute-done((bf16[8,8,9600]{2,1,0:T(8,128)(2,1)}, bf16[8,8,9600]{2,1,0:T(8,128)(2,1)S(1)}, u32[]{:S(2)}, u32[]{:S(2)}) %collective-permute-start.5) | collective-permute-done | bytes 1228832 | tf_op jit(solution)/shard_map/ppermute | solution.py:430
  93.6 2.1 collective-permute-done.6.rest_7_
  95.8 2.0 collective-permute-start.11
  99.1 1.6 slice_dynamic-update-slice_fusion.2
  100.7 1.6 slice_dynamic-update-slice_fusion.1
  102.3 0.7 slice_dynamic-update-slice_fusion
  103.0 13.7 %collective-permute-done.8.rest_1_ = bf16[7,8,9600]{2,1,0:T(8,128)(2,1)S(1)} collective-permute-done((bf16[7,8,9600]{2,1,0:T(8,128)(2,1)}, bf16[7,8,9600]{2,1,0:T(8,128)(2,1)S(1)}, u32[]{:S(2)}, u32[]{:S(2)}) %collective-permute-start.8) | collective-permute-done | bytes 1075232 | tf_op jit(solution)/shard_map/ppermute | solution.py:430
  116.7 2.1 collective-permute-done.9.rest_2_
  118.8 2.0 collective-permute-start.14
  120.8 1.6 collective-permute-start.12
  122.4 3.1 fusion.2
  125.5 36.4 %collective-permute-done.13.rest_6_ = bf16[7,8,9600]{2,1,0:T(8,128)(2,1)S(1)} collective-permute-done((bf16[7,8,9600]{2,1,0:T(8,128)(2,1)S(1)}, bf16[7,8,9600]{2,1,0:T(8,128)(2,1)S(1)}, u32[]{:S(2)}, u32[]{:S(2)}) %collective-permute-start.13) | collective-permute-done | bytes 1075232 | tf_op jit(solution)/shard_map/ppermute | solution.py:430
  161.9 1.5 collective-permute-done.14.rest_7_
  164.4 1.5 collective-permute-start.19
  166.5 18.4 %phase_0.1.before_ref = f32[16,128]{1,0:T(8,128)} custom-call(s32[18]{0:T(128)} %pad_add_fusion.who_ref, s32[32,128]{1,0:T(8,128)} %bitcast.19, s32[78]{0:T(128)} %constant.49.clone.queries_ref, bf16[64,2048]{1,0:T(8,128)(2,1)} %copy-done.2, bf16[512,1024]{1,0:T(8,128)(2,1)} %copy-done.1, bf16[256,256]{1,0:T(8,128)(2,1)} %copy-done.3, ...), custom_call_target="tpu_custom_call" | custom-call | flops 100663296000 | bytes 39321600 | tf_op jit(solution)/shard_map/phase_0/pallas_call | solution.py:231
  185.0 1.3 collective-permute-start.15
  186.4 1.2 copy-done.5
  187.7 0.9 collective-permute-start.17
  188.5 22.5 %collective-permute-done.15.rest_0_ = bf16[7,8,9600]{2,1,0:T(8,128)(2,1)} collective-permute-done((bf16[7,8,9600]{2,1,0:T(8,128)(2,1)}, bf16[7,8,9600]{2,1,0:T(8,128)(2,1)}, u32[]{:S(2)}, u32[]{:S(2)}) %collective-permute-start.15) | collective-permute-done | bytes 1075232 | tf_op jit(solution)/shard_map/ppermute | solution.py:430
  211.0 1.0 collective-permute-done.16.rest_1_
  212.0 0.9 collective-permute-start.20
  213.0 1.5 collective-permute-start.21
  214.5 13.8 %phase_1.1.before_ref = f32[16,128]{1,0:T(8,128)} custom-call(s32[18]{0:T(128)} %pad_add_fusion.who_ref, s32[32,128]{1,0:T(8,128)} %bitcast.20, s32[70]{0:T(128)} %constant.50.clone.queries_ref, bf16[64,2048]{1,0:T(8,128)(2,1)} %copy-done.2, bf16[512,1024]{1,0:T(8,128)(2,1)} %copy-done.1, bf16[256,256]{1,0:T(8,128)(2,1)} %copy-done.3, ...), custom_call_target="tpu_custom_call" | custom-call | flops 100663296000 | bytes 39321600 | tf_op jit(solution)/shard_map/phase_1/pallas_call | solution.py:231
  228.3 4.9 %collective-permute-start.23 = (bf16[7,8,9600]{2,1,0:T(8,128)(2,1)S(1)}, bf16[7,8,9600]{2,1,0:T(8,128)(2,1)}, u32[]{:S(2)}, u32[]{:S(2)}) collective-permute-start(bf16[7,8,9600]{2,1,0:T(8,128)(2,1)S(1)} %get-tuple-element.67), channel_id=1, source_target_pairs={{0,2},{1,3},{2,0},{3,1},{4,6},{5,7},{6,4},{7,5},{8,10},{9,11},{10,... | collective-permute-start | bytes 3225608 | tf_op jit(solution)/shard_map/ppermute | solution.py:430
  233.3 1.2 collective-permute-start.24
  234.5 4.4 %collective-permute-done.20.rest_5_ = bf16[7,8,9600]{2,1,0:T(8,128)(2,1)S(1)} collective-permute-done((bf16[7,8,9600]{2,1,0:T(8,128)(2,1)}, bf16[7,8,9600]{2,1,0:T(8,128)(2,1)S(1)}, u32[]{:S(2)}, u32[]{:S(2)}) %collective-permute-start.20) | collective-permute-done | bytes 1075232 | tf_op jit(solution)/shard_map/ppermute | solution.py:430
  239.5 1.6 collective-permute-start.25
  241.1 1.5 collective-permute-start.26
  242.6 12.8 %phase_2.1.before_ref = f32[16,128]{1,0:T(8,128)} custom-call(s32[18]{0:T(128)} %pad_add_fusion.who_ref, s32[32,128]{1,0:T(8,128)} %bitcast.21, s32[50]{0:T(128)} %constant.51.clone.queries_ref, bf16[64,2048]{1,0:T(8,128)(2,1)} %copy-done.2, bf16[512,1024]{1,0:T(8,128)(2,1)} %copy-done.1, bf16[256,256]{1,0:T(8,128)(2,1)} %copy-done.3, ...), custom_call_target="tpu_custom_call" | custom-call | flops 100663296000 | bytes 39321600 | tf_op jit(solution)/shard_map/phase_2/pallas_call | solution.py:231
  255.4 6.7 %collective-permute-done.23.rest_1_ = bf16[7,8,9600]{2,1,0:T(8,128)(2,1)} collective-permute-done((bf16[7,8,9600]{2,1,0:T(8,128)(2,1)S(1)}, bf16[7,8,9600]{2,1,0:T(8,128)(2,1)}, u32[]{:S(2)}, u32[]{:S(2)}) %collective-permute-start.23) | collective-permute-done | bytes 1075232 | tf_op jit(solution)/shard_map/ppermute | solution.py:430
  262.5 1.6 collective-permute-start.28
  264.1 1.5 collective-permute-start.29
  265.6 1.6 collective-permute-start.27
  267.2 17.8 %collective-permute-done.25.rest_3_ = bf16[7,8,9600]{2,1,0:T(8,128)(2,1)S(1)} collective-permute-done((bf16[7,8,9600]{2,1,0:T(8,128)(2,1)S(1)}, bf16[7,8,9600]{2,1,0:T(8,128)(2,1)S(1)}, u32[]{:S(2)}, u32[]{:S(2)}) %collective-permute-start.25) | collective-permute-done | bytes 1075232 | tf_op jit(solution)/shard_map/ppermute | solution.py:430
  286.0 9.5 %phase_3.1.before_ref = f32[16,128]{1,0:T(8,128)} custom-call(s32[18]{0:T(128)} %pad_add_fusion.who_ref, s32[32,128]{1,0:T(8,128)} %bitcast.22, s32[36]{0:T(128)} %constant.52.clone.queries_ref, bf16[64,2048]{1,0:T(8,128)(2,1)} %copy-done.2, bf16[512,1024]{1,0:T(8,128)(2,1)} %copy-done.1, bf16[256,256]{1,0:T(8,128)(2,1)} %copy-done.3, ...), custom_call_target="tpu_custom_call" | custom-call | flops 100663296000 | bytes 39321600 | tf_op jit(solution)/shard_map/phase_3/pallas_call | solution.py:231
  295.5 9.3 %collective-permute-done.28.rest_1_ = bf16[7,8,9600]{2,1,0:T(8,128)(2,1)} collective-permute-done((bf16[7,8,9600]{2,1,0:T(8,128)(2,1)}, bf16[7,8,9600]{2,1,0:T(8,128)(2,1)}, u32[]{:S(2)}, u32[]{:S(2)}) %collective-permute-start.28) | collective-permute-done | bytes 1075232 | tf_op jit(solution)/shard_map/ppermute | solution.py:430
  305.4 1.0 copy-done.15
  306.4 9.1 %phase_4.1 = f32[16,128]{1,0:T(8,128)} custom-call(s32[18]{0:T(128)} %pad_add_fusion.who_ref, s32[32,128]{1,0:T(8,128)} %bitcast.23, s32[22]{0:T(128)} %constant.53.clone.queries_ref, bf16[64,2048]{1,0:T(8,128)(2,1)} %copy-done.2, bf16[512,1024]{1,0:T(8,128)(2,1)} %copy-done.1, bf16[256,256]{1,0:T(8,128)(2,1)} %copy-done.3, f32[16,128]{1,0:T(8,128)} %phase_3.1.before_ref, ...), custom_call_target="tpu_custom_call" | custom-call | flops 50331648000 | bytes 19660800 | tf_op jit(solution)/shard_map/phase_4/pallas_call | solution.py:231
  315.5 0.7 broadcast_in_dim.44
  316.3 14.2 %all_to_all.14 = f32[32,1,128]{2,1,0:T(1,128)S(1)} all-to-all(f32[32,1,128]{2,1,0:T(1,128)S(1)} %broadcast_select_fusion), channel_id=1, replica_groups=mesh['shard'=32] {'shard'}, dimensions={0} | all-to-all | bytes 32768 | tf_op jit(solution)/shard_map/all_to_all | solution.py:442
  330.6 0.7 copy.31
  (81 shorter events, 10.3 us)
Async XLA Ops:
  6.5 159.4 %all-gather.2.cloned.1.call-start = ((), (), s32[]{:S(2)}) async-start(), calls=%async_computation.2 | async-start | bytes 58982400 | tf_op jit(solution)/shard_map/all_gather | solution.py:372
  6.5 1.7 copy-start.4
  9.8 8.6 %copy-start.11 = (bf16[32,1,3,3]{0,3,2,1:T(4,128)(2,1)S(1)}, bf16[32,1,3,3]{0,3,2,1:T(4,128)(2,1)}, u32[]{:S(2)}) copy-start(bf16[32,1,3,3]{0,3,2,1:T(4,128)(2,1)} %param.15) | copy-start | bytes 1732
  9.8 8.6 %copy-start.12 = (bf16[1,64,3,3]{1,3,2,0:T(4,128)(2,1)S(1)}, bf16[1,64,3,3]{1,3,2,0:T(4,128)(2,1)}, u32[]{:S(2)}) copy-start(bf16[1,64,3,3]{1,3,2,0:T(4,128)(2,1)} %param.17) | copy-start | bytes 3460
  9.8 9.3 %copy-start = (bf16[64,32,3,3]{0,1,3,2:T(8,128)(2,1)S(1)}, bf16[64,32,3,3]{0,1,3,2:T(8,128)(2,1)}, u32[]{:S(2)}) copy-start(bf16[64,32,3,3]{0,1,3,2:T(8,128)(2,1)} %param.16) | copy-start | bytes 110596
  9.8 31.1 %collective-permute-start = (bf16[8,8,9600]{2,1,0:T(8,128)(2,1)}, bf16[8,8,9600]{2,1,0:T(8,128)(2,1)}, u32[]{:S(2)}, u32[]{:S(2)}) collective-permute-start(bf16[8,8,9600]{2,1,0:T(8,128)(2,1)} %get-tuple-element.38), channel_id=1, source_target_pairs={{0,2},{1,3},{2,0},{3,1},{4,6},{5,7},{6,4},{7,5},{8,10},{9,11},{10,... | collective-permute-start | bytes 3686408 | tf_op jit(solution)/shard_map/ppermute | solution.py:430
  12.7 30.3 %collective-permute-start.1 = (bf16[8,8,9600]{2,1,0:T(8,128)(2,1)}, bf16[8,8,9600]{2,1,0:T(8,128)(2,1)}, u32[]{:S(2)}, u32[]{:S(2)}) collective-permute-start(bf16[8,8,9600]{2,1,0:T(8,128)(2,1)} %get-tuple-element.39), channel_id=1, source_target_pairs={{0,4},{1,5},{2,6},{3,7},{4,0},{5,1},{6,2},{7,3},{8,12},{9,13},{10,... | collective-permute-start | bytes 3686408 | tf_op jit(solution)/shard_map/ppermute | solution.py:430
  15.8 55.3 %collective-permute-start.2 = (bf16[14,8,9600]{2,1,0:T(8,128)(2,1)}, bf16[14,8,9600]{2,1,0:T(8,128)(2,1)}, u32[]{:S(2)}, u32[]{:S(2)}) collective-permute-start(bf16[14,8,9600]{2,1,0:T(8,128)(2,1)} %slice.55), channel_id=1, source_target_pairs={{0,8},{1,9},{2,10},{3,11},{4,12},{5,13},{6,14},{7,15},{8,24},{9,25... | collective-permute-start | bytes 6451208 | tf_op jit(solution)/shard_map/ppermute | solution.py:430
  17.3 58.4 %collective-permute-start.3 = (bf16[8,8,9600]{2,1,0:T(8,128)(2,1)}, bf16[8,8,9600]{2,1,0:T(8,128)(2,1)}, u32[]{:S(2)}, u32[]{:S(2)}) collective-permute-start(bf16[8,8,9600]{2,1,0:T(8,128)(2,1)} %get-tuple-element.44), channel_id=1, source_target_pairs={{0,2},{1,3},{2,0},{3,1},{4,6},{5,7},{6,4},{7,5},{8,10},{9,11},{10,... | collective-permute-start | bytes 3686408 | tf_op jit(solution)/shard_map/ppermute | solution.py:430
  17.9 51.6 %collective-permute-start.4 = (bf16[8,8,9600]{2,1,0:T(8,128)(2,1)}, bf16[8,8,9600]{2,1,0:T(8,128)(2,1)}, u32[]{:S(2)}, u32[]{:S(2)}) collective-permute-start(bf16[8,8,9600]{2,1,0:T(8,128)(2,1)} %get-tuple-element.45), channel_id=1, source_target_pairs={{0,4},{1,5},{2,6},{3,7},{4,0},{5,1},{6,2},{7,3},{8,12},{9,13},{10,... | collective-permute-start | bytes 3686408 | tf_op jit(solution)/shard_map/ppermute | solution.py:430
  19.1 23.9 %copy-start.10 = (s32[16,8]{0,1:T(8,128)S(1)}, s32[16,8]{0,1:T(8,128)}, u32[]{:S(2)}) copy-start(s32[16,8]{0,1:T(8,128)} %param.14) | copy-start | bytes 1540
  27.6 1.0 copy-start.1
  28.6 0.7 copy-start.2
  29.3 0.7 copy-start.3
  43.8 122.2 %all-to-all-start = ((s32[32,1,128]{2,1,0:T(1,128)}), s32[32,1,128]{2,1,0:T(1,128)S(1)}, u32[]{:S(2)}, u32[]{:S(2)}) async-start(s32[32,1,128]{2,1,0:T(1,128)} %broadcast_in_dim.42), calls=%async_computation | async-start | bytes 32768 | tf_op jit(solution)/shard_map/all_to_all | solution.py:435
  48.7 44.9 %collective-permute-start.5 = (bf16[8,8,9600]{2,1,0:T(8,128)(2,1)}, bf16[8,8,9600]{2,1,0:T(8,128)(2,1)S(1)}, u32[]{:S(2)}, u32[]{:S(2)}) collective-permute-start(bf16[8,8,9600]{2,1,0:T(8,128)(2,1)} %collective-permute-done.1.rest_2_), channel_id=1, source_target_pairs={{0,2},{1,3},{2,0},{3,1},{4,6},{5,7},{6,4},{7,5},{8,10},{9,11},{10,... | collective-permute-start | bytes 3686408 | tf_op jit(solution)/shard_map/ppermute | solution.py:430
  50.5 45.2 %collective-permute-start.6 = (bf16[8,8,9600]{2,1,0:T(8,128)(2,1)}, bf16[8,8,9600]{2,1,0:T(8,128)(2,1)S(1)}, u32[]{:S(2)}, u32[]{:S(2)}) collective-permute-start(bf16[8,8,9600]{2,1,0:T(8,128)(2,1)} %collective-permute-done.rest_1_), channel_id=1, source_target_pairs={{0,4},{1,5},{2,6},{3,7},{4,0},{5,1},{6,2},{7,3},{8,12},{9,13},{10,... | collective-permute-start | bytes 3686408 | tf_op jit(solution)/shard_map/ppermute | solution.py:430
  71.1 49.8 %collective-permute-start.7 = (bf16[14,8,9600]{2,1,0:T(8,128)(2,1)}, bf16[14,8,9600]{2,1,0:T(8,128)(2,1)}, u32[]{:S(2)}, u32[]{:S(2)}) collective-permute-start(bf16[14,8,9600]{2,1,0:T(8,128)(2,1)} %collective-permute-done.2.rest_3_), channel_id=1, source_target_pairs={{0,8},{1,9},{2,10},{3,11},{4,12},{5,13},{6,14},{7,15},{8,24},{9,25... | collective-permute-start | bytes 6451208 | tf_op jit(solution)/shard_map/ppermute | solution.py:430
  75.7 41.0 %collective-permute-start.8 = (bf16[7,8,9600]{2,1,0:T(8,128)(2,1)}, bf16[7,8,9600]{2,1,0:T(8,128)(2,1)S(1)}, u32[]{:S(2)}, u32[]{:S(2)}) collective-permute-start(bf16[7,8,9600]{2,1,0:T(8,128)(2,1)} %get-tuple-element.52), channel_id=1, source_target_pairs={{0,2},{1,3},{2,0},{3,1},{4,6},{5,7},{6,4},{7,5},{8,10},{9,11},{10,... | collective-permute-start | bytes 3225608 | tf_op jit(solution)/shard_map/ppermute | solution.py:430
  76.2 42.5 %collective-permute-start.9 = (bf16[7,8,9600]{2,1,0:T(8,128)(2,1)}, bf16[7,8,9600]{2,1,0:T(8,128)(2,1)S(1)}, u32[]{:S(2)}, u32[]{:S(2)}) collective-permute-start(bf16[7,8,9600]{2,1,0:T(8,128)(2,1)} %get-tuple-element.51), channel_id=1, source_target_pairs={{0,4},{1,5},{2,6},{3,7},{4,0},{5,1},{6,2},{7,3},{8,12},{9,13},{10,... | collective-permute-start | bytes 3225608 | tf_op jit(solution)/shard_map/ppermute | solution.py:430
  93.6 31.8 %copy-start.6 = (bf16[8,8,9600]{2,1,0:T(8,128)(2,1)}, bf16[8,8,9600]{2,1,0:T(8,128)(2,1)S(1)}, u32[]{:S(2)}) copy-start(bf16[8,8,9600]{2,1,0:T(8,128)(2,1)S(1)} %collective-permute-done.5.rest_6_) | copy-start | bytes 3686404
  95.7 29.7 %copy-start.7 = (bf16[8,8,9600]{2,1,0:T(8,128)(2,1)}, bf16[8,8,9600]{2,1,0:T(8,128)(2,1)S(1)}, u32[]{:S(2)}) copy-start(bf16[8,8,9600]{2,1,0:T(8,128)(2,1)S(1)} %collective-permute-done.6.rest_7_) | copy-start | bytes 3686404
  95.7 89.2 %collective-permute-start.10 = (bf16[7,8,9600]{2,1,0:T(8,128)(2,1)}, bf16[7,8,9600]{2,1,0:T(8,128)(2,1)}, u32[]{:S(2)}, u32[]{:S(2)}) collective-permute-start(bf16[7,8,9600]{2,1,0:T(8,128)(2,1)} %get-tuple-element.51), channel_id=1, source_target_pairs={{0,2},{1,3},{2,0},{3,1},{4,6},{5,7},{6,4},{7,5},{8,10},{9,11},{10,... | collective-permute-start | bytes 3225608 | tf_op jit(solution)/shard_map/ppermute | solution.py:430
  95.8 89.2 %collective-permute-start.11 = (bf16[7,8,9600]{2,1,0:T(8,128)(2,1)}, bf16[7,8,9600]{2,1,0:T(8,128)(2,1)}, u32[]{:S(2)}, u32[]{:S(2)}) collective-permute-start(bf16[7,8,9600]{2,1,0:T(8,128)(2,1)} %get-tuple-element.52), channel_id=1, source_target_pairs={{0,4},{1,5},{2,6},{3,7},{4,0},{5,1},{6,2},{7,3},{8,12},{9,13},{10,... | collective-permute-start | bytes 3225608 | tf_op jit(solution)/shard_map/ppermute | solution.py:430
  116.7 8.8 %copy-start.16 = (bf16[7,8,9600]{2,1,0:T(8,128)(2,1)}, bf16[7,8,9600]{2,1,0:T(8,128)(2,1)S(1)}, u32[]{:S(2)}) copy-start(bf16[7,8,9600]{2,1,0:T(8,128)(2,1)S(1)} %collective-permute-done.8.rest_1_) | copy-start | bytes 3225604
  118.8 6.7 %copy-start.17 = (bf16[7,8,9600]{2,1,0:T(8,128)(2,1)}, bf16[7,8,9600]{2,1,0:T(8,128)(2,1)S(1)}, u32[]{:S(2)}) copy-start(bf16[7,8,9600]{2,1,0:T(8,128)(2,1)S(1)} %collective-permute-done.9.rest_2_) | copy-start | bytes 3225604
  118.8 43.2 %collective-permute-start.13 = (bf16[7,8,9600]{2,1,0:T(8,128)(2,1)S(1)}, bf16[7,8,9600]{2,1,0:T(8,128)(2,1)S(1)}, u32[]{:S(2)}, u32[]{:S(2)}) collective-permute-start(bf16[7,8,9600]{2,1,0:T(8,128)(2,1)S(1)} %collective-permute-done.9.rest_2_), channel_id=1, source_target_pairs={{0,2},{1,3},{2,0},{3,1},{4,6},{5,7},{6,4},{7,5},{8,10},{9,11},{10,... | collective-permute-start | bytes 3225608 | tf_op jit(solution)/shard_map/ppermute | solution.py:430
  118.8 44.6 %collective-permute-start.14 = (bf16[7,8,9600]{2,1,0:T(8,128)(2,1)S(1)}, bf16[7,8,9600]{2,1,0:T(8,128)(2,1)S(1)}, u32[]{:S(2)}, u32[]{:S(2)}) collective-permute-start(bf16[7,8,9600]{2,1,0:T(8,128)(2,1)S(1)} %collective-permute-done.8.rest_1_), channel_id=1, source_target_pairs={{0,4},{1,5},{2,6},{3,7},{4,0},{5,1},{6,2},{7,3},{8,12},{9,13},{10,... | collective-permute-start | bytes 3225608 | tf_op jit(solution)/shard_map/ppermute | solution.py:430
  120.8 65.4 %collective-permute-start.12 = (bf16[14,8,9600]{2,1,0:T(8,128)(2,1)}, bf16[14,8,9600]{2,1,0:T(8,128)(2,1)S(1)}, u32[]{:S(2)}, u32[]{:S(2)}) collective-permute-start(bf16[14,8,9600]{2,1,0:T(8,128)(2,1)} %collective-permute-done.7.rest_0_), channel_id=1, source_target_pairs={{0,8},{1,9},{2,10},{3,11},{4,12},{5,13},{6,14},{7,15},{8,24},{9,25... | collective-permute-start | bytes 6451208 | tf_op jit(solution)/shard_map/ppermute | solution.py:430
  161.9 1.8 copy-start.18
  163.4 1.0 copy-start.19
  163.4 64.9 %collective-permute-start.18 = (bf16[7,8,9600]{2,1,0:T(8,128)(2,1)}, bf16[7,8,9600]{2,1,0:T(8,128)(2,1)}, u32[]{:S(2)}, u32[]{:S(2)}) collective-permute-start(bf16[7,8,9600]{2,1,0:T(8,128)(2,1)} %get-tuple-element.59), channel_id=1, source_target_pairs={{0,2},{1,3},{2,0},{3,1},{4,6},{5,7},{6,4},{7,5},{8,10},{9,11},{10,... | collective-permute-start | bytes 3225608 | tf_op jit(solution)/shard_map/ppermute | solution.py:430
  164.4 63.9 %collective-permute-start.19 = (bf16[7,8,9600]{2,1,0:T(8,128)(2,1)}, bf16[7,8,9600]{2,1,0:T(8,128)(2,1)}, u32[]{:S(2)}, u32[]{:S(2)}) collective-permute-start(bf16[7,8,9600]{2,1,0:T(8,128)(2,1)} %get-tuple-element.60), channel_id=1, source_target_pairs={{0,4},{1,5},{2,6},{3,7},{4,0},{5,1},{6,2},{7,3},{8,12},{9,13},{10,... | collective-permute-start | bytes 3225608 | tf_op jit(solution)/shard_map/ppermute | solution.py:430
  165.9 0.6 copy-start.9
  184.9 2.7 copy-start.8
  185.0 26.1 %collective-permute-start.15 = (bf16[7,8,9600]{2,1,0:T(8,128)(2,1)}, bf16[7,8,9600]{2,1,0:T(8,128)(2,1)}, u32[]{:S(2)}, u32[]{:S(2)}) collective-permute-start(bf16[7,8,9600]{2,1,0:T(8,128)(2,1)} %get-tuple-element.60), channel_id=1, source_target_pairs={{0,2},{1,3},{2,0},{3,1},{4,6},{5,7},{6,4},{7,5},{8,10},{9,11},{10,... | collective-permute-start | bytes 3225608 | tf_op jit(solution)/shard_map/ppermute | solution.py:430
  186.3 25.8 %collective-permute-start.16 = (bf16[7,8,9600]{2,1,0:T(8,128)(2,1)}, bf16[7,8,9600]{2,1,0:T(8,128)(2,1)}, u32[]{:S(2)}, u32[]{:S(2)}) collective-permute-start(bf16[7,8,9600]{2,1,0:T(8,128)(2,1)} %get-tuple-element.59), channel_id=1, source_target_pairs={{0,4},{1,5},{2,6},{3,7},{4,0},{5,1},{6,2},{7,3},{8,12},{9,13},{10,... | collective-permute-start | bytes 3225608 | tf_op jit(solution)/shard_map/ppermute | solution.py:430
  186.3 1.4 copy-start.5
  187.7 46.8 %collective-permute-start.17 = (bf16[8,8,9600]{2,1,0:T(8,128)(2,1)S(1)}, bf16[8,8,9600]{2,1,0:T(8,128)(2,1)}, u32[]{:S(2)}, u32[]{:S(2)}) collective-permute-start(bf16[8,8,9600]{2,1,0:T(8,128)(2,1)S(1)} %copy-done.8), channel_id=1, source_target_pairs={{0,8},{1,9},{2,10},{3,11},{4,12},{5,13},{6,14},{7,15},{8,24},{9,25... | collective-permute-start | bytes 3686408 | tf_op jit(solution)/shard_map/ppermute | solution.py:430
  212.0 26.9 %collective-permute-start.20 = (bf16[7,8,9600]{2,1,0:T(8,128)(2,1)}, bf16[7,8,9600]{2,1,0:T(8,128)(2,1)S(1)}, u32[]{:S(2)}, u32[]{:S(2)}) collective-permute-start(bf16[7,8,9600]{2,1,0:T(8,128)(2,1)} %collective-permute-done.16.rest_1_), channel_id=1, source_target_pairs={{0,2},{1,3},{2,0},{3,1},{4,6},{5,7},{6,4},{7,5},{8,10},{9,11},{10,... | collective-permute-start | bytes 3225608 | tf_op jit(solution)/shard_map/ppermute | solution.py:430
  213.0 26.5 %collective-permute-start.21 = (bf16[7,8,9600]{2,1,0:T(8,128)(2,1)}, bf16[7,8,9600]{2,1,0:T(8,128)(2,1)}, u32[]{:S(2)}, u32[]{:S(2)}) collective-permute-start(bf16[7,8,9600]{2,1,0:T(8,128)(2,1)} %collective-permute-done.15.rest_0_), channel_id=1, source_target_pairs={{0,4},{1,5},{2,6},{3,7},{4,0},{5,1},{6,2},{7,3},{8,12},{9,13},{10,... | collective-permute-start | bytes 3225608 | tf_op jit(solution)/shard_map/ppermute | solution.py:430
  228.3 33.7 %collective-permute-start.23 = (bf16[7,8,9600]{2,1,0:T(8,128)(2,1)S(1)}, bf16[7,8,9600]{2,1,0:T(8,128)(2,1)}, u32[]{:S(2)}, u32[]{:S(2)}) collective-permute-start(bf16[7,8,9600]{2,1,0:T(8,128)(2,1)S(1)} %get-tuple-element.67), channel_id=1, source_target_pairs={{0,2},{1,3},{2,0},{3,1},{4,6},{5,7},{6,4},{7,5},{8,10},{9,11},{10,... | collective-permute-start | bytes 3225608 | tf_op jit(solution)/shard_map/ppermute | solution.py:430
  233.3 29.2 %collective-permute-start.24 = (bf16[7,8,9600]{2,1,0:T(8,128)(2,1)S(1)}, bf16[7,8,9600]{2,1,0:T(8,128)(2,1)}, u32[]{:S(2)}, u32[]{:S(2)}) collective-permute-start(bf16[7,8,9600]{2,1,0:T(8,128)(2,1)S(1)} %get-tuple-element.66), channel_id=1, source_target_pairs={{0,4},{1,5},{2,6},{3,7},{4,0},{5,1},{6,2},{7,3},{8,12},{9,13},{10,... | collective-permute-start | bytes 3225608 | tf_op jit(solution)/shard_map/ppermute | solution.py:430
  234.5 31.1 %collective-permute-start.22 = (bf16[8,8,9600]{2,1,0:T(8,128)(2,1)}, bf16[8,8,9600]{2,1,0:T(8,128)(2,1)S(1)}, u32[]{:S(2)}, u32[]{:S(2)}) collective-permute-start(bf16[8,8,9600]{2,1,0:T(8,128)(2,1)} %collective-permute-done.17.rest_2_), channel_id=1, source_target_pairs={{0,8},{1,9},{2,10},{3,11},{4,12},{5,13},{6,14},{7,15},{8,24},{9,25... | collective-permute-start | bytes 3686408 | tf_op jit(solution)/shard_map/ppermute | solution.py:430
  238.9 3.7 %copy-start.20 = (bf16[7,8,9600]{2,1,0:T(8,128)(2,1)}, bf16[7,8,9600]{2,1,0:T(8,128)(2,1)S(1)}, u32[]{:S(2)}) copy-start(bf16[7,8,9600]{2,1,0:T(8,128)(2,1)S(1)} %collective-permute-done.20.rest_5_) | copy-start | bytes 3225604
  239.5 45.5 %collective-permute-start.25 = (bf16[7,8,9600]{2,1,0:T(8,128)(2,1)S(1)}, bf16[7,8,9600]{2,1,0:T(8,128)(2,1)S(1)}, u32[]{:S(2)}, u32[]{:S(2)}) collective-permute-start(bf16[7,8,9600]{2,1,0:T(8,128)(2,1)S(1)} %get-tuple-element.66), channel_id=1, source_target_pairs={{0,2},{1,3},{2,0},{3,1},{4,6},{5,7},{6,4},{7,5},{8,10},{9,11},{10,... | collective-permute-start | bytes 3225608 | tf_op jit(solution)/shard_map/ppermute | solution.py:430
  241.1 44.5 %collective-permute-start.26 = (bf16[7,8,9600]{2,1,0:T(8,128)(2,1)S(1)}, bf16[7,8,9600]{2,1,0:T(8,128)(2,1)}, u32[]{:S(2)}, u32[]{:S(2)}) collective-permute-start(bf16[7,8,9600]{2,1,0:T(8,128)(2,1)S(1)} %get-tuple-element.67), channel_id=1, source_target_pairs={{0,4},{1,5},{2,6},{3,7},{4,0},{5,1},{6,2},{7,3},{8,12},{9,13},{10,... | collective-permute-start | bytes 3225608 | tf_op jit(solution)/shard_map/ppermute | solution.py:430
  262.5 42.3 %collective-permute-start.28 = (bf16[7,8,9600]{2,1,0:T(8,128)(2,1)}, bf16[7,8,9600]{2,1,0:T(8,128)(2,1)}, u32[]{:S(2)}, u32[]{:S(2)}) collective-permute-start(bf16[7,8,9600]{2,1,0:T(8,128)(2,1)} %collective-permute-done.24.rest_2_), channel_id=1, source_target_pairs={{0,2},{1,3},{2,0},{3,1},{4,6},{5,7},{6,4},{7,5},{8,10},{9,11},{10,... | collective-permute-start | bytes 3225608 | tf_op jit(solution)/shard_map/ppermute | solution.py:430
  264.1 41.3 %collective-permute-start.29 = (bf16[7,8,9600]{2,1,0:T(8,128)(2,1)}, bf16[7,8,9600]{2,1,0:T(8,128)(2,1)}, u32[]{:S(2)}, u32[]{:S(2)}) collective-permute-start(bf16[7,8,9600]{2,1,0:T(8,128)(2,1)} %collective-permute-done.23.rest_1_), channel_id=1, source_target_pairs={{0,4},{1,5},{2,6},{3,7},{4,0},{5,1},{6,2},{7,3},{8,12},{9,13},{10,... | collective-permute-start | bytes 3225608 | tf_op jit(solution)/shard_map/ppermute | solution.py:430
  265.6 20.0 %copy-start.14 = (bf16[8,8,9600]{2,1,0:T(8,128)(2,1)}, bf16[8,8,9600]{2,1,0:T(8,128)(2,1)S(1)}, u32[]{:S(2)}) copy-start(bf16[8,8,9600]{2,1,0:T(8,128)(2,1)S(1)} %collective-permute-done.22.rest_0_) | copy-start | bytes 3686404
  265.6 39.8 %collective-permute-start.27 = (bf16[8,8,9600]{2,1,0:T(8,128)(2,1)S(1)}, bf16[8,8,9600]{2,1,0:T(8,128)(2,1)S(1)}, u32[]{:S(2)}, u32[]{:S(2)}) collective-permute-start(bf16[8,8,9600]{2,1,0:T(8,128)(2,1)S(1)} %collective-permute-done.22.rest_0_), channel_id=1, source_target_pairs={{0,8},{1,9},{2,10},{3,11},{4,12},{5,13},{6,14},{7,15},{8,24},{9,25... | collective-permute-start | bytes 3686408 | tf_op jit(solution)/shard_map/ppermute | solution.py:430
  285.0 1.0 copy-start.21
  295.5 20.7 %copy-start.13 = (pred[32]{0:T(512)(128)(4,1)S(1)}, pred[32]{0:T(512)(128)(4,1)}, u32[]{:S(2)}) copy-start(pred[32]{0:T(512)(128)(4,1)} %broadcast_in_dim.39) | copy-start | bytes 100
  305.4 1.0 copy-start.15
Sparse Core Ops, SparseCore 0:
  8.9 62.0 all-gather.1

commit v8 on v7

--- a/solution.py
+++ b/solution.py
@@ -11,8 +11,9 @@
 
 R = 5
 GROUP = 16
-SHARES = (1, 7, 7, 1)
+SHARES = (1, 7, 6, 2)
 HEAD = 64
+LATER = 4
 WEIGHT = 8
 
 
@@ -419,7 +420,7 @@
     for i, messages in enumerate(rounds):
         behind = list(done[i - 2]) if i >= 2 else []
         if len(tables) <= len(ends) and i >= 2:
-            if i == min(ends[len(tables) - 1] + 4, total - 1) and ends[len(tables) - 1] <= i - 2:
+            if i == min(ends[len(tables) - 1] + LATER, total - 1) and ends[len(tables) - 1] <= i - 2:
                 score()
                 behind.append(tables[-1])
         done.append([])

time: 339 us -> 326 us (0.962)
  waiting for transfers between devices: 163 us -> 147 us
  Pallas kernels: 72.1 us -> 76 us
    ppermute x30, waiting for transfers between devices: 162 us -> 146 us  [body(): gather.blocks[target] = lax.ppermute(block, 'shard', gather.steps[axis])]
    pallas_call x5, Pallas kernels: 63.6 us -> 67.5 us  [pair_scores(): pl.pallas_call(functools.partial(pair_kernel, frames, idx_dev, k_count, b...]
    slice x5 -> x8, local copies, waits for them, and re-layouts: 9.34 us -> 11.3 us  [block(): parts = [self.block(k)[at:at + n] for k, at, n in self.pieces[key]]]
    unnamed x51 -> x37, local copies, waits for them, and re-layouts: 15.1 us -> 14.3 us
  transfers between devices with their start and end apart: 32 -> 32, of which waited for: 19 -> 19; matrix products, arithmetic and copies ran while one was open for 6% -> 8% of each run, Pallas kernels for 19% -> 21%
where the time goes in v8:
time: 326 us
  waiting for transfers between devices  147 us (45%)
  Pallas kernels  76 us (23%)
  starting transfers between devices  42.1 us (13%)
  local copies, waits for them, and re-layouts  31.5 us (10%)
  blocking collectives  14.9 us (5%)
  between operations  13.6 us (4%)
    ppermute x30, waiting for transfers between devices, body(): gather.blocks[target] = lax.ppermute(block, 'shard', gather.steps[axis])  146 us
    pallas_call x5, Pallas kernels, pair_scores(): pl.pallas_call(functools.partial(pair_kernel, frames, idx_dev, k_count, b...  67.5 us
    ppermute x30, starting transfers between devices, body(): gather.blocks[target] = lax.ppermute(block, 'shard', gather.steps[axis])  37.2 us
    all_to_all x1, blocking collectives, body(): lax.all_to_all(table.reshape(devices, pairs), 'shard', split_axis=0, conc...  14.9 us
    unnamed x37, local copies, waits for them, and re-layouts  14.3 us
    slice x8, local copies, waits for them, and re-layouts, block(): parts = [self.block(k)[at:at + n] for k, at, n in self.pieces[key]]  11.3 us
    pallas_call x1, Pallas kernels, head_matrices(): pl.pallas_call(head_kernel, out_shape=[jax.ShapeDtypeStruct(s, jnp.bfloat...  8.54 us
  transfers between devices with their start and end apart: 32, of which 19 were waited for; matrix products, arithmetic and copies ran while one was open for 8% of the time, Pallas kernels for 21%

profile of v8, /device:TPU:0, one launch (start us, length us, event | category | flops | bytes accessed | tf_op | source)
XLA Modules:
  0.0 325.5 jit_solution(3023841476454612589)
XLA Ops:
  6.5 0.7 all-gather.2.cloned.1.call-update
  7.3 1.0 copy-done.4
  8.2 1.6 fusion
  9.9 2.9 collective-permute-start
  12.8 1.5 collective-permute-start.1
  14.3 1.4 slice.55
  15.8 1.6 collective-permute-start.2
  19.1 8.5 %head_matrices.1 = (bf16[64,2048]{1,0:T(8,128)(2,1)S(1)}, bf16[512,1024]{1,0:T(8,128)(2,1)S(1)}, bf16[256,256]{1,0:T(8,128)(2,1)S(1)}) custom-call(bf16[9,1,32]{2,1,0:T(2,128)(2,1)S(1)} %reshape.74.one_w, bf16[9,32,64]{2,1,0:T(8,128)(2,1)S(1)} %bitcast.16, bf16[9,1,64]{2,1,0:T(2,128)(2,1)S(1)} %reshape.75.three_w), custom_call_target="tpu_custom_call" | custom-call | flops 1000000000 | bytes 3000000 | tf_op jit(solution)/shard_map/head_matrices/pallas_call | solution.py:87
  27.7 1.0 copy-done.1
  28.6 0.7 copy-done.2
  32.0 9.0 %collective-permute-done.rest_1_ = bf16[8,8,9600]{2,1,0:T(8,128)(2,1)} collective-permute-done((bf16[8,8,9600]{2,1,0:T(8,128)(2,1)}, bf16[8,8,9600]{2,1,0:T(8,128)(2,1)}, u32[]{:S(2)}, u32[]{:S(2)}) %collective-permute-start) | collective-permute-done | bytes 1228832 | tf_op jit(solution)/shard_map/ppermute | solution.py:431
  41.0 2.1 collective-permute-done.1.rest_2_
  43.9 4.9 %all-to-all-start = ((s32[32,1,128]{2,1,0:T(1,128)}), s32[32,1,128]{2,1,0:T(1,128)S(1)}, u32[]{:S(2)}, u32[]{:S(2)}) async-start(s32[32,1,128]{2,1,0:T(1,128)} %broadcast_in_dim.42), calls=%async_computation | async-start | bytes 32768 | tf_op jit(solution)/shard_map/all_to_all | solution.py:436
  48.8 1.8 collective-permute-start.5
  50.6 1.5 collective-permute-start.6
  52.1 1.6 slice_dynamic-update-slice_fusion.6
  53.7 15.9 %collective-permute-done.4.rest_5_ = bf16[8,8,9600]{2,1,0:T(8,128)(2,1)} collective-permute-done((bf16[8,8,9600]{2,1,0:T(8,128)(2,1)}, bf16[8,8,9600]{2,1,0:T(8,128)(2,1)}, u32[]{:S(2)}, u32[]{:S(2)}) %collective-permute-start.4) | collective-permute-done | bytes 1228832 | tf_op jit(solution)/shard_map/ppermute | solution.py:431
  69.6 1.6 slice_dynamic-update-slice_fusion.5
  71.2 1.6 collective-permute-start.7
  72.7 2.3 slice.70
  75.1 2.2 slice.71
  77.8 1.5 collective-permute-start.9
  79.3 14.4 %collective-permute-done.5.rest_6_ = bf16[8,8,9600]{2,1,0:T(8,128)(2,1)S(1)} collective-permute-done((bf16[8,8,9600]{2,1,0:T(8,128)(2,1)}, bf16[8,8,9600]{2,1,0:T(8,128)(2,1)S(1)}, u32[]{:S(2)}, u32[]{:S(2)}) %collective-permute-start.5) | collective-permute-done | bytes 1228832 | tf_op jit(solution)/shard_map/ppermute | solution.py:431
  93.7 2.1 collective-permute-done.6.rest_7_
  95.9 2.0 collective-permute-start.11
  98.5 0.8 slice_dynamic-update-slice_fusion.3
  99.3 1.7 slice_dynamic-update-slice_fusion.2
  101.0 1.7 slice_dynamic-update-slice_fusion.1
  102.7 13.0 %collective-permute-done.9.rest_2_ = bf16[6,8,9600]{2,1,0:T(8,128)(2,1)} collective-permute-done((bf16[6,8,9600]{2,1,0:T(8,128)(2,1)}, bf16[6,8,9600]{2,1,0:T(8,128)(2,1)}, u32[]{:S(2)}, u32[]{:S(2)}) %collective-permute-start.9) | collective-permute-done | bytes 921632 | tf_op jit(solution)/shard_map/ppermute | solution.py:431
  115.7 1.2 collective-permute-done.8.rest_1_
  116.9 2.1 collective-permute-start.13
  118.9 1.5 collective-permute-start.14
  120.5 1.6 collective-permute-start.12
  122.0 1.3 slice.72
  123.4 2.2 slice.73
  126.2 18.1 %phase_0.1.before_ref = f32[16,128]{1,0:T(8,128)} custom-call(s32[18]{0:T(128)} %pad_add_fusion.who_ref, s32[32,128]{1,0:T(8,128)} %bitcast.19, s32[77]{0:T(128)} %constant.49.clone.queries_ref, bf16[64,2048]{1,0:T(8,128)(2,1)} %copy-done.2, bf16[512,1024]{1,0:T(8,128)(2,1)} %copy-done.1, bf16[256,256]{1,0:T(8,128)(2,1)} %copy-done.3, ...), custom_call_target="tpu_custom_call" | custom-call | flops 100663296000 | bytes 39321600 | tf_op jit(solution)/shard_map/phase_0/pallas_call | solution.py:232
  144.4 1.4 collective-permute-start.15
  145.7 1.7 slice_dynamic-update-slice_fusion
  147.5 8.9 %collective-permute-done.13.rest_6_ = bf16[6,8,9600]{2,1,0:T(8,128)(2,1)} collective-permute-done((bf16[6,8,9600]{2,1,0:T(8,128)(2,1)}, bf16[6,8,9600]{2,1,0:T(8,128)(2,1)}, u32[]{:S(2)}, u32[]{:S(2)}) %collective-permute-start.13) | collective-permute-done | bytes 921632 | tf_op jit(solution)/shard_map/ppermute | solution.py:431
  156.4 5.4 %collective-permute-done.14.rest_7_ = bf16[7,8,9600]{2,1,0:T(8,128)(2,1)} collective-permute-done((bf16[7,8,9600]{2,1,0:T(8,128)(2,1)}, bf16[7,8,9600]{2,1,0:T(8,128)(2,1)}, u32[]{:S(2)}, u32[]{:S(2)}) %collective-permute-start.14) | collective-permute-done | bytes 1075232 | tf_op jit(solution)/shard_map/ppermute | solution.py:431
  161.8 2.0 collective-permute-start.19
  164.4 1.1 copy-done.5
  165.5 1.2 collective-permute-start.17
  166.7 14.8 %collective-permute-done.16.rest_1_ = bf16[6,8,9600]{2,1,0:T(8,128)(2,1)} collective-permute-done((bf16[6,8,9600]{2,1,0:T(8,128)(2,1)}, bf16[6,8,9600]{2,1,0:T(8,128)(2,1)}, u32[]{:S(2)}, u32[]{:S(2)}) %collective-permute-start.16) | collective-permute-done | bytes 921632 | tf_op jit(solution)/shard_map/ppermute | solution.py:431
  181.5 2.0 collective-permute-start.21
  183.6 13.6 %phase_1.1.before_ref = f32[16,128]{1,0:T(8,128)} custom-call(s32[18]{0:T(128)} %pad_add_fusion.who_ref, s32[32,128]{1,0:T(8,128)} %bitcast.20, s32[65]{0:T(128)} %constant.50.clone.queries_ref, bf16[64,2048]{1,0:T(8,128)(2,1)} %copy-done.2, bf16[512,1024]{1,0:T(8,128)(2,1)} %copy-done.1, bf16[256,256]{1,0:T(8,128)(2,1)} %copy-done.3, ...), custom_call_target="tpu_custom_call" | custom-call | flops 100663296000 | bytes 39321600 | tf_op jit(solution)/shard_map/phase_1/pallas_call | solution.py:232
  197.1 2.0 collective-permute-done.18.rest_3_
  199.2 5.4 %collective-permute-done.19.rest_4_ = bf16[7,8,9600]{2,1,0:T(8,128)(2,1)} collective-permute-done((bf16[7,8,9600]{2,1,0:T(8,128)(2,1)S(1)}, bf16[7,8,9600]{2,1,0:T(8,128)(2,1)}, u32[]{:S(2)}, u32[]{:S(2)}) %collective-permute-start.19) | collective-permute-done | bytes 1075232 | tf_op jit(solution)/shard_map/ppermute | solution.py:431
  204.6 2.0 collective-permute-start.24
  206.6 1.6 collective-permute-start.22
  208.2 10.7 %collective-permute-done.20.rest_5_ = bf16[6,8,9600]{2,1,0:T(8,128)(2,1)} collective-permute-done((bf16[6,8,9600]{2,1,0:T(8,128)(2,1)}, bf16[6,8,9600]{2,1,0:T(8,128)(2,1)}, u32[]{:S(2)}, u32[]{:S(2)}) %collective-permute-start.20) | collective-permute-done | bytes 921632 | tf_op jit(solution)/shard_map/ppermute | solution.py:431
  218.9 8.7 %collective-permute-done.21.rest_6_ = bf16[7,8,9600]{2,1,0:T(8,128)(2,1)} collective-permute-done((bf16[7,8,9600]{2,1,0:T(8,128)(2,1)}, bf16[7,8,9600]{2,1,0:T(8,128)(2,1)}, u32[]{:S(2)}, u32[]{:S(2)}) %collective-permute-start.21) | collective-permute-done | bytes 1075232 | tf_op jit(solution)/shard_map/ppermute | solution.py:431
  227.6 2.0 collective-permute-start.26
  229.6 13.9 %phase_2.1.before_ref = f32[16,128]{1,0:T(8,128)} custom-call(s32[18]{0:T(128)} %pad_add_fusion.who_ref, s32[32,128]{1,0:T(8,128)} %bitcast.21, s32[51]{0:T(128)} %constant.51.clone.queries_ref, bf16[64,2048]{1,0:T(8,128)(2,1)} %copy-done.2, bf16[512,1024]{1,0:T(8,128)(2,1)} %copy-done.1, bf16[256,256]{1,0:T(8,128)(2,1)} %copy-done.3, ...), custom_call_target="tpu_custom_call" | custom-call | flops 100663296000 | bytes 39321600 | tf_op jit(solution)/shard_map/phase_2/pallas_call | solution.py:232
  243.5 3.8 %collective-permute-done.24.rest_2_ = bf16[6,8,9600]{2,1,0:T(8,128)(2,1)} collective-permute-done((bf16[6,8,9600]{2,1,0:T(8,128)(2,1)S(1)}, bf16[6,8,9600]{2,1,0:T(8,128)(2,1)}, u32[]{:S(2)}, u32[]{:S(2)}) %collective-permute-start.24) | collective-permute-done | bytes 921632 | tf_op jit(solution)/shard_map/ppermute | solution.py:431
  247.4 2.0 collective-permute-start.29
  249.4 1.6 collective-permute-start.27
  251.0 10.7 %collective-permute-done.25.rest_3_ = bf16[6,8,9600]{2,1,0:T(8,128)(2,1)} collective-permute-done((bf16[6,8,9600]{2,1,0:T(8,128)(2,1)S(1)}, bf16[6,8,9600]{2,1,0:T(8,128)(2,1)}, u32[]{:S(2)}, u32[]{:S(2)}) %collective-permute-start.25) | collective-permute-done | bytes 921632 | tf_op jit(solution)/shard_map/ppermute | solution.py:431
  261.7 8.7 %collective-permute-done.26.rest_4_ = bf16[7,8,9600]{2,1,0:T(8,128)(2,1)} collective-permute-done((bf16[7,8,9600]{2,1,0:T(8,128)(2,1)S(1)}, bf16[7,8,9600]{2,1,0:T(8,128)(2,1)}, u32[]{:S(2)}, u32[]{:S(2)}) %collective-permute-start.26) | collective-permute-done | bytes 1075232 | tf_op jit(solution)/shard_map/ppermute | solution.py:431
  270.4 12.9 %phase_3.1.before_ref = f32[16,128]{1,0:T(8,128)} custom-call(s32[18]{0:T(128)} %pad_add_fusion.who_ref, s32[32,128]{1,0:T(8,128)} %bitcast.22, s32[38]{0:T(128)} %constant.52.clone.queries_ref, bf16[64,2048]{1,0:T(8,128)(2,1)} %copy-done.2, bf16[512,1024]{1,0:T(8,128)(2,1)} %copy-done.1, bf16[256,256]{1,0:T(8,128)(2,1)} %copy-done.3, ...), custom_call_target="tpu_custom_call" | custom-call | flops 100663296000 | bytes 39321600 | tf_op jit(solution)/shard_map/phase_3/pallas_call | solution.py:232
  283.3 8.6 %collective-permute-done.29.rest_2_ = bf16[7,8,9600]{2,1,0:T(8,128)(2,1)} collective-permute-done((bf16[7,8,9600]{2,1,0:T(8,128)(2,1)}, bf16[7,8,9600]{2,1,0:T(8,128)(2,1)}, u32[]{:S(2)}, u32[]{:S(2)}) %collective-permute-start.29) | collective-permute-done | bytes 1075232 | tf_op jit(solution)/shard_map/ppermute | solution.py:431
  292.0 1.2 copy-done.14
  293.2 9.0 %phase_4.1 = f32[16,128]{1,0:T(8,128)} custom-call(s32[18]{0:T(128)} %pad_add_fusion.who_ref, s32[32,128]{1,0:T(8,128)} %bitcast.23, s32[25]{0:T(128)} %constant.53.clone.queries_ref, bf16[64,2048]{1,0:T(8,128)(2,1)} %copy-done.2, bf16[512,1024]{1,0:T(8,128)(2,1)} %copy-done.1, bf16[256,256]{1,0:T(8,128)(2,1)} %copy-done.3, f32[16,128]{1,0:T(8,128)} %phase_3.1.before_ref, ...), custom_call_target="tpu_custom_call" | custom-call | flops 50331648000 | bytes 19660800 | tf_op jit(solution)/shard_map/phase_4/pallas_call | solution.py:232
  303.0 14.9 %all_to_all.14 = f32[32,1,128]{2,1,0:T(1,128)S(1)} all-to-all(f32[32,1,128]{2,1,0:T(1,128)S(1)} %broadcast_select_fusion), channel_id=1, replica_groups=mesh['shard'=32] {'shard'}, dimensions={0} | all-to-all | bytes 32768 | tf_op jit(solution)/shard_map/all_to_all | solution.py:443
  (70 shorter events, 9.4 us)
Async XLA Ops:
  6.5 1.7 copy-start.4
  6.5 119.1 %all-gather.2.cloned.1.call-start = ((), (), s32[]{:S(2)}) async-start(), calls=%async_computation.2 | async-start | bytes 58982400 | tf_op jit(solution)/shard_map/all_gather | solution.py:373
  9.9 8.5 %copy-start.10 = (bf16[32,1,3,3]{0,3,2,1:T(4,128)(2,1)S(1)}, bf16[32,1,3,3]{0,3,2,1:T(4,128)(2,1)}, u32[]{:S(2)}) copy-start(bf16[32,1,3,3]{0,3,2,1:T(4,128)(2,1)} %param.15) | copy-start | bytes 1732
  9.9 8.5 %copy-start.11 = (bf16[1,64,3,3]{1,3,2,0:T(4,128)(2,1)S(1)}, bf16[1,64,3,3]{1,3,2,0:T(4,128)(2,1)}, u32[]{:S(2)}) copy-start(bf16[1,64,3,3]{1,3,2,0:T(4,128)(2,1)} %param.17) | copy-start | bytes 3460
  9.9 9.2 %copy-start = (bf16[64,32,3,3]{0,1,3,2:T(8,128)(2,1)S(1)}, bf16[64,32,3,3]{0,1,3,2:T(8,128)(2,1)}, u32[]{:S(2)}) copy-start(bf16[64,32,3,3]{0,1,3,2:T(8,128)(2,1)} %param.16) | copy-start | bytes 110596
  9.9 31.1 %collective-permute-start = (bf16[8,8,9600]{2,1,0:T(8,128)(2,1)}, bf16[8,8,9600]{2,1,0:T(8,128)(2,1)}, u32[]{:S(2)}, u32[]{:S(2)}) collective-permute-start(bf16[8,8,9600]{2,1,0:T(8,128)(2,1)} %get-tuple-element.38), channel_id=1, source_target_pairs={{0,2},{1,3},{2,0},{3,1},{4,6},{5,7},{6,4},{7,5},{8,10},{9,11},{10,... | collective-permute-start | bytes 3686408 | tf_op jit(solution)/shard_map/ppermute | solution.py:431
  12.8 30.3 %collective-permute-start.1 = (bf16[8,8,9600]{2,1,0:T(8,128)(2,1)}, bf16[8,8,9600]{2,1,0:T(8,128)(2,1)}, u32[]{:S(2)}, u32[]{:S(2)}) collective-permute-start(bf16[8,8,9600]{2,1,0:T(8,128)(2,1)} %get-tuple-element.39), channel_id=1, source_target_pairs={{0,4},{1,5},{2,6},{3,7},{4,0},{5,1},{6,2},{7,3},{8,12},{9,13},{10,... | collective-permute-start | bytes 3686408 | tf_op jit(solution)/shard_map/ppermute | solution.py:431
  15.8 55.4 %collective-permute-start.2 = (bf16[13,8,9600]{2,1,0:T(8,128)(2,1)}, bf16[13,8,9600]{2,1,0:T(8,128)(2,1)}, u32[]{:S(2)}, u32[]{:S(2)}) collective-permute-start(bf16[13,8,9600]{2,1,0:T(8,128)(2,1)} %slice.55), channel_id=1, source_target_pairs={{0,8},{1,9},{2,10},{3,11},{4,12},{5,13},{6,14},{7,15},{8,24},{9,25... | collective-permute-start | bytes 5990408 | tf_op jit(solution)/shard_map/ppermute | solution.py:431
  17.4 59.9 %collective-permute-start.3 = (bf16[8,8,9600]{2,1,0:T(8,128)(2,1)}, bf16[8,8,9600]{2,1,0:T(8,128)(2,1)}, u32[]{:S(2)}, u32[]{:S(2)}) collective-permute-start(bf16[8,8,9600]{2,1,0:T(8,128)(2,1)} %get-tuple-element.44), channel_id=1, source_target_pairs={{0,2},{1,3},{2,0},{3,1},{4,6},{5,7},{6,4},{7,5},{8,10},{9,11},{10,... | collective-permute-start | bytes 3686408 | tf_op jit(solution)/shard_map/ppermute | solution.py:431
  17.9 51.7 %collective-permute-start.4 = (bf16[8,8,9600]{2,1,0:T(8,128)(2,1)}, bf16[8,8,9600]{2,1,0:T(8,128)(2,1)}, u32[]{:S(2)}, u32[]{:S(2)}) collective-permute-start(bf16[8,8,9600]{2,1,0:T(8,128)(2,1)} %get-tuple-element.45), channel_id=1, source_target_pairs={{0,4},{1,5},{2,6},{3,7},{4,0},{5,1},{6,2},{7,3},{8,12},{9,13},{10,... | collective-permute-start | bytes 3686408 | tf_op jit(solution)/shard_map/ppermute | solution.py:431
  19.1 24.0 %copy-start.9 = (s32[16,8]{0,1:T(8,128)S(1)}, s32[16,8]{0,1:T(8,128)}, u32[]{:S(2)}) copy-start(s32[16,8]{0,1:T(8,128)} %param.14) | copy-start | bytes 1540
  27.7 1.0 copy-start.1
  28.6 0.7 copy-start.2
  29.3 0.7 copy-start.3
  43.9 81.7 %all-to-all-start = ((s32[32,1,128]{2,1,0:T(1,128)}), s32[32,1,128]{2,1,0:T(1,128)S(1)}, u32[]{:S(2)}, u32[]{:S(2)}) async-start(s32[32,1,128]{2,1,0:T(1,128)} %broadcast_in_dim.42), calls=%async_computation | async-start | bytes 32768 | tf_op jit(solution)/shard_map/all_to_all | solution.py:436
  48.8 44.9 %collective-permute-start.5 = (bf16[8,8,9600]{2,1,0:T(8,128)(2,1)}, bf16[8,8,9600]{2,1,0:T(8,128)(2,1)S(1)}, u32[]{:S(2)}, u32[]{:S(2)}) collective-permute-start(bf16[8,8,9600]{2,1,0:T(8,128)(2,1)} %collective-permute-done.1.rest_2_), channel_id=1, source_target_pairs={{0,2},{1,3},{2,0},{3,1},{4,6},{5,7},{6,4},{7,5},{8,10},{9,11},{10,... | collective-permute-start | bytes 3686408 | tf_op jit(solution)/shard_map/ppermute | solution.py:431
  50.6 45.2 %collective-permute-start.6 = (bf16[8,8,9600]{2,1,0:T(8,128)(2,1)}, bf16[8,8,9600]{2,1,0:T(8,128)(2,1)S(1)}, u32[]{:S(2)}, u32[]{:S(2)}) collective-permute-start(bf16[8,8,9600]{2,1,0:T(8,128)(2,1)} %collective-permute-done.rest_1_), channel_id=1, source_target_pairs={{0,4},{1,5},{2,6},{3,7},{4,0},{5,1},{6,2},{7,3},{8,12},{9,13},{10,... | collective-permute-start | bytes 3686408 | tf_op jit(solution)/shard_map/ppermute | solution.py:431
  71.2 49.3 %collective-permute-start.7 = (bf16[13,8,9600]{2,1,0:T(8,128)(2,1)}, bf16[13,8,9600]{2,1,0:T(8,128)(2,1)}, u32[]{:S(2)}, u32[]{:S(2)}) collective-permute-start(bf16[13,8,9600]{2,1,0:T(8,128)(2,1)} %collective-permute-done.2.rest_3_), channel_id=1, source_target_pairs={{0,8},{1,9},{2,10},{3,11},{4,12},{5,13},{6,14},{7,15},{8,24},{9,25... | collective-permute-start | bytes 5990408 | tf_op jit(solution)/shard_map/ppermute | solution.py:431
  77.2 39.6 %collective-permute-start.8 = (bf16[7,8,9600]{2,1,0:T(8,128)(2,1)}, bf16[7,8,9600]{2,1,0:T(8,128)(2,1)}, u32[]{:S(2)}, u32[]{:S(2)}) collective-permute-start(bf16[7,8,9600]{2,1,0:T(8,128)(2,1)} %slice.70), channel_id=1, source_target_pairs={{0,2},{1,3},{2,0},{3,1},{4,6},{5,7},{6,4},{7,5},{8,10},{9,11},{10,... | collective-permute-start | bytes 3225608 | tf_op jit(solution)/shard_map/ppermute | solution.py:431
  77.8 37.9 %collective-permute-start.9 = (bf16[6,8,9600]{2,1,0:T(8,128)(2,1)}, bf16[6,8,9600]{2,1,0:T(8,128)(2,1)}, u32[]{:S(2)}, u32[]{:S(2)}) collective-permute-start(bf16[6,8,9600]{2,1,0:T(8,128)(2,1)} %slice.71), channel_id=1, source_target_pairs={{0,4},{1,5},{2,6},{3,7},{4,0},{5,1},{6,2},{7,3},{8,12},{9,13},{10,... | collective-permute-start | bytes 2764808 | tf_op jit(solution)/shard_map/ppermute | solution.py:431
  93.7 29.7 %copy-start.6 = (bf16[8,8,9600]{2,1,0:T(8,128)(2,1)}, bf16[8,8,9600]{2,1,0:T(8,128)(2,1)S(1)}, u32[]{:S(2)}) copy-start(bf16[8,8,9600]{2,1,0:T(8,128)(2,1)S(1)} %collective-permute-done.5.rest_6_) | copy-start | bytes 3686404
  95.8 27.6 %copy-start.7 = (bf16[8,8,9600]{2,1,0:T(8,128)(2,1)}, bf16[8,8,9600]{2,1,0:T(8,128)(2,1)S(1)}, u32[]{:S(2)}) copy-start(bf16[8,8,9600]{2,1,0:T(8,128)(2,1)S(1)} %collective-permute-done.6.rest_7_) | copy-start | bytes 3686404
  95.8 48.5 %collective-permute-start.10 = (bf16[6,8,9600]{2,1,0:T(8,128)(2,1)}, bf16[6,8,9600]{2,1,0:T(8,128)(2,1)}, u32[]{:S(2)}, u32[]{:S(2)}) collective-permute-start(bf16[6,8,9600]{2,1,0:T(8,128)(2,1)} %slice.71), channel_id=1, source_target_pairs={{0,2},{1,3},{2,0},{3,1},{4,6},{5,7},{6,4},{7,5},{8,10},{9,11},{10,... | collective-permute-start | bytes 2764808 | tf_op jit(solution)/shard_map/ppermute | solution.py:431
  95.9 48.5 %collective-permute-start.11 = (bf16[7,8,9600]{2,1,0:T(8,128)(2,1)}, bf16[7,8,9600]{2,1,0:T(8,128)(2,1)}, u32[]{:S(2)}, u32[]{:S(2)}) collective-permute-start(bf16[7,8,9600]{2,1,0:T(8,128)(2,1)} %slice.70), channel_id=1, source_target_pairs={{0,4},{1,5},{2,6},{3,7},{4,0},{5,1},{6,2},{7,3},{8,12},{9,13},{10,... | collective-permute-start | bytes 3225608 | tf_op jit(solution)/shard_map/ppermute | solution.py:431
  116.9 39.5 %collective-permute-start.13 = (bf16[6,8,9600]{2,1,0:T(8,128)(2,1)}, bf16[6,8,9600]{2,1,0:T(8,128)(2,1)}, u32[]{:S(2)}, u32[]{:S(2)}) collective-permute-start(bf16[6,8,9600]{2,1,0:T(8,128)(2,1)} %collective-permute-done.9.rest_2_), channel_id=1, source_target_pairs={{0,2},{1,3},{2,0},{3,1},{4,6},{5,7},{6,4},{7,5},{8,10},{9,11},{10,... | collective-permute-start | bytes 2764808 | tf_op jit(solution)/shard_map/ppermute | solution.py:431
  118.9 42.8 %collective-permute-start.14 = (bf16[7,8,9600]{2,1,0:T(8,128)(2,1)}, bf16[7,8,9600]{2,1,0:T(8,128)(2,1)}, u32[]{:S(2)}, u32[]{:S(2)}) collective-permute-start(bf16[7,8,9600]{2,1,0:T(8,128)(2,1)} %collective-permute-done.8.rest_1_), channel_id=1, source_target_pairs={{0,4},{1,5},{2,6},{3,7},{4,0},{5,1},{6,2},{7,3},{8,12},{9,13},{10,... | collective-permute-start | bytes 3225608 | tf_op jit(solution)/shard_map/ppermute | solution.py:431
  120.5 43.8 %collective-permute-start.12 = (bf16[13,8,9600]{2,1,0:T(8,128)(2,1)}, bf16[13,8,9600]{2,1,0:T(8,128)(2,1)S(1)}, u32[]{:S(2)}, u32[]{:S(2)}) collective-permute-start(bf16[13,8,9600]{2,1,0:T(8,128)(2,1)} %collective-permute-done.7.rest_0_), channel_id=1, source_target_pairs={{0,8},{1,9},{2,10},{3,11},{4,12},{5,13},{6,14},{7,15},{8,24},{9,25... | collective-permute-start | bytes 5990408 | tf_op jit(solution)/shard_map/ppermute | solution.py:431
  125.6 0.6 copy-start.8
  144.4 37.1 %collective-permute-start.15 = (bf16[7,8,9600]{2,1,0:T(8,128)(2,1)S(1)}, bf16[7,8,9600]{2,1,0:T(8,128)(2,1)}, u32[]{:S(2)}, u32[]{:S(2)}) collective-permute-start(bf16[7,8,9600]{2,1,0:T(8,128)(2,1)S(1)} %slice.72), channel_id=1, source_target_pairs={{0,2},{1,3},{2,0},{3,1},{4,6},{5,7},{6,4},{7,5},{8,10},{9,11},{10,... | collective-permute-start | bytes 3225608 | tf_op jit(solution)/shard_map/ppermute | solution.py:431
  145.7 35.8 %collective-permute-start.16 = (bf16[6,8,9600]{2,1,0:T(8,128)(2,1)}, bf16[6,8,9600]{2,1,0:T(8,128)(2,1)}, u32[]{:S(2)}, u32[]{:S(2)}) collective-permute-start(bf16[6,8,9600]{2,1,0:T(8,128)(2,1)} %slice.73), channel_id=1, source_target_pairs={{0,4},{1,5},{2,6},{3,7},{4,0},{5,1},{6,2},{7,3},{8,12},{9,13},{10,... | collective-permute-start | bytes 2764808 | tf_op jit(solution)/shard_map/ppermute | solution.py:431
  161.8 37.4 %collective-permute-start.18 = (bf16[6,8,9600]{2,1,0:T(8,128)(2,1)}, bf16[6,8,9600]{2,1,0:T(8,128)(2,1)}, u32[]{:S(2)}, u32[]{:S(2)}) collective-permute-start(bf16[6,8,9600]{2,1,0:T(8,128)(2,1)} %slice.73), channel_id=1, source_target_pairs={{0,2},{1,3},{2,0},{3,1},{4,6},{5,7},{6,4},{7,5},{8,10},{9,11},{10,... | collective-permute-start | bytes 2764808 | tf_op jit(solution)/shard_map/ppermute | solution.py:431
  161.8 42.8 %collective-permute-start.19 = (bf16[7,8,9600]{2,1,0:T(8,128)(2,1)S(1)}, bf16[7,8,9600]{2,1,0:T(8,128)(2,1)}, u32[]{:S(2)}, u32[]{:S(2)}) collective-permute-start(bf16[7,8,9600]{2,1,0:T(8,128)(2,1)S(1)} %slice.72), channel_id=1, source_target_pairs={{0,4},{1,5},{2,6},{3,7},{4,0},{5,1},{6,2},{7,3},{8,12},{9,13},{10,... | collective-permute-start | bytes 3225608 | tf_op jit(solution)/shard_map/ppermute | solution.py:431
  164.2 1.3 copy-start.5
  165.5 41.1 %collective-permute-start.17 = (bf16[12,8,9600]{2,1,0:T(8,128)(2,1)}, bf16[12,8,9600]{2,1,0:T(8,128)(2,1)}, u32[]{:S(2)}, u32[]{:S(2)}) collective-permute-start(bf16[12,8,9600]{2,1,0:T(8,128)(2,1)} %slice_dynamic-update-slice_fusion), channel_id=1, source_target_pairs={{0,8},{1,9},{2,10},{3,11},{4,12},{5,13},{6,14},{7,15},{8,24},{9,25... | collective-permute-start | bytes 5529608 | tf_op jit(solution)/shard_map/ppermute | solution.py:431
  181.5 37.4 %collective-permute-start.20 = (bf16[6,8,9600]{2,1,0:T(8,128)(2,1)}, bf16[6,8,9600]{2,1,0:T(8,128)(2,1)}, u32[]{:S(2)}, u32[]{:S(2)}) collective-permute-start(bf16[6,8,9600]{2,1,0:T(8,128)(2,1)} %collective-permute-done.16.rest_1_), channel_id=1, source_target_pairs={{0,2},{1,3},{2,0},{3,1},{4,6},{5,7},{6,4},{7,5},{8,10},{9,11},{10,... | collective-permute-start | bytes 2764808 | tf_op jit(solution)/shard_map/ppermute | solution.py:431
  181.5 46.0 %collective-permute-start.21 = (bf16[7,8,9600]{2,1,0:T(8,128)(2,1)}, bf16[7,8,9600]{2,1,0:T(8,128)(2,1)}, u32[]{:S(2)}, u32[]{:S(2)}) collective-permute-start(bf16[7,8,9600]{2,1,0:T(8,128)(2,1)} %collective-permute-done.15.rest_0_), channel_id=1, source_target_pairs={{0,4},{1,5},{2,6},{3,7},{4,0},{5,1},{6,2},{7,3},{8,12},{9,13},{10,... | collective-permute-start | bytes 3225608 | tf_op jit(solution)/shard_map/ppermute | solution.py:431
  204.5 42.8 %collective-permute-start.23 = (bf16[7,8,9600]{2,1,0:T(8,128)(2,1)S(1)}, bf16[7,8,9600]{2,1,0:T(8,128)(2,1)}, u32[]{:S(2)}, u32[]{:S(2)}) collective-permute-start(bf16[7,8,9600]{2,1,0:T(8,128)(2,1)S(1)} %slice.80), channel_id=1, source_target_pairs={{0,2},{1,3},{2,0},{3,1},{4,6},{5,7},{6,4},{7,5},{8,10},{9,11},{10,... | collective-permute-start | bytes 3225608 | tf_op jit(solution)/shard_map/ppermute | solution.py:431
  204.6 42.8 %collective-permute-start.24 = (bf16[6,8,9600]{2,1,0:T(8,128)(2,1)S(1)}, bf16[6,8,9600]{2,1,0:T(8,128)(2,1)}, u32[]{:S(2)}, u32[]{:S(2)}) collective-permute-start(bf16[6,8,9600]{2,1,0:T(8,128)(2,1)S(1)} %slice.81), channel_id=1, source_target_pairs={{0,4},{1,5},{2,6},{3,7},{4,0},{5,1},{6,2},{7,3},{8,12},{9,13},{10,... | collective-permute-start | bytes 2764808 | tf_op jit(solution)/shard_map/ppermute | solution.py:431
  206.6 42.8 %collective-permute-start.22 = (bf16[12,8,9600]{2,1,0:T(8,128)(2,1)}, bf16[12,8,9600]{2,1,0:T(8,128)(2,1)S(1)}, u32[]{:S(2)}, u32[]{:S(2)}) collective-permute-start(bf16[12,8,9600]{2,1,0:T(8,128)(2,1)} %collective-permute-done.17.rest_2_), channel_id=1, source_target_pairs={{0,8},{1,9},{2,10},{3,11},{4,12},{5,13},{6,14},{7,15},{8,24},{9,25... | collective-permute-start | bytes 5529608 | tf_op jit(solution)/shard_map/ppermute | solution.py:431
  227.6 34.1 %collective-permute-start.25 = (bf16[6,8,9600]{2,1,0:T(8,128)(2,1)S(1)}, bf16[6,8,9600]{2,1,0:T(8,128)(2,1)}, u32[]{:S(2)}, u32[]{:S(2)}) collective-permute-start(bf16[6,8,9600]{2,1,0:T(8,128)(2,1)S(1)} %slice.81), channel_id=1, source_target_pairs={{0,2},{1,3},{2,0},{3,1},{4,6},{5,7},{6,4},{7,5},{8,10},{9,11},{10,... | collective-permute-start | bytes 2764808 | tf_op jit(solution)/shard_map/ppermute | solution.py:431
  227.6 42.8 %collective-permute-start.26 = (bf16[7,8,9600]{2,1,0:T(8,128)(2,1)S(1)}, bf16[7,8,9600]{2,1,0:T(8,128)(2,1)}, u32[]{:S(2)}, u32[]{:S(2)}) collective-permute-start(bf16[7,8,9600]{2,1,0:T(8,128)(2,1)S(1)} %slice.80), channel_id=1, source_target_pairs={{0,4},{1,5},{2,6},{3,7},{4,0},{5,1},{6,2},{7,3},{8,12},{9,13},{10,... | collective-permute-start | bytes 3225608 | tf_op jit(solution)/shard_map/ppermute | solution.py:431
  247.3 36.0 %collective-permute-start.28 = (bf16[6,8,9600]{2,1,0:T(8,128)(2,1)}, bf16[6,8,9600]{2,1,0:T(8,128)(2,1)}, u32[]{:S(2)}, u32[]{:S(2)}) collective-permute-start(bf16[6,8,9600]{2,1,0:T(8,128)(2,1)} %collective-permute-done.24.rest_2_), channel_id=1, source_target_pairs={{0,2},{1,3},{2,0},{3,1},{4,6},{5,7},{6,4},{7,5},{8,10},{9,11},{10,... | collective-permute-start | bytes 2764808 | tf_op jit(solution)/shard_map/ppermute | solution.py:431
  247.4 44.6 %collective-permute-start.29 = (bf16[7,8,9600]{2,1,0:T(8,128)(2,1)}, bf16[7,8,9600]{2,1,0:T(8,128)(2,1)}, u32[]{:S(2)}, u32[]{:S(2)}) collective-permute-start(bf16[7,8,9600]{2,1,0:T(8,128)(2,1)} %collective-permute-done.23.rest_1_), channel_id=1, source_target_pairs={{0,4},{1,5},{2,6},{3,7},{4,0},{5,1},{6,2},{7,3},{8,12},{9,13},{10,... | collective-permute-start | bytes 3225608 | tf_op jit(solution)/shard_map/ppermute | solution.py:431
  249.4 21.0 %copy-start.13 = (bf16[12,8,9600]{2,1,0:T(8,128)(2,1)}, bf16[12,8,9600]{2,1,0:T(8,128)(2,1)S(1)}, u32[]{:S(2)}) copy-start(bf16[12,8,9600]{2,1,0:T(8,128)(2,1)S(1)} %collective-permute-done.22.rest_0_) | copy-start | bytes 5529604
  249.4 42.6 %collective-permute-start.27 = (bf16[12,8,9600]{2,1,0:T(8,128)(2,1)S(1)}, bf16[12,8,9600]{2,1,0:T(8,128)(2,1)S(1)}, u32[]{:S(2)}, u32[]{:S(2)}) collective-permute-start(bf16[12,8,9600]{2,1,0:T(8,128)(2,1)S(1)} %collective-permute-done.22.rest_0_), channel_id=1, source_target_pairs={{0,8},{1,9},{2,10},{3,11},{4,12},{5,13},{6,14},{7,15},{8,24},{9,25... | collective-permute-start | bytes 5529608 | tf_op jit(solution)/shard_map/ppermute | solution.py:431
  283.3 19.5 %copy-start.12 = (pred[32]{0:T(512)(128)(4,1)S(1)}, pred[32]{0:T(512)(128)(4,1)}, u32[]{:S(2)}) copy-start(pred[32]{0:T(512)(128)(4,1)} %broadcast_in_dim.39) | copy-start | bytes 100
  292.0 1.2 copy-start.14
Sparse Core Ops, SparseCore 0:
  8.9 62.0 all-gather.1

commit v9 on v8

--- a/solution.py
+++ b/solution.py
@@ -96,12 +96,19 @@
     )(one_w, two_w, three_w)
 
 
-def pair_kernel(frames, idx_dev, k_count, bounds, scale, who_ref, ids_ref, queries_ref, one_ref,
-                two_ref, three_ref, before_ref, v_hbm, *rest):
+def pair_kernel(frames, idx_dev, k_count, bounds, scale, who_ref, ids_ref, queries_ref, before_ref,
+                one_hbm, two_hbm, three_hbm, own_hbm, other_hbm, *rest):
     buffers = len(bounds) - 1
     q_hbm, rest = rest[:buffers], rest[buffers:]
-    out_ref, q_in, v_in, q_rows, v_rows, maps, scores, list_ref, ends_ref, q_sem, v_sem = rest
-    width = v_hbm.shape[2] // R
+    (out_ref, q_in, v_in, q_rows, v_rows, maps, scores, one_ref, two_ref, three_ref, list_ref,
+     ends_ref, q_sem, v_sem, head_sem) = rest
+    heads = [
+        pltpu.make_async_copy(a, b, head_sem.at[i])
+        for i, (a, b) in enumerate(zip((one_hbm, two_hbm, three_hbm), (one_ref, two_ref, three_ref)))
+    ]
+    for copy in heads:
+        copy.start()
+    width = own_hbm.shape[2] // R
     side = GROUP * frames
     senders, pairs = out_ref.shape
     chip, core = who_ref[0], who_ref[1]
@@ -110,6 +117,7 @@
     bits = (chip_videos - 1).bit_length()
     assert chip_videos == 1 << bits and senders * pairs <= 1 << (23 - bits)
     begin = chip * chip_videos
+    turn = core * idx_dev
     count = jnp.int32(0)
     for b in range(buffers):
         def one_of(t, n):
@@ -120,7 +128,7 @@
             line = 2 * sender + core
             for k in range(k_count):
                 vid = ids_ref[line, first + k] - begin
-                list_ref[n] = base + (k << (8 + bits)) + (vid & (chip_videos - 1))
+                list_ref[n] = base + (k << (8 + bits)) + ((vid & (chip_videos - 1)) ^ turn)
                 n = n + ((vid >> bits) == 0).astype(jnp.int32)
             return n
         count = lax.fori_loop(bounds[b], bounds[b + 1], one_of, count)
@@ -145,7 +153,16 @@
 
         def one_video(p, _):
             vid = list_ref[first + p] & (chip_videos - 1)
-            pltpu.make_async_copy(v_hbm.at[vid], v_in.at[slot, p], v_sem.at[slot]).start()
+
+            @pl.when(vid < idx_dev)
+            def _():
+                pltpu.make_async_copy(own_hbm.at[vid], v_in.at[slot, p], v_sem.at[slot]).start()
+
+            @pl.when(vid >= idx_dev)
+            def _():
+                pltpu.make_async_copy(
+                    other_hbm.at[vid - idx_dev], v_in.at[slot, p], v_sem.at[slot]
+                ).start()
             return 0
         lax.fori_loop(0, GROUP, one_video, 0)
 
@@ -198,6 +215,9 @@
             best = jnp.maximum(best, x[:, i * n:(i + 1) * n])
         return jnp.maximum(best, 0.0).astype(jnp.bfloat16)
 
+    for copy in heads:
+        copy.wait()
+
     def head(g, _):
         here = pl.ds(pl.multiple_of(g * HEAD, HEAD), HEAD)
         first = pooled(dot(maps[here, :].astype(jnp.bfloat16), one_ref[...]))
@@ -221,8 +241,8 @@
     lax.fori_loop(0, count, write, 0)
 
 
-def pair_scores(blocks, videos, who, ids, queries, bounds, cap, heads, before, k_count, idx_dev, name):
-    frames, width = videos.shape[1], videos.shape[2]
+def pair_scores(blocks, own, other, who, ids, queries, bounds, cap, heads, before, k_count, idx_dev, name):
+    frames, width = own.shape[1], own.shape[2]
     pairs = before.shape[1]
     side = GROUP * frames
     scale = 1.0 / (math.sqrt(width // R) * R)
@@ -232,7 +252,7 @@
     return pl.pallas_call(
         functools.partial(pair_kernel, frames, idx_dev, k_count, bounds, scale),
         out_shape=jax.ShapeDtypeStruct(before.shape, jnp.float32),
-        in_specs=[smem] * 3 + [vmem] * 4 + [hbm] * (1 + len(blocks)),
+        in_specs=[smem] * 3 + [vmem] + [hbm] * (5 + len(blocks)),
         out_specs=vmem,
         scratch_shapes=[
             pltpu.VMEM((2, GROUP, frames, width), jnp.bfloat16),
@@ -241,10 +261,12 @@
             pltpu.VMEM((R * side, width // R), jnp.bfloat16),
             pltpu.VMEM((cap, frames * frames), jnp.float32),
             pltpu.VMEM((cap, pairs), jnp.float32),
+            *[pltpu.VMEM(h.shape, jnp.bfloat16) for h in heads],
             pltpu.SMEM((cap + GROUP,), jnp.int32),
             pltpu.SMEM((len(blocks),), jnp.int32),
             pltpu.SemaphoreType.DMA((2,)),
             pltpu.SemaphoreType.DMA((2,)),
+            pltpu.SemaphoreType.DMA((3,)),
         ],
         compiler_params=pltpu.CompilerParams(vmem_limit_bytes=58 * 1024 * 1024),
         cost_estimate=pl.CostEstimate(
@@ -252,7 +274,7 @@
             bytes_accessed=cap * frames * width * 4, transcendentals=0,
         ),
         name=name,
-    )(who, ids, queries, *heads, before, videos, *blocks)
+    )(who, ids, queries, before, *heads, own, other, *blocks)
 
 
 def chip_places(mesh):
@@ -370,10 +392,7 @@
             out += [(2 * i + c, 2 * where[tuple(to)] + c) for c in range(2)]
         return out
 
-    videos = lax.all_gather(
-        index_videos, "shard", axis=0, tiled=True,
-        axis_index_groups=[[2 * c, 2 * c + 1] for c in range(chips)],
-    )
+    other = lax.ppermute(index_videos, "shard", [(d, d ^ 1) for d in range(devices)])
     gather = Gather(sizes, [step_along(a) for a in range(3)], queries)
     rounds = gather.rounds
 
@@ -412,7 +431,7 @@
     def score():
         p = len(tables) - 1
         tables.append(pair_scores(
-            [gather.block(k) for k in phases[p]], videos, who, state["ids"], *contents(p), heads,
+            [gather.block(k) for k in phases[p]], index_videos, other, who, state["ids"], *contents(p), heads,
             tables[-1], k_count, idx_dev, "phase_" + str(p),
         ))
 
@@ -424,9 +443,16 @@
                 score()
                 behind.append(tables[-1])
         done.append([])
-        for together in ([m for m in messages if m[0]], [m for m in messages if not m[0]]):
+        flat = [m for m in messages if m[0]]
+        parts = [flat, [m for m in messages if not m[0]]]
+        if i in (1, 2):
+            parts = [flat[:1], flat[1:], parts[1]]
+        for at, together in enumerate(parts):
+            ties = list(behind)
+            if i == 2 and at == 1 or i == 3:
+                ties.append(other)
             sent = [gather.block(source) for _, source, _ in together]
-            sent = lax.optimization_barrier((*sent, *behind))[:len(sent)] if sent else []
+            sent = lax.optimization_barrier((*sent, *ties))[:len(sent)] if sent else []
             for (axis, _, target), block in zip(together, sent):
                 gather.blocks[target] = lax.ppermute(block, "shard", gather.steps[axis])
                 if axis:

time: 326 us -> 325 us (level)
  between operations: 13.6 us -> 0.19 us
  waiting for transfers between devices: 147 us -> 158 us
  starting transfers between devices: 42.1 us -> 45.8 us
    ppermute x30, waiting for transfers between devices: 146 us -> 158 us  [body(): gather.blocks[target] = lax.ppermute(block, 'shard', gather.steps[axis])]
    slice x8, local copies, waits for them, and re-layouts: 11.3 us -> 15.5 us  [block(): parts = [self.block(k)[at:at + n] for k, at, n in self.pieces[key]]]
    ppermute x30, starting transfers between devices: 37.2 us -> 40.5 us  [body(): gather.blocks[target] = lax.ppermute(block, 'shard', gather.steps[axis])]
    unnamed x37 -> x41, local copies, waits for them, and re-layouts: 14.3 us -> 12.1 us
  transfers between devices with their start and end apart: 32 -> 32, of which waited for: 19 -> 22; matrix products, arithmetic and copies ran while one was open for 8% -> 9% of each run, Pallas kernels for 21% -> 20%
where the time goes in v9:
time: 325 us; the launch traced here: 324 us
  waiting for transfers between devices  158 us (49%)
  Pallas kernels  73.6 us (23%)
  starting transfers between devices  45.8 us (14%)
  local copies, waits for them, and re-layouts  33.5 us (10%)
  blocking collectives  12.1 us (4%)
    ppermute x30, waiting for transfers between devices, body(): gather.blocks[target] = lax.ppermute(block, 'shard', gather.steps[axis])  158 us
    pallas_call x5, Pallas kernels, pair_scores(): pl.pallas_call(functools.partial(pair_kernel, frames, idx_dev, k_count, b...  65 us
    ppermute x30, starting transfers between devices, body(): gather.blocks[target] = lax.ppermute(block, 'shard', gather.steps[axis])  40.5 us
    slice x8, local copies, waits for them, and re-layouts, block(): parts = [self.block(k)[at:at + n] for k, at, n in self.pieces[key]]  15.5 us
    all_to_all x1, blocking collectives, body(): lax.all_to_all(table.reshape(devices, pairs), 'shard', split_axis=0, conc...  12.1 us
    unnamed x41, local copies, waits for them, and re-layouts  12.1 us
    pallas_call x1, Pallas kernels, head_matrices(): pl.pallas_call(head_kernel, out_shape=[jax.ShapeDtypeStruct(s, jnp.bfloat...  8.54 us
  transfers between devices with their start and end apart: 32, of which 22 were waited for; matrix products, arithmetic and copies ran while one was open for 9% of the time, Pallas kernels for 20%

profile of v9, /device:TPU:0, one launch (start us, length us, event | category | flops | bytes accessed | tf_op | source)
XLA Modules:
  0.0 324.2 jit_solution(6703124753077539937)
XLA Ops:
  0.5 3.5 %fusion = (bf16[8,8,9600]{2,1,0:T(8,128)(2,1)}, bf16[8,8,9600]{2,1,0:T(8,128)(2,1)}) fusion(bf16[16,8,9600]{2,1,0:T(8,128)(2,1)} %rest_0_.1), kind=kLoop, calls=%fused_computation.12 | loop fusion | bytes 4915200 | tf_op jit(solution)/shard_map/slice | solution.py:368
  3.9 2.5 collective-permute-start
  6.4 1.5 collective-permute-start.1
  7.9 1.5 slice.55
  9.4 1.6 collective-permute-start.3
  12.2 8.5 %head_matrices.1 = (bf16[64,2048]{1,0:T(8,128)(2,1)S(1)}, bf16[512,1024]{1,0:T(8,128)(2,1)S(1)}, bf16[256,256]{1,0:T(8,128)(2,1)S(1)}) custom-call(bf16[9,1,32]{2,1,0:T(2,128)(2,1)S(1)} %reshape.74.one_w, bf16[9,32,64]{2,1,0:T(8,128)(2,1)S(1)} %bitcast.16, bf16[9,1,64]{2,1,0:T(2,128)(2,1)S(1)} %reshape.75.three_w), custom_call_target="tpu_custom_call" | custom-call | flops 1000000000 | bytes 3000000 | tf_op jit(solution)/shard_map/head_matrices/pallas_call | solution.py:87
  20.7 1.0 copy-done.1
  25.1 9.5 %collective-permute-done.rest_1_ = bf16[8,8,9600]{2,1,0:T(8,128)(2,1)} collective-permute-done((bf16[8,8,9600]{2,1,0:T(8,128)(2,1)}, bf16[8,8,9600]{2,1,0:T(8,128)(2,1)}, u32[]{:S(2)}, u32[]{:S(2)}) %collective-permute-start) | collective-permute-done | bytes 1228832 | tf_op jit(solution)/shard_map/ppermute | solution.py:457
  34.6 2.0 collective-permute-start.5
  37.4 4.9 %all-to-all-start = ((s32[32,1,128]{2,1,0:T(1,128)}), s32[32,1,128]{2,1,0:T(1,128)S(1)}, u32[]{:S(2)}, u32[]{:S(2)}) async-start(s32[32,1,128]{2,1,0:T(1,128)} %broadcast_in_dim.42), calls=%async_computation | async-start | bytes 32768 | tf_op jit(solution)/shard_map/all_to_all | solution.py:462
  42.3 1.8 collective-permute-start.6
  44.1 1.6 slice_dynamic-update-slice_fusion.6
  45.7 10.3 %collective-permute-done.3.rest_3_ = bf16[13,8,9600]{2,1,0:T(8,128)(2,1)} collective-permute-done((bf16[13,8,9600]{2,1,0:T(8,128)(2,1)}, bf16[13,8,9600]{2,1,0:T(8,128)(2,1)}, u32[]{:S(2)}, u32[]{:S(2)}) %collective-permute-start.3) | collective-permute-done | bytes 1996832 | tf_op jit(solution)/shard_map/ppermute | solution.py:457
  56.0 0.9 collective-permute-start.8
  56.9 2.3 slice.70
  59.2 2.2 slice.71
  61.9 2.4 collective-permute-done.5.rest_5_
  64.4 2.4 collective-permute-start.9
  66.8 1.7 collective-permute-start.10
  68.5 1.6 slice_dynamic-update-slice_fusion.5
  70.1 31.4 %collective-permute-done.8.rest_0_ = bf16[13,8,9600]{2,1,0:T(8,128)(2,1)} collective-permute-done((bf16[13,8,9600]{2,1,0:T(8,128)(2,1)}, bf16[13,8,9600]{2,1,0:T(8,128)(2,1)}, u32[]{:S(2)}, u32[]{:S(2)}) %collective-permute-start.8) | collective-permute-done | bytes 1996832 | tf_op jit(solution)/shard_map/ppermute | solution.py:457
  101.5 2.3 slice.72
  103.8 1.2 slice.73
  105.1 4.6 %collective-permute-done.10.rest_2_ = bf16[6,8,9600]{2,1,0:T(8,128)(2,1)} collective-permute-done((bf16[6,8,9600]{2,1,0:T(8,128)(2,1)}, bf16[6,8,9600]{2,1,0:T(8,128)(2,1)}, u32[]{:S(2)}, u32[]{:S(2)}) %collective-permute-start.10) | collective-permute-done | bytes 921632 | tf_op jit(solution)/shard_map/ppermute | solution.py:457
  110.2 1.8 collective-permute-start.14
  112.0 1.5 collective-permute-start.15
  114.4 2.1 collective-permute-start.13
  117.9 1.7 slice_dynamic-update-slice_fusion.2
  120.2 17.4 %phase_0.1.before_ref = f32[16,128]{1,0:T(8,128)} custom-call(s32[18]{0:T(128)} %pad_add_fusion.who_ref, s32[32,128]{1,0:T(8,128)} %bitcast.19, s32[77]{0:T(128)} %constant.49.clone.queries_ref, f32[16,128]{1,0:T(8,128)} %broadcast_in_dim.43.before_ref, bf16[64,2048]{1,0:T(8,128)(2,1)} %copy-done.2, bf16[512,1024]{1,0:T(8,128)(2,1)} %copy-done.1, ...), custom_call_target="tpu_custom_call" | custom-call | flops 100663296000 | bytes 39321600 | tf_op jit(solution)/shard_map/phase_0/pallas_call | solution.py:252
  137.7 1.7 slice_dynamic-update-slice_fusion.1
  139.4 13.1 %collective-permute-done.11.rest_3_ = bf16[6,8,9600]{2,1,0:T(8,128)(2,1)} collective-permute-done((bf16[6,8,9600]{2,1,0:T(8,128)(2,1)}, bf16[6,8,9600]{2,1,0:T(8,128)(2,1)}, u32[]{:S(2)}, u32[]{:S(2)}) %collective-permute-start.11) | collective-permute-done | bytes 921632 | tf_op jit(solution)/shard_map/ppermute | solution.py:457
  152.5 7.9 %collective-permute-done.12.rest_4_ = bf16[7,8,9600]{2,1,0:T(8,128)(2,1)} collective-permute-done((bf16[7,8,9600]{2,1,0:T(8,128)(2,1)}, bf16[7,8,9600]{2,1,0:T(8,128)(2,1)}, u32[]{:S(2)}, u32[]{:S(2)}) %collective-permute-start.12) | collective-permute-done | bytes 1075232 | tf_op jit(solution)/shard_map/ppermute | solution.py:457
  160.8 1.6 collective-permute-start.17
  162.4 1.7 slice_dynamic-update-slice_fusion
  164.1 1.5 collective-permute-start.19
  166.1 18.2 %collective-permute-done.17.rest_1_ = bf16[6,8,9600]{2,1,0:T(8,128)(2,1)} collective-permute-done((bf16[6,8,9600]{2,1,0:T(8,128)(2,1)S(1)}, bf16[6,8,9600]{2,1,0:T(8,128)(2,1)}, u32[]{:S(2)}, u32[]{:S(2)}) %collective-permute-start.17) | collective-permute-done | bytes 921632 | tf_op jit(solution)/shard_map/ppermute | solution.py:457
  184.3 1.6 collective-permute-start.18
  185.9 1.2 collective-permute-done.16.rest_0_
  187.6 1.6 collective-permute-start.22
  189.2 13.7 %phase_1.1.before_ref = f32[16,128]{1,0:T(8,128)} custom-call(s32[18]{0:T(128)} %pad_add_fusion.who_ref, s32[32,128]{1,0:T(8,128)} %bitcast.20, s32[65]{0:T(128)} %constant.50.clone.queries_ref, f32[16,128]{1,0:T(8,128)} %phase_0.1.before_ref, bf16[64,2048]{1,0:T(8,128)(2,1)} %copy-done.2, bf16[512,1024]{1,0:T(8,128)(2,1)} %copy-done.1, ...), custom_call_target="tpu_custom_call" | custom-call | flops 100663296000 | bytes 39321600 | tf_op jit(solution)/shard_map/phase_1/pallas_call | solution.py:252
  202.9 1.3 slice.80
  204.2 1.2 slice.81
  205.5 1.4 collective-permute-done.19.rest_3_
  207.2 1.6 collective-permute-start.24
  208.8 1.5 collective-permute-start.25
  210.3 14.3 %collective-permute-done.18.rest_2_ = bf16[12,8,9600]{2,1,0:T(8,128)(2,1)} collective-permute-done((bf16[12,8,9600]{2,1,0:T(8,128)(2,1)}, bf16[12,8,9600]{2,1,0:T(8,128)(2,1)}, u32[]{:S(2)}, u32[]{:S(2)}) %collective-permute-start.18) | collective-permute-done | bytes 1843232 | tf_op jit(solution)/shard_map/ppermute | solution.py:457
  225.5 1.1 collective-permute-done.21.rest_5_
  226.6 3.8 %collective-permute-done.22.rest_6_ = bf16[7,8,9600]{2,1,0:T(8,128)(2,1)} collective-permute-done((bf16[7,8,9600]{2,1,0:T(8,128)(2,1)}, bf16[7,8,9600]{2,1,0:T(8,128)(2,1)}, u32[]{:S(2)}, u32[]{:S(2)}) %collective-permute-start.22) | collective-permute-done | bytes 1075232 | tf_op jit(solution)/shard_map/ppermute | solution.py:457
  230.4 1.6 collective-permute-start.26
  231.9 1.5 collective-permute-start.27
  233.4 12.8 %phase_2.1.before_ref = f32[16,128]{1,0:T(8,128)} custom-call(s32[18]{0:T(128)} %pad_add_fusion.who_ref, s32[32,128]{1,0:T(8,128)} %bitcast.21, s32[51]{0:T(128)} %constant.51.clone.queries_ref, f32[16,128]{1,0:T(8,128)} %phase_1.1.before_ref, bf16[64,2048]{1,0:T(8,128)(2,1)} %copy-done.2, bf16[512,1024]{1,0:T(8,128)(2,1)} %copy-done.1, ...), custom_call_target="tpu_custom_call" | custom-call | flops 100663296000 | bytes 39321600 | tf_op jit(solution)/shard_map/phase_2/pallas_call | solution.py:252
  246.2 3.8 %collective-permute-done.25.rest_2_ = bf16[6,8,9600]{2,1,0:T(8,128)(2,1)S(1)} collective-permute-done((bf16[6,8,9600]{2,1,0:T(8,128)(2,1)S(1)}, bf16[6,8,9600]{2,1,0:T(8,128)(2,1)S(1)}, u32[]{:S(2)}, u32[]{:S(2)}) %collective-permute-start.25) | collective-permute-done | bytes 921632 | tf_op jit(solution)/shard_map/ppermute | solution.py:457
  250.0 1.6 collective-permute-start.29
  251.6 1.5 collective-permute-start.30
  253.1 12.1 %collective-permute-done.23.rest_0_ = bf16[12,8,9600]{2,1,0:T(8,128)(2,1)S(1)} collective-permute-done((bf16[12,8,9600]{2,1,0:T(8,128)(2,1)}, bf16[12,8,9600]{2,1,0:T(8,128)(2,1)S(1)}, u32[]{:S(2)}, u32[]{:S(2)}) %collective-permute-start.23) | collective-permute-done | bytes 1843232 | tf_op jit(solution)/shard_map/ppermute | solution.py:457
  265.2 0.9 collective-permute-start.28
  266.1 3.2 collective-permute-done.26.rest_3_
  269.4 3.7 %collective-permute-done.27.rest_4_ = bf16[7,8,9600]{2,1,0:T(8,128)(2,1)S(1)} collective-permute-done((bf16[7,8,9600]{2,1,0:T(8,128)(2,1)S(1)}, bf16[7,8,9600]{2,1,0:T(8,128)(2,1)S(1)}, u32[]{:S(2)}, u32[]{:S(2)}) %collective-permute-start.27) | collective-permute-done | bytes 1075232 | tf_op jit(solution)/shard_map/ppermute | solution.py:457
  273.1 1.0 copy-done.15
  274.1 12.1 %phase_3.1.before_ref = f32[16,128]{1,0:T(8,128)} custom-call(s32[18]{0:T(128)} %pad_add_fusion.who_ref, s32[32,128]{1,0:T(8,128)} %bitcast.22, s32[38]{0:T(128)} %constant.52.clone.queries_ref, f32[16,128]{1,0:T(8,128)} %phase_2.1.before_ref, bf16[64,2048]{1,0:T(8,128)(2,1)} %copy-done.2, bf16[512,1024]{1,0:T(8,128)(2,1)} %copy-done.1, ...), custom_call_target="tpu_custom_call" | custom-call | flops 100663296000 | bytes 39321600 | tf_op jit(solution)/shard_map/phase_3/pallas_call | solution.py:252
  286.5 7.0 %collective-permute-done.30.rest_2_ = bf16[7,8,9600]{2,1,0:T(8,128)(2,1)} collective-permute-done((bf16[7,8,9600]{2,1,0:T(8,128)(2,1)}, bf16[7,8,9600]{2,1,0:T(8,128)(2,1)}, u32[]{:S(2)}, u32[]{:S(2)}) %collective-permute-start.30) | collective-permute-done | bytes 1075232 | tf_op jit(solution)/shard_map/ppermute | solution.py:457
  293.5 7.8 %collective-permute-done.28.rest_0_ = bf16[12,8,9600]{2,1,0:T(8,128)(2,1)} collective-permute-done((bf16[12,8,9600]{2,1,0:T(8,128)(2,1)S(1)}, bf16[12,8,9600]{2,1,0:T(8,128)(2,1)}, u32[]{:S(2)}, u32[]{:S(2)}) %collective-permute-start.28) | collective-permute-done | bytes 1843232 | tf_op jit(solution)/shard_map/ppermute | solution.py:457
  301.4 9.0 %phase_4.1 = f32[16,128]{1,0:T(8,128)} custom-call(s32[18]{0:T(128)} %pad_add_fusion.who_ref, s32[32,128]{1,0:T(8,128)} %bitcast.23, s32[25]{0:T(128)} %constant.53.clone.queries_ref, f32[16,128]{1,0:T(8,128)} %phase_3.1.before_ref, bf16[64,2048]{1,0:T(8,128)(2,1)} %copy-done.2, bf16[512,1024]{1,0:T(8,128)(2,1)} %copy-done.1, bf16[256,256]{1,0:T(8,128)(2,1)} %copy-done.3, ...), custom_call_target="tpu_custom_call" | custom-call | flops 50331648000 | bytes 19660800 | tf_op jit(solution)/shard_map/phase_4/pallas_call | solution.py:252
  311.2 12.1 %all_to_all.14 = f32[32,1,128]{2,1,0:T(1,128)S(1)} all-to-all(f32[32,1,128]{2,1,0:T(1,128)S(1)} %broadcast_select_fusion), channel_id=1, replica_groups=mesh['shard'=32] {'shard'}, dimensions={0} | all-to-all | bytes 32768 | tf_op jit(solution)/shard_map/all_to_all | solution.py:469
  (73 shorter events, 14.4 us)
Async XLA Ops:
  0.0 7.9 %copy-start.4 = (bf16[16,8,9600]{2,1,0:T(8,128)(2,1)S(1)}, bf16[16,8,9600]{2,1,0:T(8,128)(2,1)}, u32[]{:S(2)}) copy-start(bf16[16,8,9600]{2,1,0:T(8,128)(2,1)} %rest_0_.1) | copy-start | bytes 7372804
  0.0 61.4 %collective-permute-start.2 = (bf16[128,8,9600]{2,1,0:T(8,128)(2,1)}, bf16[128,8,9600]{2,1,0:T(8,128)(2,1)}, u32[]{:S(2)}, u32[]{:S(2)}) collective-permute-start(bf16[128,8,9600]{2,1,0:T(8,128)(2,1)} %own_hbm.9), channel_id=1, source_target_pairs={{0,1},{1,0},{2,3},{3,2},{4,5},{5,4},{6,7},{7,6},{8,9},{9,8},{10,11... | collective-permute-start | bytes 58982408 | tf_op jit(solution)/shard_map/ppermute | solution.py:395
  3.9 7.6 %copy-start.10 = (bf16[32,1,3,3]{0,3,2,1:T(4,128)(2,1)S(1)}, bf16[32,1,3,3]{0,3,2,1:T(4,128)(2,1)}, u32[]{:S(2)}) copy-start(bf16[32,1,3,3]{0,3,2,1:T(4,128)(2,1)} %param.15) | copy-start | bytes 1732
  3.9 7.6 %copy-start.11 = (bf16[1,64,3,3]{1,3,2,0:T(4,128)(2,1)S(1)}, bf16[1,64,3,3]{1,3,2,0:T(4,128)(2,1)}, u32[]{:S(2)}) copy-start(bf16[1,64,3,3]{1,3,2,0:T(4,128)(2,1)} %param.17) | copy-start | bytes 3460
  3.9 8.2 %copy-start = (bf16[64,32,3,3]{0,1,3,2:T(8,128)(2,1)S(1)}, bf16[64,32,3,3]{0,1,3,2:T(8,128)(2,1)}, u32[]{:S(2)}) copy-start(bf16[64,32,3,3]{0,1,3,2:T(8,128)(2,1)} %param.16) | copy-start | bytes 110596
  3.9 30.7 %collective-permute-start = (bf16[8,8,9600]{2,1,0:T(8,128)(2,1)}, bf16[8,8,9600]{2,1,0:T(8,128)(2,1)}, u32[]{:S(2)}, u32[]{:S(2)}) collective-permute-start(bf16[8,8,9600]{2,1,0:T(8,128)(2,1)} %get-tuple-element.36), channel_id=1, source_target_pairs={{0,2},{1,3},{2,0},{3,1},{4,6},{5,7},{6,4},{7,5},{8,10},{9,11},{10,... | collective-permute-start | bytes 3686408 | tf_op jit(solution)/shard_map/ppermute | solution.py:457
  6.4 30.2 %collective-permute-start.1 = (bf16[8,8,9600]{2,1,0:T(8,128)(2,1)}, bf16[8,8,9600]{2,1,0:T(8,128)(2,1)}, u32[]{:S(2)}, u32[]{:S(2)}) collective-permute-start(bf16[8,8,9600]{2,1,0:T(8,128)(2,1)} %get-tuple-element.37), channel_id=1, source_target_pairs={{0,4},{1,5},{2,6},{3,7},{4,0},{5,1},{6,2},{7,3},{8,12},{9,13},{10,... | collective-permute-start | bytes 3686408 | tf_op jit(solution)/shard_map/ppermute | solution.py:457
  9.4 46.6 %collective-permute-start.3 = (bf16[13,8,9600]{2,1,0:T(8,128)(2,1)}, bf16[13,8,9600]{2,1,0:T(8,128)(2,1)}, u32[]{:S(2)}, u32[]{:S(2)}) collective-permute-start(bf16[13,8,9600]{2,1,0:T(8,128)(2,1)} %slice.55), channel_id=1, source_target_pairs={{0,8},{1,9},{2,10},{3,11},{4,12},{5,13},{6,14},{7,15},{8,24},{9,25... | collective-permute-start | bytes 5990408 | tf_op jit(solution)/shard_map/ppermute | solution.py:457
  11.0 51.0 %collective-permute-start.4 = (bf16[8,8,9600]{2,1,0:T(8,128)(2,1)}, bf16[8,8,9600]{2,1,0:T(8,128)(2,1)}, u32[]{:S(2)}, u32[]{:S(2)}) collective-permute-start(bf16[8,8,9600]{2,1,0:T(8,128)(2,1)} %get-tuple-element.37), channel_id=1, source_target_pairs={{0,2},{1,3},{2,0},{3,1},{4,6},{5,7},{6,4},{7,5},{8,10},{9,11},{10,... | collective-permute-start | bytes 3686408 | tf_op jit(solution)/shard_map/ppermute | solution.py:457
  12.2 24.4 %copy-start.9 = (s32[16,8]{0,1:T(8,128)S(1)}, s32[16,8]{0,1:T(8,128)}, u32[]{:S(2)}) copy-start(s32[16,8]{0,1:T(8,128)} %param.14) | copy-start | bytes 1540
  20.7 1.0 copy-start.1
  21.8 0.7 copy-start.2
  22.5 0.6 copy-start.3
  34.6 29.8 %collective-permute-start.5 = (bf16[8,8,9600]{2,1,0:T(8,128)(2,1)}, bf16[8,8,9600]{2,1,0:T(8,128)(2,1)}, u32[]{:S(2)}, u32[]{:S(2)}) collective-permute-start(bf16[8,8,9600]{2,1,0:T(8,128)(2,1)} %get-tuple-element.36), channel_id=1, source_target_pairs={{0,4},{1,5},{2,6},{3,7},{4,0},{5,1},{6,2},{7,3},{8,12},{9,13},{10,... | collective-permute-start | bytes 3686408 | tf_op jit(solution)/shard_map/ppermute | solution.py:457
  37.4 82.3 %all-to-all-start = ((s32[32,1,128]{2,1,0:T(1,128)}), s32[32,1,128]{2,1,0:T(1,128)S(1)}, u32[]{:S(2)}, u32[]{:S(2)}) async-start(s32[32,1,128]{2,1,0:T(1,128)} %broadcast_in_dim.42), calls=%async_computation | async-start | bytes 32768 | tf_op jit(solution)/shard_map/all_to_all | solution.py:462
  42.3 71.2 %collective-permute-start.6 = (bf16[8,8,9600]{2,1,0:T(8,128)(2,1)}, bf16[8,8,9600]{2,1,0:T(8,128)(2,1)S(1)}, u32[]{:S(2)}, u32[]{:S(2)}) collective-permute-start(bf16[8,8,9600]{2,1,0:T(8,128)(2,1)} %collective-permute-done.1.rest_2_), channel_id=1, source_target_pairs={{0,2},{1,3},{2,0},{3,1},{4,6},{5,7},{6,4},{7,5},{8,10},{9,11},{10,... | collective-permute-start | bytes 3686408 | tf_op jit(solution)/shard_map/ppermute | solution.py:457
  56.0 45.5 %collective-permute-start.8 = (bf16[13,8,9600]{2,1,0:T(8,128)(2,1)}, bf16[13,8,9600]{2,1,0:T(8,128)(2,1)}, u32[]{:S(2)}, u32[]{:S(2)}) collective-permute-start(bf16[13,8,9600]{2,1,0:T(8,128)(2,1)} %collective-permute-done.3.rest_3_), channel_id=1, source_target_pairs={{0,8},{1,9},{2,10},{3,11},{4,12},{5,13},{6,14},{7,15},{8,24},{9,25... | collective-permute-start | bytes 5990408 | tf_op jit(solution)/shard_map/ppermute | solution.py:457
  61.4 52.1 %collective-permute-start.7 = (bf16[8,8,9600]{2,1,0:T(8,128)(2,1)}, bf16[8,8,9600]{2,1,0:T(8,128)(2,1)S(1)}, u32[]{:S(2)}, u32[]{:S(2)}) collective-permute-start(bf16[8,8,9600]{2,1,0:T(8,128)(2,1)} %collective-permute-done.rest_1_), channel_id=1, source_target_pairs={{0,4},{1,5},{2,6},{3,7},{4,0},{5,1},{6,2},{7,3},{8,12},{9,13},{10,... | collective-permute-start | bytes 3686408 | tf_op jit(solution)/shard_map/ppermute | solution.py:457
  64.4 45.8 %collective-permute-start.9 = (bf16[7,8,9600]{2,1,0:T(8,128)(2,1)}, bf16[7,8,9600]{2,1,0:T(8,128)(2,1)}, u32[]{:S(2)}, u32[]{:S(2)}) collective-permute-start(bf16[7,8,9600]{2,1,0:T(8,128)(2,1)} %slice.70), channel_id=1, source_target_pairs={{0,2},{1,3},{2,0},{3,1},{4,6},{5,7},{6,4},{7,5},{8,10},{9,11},{10,... | collective-permute-start | bytes 3225608 | tf_op jit(solution)/shard_map/ppermute | solution.py:457
  66.8 42.9 %collective-permute-start.10 = (bf16[6,8,9600]{2,1,0:T(8,128)(2,1)}, bf16[6,8,9600]{2,1,0:T(8,128)(2,1)}, u32[]{:S(2)}, u32[]{:S(2)}) collective-permute-start(bf16[6,8,9600]{2,1,0:T(8,128)(2,1)} %slice.71), channel_id=1, source_target_pairs={{0,4},{1,5},{2,6},{3,7},{4,0},{5,1},{6,2},{7,3},{8,12},{9,13},{10,... | collective-permute-start | bytes 2764808 | tf_op jit(solution)/shard_map/ppermute | solution.py:457
  110.2 53.9 %collective-permute-start.14 = (bf16[6,8,9600]{2,1,0:T(8,128)(2,1)}, bf16[6,8,9600]{2,1,0:T(8,128)(2,1)}, u32[]{:S(2)}, u32[]{:S(2)}) collective-permute-start(bf16[6,8,9600]{2,1,0:T(8,128)(2,1)} %collective-permute-done.10.rest_2_), channel_id=1, source_target_pairs={{0,2},{1,3},{2,0},{3,1},{4,6},{5,7},{6,4},{7,5},{8,10},{9,11},{10,... | collective-permute-start | bytes 2764808 | tf_op jit(solution)/shard_map/ppermute | solution.py:457
  112.0 52.1 %collective-permute-start.15 = (bf16[7,8,9600]{2,1,0:T(8,128)(2,1)}, bf16[7,8,9600]{2,1,0:T(8,128)(2,1)}, u32[]{:S(2)}, u32[]{:S(2)}) collective-permute-start(bf16[7,8,9600]{2,1,0:T(8,128)(2,1)} %collective-permute-done.9.rest_1_), channel_id=1, source_target_pairs={{0,4},{1,5},{2,6},{3,7},{4,0},{5,1},{6,2},{7,3},{8,12},{9,13},{10,... | collective-permute-start | bytes 3225608 | tf_op jit(solution)/shard_map/ppermute | solution.py:457
  113.5 4.4 %copy-start.6 = (bf16[8,8,9600]{2,1,0:T(8,128)(2,1)}, bf16[8,8,9600]{2,1,0:T(8,128)(2,1)S(1)}, u32[]{:S(2)}) copy-start(bf16[8,8,9600]{2,1,0:T(8,128)(2,1)S(1)} %collective-permute-done.6.rest_6_) | copy-start | bytes 3686404
  113.5 4.4 %copy-start.7 = (bf16[8,8,9600]{2,1,0:T(8,128)(2,1)}, bf16[8,8,9600]{2,1,0:T(8,128)(2,1)S(1)}, u32[]{:S(2)}) copy-start(bf16[8,8,9600]{2,1,0:T(8,128)(2,1)S(1)} %collective-permute-done.7.rest_7_) | copy-start | bytes 3686404
  113.5 39.0 %collective-permute-start.11 = (bf16[6,8,9600]{2,1,0:T(8,128)(2,1)}, bf16[6,8,9600]{2,1,0:T(8,128)(2,1)}, u32[]{:S(2)}, u32[]{:S(2)}) collective-permute-start(bf16[6,8,9600]{2,1,0:T(8,128)(2,1)} %slice.71), channel_id=1, source_target_pairs={{0,2},{1,3},{2,0},{3,1},{4,6},{5,7},{6,4},{7,5},{8,10},{9,11},{10,... | collective-permute-start | bytes 2764808 | tf_op jit(solution)/shard_map/ppermute | solution.py:457
  114.1 46.2 %collective-permute-start.12 = (bf16[7,8,9600]{2,1,0:T(8,128)(2,1)}, bf16[7,8,9600]{2,1,0:T(8,128)(2,1)}, u32[]{:S(2)}, u32[]{:S(2)}) collective-permute-start(bf16[7,8,9600]{2,1,0:T(8,128)(2,1)} %slice.70), channel_id=1, source_target_pairs={{0,4},{1,5},{2,6},{3,7},{4,0},{5,1},{6,2},{7,3},{8,12},{9,13},{10,... | collective-permute-start | bytes 3225608 | tf_op jit(solution)/shard_map/ppermute | solution.py:457
  114.4 73.2 %collective-permute-start.13 = (bf16[13,8,9600]{2,1,0:T(8,128)(2,1)}, bf16[13,8,9600]{2,1,0:T(8,128)(2,1)}, u32[]{:S(2)}, u32[]{:S(2)}) collective-permute-start(bf16[13,8,9600]{2,1,0:T(8,128)(2,1)} %collective-permute-done.8.rest_0_), channel_id=1, source_target_pairs={{0,8},{1,9},{2,10},{3,11},{4,12},{5,13},{6,14},{7,15},{8,24},{9,25... | collective-permute-start | bytes 5990408 | tf_op jit(solution)/shard_map/ppermute | solution.py:457
  119.6 0.6 copy-start.8
  120.2 40.1 %copy-start.5 = (bf16[7,8,9600]{2,1,0:T(8,128)(2,1)S(1)}, bf16[7,8,9600]{2,1,0:T(8,128)(2,1)}, u32[]{:S(2)}) copy-start(bf16[7,8,9600]{2,1,0:T(8,128)(2,1)} %slice.72) | copy-start | bytes 3225604
  160.3 26.8 %collective-permute-start.16 = (bf16[7,8,9600]{2,1,0:T(8,128)(2,1)S(1)}, bf16[7,8,9600]{2,1,0:T(8,128)(2,1)}, u32[]{:S(2)}, u32[]{:S(2)}) collective-permute-start(bf16[7,8,9600]{2,1,0:T(8,128)(2,1)S(1)} %copy-done.5), channel_id=1, source_target_pairs={{0,2},{1,3},{2,0},{3,1},{4,6},{5,7},{6,4},{7,5},{8,10},{9,11},{10,... | collective-permute-start | bytes 3225608 | tf_op jit(solution)/shard_map/ppermute | solution.py:457
  160.8 23.5 %collective-permute-start.17 = (bf16[6,8,9600]{2,1,0:T(8,128)(2,1)S(1)}, bf16[6,8,9600]{2,1,0:T(8,128)(2,1)}, u32[]{:S(2)}, u32[]{:S(2)}) collective-permute-start(bf16[6,8,9600]{2,1,0:T(8,128)(2,1)S(1)} %slice.73), channel_id=1, source_target_pairs={{0,4},{1,5},{2,6},{3,7},{4,0},{5,1},{6,2},{7,3},{8,12},{9,13},{10,... | collective-permute-start | bytes 2764808 | tf_op jit(solution)/shard_map/ppermute | solution.py:457
  164.1 42.8 %collective-permute-start.19 = (bf16[6,8,9600]{2,1,0:T(8,128)(2,1)S(1)}, bf16[6,8,9600]{2,1,0:T(8,128)(2,1)}, u32[]{:S(2)}, u32[]{:S(2)}) collective-permute-start(bf16[6,8,9600]{2,1,0:T(8,128)(2,1)S(1)} %slice.73), channel_id=1, source_target_pairs={{0,2},{1,3},{2,0},{3,1},{4,6},{5,7},{6,4},{7,5},{8,10},{9,11},{10,... | collective-permute-start | bytes 2764808 | tf_op jit(solution)/shard_map/ppermute | solution.py:457
  165.6 41.6 %collective-permute-start.20 = (bf16[7,8,9600]{2,1,0:T(8,128)(2,1)S(1)}, bf16[7,8,9600]{2,1,0:T(8,128)(2,1)S(1)}, u32[]{:S(2)}, u32[]{:S(2)}) collective-permute-start(bf16[7,8,9600]{2,1,0:T(8,128)(2,1)S(1)} %copy-done.5), channel_id=1, source_target_pairs={{0,4},{1,5},{2,6},{3,7},{4,0},{5,1},{6,2},{7,3},{8,12},{9,13},{10,... | collective-permute-start | bytes 3225608 | tf_op jit(solution)/shard_map/ppermute | solution.py:457
  184.3 40.4 %collective-permute-start.18 = (bf16[12,8,9600]{2,1,0:T(8,128)(2,1)}, bf16[12,8,9600]{2,1,0:T(8,128)(2,1)}, u32[]{:S(2)}, u32[]{:S(2)}) collective-permute-start(bf16[12,8,9600]{2,1,0:T(8,128)(2,1)} %slice_dynamic-update-slice_fusion), channel_id=1, source_target_pairs={{0,8},{1,9},{2,10},{3,11},{4,12},{5,13},{6,14},{7,15},{8,24},{9,25... | collective-permute-start | bytes 5529608 | tf_op jit(solution)/shard_map/ppermute | solution.py:457
  187.1 39.5 %collective-permute-start.21 = (bf16[6,8,9600]{2,1,0:T(8,128)(2,1)}, bf16[6,8,9600]{2,1,0:T(8,128)(2,1)}, u32[]{:S(2)}, u32[]{:S(2)}) collective-permute-start(bf16[6,8,9600]{2,1,0:T(8,128)(2,1)} %collective-permute-done.17.rest_1_), channel_id=1, source_target_pairs={{0,2},{1,3},{2,0},{3,1},{4,6},{5,7},{6,4},{7,5},{8,10},{9,11},{10,... | collective-permute-start | bytes 2764808 | tf_op jit(solution)/shard_map/ppermute | solution.py:457
  187.6 42.8 %collective-permute-start.22 = (bf16[7,8,9600]{2,1,0:T(8,128)(2,1)}, bf16[7,8,9600]{2,1,0:T(8,128)(2,1)}, u32[]{:S(2)}, u32[]{:S(2)}) collective-permute-start(bf16[7,8,9600]{2,1,0:T(8,128)(2,1)} %collective-permute-done.16.rest_0_), channel_id=1, source_target_pairs={{0,4},{1,5},{2,6},{3,7},{4,0},{5,1},{6,2},{7,3},{8,12},{9,13},{10,... | collective-permute-start | bytes 3225608 | tf_op jit(solution)/shard_map/ppermute | solution.py:457
  207.2 3.1 copy-start.14
  207.2 42.8 %collective-permute-start.24 = (bf16[7,8,9600]{2,1,0:T(8,128)(2,1)S(1)}, bf16[7,8,9600]{2,1,0:T(8,128)(2,1)}, u32[]{:S(2)}, u32[]{:S(2)}) collective-permute-start(bf16[7,8,9600]{2,1,0:T(8,128)(2,1)S(1)} %slice.80), channel_id=1, source_target_pairs={{0,2},{1,3},{2,0},{3,1},{4,6},{5,7},{6,4},{7,5},{8,10},{9,11},{10,... | collective-permute-start | bytes 3225608 | tf_op jit(solution)/shard_map/ppermute | solution.py:457
  208.8 41.2 %collective-permute-start.25 = (bf16[6,8,9600]{2,1,0:T(8,128)(2,1)S(1)}, bf16[6,8,9600]{2,1,0:T(8,128)(2,1)S(1)}, u32[]{:S(2)}, u32[]{:S(2)}) collective-permute-start(bf16[6,8,9600]{2,1,0:T(8,128)(2,1)S(1)} %slice.81), channel_id=1, source_target_pairs={{0,4},{1,5},{2,6},{3,7},{4,0},{5,1},{6,2},{7,3},{8,12},{9,13},{10,... | collective-permute-start | bytes 2764808 | tf_op jit(solution)/shard_map/ppermute | solution.py:457
  224.6 40.6 %collective-permute-start.23 = (bf16[12,8,9600]{2,1,0:T(8,128)(2,1)}, bf16[12,8,9600]{2,1,0:T(8,128)(2,1)S(1)}, u32[]{:S(2)}, u32[]{:S(2)}) collective-permute-start(bf16[12,8,9600]{2,1,0:T(8,128)(2,1)} %collective-permute-done.18.rest_2_), channel_id=1, source_target_pairs={{0,8},{1,9},{2,10},{3,11},{4,12},{5,13},{6,14},{7,15},{8,24},{9,25... | collective-permute-start | bytes 5529608 | tf_op jit(solution)/shard_map/ppermute | solution.py:457
  230.4 39.0 %collective-permute-start.26 = (bf16[6,8,9600]{2,1,0:T(8,128)(2,1)S(1)}, bf16[6,8,9600]{2,1,0:T(8,128)(2,1)}, u32[]{:S(2)}, u32[]{:S(2)}) collective-permute-start(bf16[6,8,9600]{2,1,0:T(8,128)(2,1)S(1)} %slice.81), channel_id=1, source_target_pairs={{0,2},{1,3},{2,0},{3,1},{4,6},{5,7},{6,4},{7,5},{8,10},{9,11},{10,... | collective-permute-start | bytes 2764808 | tf_op jit(solution)/shard_map/ppermute | solution.py:457
  231.9 41.1 %collective-permute-start.27 = (bf16[7,8,9600]{2,1,0:T(8,128)(2,1)S(1)}, bf16[7,8,9600]{2,1,0:T(8,128)(2,1)S(1)}, u32[]{:S(2)}, u32[]{:S(2)}) collective-permute-start(bf16[7,8,9600]{2,1,0:T(8,128)(2,1)S(1)} %slice.80), channel_id=1, source_target_pairs={{0,4},{1,5},{2,6},{3,7},{4,0},{5,1},{6,2},{7,3},{8,12},{9,13},{10,... | collective-permute-start | bytes 3225608 | tf_op jit(solution)/shard_map/ppermute | solution.py:457
  250.0 23.0 %copy-start.16 = (bf16[6,8,9600]{2,1,0:T(8,128)(2,1)}, bf16[6,8,9600]{2,1,0:T(8,128)(2,1)S(1)}, u32[]{:S(2)}) copy-start(bf16[6,8,9600]{2,1,0:T(8,128)(2,1)S(1)} %collective-permute-done.25.rest_2_) | copy-start | bytes 2764804
  250.0 36.5 %collective-permute-start.29 = (bf16[6,8,9600]{2,1,0:T(8,128)(2,1)S(1)}, bf16[6,8,9600]{2,1,0:T(8,128)(2,1)}, u32[]{:S(2)}, u32[]{:S(2)}) collective-permute-start(bf16[6,8,9600]{2,1,0:T(8,128)(2,1)S(1)} %collective-permute-done.25.rest_2_), channel_id=1, source_target_pairs={{0,2},{1,3},{2,0},{3,1},{4,6},{5,7},{6,4},{7,5},{8,10},{9,11},{10,... | collective-permute-start | bytes 2764808 | tf_op jit(solution)/shard_map/ppermute | solution.py:457
  251.6 42.0 %collective-permute-start.30 = (bf16[7,8,9600]{2,1,0:T(8,128)(2,1)}, bf16[7,8,9600]{2,1,0:T(8,128)(2,1)}, u32[]{:S(2)}, u32[]{:S(2)}) collective-permute-start(bf16[7,8,9600]{2,1,0:T(8,128)(2,1)} %collective-permute-done.24.rest_1_), channel_id=1, source_target_pairs={{0,4},{1,5},{2,6},{3,7},{4,0},{5,1},{6,2},{7,3},{8,12},{9,13},{10,... | collective-permute-start | bytes 3225608 | tf_op jit(solution)/shard_map/ppermute | solution.py:457
  265.2 7.9 %copy-start.13 = (bf16[12,8,9600]{2,1,0:T(8,128)(2,1)}, bf16[12,8,9600]{2,1,0:T(8,128)(2,1)S(1)}, u32[]{:S(2)}) copy-start(bf16[12,8,9600]{2,1,0:T(8,128)(2,1)S(1)} %collective-permute-done.23.rest_0_) | copy-start | bytes 5529604
  265.2 36.2 %collective-permute-start.28 = (bf16[12,8,9600]{2,1,0:T(8,128)(2,1)S(1)}, bf16[12,8,9600]{2,1,0:T(8,128)(2,1)}, u32[]{:S(2)}, u32[]{:S(2)}) collective-permute-start(bf16[12,8,9600]{2,1,0:T(8,128)(2,1)S(1)} %collective-permute-done.23.rest_0_), channel_id=1, source_target_pairs={{0,8},{1,9},{2,10},{3,11},{4,12},{5,13},{6,14},{7,15},{8,24},{9,25... | collective-permute-start | bytes 5529608 | tf_op jit(solution)/shard_map/ppermute | solution.py:457
  273.1 1.0 copy-start.15
  286.1 25.0 %copy-start.12 = (pred[32]{0:T(512)(128)(4,1)S(1)}, pred[32]{0:T(512)(128)(4,1)}, u32[]{:S(2)}) copy-start(pred[32]{0:T(512)(128)(4,1)} %broadcast_in_dim.39) | copy-start | bytes 100

commit v10 on v8

--- a/solution.py
+++ b/solution.py
@@ -96,55 +96,78 @@
     )(one_w, two_w, three_w)
 
 
-def pair_kernel(frames, idx_dev, k_count, bounds, scale, who_ref, ids_ref, queries_ref, one_ref,
-                two_ref, three_ref, before_ref, v_hbm, *rest):
-    buffers = len(bounds) - 1
+def list_kernel(idx_dev, k_count, pairs, bounds, who_ref, ids_ref, queries_ref, *lists):
+    chip, core = who_ref[0], who_ref[1]
+    bits = chip_bits(idx_dev)
+    begin = chip << bits
+    for p, list_ref in enumerate(lists):
+        buffers = len(bounds[p]) - 1
+        at = jnp.int32(buffers)
+        for b in range(buffers):
+            def one_of(t, n):
+                packed = queries_ref[t]
+                row, first = packed & 255, ((packed >> 8) & 255) * k_count
+                sender = who_ref[2 + (packed >> 16)]
+                base = ((sender * pairs + first) << (8 + bits)) + (row << bits)
+                line = 2 * sender + core
+                for k in range(k_count):
+                    vid = ids_ref[line, first + k] - begin
+                    list_ref[n] = base + (k << (8 + bits)) + (vid & ((1 << bits) - 1))
+                    n = n + ((vid >> bits) == 0).astype(jnp.int32)
+                return n
+            at = lax.fori_loop(bounds[p][b], bounds[p][b + 1], one_of, at)
+            list_ref[b] = at - buffers
+        for i in range(GROUP):
+            list_ref[at + i] = 0
+
+
+def chip_bits(idx_dev):
+    bits = (2 * idx_dev - 1).bit_length()
+    assert 2 * idx_dev == 1 << bits
+    return bits
+
+
+def pair_lists(who, ids, queries, bounds, caps, k_count, idx_dev):
+    smem = pl.BlockSpec(memory_space=pltpu.SMEM)
+    sizes = [len(b) - 1 + cap + GROUP for b, cap in zip(bounds, caps)]
+    return pl.pallas_call(
+        functools.partial(list_kernel, idx_dev, k_count, ids.shape[1], bounds),
+        out_shape=[jax.ShapeDtypeStruct((n,), jnp.int32) for n in sizes],
+        in_specs=[smem] * 3,
+        out_specs=[smem] * len(sizes),
+        cost_estimate=pl.CostEstimate(flops=10**7, bytes_accessed=10**6, transcendentals=0),
+        name="pair_lists",
+    )(who, ids, queries)
+
+
+def pair_kernel(frames, idx_dev, buffers, scale, list_ref, one_ref, two_ref, three_ref, before_ref,
+                v_hbm, *rest):
     q_hbm, rest = rest[:buffers], rest[buffers:]
-    out_ref, q_in, v_in, q_rows, v_rows, maps, scores, list_ref, ends_ref, q_sem, v_sem = rest
+    out_ref, q_in, v_in, q_rows, v_rows, maps, scores, q_sem, v_sem = rest
     width = v_hbm.shape[2] // R
     side = GROUP * frames
     senders, pairs = out_ref.shape
-    chip, core = who_ref[0], who_ref[1]
-
-    chip_videos = 2 * idx_dev
-    bits = (chip_videos - 1).bit_length()
-    assert chip_videos == 1 << bits and senders * pairs <= 1 << (23 - bits)
-    begin = chip * chip_videos
-    count = jnp.int32(0)
-    for b in range(buffers):
-        def one_of(t, n):
-            packed = queries_ref[t]
-            row, first = packed & 255, ((packed >> 8) & 255) * k_count
-            sender = who_ref[2 + (packed >> 16)]
-            base = ((sender * pairs + first) << (8 + bits)) + (row << bits)
-            line = 2 * sender + core
-            for k in range(k_count):
-                vid = ids_ref[line, first + k] - begin
-                list_ref[n] = base + (k << (8 + bits)) + (vid & (chip_videos - 1))
-                n = n + ((vid >> bits) == 0).astype(jnp.int32)
-            return n
-        count = lax.fori_loop(bounds[b], bounds[b + 1], one_of, count)
-        ends_ref[b] = count
-    for p in range(GROUP):
-        list_ref[count + p] = 0
+    bits = chip_bits(idx_dev)
+    assert senders * pairs <= 1 << (23 - bits)
+    count = list_ref[buffers - 1]
     groups = (count + GROUP - 1) // GROUP
 
     def fetch(step, slot):
         first = step * GROUP
         for b in range(buffers):
-            low = 0 if b == 0 else jnp.clip(ends_ref[b - 1] - first, 0, GROUP)
-            high = GROUP if b == buffers - 1 else jnp.clip(ends_ref[b] - first, 0, GROUP)
+            low = 0 if b == 0 else jnp.clip(list_ref[b - 1] - first, 0, GROUP)
+            high = GROUP if b == buffers - 1 else jnp.clip(list_ref[b] - first, 0, GROUP)
 
             def one_query(p, _):
                 pltpu.make_async_copy(
-                    q_hbm[b].at[(list_ref[first + p] >> bits) & 255], q_in.at[slot, p],
+                    q_hbm[b].at[(list_ref[buffers + first + p] >> bits) & 255], q_in.at[slot, p],
                     q_sem.at[slot],
                 ).start()
                 return 0
             lax.fori_loop(low, high, one_query, 0)
 
         def one_video(p, _):
-            vid = list_ref[first + p] & (chip_videos - 1)
+            vid = list_ref[buffers + first + p] & ((1 << bits) - 1)
             pltpu.make_async_copy(v_hbm.at[vid], v_in.at[slot, p], v_sem.at[slot]).start()
             return 0
         lax.fori_loop(0, GROUP, one_video, 0)
@@ -212,7 +235,7 @@
     out_ref[...] = before_ref[...]
 
     def write(i, _):
-        entry = list_ref[i] >> (8 + bits)
+        entry = list_ref[buffers + i] >> (8 + bits)
         at = pl.ds(lax.div(entry, pairs), 1)
         hit = iota((1, pairs), 1) == lax.rem(entry, pairs)
         out_ref[at, :] = jnp.where(hit, scores[pl.ds(i, 1), :], out_ref[at, :])
@@ -221,7 +244,7 @@
     lax.fori_loop(0, count, write, 0)
 
 
-def pair_scores(blocks, videos, who, ids, queries, bounds, cap, heads, before, k_count, idx_dev, name):
+def pair_scores(blocks, videos, pair_list, cap, heads, before, idx_dev, name):
     frames, width = videos.shape[1], videos.shape[2]
     pairs = before.shape[1]
     side = GROUP * frames
@@ -230,9 +253,9 @@
     vmem = pl.BlockSpec(memory_space=pltpu.VMEM)
     hbm = pl.BlockSpec(memory_space=pltpu.HBM)
     return pl.pallas_call(
-        functools.partial(pair_kernel, frames, idx_dev, k_count, bounds, scale),
+        functools.partial(pair_kernel, frames, idx_dev, len(blocks), scale),
         out_shape=jax.ShapeDtypeStruct(before.shape, jnp.float32),
-        in_specs=[smem] * 3 + [vmem] * 4 + [hbm] * (1 + len(blocks)),
+        in_specs=[smem] + [vmem] * 4 + [hbm] * (1 + len(blocks)),
         out_specs=vmem,
         scratch_shapes=[
             pltpu.VMEM((2, GROUP, frames, width), jnp.bfloat16),
@@ -241,8 +264,6 @@
             pltpu.VMEM((R * side, width // R), jnp.bfloat16),
             pltpu.VMEM((cap, frames * frames), jnp.float32),
             pltpu.VMEM((cap, pairs), jnp.float32),
-            pltpu.SMEM((cap + GROUP,), jnp.int32),
-            pltpu.SMEM((len(blocks),), jnp.int32),
             pltpu.SemaphoreType.DMA((2,)),
             pltpu.SemaphoreType.DMA((2,)),
         ],
@@ -252,7 +273,7 @@
             bytes_accessed=cap * frames * width * 4, transcendentals=0,
         ),
         name=name,
-    )(who, ids, queries, *heads, before, videos, *blocks)
+    )(pair_list, *heads, before, videos, *blocks)
 
 
 def chip_places(mesh):
@@ -343,7 +364,10 @@
 
     def block(self, key):
         if key not in self.blocks:
-            parts = [self.block(k)[at:at + n] for k, at, n in self.pieces[key]]
+            whole = [self.block(k) for k, _, _ in self.pieces[key]]
+            if len(whole) > 1:
+                whole = lax.optimization_barrier(whole)
+            parts = [b[at:at + n] for b, (_, at, n) in zip(whole, self.pieces[key])]
             self.blocks[key] = parts[0] if len(parts) == 1 else jnp.concatenate(parts, axis=0)
         return self.blocks[key]
 
@@ -392,18 +416,21 @@
         [jnp.stack([chip, core]), lax.dynamic_index_in_dim(jnp.asarray(back), chip, 0, keepdims=False)]
     )
 
-    def contents(p):
-        packed, bounds, found = [], [0], {}
-        for key in phases[p]:
+    contents, bounds, caps = [], [], []
+    for keys in phases:
+        found = {}
+        bounds.append([len(contents)])
+        for key in keys:
             row = 0
             for off, first, n in gather.cells[key]:
                 found[off] = found.get(off, 0) + n
                 for q in range(first, first + n):
-                    packed.append((offsets.index(off) << 16) + (q << 8) + row)
+                    contents.append((offsets.index(off) << 16) + (q << 8) + row)
                     row += 1
-            bounds.append(len(packed))
+            bounds[-1].append(len(contents))
         cap = sum(min(n * k_count, 2 * per_holder) for n in found.values())
-        return jnp.asarray(np.array(packed, np.int32)), bounds, -(-cap // HEAD) * HEAD
+        caps.append(-(-cap // HEAD) * HEAD)
+    contents = jnp.asarray(np.array(contents, np.int32))
 
     state = {}
     heads = head_matrices(conv_one, conv_two, conv_three)
@@ -412,8 +439,8 @@
     def score():
         p = len(tables) - 1
         tables.append(pair_scores(
-            [gather.block(k) for k in phases[p]], videos, who, state["ids"], *contents(p), heads,
-            tables[-1], k_count, idx_dev, "phase_" + str(p),
+            [gather.block(k) for k in phases[p]], videos, state["lists"][p], caps[p], heads,
+            tables[-1], idx_dev, "phase_" + str(p),
         ))
 
     done = []
@@ -433,10 +460,11 @@
                     done[i].append(gather.blocks[target])
         if i == 0:
             ids = lax.optimization_barrier((candidates, *done[0]))[0].reshape(1, pairs)
-            state["ids"] = lax.all_to_all(
+            ids = lax.all_to_all(
                 jnp.broadcast_to(ids, (devices, pairs)), "shard", split_axis=0, concat_axis=0,
                 tiled=True,
             )
+            state["lists"] = pair_lists(who, ids, contents, bounds, caps, k_count, idx_dev)
     while len(tables) <= len(ends):
         score()
     table = jnp.where(jnp.arange(2)[None, :, None] == core, tables[-1][:, None], 0.0)

time: 326 us -> 354 us (1.086)
  waiting for transfers between devices: 147 us -> 178 us
    all_to_all x1, waiting for transfers between devices: 0.01 us -> 30.7 us  [body(): lax.all_to_all(jnp.broadcast_to(ids, (devices, pairs)), 'shard', split_ax...]
    pallas_call x5 -> x6, Pallas kernels: 67.5 us -> 68.1 us  [the longest x5 54.2 us: pair_scores(): pl.pallas_call(functools.partial(pair_kernel, frames, idx_dev, len(blocks...]
  transfers between devices with their start and end apart: 32 -> 32, of which waited for: 19 -> 20; matrix products, arithmetic and copies ran while one was open for 8% -> 7% of each run, Pallas kernels for 21% -> 19%
where the time goes in v10:
time: 354 us; the launch traced here: 353 us
  waiting for transfers between devices  178 us (50%)
  Pallas kernels  76.7 us (22%)
  starting transfers between devices  40.9 us (12%)
  local copies, waits for them, and re-layouts  31.2 us (9%)
  between operations  13.6 us (4%)
  blocking collectives  11.8 us (3%)
    ppermute x30, waiting for transfers between devices, body(): gather.blocks[target] = lax.ppermute(block, 'shard', gather.steps[axis])  147 us
    pallas_call x5, Pallas kernels, pair_scores(): pl.pallas_call(functools.partial(pair_kernel, frames, idx_dev, len(blocks...  54.2 us
    ppermute x30, starting transfers between devices, body(): gather.blocks[target] = lax.ppermute(block, 'shard', gather.steps[axis])  36 us
    all_to_all x1, waiting for transfers between devices, body(): lax.all_to_all(jnp.broadcast_to(ids, (devices, pairs)), 'shard', split_ax...  30.7 us
    unnamed x37, local copies, waits for them, and re-layouts  16.5 us
    pallas_call x1, Pallas kernels, pair_lists(): pl.pallas_call(functools.partial(list_kernel, idx_dev, k_count, ids.shape...  13.9 us
    all_to_all x1, blocking collectives, body(): lax.all_to_all(table.reshape(devices, pairs), 'shard', split_axis=0, conc...  11.8 us
    slice x8, local copies, waits for them, and re-layouts, block(): parts = [b[at:at + n] for b, (_, at, n) in zip(whole, self.pieces[key])]  8.75 us
  transfers between devices with their start and end apart: 32, of which 20 were waited for; matrix products, arithmetic and copies ran while one was open for 7% of the time, Pallas kernels for 19%

profile of v10, /device:TPU:0, one launch (start us, length us, event | category | flops | bytes accessed | tf_op | source)
XLA Modules:
  0.0 353.3 jit_solution(7249534980877759109)
XLA Ops:
  6.5 0.7 all-gather.2.cloned.1.call-update
  7.3 1.0 copy-done.4
  8.2 1.6 fusion
  9.8 3.0 collective-permute-start
  12.8 1.5 collective-permute-start.1
  14.3 1.4 slice.53
  15.8 1.6 collective-permute-start.2
  18.4 22.6 %collective-permute-done.rest_1_ = bf16[8,8,9600]{2,1,0:T(8,128)(2,1)} collective-permute-done((bf16[8,8,9600]{2,1,0:T(8,128)(2,1)}, bf16[8,8,9600]{2,1,0:T(8,128)(2,1)}, u32[]{:S(2)}, u32[]{:S(2)}) %collective-permute-start) | collective-permute-done | bytes 1228832 | tf_op jit(solution)/shard_map/ppermute | solution.py:458
  41.0 2.1 collective-permute-done.1.rest_2_
  43.1 2.0 collective-permute-start.6
  45.2 0.7 dynamic-slice_bitcast_fusion
  47.3 4.9 %all-to-all-start = ((s32[32,1,128]{2,1,0:T(1,128)}), s32[32,1,128]{2,1,0:T(1,128)S(1)}, u32[]{:S(2)}, u32[]{:S(2)}) async-start(s32[32,1,128]{2,1,0:T(1,128)} %broadcast_in_dim.42), calls=%async_computation | async-start | bytes 32768 | tf_op jit(solution)/shard_map/all_to_all | solution.py:463
  52.3 8.5 %head_matrices.1 = (bf16[64,2048]{1,0:T(8,128)(2,1)S(1)}, bf16[512,1024]{1,0:T(8,128)(2,1)S(1)}, bf16[256,256]{1,0:T(8,128)(2,1)S(1)}) custom-call(bf16[9,1,32]{2,1,0:T(2,128)(2,1)S(1)} %reshape.74.one_w, bf16[9,32,64]{2,1,0:T(8,128)(2,1)S(1)} %bitcast.16, bf16[9,1,64]{2,1,0:T(2,128)(2,1)S(1)} %reshape.75.three_w), custom_call_target="tpu_custom_call" | custom-call | flops 1000000000 | bytes 3000000 | tf_op jit(solution)/shard_map/head_matrices/pallas_call | solution.py:87
  60.8 1.0 copy-done.1
  61.8 0.7 copy-done.2
  63.7 30.7 %all-to-all-done = s32[32,1,128]{2,1,0:T(1,128)S(1)} async-done(((s32[32,1,128]{2,1,0:T(1,128)}), s32[32,1,128]{2,1,0:T(1,128)S(1)}, u32[]{:S(2)}, u32[]{:S(2)}) %all-to-all-start) | async-done | bytes 16416 | tf_op jit(solution)/shard_map/all_to_all | solution.py:463
  95.0 13.9 %pair_lists.1 = (s32[152]{0:T(256)}, s32[152]{0:T(256)}, s32[151]{0:T(256)}, s32[149]{0:T(256)}, s32[83]{0:T(128)}) custom-call(s32[18]{0:T(128)} %pad_add_fusion.who_ref, s32[32,128]{1,0:T(8,128)} %bitcast.19, s32[256]{0:T(256)} %constant.41.clone.queries_ref), custom_call_target="tpu_custom_call" | custom-call | flops 10000000 | bytes 1000000 | tf_op jit(solution)/shard_map/pair_lists/pallas_call | solution.py:133
  109.0 1.1 slice.69
  110.1 1.6 collective-permute-start.9
  112.2 1.6 collective-permute-start.7
  113.8 1.5 collective-permute-start.10
  115.8 1.6 slice_dynamic-update-slice_fusion.7
  117.4 1.6 slice_dynamic-update-slice_fusion.6
  119.0 1.6 slice_dynamic-update-slice_fusion.5
  120.5 1.6 slice_dynamic-update-slice_fusion.4
  122.1 1.7 slice_dynamic-update-slice_fusion.3
  123.8 1.7 slice_dynamic-update-slice_fusion.2
  125.5 1.7 slice_dynamic-update-slice_fusion.1
  127.2 6.5 %collective-permute-done.9.rest_2_ = bf16[6,8,9600]{2,1,0:T(8,128)(2,1)} collective-permute-done((bf16[6,8,9600]{2,1,0:T(8,128)(2,1)}, bf16[6,8,9600]{2,1,0:T(8,128)(2,1)}, u32[]{:S(2)}, u32[]{:S(2)}) %collective-permute-start.9) | collective-permute-done | bytes 921632 | tf_op jit(solution)/shard_map/ppermute | solution.py:458
  133.8 4.6 %collective-permute-done.8.rest_1_ = bf16[7,8,9600]{2,1,0:T(8,128)(2,1)} collective-permute-done((bf16[7,8,9600]{2,1,0:T(8,128)(2,1)S(1)}, bf16[7,8,9600]{2,1,0:T(8,128)(2,1)}, u32[]{:S(2)}, u32[]{:S(2)}) %collective-permute-start.8) | collective-permute-done | bytes 1075232 | tf_op jit(solution)/shard_map/ppermute | solution.py:458
  139.0 1.1 collective-permute-start.14
  140.1 18.1 %collective-permute-done.7.rest_0_ = bf16[13,8,9600]{2,1,0:T(8,128)(2,1)} collective-permute-done((bf16[13,8,9600]{2,1,0:T(8,128)(2,1)S(1)}, bf16[13,8,9600]{2,1,0:T(8,128)(2,1)}, u32[]{:S(2)}, u32[]{:S(2)}) %collective-permute-start.7) | collective-permute-done | bytes 1996832 | tf_op jit(solution)/shard_map/ppermute | solution.py:458
  158.8 2.2 slice.71
  161.0 2.3 slice.70
  163.9 13.9 %phase_0.1.before_ref = f32[16,128]{1,0:T(8,128)} custom-call(s32[152]{0:T(256)} %get-tuple-element.61.list_ref, bf16[64,2048]{1,0:T(8,128)(2,1)} %copy-done.2, bf16[512,1024]{1,0:T(8,128)(2,1)} %copy-done.1, bf16[256,256]{1,0:T(8,128)(2,1)} %copy-done.3, f32[16,128]{1,0:T(8,128)} %broadcast_in_dim.43.before_ref, ...), custom_call_target="tpu_custom_call" | custom-call | flops 100663296000 | bytes 39321600 | tf_op jit(solution)/shard_map/phase_0/pallas_call | solution.py:255
  178.4 4.2 %collective-permute-start.15 = (bf16[7,8,9600]{2,1,0:T(8,128)(2,1)S(1)}, bf16[7,8,9600]{2,1,0:T(8,128)(2,1)}, u32[]{:S(2)}, u32[]{:S(2)}) collective-permute-start(bf16[7,8,9600]{2,1,0:T(8,128)(2,1)S(1)} %copy-done.7), channel_id=1, source_target_pairs={{0,2},{1,3},{2,0},{3,1},{4,6},{5,7},{6,4},{7,5},{8,10},{9,11},{10,... | collective-permute-start | bytes 3225608 | tf_op jit(solution)/shard_map/ppermute | solution.py:458
  182.6 1.7 slice_dynamic-update-slice_fusion
  184.5 18.8 %collective-permute-done.12.rest_5_ = bf16[13,8,9600]{2,1,0:T(8,128)(2,1)S(1)} collective-permute-done((bf16[13,8,9600]{2,1,0:T(8,128)(2,1)}, bf16[13,8,9600]{2,1,0:T(8,128)(2,1)S(1)}, u32[]{:S(2)}, u32[]{:S(2)}) %collective-permute-start.12) | collective-permute-done | bytes 1996832 | tf_op jit(solution)/shard_map/ppermute | solution.py:458
  203.4 1.2 copy-done.6
  204.6 0.9 collective-permute-start.17
  205.5 1.9 collective-permute-done.15.rest_0_
  207.4 2.0 collective-permute-start.20
  209.5 10.5 %phase_1.1.before_ref = f32[16,128]{1,0:T(8,128)} custom-call(s32[152]{0:T(256)} %get-tuple-element.60.list_ref, bf16[64,2048]{1,0:T(8,128)(2,1)} %copy-done.2, bf16[512,1024]{1,0:T(8,128)(2,1)} %copy-done.1, bf16[256,256]{1,0:T(8,128)(2,1)} %copy-done.3, f32[16,128]{1,0:T(8,128)} %phase_0.1.before_ref, ...), custom_call_target="tpu_custom_call" | custom-call | flops 100663296000 | bytes 39321600 | tf_op jit(solution)/shard_map/phase_1/pallas_call | solution.py:255
  220.0 7.2 %collective-permute-done.18.rest_3_ = bf16[6,8,9600]{2,1,0:T(8,128)(2,1)} collective-permute-done((bf16[6,8,9600]{2,1,0:T(8,128)(2,1)}, bf16[6,8,9600]{2,1,0:T(8,128)(2,1)}, u32[]{:S(2)}, u32[]{:S(2)}) %collective-permute-start.18) | collective-permute-done | bytes 921632 | tf_op jit(solution)/shard_map/ppermute | solution.py:458
  227.2 2.1 collective-permute-start.23
  229.3 16.2 %collective-permute-done.17.rest_2_ = bf16[12,8,9600]{2,1,0:T(8,128)(2,1)} collective-permute-done((bf16[12,8,9600]{2,1,0:T(8,128)(2,1)}, bf16[12,8,9600]{2,1,0:T(8,128)(2,1)}, u32[]{:S(2)}, u32[]{:S(2)}) %collective-permute-start.17) | collective-permute-done | bytes 1843232 | tf_op jit(solution)/shard_map/ppermute | solution.py:458
  245.6 0.8 collective-permute-start.22
  246.9 0.8 collective-permute-done.21.rest_6_
  247.7 2.7 collective-permute-start.25
  250.4 2.0 collective-permute-start.26
  252.4 11.3 %phase_2.1.before_ref = f32[16,128]{1,0:T(8,128)} custom-call(s32[151]{0:T(256)} %get-tuple-element.59.list_ref, bf16[64,2048]{1,0:T(8,128)(2,1)} %copy-done.2, bf16[512,1024]{1,0:T(8,128)(2,1)} %copy-done.1, bf16[256,256]{1,0:T(8,128)(2,1)} %copy-done.3, f32[16,128]{1,0:T(8,128)} %phase_1.1.before_ref, ...), custom_call_target="tpu_custom_call" | custom-call | flops 100663296000 | bytes 39321600 | tf_op jit(solution)/shard_map/phase_2/pallas_call | solution.py:255
  263.7 3.7 %collective-permute-done.24.rest_2_ = bf16[6,8,9600]{2,1,0:T(8,128)(2,1)} collective-permute-done((bf16[6,8,9600]{2,1,0:T(8,128)(2,1)S(1)}, bf16[6,8,9600]{2,1,0:T(8,128)(2,1)}, u32[]{:S(2)}, u32[]{:S(2)}) %collective-permute-start.24) | collective-permute-done | bytes 921632 | tf_op jit(solution)/shard_map/ppermute | solution.py:458
  267.5 2.3 collective-permute-done.23.rest_1_
  269.8 2.0 collective-permute-start.28
  272.1 14.0 %collective-permute-done.22.rest_0_ = bf16[12,8,9600]{2,1,0:T(8,128)(2,1)S(1)} collective-permute-done((bf16[12,8,9600]{2,1,0:T(8,128)(2,1)}, bf16[12,8,9600]{2,1,0:T(8,128)(2,1)S(1)}, u32[]{:S(2)}, u32[]{:S(2)}) %collective-permute-start.22) | collective-permute-done | bytes 1843232 | tf_op jit(solution)/shard_map/ppermute | solution.py:458
  286.2 0.9 collective-permute-start.27
  287.0 2.6 collective-permute-done.25.rest_3_
  289.7 0.8 collective-permute-done.26.rest_4_
  290.5 10.6 %phase_3.1.before_ref = f32[16,128]{1,0:T(8,128)} custom-call(s32[149]{0:T(256)} %get-tuple-element.58.list_ref, bf16[64,2048]{1,0:T(8,128)(2,1)} %copy-done.2, bf16[512,1024]{1,0:T(8,128)(2,1)} %copy-done.1, bf16[256,256]{1,0:T(8,128)(2,1)} %copy-done.3, f32[16,128]{1,0:T(8,128)} %phase_2.1.before_ref, ...), custom_call_target="tpu_custom_call" | custom-call | flops 100663296000 | bytes 39321600 | tf_op jit(solution)/shard_map/phase_3/pallas_call | solution.py:255
  301.1 6.1 %collective-permute-done.28.rest_1_ = bf16[6,8,9600]{2,1,0:T(8,128)(2,1)} collective-permute-done((bf16[6,8,9600]{2,1,0:T(8,128)(2,1)}, bf16[6,8,9600]{2,1,0:T(8,128)(2,1)}, u32[]{:S(2)}, u32[]{:S(2)}) %collective-permute-start.28) | collective-permute-done | bytes 921632 | tf_op jit(solution)/shard_map/ppermute | solution.py:458
  307.2 3.5 collective-permute-done.29.rest_2_
  310.7 14.5 %collective-permute-done.27.rest_0_ = bf16[12,8,9600]{2,1,0:T(8,128)(2,1)} collective-permute-done((bf16[12,8,9600]{2,1,0:T(8,128)(2,1)S(1)}, bf16[12,8,9600]{2,1,0:T(8,128)(2,1)}, u32[]{:S(2)}, u32[]{:S(2)}) %collective-permute-start.27) | collective-permute-done | bytes 1843232 | tf_op jit(solution)/shard_map/ppermute | solution.py:458
  325.2 7.9 %phase_4.1 = f32[16,128]{1,0:T(8,128)} custom-call(s32[83]{0:T(128)} %get-tuple-element.54.list_ref, bf16[64,2048]{1,0:T(8,128)(2,1)} %copy-done.2, bf16[512,1024]{1,0:T(8,128)(2,1)} %copy-done.1, bf16[256,256]{1,0:T(8,128)(2,1)} %copy-done.3, f32[16,128]{1,0:T(8,128)} %phase_3.1.before_ref, bf16[256,8,9600]{2,1,0:T(8,128)(2,1)} %all-gather.2.cloned.1.call-done.v_hbm, ...), custom_call_target="tpu_custom_call" | custom-call | flops 50331648000 | bytes 19660800 | tf_op jit(solution)/shard_map/phase_4/pallas_call | solution.py:255
  333.9 11.8 %all_to_all.14 = f32[32,1,128]{2,1,0:T(1,128)S(1)} all-to-all(f32[32,1,128]{2,1,0:T(1,128)S(1)} %broadcast_select_fusion), channel_id=1, replica_groups=mesh['shard'=32] {'shard'}, dimensions={0} | all-to-all | bytes 32768 | tf_op jit(solution)/shard_map/all_to_all | solution.py:471
  (71 shorter events, 10.7 us)
Async XLA Ops:
  6.5 1.7 copy-start.4
  6.5 156.8 %all-gather.2.cloned.1.call-start = ((), (), s32[]{:S(2)}) async-start(), calls=%async_computation.2 | async-start | bytes 58982400 | tf_op jit(solution)/shard_map/all_gather | solution.py:397
  9.8 35.3 %copy-start.10 = (bf16[32,1,3,3]{0,3,2,1:T(4,128)(2,1)S(1)}, bf16[32,1,3,3]{0,3,2,1:T(4,128)(2,1)}, u32[]{:S(2)}) copy-start(bf16[32,1,3,3]{0,3,2,1:T(4,128)(2,1)} %param.11) | copy-start | bytes 1732
  9.8 35.4 %copy-start.11 = (bf16[1,64,3,3]{1,3,2,0:T(4,128)(2,1)S(1)}, bf16[1,64,3,3]{1,3,2,0:T(4,128)(2,1)}, u32[]{:S(2)}) copy-start(bf16[1,64,3,3]{1,3,2,0:T(4,128)(2,1)} %param.13) | copy-start | bytes 3460
  9.8 36.8 %copy-start.9 = (s32[16,8]{0,1:T(8,128)S(1)}, s32[16,8]{0,1:T(8,128)}, u32[]{:S(2)}) copy-start(s32[16,8]{0,1:T(8,128)} %param.10) | copy-start | bytes 1540
  9.8 42.4 %copy-start = (bf16[64,32,3,3]{0,1,3,2:T(8,128)(2,1)S(1)}, bf16[64,32,3,3]{0,1,3,2:T(8,128)(2,1)}, u32[]{:S(2)}) copy-start(bf16[64,32,3,3]{0,1,3,2:T(8,128)(2,1)} %param.12) | copy-start | bytes 110596
  9.8 31.2 %collective-permute-start = (bf16[8,8,9600]{2,1,0:T(8,128)(2,1)}, bf16[8,8,9600]{2,1,0:T(8,128)(2,1)}, u32[]{:S(2)}, u32[]{:S(2)}) collective-permute-start(bf16[8,8,9600]{2,1,0:T(8,128)(2,1)} %get-tuple-element.76), channel_id=1, source_target_pairs={{0,2},{1,3},{2,0},{3,1},{4,6},{5,7},{6,4},{7,5},{8,10},{9,11},{10,... | collective-permute-start | bytes 3686408 | tf_op jit(solution)/shard_map/ppermute | solution.py:458
  12.8 30.3 %collective-permute-start.1 = (bf16[8,8,9600]{2,1,0:T(8,128)(2,1)}, bf16[8,8,9600]{2,1,0:T(8,128)(2,1)}, u32[]{:S(2)}, u32[]{:S(2)}) collective-permute-start(bf16[8,8,9600]{2,1,0:T(8,128)(2,1)} %get-tuple-element.80), channel_id=1, source_target_pairs={{0,4},{1,5},{2,6},{3,7},{4,0},{5,1},{6,2},{7,3},{8,12},{9,13},{10,... | collective-permute-start | bytes 3686408 | tf_op jit(solution)/shard_map/ppermute | solution.py:458
  15.8 93.2 %collective-permute-start.2 = (bf16[13,8,9600]{2,1,0:T(8,128)(2,1)}, bf16[13,8,9600]{2,1,0:T(8,128)(2,1)S(1)}, u32[]{:S(2)}, u32[]{:S(2)}) collective-permute-start(bf16[13,8,9600]{2,1,0:T(8,128)(2,1)} %slice.53), channel_id=1, source_target_pairs={{0,8},{1,9},{2,10},{3,11},{4,12},{5,13},{6,14},{7,15},{8,24},{9,25... | collective-permute-start | bytes 5990408 | tf_op jit(solution)/shard_map/ppermute | solution.py:458
  17.3 92.7 %collective-permute-start.3 = (bf16[8,8,9600]{2,1,0:T(8,128)(2,1)}, bf16[8,8,9600]{2,1,0:T(8,128)(2,1)}, u32[]{:S(2)}, u32[]{:S(2)}) collective-permute-start(bf16[8,8,9600]{2,1,0:T(8,128)(2,1)} %get-tuple-element.62), channel_id=1, source_target_pairs={{0,2},{1,3},{2,0},{3,1},{4,6},{5,7},{6,4},{7,5},{8,10},{9,11},{10,... | collective-permute-start | bytes 3686408 | tf_op jit(solution)/shard_map/ppermute | solution.py:458
  17.9 92.2 %collective-permute-start.4 = (bf16[8,8,9600]{2,1,0:T(8,128)(2,1)}, bf16[8,8,9600]{2,1,0:T(8,128)(2,1)}, u32[]{:S(2)}, u32[]{:S(2)}) collective-permute-start(bf16[8,8,9600]{2,1,0:T(8,128)(2,1)} %get-tuple-element.63), channel_id=1, source_target_pairs={{0,4},{1,5},{2,6},{3,7},{4,0},{5,1},{6,2},{7,3},{8,12},{9,13},{10,... | collective-permute-start | bytes 3686408 | tf_op jit(solution)/shard_map/ppermute | solution.py:458
  43.1 70.7 %collective-permute-start.5 = (bf16[8,8,9600]{2,1,0:T(8,128)(2,1)}, bf16[8,8,9600]{2,1,0:T(8,128)(2,1)}, u32[]{:S(2)}, u32[]{:S(2)}) collective-permute-start(bf16[8,8,9600]{2,1,0:T(8,128)(2,1)} %collective-permute-done.1.rest_2_), channel_id=1, source_target_pairs={{0,2},{1,3},{2,0},{3,1},{4,6},{5,7},{6,4},{7,5},{8,10},{9,11},{10,... | collective-permute-start | bytes 3686408 | tf_op jit(solution)/shard_map/ppermute | solution.py:458
  43.1 70.7 %collective-permute-start.6 = (bf16[8,8,9600]{2,1,0:T(8,128)(2,1)}, bf16[8,8,9600]{2,1,0:T(8,128)(2,1)}, u32[]{:S(2)}, u32[]{:S(2)}) collective-permute-start(bf16[8,8,9600]{2,1,0:T(8,128)(2,1)} %collective-permute-done.rest_1_), channel_id=1, source_target_pairs={{0,4},{1,5},{2,6},{3,7},{4,0},{5,1},{6,2},{7,3},{8,12},{9,13},{10,... | collective-permute-start | bytes 3686408 | tf_op jit(solution)/shard_map/ppermute | solution.py:458
  47.3 47.1 %all-to-all-start = ((s32[32,1,128]{2,1,0:T(1,128)}), s32[32,1,128]{2,1,0:T(1,128)S(1)}, u32[]{:S(2)}, u32[]{:S(2)}) async-start(s32[32,1,128]{2,1,0:T(1,128)} %broadcast_in_dim.42), calls=%async_computation | async-start | bytes 32768 | tf_op jit(solution)/shard_map/all_to_all | solution.py:463
  60.8 1.0 copy-start.1
  61.8 0.7 copy-start.2
  62.5 0.7 copy-start.3
  94.4 0.6 copy-start.8
  108.9 3.3 copy-start.5
  110.1 23.7 %collective-permute-start.9 = (bf16[6,8,9600]{2,1,0:T(8,128)(2,1)}, bf16[6,8,9600]{2,1,0:T(8,128)(2,1)}, u32[]{:S(2)}, u32[]{:S(2)}) collective-permute-start(bf16[6,8,9600]{2,1,0:T(8,128)(2,1)} %slice.69), channel_id=1, source_target_pairs={{0,4},{1,5},{2,6},{3,7},{4,0},{5,1},{6,2},{7,3},{8,12},{9,13},{10,... | collective-permute-start | bytes 2764808 | tf_op jit(solution)/shard_map/ppermute | solution.py:458
  111.7 26.7 %collective-permute-start.8 = (bf16[7,8,9600]{2,1,0:T(8,128)(2,1)S(1)}, bf16[7,8,9600]{2,1,0:T(8,128)(2,1)}, u32[]{:S(2)}, u32[]{:S(2)}) collective-permute-start(bf16[7,8,9600]{2,1,0:T(8,128)(2,1)S(1)} %slice.68), channel_id=1, source_target_pairs={{0,2},{1,3},{2,0},{3,1},{4,6},{5,7},{6,4},{7,5},{8,10},{9,11},{10,... | collective-permute-start | bytes 3225608 | tf_op jit(solution)/shard_map/ppermute | solution.py:458
  112.2 45.9 %collective-permute-start.7 = (bf16[13,8,9600]{2,1,0:T(8,128)(2,1)S(1)}, bf16[13,8,9600]{2,1,0:T(8,128)(2,1)}, u32[]{:S(2)}, u32[]{:S(2)}) collective-permute-start(bf16[13,8,9600]{2,1,0:T(8,128)(2,1)S(1)} %collective-permute-done.2.rest_3_), channel_id=1, source_target_pairs={{0,8},{1,9},{2,10},{3,11},{4,12},{5,13},{6,14},{7,15},{8,24},{9,25... | collective-permute-start | bytes 5990408 | tf_op jit(solution)/shard_map/ppermute | solution.py:458
  113.8 64.0 %collective-permute-start.10 = (bf16[6,8,9600]{2,1,0:T(8,128)(2,1)}, bf16[6,8,9600]{2,1,0:T(8,128)(2,1)}, u32[]{:S(2)}, u32[]{:S(2)}) collective-permute-start(bf16[6,8,9600]{2,1,0:T(8,128)(2,1)} %slice.69), channel_id=1, source_target_pairs={{0,2},{1,3},{2,0},{3,1},{4,6},{5,7},{6,4},{7,5},{8,10},{9,11},{10,... | collective-permute-start | bytes 2764808 | tf_op jit(solution)/shard_map/ppermute | solution.py:458
  115.3 62.6 %collective-permute-start.11 = (bf16[7,8,9600]{2,1,0:T(8,128)(2,1)S(1)}, bf16[7,8,9600]{2,1,0:T(8,128)(2,1)}, u32[]{:S(2)}, u32[]{:S(2)}) collective-permute-start(bf16[7,8,9600]{2,1,0:T(8,128)(2,1)S(1)} %slice.68), channel_id=1, source_target_pairs={{0,4},{1,5},{2,6},{3,7},{4,0},{5,1},{6,2},{7,3},{8,12},{9,13},{10,... | collective-permute-start | bytes 3225608 | tf_op jit(solution)/shard_map/ppermute | solution.py:458
  138.4 45.9 %collective-permute-start.13 = (bf16[6,8,9600]{2,1,0:T(8,128)(2,1)}, bf16[6,8,9600]{2,1,0:T(8,128)(2,1)}, u32[]{:S(2)}, u32[]{:S(2)}) collective-permute-start(bf16[6,8,9600]{2,1,0:T(8,128)(2,1)} %collective-permute-done.9.rest_2_), channel_id=1, source_target_pairs={{0,2},{1,3},{2,0},{3,1},{4,6},{5,7},{6,4},{7,5},{8,10},{9,11},{10,... | collective-permute-start | bytes 2764808 | tf_op jit(solution)/shard_map/ppermute | solution.py:458
  139.0 45.4 %collective-permute-start.14 = (bf16[7,8,9600]{2,1,0:T(8,128)(2,1)}, bf16[7,8,9600]{2,1,0:T(8,128)(2,1)}, u32[]{:S(2)}, u32[]{:S(2)}) collective-permute-start(bf16[7,8,9600]{2,1,0:T(8,128)(2,1)} %collective-permute-done.8.rest_1_), channel_id=1, source_target_pairs={{0,4},{1,5},{2,6},{3,7},{4,0},{5,1},{6,2},{7,3},{8,12},{9,13},{10,... | collective-permute-start | bytes 3225608 | tf_op jit(solution)/shard_map/ppermute | solution.py:458
  158.2 45.1 %collective-permute-start.12 = (bf16[13,8,9600]{2,1,0:T(8,128)(2,1)}, bf16[13,8,9600]{2,1,0:T(8,128)(2,1)S(1)}, u32[]{:S(2)}, u32[]{:S(2)}) collective-permute-start(bf16[13,8,9600]{2,1,0:T(8,128)(2,1)} %collective-permute-done.7.rest_0_), channel_id=1, source_target_pairs={{0,8},{1,9},{2,10},{3,11},{4,12},{5,13},{6,14},{7,15},{8,24},{9,25... | collective-permute-start | bytes 5990408 | tf_op jit(solution)/shard_map/ppermute | solution.py:458
  163.9 14.4 %copy-start.7 = (bf16[7,8,9600]{2,1,0:T(8,128)(2,1)S(1)}, bf16[7,8,9600]{2,1,0:T(8,128)(2,1)}, u32[]{:S(2)}) copy-start(bf16[7,8,9600]{2,1,0:T(8,128)(2,1)} %slice.70) | copy-start | bytes 3225604
  177.9 27.6 %collective-permute-start.16 = (bf16[6,8,9600]{2,1,0:T(8,128)(2,1)}, bf16[6,8,9600]{2,1,0:T(8,128)(2,1)}, u32[]{:S(2)}, u32[]{:S(2)}) collective-permute-start(bf16[6,8,9600]{2,1,0:T(8,128)(2,1)} %slice.71), channel_id=1, source_target_pairs={{0,4},{1,5},{2,6},{3,7},{4,0},{5,1},{6,2},{7,3},{8,12},{9,13},{10,... | collective-permute-start | bytes 2764808 | tf_op jit(solution)/shard_map/ppermute | solution.py:458
  178.4 29.0 %collective-permute-start.15 = (bf16[7,8,9600]{2,1,0:T(8,128)(2,1)S(1)}, bf16[7,8,9600]{2,1,0:T(8,128)(2,1)}, u32[]{:S(2)}, u32[]{:S(2)}) collective-permute-start(bf16[7,8,9600]{2,1,0:T(8,128)(2,1)S(1)} %copy-done.7), channel_id=1, source_target_pairs={{0,2},{1,3},{2,0},{3,1},{4,6},{5,7},{6,4},{7,5},{8,10},{9,11},{10,... | collective-permute-start | bytes 3225608 | tf_op jit(solution)/shard_map/ppermute | solution.py:458
  184.3 42.8 %collective-permute-start.18 = (bf16[6,8,9600]{2,1,0:T(8,128)(2,1)}, bf16[6,8,9600]{2,1,0:T(8,128)(2,1)}, u32[]{:S(2)}, u32[]{:S(2)}) collective-permute-start(bf16[6,8,9600]{2,1,0:T(8,128)(2,1)} %slice.71), channel_id=1, source_target_pairs={{0,2},{1,3},{2,0},{3,1},{4,6},{5,7},{6,4},{7,5},{8,10},{9,11},{10,... | collective-permute-start | bytes 2764808 | tf_op jit(solution)/shard_map/ppermute | solution.py:458
  184.3 42.8 %collective-permute-start.19 = (bf16[7,8,9600]{2,1,0:T(8,128)(2,1)S(1)}, bf16[7,8,9600]{2,1,0:T(8,128)(2,1)}, u32[]{:S(2)}, u32[]{:S(2)}) collective-permute-start(bf16[7,8,9600]{2,1,0:T(8,128)(2,1)S(1)} %copy-done.7), channel_id=1, source_target_pairs={{0,4},{1,5},{2,6},{3,7},{4,0},{5,1},{6,2},{7,3},{8,12},{9,13},{10,... | collective-permute-start | bytes 3225608 | tf_op jit(solution)/shard_map/ppermute | solution.py:458
  203.3 1.3 copy-start.6
  204.6 41.0 %collective-permute-start.17 = (bf16[12,8,9600]{2,1,0:T(8,128)(2,1)}, bf16[12,8,9600]{2,1,0:T(8,128)(2,1)}, u32[]{:S(2)}, u32[]{:S(2)}) collective-permute-start(bf16[12,8,9600]{2,1,0:T(8,128)(2,1)} %slice_dynamic-update-slice_fusion), channel_id=1, source_target_pairs={{0,8},{1,9},{2,10},{3,11},{4,12},{5,13},{6,14},{7,15},{8,24},{9,25... | collective-permute-start | bytes 5529608 | tf_op jit(solution)/shard_map/ppermute | solution.py:458
  207.4 39.5 %collective-permute-start.20 = (bf16[6,8,9600]{2,1,0:T(8,128)(2,1)}, bf16[6,8,9600]{2,1,0:T(8,128)(2,1)}, u32[]{:S(2)}, u32[]{:S(2)}) collective-permute-start(bf16[6,8,9600]{2,1,0:T(8,128)(2,1)} %collective-permute-done.16.rest_1_), channel_id=1, source_target_pairs={{0,2},{1,3},{2,0},{3,1},{4,6},{5,7},{6,4},{7,5},{8,10},{9,11},{10,... | collective-permute-start | bytes 2764808 | tf_op jit(solution)/shard_map/ppermute | solution.py:458
  209.4 38.3 %collective-permute-start.21 = (bf16[7,8,9600]{2,1,0:T(8,128)(2,1)}, bf16[7,8,9600]{2,1,0:T(8,128)(2,1)}, u32[]{:S(2)}, u32[]{:S(2)}) collective-permute-start(bf16[7,8,9600]{2,1,0:T(8,128)(2,1)} %collective-permute-done.15.rest_0_), channel_id=1, source_target_pairs={{0,4},{1,5},{2,6},{3,7},{4,0},{5,1},{6,2},{7,3},{8,12},{9,13},{10,... | collective-permute-start | bytes 3225608 | tf_op jit(solution)/shard_map/ppermute | solution.py:458
  227.1 40.3 %collective-permute-start.24 = (bf16[6,8,9600]{2,1,0:T(8,128)(2,1)S(1)}, bf16[6,8,9600]{2,1,0:T(8,128)(2,1)}, u32[]{:S(2)}, u32[]{:S(2)}) collective-permute-start(bf16[6,8,9600]{2,1,0:T(8,128)(2,1)S(1)} %slice.73), channel_id=1, source_target_pairs={{0,4},{1,5},{2,6},{3,7},{4,0},{5,1},{6,2},{7,3},{8,12},{9,13},{10,... | collective-permute-start | bytes 2764808 | tf_op jit(solution)/shard_map/ppermute | solution.py:458
  227.2 42.6 %collective-permute-start.23 = (bf16[7,8,9600]{2,1,0:T(8,128)(2,1)S(1)}, bf16[7,8,9600]{2,1,0:T(8,128)(2,1)S(1)}, u32[]{:S(2)}, u32[]{:S(2)}) collective-permute-start(bf16[7,8,9600]{2,1,0:T(8,128)(2,1)S(1)} %slice.72), channel_id=1, source_target_pairs={{0,2},{1,3},{2,0},{3,1},{4,6},{5,7},{6,4},{7,5},{8,10},{9,11},{10,... | collective-permute-start | bytes 3225608 | tf_op jit(solution)/shard_map/ppermute | solution.py:458
  245.6 40.6 %collective-permute-start.22 = (bf16[12,8,9600]{2,1,0:T(8,128)(2,1)}, bf16[12,8,9600]{2,1,0:T(8,128)(2,1)S(1)}, u32[]{:S(2)}, u32[]{:S(2)}) collective-permute-start(bf16[12,8,9600]{2,1,0:T(8,128)(2,1)} %collective-permute-done.17.rest_2_), channel_id=1, source_target_pairs={{0,8},{1,9},{2,10},{3,11},{4,12},{5,13},{6,14},{7,15},{8,24},{9,25... | collective-permute-start | bytes 5529608 | tf_op jit(solution)/shard_map/ppermute | solution.py:458
  247.7 41.9 %collective-permute-start.25 = (bf16[6,8,9600]{2,1,0:T(8,128)(2,1)S(1)}, bf16[6,8,9600]{2,1,0:T(8,128)(2,1)}, u32[]{:S(2)}, u32[]{:S(2)}) collective-permute-start(bf16[6,8,9600]{2,1,0:T(8,128)(2,1)S(1)} %slice.73), channel_id=1, source_target_pairs={{0,2},{1,3},{2,0},{3,1},{4,6},{5,7},{6,4},{7,5},{8,10},{9,11},{10,... | collective-permute-start | bytes 2764808 | tf_op jit(solution)/shard_map/ppermute | solution.py:458
  250.4 40.1 %collective-permute-start.26 = (bf16[7,8,9600]{2,1,0:T(8,128)(2,1)S(1)}, bf16[7,8,9600]{2,1,0:T(8,128)(2,1)}, u32[]{:S(2)}, u32[]{:S(2)}) collective-permute-start(bf16[7,8,9600]{2,1,0:T(8,128)(2,1)S(1)} %slice.72), channel_id=1, source_target_pairs={{0,4},{1,5},{2,6},{3,7},{4,0},{5,1},{6,2},{7,3},{8,12},{9,13},{10,... | collective-permute-start | bytes 3225608 | tf_op jit(solution)/shard_map/ppermute | solution.py:458
  269.8 20.7 %copy-start.14 = (bf16[7,8,9600]{2,1,0:T(8,128)(2,1)}, bf16[7,8,9600]{2,1,0:T(8,128)(2,1)S(1)}, u32[]{:S(2)}) copy-start(bf16[7,8,9600]{2,1,0:T(8,128)(2,1)S(1)} %collective-permute-done.23.rest_1_) | copy-start | bytes 3225604
  269.8 37.4 %collective-permute-start.28 = (bf16[6,8,9600]{2,1,0:T(8,128)(2,1)}, bf16[6,8,9600]{2,1,0:T(8,128)(2,1)}, u32[]{:S(2)}, u32[]{:S(2)}) collective-permute-start(bf16[6,8,9600]{2,1,0:T(8,128)(2,1)} %collective-permute-done.24.rest_2_), channel_id=1, source_target_pairs={{0,2},{1,3},{2,0},{3,1},{4,6},{5,7},{6,4},{7,5},{8,10},{9,11},{10,... | collective-permute-start | bytes 2764808 | tf_op jit(solution)/shard_map/ppermute | solution.py:458
  271.8 38.9 %collective-permute-start.29 = (bf16[7,8,9600]{2,1,0:T(8,128)(2,1)S(1)}, bf16[7,8,9600]{2,1,0:T(8,128)(2,1)}, u32[]{:S(2)}, u32[]{:S(2)}) collective-permute-start(bf16[7,8,9600]{2,1,0:T(8,128)(2,1)S(1)} %collective-permute-done.23.rest_1_), channel_id=1, source_target_pairs={{0,4},{1,5},{2,6},{3,7},{4,0},{5,1},{6,2},{7,3},{8,12},{9,13},{10,... | collective-permute-start | bytes 3225608 | tf_op jit(solution)/shard_map/ppermute | solution.py:458
  286.2 4.4 %copy-start.13 = (bf16[12,8,9600]{2,1,0:T(8,128)(2,1)}, bf16[12,8,9600]{2,1,0:T(8,128)(2,1)S(1)}, u32[]{:S(2)}) copy-start(bf16[12,8,9600]{2,1,0:T(8,128)(2,1)S(1)} %collective-permute-done.22.rest_0_) | copy-start | bytes 5529604
  286.2 39.0 %collective-permute-start.27 = (bf16[12,8,9600]{2,1,0:T(8,128)(2,1)S(1)}, bf16[12,8,9600]{2,1,0:T(8,128)(2,1)}, u32[]{:S(2)}, u32[]{:S(2)}) collective-permute-start(bf16[12,8,9600]{2,1,0:T(8,128)(2,1)S(1)} %collective-permute-done.22.rest_0_), channel_id=1, source_target_pairs={{0,8},{1,9},{2,10},{3,11},{4,12},{5,13},{6,14},{7,15},{8,24},{9,25... | collective-permute-start | bytes 5529608 | tf_op jit(solution)/shard_map/ppermute | solution.py:458
  325.2 8.6 %copy-start.12 = (pred[32]{0:T(512)(128)(4,1)S(1)}, pred[32]{0:T(512)(128)(4,1)}, u32[]{:S(2)}) copy-start(pred[32]{0:T(512)(128)(4,1)} %broadcast_in_dim.39) | copy-start | bytes 100
Sparse Core Ops, SparseCore 0:
  8.9 62.0 all-gather.1

commit v11 on v10

--- a/solution.py
+++ b/solution.py
@@ -14,6 +14,8 @@
 SHARES = (1, 7, 6, 2)
 HEAD = 64
 LATER = 4
+LISTS = 2
+WAITS = 5
 WEIGHT = 8
 
 
@@ -357,7 +359,7 @@
         for i, m in enumerate(deep):
             rounds[i * gap].append(m)
         self.per_plane = len(rounds) // depth
-        self.rounds = rounds
+        self.rounds, self.gap = rounds, gap
         for i, messages in enumerate(rounds):
             for axis, _, target in messages:
                 self.arrival[target] = i if axis else i + gap - 1
@@ -443,7 +445,7 @@
             tables[-1], idx_dev, "phase_" + str(p),
         ))
 
-    done = []
+    done, deep = [], []
     for i, messages in enumerate(rounds):
         behind = list(done[i - 2]) if i >= 2 else []
         if len(tables) <= len(ends) and i >= 2:
@@ -453,18 +455,24 @@
         done.append([])
         for together in ([m for m in messages if m[0]], [m for m in messages if not m[0]]):
             sent = [gather.block(source) for _, source, _ in together]
-            sent = lax.optimization_barrier((*sent, *behind))[:len(sent)] if sent else []
+            ties = list(behind)
+            if together and together[0][0] and i >= WAITS and (i - WAITS) % gather.gap == 0:
+                ties.append(deep[(i - 1) // gather.gap - 1])
+            sent = lax.optimization_barrier((*sent, *ties))[:len(sent)] if sent else []
             for (axis, _, target), block in zip(together, sent):
                 gather.blocks[target] = lax.ppermute(block, "shard", gather.steps[axis])
-                if axis:
-                    done[i].append(gather.blocks[target])
+                (done[i] if axis else deep).append(gather.blocks[target])
         if i == 0:
             ids = lax.optimization_barrier((candidates, *done[0]))[0].reshape(1, pairs)
-            ids = lax.all_to_all(
+            state["ids"] = lax.all_to_all(
                 jnp.broadcast_to(ids, (devices, pairs)), "shard", split_axis=0, concat_axis=0,
                 tiled=True,
             )
-            state["lists"] = pair_lists(who, ids, contents, bounds, caps, k_count, idx_dev)
+        if i == min(LISTS, total - 1):
+            later = lax.optimization_barrier((who, *done[i]))[0]
+            state["lists"] = pair_lists(
+                later, state["ids"], contents, bounds, caps, k_count, idx_dev
+            )
     while len(tables) <= len(ends):
         score()
     table = jnp.where(jnp.arange(2)[None, :, None] == core, tables[-1][:, None], 0.0)

time: 354 us -> 324 us (0.915)
  waiting for transfers between devices: 178 us -> 146 us
  blocking collectives: 11.8 us -> 15.5 us
    all_to_all x1, waiting for transfers between devices: 30.7 us -> 0.01 us  [body(): lax.all_to_all(jnp.broadcast_to(ids, (devices, pairs)), 'shard', split_ax...]
    all_to_all x1, blocking collectives: 11.8 us -> 15.5 us  [body(): lax.all_to_all(table.reshape(devices, pairs), 'shard', split_axis=0, conc...]
  transfers between devices with their start and end apart: 32 -> 32, of which waited for: 20 -> 17; matrix products, arithmetic and copies ran while one was open for 7% -> 8% of each run, Pallas kernels for 19% -> 21%
where the time goes in v11:
time: 324 us; the launch traced here: 322 us
  waiting for transfers between devices  146 us (45%)
  Pallas kernels  76.3 us (24%)
  starting transfers between devices  39.6 us (12%)
  local copies, waits for them, and re-layouts  30.1 us (9%)
  blocking collectives  15.5 us (5%)
  between operations  13.6 us (4%)
    ppermute x30, waiting for transfers between devices, body(): gather.blocks[target] = lax.ppermute(block, 'shard', gather.steps[axis])  146 us
    pallas_call x5, Pallas kernels, pair_scores(): pl.pallas_call(functools.partial(pair_kernel, frames, idx_dev, len(blocks...  53.9 us
    ppermute x30, starting transfers between devices, body(): gather.blocks[target] = lax.ppermute(block, 'shard', gather.steps[axis])  34.7 us
    all_to_all x1, blocking collectives, body(): lax.all_to_all(table.reshape(devices, pairs), 'shard', split_axis=0, conc...  15.5 us
    unnamed x37, local copies, waits for them, and re-layouts  15.4 us
    pallas_call x1, Pallas kernels, pair_lists(): pl.pallas_call(functools.partial(list_kernel, idx_dev, k_count, ids.shape...  13.9 us
    slice x8, local copies, waits for them, and re-layouts, block(): parts = [b[at:at + n] for b, (_, at, n) in zip(whole, self.pieces[key])]  8.77 us
    pallas_call x1, Pallas kernels, head_matrices(): pl.pallas_call(head_kernel, out_shape=[jax.ShapeDtypeStruct(s, jnp.bfloat...  8.54 us
  transfers between devices with their start and end apart: 32, of which 17 were waited for; matrix products, arithmetic and copies ran while one was open for 8% of the time, Pallas kernels for 21%

profile of v11, /device:TPU:0, one launch (start us, length us, event | category | flops | bytes accessed | tf_op | source)
XLA Modules:
  0.0 322.2 jit_solution(3270831241331385559)
XLA Ops:
  6.5 0.7 all-gather.2.cloned.1.call-update
  7.3 1.0 copy-done.4
  8.2 1.6 fusion
  9.8 3.0 collective-permute-start
  12.8 1.5 collective-permute-start.1
  14.3 1.4 slice.53
  15.7 1.6 collective-permute-start.4
  18.3 22.6 %collective-permute-done.rest_2_ = bf16[8,8,9600]{2,1,0:T(8,128)(2,1)} collective-permute-done((bf16[8,8,9600]{2,1,0:T(8,128)(2,1)}, bf16[8,8,9600]{2,1,0:T(8,128)(2,1)}, u32[]{:S(2)}, u32[]{:S(2)}) %collective-permute-start) | collective-permute-done | bytes 1228832 | tf_op jit(solution)/shard_map/ppermute | solution.py:463
  40.9 2.1 collective-permute-done.1.rest_1_
  43.0 1.5 collective-permute-start.2
  45.8 8.5 %head_matrices.1 = (bf16[64,2048]{1,0:T(8,128)(2,1)S(1)}, bf16[512,1024]{1,0:T(8,128)(2,1)S(1)}, bf16[256,256]{1,0:T(8,128)(2,1)S(1)}) custom-call(bf16[9,1,32]{2,1,0:T(2,128)(2,1)S(1)} %reshape.74.one_w, bf16[9,32,64]{2,1,0:T(8,128)(2,1)S(1)} %bitcast.16, bf16[9,1,64]{2,1,0:T(2,128)(2,1)S(1)} %reshape.75.three_w), custom_call_target="tpu_custom_call" | custom-call | flops 1000000000 | bytes 3000000 | tf_op jit(solution)/shard_map/head_matrices/pallas_call | solution.py:89
  54.4 1.0 copy-done.1
  55.3 0.7 copy-done.2
  58.8 4.9 %all-to-all-start = ((s32[32,1,128]{2,1,0:T(1,128)}), s32[32,1,128]{2,1,0:T(1,128)S(1)}, u32[]{:S(2)}, u32[]{:S(2)}) async-start(s32[32,1,128]{2,1,0:T(1,128)} %broadcast_in_dim.42), calls=%async_computation | async-start | bytes 32768 | tf_op jit(solution)/shard_map/all_to_all | solution.py:467
  63.7 1.1 slice.69
  64.8 4.6 %collective-permute-done.5.rest_4_ = bf16[8,8,9600]{2,1,0:T(8,128)(2,1)} collective-permute-done((bf16[8,8,9600]{2,1,0:T(8,128)(2,1)}, bf16[8,8,9600]{2,1,0:T(8,128)(2,1)}, u32[]{:S(2)}, u32[]{:S(2)}) %collective-permute-start.5) | collective-permute-done | bytes 1228832 | tf_op jit(solution)/shard_map/ppermute | solution.py:463
  69.5 2.0 collective-permute-start.8
  71.5 1.6 collective-permute-start.7
  73.1 22.8 %collective-permute-done.2.rest_6_ = bf16[8,8,9600]{2,1,0:T(8,128)(2,1)} collective-permute-done((bf16[8,8,9600]{2,1,0:T(8,128)(2,1)}, bf16[8,8,9600]{2,1,0:T(8,128)(2,1)}, u32[]{:S(2)}, u32[]{:S(2)}) %collective-permute-start.2) | collective-permute-done | bytes 1228832 | tf_op jit(solution)/shard_map/ppermute | solution.py:463
  95.8 1.5 collective-permute-start.10
  97.8 1.6 slice_dynamic-update-slice_fusion.7
  99.4 1.6 slice_dynamic-update-slice_fusion.6
  101.0 1.6 slice_dynamic-update-slice_fusion.5
  102.6 1.6 slice_dynamic-update-slice_fusion.4
  104.1 1.7 slice_dynamic-update-slice_fusion.3
  105.8 1.7 slice_dynamic-update-slice_fusion.2
  107.5 1.7 slice_dynamic-update-slice_fusion.1
  109.9 13.9 %pair_lists.1 = (s32[152]{0:T(256)}, s32[152]{0:T(256)}, s32[151]{0:T(256)}, s32[149]{0:T(256)}, s32[83]{0:T(128)}) custom-call(s32[18]{0:T(128)} %pad_add_fusion.who_ref, s32[32,128]{1,0:T(8,128)} %bitcast.19, s32[256]{0:T(256)} %constant.41.clone.queries_ref), custom_call_target="tpu_custom_call" | custom-call | flops 10000000 | bytes 1000000 | tf_op jit(solution)/shard_map/pair_lists/pallas_call | solution.py:135
  123.9 2.0 collective-permute-start.14
  125.9 1.6 collective-permute-start.12
  127.5 2.2 slice.71
  129.7 2.3 slice.70
  132.6 14.0 %phase_0.1.before_ref = f32[16,128]{1,0:T(8,128)} custom-call(s32[152]{0:T(256)} %get-tuple-element.65.list_ref, bf16[64,2048]{1,0:T(8,128)(2,1)} %copy-done.2, bf16[512,1024]{1,0:T(8,128)(2,1)} %copy-done.1, bf16[256,256]{1,0:T(8,128)(2,1)} %copy-done.3, f32[16,128]{1,0:T(8,128)} %broadcast_in_dim.43.before_ref, ...), custom_call_target="tpu_custom_call" | custom-call | flops 100663296000 | bytes 39321600 | tf_op jit(solution)/shard_map/phase_0/pallas_call | solution.py:257
  146.6 0.7 collective-permute-start.16
  147.3 1.3 collective-permute-start.15
  148.7 1.7 slice_dynamic-update-slice_fusion
  150.4 8.0 %collective-permute-done.13.rest_6_ = bf16[6,8,9600]{2,1,0:T(8,128)(2,1)} collective-permute-done((bf16[6,8,9600]{2,1,0:T(8,128)(2,1)}, bf16[6,8,9600]{2,1,0:T(8,128)(2,1)}, u32[]{:S(2)}, u32[]{:S(2)}) %collective-permute-start.13) | collective-permute-done | bytes 921632 | tf_op jit(solution)/shard_map/ppermute | solution.py:463
  158.4 1.2 collective-permute-done.14.rest_7_
  159.6 8.9 %collective-permute-done.12.rest_5_ = bf16[13,8,9600]{2,1,0:T(8,128)(2,1)S(1)} collective-permute-done((bf16[13,8,9600]{2,1,0:T(8,128)(2,1)}, bf16[13,8,9600]{2,1,0:T(8,128)(2,1)S(1)}, u32[]{:S(2)}, u32[]{:S(2)}) %collective-permute-start.12) | collective-permute-done | bytes 1996832 | tf_op jit(solution)/shard_map/ppermute | solution.py:463
  168.5 1.5 collective-permute-start.18
  170.7 0.9 collective-permute-start.17
  171.7 7.7 %collective-permute-done.16.rest_1_ = bf16[6,8,9600]{2,1,0:T(8,128)(2,1)} collective-permute-done((bf16[6,8,9600]{2,1,0:T(8,128)(2,1)}, bf16[6,8,9600]{2,1,0:T(8,128)(2,1)}, u32[]{:S(2)}, u32[]{:S(2)}) %collective-permute-start.16) | collective-permute-done | bytes 921632 | tf_op jit(solution)/shard_map/ppermute | solution.py:463
  179.4 2.1 collective-permute-done.15.rest_0_
  181.5 1.5 collective-permute-start.20
  183.5 10.4 %phase_1.1.before_ref = f32[16,128]{1,0:T(8,128)} custom-call(s32[152]{0:T(256)} %get-tuple-element.64.list_ref, bf16[64,2048]{1,0:T(8,128)(2,1)} %copy-done.2, bf16[512,1024]{1,0:T(8,128)(2,1)} %copy-done.1, bf16[256,256]{1,0:T(8,128)(2,1)} %copy-done.3, f32[16,128]{1,0:T(8,128)} %phase_0.1.before_ref, ...), custom_call_target="tpu_custom_call" | custom-call | flops 100663296000 | bytes 39321600 | tf_op jit(solution)/shard_map/phase_1/pallas_call | solution.py:257
  193.9 17.2 %collective-permute-done.17.rest_2_ = bf16[12,8,9600]{2,1,0:T(8,128)(2,1)} collective-permute-done((bf16[12,8,9600]{2,1,0:T(8,128)(2,1)}, bf16[12,8,9600]{2,1,0:T(8,128)(2,1)}, u32[]{:S(2)}, u32[]{:S(2)}) %collective-permute-start.17) | collective-permute-done | bytes 1843232 | tf_op jit(solution)/shard_map/ppermute | solution.py:463
  211.1 0.8 collective-permute-start.22
  211.9 1.4 collective-permute-start.24
  213.9 7.1 %collective-permute-done.20.rest_5_ = bf16[6,8,9600]{2,1,0:T(8,128)(2,1)} collective-permute-done((bf16[6,8,9600]{2,1,0:T(8,128)(2,1)}, bf16[6,8,9600]{2,1,0:T(8,128)(2,1)}, u32[]{:S(2)}, u32[]{:S(2)}) %collective-permute-start.20) | collective-permute-done | bytes 921632 | tf_op jit(solution)/shard_map/ppermute | solution.py:463
  221.0 4.5 %collective-permute-done.21.rest_6_ = bf16[7,8,9600]{2,1,0:T(8,128)(2,1)} collective-permute-done((bf16[7,8,9600]{2,1,0:T(8,128)(2,1)}, bf16[7,8,9600]{2,1,0:T(8,128)(2,1)}, u32[]{:S(2)}, u32[]{:S(2)}) %collective-permute-start.21) | collective-permute-done | bytes 1075232 | tf_op jit(solution)/shard_map/ppermute | solution.py:463
  225.4 2.0 collective-permute-start.25
  227.5 1.5 collective-permute-start.26
  229.0 11.3 %phase_2.1.before_ref = f32[16,128]{1,0:T(8,128)} custom-call(s32[151]{0:T(256)} %get-tuple-element.63.list_ref, bf16[64,2048]{1,0:T(8,128)(2,1)} %copy-done.2, bf16[512,1024]{1,0:T(8,128)(2,1)} %copy-done.1, bf16[256,256]{1,0:T(8,128)(2,1)} %copy-done.3, f32[16,128]{1,0:T(8,128)} %phase_1.1.before_ref, ...), custom_call_target="tpu_custom_call" | custom-call | flops 100663296000 | bytes 39321600 | tf_op jit(solution)/shard_map/phase_2/pallas_call | solution.py:257
  240.3 11.4 %collective-permute-done.22.rest_0_ = bf16[12,8,9600]{2,1,0:T(8,128)(2,1)S(1)} collective-permute-done((bf16[12,8,9600]{2,1,0:T(8,128)(2,1)}, bf16[12,8,9600]{2,1,0:T(8,128)(2,1)S(1)}, u32[]{:S(2)}, u32[]{:S(2)}) %collective-permute-start.22) | collective-permute-done | bytes 1843232 | tf_op jit(solution)/shard_map/ppermute | solution.py:463
  251.7 0.9 collective-permute-start.27
  252.6 0.7 collective-permute-start.28
  253.3 1.3 collective-permute-start.29
  254.6 9.1 %collective-permute-done.25.rest_3_ = bf16[6,8,9600]{2,1,0:T(8,128)(2,1)} collective-permute-done((bf16[6,8,9600]{2,1,0:T(8,128)(2,1)S(1)}, bf16[6,8,9600]{2,1,0:T(8,128)(2,1)}, u32[]{:S(2)}, u32[]{:S(2)}) %collective-permute-start.25) | collective-permute-done | bytes 921632 | tf_op jit(solution)/shard_map/ppermute | solution.py:463
  263.8 4.5 %collective-permute-done.26.rest_4_ = bf16[7,8,9600]{2,1,0:T(8,128)(2,1)} collective-permute-done((bf16[7,8,9600]{2,1,0:T(8,128)(2,1)S(1)}, bf16[7,8,9600]{2,1,0:T(8,128)(2,1)}, u32[]{:S(2)}, u32[]{:S(2)}) %collective-permute-start.26) | collective-permute-done | bytes 1075232 | tf_op jit(solution)/shard_map/ppermute | solution.py:463
  268.2 10.3 %phase_3.1.before_ref = f32[16,128]{1,0:T(8,128)} custom-call(s32[149]{0:T(256)} %get-tuple-element.62.list_ref, bf16[64,2048]{1,0:T(8,128)(2,1)} %copy-done.2, bf16[512,1024]{1,0:T(8,128)(2,1)} %copy-done.1, bf16[256,256]{1,0:T(8,128)(2,1)} %copy-done.3, f32[16,128]{1,0:T(8,128)} %phase_2.1.before_ref, ...), custom_call_target="tpu_custom_call" | custom-call | flops 100663296000 | bytes 39321600 | tf_op jit(solution)/shard_map/phase_3/pallas_call | solution.py:257
  278.6 3.4 %collective-permute-done.28.rest_1_ = bf16[6,8,9600]{2,1,0:T(8,128)(2,1)} collective-permute-done((bf16[6,8,9600]{2,1,0:T(8,128)(2,1)}, bf16[6,8,9600]{2,1,0:T(8,128)(2,1)}, u32[]{:S(2)}, u32[]{:S(2)}) %collective-permute-start.28) | collective-permute-done | bytes 921632 | tf_op jit(solution)/shard_map/ppermute | solution.py:463
  282.0 8.4 %collective-permute-done.29.rest_2_ = bf16[7,8,9600]{2,1,0:T(8,128)(2,1)} collective-permute-done((bf16[7,8,9600]{2,1,0:T(8,128)(2,1)S(1)}, bf16[7,8,9600]{2,1,0:T(8,128)(2,1)}, u32[]{:S(2)}, u32[]{:S(2)}) %collective-permute-start.29) | collective-permute-done | bytes 1075232 | tf_op jit(solution)/shard_map/ppermute | solution.py:463
  290.5 7.9 %phase_4.1 = f32[16,128]{1,0:T(8,128)} custom-call(s32[83]{0:T(128)} %get-tuple-element.58.list_ref, bf16[64,2048]{1,0:T(8,128)(2,1)} %copy-done.2, bf16[512,1024]{1,0:T(8,128)(2,1)} %copy-done.1, bf16[256,256]{1,0:T(8,128)(2,1)} %copy-done.3, f32[16,128]{1,0:T(8,128)} %phase_3.1.before_ref, bf16[256,8,9600]{2,1,0:T(8,128)(2,1)} %all-gather.2.cloned.1.call-done.v_hbm, ...), custom_call_target="tpu_custom_call" | custom-call | flops 50331648000 | bytes 19660800 | tf_op jit(solution)/shard_map/phase_4/pallas_call | solution.py:257
  299.2 15.5 %all_to_all.14 = f32[32,1,128]{2,1,0:T(1,128)S(1)} all-to-all(f32[32,1,128]{2,1,0:T(1,128)S(1)} %broadcast_select_fusion), channel_id=1, replica_groups=mesh['shard'=32] {'shard'}, dimensions={0} | all-to-all | bytes 32768 | tf_op jit(solution)/shard_map/all_to_all | solution.py:479
  (71 shorter events, 10.3 us)
Async XLA Ops:
  6.5 1.7 copy-start.4
  6.5 125.5 %all-gather.2.cloned.1.call-start = ((), (), s32[]{:S(2)}) async-start(), calls=%async_computation.2 | async-start | bytes 58982400 | tf_op jit(solution)/shard_map/all_gather | solution.py:399
  9.8 35.9 %copy-start.10 = (bf16[32,1,3,3]{0,3,2,1:T(4,128)(2,1)S(1)}, bf16[32,1,3,3]{0,3,2,1:T(4,128)(2,1)}, u32[]{:S(2)}) copy-start(bf16[32,1,3,3]{0,3,2,1:T(4,128)(2,1)} %param.11) | copy-start | bytes 1732
  9.8 35.9 %copy-start.11 = (bf16[1,64,3,3]{1,3,2,0:T(4,128)(2,1)S(1)}, bf16[1,64,3,3]{1,3,2,0:T(4,128)(2,1)}, u32[]{:S(2)}) copy-start(bf16[1,64,3,3]{1,3,2,0:T(4,128)(2,1)} %param.13) | copy-start | bytes 3460
  9.8 36.0 %copy-start = (bf16[64,32,3,3]{0,1,3,2:T(8,128)(2,1)S(1)}, bf16[64,32,3,3]{0,1,3,2:T(8,128)(2,1)}, u32[]{:S(2)}) copy-start(bf16[64,32,3,3]{0,1,3,2:T(8,128)(2,1)} %param.12) | copy-start | bytes 110596
  9.8 31.1 %collective-permute-start = (bf16[8,8,9600]{2,1,0:T(8,128)(2,1)}, bf16[8,8,9600]{2,1,0:T(8,128)(2,1)}, u32[]{:S(2)}, u32[]{:S(2)}) collective-permute-start(bf16[8,8,9600]{2,1,0:T(8,128)(2,1)} %get-tuple-element.82), channel_id=1, source_target_pairs={{0,4},{1,5},{2,6},{3,7},{4,0},{5,1},{6,2},{7,3},{8,12},{9,13},{10,... | collective-permute-start | bytes 3686408 | tf_op jit(solution)/shard_map/ppermute | solution.py:463
  12.8 30.3 %collective-permute-start.1 = (bf16[8,8,9600]{2,1,0:T(8,128)(2,1)}, bf16[8,8,9600]{2,1,0:T(8,128)(2,1)}, u32[]{:S(2)}, u32[]{:S(2)}) collective-permute-start(bf16[8,8,9600]{2,1,0:T(8,128)(2,1)} %get-tuple-element.78), channel_id=1, source_target_pairs={{0,2},{1,3},{2,0},{3,1},{4,6},{5,7},{6,4},{7,5},{8,10},{9,11},{10,... | collective-permute-start | bytes 3686408 | tf_op jit(solution)/shard_map/ppermute | solution.py:463
  15.7 48.0 %collective-permute-start.4 = (bf16[13,8,9600]{2,1,0:T(8,128)(2,1)}, bf16[13,8,9600]{2,1,0:T(8,128)(2,1)S(1)}, u32[]{:S(2)}, u32[]{:S(2)}) collective-permute-start(bf16[13,8,9600]{2,1,0:T(8,128)(2,1)} %slice.53), channel_id=1, source_target_pairs={{0,8},{1,9},{2,10},{3,11},{4,12},{5,13},{6,14},{7,15},{8,24},{9,25... | collective-permute-start | bytes 5990408 | tf_op jit(solution)/shard_map/ppermute | solution.py:463
  17.3 52.2 %collective-permute-start.5 = (bf16[8,8,9600]{2,1,0:T(8,128)(2,1)}, bf16[8,8,9600]{2,1,0:T(8,128)(2,1)}, u32[]{:S(2)}, u32[]{:S(2)}) collective-permute-start(bf16[8,8,9600]{2,1,0:T(8,128)(2,1)} %get-tuple-element.66), channel_id=1, source_target_pairs={{0,2},{1,3},{2,0},{3,1},{4,6},{5,7},{6,4},{7,5},{8,10},{9,11},{10,... | collective-permute-start | bytes 3686408 | tf_op jit(solution)/shard_map/ppermute | solution.py:463
  17.8 51.7 %collective-permute-start.6 = (bf16[8,8,9600]{2,1,0:T(8,128)(2,1)}, bf16[8,8,9600]{2,1,0:T(8,128)(2,1)}, u32[]{:S(2)}, u32[]{:S(2)}) collective-permute-start(bf16[8,8,9600]{2,1,0:T(8,128)(2,1)} %get-tuple-element.67), channel_id=1, source_target_pairs={{0,4},{1,5},{2,6},{3,7},{4,0},{5,1},{6,2},{7,3},{8,12},{9,13},{10,... | collective-permute-start | bytes 3686408 | tf_op jit(solution)/shard_map/ppermute | solution.py:463
  43.0 52.8 %collective-permute-start.2 = (bf16[8,8,9600]{2,1,0:T(8,128)(2,1)}, bf16[8,8,9600]{2,1,0:T(8,128)(2,1)}, u32[]{:S(2)}, u32[]{:S(2)}) collective-permute-start(bf16[8,8,9600]{2,1,0:T(8,128)(2,1)} %collective-permute-done.rest_2_), channel_id=1, source_target_pairs={{0,2},{1,3},{2,0},{3,1},{4,6},{5,7},{6,4},{7,5},{8,10},{9,11},{10,... | collective-permute-start | bytes 3686408 | tf_op jit(solution)/shard_map/ppermute | solution.py:463
  44.5 51.3 %collective-permute-start.3 = (bf16[8,8,9600]{2,1,0:T(8,128)(2,1)}, bf16[8,8,9600]{2,1,0:T(8,128)(2,1)}, u32[]{:S(2)}, u32[]{:S(2)}) collective-permute-start(bf16[8,8,9600]{2,1,0:T(8,128)(2,1)} %collective-permute-done.1.rest_1_), channel_id=1, source_target_pairs={{0,4},{1,5},{2,6},{3,7},{4,0},{5,1},{6,2},{7,3},{8,12},{9,13},{10,... | collective-permute-start | bytes 3686408 | tf_op jit(solution)/shard_map/ppermute | solution.py:463
  45.8 12.2 %copy-start.9 = (s32[16,8]{0,1:T(8,128)S(1)}, s32[16,8]{0,1:T(8,128)}, u32[]{:S(2)}) copy-start(s32[16,8]{0,1:T(8,128)} %param.10) | copy-start | bytes 1540
  54.3 1.0 copy-start.1
  55.3 0.7 copy-start.2
  56.0 0.7 copy-start.3
  58.8 50.5 %all-to-all-start = ((s32[32,1,128]{2,1,0:T(1,128)}), s32[32,1,128]{2,1,0:T(1,128)S(1)}, u32[]{:S(2)}, u32[]{:S(2)}) async-start(s32[32,1,128]{2,1,0:T(1,128)} %broadcast_in_dim.42), calls=%async_computation | async-start | bytes 32768 | tf_op jit(solution)/shard_map/all_to_all | solution.py:467
  63.7 7.8 %copy-start.5 = (bf16[13,8,9600]{2,1,0:T(8,128)(2,1)}, bf16[13,8,9600]{2,1,0:T(8,128)(2,1)S(1)}, u32[]{:S(2)}) copy-start(bf16[13,8,9600]{2,1,0:T(8,128)(2,1)S(1)} %collective-permute-done.4.rest_3_) | copy-start | bytes 5990404
  69.5 54.3 %collective-permute-start.9 = (bf16[6,8,9600]{2,1,0:T(8,128)(2,1)}, bf16[6,8,9600]{2,1,0:T(8,128)(2,1)}, u32[]{:S(2)}, u32[]{:S(2)}) collective-permute-start(bf16[6,8,9600]{2,1,0:T(8,128)(2,1)} %slice.69), channel_id=1, source_target_pairs={{0,4},{1,5},{2,6},{3,7},{4,0},{5,1},{6,2},{7,3},{8,12},{9,13},{10,... | collective-permute-start | bytes 2764808 | tf_op jit(solution)/shard_map/ppermute | solution.py:463
  69.5 54.3 %collective-permute-start.8 = (bf16[7,8,9600]{2,1,0:T(8,128)(2,1)S(1)}, bf16[7,8,9600]{2,1,0:T(8,128)(2,1)}, u32[]{:S(2)}, u32[]{:S(2)}) collective-permute-start(bf16[7,8,9600]{2,1,0:T(8,128)(2,1)S(1)} %slice.68), channel_id=1, source_target_pairs={{0,2},{1,3},{2,0},{3,1},{4,6},{5,7},{6,4},{7,5},{8,10},{9,11},{10,... | collective-permute-start | bytes 3225608 | tf_op jit(solution)/shard_map/ppermute | solution.py:463
  71.5 52.3 %collective-permute-start.7 = (bf16[13,8,9600]{2,1,0:T(8,128)(2,1)S(1)}, bf16[13,8,9600]{2,1,0:T(8,128)(2,1)}, u32[]{:S(2)}, u32[]{:S(2)}) collective-permute-start(bf16[13,8,9600]{2,1,0:T(8,128)(2,1)S(1)} %collective-permute-done.4.rest_3_), channel_id=1, source_target_pairs={{0,8},{1,9},{2,10},{3,11},{4,12},{5,13},{6,14},{7,15},{8,24},{9,25... | collective-permute-start | bytes 5990408 | tf_op jit(solution)/shard_map/ppermute | solution.py:463
  95.8 50.8 %collective-permute-start.10 = (bf16[6,8,9600]{2,1,0:T(8,128)(2,1)}, bf16[6,8,9600]{2,1,0:T(8,128)(2,1)}, u32[]{:S(2)}, u32[]{:S(2)}) collective-permute-start(bf16[6,8,9600]{2,1,0:T(8,128)(2,1)} %slice.69), channel_id=1, source_target_pairs={{0,2},{1,3},{2,0},{3,1},{4,6},{5,7},{6,4},{7,5},{8,10},{9,11},{10,... | collective-permute-start | bytes 2764808 | tf_op jit(solution)/shard_map/ppermute | solution.py:463
  97.3 49.3 %collective-permute-start.11 = (bf16[7,8,9600]{2,1,0:T(8,128)(2,1)S(1)}, bf16[7,8,9600]{2,1,0:T(8,128)(2,1)}, u32[]{:S(2)}, u32[]{:S(2)}) collective-permute-start(bf16[7,8,9600]{2,1,0:T(8,128)(2,1)S(1)} %slice.68), channel_id=1, source_target_pairs={{0,4},{1,5},{2,6},{3,7},{4,0},{5,1},{6,2},{7,3},{8,12},{9,13},{10,... | collective-permute-start | bytes 3225608 | tf_op jit(solution)/shard_map/ppermute | solution.py:463
  109.3 0.6 copy-start.8
  123.8 34.6 %collective-permute-start.13 = (bf16[6,8,9600]{2,1,0:T(8,128)(2,1)}, bf16[6,8,9600]{2,1,0:T(8,128)(2,1)}, u32[]{:S(2)}, u32[]{:S(2)}) collective-permute-start(bf16[6,8,9600]{2,1,0:T(8,128)(2,1)} %collective-permute-done.9.rest_2_), channel_id=1, source_target_pairs={{0,2},{1,3},{2,0},{3,1},{4,6},{5,7},{6,4},{7,5},{8,10},{9,11},{10,... | collective-permute-start | bytes 2764808 | tf_op jit(solution)/shard_map/ppermute | solution.py:463
  123.9 35.7 %collective-permute-start.14 = (bf16[7,8,9600]{2,1,0:T(8,128)(2,1)}, bf16[7,8,9600]{2,1,0:T(8,128)(2,1)}, u32[]{:S(2)}, u32[]{:S(2)}) collective-permute-start(bf16[7,8,9600]{2,1,0:T(8,128)(2,1)} %collective-permute-done.8.rest_1_), channel_id=1, source_target_pairs={{0,4},{1,5},{2,6},{3,7},{4,0},{5,1},{6,2},{7,3},{8,12},{9,13},{10,... | collective-permute-start | bytes 3225608 | tf_op jit(solution)/shard_map/ppermute | solution.py:463
  125.9 42.6 %collective-permute-start.12 = (bf16[13,8,9600]{2,1,0:T(8,128)(2,1)}, bf16[13,8,9600]{2,1,0:T(8,128)(2,1)S(1)}, u32[]{:S(2)}, u32[]{:S(2)}) collective-permute-start(bf16[13,8,9600]{2,1,0:T(8,128)(2,1)} %collective-permute-done.7.rest_0_), channel_id=1, source_target_pairs={{0,8},{1,9},{2,10},{3,11},{4,12},{5,13},{6,14},{7,15},{8,24},{9,25... | collective-permute-start | bytes 5990408 | tf_op jit(solution)/shard_map/ppermute | solution.py:463
  132.6 14.7 %copy-start.7 = (bf16[7,8,9600]{2,1,0:T(8,128)(2,1)S(1)}, bf16[7,8,9600]{2,1,0:T(8,128)(2,1)}, u32[]{:S(2)}) copy-start(bf16[7,8,9600]{2,1,0:T(8,128)(2,1)} %slice.70) | copy-start | bytes 3225604
  146.6 32.8 %collective-permute-start.16 = (bf16[6,8,9600]{2,1,0:T(8,128)(2,1)}, bf16[6,8,9600]{2,1,0:T(8,128)(2,1)}, u32[]{:S(2)}, u32[]{:S(2)}) collective-permute-start(bf16[6,8,9600]{2,1,0:T(8,128)(2,1)} %slice.71), channel_id=1, source_target_pairs={{0,4},{1,5},{2,6},{3,7},{4,0},{5,1},{6,2},{7,3},{8,12},{9,13},{10,... | collective-permute-start | bytes 2764808 | tf_op jit(solution)/shard_map/ppermute | solution.py:463
  147.3 34.1 %collective-permute-start.15 = (bf16[7,8,9600]{2,1,0:T(8,128)(2,1)S(1)}, bf16[7,8,9600]{2,1,0:T(8,128)(2,1)}, u32[]{:S(2)}, u32[]{:S(2)}) collective-permute-start(bf16[7,8,9600]{2,1,0:T(8,128)(2,1)S(1)} %copy-done.7), channel_id=1, source_target_pairs={{0,2},{1,3},{2,0},{3,1},{4,6},{5,7},{6,4},{7,5},{8,10},{9,11},{10,... | collective-permute-start | bytes 3225608 | tf_op jit(solution)/shard_map/ppermute | solution.py:463
  168.5 2.2 copy-start.6
  168.5 43.4 %collective-permute-start.18 = (bf16[6,8,9600]{2,1,0:T(8,128)(2,1)}, bf16[6,8,9600]{2,1,0:T(8,128)(2,1)}, u32[]{:S(2)}, u32[]{:S(2)}) collective-permute-start(bf16[6,8,9600]{2,1,0:T(8,128)(2,1)} %slice.71), channel_id=1, source_target_pairs={{0,2},{1,3},{2,0},{3,1},{4,6},{5,7},{6,4},{7,5},{8,10},{9,11},{10,... | collective-permute-start | bytes 2764808 | tf_op jit(solution)/shard_map/ppermute | solution.py:463
  170.0 41.9 %collective-permute-start.19 = (bf16[7,8,9600]{2,1,0:T(8,128)(2,1)S(1)}, bf16[7,8,9600]{2,1,0:T(8,128)(2,1)}, u32[]{:S(2)}, u32[]{:S(2)}) collective-permute-start(bf16[7,8,9600]{2,1,0:T(8,128)(2,1)S(1)} %copy-done.7), channel_id=1, source_target_pairs={{0,4},{1,5},{2,6},{3,7},{4,0},{5,1},{6,2},{7,3},{8,12},{9,13},{10,... | collective-permute-start | bytes 3225608 | tf_op jit(solution)/shard_map/ppermute | solution.py:463
  170.7 40.4 %collective-permute-start.17 = (bf16[12,8,9600]{2,1,0:T(8,128)(2,1)}, bf16[12,8,9600]{2,1,0:T(8,128)(2,1)}, u32[]{:S(2)}, u32[]{:S(2)}) collective-permute-start(bf16[12,8,9600]{2,1,0:T(8,128)(2,1)} %slice_dynamic-update-slice_fusion), channel_id=1, source_target_pairs={{0,8},{1,9},{2,10},{3,11},{4,12},{5,13},{6,14},{7,15},{8,24},{9,25... | collective-permute-start | bytes 5529608 | tf_op jit(solution)/shard_map/ppermute | solution.py:463
  181.5 39.5 %collective-permute-start.20 = (bf16[6,8,9600]{2,1,0:T(8,128)(2,1)}, bf16[6,8,9600]{2,1,0:T(8,128)(2,1)}, u32[]{:S(2)}, u32[]{:S(2)}) collective-permute-start(bf16[6,8,9600]{2,1,0:T(8,128)(2,1)} %collective-permute-done.16.rest_1_), channel_id=1, source_target_pairs={{0,2},{1,3},{2,0},{3,1},{4,6},{5,7},{6,4},{7,5},{8,10},{9,11},{10,... | collective-permute-start | bytes 2764808 | tf_op jit(solution)/shard_map/ppermute | solution.py:463
  183.0 42.5 %collective-permute-start.21 = (bf16[7,8,9600]{2,1,0:T(8,128)(2,1)}, bf16[7,8,9600]{2,1,0:T(8,128)(2,1)}, u32[]{:S(2)}, u32[]{:S(2)}) collective-permute-start(bf16[7,8,9600]{2,1,0:T(8,128)(2,1)} %collective-permute-done.15.rest_0_), channel_id=1, source_target_pairs={{0,4},{1,5},{2,6},{3,7},{4,0},{5,1},{6,2},{7,3},{8,12},{9,13},{10,... | collective-permute-start | bytes 3225608 | tf_op jit(solution)/shard_map/ppermute | solution.py:463
  211.1 40.6 %collective-permute-start.22 = (bf16[12,8,9600]{2,1,0:T(8,128)(2,1)}, bf16[12,8,9600]{2,1,0:T(8,128)(2,1)S(1)}, u32[]{:S(2)}, u32[]{:S(2)}) collective-permute-start(bf16[12,8,9600]{2,1,0:T(8,128)(2,1)} %collective-permute-done.17.rest_2_), channel_id=1, source_target_pairs={{0,8},{1,9},{2,10},{3,11},{4,12},{5,13},{6,14},{7,15},{8,24},{9,25... | collective-permute-start | bytes 5529608 | tf_op jit(solution)/shard_map/ppermute | solution.py:463
  211.9 40.7 %collective-permute-start.24 = (bf16[6,8,9600]{2,1,0:T(8,128)(2,1)S(1)}, bf16[6,8,9600]{2,1,0:T(8,128)(2,1)}, u32[]{:S(2)}, u32[]{:S(2)}) collective-permute-start(bf16[6,8,9600]{2,1,0:T(8,128)(2,1)S(1)} %slice.73), channel_id=1, source_target_pairs={{0,4},{1,5},{2,6},{3,7},{4,0},{5,1},{6,2},{7,3},{8,12},{9,13},{10,... | collective-permute-start | bytes 2764808 | tf_op jit(solution)/shard_map/ppermute | solution.py:463
  213.3 39.2 %collective-permute-start.23 = (bf16[7,8,9600]{2,1,0:T(8,128)(2,1)S(1)}, bf16[7,8,9600]{2,1,0:T(8,128)(2,1)S(1)}, u32[]{:S(2)}, u32[]{:S(2)}) collective-permute-start(bf16[7,8,9600]{2,1,0:T(8,128)(2,1)S(1)} %slice.72), channel_id=1, source_target_pairs={{0,2},{1,3},{2,0},{3,1},{4,6},{5,7},{6,4},{7,5},{8,10},{9,11},{10,... | collective-permute-start | bytes 3225608 | tf_op jit(solution)/shard_map/ppermute | solution.py:463
  225.4 38.3 %collective-permute-start.25 = (bf16[6,8,9600]{2,1,0:T(8,128)(2,1)S(1)}, bf16[6,8,9600]{2,1,0:T(8,128)(2,1)}, u32[]{:S(2)}, u32[]{:S(2)}) collective-permute-start(bf16[6,8,9600]{2,1,0:T(8,128)(2,1)S(1)} %slice.73), channel_id=1, source_target_pairs={{0,2},{1,3},{2,0},{3,1},{4,6},{5,7},{6,4},{7,5},{8,10},{9,11},{10,... | collective-permute-start | bytes 2764808 | tf_op jit(solution)/shard_map/ppermute | solution.py:463
  227.5 40.8 %collective-permute-start.26 = (bf16[7,8,9600]{2,1,0:T(8,128)(2,1)S(1)}, bf16[7,8,9600]{2,1,0:T(8,128)(2,1)}, u32[]{:S(2)}, u32[]{:S(2)}) collective-permute-start(bf16[7,8,9600]{2,1,0:T(8,128)(2,1)S(1)} %slice.72), channel_id=1, source_target_pairs={{0,4},{1,5},{2,6},{3,7},{4,0},{5,1},{6,2},{7,3},{8,12},{9,13},{10,... | collective-permute-start | bytes 3225608 | tf_op jit(solution)/shard_map/ppermute | solution.py:463
  251.7 16.6 %copy-start.13 = (bf16[12,8,9600]{2,1,0:T(8,128)(2,1)}, bf16[12,8,9600]{2,1,0:T(8,128)(2,1)S(1)}, u32[]{:S(2)}) copy-start(bf16[12,8,9600]{2,1,0:T(8,128)(2,1)S(1)} %collective-permute-done.22.rest_0_) | copy-start | bytes 5529604
  251.7 38.8 %collective-permute-start.27 = (bf16[12,8,9600]{2,1,0:T(8,128)(2,1)S(1)}, bf16[12,8,9600]{2,1,0:T(8,128)(2,1)}, u32[]{:S(2)}, u32[]{:S(2)}) collective-permute-start(bf16[12,8,9600]{2,1,0:T(8,128)(2,1)S(1)} %collective-permute-done.22.rest_0_), channel_id=1, source_target_pairs={{0,8},{1,9},{2,10},{3,11},{4,12},{5,13},{6,14},{7,15},{8,24},{9,25... | collective-permute-start | bytes 5529608 | tf_op jit(solution)/shard_map/ppermute | solution.py:463
  252.6 15.7 %copy-start.14 = (bf16[7,8,9600]{2,1,0:T(8,128)(2,1)}, bf16[7,8,9600]{2,1,0:T(8,128)(2,1)S(1)}, u32[]{:S(2)}) copy-start(bf16[7,8,9600]{2,1,0:T(8,128)(2,1)S(1)} %collective-permute-done.23.rest_1_) | copy-start | bytes 3225604
  252.6 29.5 %collective-permute-start.28 = (bf16[6,8,9600]{2,1,0:T(8,128)(2,1)}, bf16[6,8,9600]{2,1,0:T(8,128)(2,1)}, u32[]{:S(2)}, u32[]{:S(2)}) collective-permute-start(bf16[6,8,9600]{2,1,0:T(8,128)(2,1)} %collective-permute-done.24.rest_2_), channel_id=1, source_target_pairs={{0,2},{1,3},{2,0},{3,1},{4,6},{5,7},{6,4},{7,5},{8,10},{9,11},{10,... | collective-permute-start | bytes 2764808 | tf_op jit(solution)/shard_map/ppermute | solution.py:463
  253.3 37.2 %collective-permute-start.29 = (bf16[7,8,9600]{2,1,0:T(8,128)(2,1)S(1)}, bf16[7,8,9600]{2,1,0:T(8,128)(2,1)}, u32[]{:S(2)}, u32[]{:S(2)}) collective-permute-start(bf16[7,8,9600]{2,1,0:T(8,128)(2,1)S(1)} %collective-permute-done.23.rest_1_), channel_id=1, source_target_pairs={{0,4},{1,5},{2,6},{3,7},{4,0},{5,1},{6,2},{7,3},{8,12},{9,13},{10,... | collective-permute-start | bytes 3225608 | tf_op jit(solution)/shard_map/ppermute | solution.py:463
  290.4 8.6 %copy-start.12 = (pred[32]{0:T(512)(128)(4,1)S(1)}, pred[32]{0:T(512)(128)(4,1)}, u32[]{:S(2)}) copy-start(pred[32]{0:T(512)(128)(4,1)} %broadcast_in_dim.39) | copy-start | bytes 100
Sparse Core Ops, SparseCore 0:
  8.9 62.0 all-gather.1

commit v12 on v11

--- a/solution.py
+++ b/solution.py
@@ -98,7 +98,7 @@
     )(one_w, two_w, three_w)
 
 
-def list_kernel(idx_dev, k_count, pairs, bounds, who_ref, ids_ref, queries_ref, *lists):
+def list_kernel(idx_dev, k_count, pairs, bounds, who_ref, ids_ref, any_ref, queries_ref, *lists):
     chip, core = who_ref[0], who_ref[1]
     bits = chip_bits(idx_dev)
     begin = chip << bits
@@ -108,15 +108,20 @@
         for b in range(buffers):
             def one_of(t, n):
                 packed = queries_ref[t]
-                row, first = packed & 255, ((packed >> 8) & 255) * k_count
+                query = (packed >> 8) & 255
                 sender = who_ref[2 + (packed >> 16)]
-                base = ((sender * pairs + first) << (8 + bits)) + (row << bits)
                 line = 2 * sender + core
-                for k in range(k_count):
-                    vid = ids_ref[line, first + k] - begin
-                    list_ref[n] = base + (k << (8 + bits)) + (vid & ((1 << bits) - 1))
-                    n = n + ((vid >> bits) == 0).astype(jnp.int32)
-                return n
+
+                def some(n):
+                    first = query * k_count
+                    base = ((sender * pairs + first) << (8 + bits)) + ((packed & 255) << bits)
+                    for k in range(k_count):
+                        vid = ids_ref[line, first + k] - begin
+                        list_ref[n] = base + (k << (8 + bits)) + (vid & ((1 << bits) - 1))
+                        n = n + ((vid >> bits) == 0).astype(jnp.int32)
+                    return n
+
+                return lax.cond(any_ref[line, query] > 0, some, lambda n: n, n)
             at = lax.fori_loop(bounds[p][b], bounds[p][b + 1], one_of, at)
             list_ref[b] = at - buffers
         for i in range(GROUP):
@@ -129,17 +134,19 @@
     return bits
 
 
-def pair_lists(who, ids, queries, bounds, caps, k_count, idx_dev):
+def pair_lists(who, ids, chip, queries, bounds, caps, k_count, idx_dev):
     smem = pl.BlockSpec(memory_space=pltpu.SMEM)
     sizes = [len(b) - 1 + cap + GROUP for b, cap in zip(bounds, caps)]
+    found = (ids // (2 * idx_dev) == chip).astype(jnp.int32)
+    found = jnp.sum(found.reshape(ids.shape[0], -1, k_count), axis=2)
     return pl.pallas_call(
         functools.partial(list_kernel, idx_dev, k_count, ids.shape[1], bounds),
         out_shape=[jax.ShapeDtypeStruct((n,), jnp.int32) for n in sizes],
-        in_specs=[smem] * 3,
+        in_specs=[smem] * 4,
         out_specs=[smem] * len(sizes),
         cost_estimate=pl.CostEstimate(flops=10**7, bytes_accessed=10**6, transcendentals=0),
         name="pair_lists",
-    )(who, ids, queries)
+    )(who, ids, found, queries)
 
 
 def pair_kernel(frames, idx_dev, buffers, scale, list_ref, one_ref, two_ref, three_ref, before_ref,
@@ -385,15 +392,18 @@
     me = lax.axis_index("shard")
     chip, core = me // 2, me % 2
 
-    rings = [tuple(ring_position(c, n) for c, n in zip(p, sizes)) for p in places]
-    where = {r: i for i, r in enumerate(rings)}
+    rings = [[tuple(ring_position(c, n) for c, n in zip(p, sizes)) for p in places]] * 2
+    if sizes[1] == sizes[2]:
+        rings[1] = [(z, x, y) for z, y, x in rings[0]]
+    where = [{r: i for i, r in enumerate(rings[c])} for c in range(2)]
 
     def step_along(axis):
         out = []
-        for i, ring in enumerate(rings):
-            to = list(ring)
-            to[axis] = (to[axis] + 1) % sizes[axis]
-            out += [(2 * i + c, 2 * where[tuple(to)] + c) for c in range(2)]
+        for i in range(chips):
+            for c in range(2):
+                to = list(rings[c][i])
+                to[axis] = (to[axis] + 1) % sizes[axis]
+                out.append((2 * i + c, 2 * where[c][tuple(to)] + c))
         return out
 
     videos = lax.all_gather(
@@ -411,11 +421,11 @@
         phases[next(i for i, e in enumerate(ends) if gather.arrival[key] <= e)].append(key)
     offsets = [(z, y, x) for z in range(sizes[0]) for y in range(sizes[1]) for x in range(sizes[2])]
     back = np.array(
-        [[where[tuple((r - o) % n for r, o, n in zip(ring, off, sizes))] for off in offsets]
-         for ring in rings], np.int32,
+        [[where[c][tuple((r - o) % n for r, o, n in zip(rings[c][i], off, sizes))] for off in offsets]
+         for i in range(chips) for c in range(2)], np.int32,
     )
     who = jnp.concatenate(
-        [jnp.stack([chip, core]), lax.dynamic_index_in_dim(jnp.asarray(back), chip, 0, keepdims=False)]
+        [jnp.stack([chip, core]), lax.dynamic_index_in_dim(jnp.asarray(back), me, 0, keepdims=False)]
     )
 
     contents, bounds, caps = [], [], []
@@ -471,7 +481,7 @@
         if i == min(LISTS, total - 1):
             later = lax.optimization_barrier((who, *done[i]))[0]
             state["lists"] = pair_lists(
-                later, state["ids"], contents, bounds, caps, k_count, idx_dev
+                later, state["ids"], chip, contents, bounds, caps, k_count, idx_dev
             )
     while len(tables) <= len(ends):
         score()

time: 324 us -> 341 us (1.052)
  waiting for transfers between devices: 146 us -> 171 us
    all_to_all x1, waiting for transfers between devices: 0.01 us -> 30.2 us  [body(): lax.all_to_all(jnp.broadcast_to(ids, (devices, pairs)), 'shard', split_ax...]
    ppermute x30, waiting for transfers between devices: 146 us -> 140 us  [body(): gather.blocks[target] = lax.ppermute(block, 'shard', gather.steps[axis])]
  transfers between devices with their start and end apart: 32 -> 32, of which waited for: 17 -> 10; matrix products, arithmetic and copies ran while one was open for 8% -> 8% of each run, Pallas kernels for 21% -> 19%
where the time goes in v12:
time: 341 us
  waiting for transfers between devices  171 us (50%)
  Pallas kernels  73.7 us (22%)
  starting transfers between devices  39.3 us (12%)
  local copies, waits for them, and re-layouts  30.3 us (9%)
  between operations  13.7 us (4%)
  blocking collectives  12.4 us (4%)
    ppermute x30, waiting for transfers between devices, body(): gather.blocks[target] = lax.ppermute(block, 'shard', gather.steps[axis])  140 us
    pallas_call x5, Pallas kernels, pair_scores(): pl.pallas_call(functools.partial(pair_kernel, frames, idx_dev, len(blocks...  53.2 us
    ppermute x30, starting transfers between devices, body(): gather.blocks[target] = lax.ppermute(block, 'shard', gather.steps[axis])  34.3 us
    all_to_all x1, waiting for transfers between devices, body(): lax.all_to_all(jnp.broadcast_to(ids, (devices, pairs)), 'shard', split_ax...  30.2 us
    unnamed x37, local copies, waits for them, and re-layouts  14.8 us
    all_to_all x1, blocking collectives, body(): lax.all_to_all(table.reshape(devices, pairs), 'shard', split_axis=0, conc...  12.4 us
    pallas_call x1, Pallas kernels, pair_lists(): pl.pallas_call(functools.partial(list_kernel, idx_dev, k_count, ids.shape...  11.9 us
    slice x8, local copies, waits for them, and re-layouts, block(): parts = [b[at:at + n] for b, (_, at, n) in zip(whole, self.pieces[key])]  8.71 us
  transfers between devices with their start and end apart: 32, of which 10 were waited for; matrix products, arithmetic and copies ran while one was open for 8% of the time, Pallas kernels for 19%

profile of v12, /device:TPU:0, one launch (start us, length us, event | category | flops | bytes accessed | tf_op | source)
XLA Modules:
  0.0 340.8 jit_solution(5222133662441733662)
XLA Ops:
  6.5 0.7 all-gather.2.cloned.1.call-update
  7.3 1.0 copy-done.4
  8.2 1.6 fusion.4
  9.8 3.0 collective-permute-start
  12.8 1.5 collective-permute-start.1
  14.3 1.4 slice.53
  15.7 1.6 collective-permute-start.4
  18.4 22.1 %collective-permute-done.rest_2_ = bf16[8,8,9600]{2,1,0:T(8,128)(2,1)} collective-permute-done((bf16[8,8,9600]{2,1,0:T(8,128)(2,1)}, bf16[8,8,9600]{2,1,0:T(8,128)(2,1)}, u32[]{:S(2)}, u32[]{:S(2)}) %collective-permute-start) | collective-permute-done | bytes 1228832 | tf_op jit(solution)/shard_map/ppermute | solution.py:473
  40.5 2.6 collective-permute-done.1.rest_1_
  43.1 1.5 collective-permute-start.2
  45.2 0.7 dynamic-slice_bitcast_fusion
  46.6 0.6 broadcast_in_dim.42
  47.3 4.9 %all-to-all-start = ((s32[32,1,128]{2,1,0:T(1,128)}), s32[32,1,128]{2,1,0:T(1,128)S(1)}, u32[]{:S(2)}, u32[]{:S(2)}) async-start(s32[32,1,128]{2,1,0:T(1,128)} %broadcast_in_dim.42), calls=%async_computation | async-start | bytes 32768 | tf_op jit(solution)/shard_map/all_to_all | solution.py:477
  52.2 8.5 %head_matrices.1 = (bf16[64,2048]{1,0:T(8,128)(2,1)S(1)}, bf16[512,1024]{1,0:T(8,128)(2,1)S(1)}, bf16[256,256]{1,0:T(8,128)(2,1)S(1)}) custom-call(bf16[9,1,32]{2,1,0:T(2,128)(2,1)S(1)} %reshape.76.one_w, bf16[9,32,64]{2,1,0:T(8,128)(2,1)S(1)} %bitcast.34, bf16[9,1,64]{2,1,0:T(2,128)(2,1)S(1)} %reshape.77.three_w), custom_call_target="tpu_custom_call" | custom-call | flops 1000000000 | bytes 3000000 | tf_op jit(solution)/shard_map/head_matrices/pallas_call | solution.py:89
  60.8 1.0 copy-done.1
  61.8 0.7 copy-done.2
  62.5 0.6 copy-done.3
  63.1 0.7 broadcast_in_dim.39
  63.8 30.2 %all-to-all-done = s32[32,1,128]{2,1,0:T(1,128)S(1)} async-done(((s32[32,1,128]{2,1,0:T(1,128)}), s32[32,1,128]{2,1,0:T(1,128)S(1)}, u32[]{:S(2)}, u32[]{:S(2)}) %all-to-all-start) | async-done | bytes 16416 | tf_op jit(solution)/shard_map/all_to_all | solution.py:477
  94.2 0.7 copy.30.any_ref
  94.9 1.0 slice.69
  96.0 1.8 collective-permute-start.9
  97.8 0.7 collective-permute-start.8
  98.5 1.6 collective-permute-start.7
  100.1 1.3 collective-permute-start.10
  102.0 1.6 slice_dynamic-update-slice_fusion.7
  103.5 1.6 slice_dynamic-update-slice_fusion.6
  105.1 1.6 slice_dynamic-update-slice_fusion.5
  106.7 1.6 slice_dynamic-update-slice_fusion.4
  108.3 1.7 slice_dynamic-update-slice_fusion.3
  110.0 1.7 slice_dynamic-update-slice_fusion.2
  111.7 1.7 slice_dynamic-update-slice_fusion.1
  113.4 11.9 %pair_lists.1 = (s32[152]{0:T(256)}, s32[152]{0:T(256)}, s32[151]{0:T(256)}, s32[149]{0:T(256)}, s32[83]{0:T(128)}) custom-call(s32[18]{0:T(128)} %pad_add_fusion.who_ref, s32[32,128]{1,0:T(8,128)} %bitcast.35, s32[32,16]{1,0:T(8,128)} %copy.30.any_ref, s32[256]{0:T(256)} %constant.55.clone.queries_ref), custom_call_target="tpu_custom_call" | custom-call | flops 10000000 | bytes 1000000 | tf_op jit(solution)/shard_map/pair_lists/pallas_call | solution.py:142
  125.3 19.2 %collective-permute-done.7.rest_0_ = bf16[13,8,9600]{2,1,0:T(8,128)(2,1)} collective-permute-done((bf16[13,8,9600]{2,1,0:T(8,128)(2,1)S(1)}, bf16[13,8,9600]{2,1,0:T(8,128)(2,1)}, u32[]{:S(2)}, u32[]{:S(2)}) %collective-permute-start.7) | collective-permute-done | bytes 1996832 | tf_op jit(solution)/shard_map/ppermute | solution.py:473
  144.5 1.3 collective-permute-start.13
  146.3 0.7 collective-permute-start.12
  147.0 2.2 slice.71
  149.2 2.3 slice.70
  152.1 14.3 %phase_0.1.before_ref = f32[16,128]{1,0:T(8,128)} custom-call(s32[152]{0:T(256)} %get-tuple-element.65.list_ref, bf16[64,2048]{1,0:T(8,128)(2,1)} %copy-done.2, bf16[512,1024]{1,0:T(8,128)(2,1)} %copy-done.1, bf16[256,256]{1,0:T(8,128)(2,1)} %copy-done.3, f32[16,128]{1,0:T(8,128)} %broadcast_in_dim.43.before_ref, ...), custom_call_target="tpu_custom_call" | custom-call | flops 100663296000 | bytes 39321600 | tf_op jit(solution)/shard_map/phase_0/pallas_call | solution.py:264
  166.4 1.5 collective-permute-start.16
  167.9 2.7 collective-permute-start.15
  170.6 1.7 slice_dynamic-update-slice_fusion
  172.4 18.6 %collective-permute-done.12.rest_5_ = bf16[13,8,9600]{2,1,0:T(8,128)(2,1)S(1)} collective-permute-done((bf16[13,8,9600]{2,1,0:T(8,128)(2,1)}, bf16[13,8,9600]{2,1,0:T(8,128)(2,1)S(1)}, u32[]{:S(2)}, u32[]{:S(2)}) %collective-permute-start.12) | collective-permute-done | bytes 1996832 | tf_op jit(solution)/shard_map/ppermute | solution.py:473
  191.6 1.5 collective-permute-start.19
  193.2 0.9 collective-permute-start.17
  194.2 1.4 collective-permute-start.20
  196.1 10.4 %phase_1.1.before_ref = f32[16,128]{1,0:T(8,128)} custom-call(s32[152]{0:T(256)} %get-tuple-element.64.list_ref, bf16[64,2048]{1,0:T(8,128)(2,1)} %copy-done.2, bf16[512,1024]{1,0:T(8,128)(2,1)} %copy-done.1, bf16[256,256]{1,0:T(8,128)(2,1)} %copy-done.3, f32[16,128]{1,0:T(8,128)} %phase_0.1.before_ref, ...), custom_call_target="tpu_custom_call" | custom-call | flops 100663296000 | bytes 39321600 | tf_op jit(solution)/shard_map/phase_1/pallas_call | solution.py:264
  206.5 27.1 %collective-permute-done.17.rest_2_ = bf16[12,8,9600]{2,1,0:T(8,128)(2,1)} collective-permute-done((bf16[12,8,9600]{2,1,0:T(8,128)(2,1)}, bf16[12,8,9600]{2,1,0:T(8,128)(2,1)}, u32[]{:S(2)}, u32[]{:S(2)}) %collective-permute-start.17) | collective-permute-done | bytes 1843232 | tf_op jit(solution)/shard_map/ppermute | solution.py:473
  233.6 0.8 collective-permute-start.22
  235.0 1.3 collective-permute-start.23
  236.3 0.7 collective-permute-start.25
  237.0 1.5 collective-permute-start.26
  238.5 10.3 %phase_2.1.before_ref = f32[16,128]{1,0:T(8,128)} custom-call(s32[151]{0:T(256)} %get-tuple-element.63.list_ref, bf16[64,2048]{1,0:T(8,128)(2,1)} %copy-done.2, bf16[512,1024]{1,0:T(8,128)(2,1)} %copy-done.1, bf16[256,256]{1,0:T(8,128)(2,1)} %copy-done.3, f32[16,128]{1,0:T(8,128)} %phase_1.1.before_ref, ...), custom_call_target="tpu_custom_call" | custom-call | flops 100663296000 | bytes 39321600 | tf_op jit(solution)/shard_map/phase_2/pallas_call | solution.py:264
  248.8 25.4 %collective-permute-done.22.rest_0_ = bf16[12,8,9600]{2,1,0:T(8,128)(2,1)S(1)} collective-permute-done((bf16[12,8,9600]{2,1,0:T(8,128)(2,1)}, bf16[12,8,9600]{2,1,0:T(8,128)(2,1)S(1)}, u32[]{:S(2)}, u32[]{:S(2)}) %collective-permute-start.22) | collective-permute-done | bytes 1843232 | tf_op jit(solution)/shard_map/ppermute | solution.py:473
  274.2 0.9 collective-permute-start.27
  275.1 1.4 collective-permute-start.28
  277.0 4.5 %collective-permute-done.25.rest_3_ = bf16[6,8,9600]{2,1,0:T(8,128)(2,1)} collective-permute-done((bf16[6,8,9600]{2,1,0:T(8,128)(2,1)S(1)}, bf16[6,8,9600]{2,1,0:T(8,128)(2,1)}, u32[]{:S(2)}, u32[]{:S(2)}) %collective-permute-start.25) | collective-permute-done | bytes 921632 | tf_op jit(solution)/shard_map/ppermute | solution.py:473
  281.5 10.3 %phase_3.1.before_ref = f32[16,128]{1,0:T(8,128)} custom-call(s32[149]{0:T(256)} %get-tuple-element.62.list_ref, bf16[64,2048]{1,0:T(8,128)(2,1)} %copy-done.2, bf16[512,1024]{1,0:T(8,128)(2,1)} %copy-done.1, bf16[256,256]{1,0:T(8,128)(2,1)} %copy-done.3, f32[16,128]{1,0:T(8,128)} %phase_2.1.before_ref, ...), custom_call_target="tpu_custom_call" | custom-call | flops 100663296000 | bytes 39321600 | tf_op jit(solution)/shard_map/phase_3/pallas_call | solution.py:264
  291.9 7.1 %collective-permute-done.28.rest_1_ = bf16[6,8,9600]{2,1,0:T(8,128)(2,1)} collective-permute-done((bf16[6,8,9600]{2,1,0:T(8,128)(2,1)}, bf16[6,8,9600]{2,1,0:T(8,128)(2,1)}, u32[]{:S(2)}, u32[]{:S(2)}) %collective-permute-start.28) | collective-permute-done | bytes 921632 | tf_op jit(solution)/shard_map/ppermute | solution.py:473
  299.0 13.2 %collective-permute-done.27.rest_0_ = bf16[12,8,9600]{2,1,0:T(8,128)(2,1)} collective-permute-done((bf16[12,8,9600]{2,1,0:T(8,128)(2,1)S(1)}, bf16[12,8,9600]{2,1,0:T(8,128)(2,1)}, u32[]{:S(2)}, u32[]{:S(2)}) %collective-permute-start.27) | collective-permute-done | bytes 1843232 | tf_op jit(solution)/shard_map/ppermute | solution.py:473
  312.2 7.8 %phase_4.1 = f32[16,128]{1,0:T(8,128)} custom-call(s32[83]{0:T(128)} %get-tuple-element.58.list_ref, bf16[64,2048]{1,0:T(8,128)(2,1)} %copy-done.2, bf16[512,1024]{1,0:T(8,128)(2,1)} %copy-done.1, bf16[256,256]{1,0:T(8,128)(2,1)} %copy-done.3, f32[16,128]{1,0:T(8,128)} %phase_3.1.before_ref, bf16[256,8,9600]{2,1,0:T(8,128)(2,1)} %all-gather.2.cloned.1.call-done.v_hbm, ...), custom_call_target="tpu_custom_call" | custom-call | flops 50331648000 | bytes 19660800 | tf_op jit(solution)/shard_map/phase_4/pallas_call | solution.py:264
  320.0 0.7 broadcast_in_dim.44
  320.8 12.4 %all_to_all.17 = f32[32,1,128]{2,1,0:T(1,128)S(1)} all-to-all(f32[32,1,128]{2,1,0:T(1,128)S(1)} %broadcast_select_fusion), channel_id=1, replica_groups=mesh['shard'=32] {'shard'}, dimensions={0} | all-to-all | bytes 32768 | tf_op jit(solution)/shard_map/all_to_all | solution.py:489
  333.3 0.7 copy.34
  (74 shorter events, 6.7 us)
Async XLA Ops:
  6.5 1.7 copy-start.4
  6.5 145.0 %all-gather.2.cloned.1.call-start = ((), (), s32[]{:S(2)}) async-start(), calls=%async_computation.2 | async-start | bytes 58982400 | tf_op jit(solution)/shard_map/all_gather | solution.py:409
  9.8 35.3 %copy-start.10 = (bf16[32,1,3,3]{0,3,2,1:T(4,128)(2,1)S(1)}, bf16[32,1,3,3]{0,3,2,1:T(4,128)(2,1)}, u32[]{:S(2)}) copy-start(bf16[32,1,3,3]{0,3,2,1:T(4,128)(2,1)} %param.11) | copy-start | bytes 1732
  9.8 35.3 %copy-start.11 = (bf16[1,64,3,3]{1,3,2,0:T(4,128)(2,1)S(1)}, bf16[1,64,3,3]{1,3,2,0:T(4,128)(2,1)}, u32[]{:S(2)}) copy-start(bf16[1,64,3,3]{1,3,2,0:T(4,128)(2,1)} %param.13) | copy-start | bytes 3460
  9.8 36.7 %copy-start.9 = (s32[16,8]{0,1:T(8,128)S(1)}, s32[16,8]{0,1:T(8,128)}, u32[]{:S(2)}) copy-start(s32[16,8]{0,1:T(8,128)} %param.10) | copy-start | bytes 1540
  9.8 42.4 %copy-start = (bf16[64,32,3,3]{0,1,3,2:T(8,128)(2,1)S(1)}, bf16[64,32,3,3]{0,1,3,2:T(8,128)(2,1)}, u32[]{:S(2)}) copy-start(bf16[64,32,3,3]{0,1,3,2:T(8,128)(2,1)} %param.12) | copy-start | bytes 110596
  9.8 30.7 %collective-permute-start = (bf16[8,8,9600]{2,1,0:T(8,128)(2,1)}, bf16[8,8,9600]{2,1,0:T(8,128)(2,1)}, u32[]{:S(2)}, u32[]{:S(2)}) collective-permute-start(bf16[8,8,9600]{2,1,0:T(8,128)(2,1)} %get-tuple-element.82), channel_id=1, source_target_pairs={{0,4},{1,3},{2,6},{3,1},{4,0},{5,7},{6,2},{7,5},{8,12},{9,11},{10,... | collective-permute-start | bytes 3686408 | tf_op jit(solution)/shard_map/ppermute | solution.py:473
  12.8 30.3 %collective-permute-start.1 = (bf16[8,8,9600]{2,1,0:T(8,128)(2,1)}, bf16[8,8,9600]{2,1,0:T(8,128)(2,1)}, u32[]{:S(2)}, u32[]{:S(2)}) collective-permute-start(bf16[8,8,9600]{2,1,0:T(8,128)(2,1)} %get-tuple-element.78), channel_id=1, source_target_pairs={{0,2},{1,5},{2,0},{3,7},{4,6},{5,1},{6,4},{7,3},{8,10},{9,13},{10,... | collective-permute-start | bytes 3686408 | tf_op jit(solution)/shard_map/ppermute | solution.py:473
  15.7 79.2 %collective-permute-start.4 = (bf16[13,8,9600]{2,1,0:T(8,128)(2,1)}, bf16[13,8,9600]{2,1,0:T(8,128)(2,1)S(1)}, u32[]{:S(2)}, u32[]{:S(2)}) collective-permute-start(bf16[13,8,9600]{2,1,0:T(8,128)(2,1)} %slice.53), channel_id=1, source_target_pairs={{0,8},{1,9},{2,10},{3,11},{4,12},{5,13},{6,14},{7,15},{8,24},{9,25... | collective-permute-start | bytes 5990408 | tf_op jit(solution)/shard_map/ppermute | solution.py:473
  17.3 78.7 %collective-permute-start.5 = (bf16[8,8,9600]{2,1,0:T(8,128)(2,1)}, bf16[8,8,9600]{2,1,0:T(8,128)(2,1)}, u32[]{:S(2)}, u32[]{:S(2)}) collective-permute-start(bf16[8,8,9600]{2,1,0:T(8,128)(2,1)} %get-tuple-element.66), channel_id=1, source_target_pairs={{0,2},{1,5},{2,0},{3,7},{4,6},{5,1},{6,4},{7,3},{8,10},{9,13},{10,... | collective-permute-start | bytes 3686408 | tf_op jit(solution)/shard_map/ppermute | solution.py:473
  17.9 78.2 %collective-permute-start.6 = (bf16[8,8,9600]{2,1,0:T(8,128)(2,1)}, bf16[8,8,9600]{2,1,0:T(8,128)(2,1)}, u32[]{:S(2)}, u32[]{:S(2)}) collective-permute-start(bf16[8,8,9600]{2,1,0:T(8,128)(2,1)} %get-tuple-element.67), channel_id=1, source_target_pairs={{0,4},{1,3},{2,6},{3,1},{4,0},{5,7},{6,2},{7,5},{8,12},{9,11},{10,... | collective-permute-start | bytes 3686408 | tf_op jit(solution)/shard_map/ppermute | solution.py:473
  43.1 57.0 %collective-permute-start.2 = (bf16[8,8,9600]{2,1,0:T(8,128)(2,1)}, bf16[8,8,9600]{2,1,0:T(8,128)(2,1)}, u32[]{:S(2)}, u32[]{:S(2)}) collective-permute-start(bf16[8,8,9600]{2,1,0:T(8,128)(2,1)} %collective-permute-done.rest_2_), channel_id=1, source_target_pairs={{0,2},{1,5},{2,0},{3,7},{4,6},{5,1},{6,4},{7,3},{8,10},{9,13},{10,... | collective-permute-start | bytes 3686408 | tf_op jit(solution)/shard_map/ppermute | solution.py:473
  44.6 55.5 %collective-permute-start.3 = (bf16[8,8,9600]{2,1,0:T(8,128)(2,1)}, bf16[8,8,9600]{2,1,0:T(8,128)(2,1)}, u32[]{:S(2)}, u32[]{:S(2)}) collective-permute-start(bf16[8,8,9600]{2,1,0:T(8,128)(2,1)} %collective-permute-done.1.rest_1_), channel_id=1, source_target_pairs={{0,4},{1,3},{2,6},{3,1},{4,0},{5,7},{6,2},{7,5},{8,12},{9,11},{10,... | collective-permute-start | bytes 3686408 | tf_op jit(solution)/shard_map/ppermute | solution.py:473
  47.3 46.8 %all-to-all-start = ((s32[32,1,128]{2,1,0:T(1,128)}), s32[32,1,128]{2,1,0:T(1,128)S(1)}, u32[]{:S(2)}, u32[]{:S(2)}) async-start(s32[32,1,128]{2,1,0:T(1,128)} %broadcast_in_dim.42), calls=%async_computation | async-start | bytes 32768 | tf_op jit(solution)/shard_map/all_to_all | solution.py:477
  60.7 1.0 copy-start.1
  61.8 0.7 copy-start.2
  62.5 0.7 copy-start.3
  94.1 2.0 copy-start.8
  94.9 3.6 %copy-start.5 = (bf16[13,8,9600]{2,1,0:T(8,128)(2,1)}, bf16[13,8,9600]{2,1,0:T(8,128)(2,1)S(1)}, u32[]{:S(2)}) copy-start(bf16[13,8,9600]{2,1,0:T(8,128)(2,1)S(1)} %collective-permute-done.4.rest_3_) | copy-start | bytes 5990404
  96.0 29.3 %collective-permute-start.9 = (bf16[6,8,9600]{2,1,0:T(8,128)(2,1)}, bf16[6,8,9600]{2,1,0:T(8,128)(2,1)}, u32[]{:S(2)}, u32[]{:S(2)}) collective-permute-start(bf16[6,8,9600]{2,1,0:T(8,128)(2,1)} %slice.69), channel_id=1, source_target_pairs={{0,4},{1,3},{2,6},{3,1},{4,0},{5,7},{6,2},{7,5},{8,12},{9,11},{10,... | collective-permute-start | bytes 2764808 | tf_op jit(solution)/shard_map/ppermute | solution.py:473
  97.8 27.5 %collective-permute-start.8 = (bf16[7,8,9600]{2,1,0:T(8,128)(2,1)S(1)}, bf16[7,8,9600]{2,1,0:T(8,128)(2,1)}, u32[]{:S(2)}, u32[]{:S(2)}) collective-permute-start(bf16[7,8,9600]{2,1,0:T(8,128)(2,1)S(1)} %slice.68), channel_id=1, source_target_pairs={{0,2},{1,5},{2,0},{3,7},{4,6},{5,1},{6,4},{7,3},{8,10},{9,13},{10,... | collective-permute-start | bytes 3225608 | tf_op jit(solution)/shard_map/ppermute | solution.py:473
  98.5 45.9 %collective-permute-start.7 = (bf16[13,8,9600]{2,1,0:T(8,128)(2,1)S(1)}, bf16[13,8,9600]{2,1,0:T(8,128)(2,1)}, u32[]{:S(2)}, u32[]{:S(2)}) collective-permute-start(bf16[13,8,9600]{2,1,0:T(8,128)(2,1)S(1)} %collective-permute-done.4.rest_3_), channel_id=1, source_target_pairs={{0,8},{1,9},{2,10},{3,11},{4,12},{5,13},{6,14},{7,15},{8,24},{9,25... | collective-permute-start | bytes 5990408 | tf_op jit(solution)/shard_map/ppermute | solution.py:473
  100.1 66.3 %collective-permute-start.10 = (bf16[6,8,9600]{2,1,0:T(8,128)(2,1)}, bf16[6,8,9600]{2,1,0:T(8,128)(2,1)}, u32[]{:S(2)}, u32[]{:S(2)}) collective-permute-start(bf16[6,8,9600]{2,1,0:T(8,128)(2,1)} %slice.69), channel_id=1, source_target_pairs={{0,2},{1,5},{2,0},{3,7},{4,6},{5,1},{6,4},{7,3},{8,10},{9,13},{10,... | collective-permute-start | bytes 2764808 | tf_op jit(solution)/shard_map/ppermute | solution.py:473
  101.5 65.0 %collective-permute-start.11 = (bf16[7,8,9600]{2,1,0:T(8,128)(2,1)S(1)}, bf16[7,8,9600]{2,1,0:T(8,128)(2,1)}, u32[]{:S(2)}, u32[]{:S(2)}) collective-permute-start(bf16[7,8,9600]{2,1,0:T(8,128)(2,1)S(1)} %slice.68), channel_id=1, source_target_pairs={{0,4},{1,3},{2,6},{3,1},{4,0},{5,7},{6,2},{7,5},{8,12},{9,11},{10,... | collective-permute-start | bytes 3225608 | tf_op jit(solution)/shard_map/ppermute | solution.py:473
  144.5 27.9 %collective-permute-start.13 = (bf16[6,8,9600]{2,1,0:T(8,128)(2,1)}, bf16[6,8,9600]{2,1,0:T(8,128)(2,1)}, u32[]{:S(2)}, u32[]{:S(2)}) collective-permute-start(bf16[6,8,9600]{2,1,0:T(8,128)(2,1)} %collective-permute-done.9.rest_2_), channel_id=1, source_target_pairs={{0,2},{1,5},{2,0},{3,7},{4,6},{5,1},{6,4},{7,3},{8,10},{9,13},{10,... | collective-permute-start | bytes 2764808 | tf_op jit(solution)/shard_map/ppermute | solution.py:473
  145.8 26.6 %collective-permute-start.14 = (bf16[7,8,9600]{2,1,0:T(8,128)(2,1)}, bf16[7,8,9600]{2,1,0:T(8,128)(2,1)}, u32[]{:S(2)}, u32[]{:S(2)}) collective-permute-start(bf16[7,8,9600]{2,1,0:T(8,128)(2,1)} %collective-permute-done.8.rest_1_), channel_id=1, source_target_pairs={{0,4},{1,3},{2,6},{3,1},{4,0},{5,7},{6,2},{7,5},{8,12},{9,11},{10,... | collective-permute-start | bytes 3225608 | tf_op jit(solution)/shard_map/ppermute | solution.py:473
  146.3 44.8 %collective-permute-start.12 = (bf16[13,8,9600]{2,1,0:T(8,128)(2,1)}, bf16[13,8,9600]{2,1,0:T(8,128)(2,1)S(1)}, u32[]{:S(2)}, u32[]{:S(2)}) collective-permute-start(bf16[13,8,9600]{2,1,0:T(8,128)(2,1)} %collective-permute-done.7.rest_0_), channel_id=1, source_target_pairs={{0,8},{1,9},{2,10},{3,11},{4,12},{5,13},{6,14},{7,15},{8,24},{9,25... | collective-permute-start | bytes 5990408 | tf_op jit(solution)/shard_map/ppermute | solution.py:473
  152.1 15.8 %copy-start.7 = (bf16[7,8,9600]{2,1,0:T(8,128)(2,1)S(1)}, bf16[7,8,9600]{2,1,0:T(8,128)(2,1)}, u32[]{:S(2)}) copy-start(bf16[7,8,9600]{2,1,0:T(8,128)(2,1)} %slice.70) | copy-start | bytes 3225604
  166.4 27.8 %collective-permute-start.16 = (bf16[6,8,9600]{2,1,0:T(8,128)(2,1)}, bf16[6,8,9600]{2,1,0:T(8,128)(2,1)}, u32[]{:S(2)}, u32[]{:S(2)}) collective-permute-start(bf16[6,8,9600]{2,1,0:T(8,128)(2,1)} %slice.71), channel_id=1, source_target_pairs={{0,4},{1,3},{2,6},{3,1},{4,0},{5,7},{6,2},{7,5},{8,12},{9,11},{10,... | collective-permute-start | bytes 2764808 | tf_op jit(solution)/shard_map/ppermute | solution.py:473
  167.9 26.3 %collective-permute-start.15 = (bf16[7,8,9600]{2,1,0:T(8,128)(2,1)S(1)}, bf16[7,8,9600]{2,1,0:T(8,128)(2,1)}, u32[]{:S(2)}, u32[]{:S(2)}) collective-permute-start(bf16[7,8,9600]{2,1,0:T(8,128)(2,1)S(1)} %copy-done.7), channel_id=1, source_target_pairs={{0,2},{1,5},{2,0},{3,7},{4,6},{5,1},{6,4},{7,3},{8,10},{9,13},{10,... | collective-permute-start | bytes 3225608 | tf_op jit(solution)/shard_map/ppermute | solution.py:473
  191.0 2.2 copy-start.6
  191.0 43.4 %collective-permute-start.18 = (bf16[6,8,9600]{2,1,0:T(8,128)(2,1)}, bf16[6,8,9600]{2,1,0:T(8,128)(2,1)}, u32[]{:S(2)}, u32[]{:S(2)}) collective-permute-start(bf16[6,8,9600]{2,1,0:T(8,128)(2,1)} %slice.71), channel_id=1, source_target_pairs={{0,2},{1,5},{2,0},{3,7},{4,6},{5,1},{6,4},{7,3},{8,10},{9,13},{10,... | collective-permute-start | bytes 2764808 | tf_op jit(solution)/shard_map/ppermute | solution.py:473
  191.6 42.8 %collective-permute-start.19 = (bf16[7,8,9600]{2,1,0:T(8,128)(2,1)S(1)}, bf16[7,8,9600]{2,1,0:T(8,128)(2,1)}, u32[]{:S(2)}, u32[]{:S(2)}) collective-permute-start(bf16[7,8,9600]{2,1,0:T(8,128)(2,1)S(1)} %copy-done.7), channel_id=1, source_target_pairs={{0,4},{1,3},{2,6},{3,1},{4,0},{5,7},{6,2},{7,5},{8,12},{9,11},{10,... | collective-permute-start | bytes 3225608 | tf_op jit(solution)/shard_map/ppermute | solution.py:473
  193.2 40.4 %collective-permute-start.17 = (bf16[12,8,9600]{2,1,0:T(8,128)(2,1)}, bf16[12,8,9600]{2,1,0:T(8,128)(2,1)}, u32[]{:S(2)}, u32[]{:S(2)}) collective-permute-start(bf16[12,8,9600]{2,1,0:T(8,128)(2,1)} %slice_dynamic-update-slice_fusion), channel_id=1, source_target_pairs={{0,8},{1,9},{2,10},{3,11},{4,12},{5,13},{6,14},{7,15},{8,24},{9,25... | collective-permute-start | bytes 5529608 | tf_op jit(solution)/shard_map/ppermute | solution.py:473
  194.2 42.1 %collective-permute-start.20 = (bf16[6,8,9600]{2,1,0:T(8,128)(2,1)}, bf16[6,8,9600]{2,1,0:T(8,128)(2,1)}, u32[]{:S(2)}, u32[]{:S(2)}) collective-permute-start(bf16[6,8,9600]{2,1,0:T(8,128)(2,1)} %collective-permute-done.16.rest_1_), channel_id=1, source_target_pairs={{0,2},{1,5},{2,0},{3,7},{4,6},{5,1},{6,4},{7,3},{8,10},{9,13},{10,... | collective-permute-start | bytes 2764808 | tf_op jit(solution)/shard_map/ppermute | solution.py:473
  195.6 40.8 %collective-permute-start.21 = (bf16[7,8,9600]{2,1,0:T(8,128)(2,1)}, bf16[7,8,9600]{2,1,0:T(8,128)(2,1)}, u32[]{:S(2)}, u32[]{:S(2)}) collective-permute-start(bf16[7,8,9600]{2,1,0:T(8,128)(2,1)} %collective-permute-done.15.rest_0_), channel_id=1, source_target_pairs={{0,4},{1,3},{2,6},{3,1},{4,0},{5,7},{6,2},{7,5},{8,12},{9,11},{10,... | collective-permute-start | bytes 3225608 | tf_op jit(solution)/shard_map/ppermute | solution.py:473
  233.6 40.6 %collective-permute-start.22 = (bf16[12,8,9600]{2,1,0:T(8,128)(2,1)}, bf16[12,8,9600]{2,1,0:T(8,128)(2,1)S(1)}, u32[]{:S(2)}, u32[]{:S(2)}) collective-permute-start(bf16[12,8,9600]{2,1,0:T(8,128)(2,1)} %collective-permute-done.17.rest_2_), channel_id=1, source_target_pairs={{0,8},{1,9},{2,10},{3,11},{4,12},{5,13},{6,14},{7,15},{8,24},{9,25... | collective-permute-start | bytes 5529608 | tf_op jit(solution)/shard_map/ppermute | solution.py:473
  234.4 40.7 %collective-permute-start.24 = (bf16[6,8,9600]{2,1,0:T(8,128)(2,1)S(1)}, bf16[6,8,9600]{2,1,0:T(8,128)(2,1)}, u32[]{:S(2)}, u32[]{:S(2)}) collective-permute-start(bf16[6,8,9600]{2,1,0:T(8,128)(2,1)S(1)} %slice.73), channel_id=1, source_target_pairs={{0,4},{1,3},{2,6},{3,1},{4,0},{5,7},{6,2},{7,5},{8,12},{9,11},{10,... | collective-permute-start | bytes 2764808 | tf_op jit(solution)/shard_map/ppermute | solution.py:473
  235.0 40.1 %collective-permute-start.23 = (bf16[7,8,9600]{2,1,0:T(8,128)(2,1)S(1)}, bf16[7,8,9600]{2,1,0:T(8,128)(2,1)S(1)}, u32[]{:S(2)}, u32[]{:S(2)}) collective-permute-start(bf16[7,8,9600]{2,1,0:T(8,128)(2,1)S(1)} %slice.72), channel_id=1, source_target_pairs={{0,2},{1,5},{2,0},{3,7},{4,6},{5,1},{6,4},{7,3},{8,10},{9,13},{10,... | collective-permute-start | bytes 3225608 | tf_op jit(solution)/shard_map/ppermute | solution.py:473
  236.3 45.2 %collective-permute-start.25 = (bf16[6,8,9600]{2,1,0:T(8,128)(2,1)S(1)}, bf16[6,8,9600]{2,1,0:T(8,128)(2,1)}, u32[]{:S(2)}, u32[]{:S(2)}) collective-permute-start(bf16[6,8,9600]{2,1,0:T(8,128)(2,1)S(1)} %slice.73), channel_id=1, source_target_pairs={{0,2},{1,5},{2,0},{3,7},{4,6},{5,1},{6,4},{7,3},{8,10},{9,13},{10,... | collective-permute-start | bytes 2764808 | tf_op jit(solution)/shard_map/ppermute | solution.py:473
  237.0 44.5 %collective-permute-start.26 = (bf16[7,8,9600]{2,1,0:T(8,128)(2,1)S(1)}, bf16[7,8,9600]{2,1,0:T(8,128)(2,1)}, u32[]{:S(2)}, u32[]{:S(2)}) collective-permute-start(bf16[7,8,9600]{2,1,0:T(8,128)(2,1)S(1)} %slice.72), channel_id=1, source_target_pairs={{0,4},{1,3},{2,6},{3,1},{4,0},{5,7},{6,2},{7,5},{8,12},{9,11},{10,... | collective-permute-start | bytes 3225608 | tf_op jit(solution)/shard_map/ppermute | solution.py:473
  274.2 7.3 %copy-start.13 = (bf16[12,8,9600]{2,1,0:T(8,128)(2,1)}, bf16[12,8,9600]{2,1,0:T(8,128)(2,1)S(1)}, u32[]{:S(2)}) copy-start(bf16[12,8,9600]{2,1,0:T(8,128)(2,1)S(1)} %collective-permute-done.22.rest_0_) | copy-start | bytes 5529604
  274.2 38.0 %collective-permute-start.27 = (bf16[12,8,9600]{2,1,0:T(8,128)(2,1)S(1)}, bf16[12,8,9600]{2,1,0:T(8,128)(2,1)}, u32[]{:S(2)}, u32[]{:S(2)}) collective-permute-start(bf16[12,8,9600]{2,1,0:T(8,128)(2,1)S(1)} %collective-permute-done.22.rest_0_), channel_id=1, source_target_pairs={{0,8},{1,9},{2,10},{3,11},{4,12},{5,13},{6,14},{7,15},{8,24},{9,25... | collective-permute-start | bytes 5529608 | tf_op jit(solution)/shard_map/ppermute | solution.py:473
  275.1 6.4 %copy-start.14 = (bf16[7,8,9600]{2,1,0:T(8,128)(2,1)}, bf16[7,8,9600]{2,1,0:T(8,128)(2,1)S(1)}, u32[]{:S(2)}) copy-start(bf16[7,8,9600]{2,1,0:T(8,128)(2,1)S(1)} %collective-permute-done.23.rest_1_) | copy-start | bytes 3225604
  275.1 23.9 %collective-permute-start.28 = (bf16[6,8,9600]{2,1,0:T(8,128)(2,1)}, bf16[6,8,9600]{2,1,0:T(8,128)(2,1)}, u32[]{:S(2)}, u32[]{:S(2)}) collective-permute-start(bf16[6,8,9600]{2,1,0:T(8,128)(2,1)} %collective-permute-done.24.rest_2_), channel_id=1, source_target_pairs={{0,2},{1,5},{2,0},{3,7},{4,6},{5,1},{6,4},{7,3},{8,10},{9,13},{10,... | collective-permute-start | bytes 2764808 | tf_op jit(solution)/shard_map/ppermute | solution.py:473
  276.5 22.4 %collective-permute-start.29 = (bf16[7,8,9600]{2,1,0:T(8,128)(2,1)S(1)}, bf16[7,8,9600]{2,1,0:T(8,128)(2,1)}, u32[]{:S(2)}, u32[]{:S(2)}) collective-permute-start(bf16[7,8,9600]{2,1,0:T(8,128)(2,1)S(1)} %collective-permute-done.23.rest_1_), channel_id=1, source_target_pairs={{0,4},{1,3},{2,6},{3,1},{4,0},{5,7},{6,2},{7,5},{8,12},{9,11},{10,... | collective-permute-start | bytes 3225608 | tf_op jit(solution)/shard_map/ppermute | solution.py:473
  312.2 8.5 %copy-start.12 = (pred[32]{0:T(512)(128)(4,1)S(1)}, pred[32]{0:T(512)(128)(4,1)}, u32[]{:S(2)}) copy-start(pred[32]{0:T(512)(128)(4,1)} %broadcast_in_dim.39) | copy-start | bytes 100
Sparse Core Ops, SparseCore 0:
  8.9 62.0 all-gather.1

commit v13 on v11

--- a/solution.py
+++ b/solution.py
@@ -16,6 +16,7 @@
 LATER = 4
 LISTS = 2
 WAITS = 5
+LIST_FLOPS = 10**11
 WEIGHT = 8
 
 
@@ -137,7 +138,7 @@
         out_shape=[jax.ShapeDtypeStruct((n,), jnp.int32) for n in sizes],
         in_specs=[smem] * 3,
         out_specs=[smem] * len(sizes),
-        cost_estimate=pl.CostEstimate(flops=10**7, bytes_accessed=10**6, transcendentals=0),
+        cost_estimate=pl.CostEstimate(flops=LIST_FLOPS, bytes_accessed=10**6, transcendentals=0),
         name="pair_lists",
     )(who, ids, queries)
 
@@ -364,11 +365,11 @@
             for axis, _, target in messages:
                 self.arrival[target] = i if axis else i + gap - 1
 
-    def block(self, key):
+    def block(self, key, after=()):
         if key not in self.blocks:
             whole = [self.block(k) for k, _, _ in self.pieces[key]]
             if len(whole) > 1:
-                whole = lax.optimization_barrier(whole)
+                whole = lax.optimization_barrier((*whole, *after))[:len(whole)]
             parts = [b[at:at + n] for b, (_, at, n) in zip(whole, self.pieces[key])]
             self.blocks[key] = parts[0] if len(parts) == 1 else jnp.concatenate(parts, axis=0)
         return self.blocks[key]
@@ -385,15 +386,18 @@
     me = lax.axis_index("shard")
     chip, core = me // 2, me % 2
 
-    rings = [tuple(ring_position(c, n) for c, n in zip(p, sizes)) for p in places]
-    where = {r: i for i, r in enumerate(rings)}
+    rings = [[tuple(ring_position(c, n) for c, n in zip(p, sizes)) for p in places]] * 2
+    if sizes[1] == sizes[2]:
+        rings[1] = [(z, x, y) for z, y, x in rings[0]]
+    where = [{r: i for i, r in enumerate(rings[c])} for c in range(2)]
 
     def step_along(axis):
         out = []
-        for i, ring in enumerate(rings):
-            to = list(ring)
-            to[axis] = (to[axis] + 1) % sizes[axis]
-            out += [(2 * i + c, 2 * where[tuple(to)] + c) for c in range(2)]
+        for i in range(chips):
+            for c in range(2):
+                to = list(rings[c][i])
+                to[axis] = (to[axis] + 1) % sizes[axis]
+                out.append((2 * i + c, 2 * where[c][tuple(to)] + c))
         return out
 
     videos = lax.all_gather(
@@ -411,11 +415,11 @@
         phases[next(i for i, e in enumerate(ends) if gather.arrival[key] <= e)].append(key)
     offsets = [(z, y, x) for z in range(sizes[0]) for y in range(sizes[1]) for x in range(sizes[2])]
     back = np.array(
-        [[where[tuple((r - o) % n for r, o, n in zip(ring, off, sizes))] for off in offsets]
-         for ring in rings], np.int32,
+        [[where[c][tuple((r - o) % n for r, o, n in zip(rings[c][i], off, sizes))] for off in offsets]
+         for i in range(chips) for c in range(2)], np.int32,
     )
     who = jnp.concatenate(
-        [jnp.stack([chip, core]), lax.dynamic_index_in_dim(jnp.asarray(back), chip, 0, keepdims=False)]
+        [jnp.stack([chip, core]), lax.dynamic_index_in_dim(jnp.asarray(back), me, 0, keepdims=False)]
     )
 
     contents, bounds, caps = [], [], []
@@ -454,7 +458,7 @@
                 behind.append(tables[-1])
         done.append([])
         for together in ([m for m in messages if m[0]], [m for m in messages if not m[0]]):
-            sent = [gather.block(source) for _, source, _ in together]
+            sent = [gather.block(source, behind) for _, source, _ in together]
             ties = list(behind)
             if together and together[0][0] and i >= WAITS and (i - WAITS) % gather.gap == 0:
                 ties.append(deep[(i - 1) // gather.gap - 1])

time: 324 us -> 346 us (1.068)
  waiting for transfers between devices: 146 us -> 172 us
  blocking collectives: 15.5 us -> 10.5 us
    ppermute x30, waiting for transfers between devices: 146 us -> 172 us  [body(): gather.blocks[target] = lax.ppermute(block, 'shard', gather.steps[axis])]
    all_to_all x1, blocking collectives: 15.5 us -> 10.5 us  [body(): lax.all_to_all(table.reshape(devices, pairs), 'shard', split_axis=0, conc...]
    unnamed x37 -> x51, local copies, waits for them, and re-layouts: 15.4 us -> 12.9 us
  transfers between devices with their start and end apart: 32 -> 32, of which waited for: 17 -> 18; matrix products, arithmetic and copies ran while one was open for 8% -> 6% of each run, Pallas kernels for 21% -> 20%
where the time goes in v13:
time: 346 us; the launch traced here: 345 us
  waiting for transfers between devices  172 us (50%)
  Pallas kernels  78.4 us (23%)
  starting transfers between devices  39.5 us (11%)
  local copies, waits for them, and re-layouts  29.5 us (9%)
  between operations  13.6 us (4%)
  blocking collectives  10.5 us (3%)
    ppermute x30, waiting for transfers between devices, body(): gather.blocks[target] = lax.ppermute(block, 'shard', gather.steps[axis])  172 us
    pallas_call x5, Pallas kernels, pair_scores(): pl.pallas_call(functools.partial(pair_kernel, frames, idx_dev, len(blocks...  56 us
    ppermute x30, starting transfers between devices, body(): gather.blocks[target] = lax.ppermute(block, 'shard', gather.steps[axis])  35.1 us
    pallas_call x1, Pallas kernels, pair_lists(): pl.pallas_call(functools.partial(list_kernel, idx_dev, k_count, ids.shape...  13.9 us
    unnamed x51, local copies, waits for them, and re-layouts  12.9 us
    slice x8, local copies, waits for them, and re-layouts, block(): parts = [b[at:at + n] for b, (_, at, n) in zip(whole, self.pieces[key])]  11.3 us
    all_to_all x1, blocking collectives, body(): lax.all_to_all(table.reshape(devices, pairs), 'shard', split_axis=0, conc...  10.5 us
    pallas_call x1, Pallas kernels, head_matrices(): pl.pallas_call(head_kernel, out_shape=[jax.ShapeDtypeStruct(s, jnp.bfloat...  8.54 us
  transfers between devices with their start and end apart: 32, of which 18 were waited for; matrix products, arithmetic and copies ran while one was open for 6% of the time, Pallas kernels for 20%

profile of v13, /device:TPU:0, one launch (start us, length us, event | category | flops | bytes accessed | tf_op | source)
XLA Modules:
  0.0 344.6 jit_solution(1780715157021134922)
XLA Ops:
  6.5 0.7 all-gather.2.cloned.1.call-update
  7.3 1.0 copy-done.4
  8.4 3.1 collective-permute-start.4
  11.6 1.6 collective-permute-start
  13.2 1.5 collective-permute-start.1
  15.8 25.8 %collective-permute-done.rest_2_ = bf16[8,8,9600]{2,1,0:T(8,128)(2,1)S(1)} collective-permute-done((bf16[8,8,9600]{2,1,0:T(8,128)(2,1)S(1)}, bf16[8,8,9600]{2,1,0:T(8,128)(2,1)S(1)}, u32[]{:S(2)}, u32[]{:S(2)}) %collective-permute-start) | collective-permute-done | bytes 1228832 | tf_op jit(solution)/shard_map/ppermute | solution.py:467
  41.6 1.7 collective-permute-done.1.rest_1_
  43.3 12.8 %collective-permute-done.4.rest_3_ = bf16[13,8,9600]{2,1,0:T(8,128)(2,1)} collective-permute-done((bf16[13,8,9600]{2,1,0:T(8,128)(2,1)S(1)}, bf16[13,8,9600]{2,1,0:T(8,128)(2,1)}, u32[]{:S(2)}, u32[]{:S(2)}) %collective-permute-start.4) | collective-permute-done | bytes 1996832 | tf_op jit(solution)/shard_map/ppermute | solution.py:467
  56.0 0.7 collective-permute-start.7
  56.8 1.5 collective-permute-start.2
  58.3 1.5 collective-permute-start.3
  59.8 2.2 slice.69
  62.0 2.3 slice.68
  64.3 5.2 %collective-permute-done.5.rest_4_ = bf16[8,8,9600]{2,1,0:T(8,128)(2,1)S(1)} collective-permute-done((bf16[8,8,9600]{2,1,0:T(8,128)(2,1)S(1)}, bf16[8,8,9600]{2,1,0:T(8,128)(2,1)S(1)}, u32[]{:S(2)}, u32[]{:S(2)}) %collective-permute-start.5) | collective-permute-done | bytes 1228832 | tf_op jit(solution)/shard_map/ppermute | solution.py:467
  69.5 1.0 copy-done.11
  70.6 1.5 collective-permute-start.8
  72.6 0.7 dynamic-slice_bitcast_fusion
  74.7 4.4 %all-to-all-start = ((s32[32,1,128]{2,1,0:T(1,128)}), s32[32,1,128]{2,1,0:T(1,128)S(1)}, u32[]{:S(2)}, u32[]{:S(2)}) async-start(s32[32,1,128]{2,1,0:T(1,128)} %broadcast_in_dim.42), calls=%async_computation | async-start | bytes 32768 | tf_op jit(solution)/shard_map/all_to_all | solution.py:471
  79.1 8.5 %head_matrices.1 = (bf16[64,2048]{1,0:T(8,128)(2,1)S(1)}, bf16[512,1024]{1,0:T(8,128)(2,1)S(1)}, bf16[256,256]{1,0:T(8,128)(2,1)S(1)}) custom-call(bf16[9,1,32]{2,1,0:T(2,128)(2,1)S(1)} %reshape.74.one_w, bf16[9,32,64]{2,1,0:T(8,128)(2,1)S(1)} %bitcast.16, bf16[9,1,64]{2,1,0:T(2,128)(2,1)S(1)} %reshape.75.three_w), custom_call_target="tpu_custom_call" | custom-call | flops 1000000000 | bytes 3000000 | tf_op jit(solution)/shard_map/head_matrices/pallas_call | solution.py:90
  87.7 1.0 copy-done.1
  90.7 5.3 %collective-permute-done.2.rest_6_ = bf16[8,8,9600]{2,1,0:T(8,128)(2,1)} collective-permute-done((bf16[8,8,9600]{2,1,0:T(8,128)(2,1)S(1)}, bf16[8,8,9600]{2,1,0:T(8,128)(2,1)}, u32[]{:S(2)}, u32[]{:S(2)}) %collective-permute-start.2) | collective-permute-done | bytes 1228832 | tf_op jit(solution)/shard_map/ppermute | solution.py:467
  96.0 1.5 collective-permute-start.10
  98.0 16.3 %collective-permute-done.9.rest_2_ = bf16[6,8,9600]{2,1,0:T(8,128)(2,1)} collective-permute-done((bf16[6,8,9600]{2,1,0:T(8,128)(2,1)}, bf16[6,8,9600]{2,1,0:T(8,128)(2,1)}, u32[]{:S(2)}, u32[]{:S(2)}) %collective-permute-start.9) | collective-permute-done | bytes 921632 | tf_op jit(solution)/shard_map/ppermute | solution.py:467
  114.3 4.9 %collective-permute-done.8.rest_1_ = bf16[7,8,9600]{2,1,0:T(8,128)(2,1)} collective-permute-done((bf16[7,8,9600]{2,1,0:T(8,128)(2,1)}, bf16[7,8,9600]{2,1,0:T(8,128)(2,1)}, u32[]{:S(2)}, u32[]{:S(2)}) %collective-permute-start.8) | collective-permute-done | bytes 1075232 | tf_op jit(solution)/shard_map/ppermute | solution.py:467
  119.1 1.5 collective-permute-start.13
  121.1 2.6 collective-permute-start.12
  124.3 13.9 %pair_lists.1 = (s32[152]{0:T(256)}, s32[152]{0:T(256)}, s32[151]{0:T(256)}, s32[149]{0:T(256)}, s32[83]{0:T(128)}) custom-call(s32[18]{0:T(128)} %pad_add_fusion.who_ref, s32[32,128]{1,0:T(8,128)} %bitcast.19, s32[256]{0:T(256)} %constant.41.clone.queries_ref), custom_call_target="tpu_custom_call" | custom-call | flops 99999997952 | bytes 1000000 | tf_op jit(solution)/shard_map/pair_lists/pallas_call | solution.py:136
  138.2 1.0 slice.71
  139.2 1.1 slice.70
  140.3 17.0 %collective-permute-done.13.rest_6_ = bf16[6,8,9600]{2,1,0:T(8,128)(2,1)} collective-permute-done((bf16[6,8,9600]{2,1,0:T(8,128)(2,1)}, bf16[6,8,9600]{2,1,0:T(8,128)(2,1)}, u32[]{:S(2)}, u32[]{:S(2)}) %collective-permute-start.13) | collective-permute-done | bytes 921632 | tf_op jit(solution)/shard_map/ppermute | solution.py:467
  157.3 1.1 collective-permute-done.14.rest_7_
  158.4 6.5 %collective-permute-done.12.rest_5_ = bf16[13,8,9600]{2,1,0:T(8,128)(2,1)} collective-permute-done((bf16[13,8,9600]{2,1,0:T(8,128)(2,1)S(1)}, bf16[13,8,9600]{2,1,0:T(8,128)(2,1)}, u32[]{:S(2)}, u32[]{:S(2)}) %collective-permute-start.12) | collective-permute-done | bytes 1996832 | tf_op jit(solution)/shard_map/ppermute | solution.py:467
  164.9 1.7 collective-permute-start.18
  167.1 2.2 slice.73
  169.3 2.3 slice.72
  172.2 13.4 %phase_0.1.before_ref = f32[16,128]{1,0:T(8,128)} custom-call(s32[152]{0:T(256)} %get-tuple-element.65.list_ref, bf16[64,2048]{1,0:T(8,128)(2,1)} %copy-done.2, bf16[512,1024]{1,0:T(8,128)(2,1)} %copy-done.1, bf16[256,256]{1,0:T(8,128)(2,1)} %copy-done.3, f32[16,128]{1,0:T(8,128)} %broadcast_in_dim.43.before_ref, ...), custom_call_target="tpu_custom_call" | custom-call | flops 100663296000 | bytes 39321600 | tf_op jit(solution)/shard_map/phase_0/pallas_call | solution.py:258
  185.6 0.9 slice_dynamic-update-slice_fusion.7
  186.5 4.3 %collective-permute-start.16 = (bf16[6,8,9600]{2,1,0:T(8,128)(2,1)}, bf16[6,8,9600]{2,1,0:T(8,128)(2,1)}, u32[]{:S(2)}, u32[]{:S(2)}) collective-permute-start(bf16[6,8,9600]{2,1,0:T(8,128)(2,1)} %slice.71), channel_id=1, source_target_pairs={{0,4},{1,3},{2,6},{3,1},{4,0},{5,7},{6,2},{7,5},{8,12},{9,11},{10,... | collective-permute-start | bytes 2764808 | tf_op jit(solution)/shard_map/ppermute | solution.py:467
  190.8 0.9 slice_dynamic-update-slice_fusion.6
  191.7 0.9 slice_dynamic-update-slice_fusion.5
  192.7 0.9 slice_dynamic-update-slice_fusion.4
  193.6 1.0 slice_dynamic-update-slice_fusion.3
  194.6 1.0 slice_dynamic-update-slice_fusion.2
  195.6 1.0 slice_dynamic-update-slice_fusion.1
  196.6 1.0 slice_dynamic-update-slice_fusion
  198.3 12.4 %collective-permute-done.16.rest_1_ = bf16[6,8,9600]{2,1,0:T(8,128)(2,1)} collective-permute-done((bf16[6,8,9600]{2,1,0:T(8,128)(2,1)}, bf16[6,8,9600]{2,1,0:T(8,128)(2,1)}, u32[]{:S(2)}, u32[]{:S(2)}) %collective-permute-start.16) | collective-permute-done | bytes 921632 | tf_op jit(solution)/shard_map/ppermute | solution.py:467
  210.7 1.8 collective-permute-start.21
  212.6 14.1 %phase_1.1.before_ref = f32[16,128]{1,0:T(8,128)} custom-call(s32[152]{0:T(256)} %get-tuple-element.64.list_ref, bf16[64,2048]{1,0:T(8,128)(2,1)} %copy-done.2, bf16[512,1024]{1,0:T(8,128)(2,1)} %copy-done.1, bf16[256,256]{1,0:T(8,128)(2,1)} %copy-done.3, f32[16,128]{1,0:T(8,128)} %phase_0.1.before_ref, ...), custom_call_target="tpu_custom_call" | custom-call | flops 100663296000 | bytes 39321600 | tf_op jit(solution)/shard_map/phase_1/pallas_call | solution.py:258
  226.7 11.3 %collective-permute-done.17.rest_2_ = bf16[12,8,9600]{2,1,0:T(8,128)(2,1)S(1)} collective-permute-done((bf16[12,8,9600]{2,1,0:T(8,128)(2,1)S(1)}, bf16[12,8,9600]{2,1,0:T(8,128)(2,1)S(1)}, u32[]{:S(2)}, u32[]{:S(2)}) %collective-permute-start.17) | collective-permute-done | bytes 1843232 | tf_op jit(solution)/shard_map/ppermute | solution.py:467
  238.2 2.0 collective-permute-start.23
  240.3 1.9 collective-permute-start.26
  242.2 10.4 %phase_2.1.before_ref = f32[16,128]{1,0:T(8,128)} custom-call(s32[151]{0:T(256)} %get-tuple-element.63.list_ref, bf16[64,2048]{1,0:T(8,128)(2,1)} %copy-done.2, bf16[512,1024]{1,0:T(8,128)(2,1)} %copy-done.1, bf16[256,256]{1,0:T(8,128)(2,1)} %copy-done.3, f32[16,128]{1,0:T(8,128)} %phase_1.1.before_ref, ...), custom_call_target="tpu_custom_call" | custom-call | flops 100663296000 | bytes 39321600 | tf_op jit(solution)/shard_map/phase_2/pallas_call | solution.py:258
  252.6 25.7 %collective-permute-done.22.rest_0_ = bf16[12,8,9600]{2,1,0:T(8,128)(2,1)S(1)} collective-permute-done((bf16[12,8,9600]{2,1,0:T(8,128)(2,1)S(1)}, bf16[12,8,9600]{2,1,0:T(8,128)(2,1)S(1)}, u32[]{:S(2)}, u32[]{:S(2)}) %collective-permute-start.22) | collective-permute-done | bytes 1843232 | tf_op jit(solution)/shard_map/ppermute | solution.py:467
  278.3 2.1 collective-permute-start.28
  280.5 2.3 collective-permute-done.25.rest_3_
  282.8 1.8 collective-permute-done.26.rest_4_
  284.6 10.3 %phase_3.1.before_ref = f32[16,128]{1,0:T(8,128)} custom-call(s32[149]{0:T(256)} %get-tuple-element.62.list_ref, bf16[64,2048]{1,0:T(8,128)(2,1)} %copy-done.2, bf16[512,1024]{1,0:T(8,128)(2,1)} %copy-done.1, bf16[256,256]{1,0:T(8,128)(2,1)} %copy-done.3, f32[16,128]{1,0:T(8,128)} %phase_2.1.before_ref, ...), custom_call_target="tpu_custom_call" | custom-call | flops 100663296000 | bytes 39321600 | tf_op jit(solution)/shard_map/phase_3/pallas_call | solution.py:258
  294.9 5.6 %collective-permute-done.28.rest_1_ = bf16[6,8,9600]{2,1,0:T(8,128)(2,1)} collective-permute-done((bf16[6,8,9600]{2,1,0:T(8,128)(2,1)}, bf16[6,8,9600]{2,1,0:T(8,128)(2,1)}, u32[]{:S(2)}, u32[]{:S(2)}) %collective-permute-start.28) | collective-permute-done | bytes 921632 | tf_op jit(solution)/shard_map/ppermute | solution.py:467
  300.6 1.0 collective-permute-done.29.rest_2_
  301.6 15.0 %collective-permute-done.27.rest_0_ = bf16[12,8,9600]{2,1,0:T(8,128)(2,1)S(1)} collective-permute-done((bf16[12,8,9600]{2,1,0:T(8,128)(2,1)S(1)}, bf16[12,8,9600]{2,1,0:T(8,128)(2,1)S(1)}, u32[]{:S(2)}, u32[]{:S(2)}) %collective-permute-start.27) | collective-permute-done | bytes 1843232 | tf_op jit(solution)/shard_map/ppermute | solution.py:467
  316.6 1.2 copy-done.20
  317.8 7.8 %phase_4.1 = f32[16,128]{1,0:T(8,128)} custom-call(s32[83]{0:T(128)} %get-tuple-element.58.list_ref, bf16[64,2048]{1,0:T(8,128)(2,1)} %copy-done.2, bf16[512,1024]{1,0:T(8,128)(2,1)} %copy-done.1, bf16[256,256]{1,0:T(8,128)(2,1)} %copy-done.3, f32[16,128]{1,0:T(8,128)} %phase_3.1.before_ref, bf16[256,8,9600]{2,1,0:T(8,128)(2,1)} %all-gather.2.cloned.1.call-done.v_hbm, ...), custom_call_target="tpu_custom_call" | custom-call | flops 50331648000 | bytes 19660800 | tf_op jit(solution)/shard_map/phase_4/pallas_call | solution.py:258
  325.6 0.7 broadcast_in_dim.44
  326.4 10.5 %all_to_all.14 = f32[32,1,128]{2,1,0:T(1,128)S(1)} all-to-all(f32[32,1,128]{2,1,0:T(1,128)S(1)} %broadcast_select_fusion), channel_id=1, replica_groups=mesh['shard'=32] {'shard'}, dimensions={0} | all-to-all | bytes 32768 | tf_op jit(solution)/shard_map/all_to_all | solution.py:483
  (85 shorter events, 10.1 us)
Async XLA Ops:
  6.5 1.7 copy-start.4
  6.5 165.0 %all-gather.2.cloned.1.call-start = ((), (), s32[]{:S(2)}) async-start(), calls=%async_computation.2 | async-start | bytes 58982400 | tf_op jit(solution)/shard_map/all_gather | solution.py:403
  8.4 47.7 %collective-permute-start.4 = (bf16[13,8,9600]{2,1,0:T(8,128)(2,1)S(1)}, bf16[13,8,9600]{2,1,0:T(8,128)(2,1)}, u32[]{:S(2)}, u32[]{:S(2)}) collective-permute-start(bf16[13,8,9600]{2,1,0:T(8,128)(2,1)S(1)} %slice.53), channel_id=1, source_target_pairs={{0,8},{1,9},{2,10},{3,11},{4,12},{5,13},{6,14},{7,15},{8,24},{9,25... | collective-permute-start | bytes 5990408 | tf_op jit(solution)/shard_map/ppermute | solution.py:467
  11.6 52.7 %copy-start.6 = (bf16[8,8,9600]{2,1,0:T(8,128)(2,1)}, bf16[8,8,9600]{2,1,0:T(8,128)(2,1)S(1)}, u32[]{:S(2)}) copy-start(bf16[8,8,9600]{2,1,0:T(8,128)(2,1)S(1)} %get-tuple-element.82) | copy-start | bytes 3686404
  11.6 52.6 %copy-start.7 = (bf16[8,8,9600]{2,1,0:T(8,128)(2,1)}, bf16[8,8,9600]{2,1,0:T(8,128)(2,1)S(1)}, u32[]{:S(2)}) copy-start(bf16[8,8,9600]{2,1,0:T(8,128)(2,1)S(1)} %get-tuple-element.78) | copy-start | bytes 3686404
  11.6 30.0 %collective-permute-start = (bf16[8,8,9600]{2,1,0:T(8,128)(2,1)S(1)}, bf16[8,8,9600]{2,1,0:T(8,128)(2,1)S(1)}, u32[]{:S(2)}, u32[]{:S(2)}) collective-permute-start(bf16[8,8,9600]{2,1,0:T(8,128)(2,1)S(1)} %get-tuple-element.82), channel_id=1, source_target_pairs={{0,4},{1,3},{2,6},{3,1},{4,0},{5,7},{6,2},{7,5},{8,12},{9,11},{10,... | collective-permute-start | bytes 3686408 | tf_op jit(solution)/shard_map/ppermute | solution.py:467
  13.2 30.1 %collective-permute-start.1 = (bf16[8,8,9600]{2,1,0:T(8,128)(2,1)S(1)}, bf16[8,8,9600]{2,1,0:T(8,128)(2,1)}, u32[]{:S(2)}, u32[]{:S(2)}) collective-permute-start(bf16[8,8,9600]{2,1,0:T(8,128)(2,1)S(1)} %get-tuple-element.78), channel_id=1, source_target_pairs={{0,2},{1,5},{2,0},{3,7},{4,6},{5,1},{6,4},{7,3},{8,10},{9,13},{10,... | collective-permute-start | bytes 3686408 | tf_op jit(solution)/shard_map/ppermute | solution.py:467
  14.7 54.8 %collective-permute-start.5 = (bf16[8,8,9600]{2,1,0:T(8,128)(2,1)S(1)}, bf16[8,8,9600]{2,1,0:T(8,128)(2,1)S(1)}, u32[]{:S(2)}, u32[]{:S(2)}) collective-permute-start(bf16[8,8,9600]{2,1,0:T(8,128)(2,1)S(1)} %get-tuple-element.82), channel_id=1, source_target_pairs={{0,2},{1,5},{2,0},{3,7},{4,6},{5,1},{6,4},{7,3},{8,10},{9,13},{10,... | collective-permute-start | bytes 3686408 | tf_op jit(solution)/shard_map/ppermute | solution.py:467
  15.2 57.3 %copy-start.15 = (bf16[32,1,3,3]{0,3,2,1:T(4,128)(2,1)S(1)}, bf16[32,1,3,3]{0,3,2,1:T(4,128)(2,1)}, u32[]{:S(2)}) copy-start(bf16[32,1,3,3]{0,3,2,1:T(4,128)(2,1)} %param.11) | copy-start | bytes 1732
  15.2 57.3 %copy-start.16 = (bf16[1,64,3,3]{1,3,2,0:T(4,128)(2,1)S(1)}, bf16[1,64,3,3]{1,3,2,0:T(4,128)(2,1)}, u32[]{:S(2)}) copy-start(bf16[1,64,3,3]{1,3,2,0:T(4,128)(2,1)} %param.13) | copy-start | bytes 3460
  15.2 58.7 %copy-start.14 = (s32[16,8]{0,1:T(8,128)S(1)}, s32[16,8]{0,1:T(8,128)}, u32[]{:S(2)}) copy-start(s32[16,8]{0,1:T(8,128)} %param.10) | copy-start | bytes 1540
  15.2 63.9 %copy-start = (bf16[64,32,3,3]{0,1,3,2:T(8,128)(2,1)S(1)}, bf16[64,32,3,3]{0,1,3,2:T(8,128)(2,1)}, u32[]{:S(2)}) copy-start(bf16[64,32,3,3]{0,1,3,2:T(8,128)(2,1)} %param.12) | copy-start | bytes 110596
  15.2 54.3 %collective-permute-start.6 = (bf16[8,8,9600]{2,1,0:T(8,128)(2,1)S(1)}, bf16[8,8,9600]{2,1,0:T(8,128)(2,1)S(1)}, u32[]{:S(2)}, u32[]{:S(2)}) collective-permute-start(bf16[8,8,9600]{2,1,0:T(8,128)(2,1)S(1)} %get-tuple-element.78), channel_id=1, source_target_pairs={{0,4},{1,3},{2,6},{3,1},{4,0},{5,7},{6,2},{7,5},{8,12},{9,11},{10,... | collective-permute-start | bytes 3686408 | tf_op jit(solution)/shard_map/ppermute | solution.py:467
  41.6 22.7 %copy-start.10 = (bf16[8,8,9600]{2,1,0:T(8,128)(2,1)}, bf16[8,8,9600]{2,1,0:T(8,128)(2,1)S(1)}, u32[]{:S(2)}) copy-start(bf16[8,8,9600]{2,1,0:T(8,128)(2,1)S(1)} %collective-permute-done.rest_2_) | copy-start | bytes 3686404
  56.0 63.1 %collective-permute-start.7 = (bf16[13,8,9600]{2,1,0:T(8,128)(2,1)}, bf16[13,8,9600]{2,1,0:T(8,128)(2,1)S(1)}, u32[]{:S(2)}, u32[]{:S(2)}) collective-permute-start(bf16[13,8,9600]{2,1,0:T(8,128)(2,1)} %collective-permute-done.4.rest_3_), channel_id=1, source_target_pairs={{0,8},{1,9},{2,10},{3,11},{4,12},{5,13},{6,14},{7,15},{8,24},{9,25... | collective-permute-start | bytes 5990408 | tf_op jit(solution)/shard_map/ppermute | solution.py:467
  56.8 39.2 %collective-permute-start.2 = (bf16[8,8,9600]{2,1,0:T(8,128)(2,1)S(1)}, bf16[8,8,9600]{2,1,0:T(8,128)(2,1)}, u32[]{:S(2)}, u32[]{:S(2)}) collective-permute-start(bf16[8,8,9600]{2,1,0:T(8,128)(2,1)S(1)} %collective-permute-done.rest_2_), channel_id=1, source_target_pairs={{0,2},{1,5},{2,0},{3,7},{4,6},{5,1},{6,4},{7,3},{8,10},{9,13},{10,... | collective-permute-start | bytes 3686408 | tf_op jit(solution)/shard_map/ppermute | solution.py:467
  58.3 37.7 %collective-permute-start.3 = (bf16[8,8,9600]{2,1,0:T(8,128)(2,1)}, bf16[8,8,9600]{2,1,0:T(8,128)(2,1)}, u32[]{:S(2)}, u32[]{:S(2)}) collective-permute-start(bf16[8,8,9600]{2,1,0:T(8,128)(2,1)} %collective-permute-done.1.rest_1_), channel_id=1, source_target_pairs={{0,4},{1,3},{2,6},{3,1},{4,0},{5,7},{6,2},{7,5},{8,12},{9,11},{10,... | collective-permute-start | bytes 3686408 | tf_op jit(solution)/shard_map/ppermute | solution.py:467
  69.5 1.0 copy-start.11
  70.6 1.5 copy-start.12
  70.6 48.6 %collective-permute-start.8 = (bf16[7,8,9600]{2,1,0:T(8,128)(2,1)}, bf16[7,8,9600]{2,1,0:T(8,128)(2,1)}, u32[]{:S(2)}, u32[]{:S(2)}) collective-permute-start(bf16[7,8,9600]{2,1,0:T(8,128)(2,1)} %slice.68), channel_id=1, source_target_pairs={{0,2},{1,5},{2,0},{3,7},{4,6},{5,1},{6,4},{7,3},{8,10},{9,13},{10,... | collective-permute-start | bytes 3225608 | tf_op jit(solution)/shard_map/ppermute | solution.py:467
  72.1 42.2 %collective-permute-start.9 = (bf16[6,8,9600]{2,1,0:T(8,128)(2,1)}, bf16[6,8,9600]{2,1,0:T(8,128)(2,1)}, u32[]{:S(2)}, u32[]{:S(2)}) collective-permute-start(bf16[6,8,9600]{2,1,0:T(8,128)(2,1)} %slice.69), channel_id=1, source_target_pairs={{0,4},{1,3},{2,6},{3,1},{4,0},{5,7},{6,2},{7,5},{8,12},{9,11},{10,... | collective-permute-start | bytes 2764808 | tf_op jit(solution)/shard_map/ppermute | solution.py:467
  74.7 49.0 %all-to-all-start = ((s32[32,1,128]{2,1,0:T(1,128)}), s32[32,1,128]{2,1,0:T(1,128)S(1)}, u32[]{:S(2)}, u32[]{:S(2)}) async-start(s32[32,1,128]{2,1,0:T(1,128)} %broadcast_in_dim.42), calls=%async_computation | async-start | bytes 32768 | tf_op jit(solution)/shard_map/all_to_all | solution.py:471
  87.6 1.0 copy-start.1
  88.7 0.7 copy-start.2
  89.4 0.6 copy-start.3
  96.0 89.6 %collective-permute-start.10 = (bf16[6,8,9600]{2,1,0:T(8,128)(2,1)}, bf16[6,8,9600]{2,1,0:T(8,128)(2,1)}, u32[]{:S(2)}, u32[]{:S(2)}) collective-permute-start(bf16[6,8,9600]{2,1,0:T(8,128)(2,1)} %slice.69), channel_id=1, source_target_pairs={{0,2},{1,5},{2,0},{3,7},{4,6},{5,1},{6,4},{7,3},{8,10},{9,13},{10,... | collective-permute-start | bytes 2764808 | tf_op jit(solution)/shard_map/ppermute | solution.py:467
  97.5 88.1 %collective-permute-start.11 = (bf16[7,8,9600]{2,1,0:T(8,128)(2,1)}, bf16[7,8,9600]{2,1,0:T(8,128)(2,1)}, u32[]{:S(2)}, u32[]{:S(2)}) collective-permute-start(bf16[7,8,9600]{2,1,0:T(8,128)(2,1)} %slice.68), channel_id=1, source_target_pairs={{0,4},{1,3},{2,6},{3,1},{4,0},{5,7},{6,2},{7,5},{8,12},{9,11},{10,... | collective-permute-start | bytes 3225608 | tf_op jit(solution)/shard_map/ppermute | solution.py:467
  119.1 20.1 %copy-start.5 = (bf16[13,8,9600]{2,1,0:T(8,128)(2,1)}, bf16[13,8,9600]{2,1,0:T(8,128)(2,1)S(1)}, u32[]{:S(2)}) copy-start(bf16[13,8,9600]{2,1,0:T(8,128)(2,1)S(1)} %collective-permute-done.7.rest_0_) | copy-start | bytes 5990404
  119.1 38.2 %collective-permute-start.13 = (bf16[6,8,9600]{2,1,0:T(8,128)(2,1)}, bf16[6,8,9600]{2,1,0:T(8,128)(2,1)}, u32[]{:S(2)}, u32[]{:S(2)}) collective-permute-start(bf16[6,8,9600]{2,1,0:T(8,128)(2,1)} %collective-permute-done.9.rest_2_), channel_id=1, source_target_pairs={{0,2},{1,5},{2,0},{3,7},{4,6},{5,1},{6,4},{7,3},{8,10},{9,13},{10,... | collective-permute-start | bytes 2764808 | tf_op jit(solution)/shard_map/ppermute | solution.py:467
  120.6 37.8 %collective-permute-start.14 = (bf16[7,8,9600]{2,1,0:T(8,128)(2,1)}, bf16[7,8,9600]{2,1,0:T(8,128)(2,1)S(1)}, u32[]{:S(2)}, u32[]{:S(2)}) collective-permute-start(bf16[7,8,9600]{2,1,0:T(8,128)(2,1)} %collective-permute-done.8.rest_1_), channel_id=1, source_target_pairs={{0,4},{1,3},{2,6},{3,1},{4,0},{5,7},{6,2},{7,5},{8,12},{9,11},{10,... | collective-permute-start | bytes 3225608 | tf_op jit(solution)/shard_map/ppermute | solution.py:467
  121.1 43.8 %collective-permute-start.12 = (bf16[13,8,9600]{2,1,0:T(8,128)(2,1)S(1)}, bf16[13,8,9600]{2,1,0:T(8,128)(2,1)}, u32[]{:S(2)}, u32[]{:S(2)}) collective-permute-start(bf16[13,8,9600]{2,1,0:T(8,128)(2,1)S(1)} %collective-permute-done.7.rest_0_), channel_id=1, source_target_pairs={{0,8},{1,9},{2,10},{3,11},{4,12},{5,13},{6,14},{7,15},{8,24},{9,25... | collective-permute-start | bytes 5990408 | tf_op jit(solution)/shard_map/ppermute | solution.py:467
  123.7 0.6 copy-start.13
  158.4 13.2 %copy-start.21 = (bf16[7,8,9600]{2,1,0:T(8,128)(2,1)}, bf16[7,8,9600]{2,1,0:T(8,128)(2,1)S(1)}, u32[]{:S(2)}) copy-start(bf16[7,8,9600]{2,1,0:T(8,128)(2,1)S(1)} %collective-permute-done.14.rest_7_) | copy-start | bytes 3225604
  164.9 73.1 %collective-permute-start.18 = (bf16[6,8,9600]{2,1,0:T(8,128)(2,1)}, bf16[6,8,9600]{2,1,0:T(8,128)(2,1)}, u32[]{:S(2)}, u32[]{:S(2)}) collective-permute-start(bf16[6,8,9600]{2,1,0:T(8,128)(2,1)} %slice.71), channel_id=1, source_target_pairs={{0,2},{1,5},{2,0},{3,7},{4,6},{5,1},{6,4},{7,3},{8,10},{9,13},{10,... | collective-permute-start | bytes 2764808 | tf_op jit(solution)/shard_map/ppermute | solution.py:467
  166.6 71.4 %collective-permute-start.19 = (bf16[7,8,9600]{2,1,0:T(8,128)(2,1)}, bf16[7,8,9600]{2,1,0:T(8,128)(2,1)}, u32[]{:S(2)}, u32[]{:S(2)}) collective-permute-start(bf16[7,8,9600]{2,1,0:T(8,128)(2,1)} %slice.70), channel_id=1, source_target_pairs={{0,4},{1,3},{2,6},{3,1},{4,0},{5,7},{6,2},{7,5},{8,12},{9,11},{10,... | collective-permute-start | bytes 3225608 | tf_op jit(solution)/shard_map/ppermute | solution.py:467
  186.5 24.1 %collective-permute-start.16 = (bf16[6,8,9600]{2,1,0:T(8,128)(2,1)}, bf16[6,8,9600]{2,1,0:T(8,128)(2,1)}, u32[]{:S(2)}, u32[]{:S(2)}) collective-permute-start(bf16[6,8,9600]{2,1,0:T(8,128)(2,1)} %slice.71), channel_id=1, source_target_pairs={{0,4},{1,3},{2,6},{3,1},{4,0},{5,7},{6,2},{7,5},{8,12},{9,11},{10,... | collective-permute-start | bytes 2764808 | tf_op jit(solution)/shard_map/ppermute | solution.py:467
  190.8 19.8 %collective-permute-start.15 = (bf16[7,8,9600]{2,1,0:T(8,128)(2,1)}, bf16[7,8,9600]{2,1,0:T(8,128)(2,1)}, u32[]{:S(2)}, u32[]{:S(2)}) collective-permute-start(bf16[7,8,9600]{2,1,0:T(8,128)(2,1)} %slice.70), channel_id=1, source_target_pairs={{0,2},{1,5},{2,0},{3,7},{4,6},{5,1},{6,4},{7,3},{8,10},{9,13},{10,... | collective-permute-start | bytes 3225608 | tf_op jit(solution)/shard_map/ppermute | solution.py:467
  197.6 40.4 %collective-permute-start.17 = (bf16[12,8,9600]{2,1,0:T(8,128)(2,1)S(1)}, bf16[12,8,9600]{2,1,0:T(8,128)(2,1)S(1)}, u32[]{:S(2)}, u32[]{:S(2)}) collective-permute-start(bf16[12,8,9600]{2,1,0:T(8,128)(2,1)S(1)} %slice_dynamic-update-slice_fusion), channel_id=1, source_target_pairs={{0,8},{1,9},{2,10},{3,11},{4,12},{5,13},{6,14},{7,15},{8,24},{9,25... | collective-permute-start | bytes 5529608 | tf_op jit(solution)/shard_map/ppermute | solution.py:467
  210.6 29.6 %collective-permute-start.20 = (bf16[6,8,9600]{2,1,0:T(8,128)(2,1)}, bf16[6,8,9600]{2,1,0:T(8,128)(2,1)}, u32[]{:S(2)}, u32[]{:S(2)}) collective-permute-start(bf16[6,8,9600]{2,1,0:T(8,128)(2,1)} %collective-permute-done.16.rest_1_), channel_id=1, source_target_pairs={{0,2},{1,5},{2,0},{3,7},{4,6},{5,1},{6,4},{7,3},{8,10},{9,13},{10,... | collective-permute-start | bytes 2764808 | tf_op jit(solution)/shard_map/ppermute | solution.py:467
  210.7 29.5 %collective-permute-start.21 = (bf16[7,8,9600]{2,1,0:T(8,128)(2,1)}, bf16[7,8,9600]{2,1,0:T(8,128)(2,1)}, u32[]{:S(2)}, u32[]{:S(2)}) collective-permute-start(bf16[7,8,9600]{2,1,0:T(8,128)(2,1)} %collective-permute-done.15.rest_0_), channel_id=1, source_target_pairs={{0,4},{1,3},{2,6},{3,1},{4,0},{5,7},{6,2},{7,5},{8,12},{9,11},{10,... | collective-permute-start | bytes 3225608 | tf_op jit(solution)/shard_map/ppermute | solution.py:467
  212.6 25.4 %copy-start.9 = (bf16[6,8,9600]{2,1,0:T(8,128)(2,1)S(1)}, bf16[6,8,9600]{2,1,0:T(8,128)(2,1)}, u32[]{:S(2)}) copy-start(bf16[6,8,9600]{2,1,0:T(8,128)(2,1)} %slice.73) | copy-start | bytes 2764804
  212.6 25.6 %copy-start.8 = (bf16[7,8,9600]{2,1,0:T(8,128)(2,1)S(1)}, bf16[7,8,9600]{2,1,0:T(8,128)(2,1)}, u32[]{:S(2)}) copy-start(bf16[7,8,9600]{2,1,0:T(8,128)(2,1)} %slice.72) | copy-start | bytes 3225604
  238.0 4.2 %copy-start.19 = (bf16[12,8,9600]{2,1,0:T(8,128)(2,1)}, bf16[12,8,9600]{2,1,0:T(8,128)(2,1)S(1)}, u32[]{:S(2)}) copy-start(bf16[12,8,9600]{2,1,0:T(8,128)(2,1)S(1)} %collective-permute-done.17.rest_2_) | copy-start | bytes 5529604
  238.0 40.3 %collective-permute-start.22 = (bf16[12,8,9600]{2,1,0:T(8,128)(2,1)S(1)}, bf16[12,8,9600]{2,1,0:T(8,128)(2,1)S(1)}, u32[]{:S(2)}, u32[]{:S(2)}) collective-permute-start(bf16[12,8,9600]{2,1,0:T(8,128)(2,1)S(1)} %collective-permute-done.17.rest_2_), channel_id=1, source_target_pairs={{0,8},{1,9},{2,10},{3,11},{4,12},{5,13},{6,14},{7,15},{8,24},{9,25... | collective-permute-start | bytes 5529608 | tf_op jit(solution)/shard_map/ppermute | solution.py:467
  238.0 40.3 %collective-permute-start.24 = (bf16[6,8,9600]{2,1,0:T(8,128)(2,1)S(1)}, bf16[6,8,9600]{2,1,0:T(8,128)(2,1)}, u32[]{:S(2)}, u32[]{:S(2)}) collective-permute-start(bf16[6,8,9600]{2,1,0:T(8,128)(2,1)S(1)} %copy-done.9), channel_id=1, source_target_pairs={{0,4},{1,3},{2,6},{3,1},{4,0},{5,7},{6,2},{7,5},{8,12},{9,11},{10,... | collective-permute-start | bytes 2764808 | tf_op jit(solution)/shard_map/ppermute | solution.py:467
  238.2 40.2 %collective-permute-start.23 = (bf16[7,8,9600]{2,1,0:T(8,128)(2,1)S(1)}, bf16[7,8,9600]{2,1,0:T(8,128)(2,1)}, u32[]{:S(2)}, u32[]{:S(2)}) collective-permute-start(bf16[7,8,9600]{2,1,0:T(8,128)(2,1)S(1)} %copy-done.8), channel_id=1, source_target_pairs={{0,2},{1,5},{2,0},{3,7},{4,6},{5,1},{6,4},{7,3},{8,10},{9,13},{10,... | collective-permute-start | bytes 3225608 | tf_op jit(solution)/shard_map/ppermute | solution.py:467
  240.2 42.6 %collective-permute-start.25 = (bf16[6,8,9600]{2,1,0:T(8,128)(2,1)S(1)}, bf16[6,8,9600]{2,1,0:T(8,128)(2,1)}, u32[]{:S(2)}, u32[]{:S(2)}) collective-permute-start(bf16[6,8,9600]{2,1,0:T(8,128)(2,1)S(1)} %copy-done.9), channel_id=1, source_target_pairs={{0,2},{1,5},{2,0},{3,7},{4,6},{5,1},{6,4},{7,3},{8,10},{9,13},{10,... | collective-permute-start | bytes 2764808 | tf_op jit(solution)/shard_map/ppermute | solution.py:467
  240.3 44.3 %collective-permute-start.26 = (bf16[7,8,9600]{2,1,0:T(8,128)(2,1)S(1)}, bf16[7,8,9600]{2,1,0:T(8,128)(2,1)}, u32[]{:S(2)}, u32[]{:S(2)}) collective-permute-start(bf16[7,8,9600]{2,1,0:T(8,128)(2,1)S(1)} %copy-done.8), channel_id=1, source_target_pairs={{0,4},{1,3},{2,6},{3,1},{4,0},{5,7},{6,2},{7,5},{8,12},{9,11},{10,... | collective-permute-start | bytes 3225608 | tf_op jit(solution)/shard_map/ppermute | solution.py:467
  278.3 6.3 %copy-start.18 = (bf16[12,8,9600]{2,1,0:T(8,128)(2,1)}, bf16[12,8,9600]{2,1,0:T(8,128)(2,1)S(1)}, u32[]{:S(2)}) copy-start(bf16[12,8,9600]{2,1,0:T(8,128)(2,1)S(1)} %collective-permute-done.22.rest_0_) | copy-start | bytes 5529604
  278.3 38.2 %collective-permute-start.27 = (bf16[12,8,9600]{2,1,0:T(8,128)(2,1)S(1)}, bf16[12,8,9600]{2,1,0:T(8,128)(2,1)S(1)}, u32[]{:S(2)}, u32[]{:S(2)}) collective-permute-start(bf16[12,8,9600]{2,1,0:T(8,128)(2,1)S(1)} %collective-permute-done.22.rest_0_), channel_id=1, source_target_pairs={{0,8},{1,9},{2,10},{3,11},{4,12},{5,13},{6,14},{7,15},{8,24},{9,25... | collective-permute-start | bytes 5529608 | tf_op jit(solution)/shard_map/ppermute | solution.py:467
  278.3 22.2 %collective-permute-start.28 = (bf16[6,8,9600]{2,1,0:T(8,128)(2,1)}, bf16[6,8,9600]{2,1,0:T(8,128)(2,1)}, u32[]{:S(2)}, u32[]{:S(2)}) collective-permute-start(bf16[6,8,9600]{2,1,0:T(8,128)(2,1)} %collective-permute-done.24.rest_2_), channel_id=1, source_target_pairs={{0,2},{1,5},{2,0},{3,7},{4,6},{5,1},{6,4},{7,3},{8,10},{9,13},{10,... | collective-permute-start | bytes 2764808 | tf_op jit(solution)/shard_map/ppermute | solution.py:467
  280.4 21.2 %collective-permute-start.29 = (bf16[7,8,9600]{2,1,0:T(8,128)(2,1)}, bf16[7,8,9600]{2,1,0:T(8,128)(2,1)}, u32[]{:S(2)}, u32[]{:S(2)}) collective-permute-start(bf16[7,8,9600]{2,1,0:T(8,128)(2,1)} %collective-permute-done.23.rest_1_), channel_id=1, source_target_pairs={{0,4},{1,3},{2,6},{3,1},{4,0},{5,7},{6,2},{7,5},{8,12},{9,11},{10,... | collective-permute-start | bytes 3225608 | tf_op jit(solution)/shard_map/ppermute | solution.py:467
  316.6 1.2 copy-start.20
  317.8 8.5 %copy-start.17 = (pred[32]{0:T(512)(128)(4,1)S(1)}, pred[32]{0:T(512)(128)(4,1)}, u32[]{:S(2)}) copy-start(pred[32]{0:T(512)(128)(4,1)} %broadcast_in_dim.39) | copy-start | bytes 100
Sparse Core Ops, SparseCore 0:
  8.9 62.0 all-gather.1

commit v14 on v13

--- a/solution.py
+++ b/solution.py
@@ -368,8 +368,7 @@
     def block(self, key, after=()):
         if key not in self.blocks:
             whole = [self.block(k) for k, _, _ in self.pieces[key]]
-            if len(whole) > 1:
-                whole = lax.optimization_barrier((*whole, *after))[:len(whole)]
+            whole = lax.optimization_barrier((*whole, *after))[:len(whole)]
             parts = [b[at:at + n] for b, (_, at, n) in zip(whole, self.pieces[key])]
             self.blocks[key] = parts[0] if len(parts) == 1 else jnp.concatenate(parts, axis=0)
         return self.blocks[key]

time: 346 us -> 321 us (0.928)
  waiting for transfers between devices: 172 us -> 135 us
  starting transfers between devices: 39.5 us -> 45.6 us
  local copies, waits for them, and re-layouts: 29.5 us -> 33.3 us
    ppermute x30, waiting for transfers between devices: 172 us -> 134 us  [body(): gather.blocks[target] = lax.ppermute(block, 'shard', gather.steps[axis])]
    ppermute x30, starting transfers between devices: 35.1 us -> 40.7 us  [body(): gather.blocks[target] = lax.ppermute(block, 'shard', gather.steps[axis])]
    unnamed x51 -> x41, local copies, waits for them, and re-layouts: 12.9 us -> 16.6 us
  transfers between devices with their start and end apart: 32 -> 32, of which waited for: 18 -> 21; matrix products, arithmetic and copies ran while one was open for 6% -> 9% of each run, Pallas kernels for 20% -> 21%
where the time goes in v14:
time: 321 us; the launch traced here: 317 us
  waiting for transfers between devices  135 us (42%)
  Pallas kernels  75.4 us (23%)
  starting transfers between devices  45.6 us (14%)
  local copies, waits for them, and re-layouts  33.3 us (10%)
  between operations  13.6 us (4%)
  blocking collectives  13.2 us (4%)
    ppermute x30, waiting for transfers between devices, body(): gather.blocks[target] = lax.ppermute(block, 'shard', gather.steps[axis])  134 us
    pallas_call x5, Pallas kernels, pair_scores(): pl.pallas_call(functools.partial(pair_kernel, frames, idx_dev, len(blocks...  53 us
    ppermute x30, starting transfers between devices, body(): gather.blocks[target] = lax.ppermute(block, 'shard', gather.steps[axis])  40.7 us
    unnamed x41, local copies, waits for them, and re-layouts  16.6 us
    pallas_call x1, Pallas kernels, pair_lists(): pl.pallas_call(functools.partial(list_kernel, idx_dev, k_count, ids.shape...  13.9 us
    all_to_all x1, blocking collectives, body(): lax.all_to_all(table.reshape(devices, pairs), 'shard', split_axis=0, conc...  13.2 us
    slice x8, local copies, waits for them, and re-layouts, block(): parts = [b[at:at + n] for b, (_, at, n) in zip(whole, self.pieces[key])]  10.8 us
    pallas_call x1, Pallas kernels, head_matrices(): pl.pallas_call(head_kernel, out_shape=[jax.ShapeDtypeStruct(s, jnp.bfloat...  8.54 us
  transfers between devices with their start and end apart: 32, of which 21 were waited for; matrix products, arithmetic and copies ran while one was open for 9% of the time, Pallas kernels for 21%

profile of v14, /device:TPU:0, one launch (start us, length us, event | category | flops | bytes accessed | tf_op | source)
XLA Modules:
  0.0 317.1 jit_solution(13046916197736840596)
XLA Ops:
  8.2 1.6 fusion
  9.8 3.0 collective-permute-start
  12.9 1.5 collective-permute-start.1
  14.4 1.4 slice.70
  15.8 1.6 collective-permute-start.4
  18.4 22.1 %collective-permute-done.rest_2_ = bf16[8,8,9600]{2,1,0:T(8,128)(2,1)} collective-permute-done((bf16[8,8,9600]{2,1,0:T(8,128)(2,1)}, bf16[8,8,9600]{2,1,0:T(8,128)(2,1)}, u32[]{:S(2)}, u32[]{:S(2)}) %collective-permute-start) | collective-permute-done | bytes 1228832 | tf_op jit(solution)/shard_map/ppermute | solution.py:466
  40.5 2.6 collective-permute-done.1.rest_1_
  43.1 1.5 collective-permute-start.2
  47.3 4.9 %all-to-all-start = ((s32[32,1,128]{2,1,0:T(1,128)}), s32[32,1,128]{2,1,0:T(1,128)S(1)}, u32[]{:S(2)}, u32[]{:S(2)}) async-start(s32[32,1,128]{2,1,0:T(1,128)} %broadcast_in_dim.42), calls=%async_computation | async-start | bytes 32768 | tf_op jit(solution)/shard_map/all_to_all | solution.py:470
  52.3 8.5 %head_matrices.1 = (bf16[64,2048]{1,0:T(8,128)(2,1)S(1)}, bf16[512,1024]{1,0:T(8,128)(2,1)S(1)}, bf16[256,256]{1,0:T(8,128)(2,1)S(1)}) custom-call(bf16[9,1,32]{2,1,0:T(2,128)(2,1)S(1)} %reshape.74.one_w, bf16[9,32,64]{2,1,0:T(8,128)(2,1)S(1)} %bitcast.16, bf16[9,1,64]{2,1,0:T(2,128)(2,1)S(1)} %reshape.75.three_w), custom_call_target="tpu_custom_call" | custom-call | flops 1000000000 | bytes 3000000 | tf_op jit(solution)/shard_map/head_matrices/pallas_call | solution.py:90
  63.8 5.7 %collective-permute-done.5.rest_4_ = bf16[8,8,9600]{2,1,0:T(8,128)(2,1)S(1)} collective-permute-done((bf16[8,8,9600]{2,1,0:T(8,128)(2,1)}, bf16[8,8,9600]{2,1,0:T(8,128)(2,1)S(1)}, u32[]{:S(2)}, u32[]{:S(2)}) %collective-permute-start.5) | collective-permute-done | bytes 1228832 | tf_op jit(solution)/shard_map/ppermute | solution.py:466
  70.6 1.3 slice.54
  71.9 2.0 collective-permute-start.8
  73.9 1.6 collective-permute-start.7
  75.4 20.5 %collective-permute-done.2.rest_6_ = bf16[8,8,9600]{2,1,0:T(8,128)(2,1)} collective-permute-done((bf16[8,8,9600]{2,1,0:T(8,128)(2,1)}, bf16[8,8,9600]{2,1,0:T(8,128)(2,1)}, u32[]{:S(2)}, u32[]{:S(2)}) %collective-permute-start.2) | collective-permute-done | bytes 1228832 | tf_op jit(solution)/shard_map/ppermute | solution.py:466
  95.9 1.5 collective-permute-start.10
  98.5 13.9 %pair_lists.1 = (s32[152]{0:T(256)}, s32[152]{0:T(256)}, s32[151]{0:T(256)}, s32[149]{0:T(256)}, s32[83]{0:T(128)}) custom-call(s32[18]{0:T(128)} %pad_add_fusion.who_ref, s32[32,128]{1,0:T(8,128)} %bitcast.19, s32[256]{0:T(256)} %constant.41.clone.queries_ref), custom_call_target="tpu_custom_call" | custom-call | flops 99999997952 | bytes 1000000 | tf_op jit(solution)/shard_map/pair_lists/pallas_call | solution.py:136
  113.1 5.8 %collective-permute-done.8.rest_1_ = bf16[7,8,9600]{2,1,0:T(8,128)(2,1)S(1)} collective-permute-done((bf16[7,8,9600]{2,1,0:T(8,128)(2,1)}, bf16[7,8,9600]{2,1,0:T(8,128)(2,1)S(1)}, u32[]{:S(2)}, u32[]{:S(2)}) %collective-permute-start.8) | collective-permute-done | bytes 1075232 | tf_op jit(solution)/shard_map/ppermute | solution.py:466
  118.9 1.5 collective-permute-start.13
  120.9 1.6 collective-permute-start.12
  123.1 13.6 %phase_0.1.before_ref = f32[16,128]{1,0:T(8,128)} custom-call(s32[152]{0:T(256)} %get-tuple-element.68.list_ref, bf16[64,2048]{1,0:T(8,128)(2,1)} %copy-done.2, bf16[512,1024]{1,0:T(8,128)(2,1)} %copy-done.1, bf16[256,256]{1,0:T(8,128)(2,1)} %copy-done.3, f32[16,128]{1,0:T(8,128)} %broadcast_in_dim.43.before_ref, ...), custom_call_target="tpu_custom_call" | custom-call | flops 100663296000 | bytes 39321600 | tf_op jit(solution)/shard_map/phase_0/pallas_call | solution.py:258
  136.7 2.0 collective-permute-done.10.rest_3_
  138.8 1.2 slice.57
  140.0 1.3 slice.56
  141.3 1.6 slice_dynamic-update-slice_fusion.7
  142.9 2.0 collective-permute-start.16
  144.9 1.6 slice_dynamic-update-slice_fusion.6
  146.5 1.6 slice_dynamic-update-slice_fusion.5
  148.1 1.6 slice_dynamic-update-slice_fusion.4
  149.7 1.7 slice_dynamic-update-slice_fusion.3
  151.4 1.7 slice_dynamic-update-slice_fusion.2
  153.1 1.7 slice_dynamic-update-slice_fusion.1
  154.8 1.7 slice_dynamic-update-slice_fusion
  156.5 2.0 collective-permute-done.13.rest_6_
  158.5 2.0 collective-permute-start.17
  160.6 7.9 %collective-permute-done.12.rest_5_ = bf16[13,8,9600]{2,1,0:T(8,128)(2,1)S(1)} collective-permute-done((bf16[13,8,9600]{2,1,0:T(8,128)(2,1)}, bf16[13,8,9600]{2,1,0:T(8,128)(2,1)S(1)}, u32[]{:S(2)}, u32[]{:S(2)}) %collective-permute-start.12) | collective-permute-done | bytes 1996832 | tf_op jit(solution)/shard_map/ppermute | solution.py:466
  168.7 1.9 collective-permute-start.19
  170.5 8.5 %collective-permute-done.16.rest_1_ = bf16[6,8,9600]{2,1,0:T(8,128)(2,1)} collective-permute-done((bf16[6,8,9600]{2,1,0:T(8,128)(2,1)S(1)}, bf16[6,8,9600]{2,1,0:T(8,128)(2,1)}, u32[]{:S(2)}, u32[]{:S(2)}) %collective-permute-start.16) | collective-permute-done | bytes 921632 | tf_op jit(solution)/shard_map/ppermute | solution.py:466
  179.0 2.6 collective-permute-done.15.rest_0_
  181.6 1.5 collective-permute-start.20
  183.6 10.4 %phase_1.1.before_ref = f32[16,128]{1,0:T(8,128)} custom-call(s32[152]{0:T(256)} %get-tuple-element.67.list_ref, bf16[64,2048]{1,0:T(8,128)(2,1)} %copy-done.2, bf16[512,1024]{1,0:T(8,128)(2,1)} %copy-done.1, bf16[256,256]{1,0:T(8,128)(2,1)} %copy-done.3, f32[16,128]{1,0:T(8,128)} %phase_0.1.before_ref, ...), custom_call_target="tpu_custom_call" | custom-call | flops 100663296000 | bytes 39321600 | tf_op jit(solution)/shard_map/phase_1/pallas_call | solution.py:258
  194.0 7.3 %collective-permute-done.18.rest_3_ = bf16[6,8,9600]{2,1,0:T(8,128)(2,1)} collective-permute-done((bf16[6,8,9600]{2,1,0:T(8,128)(2,1)S(1)}, bf16[6,8,9600]{2,1,0:T(8,128)(2,1)}, u32[]{:S(2)}, u32[]{:S(2)}) %collective-permute-start.18) | collective-permute-done | bytes 921632 | tf_op jit(solution)/shard_map/ppermute | solution.py:466
  201.9 1.6 slice.67
  203.5 1.3 slice.66
  205.0 2.5 collective-permute-start.22
  207.4 1.5 collective-permute-start.24
  209.0 1.5 collective-permute-start.23
  210.5 10.6 %collective-permute-done.20.rest_5_ = bf16[6,8,9600]{2,1,0:T(8,128)(2,1)} collective-permute-done((bf16[6,8,9600]{2,1,0:T(8,128)(2,1)}, bf16[6,8,9600]{2,1,0:T(8,128)(2,1)}, u32[]{:S(2)}, u32[]{:S(2)}) %collective-permute-start.20) | collective-permute-done | bytes 921632 | tf_op jit(solution)/shard_map/ppermute | solution.py:466
  221.1 4.0 %collective-permute-done.21.rest_6_ = bf16[7,8,9600]{2,1,0:T(8,128)(2,1)} collective-permute-done((bf16[7,8,9600]{2,1,0:T(8,128)(2,1)}, bf16[7,8,9600]{2,1,0:T(8,128)(2,1)}, u32[]{:S(2)}, u32[]{:S(2)}) %collective-permute-start.21) | collective-permute-done | bytes 1075232 | tf_op jit(solution)/shard_map/ppermute | solution.py:466
  225.0 2.5 collective-permute-start.25
  227.6 1.5 collective-permute-start.26
  229.1 10.9 %phase_2.1.before_ref = f32[16,128]{1,0:T(8,128)} custom-call(s32[151]{0:T(256)} %get-tuple-element.66.list_ref, bf16[64,2048]{1,0:T(8,128)(2,1)} %copy-done.2, bf16[512,1024]{1,0:T(8,128)(2,1)} %copy-done.1, bf16[256,256]{1,0:T(8,128)(2,1)} %copy-done.3, f32[16,128]{1,0:T(8,128)} %phase_1.1.before_ref, ...), custom_call_target="tpu_custom_call" | custom-call | flops 100663296000 | bytes 39321600 | tf_op jit(solution)/shard_map/phase_2/pallas_call | solution.py:258
  239.9 6.2 %collective-permute-done.22.rest_0_ = bf16[12,8,9600]{2,1,0:T(8,128)(2,1)S(1)} collective-permute-done((bf16[12,8,9600]{2,1,0:T(8,128)(2,1)}, bf16[12,8,9600]{2,1,0:T(8,128)(2,1)S(1)}, u32[]{:S(2)}, u32[]{:S(2)}) %collective-permute-start.22) | collective-permute-done | bytes 1843232 | tf_op jit(solution)/shard_map/ppermute | solution.py:466
  246.1 1.7 collective-permute-start.27
  247.8 1.3 collective-permute-start.28
  249.1 1.8 collective-permute-start.29
  250.9 13.0 %collective-permute-done.25.rest_3_ = bf16[6,8,9600]{2,1,0:T(8,128)(2,1)} collective-permute-done((bf16[6,8,9600]{2,1,0:T(8,128)(2,1)S(1)}, bf16[6,8,9600]{2,1,0:T(8,128)(2,1)}, u32[]{:S(2)}, u32[]{:S(2)}) %collective-permute-start.25) | collective-permute-done | bytes 921632 | tf_op jit(solution)/shard_map/ppermute | solution.py:466
  263.9 4.0 %collective-permute-done.26.rest_4_ = bf16[7,8,9600]{2,1,0:T(8,128)(2,1)} collective-permute-done((bf16[7,8,9600]{2,1,0:T(8,128)(2,1)S(1)}, bf16[7,8,9600]{2,1,0:T(8,128)(2,1)}, u32[]{:S(2)}, u32[]{:S(2)}) %collective-permute-start.26) | collective-permute-done | bytes 1075232 | tf_op jit(solution)/shard_map/ppermute | solution.py:466
  267.8 10.3 %phase_3.1.before_ref = f32[16,128]{1,0:T(8,128)} custom-call(s32[149]{0:T(256)} %get-tuple-element.65.list_ref, bf16[64,2048]{1,0:T(8,128)(2,1)} %copy-done.2, bf16[512,1024]{1,0:T(8,128)(2,1)} %copy-done.1, bf16[256,256]{1,0:T(8,128)(2,1)} %copy-done.3, f32[16,128]{1,0:T(8,128)} %phase_2.1.before_ref, ...), custom_call_target="tpu_custom_call" | custom-call | flops 100663296000 | bytes 39321600 | tf_op jit(solution)/shard_map/phase_3/pallas_call | solution.py:258
  278.2 5.4 %collective-permute-done.28.rest_1_ = bf16[6,8,9600]{2,1,0:T(8,128)(2,1)} collective-permute-done((bf16[6,8,9600]{2,1,0:T(8,128)(2,1)}, bf16[6,8,9600]{2,1,0:T(8,128)(2,1)}, u32[]{:S(2)}, u32[]{:S(2)}) %collective-permute-start.28) | collective-permute-done | bytes 921632 | tf_op jit(solution)/shard_map/ppermute | solution.py:466
  283.6 2.9 collective-permute-done.29.rest_2_
  286.5 1.2 copy-done.14
  287.7 7.8 %phase_4.1 = f32[16,128]{1,0:T(8,128)} custom-call(s32[83]{0:T(128)} %get-tuple-element.61.list_ref, bf16[64,2048]{1,0:T(8,128)(2,1)} %copy-done.2, bf16[512,1024]{1,0:T(8,128)(2,1)} %copy-done.1, bf16[256,256]{1,0:T(8,128)(2,1)} %copy-done.3, f32[16,128]{1,0:T(8,128)} %phase_3.1.before_ref, bf16[256,8,9600]{2,1,0:T(8,128)(2,1)} %all-gather.2.cloned.1.call-done.v_hbm, ...), custom_call_target="tpu_custom_call" | custom-call | flops 50331648000 | bytes 19660800 | tf_op jit(solution)/shard_map/phase_4/pallas_call | solution.py:258
  296.3 13.2 %all_to_all.14 = f32[32,1,128]{2,1,0:T(1,128)S(1)} all-to-all(f32[32,1,128]{2,1,0:T(1,128)S(1)} %broadcast_select_fusion), channel_id=1, replica_groups=mesh['shard'=32] {'shard'}, dimensions={0} | all-to-all | bytes 32768 | tf_op jit(solution)/shard_map/all_to_all | solution.py:482
  (75 shorter events, 15.4 us)
Async XLA Ops:
  6.5 1.7 copy-start.4
  6.5 116.0 %all-gather.2.cloned.1.call-start = ((), (), s32[]{:S(2)}) async-start(), calls=%async_computation.2 | async-start | bytes 58982400 | tf_op jit(solution)/shard_map/all_gather | solution.py:402
  9.8 35.3 %copy-start.10 = (bf16[32,1,3,3]{0,3,2,1:T(4,128)(2,1)S(1)}, bf16[32,1,3,3]{0,3,2,1:T(4,128)(2,1)}, u32[]{:S(2)}) copy-start(bf16[32,1,3,3]{0,3,2,1:T(4,128)(2,1)} %param.11) | copy-start | bytes 1732
  9.8 35.3 %copy-start.11 = (bf16[1,64,3,3]{1,3,2,0:T(4,128)(2,1)S(1)}, bf16[1,64,3,3]{1,3,2,0:T(4,128)(2,1)}, u32[]{:S(2)}) copy-start(bf16[1,64,3,3]{1,3,2,0:T(4,128)(2,1)} %param.13) | copy-start | bytes 3460
  9.8 36.7 %copy-start.9 = (s32[16,8]{0,1:T(8,128)S(1)}, s32[16,8]{0,1:T(8,128)}, u32[]{:S(2)}) copy-start(s32[16,8]{0,1:T(8,128)} %param.10) | copy-start | bytes 1540
  9.8 42.4 %copy-start = (bf16[64,32,3,3]{0,1,3,2:T(8,128)(2,1)S(1)}, bf16[64,32,3,3]{0,1,3,2:T(8,128)(2,1)}, u32[]{:S(2)}) copy-start(bf16[64,32,3,3]{0,1,3,2:T(8,128)(2,1)} %param.12) | copy-start | bytes 110596
  9.8 30.7 %collective-permute-start = (bf16[8,8,9600]{2,1,0:T(8,128)(2,1)}, bf16[8,8,9600]{2,1,0:T(8,128)(2,1)}, u32[]{:S(2)}, u32[]{:S(2)}) collective-permute-start(bf16[8,8,9600]{2,1,0:T(8,128)(2,1)} %get-tuple-element.87), channel_id=1, source_target_pairs={{0,4},{1,3},{2,6},{3,1},{4,0},{5,7},{6,2},{7,5},{8,12},{9,11},{10,... | collective-permute-start | bytes 3686408 | tf_op jit(solution)/shard_map/ppermute | solution.py:466
  12.9 30.3 %collective-permute-start.1 = (bf16[8,8,9600]{2,1,0:T(8,128)(2,1)}, bf16[8,8,9600]{2,1,0:T(8,128)(2,1)}, u32[]{:S(2)}, u32[]{:S(2)}) collective-permute-start(bf16[8,8,9600]{2,1,0:T(8,128)(2,1)} %get-tuple-element.83), channel_id=1, source_target_pairs={{0,2},{1,5},{2,0},{3,7},{4,6},{5,1},{6,4},{7,3},{8,10},{9,13},{10,... | collective-permute-start | bytes 3686408 | tf_op jit(solution)/shard_map/ppermute | solution.py:466
  15.8 53.7 %collective-permute-start.4 = (bf16[13,8,9600]{2,1,0:T(8,128)(2,1)}, bf16[13,8,9600]{2,1,0:T(8,128)(2,1)S(1)}, u32[]{:S(2)}, u32[]{:S(2)}) collective-permute-start(bf16[13,8,9600]{2,1,0:T(8,128)(2,1)} %slice.70), channel_id=1, source_target_pairs={{0,8},{1,9},{2,10},{3,11},{4,12},{5,13},{6,14},{7,15},{8,24},{9,25... | collective-permute-start | bytes 5990408 | tf_op jit(solution)/shard_map/ppermute | solution.py:466
  17.3 52.1 %collective-permute-start.5 = (bf16[8,8,9600]{2,1,0:T(8,128)(2,1)}, bf16[8,8,9600]{2,1,0:T(8,128)(2,1)S(1)}, u32[]{:S(2)}, u32[]{:S(2)}) collective-permute-start(bf16[8,8,9600]{2,1,0:T(8,128)(2,1)} %get-tuple-element.69), channel_id=1, source_target_pairs={{0,2},{1,5},{2,0},{3,7},{4,6},{5,1},{6,4},{7,3},{8,10},{9,13},{10,... | collective-permute-start | bytes 3686408 | tf_op jit(solution)/shard_map/ppermute | solution.py:466
  17.9 51.6 %collective-permute-start.6 = (bf16[8,8,9600]{2,1,0:T(8,128)(2,1)}, bf16[8,8,9600]{2,1,0:T(8,128)(2,1)}, u32[]{:S(2)}, u32[]{:S(2)}) collective-permute-start(bf16[8,8,9600]{2,1,0:T(8,128)(2,1)} %get-tuple-element.70), channel_id=1, source_target_pairs={{0,4},{1,3},{2,6},{3,1},{4,0},{5,7},{6,2},{7,5},{8,12},{9,11},{10,... | collective-permute-start | bytes 3686408 | tf_op jit(solution)/shard_map/ppermute | solution.py:466
  43.1 52.8 %collective-permute-start.2 = (bf16[8,8,9600]{2,1,0:T(8,128)(2,1)}, bf16[8,8,9600]{2,1,0:T(8,128)(2,1)}, u32[]{:S(2)}, u32[]{:S(2)}) collective-permute-start(bf16[8,8,9600]{2,1,0:T(8,128)(2,1)} %collective-permute-done.rest_2_), channel_id=1, source_target_pairs={{0,2},{1,5},{2,0},{3,7},{4,6},{5,1},{6,4},{7,3},{8,10},{9,13},{10,... | collective-permute-start | bytes 3686408 | tf_op jit(solution)/shard_map/ppermute | solution.py:466
  44.6 51.3 %collective-permute-start.3 = (bf16[8,8,9600]{2,1,0:T(8,128)(2,1)}, bf16[8,8,9600]{2,1,0:T(8,128)(2,1)}, u32[]{:S(2)}, u32[]{:S(2)}) collective-permute-start(bf16[8,8,9600]{2,1,0:T(8,128)(2,1)} %collective-permute-done.1.rest_1_), channel_id=1, source_target_pairs={{0,4},{1,3},{2,6},{3,1},{4,0},{5,7},{6,2},{7,5},{8,12},{9,11},{10,... | collective-permute-start | bytes 3686408 | tf_op jit(solution)/shard_map/ppermute | solution.py:466
  47.3 50.6 %all-to-all-start = ((s32[32,1,128]{2,1,0:T(1,128)}), s32[32,1,128]{2,1,0:T(1,128)S(1)}, u32[]{:S(2)}, u32[]{:S(2)}) async-start(s32[32,1,128]{2,1,0:T(1,128)} %broadcast_in_dim.42), calls=%async_computation | async-start | bytes 32768 | tf_op jit(solution)/shard_map/all_to_all | solution.py:470
  60.8 1.0 copy-start.1
  61.8 0.7 copy-start.2
  62.5 0.7 copy-start.3
  69.5 2.4 copy-start.7
  69.5 4.4 %copy-start.5 = (bf16[13,8,9600]{2,1,0:T(8,128)(2,1)}, bf16[13,8,9600]{2,1,0:T(8,128)(2,1)S(1)}, u32[]{:S(2)}) copy-start(bf16[13,8,9600]{2,1,0:T(8,128)(2,1)S(1)} %collective-permute-done.4.rest_3_) | copy-start | bytes 5990404
  71.9 41.3 %collective-permute-start.9 = (bf16[6,8,9600]{2,1,0:T(8,128)(2,1)}, bf16[6,8,9600]{2,1,0:T(8,128)(2,1)}, u32[]{:S(2)}, u32[]{:S(2)}) collective-permute-start(bf16[6,8,9600]{2,1,0:T(8,128)(2,1)} %slice.55), channel_id=1, source_target_pairs={{0,4},{1,3},{2,6},{3,1},{4,0},{5,7},{6,2},{7,5},{8,12},{9,11},{10,... | collective-permute-start | bytes 2764808 | tf_op jit(solution)/shard_map/ppermute | solution.py:466
  71.9 47.0 %collective-permute-start.8 = (bf16[7,8,9600]{2,1,0:T(8,128)(2,1)}, bf16[7,8,9600]{2,1,0:T(8,128)(2,1)S(1)}, u32[]{:S(2)}, u32[]{:S(2)}) collective-permute-start(bf16[7,8,9600]{2,1,0:T(8,128)(2,1)} %slice.54), channel_id=1, source_target_pairs={{0,2},{1,5},{2,0},{3,7},{4,6},{5,1},{6,4},{7,3},{8,10},{9,13},{10,... | collective-permute-start | bytes 3225608 | tf_op jit(solution)/shard_map/ppermute | solution.py:466
  73.9 45.1 %collective-permute-start.7 = (bf16[13,8,9600]{2,1,0:T(8,128)(2,1)S(1)}, bf16[13,8,9600]{2,1,0:T(8,128)(2,1)}, u32[]{:S(2)}, u32[]{:S(2)}) collective-permute-start(bf16[13,8,9600]{2,1,0:T(8,128)(2,1)S(1)} %collective-permute-done.4.rest_3_), channel_id=1, source_target_pairs={{0,8},{1,9},{2,10},{3,11},{4,12},{5,13},{6,14},{7,15},{8,24},{9,25... | collective-permute-start | bytes 5990408 | tf_op jit(solution)/shard_map/ppermute | solution.py:466
  95.9 42.8 %collective-permute-start.10 = (bf16[6,8,9600]{2,1,0:T(8,128)(2,1)}, bf16[6,8,9600]{2,1,0:T(8,128)(2,1)}, u32[]{:S(2)}, u32[]{:S(2)}) collective-permute-start(bf16[6,8,9600]{2,1,0:T(8,128)(2,1)} %slice.55), channel_id=1, source_target_pairs={{0,2},{1,5},{2,0},{3,7},{4,6},{5,1},{6,4},{7,3},{8,10},{9,13},{10,... | collective-permute-start | bytes 2764808 | tf_op jit(solution)/shard_map/ppermute | solution.py:466
  97.4 41.3 %collective-permute-start.11 = (bf16[7,8,9600]{2,1,0:T(8,128)(2,1)}, bf16[7,8,9600]{2,1,0:T(8,128)(2,1)}, u32[]{:S(2)}, u32[]{:S(2)}) collective-permute-start(bf16[7,8,9600]{2,1,0:T(8,128)(2,1)} %slice.54), channel_id=1, source_target_pairs={{0,4},{1,3},{2,6},{3,1},{4,0},{5,7},{6,2},{7,5},{8,12},{9,11},{10,... | collective-permute-start | bytes 3225608 | tf_op jit(solution)/shard_map/ppermute | solution.py:466
  97.9 0.6 copy-start.8
  118.9 17.8 %copy-start.15 = (bf16[7,8,9600]{2,1,0:T(8,128)(2,1)}, bf16[7,8,9600]{2,1,0:T(8,128)(2,1)S(1)}, u32[]{:S(2)}) copy-start(bf16[7,8,9600]{2,1,0:T(8,128)(2,1)S(1)} %collective-permute-done.8.rest_1_) | copy-start | bytes 3225604
  118.9 39.6 %collective-permute-start.13 = (bf16[6,8,9600]{2,1,0:T(8,128)(2,1)}, bf16[6,8,9600]{2,1,0:T(8,128)(2,1)}, u32[]{:S(2)}, u32[]{:S(2)}) collective-permute-start(bf16[6,8,9600]{2,1,0:T(8,128)(2,1)} %collective-permute-done.9.rest_2_), channel_id=1, source_target_pairs={{0,2},{1,5},{2,0},{3,7},{4,6},{5,1},{6,4},{7,3},{8,10},{9,13},{10,... | collective-permute-start | bytes 2764808 | tf_op jit(solution)/shard_map/ppermute | solution.py:466
  120.4 40.1 %collective-permute-start.14 = (bf16[7,8,9600]{2,1,0:T(8,128)(2,1)S(1)}, bf16[7,8,9600]{2,1,0:T(8,128)(2,1)}, u32[]{:S(2)}, u32[]{:S(2)}) collective-permute-start(bf16[7,8,9600]{2,1,0:T(8,128)(2,1)S(1)} %collective-permute-done.8.rest_1_), channel_id=1, source_target_pairs={{0,4},{1,3},{2,6},{3,1},{4,0},{5,7},{6,2},{7,5},{8,12},{9,11},{10,... | collective-permute-start | bytes 3225608 | tf_op jit(solution)/shard_map/ppermute | solution.py:466
  120.9 47.5 %collective-permute-start.12 = (bf16[13,8,9600]{2,1,0:T(8,128)(2,1)}, bf16[13,8,9600]{2,1,0:T(8,128)(2,1)S(1)}, u32[]{:S(2)}, u32[]{:S(2)}) collective-permute-start(bf16[13,8,9600]{2,1,0:T(8,128)(2,1)} %collective-permute-done.7.rest_0_), channel_id=1, source_target_pairs={{0,8},{1,9},{2,10},{3,11},{4,12},{5,13},{6,14},{7,15},{8,24},{9,25... | collective-permute-start | bytes 5990408 | tf_op jit(solution)/shard_map/ppermute | solution.py:466
  142.9 36.0 %collective-permute-start.16 = (bf16[6,8,9600]{2,1,0:T(8,128)(2,1)S(1)}, bf16[6,8,9600]{2,1,0:T(8,128)(2,1)}, u32[]{:S(2)}, u32[]{:S(2)}) collective-permute-start(bf16[6,8,9600]{2,1,0:T(8,128)(2,1)S(1)} %slice.57), channel_id=1, source_target_pairs={{0,4},{1,3},{2,6},{3,1},{4,0},{5,7},{6,2},{7,5},{8,12},{9,11},{10,... | collective-permute-start | bytes 2764808 | tf_op jit(solution)/shard_map/ppermute | solution.py:466
  144.9 36.6 %collective-permute-start.15 = (bf16[7,8,9600]{2,1,0:T(8,128)(2,1)S(1)}, bf16[7,8,9600]{2,1,0:T(8,128)(2,1)}, u32[]{:S(2)}, u32[]{:S(2)}) collective-permute-start(bf16[7,8,9600]{2,1,0:T(8,128)(2,1)S(1)} %slice.56), channel_id=1, source_target_pairs={{0,2},{1,5},{2,0},{3,7},{4,6},{5,1},{6,4},{7,3},{8,10},{9,13},{10,... | collective-permute-start | bytes 3225608 | tf_op jit(solution)/shard_map/ppermute | solution.py:466
  158.5 46.5 %collective-permute-start.17 = (bf16[12,8,9600]{2,1,0:T(8,128)(2,1)}, bf16[12,8,9600]{2,1,0:T(8,128)(2,1)}, u32[]{:S(2)}, u32[]{:S(2)}) collective-permute-start(bf16[12,8,9600]{2,1,0:T(8,128)(2,1)} %slice_dynamic-update-slice_fusion), channel_id=1, source_target_pairs={{0,8},{1,9},{2,10},{3,11},{4,12},{5,13},{6,14},{7,15},{8,24},{9,25... | collective-permute-start | bytes 5529608 | tf_op jit(solution)/shard_map/ppermute | solution.py:466
  168.5 15.1 %copy-start.6 = (bf16[13,8,9600]{2,1,0:T(8,128)(2,1)}, bf16[13,8,9600]{2,1,0:T(8,128)(2,1)S(1)}, u32[]{:S(2)}) copy-start(bf16[13,8,9600]{2,1,0:T(8,128)(2,1)S(1)} %collective-permute-done.12.rest_5_) | copy-start | bytes 5990404
  168.5 32.9 %collective-permute-start.18 = (bf16[6,8,9600]{2,1,0:T(8,128)(2,1)S(1)}, bf16[6,8,9600]{2,1,0:T(8,128)(2,1)}, u32[]{:S(2)}, u32[]{:S(2)}) collective-permute-start(bf16[6,8,9600]{2,1,0:T(8,128)(2,1)S(1)} %slice.57), channel_id=1, source_target_pairs={{0,2},{1,5},{2,0},{3,7},{4,6},{5,1},{6,4},{7,3},{8,10},{9,13},{10,... | collective-permute-start | bytes 2764808 | tf_op jit(solution)/shard_map/ppermute | solution.py:466
  168.7 33.2 %collective-permute-start.19 = (bf16[7,8,9600]{2,1,0:T(8,128)(2,1)S(1)}, bf16[7,8,9600]{2,1,0:T(8,128)(2,1)S(1)}, u32[]{:S(2)}, u32[]{:S(2)}) collective-permute-start(bf16[7,8,9600]{2,1,0:T(8,128)(2,1)S(1)} %slice.56), channel_id=1, source_target_pairs={{0,4},{1,3},{2,6},{3,1},{4,0},{5,7},{6,2},{7,5},{8,12},{9,11},{10,... | collective-permute-start | bytes 3225608 | tf_op jit(solution)/shard_map/ppermute | solution.py:466
  181.6 39.5 %collective-permute-start.20 = (bf16[6,8,9600]{2,1,0:T(8,128)(2,1)}, bf16[6,8,9600]{2,1,0:T(8,128)(2,1)}, u32[]{:S(2)}, u32[]{:S(2)}) collective-permute-start(bf16[6,8,9600]{2,1,0:T(8,128)(2,1)} %collective-permute-done.16.rest_1_), channel_id=1, source_target_pairs={{0,2},{1,5},{2,0},{3,7},{4,6},{5,1},{6,4},{7,3},{8,10},{9,13},{10,... | collective-permute-start | bytes 2764808 | tf_op jit(solution)/shard_map/ppermute | solution.py:466
  183.1 42.0 %collective-permute-start.21 = (bf16[7,8,9600]{2,1,0:T(8,128)(2,1)}, bf16[7,8,9600]{2,1,0:T(8,128)(2,1)}, u32[]{:S(2)}, u32[]{:S(2)}) collective-permute-start(bf16[7,8,9600]{2,1,0:T(8,128)(2,1)} %collective-permute-done.15.rest_0_), channel_id=1, source_target_pairs={{0,4},{1,3},{2,6},{3,1},{4,0},{5,7},{6,2},{7,5},{8,12},{9,11},{10,... | collective-permute-start | bytes 3225608 | tf_op jit(solution)/shard_map/ppermute | solution.py:466
  201.9 2.9 copy-start.16
  205.0 41.1 %collective-permute-start.22 = (bf16[12,8,9600]{2,1,0:T(8,128)(2,1)}, bf16[12,8,9600]{2,1,0:T(8,128)(2,1)S(1)}, u32[]{:S(2)}, u32[]{:S(2)}) collective-permute-start(bf16[12,8,9600]{2,1,0:T(8,128)(2,1)} %collective-permute-done.17.rest_2_), channel_id=1, source_target_pairs={{0,8},{1,9},{2,10},{3,11},{4,12},{5,13},{6,14},{7,15},{8,24},{9,25... | collective-permute-start | bytes 5529608 | tf_op jit(solution)/shard_map/ppermute | solution.py:466
  207.4 40.4 %collective-permute-start.24 = (bf16[6,8,9600]{2,1,0:T(8,128)(2,1)S(1)}, bf16[6,8,9600]{2,1,0:T(8,128)(2,1)}, u32[]{:S(2)}, u32[]{:S(2)}) collective-permute-start(bf16[6,8,9600]{2,1,0:T(8,128)(2,1)S(1)} %slice.67), channel_id=1, source_target_pairs={{0,4},{1,3},{2,6},{3,1},{4,0},{5,7},{6,2},{7,5},{8,12},{9,11},{10,... | collective-permute-start | bytes 2764808 | tf_op jit(solution)/shard_map/ppermute | solution.py:466
  209.0 38.8 %collective-permute-start.23 = (bf16[7,8,9600]{2,1,0:T(8,128)(2,1)S(1)}, bf16[7,8,9600]{2,1,0:T(8,128)(2,1)}, u32[]{:S(2)}, u32[]{:S(2)}) collective-permute-start(bf16[7,8,9600]{2,1,0:T(8,128)(2,1)S(1)} %slice.66), channel_id=1, source_target_pairs={{0,2},{1,5},{2,0},{3,7},{4,6},{5,1},{6,4},{7,3},{8,10},{9,13},{10,... | collective-permute-start | bytes 3225608 | tf_op jit(solution)/shard_map/ppermute | solution.py:466
  225.0 38.8 %collective-permute-start.25 = (bf16[6,8,9600]{2,1,0:T(8,128)(2,1)S(1)}, bf16[6,8,9600]{2,1,0:T(8,128)(2,1)}, u32[]{:S(2)}, u32[]{:S(2)}) collective-permute-start(bf16[6,8,9600]{2,1,0:T(8,128)(2,1)S(1)} %slice.67), channel_id=1, source_target_pairs={{0,2},{1,5},{2,0},{3,7},{4,6},{5,1},{6,4},{7,3},{8,10},{9,13},{10,... | collective-permute-start | bytes 2764808 | tf_op jit(solution)/shard_map/ppermute | solution.py:466
  227.6 40.3 %collective-permute-start.26 = (bf16[7,8,9600]{2,1,0:T(8,128)(2,1)S(1)}, bf16[7,8,9600]{2,1,0:T(8,128)(2,1)}, u32[]{:S(2)}, u32[]{:S(2)}) collective-permute-start(bf16[7,8,9600]{2,1,0:T(8,128)(2,1)S(1)} %slice.66), channel_id=1, source_target_pairs={{0,4},{1,3},{2,6},{3,1},{4,0},{5,7},{6,2},{7,5},{8,12},{9,11},{10,... | collective-permute-start | bytes 3225608 | tf_op jit(solution)/shard_map/ppermute | solution.py:466
  246.1 21.7 %copy-start.13 = (bf16[12,8,9600]{2,1,0:T(8,128)(2,1)}, bf16[12,8,9600]{2,1,0:T(8,128)(2,1)S(1)}, u32[]{:S(2)}) copy-start(bf16[12,8,9600]{2,1,0:T(8,128)(2,1)S(1)} %collective-permute-done.22.rest_0_) | copy-start | bytes 5529604
  246.1 40.4 %collective-permute-start.27 = (bf16[12,8,9600]{2,1,0:T(8,128)(2,1)S(1)}, bf16[12,8,9600]{2,1,0:T(8,128)(2,1)S(1)}, u32[]{:S(2)}, u32[]{:S(2)}) collective-permute-start(bf16[12,8,9600]{2,1,0:T(8,128)(2,1)S(1)} %collective-permute-done.22.rest_0_), channel_id=1, source_target_pairs={{0,8},{1,9},{2,10},{3,11},{4,12},{5,13},{6,14},{7,15},{8,24},{9,25... | collective-permute-start | bytes 5529608 | tf_op jit(solution)/shard_map/ppermute | solution.py:466
  247.8 35.8 %collective-permute-start.28 = (bf16[6,8,9600]{2,1,0:T(8,128)(2,1)}, bf16[6,8,9600]{2,1,0:T(8,128)(2,1)}, u32[]{:S(2)}, u32[]{:S(2)}) collective-permute-start(bf16[6,8,9600]{2,1,0:T(8,128)(2,1)} %collective-permute-done.24.rest_2_), channel_id=1, source_target_pairs={{0,2},{1,5},{2,0},{3,7},{4,6},{5,1},{6,4},{7,3},{8,10},{9,13},{10,... | collective-permute-start | bytes 2764808 | tf_op jit(solution)/shard_map/ppermute | solution.py:466
  249.1 37.4 %collective-permute-start.29 = (bf16[7,8,9600]{2,1,0:T(8,128)(2,1)}, bf16[7,8,9600]{2,1,0:T(8,128)(2,1)}, u32[]{:S(2)}, u32[]{:S(2)}) collective-permute-start(bf16[7,8,9600]{2,1,0:T(8,128)(2,1)} %collective-permute-done.23.rest_1_), channel_id=1, source_target_pairs={{0,4},{1,3},{2,6},{3,1},{4,0},{5,7},{6,2},{7,5},{8,12},{9,11},{10,... | collective-permute-start | bytes 3225608 | tf_op jit(solution)/shard_map/ppermute | solution.py:466
  286.5 1.2 copy-start.14
  287.7 8.5 %copy-start.12 = (pred[32]{0:T(512)(128)(4,1)S(1)}, pred[32]{0:T(512)(128)(4,1)}, u32[]{:S(2)}) copy-start(pred[32]{0:T(512)(128)(4,1)} %broadcast_in_dim.39) | copy-start | bytes 100
Sparse Core Ops, SparseCore 0:
  8.9 62.0 all-gather.1

commit v15 on v14

--- a/solution.py
+++ b/solution.py
@@ -111,8 +111,8 @@
                 packed = queries_ref[t]
                 row, first = packed & 255, ((packed >> 8) & 255) * k_count
                 sender = who_ref[2 + (packed >> 16)]
-                base = ((sender * pairs + first) << (8 + bits)) + (row << bits)
                 line = 2 * sender + core
+                base = ((line * pairs + first) << (8 + bits)) + (row << bits)
                 for k in range(k_count):
                     vid = ids_ref[line, first + k] - begin
                     list_ref[n] = base + (k << (8 + bits)) + (vid & ((1 << bits) - 1))
@@ -270,7 +270,7 @@
             pltpu.SemaphoreType.DMA((2,)),
             pltpu.SemaphoreType.DMA((2,)),
         ],
-        compiler_params=pltpu.CompilerParams(vmem_limit_bytes=58 * 1024 * 1024),
+        compiler_params=pltpu.CompilerParams(vmem_limit_bytes=66000000),
         cost_estimate=pl.CostEstimate(
             flops=WEIGHT * 2 * cap * side * R * R * frames * (width // R),
             bytes_accessed=cap * frames * width * 4, transcendentals=0,
@@ -439,7 +439,7 @@
 
     state = {}
     heads = head_matrices(conv_one, conv_two, conv_three)
-    tables = [jnp.zeros((chips, pairs), jnp.float32)]
+    tables = [jnp.zeros((devices, pairs), jnp.float32)]
 
     def score():
         p = len(tables) - 1
@@ -478,10 +478,7 @@
             )
     while len(tables) <= len(ends):
         score()
-    table = jnp.where(jnp.arange(2)[None, :, None] == core, tables[-1][:, None], 0.0)
-    scores = lax.all_to_all(
-        table.reshape(devices, pairs), "shard", split_axis=0, concat_axis=0, tiled=True
-    )
+    scores = lax.all_to_all(tables[-1], "shard", split_axis=0, concat_axis=0, tiled=True)
     return jnp.sum(scores, axis=0).reshape(q_dev, k_count)
 
 

time: 321 us -> 317 us (0.988); the launches traced: 317 us -> 317 us
  local copies, waits for them, and re-layouts: 33.3 us -> 30 us
    unnamed x41 -> x29, local copies, waits for them, and re-layouts: 16.6 us -> 13 us
    ppermute x30, waiting for transfers between devices: 134 us -> 138 us  [body(): gather.blocks[target] = lax.ppermute(block, 'shard', gather.steps[axis])]
  transfers between devices with their start and end apart: 32 -> 32, of which waited for: 21 -> 20; matrix products, arithmetic and copies ran while one was open for 9% -> 9% of each run, Pallas kernels for 21% -> 21%
where the time goes in v15:
time: 317 us
  waiting for transfers between devices  138 us (44%)
  Pallas kernels  74 us (23%)
  starting transfers between devices  45.2 us (14%)
  local copies, waits for them, and re-layouts  30 us (9%)
  blocking collectives  15.4 us (5%)
  between operations  13.6 us (4%)
    ppermute x30, waiting for transfers between devices, body(): gather.blocks[target] = lax.ppermute(block, 'shard', gather.steps[axis])  138 us
    pallas_call x5, Pallas kernels, pair_scores(): pl.pallas_call(functools.partial(pair_kernel, frames, idx_dev, len(blocks...  51.5 us
    ppermute x30, starting transfers between devices, body(): gather.blocks[target] = lax.ppermute(block, 'shard', gather.steps[axis])  40.3 us
    all_to_all x1, blocking collectives, body(): lax.all_to_all(tables[-1], 'shard', split_axis=0, concat_axis=0, tiled=True)  15.4 us
    pallas_call x1, Pallas kernels, pair_lists(): pl.pallas_call(functools.partial(list_kernel, idx_dev, k_count, ids.shape...  14 us
    unnamed x29, local copies, waits for them, and re-layouts  13 us
    slice x8, local copies, waits for them, and re-layouts, block(): parts = [b[at:at + n] for b, (_, at, n) in zip(whole, self.pieces[key])]  12.4 us
    pallas_call x1, Pallas kernels, head_matrices(): pl.pallas_call(head_kernel, out_shape=[jax.ShapeDtypeStruct(s, jnp.bfloat...  8.54 us
  transfers between devices with their start and end apart: 32, of which 20 were waited for; matrix products, arithmetic and copies ran while one was open for 9% of the time, Pallas kernels for 21%

profile of v15, /device:TPU:0, one launch (start us, length us, event | category | flops | bytes accessed | tf_op | source)
XLA Modules:
  0.0 317.3 jit_solution(13211498252310985422)
XLA Ops:
  7.3 1.0 copy-done.4
  8.2 1.6 fusion
  9.8 3.0 collective-permute-start
  12.9 1.5 collective-permute-start.1
  14.4 1.5 slice.70
  15.8 1.6 collective-permute-start.4
  18.4 22.1 %collective-permute-done.rest_2_ = bf16[8,8,9600]{2,1,0:T(8,128)(2,1)} collective-permute-done((bf16[8,8,9600]{2,1,0:T(8,128)(2,1)}, bf16[8,8,9600]{2,1,0:T(8,128)(2,1)}, u32[]{:S(2)}, u32[]{:S(2)}) %collective-permute-start) | collective-permute-done | bytes 1228832 | tf_op jit(solution)/shard_map/ppermute | solution.py:466
  40.5 2.6 collective-permute-done.1.rest_1_
  43.1 1.5 collective-permute-start.2
  47.3 4.9 %all-to-all-start = ((s32[32,1,128]{2,1,0:T(1,128)}), s32[32,1,128]{2,1,0:T(1,128)S(1)}, u32[]{:S(2)}, u32[]{:S(2)}) async-start(s32[32,1,128]{2,1,0:T(1,128)} %broadcast_in_dim.11), calls=%async_computation | async-start | bytes 32768 | tf_op jit(solution)/shard_map/all_to_all | solution.py:470
  52.2 8.5 %head_matrices.1 = (bf16[64,2048]{1,0:T(8,128)(2,1)S(1)}, bf16[512,1024]{1,0:T(8,128)(2,1)S(1)}, bf16[256,256]{1,0:T(8,128)(2,1)S(1)}) custom-call(bf16[9,1,32]{2,1,0:T(2,128)(2,1)S(1)} %reshape.27.one_w, bf16[9,32,64]{2,1,0:T(8,128)(2,1)S(1)} %bitcast.17, bf16[9,1,64]{2,1,0:T(2,128)(2,1)S(1)} %reshape.28.three_w), custom_call_target="tpu_custom_call" | custom-call | flops 1000000000 | bytes 3000000 | tf_op jit(solution)/shard_map/head_matrices/pallas_call | solution.py:90
  60.8 8.7 %collective-permute-done.5.rest_4_ = bf16[8,8,9600]{2,1,0:T(8,128)(2,1)S(1)} collective-permute-done((bf16[8,8,9600]{2,1,0:T(8,128)(2,1)}, bf16[8,8,9600]{2,1,0:T(8,128)(2,1)S(1)}, u32[]{:S(2)}, u32[]{:S(2)}) %collective-permute-start.5) | collective-permute-done | bytes 1228832 | tf_op jit(solution)/shard_map/ppermute | solution.py:466
  69.5 1.1 slice.55
  70.7 1.1 slice.54
  71.9 2.0 collective-permute-start.8
  73.9 1.6 collective-permute-start.7
  75.5 20.5 %collective-permute-done.2.rest_6_ = bf16[8,8,9600]{2,1,0:T(8,128)(2,1)} collective-permute-done((bf16[8,8,9600]{2,1,0:T(8,128)(2,1)}, bf16[8,8,9600]{2,1,0:T(8,128)(2,1)}, u32[]{:S(2)}, u32[]{:S(2)}) %collective-permute-start.2) | collective-permute-done | bytes 1228832 | tf_op jit(solution)/shard_map/ppermute | solution.py:466
  96.0 1.5 collective-permute-start.10
  98.6 14.0 %pair_lists.1 = (s32[152]{0:T(256)}, s32[152]{0:T(256)}, s32[151]{0:T(256)}, s32[149]{0:T(256)}, s32[83]{0:T(128)}) custom-call(s32[18]{0:T(128)} %pad_add_fusion.who_ref, s32[32,128]{1,0:T(8,128)} %bitcast.18, s32[256]{0:T(256)} %constant.41.clone.queries_ref), custom_call_target="tpu_custom_call" | custom-call | flops 99999997952 | bytes 1000000 | tf_op jit(solution)/shard_map/pair_lists/pallas_call | solution.py:136
  113.1 5.9 %collective-permute-done.8.rest_1_ = bf16[7,8,9600]{2,1,0:T(8,128)(2,1)} collective-permute-done((bf16[7,8,9600]{2,1,0:T(8,128)(2,1)}, bf16[7,8,9600]{2,1,0:T(8,128)(2,1)}, u32[]{:S(2)}, u32[]{:S(2)}) %collective-permute-start.8) | collective-permute-done | bytes 1075232 | tf_op jit(solution)/shard_map/ppermute | solution.py:466
  119.0 1.5 collective-permute-start.13
  121.0 1.6 collective-permute-start.12
  123.2 14.5 %phase_0.1.before_ref = f32[32,128]{1,0:T(8,128)} custom-call(s32[152]{0:T(256)} %get-tuple-element.68.list_ref, bf16[64,2048]{1,0:T(8,128)(2,1)} %copy-done.2, bf16[512,1024]{1,0:T(8,128)(2,1)} %copy-done.1, bf16[256,256]{1,0:T(8,128)(2,1)} %copy-done.3, f32[32,128]{1,0:T(8,128)} %broadcast_in_dim.12.before_ref, ...), custom_call_target="tpu_custom_call" | custom-call | flops 100663296000 | bytes 39321600 | tf_op jit(solution)/shard_map/phase_0/pallas_call | solution.py:258
  137.7 1.1 collective-permute-done.10.rest_3_
  138.8 1.2 slice.57
  140.0 2.3 slice.56
  142.4 1.6 slice_dynamic-update-slice_fusion.7
  144.1 1.9 collective-permute-start.15
  146.0 1.6 slice_dynamic-update-slice_fusion.6
  147.6 1.6 slice_dynamic-update-slice_fusion.5
  149.1 1.6 slice_dynamic-update-slice_fusion.4
  150.7 1.7 slice_dynamic-update-slice_fusion.3
  152.4 1.7 slice_dynamic-update-slice_fusion.2
  154.1 1.7 slice_dynamic-update-slice_fusion.1
  155.8 1.7 slice_dynamic-update-slice_fusion
  157.5 1.0 collective-permute-done.13.rest_6_
  158.5 1.6 collective-permute-start.17
  160.1 8.6 %collective-permute-done.12.rest_5_ = bf16[13,8,9600]{2,1,0:T(8,128)(2,1)} collective-permute-done((bf16[13,8,9600]{2,1,0:T(8,128)(2,1)}, bf16[13,8,9600]{2,1,0:T(8,128)(2,1)}, u32[]{:S(2)}, u32[]{:S(2)}) %collective-permute-start.12) | collective-permute-done | bytes 1996832 | tf_op jit(solution)/shard_map/ppermute | solution.py:466
  168.9 1.9 collective-permute-start.19
  170.7 8.2 %collective-permute-done.16.rest_1_ = bf16[6,8,9600]{2,1,0:T(8,128)(2,1)} collective-permute-done((bf16[6,8,9600]{2,1,0:T(8,128)(2,1)S(1)}, bf16[6,8,9600]{2,1,0:T(8,128)(2,1)}, u32[]{:S(2)}, u32[]{:S(2)}) %collective-permute-start.16) | collective-permute-done | bytes 921632 | tf_op jit(solution)/shard_map/ppermute | solution.py:466
  179.0 2.6 collective-permute-done.15.rest_0_
  181.6 1.5 collective-permute-start.20
  183.6 10.5 %phase_1.1.before_ref = f32[32,128]{1,0:T(8,128)} custom-call(s32[152]{0:T(256)} %get-tuple-element.67.list_ref, bf16[64,2048]{1,0:T(8,128)(2,1)} %copy-done.2, bf16[512,1024]{1,0:T(8,128)(2,1)} %copy-done.1, bf16[256,256]{1,0:T(8,128)(2,1)} %copy-done.3, f32[32,128]{1,0:T(8,128)} %phase_0.1.before_ref, ...), custom_call_target="tpu_custom_call" | custom-call | flops 100663296000 | bytes 39321600 | tf_op jit(solution)/shard_map/phase_1/pallas_call | solution.py:258
  194.1 7.3 %collective-permute-done.18.rest_3_ = bf16[6,8,9600]{2,1,0:T(8,128)(2,1)} collective-permute-done((bf16[6,8,9600]{2,1,0:T(8,128)(2,1)S(1)}, bf16[6,8,9600]{2,1,0:T(8,128)(2,1)}, u32[]{:S(2)}, u32[]{:S(2)}) %collective-permute-start.18) | collective-permute-done | bytes 921632 | tf_op jit(solution)/shard_map/ppermute | solution.py:466
  202.0 1.2 slice.67
  203.3 2.3 slice.66
  205.6 2.5 collective-permute-start.22
  208.1 1.5 collective-permute-start.24
  209.6 1.5 collective-permute-start.23
  211.1 9.9 %collective-permute-done.20.rest_5_ = bf16[6,8,9600]{2,1,0:T(8,128)(2,1)} collective-permute-done((bf16[6,8,9600]{2,1,0:T(8,128)(2,1)}, bf16[6,8,9600]{2,1,0:T(8,128)(2,1)}, u32[]{:S(2)}, u32[]{:S(2)}) %collective-permute-start.20) | collective-permute-done | bytes 921632 | tf_op jit(solution)/shard_map/ppermute | solution.py:466
  221.1 4.0 %collective-permute-done.21.rest_6_ = bf16[7,8,9600]{2,1,0:T(8,128)(2,1)} collective-permute-done((bf16[7,8,9600]{2,1,0:T(8,128)(2,1)}, bf16[7,8,9600]{2,1,0:T(8,128)(2,1)}, u32[]{:S(2)}, u32[]{:S(2)}) %collective-permute-start.21) | collective-permute-done | bytes 1075232 | tf_op jit(solution)/shard_map/ppermute | solution.py:466
  225.1 2.5 collective-permute-start.25
  227.6 1.5 collective-permute-start.26
  229.1 11.0 %phase_2.1.before_ref = f32[32,128]{1,0:T(8,128)} custom-call(s32[151]{0:T(256)} %get-tuple-element.66.list_ref, bf16[64,2048]{1,0:T(8,128)(2,1)} %copy-done.2, bf16[512,1024]{1,0:T(8,128)(2,1)} %copy-done.1, bf16[256,256]{1,0:T(8,128)(2,1)} %copy-done.3, f32[32,128]{1,0:T(8,128)} %phase_1.1.before_ref, ...), custom_call_target="tpu_custom_call" | custom-call | flops 100663296000 | bytes 39321600 | tf_op jit(solution)/shard_map/phase_2/pallas_call | solution.py:258
  240.0 6.7 %collective-permute-done.22.rest_0_ = bf16[12,8,9600]{2,1,0:T(8,128)(2,1)} collective-permute-done((bf16[12,8,9600]{2,1,0:T(8,128)(2,1)}, bf16[12,8,9600]{2,1,0:T(8,128)(2,1)}, u32[]{:S(2)}, u32[]{:S(2)}) %collective-permute-start.22) | collective-permute-done | bytes 1843232 | tf_op jit(solution)/shard_map/ppermute | solution.py:466
  246.7 1.6 collective-permute-start.27
  249.2 2.2 collective-permute-start.29
  251.4 12.5 %collective-permute-done.25.rest_3_ = bf16[6,8,9600]{2,1,0:T(8,128)(2,1)} collective-permute-done((bf16[6,8,9600]{2,1,0:T(8,128)(2,1)S(1)}, bf16[6,8,9600]{2,1,0:T(8,128)(2,1)}, u32[]{:S(2)}, u32[]{:S(2)}) %collective-permute-start.25) | collective-permute-done | bytes 921632 | tf_op jit(solution)/shard_map/ppermute | solution.py:466
  263.9 4.0 %collective-permute-done.26.rest_4_ = bf16[7,8,9600]{2,1,0:T(8,128)(2,1)} collective-permute-done((bf16[7,8,9600]{2,1,0:T(8,128)(2,1)}, bf16[7,8,9600]{2,1,0:T(8,128)(2,1)}, u32[]{:S(2)}, u32[]{:S(2)}) %collective-permute-start.26) | collective-permute-done | bytes 1075232 | tf_op jit(solution)/shard_map/ppermute | solution.py:466
  267.8 7.8 %phase_3.1.before_ref = f32[32,128]{1,0:T(8,128)} custom-call(s32[149]{0:T(256)} %get-tuple-element.65.list_ref, bf16[64,2048]{1,0:T(8,128)(2,1)} %copy-done.2, bf16[512,1024]{1,0:T(8,128)(2,1)} %copy-done.1, bf16[256,256]{1,0:T(8,128)(2,1)} %copy-done.3, f32[32,128]{1,0:T(8,128)} %phase_2.1.before_ref, ...), custom_call_target="tpu_custom_call" | custom-call | flops 100663296000 | bytes 39321600 | tf_op jit(solution)/shard_map/phase_3/pallas_call | solution.py:258
  275.6 8.0 %collective-permute-done.28.rest_1_ = bf16[6,8,9600]{2,1,0:T(8,128)(2,1)} collective-permute-done((bf16[6,8,9600]{2,1,0:T(8,128)(2,1)}, bf16[6,8,9600]{2,1,0:T(8,128)(2,1)}, u32[]{:S(2)}, u32[]{:S(2)}) %collective-permute-start.28) | collective-permute-done | bytes 921632 | tf_op jit(solution)/shard_map/ppermute | solution.py:466
  283.6 2.9 collective-permute-done.29.rest_2_
  286.5 7.8 %phase_4.1 = f32[32,128]{1,0:T(8,128)} custom-call(s32[83]{0:T(128)} %get-tuple-element.61.list_ref, bf16[64,2048]{1,0:T(8,128)(2,1)} %copy-done.2, bf16[512,1024]{1,0:T(8,128)(2,1)} %copy-done.1, bf16[256,256]{1,0:T(8,128)(2,1)} %copy-done.3, f32[32,128]{1,0:T(8,128)} %phase_3.1.before_ref, bf16[256,8,9600]{2,1,0:T(8,128)(2,1)} %all-gather.2.cloned.1.call-done.v_hbm, ...), custom_call_target="tpu_custom_call" | custom-call | flops 50331648000 | bytes 19660800 | tf_op jit(solution)/shard_map/phase_4/pallas_call | solution.py:258
  294.3 15.4 %all_to_all.17 = f32[32,1,128]{2,1,0:T(1,128)S(1)} all-to-all(f32[32,1,128]{2,1,0:T(1,128)} %bitcast.19), channel_id=1, replica_groups=mesh['shard'=32] {'shard'}, dimensions={0} | all-to-all | bytes 32768 | tf_op jit(solution)/shard_map/all_to_all | solution.py:481
  (58 shorter events, 10.5 us)
Async XLA Ops:
  6.5 1.7 copy-start.4
  6.5 116.1 %all-gather.2.cloned.1.call-start = ((), (), s32[]{:S(2)}) async-start(), calls=%async_computation.2 | async-start | bytes 58982400 | tf_op jit(solution)/shard_map/all_gather | solution.py:402
  9.8 35.3 %copy-start.9 = (bf16[32,1,3,3]{0,3,2,1:T(4,128)(2,1)S(1)}, bf16[32,1,3,3]{0,3,2,1:T(4,128)(2,1)}, u32[]{:S(2)}) copy-start(bf16[32,1,3,3]{0,3,2,1:T(4,128)(2,1)} %param.11) | copy-start | bytes 1732
  9.8 35.3 %copy-start.10 = (bf16[1,64,3,3]{1,3,2,0:T(4,128)(2,1)S(1)}, bf16[1,64,3,3]{1,3,2,0:T(4,128)(2,1)}, u32[]{:S(2)}) copy-start(bf16[1,64,3,3]{1,3,2,0:T(4,128)(2,1)} %param.13) | copy-start | bytes 3460
  9.8 36.7 %copy-start.8 = (s32[16,8]{0,1:T(8,128)S(1)}, s32[16,8]{0,1:T(8,128)}, u32[]{:S(2)}) copy-start(s32[16,8]{0,1:T(8,128)} %param.10) | copy-start | bytes 1540
  9.8 42.4 %copy-start = (bf16[64,32,3,3]{0,1,3,2:T(8,128)(2,1)S(1)}, bf16[64,32,3,3]{0,1,3,2:T(8,128)(2,1)}, u32[]{:S(2)}) copy-start(bf16[64,32,3,3]{0,1,3,2:T(8,128)(2,1)} %param.12) | copy-start | bytes 110596
  9.8 30.7 %collective-permute-start = (bf16[8,8,9600]{2,1,0:T(8,128)(2,1)}, bf16[8,8,9600]{2,1,0:T(8,128)(2,1)}, u32[]{:S(2)}, u32[]{:S(2)}) collective-permute-start(bf16[8,8,9600]{2,1,0:T(8,128)(2,1)} %get-tuple-element.87), channel_id=1, source_target_pairs={{0,4},{1,3},{2,6},{3,1},{4,0},{5,7},{6,2},{7,5},{8,12},{9,11},{10,... | collective-permute-start | bytes 3686408 | tf_op jit(solution)/shard_map/ppermute | solution.py:466
  12.9 30.3 %collective-permute-start.1 = (bf16[8,8,9600]{2,1,0:T(8,128)(2,1)}, bf16[8,8,9600]{2,1,0:T(8,128)(2,1)}, u32[]{:S(2)}, u32[]{:S(2)}) collective-permute-start(bf16[8,8,9600]{2,1,0:T(8,128)(2,1)} %get-tuple-element.83), channel_id=1, source_target_pairs={{0,2},{1,5},{2,0},{3,7},{4,6},{5,1},{6,4},{7,3},{8,10},{9,13},{10,... | collective-permute-start | bytes 3686408 | tf_op jit(solution)/shard_map/ppermute | solution.py:466
  15.8 53.7 %collective-permute-start.4 = (bf16[13,8,9600]{2,1,0:T(8,128)(2,1)}, bf16[13,8,9600]{2,1,0:T(8,128)(2,1)S(1)}, u32[]{:S(2)}, u32[]{:S(2)}) collective-permute-start(bf16[13,8,9600]{2,1,0:T(8,128)(2,1)} %slice.70), channel_id=1, source_target_pairs={{0,8},{1,9},{2,10},{3,11},{4,12},{5,13},{6,14},{7,15},{8,24},{9,25... | collective-permute-start | bytes 5990408 | tf_op jit(solution)/shard_map/ppermute | solution.py:466
  17.4 52.1 %collective-permute-start.5 = (bf16[8,8,9600]{2,1,0:T(8,128)(2,1)}, bf16[8,8,9600]{2,1,0:T(8,128)(2,1)S(1)}, u32[]{:S(2)}, u32[]{:S(2)}) collective-permute-start(bf16[8,8,9600]{2,1,0:T(8,128)(2,1)} %get-tuple-element.69), channel_id=1, source_target_pairs={{0,2},{1,5},{2,0},{3,7},{4,6},{5,1},{6,4},{7,3},{8,10},{9,13},{10,... | collective-permute-start | bytes 3686408 | tf_op jit(solution)/shard_map/ppermute | solution.py:466
  17.9 51.6 %collective-permute-start.6 = (bf16[8,8,9600]{2,1,0:T(8,128)(2,1)}, bf16[8,8,9600]{2,1,0:T(8,128)(2,1)}, u32[]{:S(2)}, u32[]{:S(2)}) collective-permute-start(bf16[8,8,9600]{2,1,0:T(8,128)(2,1)} %get-tuple-element.70), channel_id=1, source_target_pairs={{0,4},{1,3},{2,6},{3,1},{4,0},{5,7},{6,2},{7,5},{8,12},{9,11},{10,... | collective-permute-start | bytes 3686408 | tf_op jit(solution)/shard_map/ppermute | solution.py:466
  43.1 52.8 %collective-permute-start.2 = (bf16[8,8,9600]{2,1,0:T(8,128)(2,1)}, bf16[8,8,9600]{2,1,0:T(8,128)(2,1)}, u32[]{:S(2)}, u32[]{:S(2)}) collective-permute-start(bf16[8,8,9600]{2,1,0:T(8,128)(2,1)} %collective-permute-done.rest_2_), channel_id=1, source_target_pairs={{0,2},{1,5},{2,0},{3,7},{4,6},{5,1},{6,4},{7,3},{8,10},{9,13},{10,... | collective-permute-start | bytes 3686408 | tf_op jit(solution)/shard_map/ppermute | solution.py:466
  44.6 51.3 %collective-permute-start.3 = (bf16[8,8,9600]{2,1,0:T(8,128)(2,1)}, bf16[8,8,9600]{2,1,0:T(8,128)(2,1)}, u32[]{:S(2)}, u32[]{:S(2)}) collective-permute-start(bf16[8,8,9600]{2,1,0:T(8,128)(2,1)} %collective-permute-done.1.rest_1_), channel_id=1, source_target_pairs={{0,4},{1,3},{2,6},{3,1},{4,0},{5,7},{6,2},{7,5},{8,12},{9,11},{10,... | collective-permute-start | bytes 3686408 | tf_op jit(solution)/shard_map/ppermute | solution.py:466
  47.3 50.7 %all-to-all-start = ((s32[32,1,128]{2,1,0:T(1,128)}), s32[32,1,128]{2,1,0:T(1,128)S(1)}, u32[]{:S(2)}, u32[]{:S(2)}) async-start(s32[32,1,128]{2,1,0:T(1,128)} %broadcast_in_dim.11), calls=%async_computation | async-start | bytes 32768 | tf_op jit(solution)/shard_map/all_to_all | solution.py:470
  60.8 11.0 %copy-start.1 = (bf16[512,1024]{1,0:T(8,128)(2,1)}, bf16[512,1024]{1,0:T(8,128)(2,1)S(1)}, u32[]{:S(2)}) copy-start(bf16[512,1024]{1,0:T(8,128)(2,1)S(1)} %get-tuple-element.63.two_ref) | copy-start | bytes 3145732
  60.8 11.0 %copy-start.2 = (bf16[64,2048]{1,0:T(8,128)(2,1)}, bf16[64,2048]{1,0:T(8,128)(2,1)S(1)}, u32[]{:S(2)}) copy-start(bf16[64,2048]{1,0:T(8,128)(2,1)S(1)} %get-tuple-element.62.one_ref) | copy-start | bytes 786436
  60.8 11.0 %copy-start.3 = (bf16[256,256]{1,0:T(8,128)(2,1)}, bf16[256,256]{1,0:T(8,128)(2,1)S(1)}, u32[]{:S(2)}) copy-start(bf16[256,256]{1,0:T(8,128)(2,1)S(1)} %get-tuple-element.64.three_ref) | copy-start | bytes 393220
  69.5 43.1 %copy-start.6 = (bf16[8,8,9600]{2,1,0:T(8,128)(2,1)}, bf16[8,8,9600]{2,1,0:T(8,128)(2,1)S(1)}, u32[]{:S(2)}) copy-start(bf16[8,8,9600]{2,1,0:T(8,128)(2,1)S(1)} %collective-permute-done.5.rest_4_) | copy-start | bytes 3686404
  69.5 4.4 %copy-start.5 = (bf16[13,8,9600]{2,1,0:T(8,128)(2,1)}, bf16[13,8,9600]{2,1,0:T(8,128)(2,1)S(1)}, u32[]{:S(2)}) copy-start(bf16[13,8,9600]{2,1,0:T(8,128)(2,1)S(1)} %collective-permute-done.4.rest_3_) | copy-start | bytes 5990404
  71.8 41.3 %collective-permute-start.9 = (bf16[6,8,9600]{2,1,0:T(8,128)(2,1)}, bf16[6,8,9600]{2,1,0:T(8,128)(2,1)}, u32[]{:S(2)}, u32[]{:S(2)}) collective-permute-start(bf16[6,8,9600]{2,1,0:T(8,128)(2,1)} %slice.55), channel_id=1, source_target_pairs={{0,4},{1,3},{2,6},{3,1},{4,0},{5,7},{6,2},{7,5},{8,12},{9,11},{10,... | collective-permute-start | bytes 2764808 | tf_op jit(solution)/shard_map/ppermute | solution.py:466
  71.9 47.1 %collective-permute-start.8 = (bf16[7,8,9600]{2,1,0:T(8,128)(2,1)}, bf16[7,8,9600]{2,1,0:T(8,128)(2,1)}, u32[]{:S(2)}, u32[]{:S(2)}) collective-permute-start(bf16[7,8,9600]{2,1,0:T(8,128)(2,1)} %slice.54), channel_id=1, source_target_pairs={{0,2},{1,5},{2,0},{3,7},{4,6},{5,1},{6,4},{7,3},{8,10},{9,13},{10,... | collective-permute-start | bytes 3225608 | tf_op jit(solution)/shard_map/ppermute | solution.py:466
  73.9 45.2 %collective-permute-start.7 = (bf16[13,8,9600]{2,1,0:T(8,128)(2,1)S(1)}, bf16[13,8,9600]{2,1,0:T(8,128)(2,1)}, u32[]{:S(2)}, u32[]{:S(2)}) collective-permute-start(bf16[13,8,9600]{2,1,0:T(8,128)(2,1)S(1)} %collective-permute-done.4.rest_3_), channel_id=1, source_target_pairs={{0,8},{1,9},{2,10},{3,11},{4,12},{5,13},{6,14},{7,15},{8,24},{9,25... | collective-permute-start | bytes 5990408 | tf_op jit(solution)/shard_map/ppermute | solution.py:466
  96.0 42.8 %collective-permute-start.10 = (bf16[6,8,9600]{2,1,0:T(8,128)(2,1)}, bf16[6,8,9600]{2,1,0:T(8,128)(2,1)}, u32[]{:S(2)}, u32[]{:S(2)}) collective-permute-start(bf16[6,8,9600]{2,1,0:T(8,128)(2,1)} %slice.55), channel_id=1, source_target_pairs={{0,2},{1,5},{2,0},{3,7},{4,6},{5,1},{6,4},{7,3},{8,10},{9,13},{10,... | collective-permute-start | bytes 2764808 | tf_op jit(solution)/shard_map/ppermute | solution.py:466
  97.4 41.3 %collective-permute-start.11 = (bf16[7,8,9600]{2,1,0:T(8,128)(2,1)}, bf16[7,8,9600]{2,1,0:T(8,128)(2,1)}, u32[]{:S(2)}, u32[]{:S(2)}) collective-permute-start(bf16[7,8,9600]{2,1,0:T(8,128)(2,1)} %slice.54), channel_id=1, source_target_pairs={{0,4},{1,3},{2,6},{3,1},{4,0},{5,7},{6,2},{7,5},{8,12},{9,11},{10,... | collective-permute-start | bytes 3225608 | tf_op jit(solution)/shard_map/ppermute | solution.py:466
  98.0 0.6 copy-start.7
  119.0 39.5 %collective-permute-start.13 = (bf16[6,8,9600]{2,1,0:T(8,128)(2,1)}, bf16[6,8,9600]{2,1,0:T(8,128)(2,1)}, u32[]{:S(2)}, u32[]{:S(2)}) collective-permute-start(bf16[6,8,9600]{2,1,0:T(8,128)(2,1)} %collective-permute-done.9.rest_2_), channel_id=1, source_target_pairs={{0,2},{1,5},{2,0},{3,7},{4,6},{5,1},{6,4},{7,3},{8,10},{9,13},{10,... | collective-permute-start | bytes 2764808 | tf_op jit(solution)/shard_map/ppermute | solution.py:466
  120.5 39.6 %collective-permute-start.14 = (bf16[7,8,9600]{2,1,0:T(8,128)(2,1)}, bf16[7,8,9600]{2,1,0:T(8,128)(2,1)}, u32[]{:S(2)}, u32[]{:S(2)}) collective-permute-start(bf16[7,8,9600]{2,1,0:T(8,128)(2,1)} %collective-permute-done.8.rest_1_), channel_id=1, source_target_pairs={{0,4},{1,3},{2,6},{3,1},{4,0},{5,7},{6,2},{7,5},{8,12},{9,11},{10,... | collective-permute-start | bytes 3225608 | tf_op jit(solution)/shard_map/ppermute | solution.py:466
  121.0 47.6 %collective-permute-start.12 = (bf16[13,8,9600]{2,1,0:T(8,128)(2,1)}, bf16[13,8,9600]{2,1,0:T(8,128)(2,1)}, u32[]{:S(2)}, u32[]{:S(2)}) collective-permute-start(bf16[13,8,9600]{2,1,0:T(8,128)(2,1)} %collective-permute-done.7.rest_0_), channel_id=1, source_target_pairs={{0,8},{1,9},{2,10},{3,11},{4,12},{5,13},{6,14},{7,15},{8,24},{9,25... | collective-permute-start | bytes 5990408 | tf_op jit(solution)/shard_map/ppermute | solution.py:466
  143.9 35.0 %collective-permute-start.16 = (bf16[6,8,9600]{2,1,0:T(8,128)(2,1)S(1)}, bf16[6,8,9600]{2,1,0:T(8,128)(2,1)}, u32[]{:S(2)}, u32[]{:S(2)}) collective-permute-start(bf16[6,8,9600]{2,1,0:T(8,128)(2,1)S(1)} %slice.57), channel_id=1, source_target_pairs={{0,4},{1,3},{2,6},{3,1},{4,0},{5,7},{6,2},{7,5},{8,12},{9,11},{10,... | collective-permute-start | bytes 2764808 | tf_op jit(solution)/shard_map/ppermute | solution.py:466
  144.1 37.5 %collective-permute-start.15 = (bf16[7,8,9600]{2,1,0:T(8,128)(2,1)}, bf16[7,8,9600]{2,1,0:T(8,128)(2,1)}, u32[]{:S(2)}, u32[]{:S(2)}) collective-permute-start(bf16[7,8,9600]{2,1,0:T(8,128)(2,1)} %slice.56), channel_id=1, source_target_pairs={{0,2},{1,5},{2,0},{3,7},{4,6},{5,1},{6,4},{7,3},{8,10},{9,13},{10,... | collective-permute-start | bytes 3225608 | tf_op jit(solution)/shard_map/ppermute | solution.py:466
  158.5 47.0 %collective-permute-start.17 = (bf16[12,8,9600]{2,1,0:T(8,128)(2,1)}, bf16[12,8,9600]{2,1,0:T(8,128)(2,1)}, u32[]{:S(2)}, u32[]{:S(2)}) collective-permute-start(bf16[12,8,9600]{2,1,0:T(8,128)(2,1)} %slice_dynamic-update-slice_fusion), channel_id=1, source_target_pairs={{0,8},{1,9},{2,10},{3,11},{4,12},{5,13},{6,14},{7,15},{8,24},{9,25... | collective-permute-start | bytes 5529608 | tf_op jit(solution)/shard_map/ppermute | solution.py:466
  168.7 32.7 %collective-permute-start.18 = (bf16[6,8,9600]{2,1,0:T(8,128)(2,1)S(1)}, bf16[6,8,9600]{2,1,0:T(8,128)(2,1)}, u32[]{:S(2)}, u32[]{:S(2)}) collective-permute-start(bf16[6,8,9600]{2,1,0:T(8,128)(2,1)S(1)} %slice.57), channel_id=1, source_target_pairs={{0,2},{1,5},{2,0},{3,7},{4,6},{5,1},{6,4},{7,3},{8,10},{9,13},{10,... | collective-permute-start | bytes 2764808 | tf_op jit(solution)/shard_map/ppermute | solution.py:466
  168.9 33.1 %collective-permute-start.19 = (bf16[7,8,9600]{2,1,0:T(8,128)(2,1)}, bf16[7,8,9600]{2,1,0:T(8,128)(2,1)}, u32[]{:S(2)}, u32[]{:S(2)}) collective-permute-start(bf16[7,8,9600]{2,1,0:T(8,128)(2,1)} %slice.56), channel_id=1, source_target_pairs={{0,4},{1,3},{2,6},{3,1},{4,0},{5,7},{6,2},{7,5},{8,12},{9,11},{10,... | collective-permute-start | bytes 3225608 | tf_op jit(solution)/shard_map/ppermute | solution.py:466
  181.6 39.5 %collective-permute-start.20 = (bf16[6,8,9600]{2,1,0:T(8,128)(2,1)}, bf16[6,8,9600]{2,1,0:T(8,128)(2,1)}, u32[]{:S(2)}, u32[]{:S(2)}) collective-permute-start(bf16[6,8,9600]{2,1,0:T(8,128)(2,1)} %collective-permute-done.16.rest_1_), channel_id=1, source_target_pairs={{0,2},{1,5},{2,0},{3,7},{4,6},{5,1},{6,4},{7,3},{8,10},{9,13},{10,... | collective-permute-start | bytes 2764808 | tf_op jit(solution)/shard_map/ppermute | solution.py:466
  183.1 42.0 %collective-permute-start.21 = (bf16[7,8,9600]{2,1,0:T(8,128)(2,1)}, bf16[7,8,9600]{2,1,0:T(8,128)(2,1)}, u32[]{:S(2)}, u32[]{:S(2)}) collective-permute-start(bf16[7,8,9600]{2,1,0:T(8,128)(2,1)} %collective-permute-done.15.rest_0_), channel_id=1, source_target_pairs={{0,4},{1,3},{2,6},{3,1},{4,0},{5,7},{6,2},{7,5},{8,12},{9,11},{10,... | collective-permute-start | bytes 3225608 | tf_op jit(solution)/shard_map/ppermute | solution.py:466
  205.6 41.2 %collective-permute-start.22 = (bf16[12,8,9600]{2,1,0:T(8,128)(2,1)}, bf16[12,8,9600]{2,1,0:T(8,128)(2,1)}, u32[]{:S(2)}, u32[]{:S(2)}) collective-permute-start(bf16[12,8,9600]{2,1,0:T(8,128)(2,1)} %collective-permute-done.17.rest_2_), channel_id=1, source_target_pairs={{0,8},{1,9},{2,10},{3,11},{4,12},{5,13},{6,14},{7,15},{8,24},{9,25... | collective-permute-start | bytes 5529608 | tf_op jit(solution)/shard_map/ppermute | solution.py:466
  208.1 40.2 %collective-permute-start.24 = (bf16[6,8,9600]{2,1,0:T(8,128)(2,1)S(1)}, bf16[6,8,9600]{2,1,0:T(8,128)(2,1)}, u32[]{:S(2)}, u32[]{:S(2)}) collective-permute-start(bf16[6,8,9600]{2,1,0:T(8,128)(2,1)S(1)} %slice.67), channel_id=1, source_target_pairs={{0,4},{1,3},{2,6},{3,1},{4,0},{5,7},{6,2},{7,5},{8,12},{9,11},{10,... | collective-permute-start | bytes 2764808 | tf_op jit(solution)/shard_map/ppermute | solution.py:466
  209.6 38.7 %collective-permute-start.23 = (bf16[7,8,9600]{2,1,0:T(8,128)(2,1)}, bf16[7,8,9600]{2,1,0:T(8,128)(2,1)}, u32[]{:S(2)}, u32[]{:S(2)}) collective-permute-start(bf16[7,8,9600]{2,1,0:T(8,128)(2,1)} %slice.66), channel_id=1, source_target_pairs={{0,2},{1,5},{2,0},{3,7},{4,6},{5,1},{6,4},{7,3},{8,10},{9,13},{10,... | collective-permute-start | bytes 3225608 | tf_op jit(solution)/shard_map/ppermute | solution.py:466
  225.1 38.8 %collective-permute-start.25 = (bf16[6,8,9600]{2,1,0:T(8,128)(2,1)S(1)}, bf16[6,8,9600]{2,1,0:T(8,128)(2,1)}, u32[]{:S(2)}, u32[]{:S(2)}) collective-permute-start(bf16[6,8,9600]{2,1,0:T(8,128)(2,1)S(1)} %slice.67), channel_id=1, source_target_pairs={{0,2},{1,5},{2,0},{3,7},{4,6},{5,1},{6,4},{7,3},{8,10},{9,13},{10,... | collective-permute-start | bytes 2764808 | tf_op jit(solution)/shard_map/ppermute | solution.py:466
  227.6 40.3 %collective-permute-start.26 = (bf16[7,8,9600]{2,1,0:T(8,128)(2,1)}, bf16[7,8,9600]{2,1,0:T(8,128)(2,1)}, u32[]{:S(2)}, u32[]{:S(2)}) collective-permute-start(bf16[7,8,9600]{2,1,0:T(8,128)(2,1)} %slice.66), channel_id=1, source_target_pairs={{0,4},{1,3},{2,6},{3,1},{4,0},{5,7},{6,2},{7,5},{8,12},{9,11},{10,... | collective-permute-start | bytes 3225608 | tf_op jit(solution)/shard_map/ppermute | solution.py:466
  246.7 39.7 %collective-permute-start.27 = (bf16[12,8,9600]{2,1,0:T(8,128)(2,1)}, bf16[12,8,9600]{2,1,0:T(8,128)(2,1)}, u32[]{:S(2)}, u32[]{:S(2)}) collective-permute-start(bf16[12,8,9600]{2,1,0:T(8,128)(2,1)} %collective-permute-done.22.rest_0_), channel_id=1, source_target_pairs={{0,8},{1,9},{2,10},{3,11},{4,12},{5,13},{6,14},{7,15},{8,24},{9,25... | collective-permute-start | bytes 5529608 | tf_op jit(solution)/shard_map/ppermute | solution.py:466
  248.3 35.3 %collective-permute-start.28 = (bf16[6,8,9600]{2,1,0:T(8,128)(2,1)}, bf16[6,8,9600]{2,1,0:T(8,128)(2,1)}, u32[]{:S(2)}, u32[]{:S(2)}) collective-permute-start(bf16[6,8,9600]{2,1,0:T(8,128)(2,1)} %collective-permute-done.24.rest_2_), channel_id=1, source_target_pairs={{0,2},{1,5},{2,0},{3,7},{4,6},{5,1},{6,4},{7,3},{8,10},{9,13},{10,... | collective-permute-start | bytes 2764808 | tf_op jit(solution)/shard_map/ppermute | solution.py:466
  249.2 37.3 %collective-permute-start.29 = (bf16[7,8,9600]{2,1,0:T(8,128)(2,1)}, bf16[7,8,9600]{2,1,0:T(8,128)(2,1)}, u32[]{:S(2)}, u32[]{:S(2)}) collective-permute-start(bf16[7,8,9600]{2,1,0:T(8,128)(2,1)} %collective-permute-done.23.rest_1_), channel_id=1, source_target_pairs={{0,4},{1,3},{2,6},{3,1},{4,0},{5,7},{6,2},{7,5},{8,12},{9,11},{10,... | collective-permute-start | bytes 3225608 | tf_op jit(solution)/shard_map/ppermute | solution.py:466
Sparse Core Ops, SparseCore 0:
  8.9 62.0 all-gather.1

commit v16 on v15

--- a/solution.py
+++ b/solution.py
@@ -157,9 +157,10 @@
 
     def fetch(step, slot):
         first = step * GROUP
+        here = jnp.minimum(count - first, GROUP)
         for b in range(buffers):
             low = 0 if b == 0 else jnp.clip(list_ref[b - 1] - first, 0, GROUP)
-            high = GROUP if b == buffers - 1 else jnp.clip(list_ref[b] - first, 0, GROUP)
+            high = here if b == buffers - 1 else jnp.clip(list_ref[b] - first, 0, GROUP)
 
             def one_query(p, _):
                 pltpu.make_async_copy(
@@ -173,7 +174,7 @@
             vid = list_ref[buffers + first + p] & ((1 << bits) - 1)
             pltpu.make_async_copy(v_hbm.at[vid], v_in.at[slot, p], v_sem.at[slot]).start()
             return 0
-        lax.fori_loop(0, GROUP, one_video, 0)
+        lax.fori_loop(0, here, one_video, 0)
 
     maps[...] = jnp.zeros_like(maps)
 
@@ -188,8 +189,13 @@
         def _():
             fetch(g + 1, 1 - slot)
 
-        pltpu.make_async_copy(q_in.at[slot], q_in.at[slot], q_sem.at[slot]).wait()
-        pltpu.make_async_copy(v_in.at[slot], v_in.at[slot], v_sem.at[slot]).wait()
+        here = jnp.minimum(count - g * GROUP, GROUP)
+
+        def arrived(p, _):
+            pltpu.make_async_copy(v_hbm.at[0], q_in.at[slot, p], q_sem.at[slot]).wait()
+            pltpu.make_async_copy(v_hbm.at[0], v_in.at[slot, p], v_sem.at[slot]).wait()
+            return 0
+        lax.fori_loop(0, here, arrived, 0)
         for r in range(R):
             cols = pl.ds(r * width, width)
             q_rows[pl.ds(r * side, side), :] = q_in[slot, :, :, cols].reshape(side, width)
@@ -205,7 +211,8 @@
         for r in range(1, R):
             total = total + best[r * side:(r + 1) * side]
         cells = frames * frames
-        same_pair = iota((side, side), 0) // frames == iota((side, side), 1) // frames
+        row = iota((side, side), 0) // frames
+        same_pair = (row == iota((side, side), 1) // frames) & (row < here)
         lane, sub = iota((side, cells), 1), iota((side, cells), 0)
         spread = (lane % frames == sub % frames).astype(jnp.bfloat16)
         own_frame = lane // frames == sub % frames

time: 317 us -> 317 us (level)
  no operation moved by 1% of the time
where the time goes in v16:
time: 317 us; the launch traced here: 315 us
  waiting for transfers between devices  140 us (44%)
  Pallas kernels  72.4 us (23%)
  starting transfers between devices  45.1 us (14%)
  local copies, waits for them, and re-layouts  30 us (9%)
  between operations  13.6 us (4%)
  blocking collectives  13.1 us (4%)
    ppermute x30, waiting for transfers between devices, body(): gather.blocks[target] = lax.ppermute(block, 'shard', gather.steps[axis])  139 us
    pallas_call x5, Pallas kernels, pair_scores(): pl.pallas_call(functools.partial(pair_kernel, frames, idx_dev, len(blocks...  49.8 us
    ppermute x30, starting transfers between devices, body(): gather.blocks[target] = lax.ppermute(block, 'shard', gather.steps[axis])  40.2 us
    pallas_call x1, Pallas kernels, pair_lists(): pl.pallas_call(functools.partial(list_kernel, idx_dev, k_count, ids.shape...  14 us
    all_to_all x1, blocking collectives, body(): lax.all_to_all(tables[-1], 'shard', split_axis=0, concat_axis=0, tiled=True)  13.1 us
    unnamed x29, local copies, waits for them, and re-layouts  13 us
    slice x8, local copies, waits for them, and re-layouts, block(): parts = [b[at:at + n] for b, (_, at, n) in zip(whole, self.pieces[key])]  12.4 us
    pallas_call x1, Pallas kernels, head_matrices(): pl.pallas_call(head_kernel, out_shape=[jax.ShapeDtypeStruct(s, jnp.bfloat...  8.54 us
  transfers between devices with their start and end apart: 32, of which 20 were waited for; matrix products, arithmetic and copies ran while one was open for 9% of the time, Pallas kernels for 21%

profile of v16, /device:TPU:0, one launch (start us, length us, event | category | flops | bytes accessed | tf_op | source)
XLA Modules:
  0.0 314.9 jit_solution(899465027795177769)
XLA Ops:
  7.3 1.0 copy-done.4
  8.2 1.6 fusion
  9.8 3.0 collective-permute-start
  12.9 1.5 collective-permute-start.1
  14.4 1.5 slice.70
  15.8 1.6 collective-permute-start.4
  18.4 22.1 %collective-permute-done.rest_2_ = bf16[8,8,9600]{2,1,0:T(8,128)(2,1)} collective-permute-done((bf16[8,8,9600]{2,1,0:T(8,128)(2,1)}, bf16[8,8,9600]{2,1,0:T(8,128)(2,1)}, u32[]{:S(2)}, u32[]{:S(2)}) %collective-permute-start) | collective-permute-done | bytes 1228832 | tf_op jit(solution)/shard_map/ppermute | solution.py:473
  40.5 2.6 collective-permute-done.1.rest_1_
  43.1 1.5 collective-permute-start.2
  47.3 4.9 %all-to-all-start = ((s32[32,1,128]{2,1,0:T(1,128)}), s32[32,1,128]{2,1,0:T(1,128)S(1)}, u32[]{:S(2)}, u32[]{:S(2)}) async-start(s32[32,1,128]{2,1,0:T(1,128)} %broadcast_in_dim.11), calls=%async_computation | async-start | bytes 32768 | tf_op jit(solution)/shard_map/all_to_all | solution.py:477
  52.2 8.5 %head_matrices.1 = (bf16[64,2048]{1,0:T(8,128)(2,1)S(1)}, bf16[512,1024]{1,0:T(8,128)(2,1)S(1)}, bf16[256,256]{1,0:T(8,128)(2,1)S(1)}) custom-call(bf16[9,1,32]{2,1,0:T(2,128)(2,1)S(1)} %reshape.27.one_w, bf16[9,32,64]{2,1,0:T(8,128)(2,1)S(1)} %bitcast.17, bf16[9,1,64]{2,1,0:T(2,128)(2,1)S(1)} %reshape.28.three_w), custom_call_target="tpu_custom_call" | custom-call | flops 1000000000 | bytes 3000000 | tf_op jit(solution)/shard_map/head_matrices/pallas_call | solution.py:90
  60.8 8.7 %collective-permute-done.5.rest_4_ = bf16[8,8,9600]{2,1,0:T(8,128)(2,1)S(1)} collective-permute-done((bf16[8,8,9600]{2,1,0:T(8,128)(2,1)}, bf16[8,8,9600]{2,1,0:T(8,128)(2,1)S(1)}, u32[]{:S(2)}, u32[]{:S(2)}) %collective-permute-start.5) | collective-permute-done | bytes 1228832 | tf_op jit(solution)/shard_map/ppermute | solution.py:473
  69.5 1.1 slice.55
  70.7 1.1 slice.54
  71.9 2.0 collective-permute-start.8
  73.9 1.6 collective-permute-start.7
  75.5 20.5 %collective-permute-done.2.rest_6_ = bf16[8,8,9600]{2,1,0:T(8,128)(2,1)} collective-permute-done((bf16[8,8,9600]{2,1,0:T(8,128)(2,1)}, bf16[8,8,9600]{2,1,0:T(8,128)(2,1)}, u32[]{:S(2)}, u32[]{:S(2)}) %collective-permute-start.2) | collective-permute-done | bytes 1228832 | tf_op jit(solution)/shard_map/ppermute | solution.py:473
  96.0 1.5 collective-permute-start.10
  98.6 14.0 %pair_lists.1 = (s32[152]{0:T(256)}, s32[152]{0:T(256)}, s32[151]{0:T(256)}, s32[149]{0:T(256)}, s32[83]{0:T(128)}) custom-call(s32[18]{0:T(128)} %pad_add_fusion.who_ref, s32[32,128]{1,0:T(8,128)} %bitcast.18, s32[256]{0:T(256)} %constant.41.clone.queries_ref), custom_call_target="tpu_custom_call" | custom-call | flops 99999997952 | bytes 1000000 | tf_op jit(solution)/shard_map/pair_lists/pallas_call | solution.py:136
  113.1 5.9 %collective-permute-done.8.rest_1_ = bf16[7,8,9600]{2,1,0:T(8,128)(2,1)} collective-permute-done((bf16[7,8,9600]{2,1,0:T(8,128)(2,1)}, bf16[7,8,9600]{2,1,0:T(8,128)(2,1)}, u32[]{:S(2)}, u32[]{:S(2)}) %collective-permute-start.8) | collective-permute-done | bytes 1075232 | tf_op jit(solution)/shard_map/ppermute | solution.py:473
  119.0 1.5 collective-permute-start.13
  121.0 1.6 collective-permute-start.12
  123.2 13.4 %phase_0.1.before_ref = f32[32,128]{1,0:T(8,128)} custom-call(s32[152]{0:T(256)} %get-tuple-element.68.list_ref, bf16[64,2048]{1,0:T(8,128)(2,1)} %copy-done.2, bf16[512,1024]{1,0:T(8,128)(2,1)} %copy-done.1, bf16[256,256]{1,0:T(8,128)(2,1)} %copy-done.3, f32[32,128]{1,0:T(8,128)} %broadcast_in_dim.12.before_ref, ...), custom_call_target="tpu_custom_call" | custom-call | flops 100663296000 | bytes 39321600 | tf_op jit(solution)/shard_map/phase_0/pallas_call | solution.py:265
  136.6 2.2 collective-permute-done.10.rest_3_
  138.8 1.2 slice.57
  140.0 2.3 slice.56
  142.4 1.6 slice_dynamic-update-slice_fusion.7
  144.0 2.0 collective-permute-start.15
  145.9 1.6 slice_dynamic-update-slice_fusion.6
  147.5 1.6 slice_dynamic-update-slice_fusion.5
  149.1 1.6 slice_dynamic-update-slice_fusion.4
  150.7 1.7 slice_dynamic-update-slice_fusion.3
  152.4 1.7 slice_dynamic-update-slice_fusion.2
  154.1 1.7 slice_dynamic-update-slice_fusion.1
  155.8 1.7 slice_dynamic-update-slice_fusion
  157.5 1.1 collective-permute-done.13.rest_6_
  158.5 1.6 collective-permute-start.17
  160.1 8.6 %collective-permute-done.12.rest_5_ = bf16[13,8,9600]{2,1,0:T(8,128)(2,1)} collective-permute-done((bf16[13,8,9600]{2,1,0:T(8,128)(2,1)}, bf16[13,8,9600]{2,1,0:T(8,128)(2,1)}, u32[]{:S(2)}, u32[]{:S(2)}) %collective-permute-start.12) | collective-permute-done | bytes 1996832 | tf_op jit(solution)/shard_map/ppermute | solution.py:473
  168.9 1.9 collective-permute-start.19
  170.7 8.2 %collective-permute-done.16.rest_1_ = bf16[6,8,9600]{2,1,0:T(8,128)(2,1)} collective-permute-done((bf16[6,8,9600]{2,1,0:T(8,128)(2,1)S(1)}, bf16[6,8,9600]{2,1,0:T(8,128)(2,1)}, u32[]{:S(2)}, u32[]{:S(2)}) %collective-permute-start.16) | collective-permute-done | bytes 921632 | tf_op jit(solution)/shard_map/ppermute | solution.py:473
  179.0 2.6 collective-permute-done.15.rest_0_
  181.6 1.5 collective-permute-start.20
  183.6 10.6 %phase_1.1.before_ref = f32[32,128]{1,0:T(8,128)} custom-call(s32[152]{0:T(256)} %get-tuple-element.67.list_ref, bf16[64,2048]{1,0:T(8,128)(2,1)} %copy-done.2, bf16[512,1024]{1,0:T(8,128)(2,1)} %copy-done.1, bf16[256,256]{1,0:T(8,128)(2,1)} %copy-done.3, f32[32,128]{1,0:T(8,128)} %phase_0.1.before_ref, ...), custom_call_target="tpu_custom_call" | custom-call | flops 100663296000 | bytes 39321600 | tf_op jit(solution)/shard_map/phase_1/pallas_call | solution.py:265
  194.1 7.2 %collective-permute-done.18.rest_3_ = bf16[6,8,9600]{2,1,0:T(8,128)(2,1)} collective-permute-done((bf16[6,8,9600]{2,1,0:T(8,128)(2,1)S(1)}, bf16[6,8,9600]{2,1,0:T(8,128)(2,1)}, u32[]{:S(2)}, u32[]{:S(2)}) %collective-permute-start.18) | collective-permute-done | bytes 921632 | tf_op jit(solution)/shard_map/ppermute | solution.py:473
  202.0 1.2 slice.67
  203.3 2.3 slice.66
  205.6 2.5 collective-permute-start.22
  208.1 1.5 collective-permute-start.24
  209.6 1.5 collective-permute-start.23
  211.1 9.9 %collective-permute-done.20.rest_5_ = bf16[6,8,9600]{2,1,0:T(8,128)(2,1)} collective-permute-done((bf16[6,8,9600]{2,1,0:T(8,128)(2,1)}, bf16[6,8,9600]{2,1,0:T(8,128)(2,1)}, u32[]{:S(2)}, u32[]{:S(2)}) %collective-permute-start.20) | collective-permute-done | bytes 921632 | tf_op jit(solution)/shard_map/ppermute | solution.py:473
  221.1 4.0 %collective-permute-done.21.rest_6_ = bf16[7,8,9600]{2,1,0:T(8,128)(2,1)} collective-permute-done((bf16[7,8,9600]{2,1,0:T(8,128)(2,1)}, bf16[7,8,9600]{2,1,0:T(8,128)(2,1)}, u32[]{:S(2)}, u32[]{:S(2)}) %collective-permute-start.21) | collective-permute-done | bytes 1075232 | tf_op jit(solution)/shard_map/ppermute | solution.py:473
  225.1 2.5 collective-permute-start.25
  227.6 1.5 collective-permute-start.26
  229.1 10.4 %phase_2.1.before_ref = f32[32,128]{1,0:T(8,128)} custom-call(s32[151]{0:T(256)} %get-tuple-element.66.list_ref, bf16[64,2048]{1,0:T(8,128)(2,1)} %copy-done.2, bf16[512,1024]{1,0:T(8,128)(2,1)} %copy-done.1, bf16[256,256]{1,0:T(8,128)(2,1)} %copy-done.3, f32[32,128]{1,0:T(8,128)} %phase_1.1.before_ref, ...), custom_call_target="tpu_custom_call" | custom-call | flops 100663296000 | bytes 39321600 | tf_op jit(solution)/shard_map/phase_2/pallas_call | solution.py:265
  239.5 7.2 %collective-permute-done.22.rest_0_ = bf16[12,8,9600]{2,1,0:T(8,128)(2,1)} collective-permute-done((bf16[12,8,9600]{2,1,0:T(8,128)(2,1)}, bf16[12,8,9600]{2,1,0:T(8,128)(2,1)}, u32[]{:S(2)}, u32[]{:S(2)}) %collective-permute-start.22) | collective-permute-done | bytes 1843232 | tf_op jit(solution)/shard_map/ppermute | solution.py:473
  246.7 1.6 collective-permute-start.27
  249.2 2.2 collective-permute-start.29
  251.4 12.5 %collective-permute-done.25.rest_3_ = bf16[6,8,9600]{2,1,0:T(8,128)(2,1)} collective-permute-done((bf16[6,8,9600]{2,1,0:T(8,128)(2,1)S(1)}, bf16[6,8,9600]{2,1,0:T(8,128)(2,1)}, u32[]{:S(2)}, u32[]{:S(2)}) %collective-permute-start.25) | collective-permute-done | bytes 921632 | tf_op jit(solution)/shard_map/ppermute | solution.py:473
  263.9 4.0 %collective-permute-done.26.rest_4_ = bf16[7,8,9600]{2,1,0:T(8,128)(2,1)} collective-permute-done((bf16[7,8,9600]{2,1,0:T(8,128)(2,1)}, bf16[7,8,9600]{2,1,0:T(8,128)(2,1)}, u32[]{:S(2)}, u32[]{:S(2)}) %collective-permute-start.26) | collective-permute-done | bytes 1075232 | tf_op jit(solution)/shard_map/ppermute | solution.py:473
  267.8 7.8 %phase_3.1.before_ref = f32[32,128]{1,0:T(8,128)} custom-call(s32[149]{0:T(256)} %get-tuple-element.65.list_ref, bf16[64,2048]{1,0:T(8,128)(2,1)} %copy-done.2, bf16[512,1024]{1,0:T(8,128)(2,1)} %copy-done.1, bf16[256,256]{1,0:T(8,128)(2,1)} %copy-done.3, f32[32,128]{1,0:T(8,128)} %phase_2.1.before_ref, ...), custom_call_target="tpu_custom_call" | custom-call | flops 100663296000 | bytes 39321600 | tf_op jit(solution)/shard_map/phase_3/pallas_call | solution.py:265
  275.7 7.9 %collective-permute-done.28.rest_1_ = bf16[6,8,9600]{2,1,0:T(8,128)(2,1)} collective-permute-done((bf16[6,8,9600]{2,1,0:T(8,128)(2,1)}, bf16[6,8,9600]{2,1,0:T(8,128)(2,1)}, u32[]{:S(2)}, u32[]{:S(2)}) %collective-permute-start.28) | collective-permute-done | bytes 921632 | tf_op jit(solution)/shard_map/ppermute | solution.py:473
  283.6 2.9 collective-permute-done.29.rest_2_
  286.5 7.6 %phase_4.1 = f32[32,128]{1,0:T(8,128)} custom-call(s32[83]{0:T(128)} %get-tuple-element.61.list_ref, bf16[64,2048]{1,0:T(8,128)(2,1)} %copy-done.2, bf16[512,1024]{1,0:T(8,128)(2,1)} %copy-done.1, bf16[256,256]{1,0:T(8,128)(2,1)} %copy-done.3, f32[32,128]{1,0:T(8,128)} %phase_3.1.before_ref, bf16[256,8,9600]{2,1,0:T(8,128)(2,1)} %all-gather.2.cloned.1.call-done.v_hbm, ...), custom_call_target="tpu_custom_call" | custom-call | flops 50331648000 | bytes 19660800 | tf_op jit(solution)/shard_map/phase_4/pallas_call | solution.py:265
  294.1 13.1 %all_to_all.17 = f32[32,1,128]{2,1,0:T(1,128)S(1)} all-to-all(f32[32,1,128]{2,1,0:T(1,128)} %bitcast.19), channel_id=1, replica_groups=mesh['shard'=32] {'shard'}, dimensions={0} | all-to-all | bytes 32768 | tf_op jit(solution)/shard_map/all_to_all | solution.py:488
  (58 shorter events, 10.4 us)
Async XLA Ops:
  6.5 1.7 copy-start.4
  6.5 116.1 %all-gather.2.cloned.1.call-start = ((), (), s32[]{:S(2)}) async-start(), calls=%async_computation.2 | async-start | bytes 58982400 | tf_op jit(solution)/shard_map/all_gather | solution.py:409
  9.8 35.3 %copy-start.9 = (bf16[32,1,3,3]{0,3,2,1:T(4,128)(2,1)S(1)}, bf16[32,1,3,3]{0,3,2,1:T(4,128)(2,1)}, u32[]{:S(2)}) copy-start(bf16[32,1,3,3]{0,3,2,1:T(4,128)(2,1)} %param.11) | copy-start | bytes 1732
  9.8 35.3 %copy-start.10 = (bf16[1,64,3,3]{1,3,2,0:T(4,128)(2,1)S(1)}, bf16[1,64,3,3]{1,3,2,0:T(4,128)(2,1)}, u32[]{:S(2)}) copy-start(bf16[1,64,3,3]{1,3,2,0:T(4,128)(2,1)} %param.13) | copy-start | bytes 3460
  9.8 36.7 %copy-start.8 = (s32[16,8]{0,1:T(8,128)S(1)}, s32[16,8]{0,1:T(8,128)}, u32[]{:S(2)}) copy-start(s32[16,8]{0,1:T(8,128)} %param.10) | copy-start | bytes 1540
  9.8 42.4 %copy-start = (bf16[64,32,3,3]{0,1,3,2:T(8,128)(2,1)S(1)}, bf16[64,32,3,3]{0,1,3,2:T(8,128)(2,1)}, u32[]{:S(2)}) copy-start(bf16[64,32,3,3]{0,1,3,2:T(8,128)(2,1)} %param.12) | copy-start | bytes 110596
  9.8 30.7 %collective-permute-start = (bf16[8,8,9600]{2,1,0:T(8,128)(2,1)}, bf16[8,8,9600]{2,1,0:T(8,128)(2,1)}, u32[]{:S(2)}, u32[]{:S(2)}) collective-permute-start(bf16[8,8,9600]{2,1,0:T(8,128)(2,1)} %get-tuple-element.87), channel_id=1, source_target_pairs={{0,4},{1,3},{2,6},{3,1},{4,0},{5,7},{6,2},{7,5},{8,12},{9,11},{10,... | collective-permute-start | bytes 3686408 | tf_op jit(solution)/shard_map/ppermute | solution.py:473
  12.9 30.3 %collective-permute-start.1 = (bf16[8,8,9600]{2,1,0:T(8,128)(2,1)}, bf16[8,8,9600]{2,1,0:T(8,128)(2,1)}, u32[]{:S(2)}, u32[]{:S(2)}) collective-permute-start(bf16[8,8,9600]{2,1,0:T(8,128)(2,1)} %get-tuple-element.83), channel_id=1, source_target_pairs={{0,2},{1,5},{2,0},{3,7},{4,6},{5,1},{6,4},{7,3},{8,10},{9,13},{10,... | collective-permute-start | bytes 3686408 | tf_op jit(solution)/shard_map/ppermute | solution.py:473
  15.8 53.7 %collective-permute-start.4 = (bf16[13,8,9600]{2,1,0:T(8,128)(2,1)}, bf16[13,8,9600]{2,1,0:T(8,128)(2,1)S(1)}, u32[]{:S(2)}, u32[]{:S(2)}) collective-permute-start(bf16[13,8,9600]{2,1,0:T(8,128)(2,1)} %slice.70), channel_id=1, source_target_pairs={{0,8},{1,9},{2,10},{3,11},{4,12},{5,13},{6,14},{7,15},{8,24},{9,25... | collective-permute-start | bytes 5990408 | tf_op jit(solution)/shard_map/ppermute | solution.py:473
  17.4 52.1 %collective-permute-start.5 = (bf16[8,8,9600]{2,1,0:T(8,128)(2,1)}, bf16[8,8,9600]{2,1,0:T(8,128)(2,1)S(1)}, u32[]{:S(2)}, u32[]{:S(2)}) collective-permute-start(bf16[8,8,9600]{2,1,0:T(8,128)(2,1)} %get-tuple-element.69), channel_id=1, source_target_pairs={{0,2},{1,5},{2,0},{3,7},{4,6},{5,1},{6,4},{7,3},{8,10},{9,13},{10,... | collective-permute-start | bytes 3686408 | tf_op jit(solution)/shard_map/ppermute | solution.py:473
  17.9 51.6 %collective-permute-start.6 = (bf16[8,8,9600]{2,1,0:T(8,128)(2,1)}, bf16[8,8,9600]{2,1,0:T(8,128)(2,1)}, u32[]{:S(2)}, u32[]{:S(2)}) collective-permute-start(bf16[8,8,9600]{2,1,0:T(8,128)(2,1)} %get-tuple-element.70), channel_id=1, source_target_pairs={{0,4},{1,3},{2,6},{3,1},{4,0},{5,7},{6,2},{7,5},{8,12},{9,11},{10,... | collective-permute-start | bytes 3686408 | tf_op jit(solution)/shard_map/ppermute | solution.py:473
  43.1 52.8 %collective-permute-start.2 = (bf16[8,8,9600]{2,1,0:T(8,128)(2,1)}, bf16[8,8,9600]{2,1,0:T(8,128)(2,1)}, u32[]{:S(2)}, u32[]{:S(2)}) collective-permute-start(bf16[8,8,9600]{2,1,0:T(8,128)(2,1)} %collective-permute-done.rest_2_), channel_id=1, source_target_pairs={{0,2},{1,5},{2,0},{3,7},{4,6},{5,1},{6,4},{7,3},{8,10},{9,13},{10,... | collective-permute-start | bytes 3686408 | tf_op jit(solution)/shard_map/ppermute | solution.py:473
  44.6 51.3 %collective-permute-start.3 = (bf16[8,8,9600]{2,1,0:T(8,128)(2,1)}, bf16[8,8,9600]{2,1,0:T(8,128)(2,1)}, u32[]{:S(2)}, u32[]{:S(2)}) collective-permute-start(bf16[8,8,9600]{2,1,0:T(8,128)(2,1)} %collective-permute-done.1.rest_1_), channel_id=1, source_target_pairs={{0,4},{1,3},{2,6},{3,1},{4,0},{5,7},{6,2},{7,5},{8,12},{9,11},{10,... | collective-permute-start | bytes 3686408 | tf_op jit(solution)/shard_map/ppermute | solution.py:473
  47.3 50.7 %all-to-all-start = ((s32[32,1,128]{2,1,0:T(1,128)}), s32[32,1,128]{2,1,0:T(1,128)S(1)}, u32[]{:S(2)}, u32[]{:S(2)}) async-start(s32[32,1,128]{2,1,0:T(1,128)} %broadcast_in_dim.11), calls=%async_computation | async-start | bytes 32768 | tf_op jit(solution)/shard_map/all_to_all | solution.py:477
  60.8 11.0 %copy-start.1 = (bf16[512,1024]{1,0:T(8,128)(2,1)}, bf16[512,1024]{1,0:T(8,128)(2,1)S(1)}, u32[]{:S(2)}) copy-start(bf16[512,1024]{1,0:T(8,128)(2,1)S(1)} %get-tuple-element.63.two_ref) | copy-start | bytes 3145732
  60.8 11.0 %copy-start.2 = (bf16[64,2048]{1,0:T(8,128)(2,1)}, bf16[64,2048]{1,0:T(8,128)(2,1)S(1)}, u32[]{:S(2)}) copy-start(bf16[64,2048]{1,0:T(8,128)(2,1)S(1)} %get-tuple-element.62.one_ref) | copy-start | bytes 786436
  60.8 11.0 %copy-start.3 = (bf16[256,256]{1,0:T(8,128)(2,1)}, bf16[256,256]{1,0:T(8,128)(2,1)S(1)}, u32[]{:S(2)}) copy-start(bf16[256,256]{1,0:T(8,128)(2,1)S(1)} %get-tuple-element.64.three_ref) | copy-start | bytes 393220
  69.5 43.1 %copy-start.6 = (bf16[8,8,9600]{2,1,0:T(8,128)(2,1)}, bf16[8,8,9600]{2,1,0:T(8,128)(2,1)S(1)}, u32[]{:S(2)}) copy-start(bf16[8,8,9600]{2,1,0:T(8,128)(2,1)S(1)} %collective-permute-done.5.rest_4_) | copy-start | bytes 3686404
  69.5 4.4 %copy-start.5 = (bf16[13,8,9600]{2,1,0:T(8,128)(2,1)}, bf16[13,8,9600]{2,1,0:T(8,128)(2,1)S(1)}, u32[]{:S(2)}) copy-start(bf16[13,8,9600]{2,1,0:T(8,128)(2,1)S(1)} %collective-permute-done.4.rest_3_) | copy-start | bytes 5990404
  71.8 41.3 %collective-permute-start.9 = (bf16[6,8,9600]{2,1,0:T(8,128)(2,1)}, bf16[6,8,9600]{2,1,0:T(8,128)(2,1)}, u32[]{:S(2)}, u32[]{:S(2)}) collective-permute-start(bf16[6,8,9600]{2,1,0:T(8,128)(2,1)} %slice.55), channel_id=1, source_target_pairs={{0,4},{1,3},{2,6},{3,1},{4,0},{5,7},{6,2},{7,5},{8,12},{9,11},{10,... | collective-permute-start | bytes 2764808 | tf_op jit(solution)/shard_map/ppermute | solution.py:473
  71.9 47.1 %collective-permute-start.8 = (bf16[7,8,9600]{2,1,0:T(8,128)(2,1)}, bf16[7,8,9600]{2,1,0:T(8,128)(2,1)}, u32[]{:S(2)}, u32[]{:S(2)}) collective-permute-start(bf16[7,8,9600]{2,1,0:T(8,128)(2,1)} %slice.54), channel_id=1, source_target_pairs={{0,2},{1,5},{2,0},{3,7},{4,6},{5,1},{6,4},{7,3},{8,10},{9,13},{10,... | collective-permute-start | bytes 3225608 | tf_op jit(solution)/shard_map/ppermute | solution.py:473
  73.9 45.2 %collective-permute-start.7 = (bf16[13,8,9600]{2,1,0:T(8,128)(2,1)S(1)}, bf16[13,8,9600]{2,1,0:T(8,128)(2,1)}, u32[]{:S(2)}, u32[]{:S(2)}) collective-permute-start(bf16[13,8,9600]{2,1,0:T(8,128)(2,1)S(1)} %collective-permute-done.4.rest_3_), channel_id=1, source_target_pairs={{0,8},{1,9},{2,10},{3,11},{4,12},{5,13},{6,14},{7,15},{8,24},{9,25... | collective-permute-start | bytes 5990408 | tf_op jit(solution)/shard_map/ppermute | solution.py:473
  96.0 42.8 %collective-permute-start.10 = (bf16[6,8,9600]{2,1,0:T(8,128)(2,1)}, bf16[6,8,9600]{2,1,0:T(8,128)(2,1)}, u32[]{:S(2)}, u32[]{:S(2)}) collective-permute-start(bf16[6,8,9600]{2,1,0:T(8,128)(2,1)} %slice.55), channel_id=1, source_target_pairs={{0,2},{1,5},{2,0},{3,7},{4,6},{5,1},{6,4},{7,3},{8,10},{9,13},{10,... | collective-permute-start | bytes 2764808 | tf_op jit(solution)/shard_map/ppermute | solution.py:473
  97.4 41.3 %collective-permute-start.11 = (bf16[7,8,9600]{2,1,0:T(8,128)(2,1)}, bf16[7,8,9600]{2,1,0:T(8,128)(2,1)}, u32[]{:S(2)}, u32[]{:S(2)}) collective-permute-start(bf16[7,8,9600]{2,1,0:T(8,128)(2,1)} %slice.54), channel_id=1, source_target_pairs={{0,4},{1,3},{2,6},{3,1},{4,0},{5,7},{6,2},{7,5},{8,12},{9,11},{10,... | collective-permute-start | bytes 3225608 | tf_op jit(solution)/shard_map/ppermute | solution.py:473
  98.0 0.6 copy-start.7
  119.0 39.5 %collective-permute-start.13 = (bf16[6,8,9600]{2,1,0:T(8,128)(2,1)}, bf16[6,8,9600]{2,1,0:T(8,128)(2,1)}, u32[]{:S(2)}, u32[]{:S(2)}) collective-permute-start(bf16[6,8,9600]{2,1,0:T(8,128)(2,1)} %collective-permute-done.9.rest_2_), channel_id=1, source_target_pairs={{0,2},{1,5},{2,0},{3,7},{4,6},{5,1},{6,4},{7,3},{8,10},{9,13},{10,... | collective-permute-start | bytes 2764808 | tf_op jit(solution)/shard_map/ppermute | solution.py:473
  120.5 39.6 %collective-permute-start.14 = (bf16[7,8,9600]{2,1,0:T(8,128)(2,1)}, bf16[7,8,9600]{2,1,0:T(8,128)(2,1)}, u32[]{:S(2)}, u32[]{:S(2)}) collective-permute-start(bf16[7,8,9600]{2,1,0:T(8,128)(2,1)} %collective-permute-done.8.rest_1_), channel_id=1, source_target_pairs={{0,4},{1,3},{2,6},{3,1},{4,0},{5,7},{6,2},{7,5},{8,12},{9,11},{10,... | collective-permute-start | bytes 3225608 | tf_op jit(solution)/shard_map/ppermute | solution.py:473
  121.0 47.6 %collective-permute-start.12 = (bf16[13,8,9600]{2,1,0:T(8,128)(2,1)}, bf16[13,8,9600]{2,1,0:T(8,128)(2,1)}, u32[]{:S(2)}, u32[]{:S(2)}) collective-permute-start(bf16[13,8,9600]{2,1,0:T(8,128)(2,1)} %collective-permute-done.7.rest_0_), channel_id=1, source_target_pairs={{0,8},{1,9},{2,10},{3,11},{4,12},{5,13},{6,14},{7,15},{8,24},{9,25... | collective-permute-start | bytes 5990408 | tf_op jit(solution)/shard_map/ppermute | solution.py:473
  143.9 35.0 %collective-permute-start.16 = (bf16[6,8,9600]{2,1,0:T(8,128)(2,1)S(1)}, bf16[6,8,9600]{2,1,0:T(8,128)(2,1)}, u32[]{:S(2)}, u32[]{:S(2)}) collective-permute-start(bf16[6,8,9600]{2,1,0:T(8,128)(2,1)S(1)} %slice.57), channel_id=1, source_target_pairs={{0,4},{1,3},{2,6},{3,1},{4,0},{5,7},{6,2},{7,5},{8,12},{9,11},{10,... | collective-permute-start | bytes 2764808 | tf_op jit(solution)/shard_map/ppermute | solution.py:473
  144.0 37.6 %collective-permute-start.15 = (bf16[7,8,9600]{2,1,0:T(8,128)(2,1)}, bf16[7,8,9600]{2,1,0:T(8,128)(2,1)}, u32[]{:S(2)}, u32[]{:S(2)}) collective-permute-start(bf16[7,8,9600]{2,1,0:T(8,128)(2,1)} %slice.56), channel_id=1, source_target_pairs={{0,2},{1,5},{2,0},{3,7},{4,6},{5,1},{6,4},{7,3},{8,10},{9,13},{10,... | collective-permute-start | bytes 3225608 | tf_op jit(solution)/shard_map/ppermute | solution.py:473
  158.5 47.0 %collective-permute-start.17 = (bf16[12,8,9600]{2,1,0:T(8,128)(2,1)}, bf16[12,8,9600]{2,1,0:T(8,128)(2,1)}, u32[]{:S(2)}, u32[]{:S(2)}) collective-permute-start(bf16[12,8,9600]{2,1,0:T(8,128)(2,1)} %slice_dynamic-update-slice_fusion), channel_id=1, source_target_pairs={{0,8},{1,9},{2,10},{3,11},{4,12},{5,13},{6,14},{7,15},{8,24},{9,25... | collective-permute-start | bytes 5529608 | tf_op jit(solution)/shard_map/ppermute | solution.py:473
  168.7 32.7 %collective-permute-start.18 = (bf16[6,8,9600]{2,1,0:T(8,128)(2,1)S(1)}, bf16[6,8,9600]{2,1,0:T(8,128)(2,1)}, u32[]{:S(2)}, u32[]{:S(2)}) collective-permute-start(bf16[6,8,9600]{2,1,0:T(8,128)(2,1)S(1)} %slice.57), channel_id=1, source_target_pairs={{0,2},{1,5},{2,0},{3,7},{4,6},{5,1},{6,4},{7,3},{8,10},{9,13},{10,... | collective-permute-start | bytes 2764808 | tf_op jit(solution)/shard_map/ppermute | solution.py:473
  168.9 33.1 %collective-permute-start.19 = (bf16[7,8,9600]{2,1,0:T(8,128)(2,1)}, bf16[7,8,9600]{2,1,0:T(8,128)(2,1)}, u32[]{:S(2)}, u32[]{:S(2)}) collective-permute-start(bf16[7,8,9600]{2,1,0:T(8,128)(2,1)} %slice.56), channel_id=1, source_target_pairs={{0,4},{1,3},{2,6},{3,1},{4,0},{5,7},{6,2},{7,5},{8,12},{9,11},{10,... | collective-permute-start | bytes 3225608 | tf_op jit(solution)/shard_map/ppermute | solution.py:473
  181.6 39.5 %collective-permute-start.20 = (bf16[6,8,9600]{2,1,0:T(8,128)(2,1)}, bf16[6,8,9600]{2,1,0:T(8,128)(2,1)}, u32[]{:S(2)}, u32[]{:S(2)}) collective-permute-start(bf16[6,8,9600]{2,1,0:T(8,128)(2,1)} %collective-permute-done.16.rest_1_), channel_id=1, source_target_pairs={{0,2},{1,5},{2,0},{3,7},{4,6},{5,1},{6,4},{7,3},{8,10},{9,13},{10,... | collective-permute-start | bytes 2764808 | tf_op jit(solution)/shard_map/ppermute | solution.py:473
  183.1 42.0 %collective-permute-start.21 = (bf16[7,8,9600]{2,1,0:T(8,128)(2,1)}, bf16[7,8,9600]{2,1,0:T(8,128)(2,1)}, u32[]{:S(2)}, u32[]{:S(2)}) collective-permute-start(bf16[7,8,9600]{2,1,0:T(8,128)(2,1)} %collective-permute-done.15.rest_0_), channel_id=1, source_target_pairs={{0,4},{1,3},{2,6},{3,1},{4,0},{5,7},{6,2},{7,5},{8,12},{9,11},{10,... | collective-permute-start | bytes 3225608 | tf_op jit(solution)/shard_map/ppermute | solution.py:473
  205.6 41.2 %collective-permute-start.22 = (bf16[12,8,9600]{2,1,0:T(8,128)(2,1)}, bf16[12,8,9600]{2,1,0:T(8,128)(2,1)}, u32[]{:S(2)}, u32[]{:S(2)}) collective-permute-start(bf16[12,8,9600]{2,1,0:T(8,128)(2,1)} %collective-permute-done.17.rest_2_), channel_id=1, source_target_pairs={{0,8},{1,9},{2,10},{3,11},{4,12},{5,13},{6,14},{7,15},{8,24},{9,25... | collective-permute-start | bytes 5529608 | tf_op jit(solution)/shard_map/ppermute | solution.py:473
  208.1 40.2 %collective-permute-start.24 = (bf16[6,8,9600]{2,1,0:T(8,128)(2,1)S(1)}, bf16[6,8,9600]{2,1,0:T(8,128)(2,1)}, u32[]{:S(2)}, u32[]{:S(2)}) collective-permute-start(bf16[6,8,9600]{2,1,0:T(8,128)(2,1)S(1)} %slice.67), channel_id=1, source_target_pairs={{0,4},{1,3},{2,6},{3,1},{4,0},{5,7},{6,2},{7,5},{8,12},{9,11},{10,... | collective-permute-start | bytes 2764808 | tf_op jit(solution)/shard_map/ppermute | solution.py:473
  209.6 38.7 %collective-permute-start.23 = (bf16[7,8,9600]{2,1,0:T(8,128)(2,1)}, bf16[7,8,9600]{2,1,0:T(8,128)(2,1)}, u32[]{:S(2)}, u32[]{:S(2)}) collective-permute-start(bf16[7,8,9600]{2,1,0:T(8,128)(2,1)} %slice.66), channel_id=1, source_target_pairs={{0,2},{1,5},{2,0},{3,7},{4,6},{5,1},{6,4},{7,3},{8,10},{9,13},{10,... | collective-permute-start | bytes 3225608 | tf_op jit(solution)/shard_map/ppermute | solution.py:473
  225.1 38.8 %collective-permute-start.25 = (bf16[6,8,9600]{2,1,0:T(8,128)(2,1)S(1)}, bf16[6,8,9600]{2,1,0:T(8,128)(2,1)}, u32[]{:S(2)}, u32[]{:S(2)}) collective-permute-start(bf16[6,8,9600]{2,1,0:T(8,128)(2,1)S(1)} %slice.67), channel_id=1, source_target_pairs={{0,2},{1,5},{2,0},{3,7},{4,6},{5,1},{6,4},{7,3},{8,10},{9,13},{10,... | collective-permute-start | bytes 2764808 | tf_op jit(solution)/shard_map/ppermute | solution.py:473
  227.6 40.3 %collective-permute-start.26 = (bf16[7,8,9600]{2,1,0:T(8,128)(2,1)}, bf16[7,8,9600]{2,1,0:T(8,128)(2,1)}, u32[]{:S(2)}, u32[]{:S(2)}) collective-permute-start(bf16[7,8,9600]{2,1,0:T(8,128)(2,1)} %slice.66), channel_id=1, source_target_pairs={{0,4},{1,3},{2,6},{3,1},{4,0},{5,7},{6,2},{7,5},{8,12},{9,11},{10,... | collective-permute-start | bytes 3225608 | tf_op jit(solution)/shard_map/ppermute | solution.py:473
  246.7 39.7 %collective-permute-start.27 = (bf16[12,8,9600]{2,1,0:T(8,128)(2,1)}, bf16[12,8,9600]{2,1,0:T(8,128)(2,1)}, u32[]{:S(2)}, u32[]{:S(2)}) collective-permute-start(bf16[12,8,9600]{2,1,0:T(8,128)(2,1)} %collective-permute-done.22.rest_0_), channel_id=1, source_target_pairs={{0,8},{1,9},{2,10},{3,11},{4,12},{5,13},{6,14},{7,15},{8,24},{9,25... | collective-permute-start | bytes 5529608 | tf_op jit(solution)/shard_map/ppermute | solution.py:473
  248.3 35.3 %collective-permute-start.28 = (bf16[6,8,9600]{2,1,0:T(8,128)(2,1)}, bf16[6,8,9600]{2,1,0:T(8,128)(2,1)}, u32[]{:S(2)}, u32[]{:S(2)}) collective-permute-start(bf16[6,8,9600]{2,1,0:T(8,128)(2,1)} %collective-permute-done.24.rest_2_), channel_id=1, source_target_pairs={{0,2},{1,5},{2,0},{3,7},{4,6},{5,1},{6,4},{7,3},{8,10},{9,13},{10,... | collective-permute-start | bytes 2764808 | tf_op jit(solution)/shard_map/ppermute | solution.py:473
  249.2 37.3 %collective-permute-start.29 = (bf16[7,8,9600]{2,1,0:T(8,128)(2,1)}, bf16[7,8,9600]{2,1,0:T(8,128)(2,1)}, u32[]{:S(2)}, u32[]{:S(2)}) collective-permute-start(bf16[7,8,9600]{2,1,0:T(8,128)(2,1)} %collective-permute-done.23.rest_1_), channel_id=1, source_target_pairs={{0,4},{1,3},{2,6},{3,1},{4,0},{5,7},{6,2},{7,5},{8,12},{9,11},{10,... | collective-permute-start | bytes 3225608 | tf_op jit(solution)/shard_map/ppermute | solution.py:473
Sparse Core Ops, SparseCore 0:
  8.9 62.0 all-gather.1

commit v17 on v16

--- a/solution.py
+++ b/solution.py
@@ -12,7 +12,7 @@
 R = 5
 GROUP = 16
 SHARES = (1, 7, 6, 2)
-HEAD = 64
+HEAD = 32
 LATER = 4
 LISTS = 2
 WAITS = 5

time: 317 us -> 316 us (level)
  no operation moved by 1% of the time
where the time goes in v17:
time: 316 us; the launch traced here: 315 us
  waiting for transfers between devices  139 us (44%)
  Pallas kernels  72.9 us (23%)
  starting transfers between devices  45.3 us (14%)
  local copies, waits for them, and re-layouts  30 us (9%)
  between operations  13.6 us (4%)
  blocking collectives  13.3 us (4%)
    ppermute x30, waiting for transfers between devices, body(): gather.blocks[target] = lax.ppermute(block, 'shard', gather.steps[axis])  138 us
    pallas_call x5, Pallas kernels, pair_scores(): pl.pallas_call(functools.partial(pair_kernel, frames, idx_dev, len(blocks...  50.4 us
    ppermute x30, starting transfers between devices, body(): gather.blocks[target] = lax.ppermute(block, 'shard', gather.steps[axis])  40.3 us
    pallas_call x1, Pallas kernels, pair_lists(): pl.pallas_call(functools.partial(list_kernel, idx_dev, k_count, ids.shape...  14 us
    all_to_all x1, blocking collectives, body(): lax.all_to_all(tables[-1], 'shard', split_axis=0, concat_axis=0, tiled=True)  13.3 us
    unnamed x29, local copies, waits for them, and re-layouts  13.1 us
    slice x8, local copies, waits for them, and re-layouts, block(): parts = [b[at:at + n] for b, (_, at, n) in zip(whole, self.pieces[key])]  12.3 us
    pallas_call x1, Pallas kernels, head_matrices(): pl.pallas_call(head_kernel, out_shape=[jax.ShapeDtypeStruct(s, jnp.bfloat...  8.54 us
  transfers between devices with their start and end apart: 32, of which 20 were waited for; matrix products, arithmetic and copies ran while one was open for 9% of the time, Pallas kernels for 21%

profile of v17, /device:TPU:0, one launch (start us, length us, event | category | flops | bytes accessed | tf_op | source)
XLA Modules:
  0.0 314.5 jit_solution(6374244189706649300)
XLA Ops:
  7.3 1.0 copy-done.4
  8.2 1.6 fusion
  9.8 3.0 collective-permute-start
  12.9 1.5 collective-permute-start.1
  14.4 1.4 slice.70
  15.8 1.6 collective-permute-start.4
  18.4 22.2 %collective-permute-done.rest_2_ = bf16[8,8,9600]{2,1,0:T(8,128)(2,1)} collective-permute-done((bf16[8,8,9600]{2,1,0:T(8,128)(2,1)}, bf16[8,8,9600]{2,1,0:T(8,128)(2,1)}, u32[]{:S(2)}, u32[]{:S(2)}) %collective-permute-start) | collective-permute-done | bytes 1228832 | tf_op jit(solution)/shard_map/ppermute | solution.py:473
  40.6 2.6 collective-permute-done.1.rest_1_
  43.2 1.5 collective-permute-start.2
  47.3 4.9 %all-to-all-start = ((s32[32,1,128]{2,1,0:T(1,128)}), s32[32,1,128]{2,1,0:T(1,128)S(1)}, u32[]{:S(2)}, u32[]{:S(2)}) async-start(s32[32,1,128]{2,1,0:T(1,128)} %broadcast_in_dim.11), calls=%async_computation | async-start | bytes 32768 | tf_op jit(solution)/shard_map/all_to_all | solution.py:477
  52.2 8.5 %head_matrices.1 = (bf16[64,2048]{1,0:T(8,128)(2,1)S(1)}, bf16[512,1024]{1,0:T(8,128)(2,1)S(1)}, bf16[256,256]{1,0:T(8,128)(2,1)S(1)}) custom-call(bf16[9,1,32]{2,1,0:T(2,128)(2,1)S(1)} %reshape.27.one_w, bf16[9,32,64]{2,1,0:T(8,128)(2,1)S(1)} %bitcast.17, bf16[9,1,64]{2,1,0:T(2,128)(2,1)S(1)} %reshape.28.three_w), custom_call_target="tpu_custom_call" | custom-call | flops 1000000000 | bytes 3000000 | tf_op jit(solution)/shard_map/head_matrices/pallas_call | solution.py:90
  60.8 8.7 %collective-permute-done.5.rest_4_ = bf16[8,8,9600]{2,1,0:T(8,128)(2,1)S(1)} collective-permute-done((bf16[8,8,9600]{2,1,0:T(8,128)(2,1)}, bf16[8,8,9600]{2,1,0:T(8,128)(2,1)S(1)}, u32[]{:S(2)}, u32[]{:S(2)}) %collective-permute-start.5) | collective-permute-done | bytes 1228832 | tf_op jit(solution)/shard_map/ppermute | solution.py:473
  69.5 1.1 slice.55
  70.6 1.2 slice.54
  72.0 2.0 collective-permute-start.8
  73.9 1.6 collective-permute-start.7
  75.5 20.5 %collective-permute-done.2.rest_6_ = bf16[8,8,9600]{2,1,0:T(8,128)(2,1)} collective-permute-done((bf16[8,8,9600]{2,1,0:T(8,128)(2,1)}, bf16[8,8,9600]{2,1,0:T(8,128)(2,1)}, u32[]{:S(2)}, u32[]{:S(2)}) %collective-permute-start.2) | collective-permute-done | bytes 1228832 | tf_op jit(solution)/shard_map/ppermute | solution.py:473
  96.0 1.5 collective-permute-start.10
  98.6 14.0 %pair_lists.1 = (s32[120]{0:T(128)}, s32[120]{0:T(128)}, s32[151]{0:T(256)}, s32[117]{0:T(128)}, s32[83]{0:T(128)}) custom-call(s32[18]{0:T(128)} %pad_add_fusion.who_ref, s32[32,128]{1,0:T(8,128)} %bitcast.18, s32[256]{0:T(256)} %constant.41.clone.queries_ref), custom_call_target="tpu_custom_call" | custom-call | flops 99999997952 | bytes 1000000 | tf_op jit(solution)/shard_map/pair_lists/pallas_call | solution.py:136
  113.1 5.9 %collective-permute-done.8.rest_1_ = bf16[7,8,9600]{2,1,0:T(8,128)(2,1)} collective-permute-done((bf16[7,8,9600]{2,1,0:T(8,128)(2,1)}, bf16[7,8,9600]{2,1,0:T(8,128)(2,1)}, u32[]{:S(2)}, u32[]{:S(2)}) %collective-permute-start.8) | collective-permute-done | bytes 1075232 | tf_op jit(solution)/shard_map/ppermute | solution.py:473
  119.0 1.5 collective-permute-start.13
  121.0 1.6 collective-permute-start.12
  123.2 13.9 %phase_0.1.before_ref = f32[32,128]{1,0:T(8,128)} custom-call(s32[120]{0:T(128)} %get-tuple-element.68.list_ref, bf16[64,2048]{1,0:T(8,128)(2,1)} %copy-done.2, bf16[512,1024]{1,0:T(8,128)(2,1)} %copy-done.1, bf16[256,256]{1,0:T(8,128)(2,1)} %copy-done.3, f32[32,128]{1,0:T(8,128)} %broadcast_in_dim.12.before_ref, ...), custom_call_target="tpu_custom_call" | custom-call | flops 75497472000 | bytes 29491200 | tf_op jit(solution)/shard_map/phase_0/pallas_call | solution.py:265
  137.1 1.7 collective-permute-done.10.rest_3_
  138.8 1.2 slice.57
  140.0 2.3 slice.56
  142.3 1.6 slice_dynamic-update-slice_fusion.7
  144.5 1.5 collective-permute-start.15
  146.0 1.6 slice_dynamic-update-slice_fusion.6
  147.6 1.6 slice_dynamic-update-slice_fusion.5
  149.2 1.6 slice_dynamic-update-slice_fusion.4
  150.8 1.7 slice_dynamic-update-slice_fusion.3
  152.5 1.7 slice_dynamic-update-slice_fusion.2
  154.2 1.7 slice_dynamic-update-slice_fusion.1
  155.9 1.7 slice_dynamic-update-slice_fusion
  157.6 0.9 collective-permute-done.13.rest_6_
  158.5 1.6 collective-permute-start.17
  160.1 8.6 %collective-permute-done.12.rest_5_ = bf16[13,8,9600]{2,1,0:T(8,128)(2,1)} collective-permute-done((bf16[13,8,9600]{2,1,0:T(8,128)(2,1)}, bf16[13,8,9600]{2,1,0:T(8,128)(2,1)}, u32[]{:S(2)}, u32[]{:S(2)}) %collective-permute-start.12) | collective-permute-done | bytes 1996832 | tf_op jit(solution)/shard_map/ppermute | solution.py:473
  168.9 1.9 collective-permute-start.19
  170.7 8.2 %collective-permute-done.16.rest_1_ = bf16[6,8,9600]{2,1,0:T(8,128)(2,1)} collective-permute-done((bf16[6,8,9600]{2,1,0:T(8,128)(2,1)S(1)}, bf16[6,8,9600]{2,1,0:T(8,128)(2,1)}, u32[]{:S(2)}, u32[]{:S(2)}) %collective-permute-start.16) | collective-permute-done | bytes 921632 | tf_op jit(solution)/shard_map/ppermute | solution.py:473
  179.0 2.6 collective-permute-done.15.rest_0_
  181.6 1.5 collective-permute-start.20
  183.6 11.3 %phase_1.1.before_ref = f32[32,128]{1,0:T(8,128)} custom-call(s32[120]{0:T(128)} %get-tuple-element.67.list_ref, bf16[64,2048]{1,0:T(8,128)(2,1)} %copy-done.2, bf16[512,1024]{1,0:T(8,128)(2,1)} %copy-done.1, bf16[256,256]{1,0:T(8,128)(2,1)} %copy-done.3, f32[32,128]{1,0:T(8,128)} %phase_0.1.before_ref, ...), custom_call_target="tpu_custom_call" | custom-call | flops 75497472000 | bytes 29491200 | tf_op jit(solution)/shard_map/phase_1/pallas_call | solution.py:265
  194.9 6.4 %collective-permute-done.18.rest_3_ = bf16[6,8,9600]{2,1,0:T(8,128)(2,1)} collective-permute-done((bf16[6,8,9600]{2,1,0:T(8,128)(2,1)S(1)}, bf16[6,8,9600]{2,1,0:T(8,128)(2,1)}, u32[]{:S(2)}, u32[]{:S(2)}) %collective-permute-start.18) | collective-permute-done | bytes 921632 | tf_op jit(solution)/shard_map/ppermute | solution.py:473
  202.0 1.2 slice.67
  203.3 2.3 slice.66
  205.5 2.5 collective-permute-start.22
  208.0 1.5 collective-permute-start.24
  209.6 1.5 collective-permute-start.23
  211.1 10.0 %collective-permute-done.20.rest_5_ = bf16[6,8,9600]{2,1,0:T(8,128)(2,1)} collective-permute-done((bf16[6,8,9600]{2,1,0:T(8,128)(2,1)}, bf16[6,8,9600]{2,1,0:T(8,128)(2,1)}, u32[]{:S(2)}, u32[]{:S(2)}) %collective-permute-start.20) | collective-permute-done | bytes 921632 | tf_op jit(solution)/shard_map/ppermute | solution.py:473
  221.1 4.0 %collective-permute-done.21.rest_6_ = bf16[7,8,9600]{2,1,0:T(8,128)(2,1)} collective-permute-done((bf16[7,8,9600]{2,1,0:T(8,128)(2,1)}, bf16[7,8,9600]{2,1,0:T(8,128)(2,1)}, u32[]{:S(2)}, u32[]{:S(2)}) %collective-permute-start.21) | collective-permute-done | bytes 1075232 | tf_op jit(solution)/shard_map/ppermute | solution.py:473
  225.1 2.5 collective-permute-start.25
  227.6 1.5 collective-permute-start.26
  229.1 10.4 %phase_2.1.before_ref = f32[32,128]{1,0:T(8,128)} custom-call(s32[151]{0:T(256)} %get-tuple-element.66.list_ref, bf16[64,2048]{1,0:T(8,128)(2,1)} %copy-done.2, bf16[512,1024]{1,0:T(8,128)(2,1)} %copy-done.1, bf16[256,256]{1,0:T(8,128)(2,1)} %copy-done.3, f32[32,128]{1,0:T(8,128)} %phase_1.1.before_ref, ...), custom_call_target="tpu_custom_call" | custom-call | flops 100663296000 | bytes 39321600 | tf_op jit(solution)/shard_map/phase_2/pallas_call | solution.py:265
  239.5 7.2 %collective-permute-done.22.rest_0_ = bf16[12,8,9600]{2,1,0:T(8,128)(2,1)} collective-permute-done((bf16[12,8,9600]{2,1,0:T(8,128)(2,1)}, bf16[12,8,9600]{2,1,0:T(8,128)(2,1)}, u32[]{:S(2)}, u32[]{:S(2)}) %collective-permute-start.22) | collective-permute-done | bytes 1843232 | tf_op jit(solution)/shard_map/ppermute | solution.py:473
  246.7 1.6 collective-permute-start.27
  249.2 2.2 collective-permute-start.29
  251.4 12.5 %collective-permute-done.25.rest_3_ = bf16[6,8,9600]{2,1,0:T(8,128)(2,1)} collective-permute-done((bf16[6,8,9600]{2,1,0:T(8,128)(2,1)S(1)}, bf16[6,8,9600]{2,1,0:T(8,128)(2,1)}, u32[]{:S(2)}, u32[]{:S(2)}) %collective-permute-start.25) | collective-permute-done | bytes 921632 | tf_op jit(solution)/shard_map/ppermute | solution.py:473
  263.9 4.0 %collective-permute-done.26.rest_4_ = bf16[7,8,9600]{2,1,0:T(8,128)(2,1)} collective-permute-done((bf16[7,8,9600]{2,1,0:T(8,128)(2,1)}, bf16[7,8,9600]{2,1,0:T(8,128)(2,1)}, u32[]{:S(2)}, u32[]{:S(2)}) %collective-permute-start.26) | collective-permute-done | bytes 1075232 | tf_op jit(solution)/shard_map/ppermute | solution.py:473
  267.9 7.7 %phase_3.1.before_ref = f32[32,128]{1,0:T(8,128)} custom-call(s32[117]{0:T(128)} %get-tuple-element.65.list_ref, bf16[64,2048]{1,0:T(8,128)(2,1)} %copy-done.2, bf16[512,1024]{1,0:T(8,128)(2,1)} %copy-done.1, bf16[256,256]{1,0:T(8,128)(2,1)} %copy-done.3, f32[32,128]{1,0:T(8,128)} %phase_2.1.before_ref, ...), custom_call_target="tpu_custom_call" | custom-call | flops 75497472000 | bytes 29491200 | tf_op jit(solution)/shard_map/phase_3/pallas_call | solution.py:265
  275.5 8.1 %collective-permute-done.28.rest_1_ = bf16[6,8,9600]{2,1,0:T(8,128)(2,1)} collective-permute-done((bf16[6,8,9600]{2,1,0:T(8,128)(2,1)}, bf16[6,8,9600]{2,1,0:T(8,128)(2,1)}, u32[]{:S(2)}, u32[]{:S(2)}) %collective-permute-start.28) | collective-permute-done | bytes 921632 | tf_op jit(solution)/shard_map/ppermute | solution.py:473
  283.6 2.9 collective-permute-done.29.rest_2_
  286.5 7.1 %phase_4.1 = f32[32,128]{1,0:T(8,128)} custom-call(s32[83]{0:T(128)} %get-tuple-element.61.list_ref, bf16[64,2048]{1,0:T(8,128)(2,1)} %copy-done.2, bf16[512,1024]{1,0:T(8,128)(2,1)} %copy-done.1, bf16[256,256]{1,0:T(8,128)(2,1)} %copy-done.3, f32[32,128]{1,0:T(8,128)} %phase_3.1.before_ref, bf16[256,8,9600]{2,1,0:T(8,128)(2,1)} %all-gather.2.cloned.1.call-done.v_hbm, ...), custom_call_target="tpu_custom_call" | custom-call | flops 50331648000 | bytes 19660800 | tf_op jit(solution)/shard_map/phase_4/pallas_call | solution.py:265
  293.5 13.3 %all_to_all.17 = f32[32,1,128]{2,1,0:T(1,128)S(1)} all-to-all(f32[32,1,128]{2,1,0:T(1,128)} %bitcast.19), channel_id=1, replica_groups=mesh['shard'=32] {'shard'}, dimensions={0} | all-to-all | bytes 32768 | tf_op jit(solution)/shard_map/all_to_all | solution.py:488
  (58 shorter events, 11.0 us)
Async XLA Ops:
  6.5 1.7 copy-start.4
  6.5 116.1 %all-gather.2.cloned.1.call-start = ((), (), s32[]{:S(2)}) async-start(), calls=%async_computation.2 | async-start | bytes 58982400 | tf_op jit(solution)/shard_map/all_gather | solution.py:409
  9.8 35.3 %copy-start.9 = (bf16[32,1,3,3]{0,3,2,1:T(4,128)(2,1)S(1)}, bf16[32,1,3,3]{0,3,2,1:T(4,128)(2,1)}, u32[]{:S(2)}) copy-start(bf16[32,1,3,3]{0,3,2,1:T(4,128)(2,1)} %param.11) | copy-start | bytes 1732
  9.8 35.3 %copy-start.10 = (bf16[1,64,3,3]{1,3,2,0:T(4,128)(2,1)S(1)}, bf16[1,64,3,3]{1,3,2,0:T(4,128)(2,1)}, u32[]{:S(2)}) copy-start(bf16[1,64,3,3]{1,3,2,0:T(4,128)(2,1)} %param.13) | copy-start | bytes 3460
  9.8 36.7 %copy-start.8 = (s32[16,8]{0,1:T(8,128)S(1)}, s32[16,8]{0,1:T(8,128)}, u32[]{:S(2)}) copy-start(s32[16,8]{0,1:T(8,128)} %param.10) | copy-start | bytes 1540
  9.8 42.4 %copy-start = (bf16[64,32,3,3]{0,1,3,2:T(8,128)(2,1)S(1)}, bf16[64,32,3,3]{0,1,3,2:T(8,128)(2,1)}, u32[]{:S(2)}) copy-start(bf16[64,32,3,3]{0,1,3,2:T(8,128)(2,1)} %param.12) | copy-start | bytes 110596
  9.8 30.7 %collective-permute-start = (bf16[8,8,9600]{2,1,0:T(8,128)(2,1)}, bf16[8,8,9600]{2,1,0:T(8,128)(2,1)}, u32[]{:S(2)}, u32[]{:S(2)}) collective-permute-start(bf16[8,8,9600]{2,1,0:T(8,128)(2,1)} %get-tuple-element.87), channel_id=1, source_target_pairs={{0,4},{1,3},{2,6},{3,1},{4,0},{5,7},{6,2},{7,5},{8,12},{9,11},{10,... | collective-permute-start | bytes 3686408 | tf_op jit(solution)/shard_map/ppermute | solution.py:473
  12.9 30.3 %collective-permute-start.1 = (bf16[8,8,9600]{2,1,0:T(8,128)(2,1)}, bf16[8,8,9600]{2,1,0:T(8,128)(2,1)}, u32[]{:S(2)}, u32[]{:S(2)}) collective-permute-start(bf16[8,8,9600]{2,1,0:T(8,128)(2,1)} %get-tuple-element.83), channel_id=1, source_target_pairs={{0,2},{1,5},{2,0},{3,7},{4,6},{5,1},{6,4},{7,3},{8,10},{9,13},{10,... | collective-permute-start | bytes 3686408 | tf_op jit(solution)/shard_map/ppermute | solution.py:473
  15.8 53.7 %collective-permute-start.4 = (bf16[13,8,9600]{2,1,0:T(8,128)(2,1)}, bf16[13,8,9600]{2,1,0:T(8,128)(2,1)S(1)}, u32[]{:S(2)}, u32[]{:S(2)}) collective-permute-start(bf16[13,8,9600]{2,1,0:T(8,128)(2,1)} %slice.70), channel_id=1, source_target_pairs={{0,8},{1,9},{2,10},{3,11},{4,12},{5,13},{6,14},{7,15},{8,24},{9,25... | collective-permute-start | bytes 5990408 | tf_op jit(solution)/shard_map/ppermute | solution.py:473
  17.4 52.2 %collective-permute-start.5 = (bf16[8,8,9600]{2,1,0:T(8,128)(2,1)}, bf16[8,8,9600]{2,1,0:T(8,128)(2,1)S(1)}, u32[]{:S(2)}, u32[]{:S(2)}) collective-permute-start(bf16[8,8,9600]{2,1,0:T(8,128)(2,1)} %get-tuple-element.69), channel_id=1, source_target_pairs={{0,2},{1,5},{2,0},{3,7},{4,6},{5,1},{6,4},{7,3},{8,10},{9,13},{10,... | collective-permute-start | bytes 3686408 | tf_op jit(solution)/shard_map/ppermute | solution.py:473
  17.9 51.6 %collective-permute-start.6 = (bf16[8,8,9600]{2,1,0:T(8,128)(2,1)}, bf16[8,8,9600]{2,1,0:T(8,128)(2,1)}, u32[]{:S(2)}, u32[]{:S(2)}) collective-permute-start(bf16[8,8,9600]{2,1,0:T(8,128)(2,1)} %get-tuple-element.70), channel_id=1, source_target_pairs={{0,4},{1,3},{2,6},{3,1},{4,0},{5,7},{6,2},{7,5},{8,12},{9,11},{10,... | collective-permute-start | bytes 3686408 | tf_op jit(solution)/shard_map/ppermute | solution.py:473
  43.2 52.8 %collective-permute-start.2 = (bf16[8,8,9600]{2,1,0:T(8,128)(2,1)}, bf16[8,8,9600]{2,1,0:T(8,128)(2,1)}, u32[]{:S(2)}, u32[]{:S(2)}) collective-permute-start(bf16[8,8,9600]{2,1,0:T(8,128)(2,1)} %collective-permute-done.rest_2_), channel_id=1, source_target_pairs={{0,2},{1,5},{2,0},{3,7},{4,6},{5,1},{6,4},{7,3},{8,10},{9,13},{10,... | collective-permute-start | bytes 3686408 | tf_op jit(solution)/shard_map/ppermute | solution.py:473
  44.6 51.3 %collective-permute-start.3 = (bf16[8,8,9600]{2,1,0:T(8,128)(2,1)}, bf16[8,8,9600]{2,1,0:T(8,128)(2,1)}, u32[]{:S(2)}, u32[]{:S(2)}) collective-permute-start(bf16[8,8,9600]{2,1,0:T(8,128)(2,1)} %collective-permute-done.1.rest_1_), channel_id=1, source_target_pairs={{0,4},{1,3},{2,6},{3,1},{4,0},{5,7},{6,2},{7,5},{8,12},{9,11},{10,... | collective-permute-start | bytes 3686408 | tf_op jit(solution)/shard_map/ppermute | solution.py:473
  47.3 50.7 %all-to-all-start = ((s32[32,1,128]{2,1,0:T(1,128)}), s32[32,1,128]{2,1,0:T(1,128)S(1)}, u32[]{:S(2)}, u32[]{:S(2)}) async-start(s32[32,1,128]{2,1,0:T(1,128)} %broadcast_in_dim.11), calls=%async_computation | async-start | bytes 32768 | tf_op jit(solution)/shard_map/all_to_all | solution.py:477
  60.8 11.0 %copy-start.1 = (bf16[512,1024]{1,0:T(8,128)(2,1)}, bf16[512,1024]{1,0:T(8,128)(2,1)S(1)}, u32[]{:S(2)}) copy-start(bf16[512,1024]{1,0:T(8,128)(2,1)S(1)} %get-tuple-element.63.two_ref) | copy-start | bytes 3145732
  60.8 11.0 %copy-start.2 = (bf16[64,2048]{1,0:T(8,128)(2,1)}, bf16[64,2048]{1,0:T(8,128)(2,1)S(1)}, u32[]{:S(2)}) copy-start(bf16[64,2048]{1,0:T(8,128)(2,1)S(1)} %get-tuple-element.62.one_ref) | copy-start | bytes 786436
  60.8 11.0 %copy-start.3 = (bf16[256,256]{1,0:T(8,128)(2,1)}, bf16[256,256]{1,0:T(8,128)(2,1)S(1)}, u32[]{:S(2)}) copy-start(bf16[256,256]{1,0:T(8,128)(2,1)S(1)} %get-tuple-element.64.three_ref) | copy-start | bytes 393220
  69.5 43.0 %copy-start.6 = (bf16[8,8,9600]{2,1,0:T(8,128)(2,1)}, bf16[8,8,9600]{2,1,0:T(8,128)(2,1)S(1)}, u32[]{:S(2)}) copy-start(bf16[8,8,9600]{2,1,0:T(8,128)(2,1)S(1)} %collective-permute-done.5.rest_4_) | copy-start | bytes 3686404
  69.5 4.4 %copy-start.5 = (bf16[13,8,9600]{2,1,0:T(8,128)(2,1)}, bf16[13,8,9600]{2,1,0:T(8,128)(2,1)S(1)}, u32[]{:S(2)}) copy-start(bf16[13,8,9600]{2,1,0:T(8,128)(2,1)S(1)} %collective-permute-done.4.rest_3_) | copy-start | bytes 5990404
  71.8 41.3 %collective-permute-start.9 = (bf16[6,8,9600]{2,1,0:T(8,128)(2,1)}, bf16[6,8,9600]{2,1,0:T(8,128)(2,1)}, u32[]{:S(2)}, u32[]{:S(2)}) collective-permute-start(bf16[6,8,9600]{2,1,0:T(8,128)(2,1)} %slice.55), channel_id=1, source_target_pairs={{0,4},{1,3},{2,6},{3,1},{4,0},{5,7},{6,2},{7,5},{8,12},{9,11},{10,... | collective-permute-start | bytes 2764808 | tf_op jit(solution)/shard_map/ppermute | solution.py:473
  72.0 47.1 %collective-permute-start.8 = (bf16[7,8,9600]{2,1,0:T(8,128)(2,1)}, bf16[7,8,9600]{2,1,0:T(8,128)(2,1)}, u32[]{:S(2)}, u32[]{:S(2)}) collective-permute-start(bf16[7,8,9600]{2,1,0:T(8,128)(2,1)} %slice.54), channel_id=1, source_target_pairs={{0,2},{1,5},{2,0},{3,7},{4,6},{5,1},{6,4},{7,3},{8,10},{9,13},{10,... | collective-permute-start | bytes 3225608 | tf_op jit(solution)/shard_map/ppermute | solution.py:473
  73.9 45.1 %collective-permute-start.7 = (bf16[13,8,9600]{2,1,0:T(8,128)(2,1)S(1)}, bf16[13,8,9600]{2,1,0:T(8,128)(2,1)}, u32[]{:S(2)}, u32[]{:S(2)}) collective-permute-start(bf16[13,8,9600]{2,1,0:T(8,128)(2,1)S(1)} %collective-permute-done.4.rest_3_), channel_id=1, source_target_pairs={{0,8},{1,9},{2,10},{3,11},{4,12},{5,13},{6,14},{7,15},{8,24},{9,25... | collective-permute-start | bytes 5990408 | tf_op jit(solution)/shard_map/ppermute | solution.py:473
  96.0 42.8 %collective-permute-start.10 = (bf16[6,8,9600]{2,1,0:T(8,128)(2,1)}, bf16[6,8,9600]{2,1,0:T(8,128)(2,1)}, u32[]{:S(2)}, u32[]{:S(2)}) collective-permute-start(bf16[6,8,9600]{2,1,0:T(8,128)(2,1)} %slice.55), channel_id=1, source_target_pairs={{0,2},{1,5},{2,0},{3,7},{4,6},{5,1},{6,4},{7,3},{8,10},{9,13},{10,... | collective-permute-start | bytes 2764808 | tf_op jit(solution)/shard_map/ppermute | solution.py:473
  97.4 41.3 %collective-permute-start.11 = (bf16[7,8,9600]{2,1,0:T(8,128)(2,1)}, bf16[7,8,9600]{2,1,0:T(8,128)(2,1)}, u32[]{:S(2)}, u32[]{:S(2)}) collective-permute-start(bf16[7,8,9600]{2,1,0:T(8,128)(2,1)} %slice.54), channel_id=1, source_target_pairs={{0,4},{1,3},{2,6},{3,1},{4,0},{5,7},{6,2},{7,5},{8,12},{9,11},{10,... | collective-permute-start | bytes 3225608 | tf_op jit(solution)/shard_map/ppermute | solution.py:473
  98.0 0.6 copy-start.7
  119.0 39.5 %collective-permute-start.13 = (bf16[6,8,9600]{2,1,0:T(8,128)(2,1)}, bf16[6,8,9600]{2,1,0:T(8,128)(2,1)}, u32[]{:S(2)}, u32[]{:S(2)}) collective-permute-start(bf16[6,8,9600]{2,1,0:T(8,128)(2,1)} %collective-permute-done.9.rest_2_), channel_id=1, source_target_pairs={{0,2},{1,5},{2,0},{3,7},{4,6},{5,1},{6,4},{7,3},{8,10},{9,13},{10,... | collective-permute-start | bytes 2764808 | tf_op jit(solution)/shard_map/ppermute | solution.py:473
  120.5 39.6 %collective-permute-start.14 = (bf16[7,8,9600]{2,1,0:T(8,128)(2,1)}, bf16[7,8,9600]{2,1,0:T(8,128)(2,1)}, u32[]{:S(2)}, u32[]{:S(2)}) collective-permute-start(bf16[7,8,9600]{2,1,0:T(8,128)(2,1)} %collective-permute-done.8.rest_1_), channel_id=1, source_target_pairs={{0,4},{1,3},{2,6},{3,1},{4,0},{5,7},{6,2},{7,5},{8,12},{9,11},{10,... | collective-permute-start | bytes 3225608 | tf_op jit(solution)/shard_map/ppermute | solution.py:473
  121.0 47.6 %collective-permute-start.12 = (bf16[13,8,9600]{2,1,0:T(8,128)(2,1)}, bf16[13,8,9600]{2,1,0:T(8,128)(2,1)}, u32[]{:S(2)}, u32[]{:S(2)}) collective-permute-start(bf16[13,8,9600]{2,1,0:T(8,128)(2,1)} %collective-permute-done.7.rest_0_), channel_id=1, source_target_pairs={{0,8},{1,9},{2,10},{3,11},{4,12},{5,13},{6,14},{7,15},{8,24},{9,25... | collective-permute-start | bytes 5990408 | tf_op jit(solution)/shard_map/ppermute | solution.py:473
  143.9 35.1 %collective-permute-start.16 = (bf16[6,8,9600]{2,1,0:T(8,128)(2,1)S(1)}, bf16[6,8,9600]{2,1,0:T(8,128)(2,1)}, u32[]{:S(2)}, u32[]{:S(2)}) collective-permute-start(bf16[6,8,9600]{2,1,0:T(8,128)(2,1)S(1)} %slice.57), channel_id=1, source_target_pairs={{0,4},{1,3},{2,6},{3,1},{4,0},{5,7},{6,2},{7,5},{8,12},{9,11},{10,... | collective-permute-start | bytes 2764808 | tf_op jit(solution)/shard_map/ppermute | solution.py:473
  144.5 37.1 %collective-permute-start.15 = (bf16[7,8,9600]{2,1,0:T(8,128)(2,1)}, bf16[7,8,9600]{2,1,0:T(8,128)(2,1)}, u32[]{:S(2)}, u32[]{:S(2)}) collective-permute-start(bf16[7,8,9600]{2,1,0:T(8,128)(2,1)} %slice.56), channel_id=1, source_target_pairs={{0,2},{1,5},{2,0},{3,7},{4,6},{5,1},{6,4},{7,3},{8,10},{9,13},{10,... | collective-permute-start | bytes 3225608 | tf_op jit(solution)/shard_map/ppermute | solution.py:473
  158.5 47.0 %collective-permute-start.17 = (bf16[12,8,9600]{2,1,0:T(8,128)(2,1)}, bf16[12,8,9600]{2,1,0:T(8,128)(2,1)}, u32[]{:S(2)}, u32[]{:S(2)}) collective-permute-start(bf16[12,8,9600]{2,1,0:T(8,128)(2,1)} %slice_dynamic-update-slice_fusion), channel_id=1, source_target_pairs={{0,8},{1,9},{2,10},{3,11},{4,12},{5,13},{6,14},{7,15},{8,24},{9,25... | collective-permute-start | bytes 5529608 | tf_op jit(solution)/shard_map/ppermute | solution.py:473
  168.7 32.7 %collective-permute-start.18 = (bf16[6,8,9600]{2,1,0:T(8,128)(2,1)S(1)}, bf16[6,8,9600]{2,1,0:T(8,128)(2,1)}, u32[]{:S(2)}, u32[]{:S(2)}) collective-permute-start(bf16[6,8,9600]{2,1,0:T(8,128)(2,1)S(1)} %slice.57), channel_id=1, source_target_pairs={{0,2},{1,5},{2,0},{3,7},{4,6},{5,1},{6,4},{7,3},{8,10},{9,13},{10,... | collective-permute-start | bytes 2764808 | tf_op jit(solution)/shard_map/ppermute | solution.py:473
  168.9 33.1 %collective-permute-start.19 = (bf16[7,8,9600]{2,1,0:T(8,128)(2,1)}, bf16[7,8,9600]{2,1,0:T(8,128)(2,1)}, u32[]{:S(2)}, u32[]{:S(2)}) collective-permute-start(bf16[7,8,9600]{2,1,0:T(8,128)(2,1)} %slice.56), channel_id=1, source_target_pairs={{0,4},{1,3},{2,6},{3,1},{4,0},{5,7},{6,2},{7,5},{8,12},{9,11},{10,... | collective-permute-start | bytes 3225608 | tf_op jit(solution)/shard_map/ppermute | solution.py:473
  181.6 39.5 %collective-permute-start.20 = (bf16[6,8,9600]{2,1,0:T(8,128)(2,1)}, bf16[6,8,9600]{2,1,0:T(8,128)(2,1)}, u32[]{:S(2)}, u32[]{:S(2)}) collective-permute-start(bf16[6,8,9600]{2,1,0:T(8,128)(2,1)} %collective-permute-done.16.rest_1_), channel_id=1, source_target_pairs={{0,2},{1,5},{2,0},{3,7},{4,6},{5,1},{6,4},{7,3},{8,10},{9,13},{10,... | collective-permute-start | bytes 2764808 | tf_op jit(solution)/shard_map/ppermute | solution.py:473
  183.1 42.0 %collective-permute-start.21 = (bf16[7,8,9600]{2,1,0:T(8,128)(2,1)}, bf16[7,8,9600]{2,1,0:T(8,128)(2,1)}, u32[]{:S(2)}, u32[]{:S(2)}) collective-permute-start(bf16[7,8,9600]{2,1,0:T(8,128)(2,1)} %collective-permute-done.15.rest_0_), channel_id=1, source_target_pairs={{0,4},{1,3},{2,6},{3,1},{4,0},{5,7},{6,2},{7,5},{8,12},{9,11},{10,... | collective-permute-start | bytes 3225608 | tf_op jit(solution)/shard_map/ppermute | solution.py:473
  205.5 41.2 %collective-permute-start.22 = (bf16[12,8,9600]{2,1,0:T(8,128)(2,1)}, bf16[12,8,9600]{2,1,0:T(8,128)(2,1)}, u32[]{:S(2)}, u32[]{:S(2)}) collective-permute-start(bf16[12,8,9600]{2,1,0:T(8,128)(2,1)} %collective-permute-done.17.rest_2_), channel_id=1, source_target_pairs={{0,8},{1,9},{2,10},{3,11},{4,12},{5,13},{6,14},{7,15},{8,24},{9,25... | collective-permute-start | bytes 5529608 | tf_op jit(solution)/shard_map/ppermute | solution.py:473
  208.0 40.2 %collective-permute-start.24 = (bf16[6,8,9600]{2,1,0:T(8,128)(2,1)S(1)}, bf16[6,8,9600]{2,1,0:T(8,128)(2,1)}, u32[]{:S(2)}, u32[]{:S(2)}) collective-permute-start(bf16[6,8,9600]{2,1,0:T(8,128)(2,1)S(1)} %slice.67), channel_id=1, source_target_pairs={{0,4},{1,3},{2,6},{3,1},{4,0},{5,7},{6,2},{7,5},{8,12},{9,11},{10,... | collective-permute-start | bytes 2764808 | tf_op jit(solution)/shard_map/ppermute | solution.py:473
  209.6 38.7 %collective-permute-start.23 = (bf16[7,8,9600]{2,1,0:T(8,128)(2,1)}, bf16[7,8,9600]{2,1,0:T(8,128)(2,1)}, u32[]{:S(2)}, u32[]{:S(2)}) collective-permute-start(bf16[7,8,9600]{2,1,0:T(8,128)(2,1)} %slice.66), channel_id=1, source_target_pairs={{0,2},{1,5},{2,0},{3,7},{4,6},{5,1},{6,4},{7,3},{8,10},{9,13},{10,... | collective-permute-start | bytes 3225608 | tf_op jit(solution)/shard_map/ppermute | solution.py:473
  225.1 38.8 %collective-permute-start.25 = (bf16[6,8,9600]{2,1,0:T(8,128)(2,1)S(1)}, bf16[6,8,9600]{2,1,0:T(8,128)(2,1)}, u32[]{:S(2)}, u32[]{:S(2)}) collective-permute-start(bf16[6,8,9600]{2,1,0:T(8,128)(2,1)S(1)} %slice.67), channel_id=1, source_target_pairs={{0,2},{1,5},{2,0},{3,7},{4,6},{5,1},{6,4},{7,3},{8,10},{9,13},{10,... | collective-permute-start | bytes 2764808 | tf_op jit(solution)/shard_map/ppermute | solution.py:473
  227.6 40.3 %collective-permute-start.26 = (bf16[7,8,9600]{2,1,0:T(8,128)(2,1)}, bf16[7,8,9600]{2,1,0:T(8,128)(2,1)}, u32[]{:S(2)}, u32[]{:S(2)}) collective-permute-start(bf16[7,8,9600]{2,1,0:T(8,128)(2,1)} %slice.66), channel_id=1, source_target_pairs={{0,4},{1,3},{2,6},{3,1},{4,0},{5,7},{6,2},{7,5},{8,12},{9,11},{10,... | collective-permute-start | bytes 3225608 | tf_op jit(solution)/shard_map/ppermute | solution.py:473
  246.7 39.8 %collective-permute-start.27 = (bf16[12,8,9600]{2,1,0:T(8,128)(2,1)}, bf16[12,8,9600]{2,1,0:T(8,128)(2,1)}, u32[]{:S(2)}, u32[]{:S(2)}) collective-permute-start(bf16[12,8,9600]{2,1,0:T(8,128)(2,1)} %collective-permute-done.22.rest_0_), channel_id=1, source_target_pairs={{0,8},{1,9},{2,10},{3,11},{4,12},{5,13},{6,14},{7,15},{8,24},{9,25... | collective-permute-start | bytes 5529608 | tf_op jit(solution)/shard_map/ppermute | solution.py:473
  248.3 35.3 %collective-permute-start.28 = (bf16[6,8,9600]{2,1,0:T(8,128)(2,1)}, bf16[6,8,9600]{2,1,0:T(8,128)(2,1)}, u32[]{:S(2)}, u32[]{:S(2)}) collective-permute-start(bf16[6,8,9600]{2,1,0:T(8,128)(2,1)} %collective-permute-done.24.rest_2_), channel_id=1, source_target_pairs={{0,2},{1,5},{2,0},{3,7},{4,6},{5,1},{6,4},{7,3},{8,10},{9,13},{10,... | collective-permute-start | bytes 2764808 | tf_op jit(solution)/shard_map/ppermute | solution.py:473
  249.2 37.3 %collective-permute-start.29 = (bf16[7,8,9600]{2,1,0:T(8,128)(2,1)}, bf16[7,8,9600]{2,1,0:T(8,128)(2,1)}, u32[]{:S(2)}, u32[]{:S(2)}) collective-permute-start(bf16[7,8,9600]{2,1,0:T(8,128)(2,1)} %collective-permute-done.23.rest_1_), channel_id=1, source_target_pairs={{0,4},{1,3},{2,6},{3,1},{4,0},{5,7},{6,2},{7,5},{8,12},{9,11},{10,... | collective-permute-start | bytes 3225608 | tf_op jit(solution)/shard_map/ppermute | solution.py:473
Sparse Core Ops, SparseCore 0:
  8.9 62.0 all-gather.1
